TPU v7x, 32 devices: a whole 2x2x4 slice. The times are simulated.
32 devices in a mesh: px: 2 (over core), py: 16 (over z, y, x).
Axes of the slice: x: 2, y: 2, z: 4, core: 2. Of those that a mesh axis runs over, the one named last changes fastest.
Arguments:
- span: float32 [64, 8, 64, 128], P(None, 'px', 'py'), may hold values from -4 to 4
- potential: float32 [8, 64, 128], P('px', 'py'), may hold values from 0.1 to 2
- cell_matrix: float32 [125, 125], replicated, may hold values from -2 to 7, as said below
- block: bfloat16 [256, 8, 64, 128], P(None, 'px', 'py'), may hold values from -0.03125 to 0.03125
Outputs:
- filtered: float32 [64, 8, 64, 128], P(None, 'px', 'py')
- margin: float32 [64, 256], P('px', 'py')
Inputs may be any that keep to these rules, and one draw needn't show every extreme that they name: `cell_matrix`: symmetric.
All inputs are finite; a program needn't handle non-finite values.
Results may differ from a plain program's by a relative error of at most 0.0029.
Values sent between devices are 32-bit elements; how exact they have to be, the bound alone decides.
No kernel may reach another device: no remote copies, remote signals or barrier semaphores. Data moves between devices by JAX's collectives and lax.ppermute only.
A program may use at most 128 MiB of HBM per device.

v0:
```python
import jax
import jax.numpy as jnp
from jax import lax
from jax.sharding import PartitionSpec as P

centre = 13.0
half_width = 9.0


def shifted(value, axis, steps):
    count = lax.axis_size(axis)
    pairs = [(source, (source + steps) % count) for source in range(count)]
    return lax.ppermute(value, axis, pairs)


def unfold_open(values, which_axis):
    reordered = jnp.moveaxis(values, which_axis, 0)
    cell_count = (reordered.shape[0] - 1) // 4
    rest_shape = reordered.shape[1:]
    lower_part = reordered[: 4 * cell_count].reshape((cell_count, 4) + rest_shape)
    upper_part = reordered[4::4]
    return jnp.concatenate([lower_part, upper_part[:, None]], 1)


def unfold_cyclic(values, which_axis):
    reordered = jnp.moveaxis(values, which_axis, 0)
    cell_count = reordered.shape[0] // 4
    rest_shape = reordered.shape[1:]
    lower_part = reordered.reshape((cell_count, 4) + rest_shape)
    upper_part = jnp.roll(lower_part[:, 0], -1, axis=0)
    return jnp.concatenate([lower_part, upper_part[:, None]], 1)


def fold_open(values):
    cell_count = values.shape[0]
    rest_shape = values.shape[2:]
    zero_row = jnp.zeros((1,) + rest_shape, values.dtype)
    base_rows = jnp.concatenate(
        [values[:, :4].reshape((4 * cell_count,) + rest_shape), zero_row], 0
    )
    tail_rows = jnp.concatenate(
        [jnp.zeros((cell_count, 3) + rest_shape, values.dtype), values[:, 4:5]], 1
    )
    tail_rows = tail_rows.reshape((4 * cell_count,) + rest_shape)
    return base_rows + jnp.concatenate([zero_row, tail_rows], 0)


def fold_cyclic(values):
    cell_count = values.shape[0]
    rest_shape = values.shape[2:]
    shared = values[:, 0] + jnp.roll(values[:, 4], 1, axis=0)
    joined = jnp.concatenate([shared[:, None], values[:, 1:4]], 1)
    return joined.reshape((4 * cell_count,) + rest_shape)


def cell_products(sectioned, cell_matrix):
    cell_values = jnp.transpose(sectioned, (6, 5, 3, 1, 4, 2, 0))
    shape_cells = cell_values.shape
    flat_cells = cell_values.reshape((shape_cells[0], 125, -1))
    products = jnp.einsum("ij,sjc->sic", cell_matrix, flat_cells, precision=lax.Precision.HIGHEST)
    return jnp.transpose(products.reshape(shape_cells), (4, 1, 5, 2, 6, 3, 0))


def cell_apply(extended, cell_matrix):
    sectioned = unfold_open(extended, 1)
    sectioned = unfold_open(sectioned, 3)
    sectioned = unfold_cyclic(sectioned, 5)
    sectioned = cell_products(sectioned, cell_matrix)
    sectioned = fold_open(sectioned)
    sectioned = fold_open(jnp.moveaxis(sectioned, 0, -1))
    sectioned = fold_cyclic(jnp.moveaxis(sectioned, 0, -1))
    return jnp.moveaxis(sectioned, 0, -1)


def apply_shifted(vector, potential, cell_matrix):
    above_x = shifted(vector[:, :1], "px", -1)
    extended = jnp.concatenate([vector, above_x], 1)
    above_y = shifted(extended[:, :, :1], "py", -1)
    extended = jnp.concatenate([extended, above_y], 2)
    summed = cell_apply(extended, cell_matrix)
    returned_y = shifted(summed[:, :, -1:], "py", 1)
    half_done = jnp.concatenate([summed[:, :, :1] + returned_y, summed[:, :, 1:-1]], 2)
    returned_x = shifted(half_done[:, -1:], "px", 1)
    assembled = jnp.concatenate([half_done[:, :1] + returned_x, half_done[:, 1:-1]], 1)
    return assembled + potential * vector - centre * vector


def local(span, potential, cell_matrix, block):
    first = apply_shifted(span, potential, cell_matrix) / half_width
    second = 2.0 * apply_shifted(first, potential, cell_matrix) / half_width - span
    filtered = 2.0 * apply_shifted(second, potential, cell_matrix) / half_width - first
    state_count = span.shape[0]
    block_count = block.shape[0]
    rounded = filtered.astype(jnp.bfloat16).reshape((state_count, -1))
    partial_margin = lax.dot_general(
        rounded,
        block.reshape((block_count, -1)),
        (((1,), (1,)), ((), ())),
        preferred_element_type=jnp.float32,
    )
    total = lax.psum(partial_margin, ("px", "py"))
    tile_rows = state_count // lax.axis_size("px")
    tile_cols = block_count // lax.axis_size("py")
    tile = lax.dynamic_slice(
        total,
        (lax.axis_index("px") * tile_rows, lax.axis_index("py") * tile_cols),
        (tile_rows, tile_cols),
    )
    return (filtered, tile)


def solution(mesh):
    in_specs = (P(None, "px", "py", None), P("px", "py", None), P(), P(None, "px", "py", None))
    out_specs = (P(None, "px", "py", None), P("px", "py"))
    return jax.shard_map(local, mesh=mesh, in_specs=in_specs, out_specs=out_specs, check_vma=False)
```

profile of v0, /device:TPU:0, one launch (start us, length us, event | category | flops | bytes accessed | tf_op | source)
XLA Modules:
  0.0 272.1 jit_solution(12518494817798848183)
XLA Ops:
  9.9 6.7 %collective-permute-start.1 = (f32[64,5,1,128]{3,0,2,1:T(8,128)S(1)}, f32[64,5,1,128]{3,0,2,1:T(8,128)S(1)}, u32[]{:S(2)}, u32[]{:S(2)}) collective-permute-start(f32[64,5,1,128]{3,0,2,1:T(8,128)S(1)} %slice.323), channel_id=1, source_target_pairs={{0,15},{1,0},{2,1},{3,2},{4,3},{5,4},{6,5},{7,6},{8,7},{9,8},{10,9... | collective-permute-start | bytes 491528 | tf_op jit(solution)/shard_map/ppermute | solution.py:13
  16.6 4.0 %collective-permute-done.1 = f32[64,5,1,128]{3,0,2,1:T(8,128)S(1)} collective-permute-done((f32[64,5,1,128]{3,0,2,1:T(8,128)S(1)}, f32[64,5,1,128]{3,0,2,1:T(8,128)S(1)}, u32[]{:S(2)}, u32[]{:S(2)}) %collective-permute-start.1) | collective-permute-done | bytes 163872 | tf_op jit(solution)/shard_map/ppermute | solution.py:13
  23.0 4.2 %fusion.6 = f32[64,125,32]{1,0,2:T(8,128)S(1)} fusion(f32[64,125,32]{0,2,1:T(8,128)S(1)} %bitcast.163, f32[125,125]{1,0:T(8,128)S(1)} %copy-done), kind=kOutput, calls=%fused_computation.36 | convolution fusion | flops 384000000 | bytes 2110500 | tf_op jit(solution)/shard_map/ij,sjc->sic/dot_general | solution.py:60
  27.2 1.8 copy.70
  32.9 13.4 %collective-permute-done.2 = f32[64,5,1,128]{0,3,2,1:T(8,128)S(1)} collective-permute-done((f32[64,5,1,128]{0,3,2,1:T(8,128)S(1)}, f32[64,5,1,128]{0,3,2,1:T(8,128)S(1)}, u32[]{:S(2)}, u32[]{:S(2)}) %collective-permute-start.2) | collective-permute-done | bytes 163872 | tf_op jit(solution)/shard_map/ppermute | solution.py:13
  49.0 1.4 collective-permute-done.4
  50.4 1.8 collective-permute-start.5
  52.2 8.0 %collective-permute-done.5 = f32[64,5,1,128]{0,3,2,1:T(8,128)S(1)} collective-permute-done((f32[64,5,1,128]{0,3,2,1:T(8,128)S(1)}, f32[64,5,1,128]{0,3,2,1:T(8,128)S(1)}, u32[]{:S(2)}, u32[]{:S(2)}) %collective-permute-start.5) | collective-permute-done | bytes 163872 | tf_op jit(solution)/shard_map/ppermute | solution.py:13
  62.8 4.2 %fusion.9 = f32[64,125,32]{1,0,2:T(8,128)S(1)} fusion(f32[64,125,32]{0,2,1:T(8,128)S(1)} %bitcast.164, f32[125,125]{1,0:T(8,128)S(1)} %copy-done), kind=kOutput, calls=%fused_computation.37 | convolution fusion | flops 384000000 | bytes 2110500 | tf_op jit(solution)/shard_map/ij,sjc->sic/dot_general | solution.py:60
  67.0 2.8 %copy.81 = f32[64,125,32]{0,2,1:T(8,128)} copy(f32[64,125,32]{1,0,2:T(8,128)S(1)} %fusion.9) | data formatting | bytes 2048000 | tf_op jit(solution)/shard_map/ij,sjc->sic/transpose | solution.py:60
  70.8 1.6 slice_bitcast_fusion.3
  75.6 9.4 %collective-permute-start.6 = (f32[64,5,1,128]{0,3,2,1:T(8,128)S(1)}, f32[64,5,1,128]{0,3,2,1:T(8,128)S(1)}, u32[]{:S(2)}, u32[]{:S(2)}) collective-permute-start(f32[64,5,1,128]{0,3,2,1:T(8,128)S(1)} %slice.357), channel_id=1, source_target_pairs={{0,1},{1,2},{2,3},{3,4},{4,5},{5,6},{6,7},{7,8},{8,9},{9,10},{10,1... | collective-permute-start | bytes 491528 | tf_op jit(solution)/shard_map/ppermute | solution.py:13
  85.1 12.4 %collective-permute-done.6 = f32[64,5,1,128]{0,3,2,1:T(8,128)S(1)} collective-permute-done((f32[64,5,1,128]{0,3,2,1:T(8,128)S(1)}, f32[64,5,1,128]{0,3,2,1:T(8,128)S(1)}, u32[]{:S(2)}, u32[]{:S(2)}) %collective-permute-start.6) | collective-permute-done | bytes 163872 | tf_op jit(solution)/shard_map/ppermute | solution.py:13
  97.7 1.5 collective-permute-done.7
  100.2 1.4 collective-permute-done.8
  101.7 1.8 collective-permute-start.9
  103.5 8.0 %collective-permute-done.9 = f32[64,5,1,128]{0,3,2,1:T(8,128)S(1)} collective-permute-done((f32[64,5,1,128]{0,3,2,1:T(8,128)S(1)}, f32[64,5,1,128]{0,3,2,1:T(8,128)S(1)}, u32[]{:S(2)}, u32[]{:S(2)}) %collective-permute-start.9) | collective-permute-done | bytes 163872 | tf_op jit(solution)/shard_map/ppermute | solution.py:13
  114.0 4.2 %fusion.12 = f32[64,125,32]{1,0,2:T(8,128)S(1)} fusion(f32[64,125,32]{0,2,1:T(8,128)S(1)} %bitcast.165, f32[125,125]{1,0:T(8,128)S(1)} %copy-done), kind=kOutput, calls=%fused_computation.38 | convolution fusion | flops 384000000 | bytes 2110500 | tf_op jit(solution)/shard_map/ij,sjc->sic/dot_general | solution.py:60
  118.2 2.8 %copy.91 = f32[64,125,32]{0,2,1:T(8,128)} copy(f32[64,125,32]{1,0,2:T(8,128)S(1)} %fusion.12) | data formatting | bytes 2048000 | tf_op jit(solution)/shard_map/ij,sjc->sic/transpose | solution.py:60
  122.1 1.6 slice_bitcast_fusion.1
  127.0 12.4 %collective-permute-done.10 = f32[64,5,1,128]{0,3,2,1:T(8,128)S(1)} collective-permute-done((f32[64,5,1,128]{0,3,2,1:T(8,128)S(1)}, f32[64,5,1,128]{0,3,2,1:T(8,128)S(1)}, u32[]{:S(2)}, u32[]{:S(2)}) %collective-permute-start.10) | collective-permute-done | bytes 163872 | tf_op jit(solution)/shard_map/ppermute | solution.py:13
  139.5 1.5 collective-permute-done.11
  143.6 2.4 copy.95
  146.0 117.7 %all-reduce.20.cloned.1.call-done = f32[64,256]{0,1:T(8,128)} async-done(((f32[64,256]{0,1:T(8,128)}), f32[64,256]{0,1:T(8,128)}) %all-reduce.20.cloned.1.call-update) | async-done | bytes 65552 | tf_op jit(solution)/shard_map/psum | solution.py:101
  (141 shorter events, 30.0 us)
Async XLA Ops:
  7.2 15.8 %copy-start = (f32[125,125]{1,0:T(8,128)S(1)}, f32[125,125]{1,0:T(8,128)}, u32[]{:S(2)}) copy-start(f32[125,125]{1,0:T(8,128)} %param.6) | copy-start | bytes 187504
  7.2 256.5 %all-reduce.20.cloned.1.call-start = ((), (), s32[]{:S(2)}) async-start(), calls=%async_computation | async-start | bytes 262144 | tf_op jit(solution)/shard_map/psum | solution.py:101
  8.2 1.7 collective-permute-start
  9.9 10.7 %collective-permute-start.1 = (f32[64,5,1,128]{3,0,2,1:T(8,128)S(1)}, f32[64,5,1,128]{3,0,2,1:T(8,128)S(1)}, u32[]{:S(2)}, u32[]{:S(2)}) collective-permute-start(f32[64,5,1,128]{3,0,2,1:T(8,128)S(1)} %slice.323), channel_id=1, source_target_pairs={{0,15},{1,0},{2,1},{3,2},{4,3},{5,4},{6,5},{7,6},{8,7},{9,8},{10,9... | collective-permute-start | bytes 491528 | tf_op jit(solution)/shard_map/ppermute | solution.py:13
  32.5 13.8 %collective-permute-start.2 = (f32[64,5,1,128]{0,3,2,1:T(8,128)S(1)}, f32[64,5,1,128]{0,3,2,1:T(8,128)S(1)}, u32[]{:S(2)}, u32[]{:S(2)}) collective-permute-start(f32[64,5,1,128]{0,3,2,1:T(8,128)S(1)} %slice.339), channel_id=1, source_target_pairs={{0,1},{1,2},{2,3},{3,4},{4,5},{5,6},{6,7},{7,8},{8,9},{9,10},{10,1... | collective-permute-start | bytes 491528 | tf_op jit(solution)/shard_map/ppermute | solution.py:13
  32.9 13.6 %copy-start.4 = (f32[64,4,4,128]{3,2,1,0:T(4,128)S(1)}, f32[64,4,4,128]{3,2,1,0:T(4,128)}, u32[]{:S(2)}) copy-start(f32[64,4,4,128]{3,2,1,0:T(4,128)} %param.4) | copy-start | bytes 1572868
  46.4 1.6 copy-start.8
  46.4 1.6 collective-permute-start.3
  46.9 1.6 copy-start.1
  48.1 0.7 copy-start.5
  48.8 1.6 collective-permute-start.4
  50.4 9.8 %collective-permute-start.5 = (f32[64,5,1,128]{0,3,2,1:T(8,128)S(1)}, f32[64,5,1,128]{0,3,2,1:T(8,128)S(1)}, u32[]{:S(2)}, u32[]{:S(2)}) collective-permute-start(f32[64,5,1,128]{0,3,2,1:T(8,128)S(1)} %pad_maximum_fusion.7), channel_id=1, source_target_pairs={{0,15},{1,0},{2,1},{3,2},{4,3},{5,4},{6,5},{7,6},{8,7},{9,8},{10,9... | collective-permute-start | bytes 491528 | tf_op jit(solution)/shard_map/ppermute | solution.py:13
  75.6 21.9 %collective-permute-start.6 = (f32[64,5,1,128]{0,3,2,1:T(8,128)S(1)}, f32[64,5,1,128]{0,3,2,1:T(8,128)S(1)}, u32[]{:S(2)}, u32[]{:S(2)}) collective-permute-start(f32[64,5,1,128]{0,3,2,1:T(8,128)S(1)} %slice.357), channel_id=1, source_target_pairs={{0,1},{1,2},{2,3},{3,4},{4,5},{5,6},{6,7},{7,8},{8,9},{9,10},{10,1... | collective-permute-start | bytes 491528 | tf_op jit(solution)/shard_map/ppermute | solution.py:13
  97.5 1.7 copy-start.2
  97.5 1.7 copy-start.6
  97.6 1.6 collective-permute-start.7
  100.0 1.6 collective-permute-start.8
  101.7 9.8 %collective-permute-start.9 = (f32[64,5,1,128]{0,3,2,1:T(8,128)S(1)}, f32[64,5,1,128]{0,3,2,1:T(8,128)S(1)}, u32[]{:S(2)}, u32[]{:S(2)}) collective-permute-start(f32[64,5,1,128]{0,3,2,1:T(8,128)S(1)} %pad_maximum_fusion.6), channel_id=1, source_target_pairs={{0,15},{1,0},{2,1},{3,2},{4,3},{5,4},{6,5},{7,6},{8,7},{9,8},{10,9... | collective-permute-start | bytes 491528 | tf_op jit(solution)/shard_map/ppermute | solution.py:13
  126.8 12.6 %collective-permute-start.10 = (f32[64,5,1,128]{0,3,2,1:T(8,128)S(1)}, f32[64,5,1,128]{0,3,2,1:T(8,128)S(1)}, u32[]{:S(2)}, u32[]{:S(2)}) collective-permute-start(f32[64,5,1,128]{0,3,2,1:T(8,128)S(1)} %slice.375), channel_id=1, source_target_pairs={{0,1},{1,2},{2,3},{3,4},{4,5},{5,6},{6,7},{7,8},{8,9},{9,10},{10,1... | collective-permute-start | bytes 491528 | tf_op jit(solution)/shard_map/ppermute | solution.py:13
  139.5 1.6 collective-permute-start.11
  141.1 1.4 copy-start.7
  141.5 1.0 copy-start.3
Sparse Core Ops, SparseCore 0:
  143.7 119.9 all-reduce.19
where the time goes:
time: 276 us; the launch traced here: 272 us
  waiting for transfers between devices  183 us (66%)
  local copies, waits for them, and re-layouts  30.4 us (11%)
  starting transfers between devices  21.2 us (8%)
  between operations  15.2 us (6%)
  matrix products  13.6 us (5%)
  other arithmetic  8.73 us (3%)
    psum x1, waiting for transfers between devices, local(): total = lax.psum(partial_margin, ('px', 'py'))  118 us
    ppermute x12, waiting for transfers between devices, shifted(): return lax.ppermute(value, axis, pairs)  65.2 us
    ppermute x12, starting transfers between devices, shifted(): return lax.ppermute(value, axis, pairs)  21.1 us
    dot_general x3, matrix products, cell_products(): jnp.einsum('ij,sjc->sic', cell_matrix, flat_cells, precision=lax.Precisio...  12.6 us
    transpose x3, local copies, waits for them, and re-layouts, cell_products(): jnp.einsum('ij,sjc->sic', cell_matrix, flat_cells, precision=lax.Precisio...  7.47 us
  transfers between devices with their start and end apart: 13, of which 12 were waited for; matrix products, arithmetic and copies ran while one was open for 2% of the time, Pallas kernels for 0%

commit v1 on v0

v1 whole, which is shorter than its diff:
```python
import functools

import jax
import jax.numpy as jnp
import ml_dtypes
import numpy as np
from jax import lax
from jax.experimental import pallas as pl
from jax.experimental.pallas import tpu as pltpu
from jax.sharding import Mesh, PartitionSpec as P

centre = 13.0
half_width = 9.0
lanes = 128
bf16 = jnp.bfloat16
f32 = jnp.float32
whole = pl.BlockSpec(memory_space=pltpu.VMEM)
anywhere = pl.BlockSpec(memory_space=pl.ANY)
params = pltpu.CompilerParams(vmem_limit_bytes=48 * 2**20)

BLOCKS = (
    [(iz, iy) for iz in range(4) for iy in range(4)]
    + [(4, iy) for iy in range(4)]
    + [(iz, 4) for iz in range(4)]
    + [(4, 4)]
)
PADDED = 26


def two_parts(value):
    high = value.astype(bf16)
    return high, (value - high.astype(f32)).astype(bf16)


def dot(a, b):
    return jnp.dot(a, b, preferred_element_type=f32)


def selections(first_nodes):
    cells = first_nodes // 4
    table = np.zeros((cells, PADDED * first_nodes, 125), np.float32)
    for cell in range(cells):
        for place, (jz, jy) in enumerate(BLOCKS):
            for jx in range(5):
                row = place * first_nodes + (4 * cell + jx) % first_nodes
                table[cell, row, (jx * 5 + jy) * 5 + jz] = 1.0
    return table.astype(ml_dtypes.bfloat16)


def lane_orders(group, thickness):
    cells = thickness // 4
    order = np.zeros((group, cells, 4, 4, group, cells), np.float32)
    spread = np.zeros((cells, 4, 4, group, cells), np.float32)
    for iz in range(4):
        for cell in range(cells):
            for state in range(group):
                order[state, cell, iz, iz, state, cell] = 1.0
                spread[cell, iz, iz, state, cell] = 1.0
    order = order.reshape(group * thickness, 4 * group * cells)
    spread = spread.reshape(thickness, 4 * group * cells)
    return order.astype(ml_dtypes.bfloat16), spread.astype(ml_dtypes.bfloat16)


def matrix_kernel(cell_ref, select_ref, high_ref, low_ref):
    rest = cell_ref[...]
    total = jnp.zeros(high_ref.shape, f32)
    for _ in range(3):
        part = rest.astype(bf16)
        rest = rest - part.astype(f32)
        for cell in range(select_ref.shape[0]):
            chosen = select_ref[cell]
            left = dot(chosen, part).astype(bf16)
            total = total + lax.dot_general(left, chosen, (((1,), (1,)), ((), ())), preferred_element_type=f32)
    high_ref[...], low_ref[...] = two_parts(total)


def roll_cells(value, cells, forward):
    out = []
    place = lax.broadcasted_iota(jnp.int32, (value.shape[0], lanes), 1) % cells
    for start in range(0, value.shape[1], lanes):
        part = value[:, start : start + lanes]
        if forward:
            moved = jnp.where(place == cells - 1, pltpu.roll(part, cells - 1, 1), pltpu.roll(part, lanes - 1, 1))
        else:
            moved = jnp.where(place == 0, pltpu.roll(part, lanes - cells + 1, 1), pltpu.roll(part, 1, 1))
        out.append(moved)
    return out[0] if len(out) == 1 else jnp.concatenate(out, 1)


def three_products(high, low, value):
    value_high, value_low = two_parts(value)
    return dot(high, value_high) + (dot(low, value_high) + dot(high, value_low))


def fold_last(rows, nodes, cells):
    parts = [rows[iz * nodes : (iz + 1) * nodes] for iz in range(5)]
    parts[0] = parts[0] + roll_cells(parts[4], cells, False)
    return parts[:4]


def outgoing(high_ref, low_ref, last_cell, cells):
    nodes = last_cell[0].shape[0]
    stacked = jnp.concatenate(last_cell + [roll_cells(last_cell[iy], cells, True) for iy in range(4)], 0)
    rows, cols = slice(20 * nodes, PADDED * nodes), slice(0, 20 * nodes)
    return fold_last(three_products(high_ref[rows, cols], low_ref[rows, cols], stacked), nodes, cells)


def to_cells_kernel(cells, second, raw_ref, order_ref, spread_ref, high_ref, low_ref, w_ref, pot_ref, down_ref, up_ref, held, sems):
    parts_x, parts_y, count = raw_ref.shape[:3]
    states = count - 1
    layer = raw_ref.shape[3]
    copies = [
        pltpu.make_async_copy(raw_ref.at[px], held.at[:, :, pl.ds(px * layer, layer), :], sems.at[px])
        for px in range(parts_x)
    ]
    for copy in copies:
        copy.start()
    for copy in copies:
        copy.wait()
    nodes = parts_x * layer // second
    rows_y = parts_y * second
    group = lanes // cells
    groups = states // group

    def gathered(state):
        rows = [held[y // second, state, pl.ds(y % second, nodes, stride=second), :] for y in range(rows_y)]
        return jnp.concatenate(rows, 0)

    sources = []
    for h in range(groups):
        sources += list(two_parts(jnp.concatenate([gathered(h * group + s) for s in range(group)], 1)))
    ordered = dot(jnp.concatenate(sources, 0), order_ref[...])
    high, low = two_parts(gathered(states))
    potential = dot(jnp.concatenate([high, low], 0), spread_ref[...])
    size = rows_y * nodes
    potential = potential[:size] + potential[size:]
    values = [ordered[2 * h * size : (2 * h + 1) * size] + ordered[(2 * h + 1) * size : (2 * h + 2) * size] for h in range(groups)]

    def block(cy, iz, iy):
        start = (4 * cy + iy) * nodes
        parts = [value[start : start + nodes, iz * lanes : (iz + 1) * lanes] for value in values]
        return parts[0] if groups == 1 else jnp.concatenate(parts, 1)

    for cy in range(rows_y // 4):
        for iz in range(4):
            for iy in range(4):
                start = (4 * cy + iy) * nodes
                w_ref[iz, cy, iy] = block(cy, iz, iy)
                pot_ref[iz, cy, iy] = potential[start : start + nodes, iz * lanes : (iz + 1) * lanes]
    last = rows_y // 4 - 1
    up = outgoing(high_ref, low_ref, [block(last, iz, iy) for iz in range(4) for iy in range(4)], cells)
    for iz in range(4):
        down_ref[iz] = block(0, iz, 0)
        up_ref[iz] = up[iz]


def apply_kernel(cells, second, step, *refs):
    refs = list(refs)
    w_ref, pot_ref, high_ref, low_ref, halo_ref, from_ref = refs[:6]
    del refs[:6]
    before_ref = refs.pop(0) if step > 0 else None
    order_ref = refs.pop(0) if step == 2 else None
    cy_count, nodes, width = w_ref.shape[1], w_ref.shape[3], w_ref.shape[4]
    groups = width // lanes
    high, low = high_ref[...], low_ref[...]

    columns = []
    for cy in range(cy_count):
        own = [w_ref[iz, cy, iy] for iz in range(4) for iy in range(4)]
        after = [w_ref[iz, cy + 1, 0] if cy + 1 < cy_count else halo_ref[iz] for iz in range(4)]
        stacked = own + [roll_cells(own[iy], cells, True) for iy in range(4)]
        stacked += after + [roll_cells(after[0], cells, True), jnp.zeros((nodes, width), f32)]
        columns.append(jnp.concatenate(stacked, 0))
    product = three_products(high, low, jnp.concatenate(columns, 1))
    product = [product[:, cy * width : (cy + 1) * width] for cy in range(cy_count)]

    edge = [w_ref[iz, 0, 0] for iz in range(4)]
    edge = jnp.concatenate(edge + [roll_cells(edge[0], cells, True), jnp.zeros((nodes, width), f32)], 0)
    tail = slice(20 * nodes, PADDED * nodes)
    edge = fold_last(three_products(high_ref[tail, tail], low_ref[tail, tail], edge), nodes, cells)
    incoming = [edge[iz] + from_ref[iz] for iz in range(4)]

    result = {}
    for cy in range(cy_count):
        for iz in range(4):
            for iy in range(4):
                start = (iz * 4 + iy) * nodes
                total = product[cy][start : start + nodes]
                if iz == 0:
                    start = (16 + iy) * nodes
                    total = total + roll_cells(product[cy][start : start + nodes], cells, False)
                if iy == 0:
                    total = total + incoming[iz]
                value = w_ref[iz, cy, iy]
                level = pot_ref[iz, cy, iy] - centre
                level = level if groups == 1 else jnp.concatenate([level] * groups, 1)
                total = total + level * value
                if step == 0:
                    total = total * (1.0 / half_width)
                else:
                    total = total * (2.0 / half_width) - before_ref[iz, cy, iy]
                result[cy, iz, iy] = total
        incoming = fold_last(product[cy][20 * nodes :], nodes, cells)

    if step < 2:
        next_ref, down_ref, up_ref = refs
        for (cy, iz, iy), value in result.items():
            next_ref[iz, cy, iy] = value
        up = outgoing(high_ref, low_ref, [result[cy_count - 1, iz, iy] for iz in range(4) for iy in range(4)], cells)
        for iz in range(4):
            down_ref[iz] = result[0, iz, 0]
            up_ref[iz] = up[iz]
        return

    out_ref, held, sems = refs
    parts_x, _, _, layer, thickness = out_ref.shape
    group = lanes // cells
    sources = []
    for h in range(groups):
        rows = [
            jnp.concatenate([result[cy, iz, iy][:, h * lanes : (h + 1) * lanes] for iz in range(4)], 1)
            for cy in range(cy_count)
            for iy in range(4)
        ]
        sources += list(two_parts(jnp.concatenate(rows, 0)))
    ordered = dot(jnp.concatenate(sources, 0), order_ref[...])
    size = 4 * cy_count * nodes
    for h in range(groups):
        value = ordered[2 * h * size : (2 * h + 1) * size] + ordered[(2 * h + 1) * size : (2 * h + 2) * size]
        for y in range(4 * cy_count):
            for s in range(group):
                part = value[y * nodes : (y + 1) * nodes, s * thickness : (s + 1) * thickness]
                held[y // second, h * group + s, pl.ds(y % second, nodes, stride=second), :] = part
    copies = [
        pltpu.make_async_copy(held.at[:, :, pl.ds(px * layer, layer), :], out_ref.at[px], sems.at[px])
        for px in range(parts_x)
    ]
    for copy in copies:
        copy.start()
    for copy in copies:
        copy.wait()


def margin_kernel(filtered_ref, block_ref, out_ref):
    states = out_ref.shape[1]
    layer = filtered_ref.shape[0] // states
    rows = [filtered_ref[pl.ds(n, states, stride=layer), :].astype(bf16) for n in range(layer)]
    out_ref[...] = lax.dot_general(
        block_ref[...], jnp.concatenate(rows, 1), (((1,), (1,)), ((), ())), preferred_element_type=f32
    )


def shifted(value, axis, steps):
    count = lax.axis_size(axis)
    return lax.ppermute(value, axis, [(source, (source + steps) % count) for source in range(count)])


def local(span, potential, cell_matrix, block):
    states, first, second, thickness = span.shape
    block_count = block.shape[0]
    parts_x, parts_q, parts_r = (lax.axis_size(axis) for axis in ("px", "pq", "pr"))
    members = parts_x * parts_r
    mine = states // members
    layer = first * second
    nodes = parts_x * first
    cells = thickness // 4
    cy_count = parts_r * second // 4
    width = mine * cells
    rows = PADDED * nodes

    order, spread = lane_orders(lanes // cells, thickness)
    high, low = pl.pallas_call(
        matrix_kernel,
        out_shape=[jax.ShapeDtypeStruct((rows, rows), bf16)] * 2,
        in_specs=[whole] * 2,
        out_specs=[whole] * 2,
        compiler_params=params,
        name="assemble",
    )(cell_matrix, jnp.asarray(selections(nodes)))

    levels = jnp.broadcast_to(potential.reshape(1, 1, layer, thickness), (members, 1, layer, thickness))
    raw = jnp.concatenate([span.reshape(members, mine, layer, thickness), levels], 1)
    raw = lax.all_to_all(raw, ("px", "pr"), 0, 0, tiled=True)
    raw = raw.reshape(parts_x, parts_r, mine + 1, layer, thickness)

    field = jax.ShapeDtypeStruct((4, cy_count, 4, nodes, width), f32)
    message = jax.ShapeDtypeStruct((4, nodes, width), f32)
    field_levels = jax.ShapeDtypeStruct((4, cy_count, 4, nodes, lanes), f32)
    w, levels, down, up = pl.pallas_call(
        functools.partial(to_cells_kernel, cells, second),
        out_shape=[field, field_levels, message, message],
        in_specs=[anywhere] + [whole] * 4,
        out_specs=[whole] * 4,
        scratch_shapes=[
            pltpu.VMEM((parts_r, mine + 1, parts_x * layer, thickness), f32),
            pltpu.SemaphoreType.DMA((parts_x,)),
        ],
        compiler_params=params,
        name="to_cells",
    )(raw, jnp.asarray(order), jnp.asarray(spread), high, low)

    before = None
    for step in range(3):
        halo = shifted(down, "pq", -1)
        given = shifted(up, "pq", 1)
        operands = [w, levels, high, low, halo, given]
        if step > 0:
            operands.append(before)
        if step < 2:
            before, (w, down, up) = w, pl.pallas_call(
                functools.partial(apply_kernel, cells, second, step),
                out_shape=[field, message, message],
                in_specs=[whole] * len(operands),
                out_specs=[whole] * 3,
                compiler_params=params,
                name="apply",
            )(*operands)
        else:
            operands.append(jnp.asarray(np.ascontiguousarray(order.T)))
            filtered = pl.pallas_call(
                functools.partial(apply_kernel, cells, second, step),
                out_shape=jax.ShapeDtypeStruct((parts_x, parts_r, mine, layer, thickness), f32),
                in_specs=[whole] * len(operands),
                out_specs=anywhere,
                scratch_shapes=[
                    pltpu.VMEM((parts_r, mine, parts_x * layer, thickness), f32),
                    pltpu.SemaphoreType.DMA((parts_x,)),
                ],
                compiler_params=params,
                name="apply_last",
            )(*operands)

    filtered = filtered.reshape(members, mine, layer, thickness)
    filtered = lax.all_to_all(filtered, ("px", "pr"), 0, 0, tiled=True)
    partial = pl.pallas_call(
        margin_kernel,
        out_shape=jax.ShapeDtypeStruct((block_count, states), f32),
        in_specs=[whole] * 2,
        out_specs=whole,
        compiler_params=params,
        name="margin",
    )(filtered.reshape(states * layer, thickness), block.reshape(block_count, layer * thickness))

    parts_y = parts_q * parts_r
    tile_rows, tile_cols = states // parts_x, block_count // parts_y
    tiles = partial.reshape(parts_y, tile_cols, parts_x, tile_rows).transpose(2, 0, 3, 1)
    tiles = tiles.reshape(parts_x * parts_y, -1, min(lanes, tile_rows * tile_cols))
    tiles = lax.all_to_all(tiles, ("px", "pq", "pr"), 0, 0, tiled=True)
    margin = tiles.sum(0).reshape(tile_rows, tile_cols)
    return filtered.reshape(span.shape), margin


def solution(mesh):
    parts_x, parts_y = mesh.devices.shape
    parts_r = 4 if parts_x * 4 * 4 <= 64 else 2
    finer = Mesh(mesh.devices.reshape(parts_x, parts_y // parts_r, parts_r), ("px", "pq", "pr"))
    py = ("pq", "pr")
    in_specs = (P(None, "px", py, None), P("px", py, None), P(), P(None, "px", py, None))
    out_specs = (P(None, "px", py, None), P("px", py))
    return jax.shard_map(local, mesh=finer, in_specs=in_specs, out_specs=out_specs, check_vma=False)
```

time: 276 us -> 70.8 us (0.26); the launches traced: 272 us -> 70.3 us
  waiting for transfers between devices: 183 us -> 38.1 us
  local copies, waits for them, and re-layouts: 30.4 us -> 4.35 us
  between operations: 15.2 us -> 0.77 us
  matrix products: 13.6 us -> 0 us
  other arithmetic: 8.73 us -> 1.96 us
  Pallas kernels: 0 us -> 5.81 us
    psum x1 -> x0, waiting for transfers between devices: 118 us -> none  [local(): total = lax.psum(partial_margin, ('px', 'py'))]
    ppermute x12 -> x6, waiting for transfers between devices: 65.2 us -> 13.2 us  [shifted(): lax.ppermute(value, axis, [(source, (source + steps) % count) for source...]
    all_to_all x0 -> x3, waiting for transfers between devices: none -> 24.9 us  [the longest x1 9.26 us: local(): raw = lax.all_to_all(raw, ('px', 'pr'), 0, 0, tiled=True)]
    dot_general x4 -> x0, matrix products: 13.6 us -> none  [the longest x3 12.6 us: cell_products(): jnp.einsum('ij,sjc->sic', cell_matrix, flat_cells, precision=lax.Precisio...]
    ppermute x12 -> x6, starting transfers between devices: 21.1 us -> 7.8 us  [shifted(): lax.ppermute(value, axis, [(source, (source + steps) % count) for source...]
    all_to_all x0 -> x3, starting transfers between devices: none -> 11.5 us  [the longest x1 5.3 us: local(): raw = lax.all_to_all(raw, ('px', 'pr'), 0, 0, tiled=True)]
    transpose x9 -> x1, local copies, waits for them, and re-layouts: 9.37 us -> 0.23 us  [local(): partial.reshape(parts_y, tile_cols, parts_x, tile_rows)]
    transpose x18 -> x0, other arithmetic: 5.91 us -> none  [the longest x3 2.39 us: cell_products(): cell_values = jnp.transpose(sectioned, (6, 5, 3, 1, 4, 2, 0))]
  transfers between devices with their start and end apart: 13 -> 9, of which waited for: 12 -> 9; matrix products, arithmetic and copies ran while one was open for 2% -> 1% of each run, Pallas kernels for 0% -> 1%
where the time goes in v1:
time: 70.8 us; the launch traced here: 70.3 us
  waiting for transfers between devices  38.1 us (54%)
  starting transfers between devices  19.3 us (27%)
  Pallas kernels  5.81 us (8%)
  local copies, waits for them, and re-layouts  4.35 us (6%)
  other arithmetic  1.96 us (3%)
  between operations  0.77 us (1%)
    ppermute x6, waiting for transfers between devices, shifted(): lax.ppermute(value, axis, [(source, (source + steps) % count) for source...  13.2 us
    all_to_all x1, waiting for transfers between devices, local(): raw = lax.all_to_all(raw, ('px', 'pr'), 0, 0, tiled=True)  9.26 us
    all_to_all x1, waiting for transfers between devices, local(): filtered = lax.all_to_all(filtered, ('px', 'pr'), 0, 0, tiled=True)  8.35 us
    ppermute x6, starting transfers between devices, shifted(): lax.ppermute(value, axis, [(source, (source + steps) % count) for source...  7.8 us
    all_to_all x1, waiting for transfers between devices, local(): tiles = lax.all_to_all(tiles, ('px', 'pq', 'pr'), 0, 0, tiled=True)  7.32 us
    all_to_all x1, starting transfers between devices, local(): raw = lax.all_to_all(raw, ('px', 'pr'), 0, 0, tiled=True)  5.3 us
    pallas_call x3, Pallas kernels, local(): pl.pallas_call(functools.partial(apply_kernel, cells, second, step), out_...  3.86 us
    all_to_all x1, starting transfers between devices, local(): filtered = lax.all_to_all(filtered, ('px', 'pr'), 0, 0, tiled=True)  3.64 us
  transfers between devices with their start and end apart: 9, of which 9 were waited for; matrix products, arithmetic and copies ran while one was open for 1% of the time, Pallas kernels for 1%

profile of v1, /device:TPU:0, one launch (start us, length us, event | category | flops | bytes accessed | tf_op | source)
XLA Modules:
  0.0 70.3 jit_solution(7845407448598093510)
XLA Ops:
  0.6 0.7 broadcast_in_dim.8
  1.3 1.9 %pad_maximum_fusion = f32[8,9,16,128]{3,2,1,0:T(8,128)} fusion(f32[8,1,16,128]{3,2,1,0:T(8,128)S(1)} %broadcast_in_dim.8, f32[8,8,16,128]{3,2,1,0:T(8,128)} %bitcast.13), kind=kLoop, calls=%fused_computation | loop fusion | flops 147456 | bytes 1179648 | tf_op jit(solution)/shard_map/concatenate | solution.py:282
  3.3 5.3 %all-to-all-start = ((f32[8,9,16,128]{3,2,1,0:T(8,128)}), f32[8,9,16,128]{3,2,1,0:T(8,128)S(1)}, u32[]{:S(2)}, u32[]{:S(2)}) async-start(f32[8,9,16,128]{3,2,1,0:T(8,128)} %pad_maximum_fusion), calls=%async_computation | async-start | bytes 1179648 | tf_op jit(solution)/shard_map/all_to_all | solution.py:283
  9.3 9.3 %all-to-all-done = f32[8,9,16,128]{3,2,1,0:T(8,128)S(1)} async-done(((f32[8,9,16,128]{3,2,1,0:T(8,128)}), f32[8,9,16,128]{3,2,1,0:T(8,128)S(1)}, u32[]{:S(2)}, u32[]{:S(2)}) %all-to-all-start) | async-done | bytes 589856 | tf_op jit(solution)/shard_map/all_to_all | solution.py:283
  18.5 0.8 %to_cells.1 = (f32[4,4,4,8,256]{4,3,2,1,0:T(8,128)S(1)}, f32[4,4,4,8,128]{4,3,2,1,0:T(8,128)S(1)}, f32[4,8,256]{2,1,0:T(8,128)S(1)}, f32[4,8,256]{2,1,0:T(8,128)S(1)}) custom-call(f32[2,4,9,16,128]{4,3,2,1,0:T(8,128)S(1)} %bitcast.11, bf16[512,512]{1,0:T(8,128)(2,1)S(1)} %copy-done.1, bf16[128,512]{1,0:T(8,128)(2,1)S(1)} %copy-done.2, ...), custom_call_target="tpu_custom_call" | custom-call | tf_op jit(solution)/shard_map/to_cells/pallas_call | solution.py:289
  19.4 3.6 %collective-permute-start = (f32[4,8,256]{2,1,0:T(8,128)S(1)}, f32[4,8,256]{2,1,0:T(8,128)S(1)}, u32[]{:S(2)}, u32[]{:S(2)}) collective-permute-start(f32[4,8,256]{2,1,0:T(8,128)S(1)} %get-tuple-element.18), channel_id=1, source_target_pairs={{0,12},{4,0},{8,4},{12,8},{1,13},{5,1},{9,5},{13,9},{2,14},{6,2},{... | collective-permute-start | bytes 98312 | tf_op jit(solution)/shard_map/ppermute | solution.py:255
  23.0 1.6 %collective-permute-done.refs_4_ = f32[4,8,256]{2,1,0:T(8,128)S(1)} collective-permute-done((f32[4,8,256]{2,1,0:T(8,128)S(1)}, f32[4,8,256]{2,1,0:T(8,128)S(1)}, u32[]{:S(2)}, u32[]{:S(2)}) %collective-permute-start) | collective-permute-done | bytes 32800 | tf_op jit(solution)/shard_map/ppermute | solution.py:255
  24.6 4.1 %collective-permute-done.1.refs_5_ = f32[4,8,256]{2,1,0:T(8,128)S(1)} collective-permute-done((f32[4,8,256]{2,1,0:T(8,128)S(1)}, f32[4,8,256]{2,1,0:T(8,128)S(1)}, u32[]{:S(2)}, u32[]{:S(2)}) %collective-permute-start.1) | collective-permute-done | bytes 32800 | tf_op jit(solution)/shard_map/ppermute | solution.py:255
  28.7 1.0 %apply.2 = (f32[4,4,4,8,256]{4,3,2,1,0:T(8,128)S(1)}, f32[4,8,256]{2,1,0:T(8,128)S(1)}, f32[4,8,256]{2,1,0:T(8,128)S(1)}) custom-call(f32[4,4,4,8,256]{4,3,2,1,0:T(8,128)S(1)} %get-tuple-element.16.refs_0_.refs_6_, f32[4,4,4,8,128]{4,3,2,1,0:T(8,128)S(1)} %get-tuple-element.17.refs_1_, bf16[208,208]{1,0:T(8,128)(2,1)S(1)} %get-tuple-element.14.high_ref.refs_2_, ...), custom_call_target="tpu_custom_call" | custom-call | tf_op jit(solution)/shard_map/apply/pallas_call | solution.py:310
  29.8 2.0 %collective-permute-start.3 = (f32[4,8,256]{2,1,0:T(8,128)S(1)}, f32[4,8,256]{2,1,0:T(8,128)S(1)}, u32[]{:S(2)}, u32[]{:S(2)}) collective-permute-start(f32[4,8,256]{2,1,0:T(8,128)S(1)} %get-tuple-element.22), channel_id=1, source_target_pairs={{0,4},{4,8},{8,12},{12,0},{1,5},{5,9},{9,13},{13,1},{2,6},{6,10},{... | collective-permute-start | bytes 98312 | tf_op jit(solution)/shard_map/ppermute | solution.py:255
  31.8 2.0 %collective-permute-done.2.refs_4_ = f32[4,8,256]{2,1,0:T(8,128)S(1)} collective-permute-done((f32[4,8,256]{2,1,0:T(8,128)S(1)}, f32[4,8,256]{2,1,0:T(8,128)S(1)}, u32[]{:S(2)}, u32[]{:S(2)}) %collective-permute-start.2) | collective-permute-done | bytes 32800 | tf_op jit(solution)/shard_map/ppermute | solution.py:255
  33.8 1.8 %collective-permute-done.3.refs_5_ = f32[4,8,256]{2,1,0:T(8,128)S(1)} collective-permute-done((f32[4,8,256]{2,1,0:T(8,128)S(1)}, f32[4,8,256]{2,1,0:T(8,128)S(1)}, u32[]{:S(2)}, u32[]{:S(2)}) %collective-permute-start.3) | collective-permute-done | bytes 32800 | tf_op jit(solution)/shard_map/ppermute | solution.py:255
  35.6 1.0 %apply.3 = (f32[4,4,4,8,256]{4,3,2,1,0:T(8,128)S(1)}, f32[4,8,256]{2,1,0:T(8,128)S(1)}, f32[4,8,256]{2,1,0:T(8,128)S(1)}) custom-call(f32[4,4,4,8,256]{4,3,2,1,0:T(8,128)S(1)} %get-tuple-element.20.refs_0_.refs_6_, f32[4,4,4,8,128]{4,3,2,1,0:T(8,128)S(1)} %get-tuple-element.17.refs_1_, bf16[208,208]{1,0:T(8,128)(2,1)S(1)} %get-tuple-element.14.high_ref.refs_2_, ...), custom_call_target="tpu_custom_call" | custom-call | tf_op jit(solution)/shard_map/apply/pallas_call | solution.py:310
  36.6 2.0 %collective-permute-start.5 = (f32[4,8,256]{2,1,0:T(8,128)S(1)}, f32[4,8,256]{2,1,0:T(8,128)S(1)}, u32[]{:S(2)}, u32[]{:S(2)}) collective-permute-start(f32[4,8,256]{2,1,0:T(8,128)S(1)} %get-tuple-element.25), channel_id=1, source_target_pairs={{0,4},{4,8},{8,12},{12,0},{1,5},{5,9},{9,13},{13,1},{2,6},{6,10},{... | collective-permute-start | bytes 98312 | tf_op jit(solution)/shard_map/ppermute | solution.py:255
  38.7 1.9 %collective-permute-done.4.refs_4_ = f32[4,8,256]{2,1,0:T(8,128)S(1)} collective-permute-done((f32[4,8,256]{2,1,0:T(8,128)S(1)}, f32[4,8,256]{2,1,0:T(8,128)S(1)}, u32[]{:S(2)}, u32[]{:S(2)}) %collective-permute-start.4) | collective-permute-done | bytes 32800 | tf_op jit(solution)/shard_map/ppermute | solution.py:255
  40.6 1.9 %collective-permute-done.5.refs_5_ = f32[4,8,256]{2,1,0:T(8,128)S(1)} collective-permute-done((f32[4,8,256]{2,1,0:T(8,128)S(1)}, f32[4,8,256]{2,1,0:T(8,128)S(1)}, u32[]{:S(2)}, u32[]{:S(2)}) %collective-permute-start.5) | collective-permute-done | bytes 32800 | tf_op jit(solution)/shard_map/ppermute | solution.py:255
  42.4 1.9 %apply_last.1 = f32[2,4,8,16,128]{4,3,2,1,0:T(8,128)} custom-call(f32[4,4,4,8,256]{4,3,2,1,0:T(8,128)S(1)} %get-tuple-element.23.refs_0_, f32[4,4,4,8,128]{4,3,2,1,0:T(8,128)S(1)} %get-tuple-element.17.refs_1_, bf16[208,208]{1,0:T(8,128)(2,1)S(1)} %get-tuple-element.14.high_ref.refs_2_, bf16[208,208]{1,0:T(8,128)(2,1)S(1)} %get-tuple-element.15.low_ref.refs_3_, ...), custom_call_target="tpu_custom_call" | custom-call | tf_op jit(solution)/shard_map/apply_last/pallas_call | solution.py:320
  44.3 3.6 %all-to-all-start.1 = ((f32[8,8,16,128]{3,2,1,0:T(8,128)}), f32[8,8,16,128]{3,2,1,0:T(8,128)S(1)}, u32[]{:S(2)}, u32[]{:S(2)}) async-start(f32[8,8,16,128]{3,2,1,0:T(8,128)} %bitcast.3), calls=%async_computation.1 | async-start | bytes 1048576 | tf_op jit(solution)/shard_map/all_to_all | solution.py:334
  47.9 0.8 %reshape.40.block_ref = bf16[256,2048]{1,0:T(8,128)(2,1)S(1)} reshape(bf16[256,4,4,128]{3,2,1,0:T(4,128)(2,1)S(1)} %copy-done.5) | data formatting | bytes 2097152 | tf_op jit(solution)/shard_map/reshape | solution.py:342
  48.8 8.4 %all-to-all-done.1 = f32[8,8,16,128]{3,2,1,0:T(8,128)S(1)} async-done(((f32[8,8,16,128]{3,2,1,0:T(8,128)}), f32[8,8,16,128]{3,2,1,0:T(8,128)S(1)}, u32[]{:S(2)}, u32[]{:S(2)}) %all-to-all-start.1) | async-done | bytes 524320 | tf_op jit(solution)/shard_map/all_to_all | solution.py:334
  58.0 0.8 %reshape.42 = f32[32,4,128]{2,1,0:T(4,128)} reshape(f32[2,16,32,16]{3,2,1,0:T(8,128)S(1)} %copy.10) | data formatting | bytes 131072 | tf_op jit(solution)/shard_map/reshape | solution.py:347
  58.8 2.6 %all-to-all-start.2 = ((f32[32,4,128]{2,1,0:T(4,128)}), f32[32,4,128]{2,1,0:T(4,128)S(1)}, u32[]{:S(2)}, u32[]{:S(2)}) async-start(f32[32,4,128]{2,1,0:T(4,128)} %reshape.42), calls=%async_computation.2 | async-start | bytes 131072 | tf_op jit(solution)/shard_map/all_to_all | solution.py:348
  61.4 7.3 %all-to-all-done.2 = f32[32,4,128]{2,1,0:T(4,128)S(1)} async-done(((f32[32,4,128]{2,1,0:T(4,128)}), f32[32,4,128]{2,1,0:T(4,128)S(1)}, u32[]{:S(2)}, u32[]{:S(2)}) %all-to-all-start.2) | async-done | bytes 65568 | tf_op jit(solution)/shard_map/all_to_all | solution.py:348
  69.5 0.8 %copy.13 = f32[64,4,4,128]{3,2,1,0:T(4,128)} copy(f32[64,4,4,128]{3,2,1,0:T(4,128)S(1)} %bitcast.10) | data formatting | bytes 1048576
  (22 shorter events, 2.5 us)
Async XLA Ops:
  3.2 5.3 %copy-start.3 = (bf16[2,208,125]{2,1,0:T(8,128)(2,1)S(1)}, bf16[2,208,125]{2,1,0:T(8,128)(2,1)}, u32[]{:S(2)}) copy-start(bf16[2,208,125]{2,1,0:T(8,128)(2,1)} %constant.10.clone.select_ref) | copy-start | bytes 312004
  3.2 5.3 %copy-start.4 = (f32[125,125]{1,0:T(8,128)S(1)}, f32[125,125]{1,0:T(8,128)}, u32[]{:S(2)}) copy-start(f32[125,125]{1,0:T(8,128)} %cell_ref.1) | copy-start | bytes 187504
  3.3 15.3 %copy-start.1 = (bf16[512,512]{1,0:T(8,128)(2,1)S(1)}, bf16[512,512]{1,0:T(8,128)(2,1)}, u32[]{:S(2)}) copy-start(bf16[512,512]{1,0:T(8,128)(2,1)} %constant.11.clone.order_ref) | copy-start | bytes 1572868
  3.3 15.3 %all-to-all-start = ((f32[8,9,16,128]{3,2,1,0:T(8,128)}), f32[8,9,16,128]{3,2,1,0:T(8,128)S(1)}, u32[]{:S(2)}, u32[]{:S(2)}) async-start(f32[8,9,16,128]{3,2,1,0:T(8,128)} %pad_maximum_fusion), calls=%async_computation | async-start | bytes 1179648 | tf_op jit(solution)/shard_map/all_to_all | solution.py:283
  8.6 10.0 %copy-start.2 = (bf16[128,512]{1,0:T(8,128)(2,1)S(1)}, bf16[128,512]{1,0:T(8,128)(2,1)}, u32[]{:S(2)}) copy-start(bf16[128,512]{1,0:T(8,128)(2,1)} %constant.12.clone.spread_ref) | copy-start | bytes 393220
  19.4 5.2 %collective-permute-start = (f32[4,8,256]{2,1,0:T(8,128)S(1)}, f32[4,8,256]{2,1,0:T(8,128)S(1)}, u32[]{:S(2)}, u32[]{:S(2)}) collective-permute-start(f32[4,8,256]{2,1,0:T(8,128)S(1)} %get-tuple-element.18), channel_id=1, source_target_pairs={{0,12},{4,0},{8,4},{12,8},{1,13},{5,1},{9,5},{13,9},{2,14},{6,2},{... | collective-permute-start | bytes 98312 | tf_op jit(solution)/shard_map/ppermute | solution.py:255
  23.0 5.7 %collective-permute-start.1 = (f32[4,8,256]{2,1,0:T(8,128)S(1)}, f32[4,8,256]{2,1,0:T(8,128)S(1)}, u32[]{:S(2)}, u32[]{:S(2)}) collective-permute-start(f32[4,8,256]{2,1,0:T(8,128)S(1)} %get-tuple-element.19), channel_id=1, source_target_pairs={{0,4},{4,8},{8,12},{12,0},{1,5},{5,9},{9,13},{13,1},{2,6},{6,10},{... | collective-permute-start | bytes 98312 | tf_op jit(solution)/shard_map/ppermute | solution.py:255
  29.7 4.1 %collective-permute-start.2 = (f32[4,8,256]{2,1,0:T(8,128)S(1)}, f32[4,8,256]{2,1,0:T(8,128)S(1)}, u32[]{:S(2)}, u32[]{:S(2)}) collective-permute-start(f32[4,8,256]{2,1,0:T(8,128)S(1)} %get-tuple-element.21), channel_id=1, source_target_pairs={{0,12},{4,0},{8,4},{12,8},{1,13},{5,1},{9,5},{13,9},{2,14},{6,2},{... | collective-permute-start | bytes 98312 | tf_op jit(solution)/shard_map/ppermute | solution.py:255
  29.8 5.7 %collective-permute-start.3 = (f32[4,8,256]{2,1,0:T(8,128)S(1)}, f32[4,8,256]{2,1,0:T(8,128)S(1)}, u32[]{:S(2)}, u32[]{:S(2)}) collective-permute-start(f32[4,8,256]{2,1,0:T(8,128)S(1)} %get-tuple-element.22), channel_id=1, source_target_pairs={{0,4},{4,8},{8,12},{12,0},{1,5},{5,9},{9,13},{13,1},{2,6},{6,10},{... | collective-permute-start | bytes 98312 | tf_op jit(solution)/shard_map/ppermute | solution.py:255
  35.6 6.8 %copy-start = (bf16[512,512]{1,0:T(8,128)(2,1)S(1)}, bf16[512,512]{1,0:T(8,128)(2,1)}, u32[]{:S(2)}) copy-start(bf16[512,512]{1,0:T(8,128)(2,1)} %constant.13.clone.refs_7_) | copy-start | bytes 1572868
  36.6 4.0 %collective-permute-start.4 = (f32[4,8,256]{2,1,0:T(8,128)S(1)}, f32[4,8,256]{2,1,0:T(8,128)S(1)}, u32[]{:S(2)}, u32[]{:S(2)}) collective-permute-start(f32[4,8,256]{2,1,0:T(8,128)S(1)} %get-tuple-element.24), channel_id=1, source_target_pairs={{0,12},{4,0},{8,4},{12,8},{1,13},{5,1},{9,5},{13,9},{2,14},{6,2},{... | collective-permute-start | bytes 98312 | tf_op jit(solution)/shard_map/ppermute | solution.py:255
  36.6 5.8 %collective-permute-start.5 = (f32[4,8,256]{2,1,0:T(8,128)S(1)}, f32[4,8,256]{2,1,0:T(8,128)S(1)}, u32[]{:S(2)}, u32[]{:S(2)}) collective-permute-start(f32[4,8,256]{2,1,0:T(8,128)S(1)} %get-tuple-element.25), channel_id=1, source_target_pairs={{0,4},{4,8},{8,12},{12,0},{1,5},{5,9},{9,13},{13,1},{2,6},{6,10},{... | collective-permute-start | bytes 98312 | tf_op jit(solution)/shard_map/ppermute | solution.py:255
  44.3 3.7 %copy-start.5 = (bf16[256,4,4,128]{3,2,1,0:T(4,128)(2,1)S(1)}, bf16[256,4,4,128]{3,2,1,0:T(4,128)(2,1)}, u32[]{:S(2)}) copy-start(bf16[256,4,4,128]{3,2,1,0:T(4,128)(2,1)} %param.11) | copy-start | bytes 3145732
  44.3 12.8 %all-to-all-start.1 = ((f32[8,8,16,128]{3,2,1,0:T(8,128)}), f32[8,8,16,128]{3,2,1,0:T(8,128)S(1)}, u32[]{:S(2)}, u32[]{:S(2)}) async-start(f32[8,8,16,128]{3,2,1,0:T(8,128)} %bitcast.3), calls=%async_computation.1 | async-start | bytes 1048576 | tf_op jit(solution)/shard_map/all_to_all | solution.py:334
  58.8 9.9 %all-to-all-start.2 = ((f32[32,4,128]{2,1,0:T(4,128)}), f32[32,4,128]{2,1,0:T(4,128)S(1)}, u32[]{:S(2)}, u32[]{:S(2)}) async-start(f32[32,4,128]{2,1,0:T(4,128)} %reshape.42), calls=%async_computation.2 | async-start | bytes 131072 | tf_op jit(solution)/shard_map/all_to_all | solution.py:348

commit v2 on v1

--- a/solution.py
+++ b/solution.py
@@ -105,22 +105,26 @@
     return fold_last(three_products(high_ref[rows, cols], low_ref[rows, cols], stacked), nodes, cells)
 
 
-def to_cells_kernel(cells, second, raw_ref, order_ref, spread_ref, high_ref, low_ref, w_ref, pot_ref, down_ref, up_ref, held, sems):
-    parts_x, parts_y, count = raw_ref.shape[:3]
-    states = count - 1
-    layer = raw_ref.shape[3]
-    copies = [
-        pltpu.make_async_copy(raw_ref.at[px], held.at[:, :, pl.ds(px * layer, layer), :], sems.at[px])
-        for px in range(parts_x)
-    ]
+def rows_of(raw_ref, held, sems):
+    layer = raw_ref.shape[-2]
+    copies = []
+    for px in range(raw_ref.shape[0]):
+        target = held.at[(slice(None),) * (len(held.shape) - 2) + (pl.ds(px * layer, layer), slice(None))]
+        copies.append(pltpu.make_async_copy(raw_ref.at[px], target, sems.at[px]))
     for copy in copies:
         copy.start()
     for copy in copies:
         copy.wait()
-    nodes = parts_x * layer // second
+
+
+def to_cells_kernel(cells, second, raw_ref, order_ref, high_ref, low_ref, w_ref, message_ref, held, sems):
+    rows_of(raw_ref, held, sems)
+    parts_y, states = held.shape[:2]
+    nodes = held.shape[2] // second
     rows_y = parts_y * second
     group = lanes // cells
     groups = states // group
+    size = rows_y * nodes
 
     def gathered(state):
         rows = [held[y // second, state, pl.ds(y % second, nodes, stride=second), :] for y in range(rows_y)]
@@ -130,10 +134,6 @@
     for h in range(groups):
         sources += list(two_parts(jnp.concatenate([gathered(h * group + s) for s in range(group)], 1)))
     ordered = dot(jnp.concatenate(sources, 0), order_ref[...])
-    high, low = two_parts(gathered(states))
-    potential = dot(jnp.concatenate([high, low], 0), spread_ref[...])
-    size = rows_y * nodes
-    potential = potential[:size] + potential[size:]
     values = [ordered[2 * h * size : (2 * h + 1) * size] + ordered[(2 * h + 1) * size : (2 * h + 2) * size] for h in range(groups)]
 
     def block(cy, iz, iy):
@@ -144,20 +144,32 @@
     for cy in range(rows_y // 4):
         for iz in range(4):
             for iy in range(4):
-                start = (4 * cy + iy) * nodes
                 w_ref[iz, cy, iy] = block(cy, iz, iy)
-                pot_ref[iz, cy, iy] = potential[start : start + nodes, iz * lanes : (iz + 1) * lanes]
     last = rows_y // 4 - 1
     up = outgoing(high_ref, low_ref, [block(last, iz, iy) for iz in range(4) for iy in range(4)], cells)
     for iz in range(4):
-        down_ref[iz] = block(0, iz, 0)
-        up_ref[iz] = up[iz]
-
-
-def apply_kernel(cells, second, step, *refs):
+        message_ref[iz] = block(0, iz, 0)
+        message_ref[4 + iz] = up[iz]
+
+
+def levels_kernel(second, raw_ref, spread_ref, levels_ref, held, sems):
+    rows_of(raw_ref, held, sems)
+    parts_y = held.shape[0]
+    nodes = held.shape[1] // second
+    rows = [held[y // second, pl.ds(y % second, nodes, stride=second), :] for y in range(parts_y * second)]
+    high, low = two_parts(jnp.concatenate(rows, 0))
+    spread = dot(high, spread_ref[...]) + dot(low, spread_ref[...])
+    for y in range(parts_y * second):
+        for iz in range(4):
+            part = spread[y * nodes : (y + 1) * nodes, iz * lanes : (iz + 1) * lanes]
+            levels_ref[iz, y // 4, y % 4] = part - centre
+
+
+def apply_kernel(cells, second, paired, step, *refs):
     refs = list(refs)
-    w_ref, pot_ref, high_ref, low_ref, halo_ref, from_ref = refs[:6]
-    del refs[:6]
+    w_ref, levels_ref, high_ref, low_ref, halo_ref = refs[:5]
+    del refs[:5]
+    from_ref = halo_ref if paired else refs.pop(0)
     before_ref = refs.pop(0) if step > 0 else None
     order_ref = refs.pop(0) if step == 2 else None
     cy_count, nodes, width = w_ref.shape[1], w_ref.shape[3], w_ref.shape[4]
@@ -178,7 +190,7 @@
     edge = jnp.concatenate(edge + [roll_cells(edge[0], cells, True), jnp.zeros((nodes, width), f32)], 0)
     tail = slice(20 * nodes, PADDED * nodes)
     edge = fold_last(three_products(high_ref[tail, tail], low_ref[tail, tail], edge), nodes, cells)
-    incoming = [edge[iz] + from_ref[iz] for iz in range(4)]
+    incoming = [edge[iz] + from_ref[from_ref.shape[0] - 4 + iz] for iz in range(4)]
 
     result = {}
     for cy in range(cy_count):
@@ -192,7 +204,7 @@
                 if iy == 0:
                     total = total + incoming[iz]
                 value = w_ref[iz, cy, iy]
-                level = pot_ref[iz, cy, iy] - centre
+                level = levels_ref[iz, cy, iy]
                 level = level if groups == 1 else jnp.concatenate([level] * groups, 1)
                 total = total + level * value
                 if step == 0:
@@ -203,13 +215,13 @@
         incoming = fold_last(product[cy][20 * nodes :], nodes, cells)
 
     if step < 2:
-        next_ref, down_ref, up_ref = refs
+        next_ref, message_ref = refs
         for (cy, iz, iy), value in result.items():
             next_ref[iz, cy, iy] = value
         up = outgoing(high_ref, low_ref, [result[cy_count - 1, iz, iy] for iz in range(4) for iy in range(4)], cells)
         for iz in range(4):
-            down_ref[iz] = result[0, iz, 0]
-            up_ref[iz] = up[iz]
+            message_ref[iz] = result[0, iz, 0]
+            message_ref[4 + iz] = up[iz]
         return
 
     out_ref, held, sems = refs
@@ -241,13 +253,31 @@
         copy.wait()
 
 
-def margin_kernel(filtered_ref, block_ref, out_ref):
-    states = out_ref.shape[1]
+def margin_kernel(filtered_ref, block_ref, tiles_ref, copy_ref, sem):
+    copy = pltpu.make_async_copy(filtered_ref, copy_ref, sem)
+    copy.start()
+    parts_x, group_rows, width = tiles_ref.shape
+    groups = block_ref.shape[0] // group_rows
+    tile_rows = width // groups
+    states = parts_x * tile_rows
     layer = filtered_ref.shape[0] // states
     rows = [filtered_ref[pl.ds(n, states, stride=layer), :].astype(bf16) for n in range(layer)]
-    out_ref[...] = lax.dot_general(
+    product = lax.dot_general(
         block_ref[...], jnp.concatenate(rows, 1), (((1,), (1,)), ((), ())), preferred_element_type=f32
     )
+    for px in range(parts_x):
+        columns = slice(px * tile_rows, (px + 1) * tile_rows)
+        tiles_ref[px] = jnp.concatenate(
+            [product[g * group_rows : (g + 1) * group_rows, columns] for g in range(groups)], 1
+        )
+    copy.wait()
+
+
+def sum_kernel(tiles_ref, out_ref):
+    total = jnp.sum(tiles_ref[...], axis=0)
+    tile_rows = out_ref.shape[1]
+    groups = total.shape[1] // tile_rows
+    out_ref[...] = jnp.concatenate([total[:, g * tile_rows : (g + 1) * tile_rows] for g in range(groups)], 0)
 
 
 def shifted(value, axis, steps):
@@ -278,81 +308,100 @@
         name="assemble",
     )(cell_matrix, jnp.asarray(selections(nodes)))
 
-    levels = jnp.broadcast_to(potential.reshape(1, 1, layer, thickness), (members, 1, layer, thickness))
-    raw = jnp.concatenate([span.reshape(members, mine, layer, thickness), levels], 1)
-    raw = lax.all_to_all(raw, ("px", "pr"), 0, 0, tiled=True)
-    raw = raw.reshape(parts_x, parts_r, mine + 1, layer, thickness)
+    raw = lax.all_to_all(span.reshape(members, mine, layer, thickness), ("px", "pr"), 0, 0, tiled=True)
+    levels = jnp.broadcast_to(potential.reshape(1, layer, thickness), (members, layer, thickness))
+    levels = lax.all_to_all(levels, ("px", "pr"), 0, 0, tiled=True)
 
     field = jax.ShapeDtypeStruct((4, cy_count, 4, nodes, width), f32)
-    message = jax.ShapeDtypeStruct((4, nodes, width), f32)
-    field_levels = jax.ShapeDtypeStruct((4, cy_count, 4, nodes, lanes), f32)
-    w, levels, down, up = pl.pallas_call(
+    message_shape = jax.ShapeDtypeStruct((8, nodes, width), f32)
+    sems = pltpu.SemaphoreType.DMA((parts_x,))
+    w, message = pl.pallas_call(
         functools.partial(to_cells_kernel, cells, second),
-        out_shape=[field, field_levels, message, message],
-        in_specs=[anywhere] + [whole] * 4,
-        out_specs=[whole] * 4,
-        scratch_shapes=[
-            pltpu.VMEM((parts_r, mine + 1, parts_x * layer, thickness), f32),
-            pltpu.SemaphoreType.DMA((parts_x,)),
-        ],
+        out_shape=[field, message_shape],
+        in_specs=[anywhere] + [whole] * 3,
+        out_specs=[whole] * 2,
+        scratch_shapes=[pltpu.VMEM((parts_r, mine, parts_x * layer, thickness), f32), sems],
         compiler_params=params,
         name="to_cells",
-    )(raw, jnp.asarray(order), jnp.asarray(spread), high, low)
+    )(raw.reshape(parts_x, parts_r, mine, layer, thickness), jnp.asarray(order), high, low)
+    levels = pl.pallas_call(
+        functools.partial(levels_kernel, second),
+        out_shape=jax.ShapeDtypeStruct((4, cy_count, 4, nodes, lanes), f32),
+        in_specs=[anywhere, whole],
+        out_specs=whole,
+        scratch_shapes=[pltpu.VMEM((parts_r, parts_x * layer, thickness), f32), sems],
+        compiler_params=params,
+        name="levels",
+    )(levels.reshape(parts_x, parts_r, layer, thickness), jnp.asarray(spread))
 
     before = None
+    paired = parts_q == 2
     for step in range(3):
-        halo = shifted(down, "pq", -1)
-        given = shifted(up, "pq", 1)
-        operands = [w, levels, high, low, halo, given]
+        operands = [w, levels, high, low]
+        if paired:
+            operands.append(shifted(message, "pq", 1))
+        else:
+            operands += [shifted(message[:4], "pq", -1), shifted(message[4:], "pq", 1)]
         if step > 0:
             operands.append(before)
+        kernel = functools.partial(apply_kernel, cells, second, paired, step)
         if step < 2:
-            before, (w, down, up) = w, pl.pallas_call(
-                functools.partial(apply_kernel, cells, second, step),
-                out_shape=[field, message, message],
+            before, (w, message) = w, pl.pallas_call(
+                kernel,
+                out_shape=[field, message_shape],
                 in_specs=[whole] * len(operands),
-                out_specs=[whole] * 3,
+                out_specs=[whole] * 2,
                 compiler_params=params,
                 name="apply",
             )(*operands)
         else:
             operands.append(jnp.asarray(np.ascontiguousarray(order.T)))
             filtered = pl.pallas_call(
-                functools.partial(apply_kernel, cells, second, step),
+                kernel,
                 out_shape=jax.ShapeDtypeStruct((parts_x, parts_r, mine, layer, thickness), f32),
                 in_specs=[whole] * len(operands),
                 out_specs=anywhere,
-                scratch_shapes=[
-                    pltpu.VMEM((parts_r, mine, parts_x * layer, thickness), f32),
-                    pltpu.SemaphoreType.DMA((parts_x,)),
-                ],
+                scratch_shapes=[pltpu.VMEM((parts_r, mine, parts_x * layer, thickness), f32), sems],
                 compiler_params=params,
                 name="apply_last",
             )(*operands)
 
     filtered = filtered.reshape(members, mine, layer, thickness)
     filtered = lax.all_to_all(filtered, ("px", "pr"), 0, 0, tiled=True)
-    partial = pl.pallas_call(
+
+    parts_y = parts_q * parts_r
+    tile_rows, tile_cols = states // parts_x, block_count // parts_y
+    groups = min(tile_cols, lanes // tile_rows)
+    ordered = block.reshape(parts_y, groups, tile_cols // groups, layer * thickness)
+    ordered = ordered.transpose(1, 0, 2, 3).reshape(block_count, layer * thickness)
+    tiles, filtered = pl.pallas_call(
         margin_kernel,
-        out_shape=jax.ShapeDtypeStruct((block_count, states), f32),
+        out_shape=[
+            jax.ShapeDtypeStruct((parts_x, block_count // groups, groups * tile_rows), f32),
+            jax.ShapeDtypeStruct((states * layer, thickness), f32),
+        ],
         in_specs=[whole] * 2,
+        out_specs=[whole, anywhere],
+        scratch_shapes=[pltpu.SemaphoreType.DMA],
+        compiler_params=params,
+        name="margin",
+    )(filtered.reshape(states * layer, thickness), ordered)
+    tiles = tiles.reshape(parts_x * parts_y, tile_cols // groups, groups * tile_rows)
+    tiles = lax.all_to_all(tiles, ("px", "pq", "pr"), 0, 0, tiled=True)
+    margin = pl.pallas_call(
+        sum_kernel,
+        out_shape=jax.ShapeDtypeStruct((tile_cols, tile_rows), f32),
+        in_specs=[whole],
         out_specs=whole,
         compiler_params=params,
-        name="margin",
-    )(filtered.reshape(states * layer, thickness), block.reshape(block_count, layer * thickness))
-
-    parts_y = parts_q * parts_r
-    tile_rows, tile_cols = states // parts_x, block_count // parts_y
-    tiles = partial.reshape(parts_y, tile_cols, parts_x, tile_rows).transpose(2, 0, 3, 1)
-    tiles = tiles.reshape(parts_x * parts_y, -1, min(lanes, tile_rows * tile_cols))
-    tiles = lax.all_to_all(tiles, ("px", "pq", "pr"), 0, 0, tiled=True)
-    margin = tiles.sum(0).reshape(tile_rows, tile_cols)
-    return filtered.reshape(span.shape), margin
+        name="tile_sum",
+    )(tiles)
+    return filtered.reshape(span.shape), margin.T
 
 
 def solution(mesh):
     parts_x, parts_y = mesh.devices.shape
-    parts_r = 4 if parts_x * 4 * 4 <= 64 else 2
+    parts_r = min(parts_y // 2, 16 // parts_x)
     finer = Mesh(mesh.devices.reshape(parts_x, parts_y // parts_r, parts_r), ("px", "pq", "pr"))
     py = ("pq", "pr")
     in_specs = (P(None, "px", py, None), P("px", py, None), P(), P(None, "px", py, None))

time: 70.8 us -> 69.6 us (0.983)
  blocking collectives: 0 us -> 27.7 us
  waiting for transfers between devices: 38.1 us -> 15.7 us
  starting transfers between devices: 19.3 us -> 15.9 us
  local copies, waits for them, and re-layouts: 4.35 us -> 1.82 us
  other arithmetic: 1.96 us -> 0 us
  Pallas kernels: 5.81 us -> 7.15 us
    all_to_all x0 -> x2, blocking collectives: none -> 27.7 us  [the longest x1 16.2 us: local(): lax.all_to_all(span.reshape(members, mine, layer, thickness), ('px', 'pr'...]
    all_to_all x2 -> x1, waiting for transfers between devices: 16.6 us -> 1.91 us  [local(): levels = lax.all_to_all(levels, ('px', 'pr'), 0, 0, tiled=True)]
    ppermute x6 -> x3, waiting for transfers between devices: 13.2 us -> 5.14 us  [shifted(): lax.ppermute(value, axis, [(source, (source + steps) % count) for source...]
    all_to_all x2 -> x1, starting transfers between devices: 7.87 us -> 3.51 us  [local(): levels = lax.all_to_all(levels, ('px', 'pr'), 0, 0, tiled=True)]
    concatenate x1 -> x0, other arithmetic: 1.91 us -> none  [local(): jnp.concatenate([span.reshape(members, mine, layer, thickness), levels], 1)]
    unnamed x14, local copies, waits for them, and re-layouts: 1.5 us -> 0.04 us
    pallas_call x4 -> x6, Pallas kernels: 4.3 us -> 5.68 us  [the longest x2 1.98 us: local(): pl.pallas_call(kernel, out_shape=[field, message_shape], in_specs=[whole]...]
    all_to_all x1, starting transfers between devices: 3.64 us -> 4.8 us  [local(): filtered = lax.all_to_all(filtered, ('px', 'pr'), 0, 0, tiled=True)]
  transfers between devices with their start and end apart: 9 -> 5, of which waited for: 9 -> 4; matrix products, arithmetic and copies ran while one was open for 1% -> 2% of each run, Pallas kernels for 1% -> 3%
where the time goes in v2:
time: 69.6 us; the launch traced here: 69.1 us
  blocking collectives  27.7 us (40%)
  starting transfers between devices  15.9 us (23%)
  waiting for transfers between devices  15.7 us (23%)
  Pallas kernels  7.15 us (10%)
  local copies, waits for them, and re-layouts  1.82 us (3%)
  between operations  0.81 us (1%)
    all_to_all x1, blocking collectives, local(): lax.all_to_all(span.reshape(members, mine, layer, thickness), ('px', 'pr'...  16.2 us
    all_to_all x1, blocking collectives, local(): tiles = lax.all_to_all(tiles, ('px', 'pq', 'pr'), 0, 0, tiled=True)  11.5 us
    all_to_all x1, waiting for transfers between devices, local(): filtered = lax.all_to_all(filtered, ('px', 'pr'), 0, 0, tiled=True)  8.61 us
    ppermute x3, starting transfers between devices, shifted(): lax.ppermute(value, axis, [(source, (source + steps) % count) for source...  7.62 us
    ppermute x3, waiting for transfers between devices, shifted(): lax.ppermute(value, axis, [(source, (source + steps) % count) for source...  5.14 us
    all_to_all x1, starting transfers between devices, local(): filtered = lax.all_to_all(filtered, ('px', 'pr'), 0, 0, tiled=True)  4.8 us
    all_to_all x1, starting transfers between devices, local(): levels = lax.all_to_all(levels, ('px', 'pr'), 0, 0, tiled=True)  3.51 us
    pallas_call x2, Pallas kernels, local(): pl.pallas_call(kernel, out_shape=[field, message_shape], in_specs=[whole]...  1.98 us
  transfers between devices with their start and end apart: 5, of which 4 were waited for; matrix products, arithmetic and copies ran while one was open for 2% of the time, Pallas kernels for 3%

profile of v2, /device:TPU:0, one launch (start us, length us, event | category | flops | bytes accessed | tf_op | source)
XLA Modules:
  0.0 69.1 jit_solution(6198446926736640390)
XLA Ops:
  0.6 0.0 copy-start.3
  0.7 16.2 %all_to_all.20 = f32[16,4,16,128]{3,2,1,0:T(8,128)S(1)} all-to-all(f32[16,4,16,128]{3,2,1,0:T(8,128)} %bitcast.17), channel_id=1, replica_groups=mesh['px'=2,'pq'=2,'pr'=8] {'px','pr'}, dimensions={0} | all-to-all | bytes 1048576 | tf_op jit(solution)/shard_map/all_to_all | solution.py:311
  16.9 0.7 broadcast_in_dim.8
  17.5 3.5 %all-to-all-start.1 = ((f32[16,16,128]{2,1,0:T(8,128)}), f32[16,16,128]{2,1,0:T(8,128)S(1)}, u32[]{:S(2)}, u32[]{:S(2)}) async-start(f32[16,16,128]{2,1,0:T(8,128)} %broadcast_in_dim.8), calls=%async_computation.1 | async-start | bytes 262144 | tf_op jit(solution)/shard_map/all_to_all | solution.py:313
  21.1 0.7 assemble.1
  21.8 0.8 %to_cells.1 = (f32[4,8,4,8,128]{4,3,2,1,0:T(8,128)S(1)}, f32[8,8,128]{2,1,0:T(8,128)S(1)}) custom-call(f32[2,8,4,16,128]{4,3,2,1,0:T(8,128)S(1)} %bitcast.13, bf16[512,512]{1,0:T(8,128)(2,1)S(1)} %copy-done, bf16[208,208]{1,0:T(8,128)(2,1)S(1)} %get-tuple-element.12.high_ref.refs_2_, bf16[208,208]{1,0:T(8,128)(2,1)S(1)} %get-tuple-element.13.low_ref.refs_3_), custom_call_target="tpu_custom_call" | custom-call | tf_op jit(solution)/shard_map/to_cells/pallas_call | solution.py:318
  22.6 2.7 %collective-permute-start = (f32[8,8,128]{2,1,0:T(8,128)S(1)}, f32[8,8,128]{2,1,0:T(8,128)S(1)}, u32[]{:S(2)}, u32[]{:S(2)}) collective-permute-start(f32[8,8,128]{2,1,0:T(8,128)S(1)} %get-tuple-element.15), channel_id=1, source_target_pairs={{0,8},{8,0},{1,9},{9,1},{2,10},{10,2},{3,11},{11,3},{4,12},{12,4},... | collective-permute-start | bytes 98312 | tf_op jit(solution)/shard_map/ppermute | solution.py:285
  25.2 1.9 %all-to-all-done.1 = f32[16,16,128]{2,1,0:T(8,128)S(1)} async-done(((f32[16,16,128]{2,1,0:T(8,128)}), f32[16,16,128]{2,1,0:T(8,128)S(1)}, u32[]{:S(2)}, u32[]{:S(2)}) %all-to-all-start.1) | async-done | bytes 131104 | tf_op jit(solution)/shard_map/all_to_all | solution.py:313
  27.1 0.3 levels.1.refs_1_
  27.5 1.0 %apply.2 = (f32[4,8,4,8,128]{4,3,2,1,0:T(8,128)S(1)}, f32[8,8,128]{2,1,0:T(8,128)S(1)}) custom-call(f32[4,8,4,8,128]{4,3,2,1,0:T(8,128)S(1)} %get-tuple-element.14.refs_0_.refs_5_, f32[4,8,4,8,128]{4,3,2,1,0:T(8,128)S(1)} %levels.1.refs_1_, bf16[208,208]{1,0:T(8,128)(2,1)S(1)} %get-tuple-element.12.high_ref.refs_2_, ...), custom_call_target="tpu_custom_call" | custom-call | tf_op jit(solution)/shard_map/apply/pallas_call | solution.py:349
  28.5 2.7 %collective-permute-start.1 = (f32[8,8,128]{2,1,0:T(8,128)S(1)}, f32[8,8,128]{2,1,0:T(8,128)S(1)}, u32[]{:S(2)}, u32[]{:S(2)}) collective-permute-start(f32[8,8,128]{2,1,0:T(8,128)S(1)} %get-tuple-element.17), channel_id=1, source_target_pairs={{0,8},{8,0},{1,9},{9,1},{2,10},{10,2},{3,11},{11,3},{4,12},{12,4},... | collective-permute-start | bytes 98312 | tf_op jit(solution)/shard_map/ppermute | solution.py:285
  31.1 2.6 %collective-permute-done.1.refs_4_ = f32[8,8,128]{2,1,0:T(8,128)S(1)} collective-permute-done((f32[8,8,128]{2,1,0:T(8,128)S(1)}, f32[8,8,128]{2,1,0:T(8,128)S(1)}, u32[]{:S(2)}, u32[]{:S(2)}) %collective-permute-start.1) | collective-permute-done | bytes 32800 | tf_op jit(solution)/shard_map/ppermute | solution.py:285
  33.7 1.0 %apply.3 = (f32[4,8,4,8,128]{4,3,2,1,0:T(8,128)S(1)}, f32[8,8,128]{2,1,0:T(8,128)S(1)}) custom-call(f32[4,8,4,8,128]{4,3,2,1,0:T(8,128)S(1)} %get-tuple-element.16.refs_0_.refs_5_, f32[4,8,4,8,128]{4,3,2,1,0:T(8,128)S(1)} %levels.1.refs_1_, bf16[208,208]{1,0:T(8,128)(2,1)S(1)} %get-tuple-element.12.high_ref.refs_2_, ...), custom_call_target="tpu_custom_call" | custom-call | tf_op jit(solution)/shard_map/apply/pallas_call | solution.py:349
  34.7 2.3 %collective-permute-start.2 = (f32[8,8,128]{2,1,0:T(8,128)S(1)}, f32[8,8,128]{2,1,0:T(8,128)S(1)}, u32[]{:S(2)}, u32[]{:S(2)}) collective-permute-start(f32[8,8,128]{2,1,0:T(8,128)S(1)} %get-tuple-element.19), channel_id=1, source_target_pairs={{0,8},{8,0},{1,9},{9,1},{2,10},{10,2},{3,11},{11,3},{4,12},{12,4},... | collective-permute-start | bytes 98312 | tf_op jit(solution)/shard_map/ppermute | solution.py:285
  37.0 2.6 %collective-permute-done.2.refs_4_ = f32[8,8,128]{2,1,0:T(8,128)S(1)} collective-permute-done((f32[8,8,128]{2,1,0:T(8,128)S(1)}, f32[8,8,128]{2,1,0:T(8,128)S(1)}, u32[]{:S(2)}, u32[]{:S(2)}) %collective-permute-start.2) | collective-permute-done | bytes 32800 | tf_op jit(solution)/shard_map/ppermute | solution.py:285
  39.6 1.8 %apply_last.1 = f32[2,8,4,16,128]{4,3,2,1,0:T(8,128)} custom-call(f32[4,8,4,8,128]{4,3,2,1,0:T(8,128)S(1)} %get-tuple-element.18.refs_0_, f32[4,8,4,8,128]{4,3,2,1,0:T(8,128)S(1)} %levels.1.refs_1_, bf16[208,208]{1,0:T(8,128)(2,1)S(1)} %get-tuple-element.12.high_ref.refs_2_, bf16[208,208]{1,0:T(8,128)(2,1)S(1)} %get-tuple-element.13.low_ref.refs_3_, ...), custom_call_target="tpu_custom_call" | custom-call | tf_op jit(solution)/shard_map/apply_last/pallas_call | solution.py:359
  41.4 4.8 %all-to-all-start.2 = ((f32[16,4,16,128]{3,2,1,0:T(8,128)}), f32[16,4,16,128]{3,2,1,0:T(8,128)S(1)}, u32[]{:S(2)}, u32[]{:S(2)}) async-start(f32[16,4,16,128]{3,2,1,0:T(8,128)} %bitcast.4), calls=%async_computation.2 | async-start | bytes 1048576 | tf_op jit(solution)/shard_map/all_to_all | solution.py:370
  46.3 0.3 reshape.38
  46.6 0.6 copy.12
  47.1 0.3 reshape.39.block_ref
  47.4 8.6 %all-to-all-done.2 = f32[16,4,16,128]{3,2,1,0:T(8,128)S(1)} async-done(((f32[16,4,16,128]{3,2,1,0:T(8,128)}), f32[16,4,16,128]{3,2,1,0:T(8,128)S(1)}, u32[]{:S(2)}, u32[]{:S(2)}) %all-to-all-start.2) | async-done | bytes 524320 | tf_op jit(solution)/shard_map/all_to_all | solution.py:370
  56.0 0.8 %margin.1 = (f32[2,64,128]{2,1,0:T(8,128)S(1)}, f32[1024,128]{1,0:T(8,128)}) custom-call(f32[1024,128]{1,0:T(8,128)S(1)} %bitcast.12, bf16[256,2048]{1,0:T(8,128)(2,1)S(1)} %reshape.39.block_ref), custom_call_target="tpu_custom_call" | custom-call | tf_op jit(solution)/shard_map/margin/pallas_call | solution.py:377
  56.9 11.5 %all_to_all.21.tiles_ref = f32[32,4,128]{2,1,0:T(4,128)S(1)} all-to-all(f32[32,4,128]{2,1,0:T(4,128)S(1)} %bitcast.15), channel_id=1, replica_groups=mesh['px'=2,'pq'=2,'pr'=8] {'px','pq','pr'}, dimensions={0} | all-to-all | bytes 131072 | tf_op jit(solution)/shard_map/all_to_all | solution.py:390
  68.4 0.7 %tile_sum.1 = f32[16,32]{1,0:T(8,128)} custom-call(f32[32,4,128]{2,1,0:T(4,128)S(1)} %all_to_all.21.tiles_ref), custom_call_target="tpu_custom_call" | custom-call | tf_op jit(solution)/shard_map/tile_sum/pallas_call | solution.py:391
  (14 shorter events, 0.0 us)
Async XLA Ops:
  0.6 16.2 %copy-start.6 = (f32[4,4,128]{2,1,0:T(4,128)S(1)}, f32[4,4,128]{2,1,0:T(4,128)}, u32[]{:S(2)}) copy-start(f32[4,4,128]{2,1,0:T(4,128)} %param.9) | copy-start | bytes 24580
  0.6 20.4 %copy-start.3 = (bf16[2,208,125]{2,1,0:T(8,128)(2,1)S(1)}, bf16[2,208,125]{2,1,0:T(8,128)(2,1)}, u32[]{:S(2)}) copy-start(bf16[2,208,125]{2,1,0:T(8,128)(2,1)} %constant.8.clone.select_ref) | copy-start | bytes 312004
  0.7 20.4 %copy-start.4 = (f32[125,125]{1,0:T(8,128)S(1)}, f32[125,125]{1,0:T(8,128)}, u32[]{:S(2)}) copy-start(f32[125,125]{1,0:T(8,128)} %cell_ref.1) | copy-start | bytes 187504
  16.9 4.9 %copy-start = (bf16[512,512]{1,0:T(8,128)(2,1)S(1)}, bf16[512,512]{1,0:T(8,128)(2,1)}, u32[]{:S(2)}) copy-start(bf16[512,512]{1,0:T(8,128)(2,1)} %constant.9.clone.order_ref) | copy-start | bytes 1572868
  17.5 9.6 %all-to-all-start.1 = ((f32[16,16,128]{2,1,0:T(8,128)}), f32[16,16,128]{2,1,0:T(8,128)S(1)}, u32[]{:S(2)}, u32[]{:S(2)}) async-start(f32[16,16,128]{2,1,0:T(8,128)} %broadcast_in_dim.8), calls=%async_computation.1 | async-start | bytes 262144 | tf_op jit(solution)/shard_map/all_to_all | solution.py:313
  21.8 5.4 %copy-start.2 = (bf16[128,512]{1,0:T(8,128)(2,1)S(1)}, bf16[128,512]{1,0:T(8,128)(2,1)}, u32[]{:S(2)}) copy-start(bf16[128,512]{1,0:T(8,128)(2,1)} %constant.10.clone.spread_ref) | copy-start | bytes 393220
  22.6 4.9 %collective-permute-start = (f32[8,8,128]{2,1,0:T(8,128)S(1)}, f32[8,8,128]{2,1,0:T(8,128)S(1)}, u32[]{:S(2)}, u32[]{:S(2)}) collective-permute-start(f32[8,8,128]{2,1,0:T(8,128)S(1)} %get-tuple-element.15), channel_id=1, source_target_pairs={{0,8},{8,0},{1,9},{9,1},{2,10},{10,2},{3,11},{11,3},{4,12},{12,4},... | collective-permute-start | bytes 98312 | tf_op jit(solution)/shard_map/ppermute | solution.py:285
  28.5 5.2 %collective-permute-start.1 = (f32[8,8,128]{2,1,0:T(8,128)S(1)}, f32[8,8,128]{2,1,0:T(8,128)S(1)}, u32[]{:S(2)}, u32[]{:S(2)}) collective-permute-start(f32[8,8,128]{2,1,0:T(8,128)S(1)} %get-tuple-element.17), channel_id=1, source_target_pairs={{0,8},{8,0},{1,9},{9,1},{2,10},{10,2},{3,11},{11,3},{4,12},{12,4},... | collective-permute-start | bytes 98312 | tf_op jit(solution)/shard_map/ppermute | solution.py:285
  33.7 5.9 %copy-start.1 = (bf16[512,512]{1,0:T(8,128)(2,1)S(1)}, bf16[512,512]{1,0:T(8,128)(2,1)}, u32[]{:S(2)}) copy-start(bf16[512,512]{1,0:T(8,128)(2,1)} %constant.11.clone.refs_6_) | copy-start | bytes 1572868
  34.7 4.9 %collective-permute-start.2 = (f32[8,8,128]{2,1,0:T(8,128)S(1)}, f32[8,8,128]{2,1,0:T(8,128)S(1)}, u32[]{:S(2)}, u32[]{:S(2)}) collective-permute-start(f32[8,8,128]{2,1,0:T(8,128)S(1)} %get-tuple-element.19), channel_id=1, source_target_pairs={{0,8},{8,0},{1,9},{9,1},{2,10},{10,2},{3,11},{11,3},{4,12},{12,4},... | collective-permute-start | bytes 98312 | tf_op jit(solution)/shard_map/ppermute | solution.py:285
  41.4 4.8 %copy-start.5 = (bf16[256,4,4,128]{3,2,1,0:T(4,128)(2,1)S(1)}, bf16[256,4,4,128]{3,2,1,0:T(4,128)(2,1)}, u32[]{:S(2)}) copy-start(bf16[256,4,4,128]{3,2,1,0:T(4,128)(2,1)} %param.11) | copy-start | bytes 3145732
  41.4 14.6 %all-to-all-start.2 = ((f32[16,4,16,128]{3,2,1,0:T(8,128)}), f32[16,4,16,128]{3,2,1,0:T(8,128)S(1)}, u32[]{:S(2)}, u32[]{:S(2)}) async-start(f32[16,4,16,128]{3,2,1,0:T(8,128)} %bitcast.4), calls=%async_computation.2 | async-start | bytes 1048576 | tf_op jit(solution)/shard_map/all_to_all | solution.py:370

commit v3 on v0

v3 whole, which is shorter than its diff:
```python
import functools

import jax
import jax.numpy as jnp
import ml_dtypes
import numpy as np
from jax import lax
from jax.experimental import pallas as pl
from jax.experimental.pallas import tpu as pltpu
from jax.sharding import PartitionSpec as P

centre = 13.0
half_width = 9.0
lanes = 128
bf16 = jnp.bfloat16
f32 = jnp.float32
whole = pl.BlockSpec(memory_space=pltpu.VMEM)
anywhere = pl.BlockSpec(memory_space=pl.ANY)
params = pltpu.CompilerParams(vmem_limit_bytes=48 * 2**20)

BLOCKS = (
    [(iz, iy) for iz in range(4) for iy in range(4)]
    + [(4, iy) for iy in range(4)]
    + [(iz, 4) for iz in range(4)]
    + [(4, 4)]
)
PADDED = 26


def two_parts(value):
    high = value.astype(bf16)
    return high, (value - high.astype(f32)).astype(bf16)


def dot(a, b):
    return jnp.dot(a, b, preferred_element_type=f32)


def selections(first_nodes):
    cells = first_nodes // 4
    table = np.zeros((cells, PADDED * first_nodes, 125), np.float32)
    for cell in range(cells):
        for place, (jz, jy) in enumerate(BLOCKS):
            for jx in range(5):
                row = place * first_nodes + (4 * cell + jx) % first_nodes
                table[cell, row, (jx * 5 + jy) * 5 + jz] = 1.0
    return table.astype(ml_dtypes.bfloat16)


def lane_orders(group, thickness):
    cells = thickness // 4
    order = np.zeros((group, cells, 4, 4, group, cells), np.float32)
    spread = np.zeros((cells, 4, 4, group, cells), np.float32)
    for iz in range(4):
        for cell in range(cells):
            for state in range(group):
                order[state, cell, iz, iz, state, cell] = 1.0
                spread[cell, iz, iz, state, cell] = 1.0
    order = order.reshape(group * thickness, 4 * group * cells)
    spread = spread.reshape(thickness, 4 * group * cells)
    return order.astype(ml_dtypes.bfloat16), spread.astype(ml_dtypes.bfloat16)


def matrix_kernel(cell_ref, select_ref, high_ref, low_ref):
    rest = cell_ref[...]
    total = jnp.zeros(high_ref.shape, f32)
    for _ in range(3):
        part = rest.astype(bf16)
        rest = rest - part.astype(f32)
        for cell in range(select_ref.shape[0]):
            chosen = select_ref[cell]
            left = dot(chosen, part).astype(bf16)
            total = total + lax.dot_general(left, chosen, (((1,), (1,)), ((), ())), preferred_element_type=f32)
    high_ref[...], low_ref[...] = two_parts(total)


def roll_cells(value, cells, forward):
    out = []
    place = lax.broadcasted_iota(jnp.int32, (value.shape[0], lanes), 1) % cells
    for start in range(0, value.shape[1], lanes):
        part = value[:, start : start + lanes]
        if forward:
            moved = jnp.where(place == cells - 1, pltpu.roll(part, cells - 1, 1), pltpu.roll(part, lanes - 1, 1))
        else:
            moved = jnp.where(place == 0, pltpu.roll(part, lanes - cells + 1, 1), pltpu.roll(part, 1, 1))
        out.append(moved)
    return out[0] if len(out) == 1 else jnp.concatenate(out, 1)


def three_products(high, low, value):
    value_high, value_low = two_parts(value)
    return dot(high, value_high) + (dot(low, value_high) + dot(high, value_low))


def fold_last(rows, nodes, cells):
    parts = [rows[iz * nodes : (iz + 1) * nodes] for iz in range(5)]
    parts[0] = parts[0] + roll_cells(parts[4], cells, False)
    return parts[:4]


def roll_rows(rows, cells):
    return [roll_cells(row, cells, True) for row in rows]


def send_edges(high_ref, low_ref, value, down_ref, up_ref, cells):
    nodes = down_ref.shape[1]
    own = [value[iz, iy] for iz in range(4) for iy in range(4)]
    stacked = jnp.concatenate(own + roll_rows(own[:4], cells), 0)
    rows, cols = slice(20 * nodes, PADDED * nodes), slice(0, 20 * nodes)
    up = fold_last(three_products(high_ref[rows, cols], low_ref[rows, cols], stacked), nodes, cells)
    for iz in range(4):
        down_ref[iz] = value[iz, 0]
        up_ref[iz] = up[iz]


def start_all(copies):
    for copy in copies:
        copy.start()


def wait_all(copies):
    for copy in copies:
        copy.wait()


def to_cells_kernel(cells, second, parts_x, *refs):
    span_ref, other_refs = refs[0], refs[1:parts_x]
    order_ref, high_ref, low_ref, w_ref, down_ref, up_ref, held, sems = refs[parts_x:]
    me = lax.axis_index("px")
    states, rows = held.shape[:2]
    layer = rows // parts_x
    nodes = rows // second
    copies = []
    for step in range(parts_x):
        place = lax.rem(me + (parts_x - step), parts_x)
        target = held.at[:, pl.ds(pl.multiple_of(place * layer, layer), layer), :]
        source = span_ref.at[pl.ds(me * states, states)] if step == 0 else other_refs[step - 1]
        copies.append(pltpu.make_async_copy(source, target, sems.at[step]))
    start_all(copies)
    wait_all(copies)
    group = lanes // cells
    groups = states // group
    size = second * nodes

    def gathered(state):
        return jnp.concatenate([held[state, pl.ds(y, nodes, stride=second), :] for y in range(second)], 0)

    sources = []
    for h in range(groups):
        sources += list(two_parts(jnp.concatenate([gathered(h * group + s) for s in range(group)], 1)))
    ordered = dot(jnp.concatenate(sources, 0), order_ref[...])
    values = [ordered[2 * h * size : (2 * h + 1) * size] + ordered[(2 * h + 1) * size : (2 * h + 2) * size] for h in range(groups)]
    value = {}
    for iz in range(4):
        for iy in range(4):
            parts = [part[iy * nodes : (iy + 1) * nodes, iz * lanes : (iz + 1) * lanes] for part in values]
            value[iz, iy] = parts[0] if groups == 1 else jnp.concatenate(parts, 1)
            w_ref[iz, iy] = value[iz, iy]
    send_edges(high_ref, low_ref, value, down_ref, up_ref, cells)


def levels_kernel(second, parts_x, *refs):
    spread_ref, levels_ref, held = refs[parts_x:]
    me = lax.axis_index("px")
    layer = held.shape[0] // parts_x
    nodes = held.shape[0] // second
    for step in range(parts_x):
        place = lax.rem(me + (parts_x - step), parts_x)
        held[pl.ds(pl.multiple_of(place * layer, layer), layer), :] = refs[step][...]
    rows = [held[pl.ds(y, nodes, stride=second), :] for y in range(second)]
    high, low = two_parts(jnp.concatenate(rows, 0))
    spread = dot(high, spread_ref[...]) + dot(low, spread_ref[...])
    for y in range(second):
        for iz in range(4):
            levels_ref[iz, y] = spread[y * nodes : (y + 1) * nodes, iz * lanes : (iz + 1) * lanes] - centre


def scale_of(step):
    return 1.0 / half_width if step == 0 else 2.0 / half_width


def inner_kernel(cells, step, *refs):
    w_ref, levels_ref, high_ref, low_ref = refs[:4]
    before_ref, out_ref = refs[4] if step > 0 else None, refs[-1]
    nodes, width = w_ref.shape[2:]
    groups = width // lanes
    inside = 20 * nodes
    own = [w_ref[iz, iy] for iz in range(4) for iy in range(4)]
    stacked = jnp.concatenate(own + roll_rows(own[:4], cells), 0)
    product = three_products(high_ref[:inside, :inside], low_ref[:inside, :inside], stacked)

    edge = [w_ref[iz, 0] for iz in range(4)]
    edge = jnp.concatenate(edge + roll_rows(edge[:1], cells) + [jnp.zeros((nodes, width), f32)], 0)
    tail = slice(inside, PADDED * nodes)
    edge = fold_last(three_products(high_ref[tail, tail], low_ref[tail, tail], edge), nodes, cells)
    for iz in range(4):
        for iy in range(4):
            start = (iz * 4 + iy) * nodes
            total = product[start : start + nodes]
            if iz == 0:
                start = (16 + iy) * nodes
                total = total + roll_cells(product[start : start + nodes], cells, False)
            if iy == 0:
                total = total + edge[iz]
            level = levels_ref[iz, iy]
            level = level if groups == 1 else jnp.concatenate([level] * groups, 1)
            total = (total + level * w_ref[iz, iy]) * scale_of(step)
            out_ref[iz, iy] = total if step == 0 else total - before_ref[iz, iy]


def finish(cells, step, inner_ref, halo_ref, given_ref, high_ref, low_ref):
    nodes, width = inner_ref.shape[2:]
    inside = 20 * nodes
    halo = [halo_ref[iz] for iz in range(4)]
    halo = jnp.concatenate(halo + roll_rows(halo[:1], cells) + [jnp.zeros((nodes, width), f32)], 0)
    product = three_products(high_ref[:inside, inside:], low_ref[:inside, inside:], halo)
    result = {}
    for iz in range(4):
        for iy in range(4):
            start = (iz * 4 + iy) * nodes
            total = product[start : start + nodes]
            if iz == 0:
                start = (16 + iy) * nodes
                total = total + roll_cells(product[start : start + nodes], cells, False)
            if iy == 0:
                total = total + given_ref[iz]
            result[iz, iy] = inner_ref[iz, iy] + total * scale_of(step)
    return result


def finish_kernel(cells, step, inner_ref, halo_ref, given_ref, high_ref, low_ref, next_ref, down_ref, up_ref):
    value = finish(cells, step, inner_ref, halo_ref, given_ref, high_ref, low_ref)
    for (iz, iy), part in value.items():
        next_ref[iz, iy] = part
    send_edges(high_ref, low_ref, value, down_ref, up_ref, cells)


def from_cells_kernel(cells, second, parts_x, *refs):
    inner_ref, halo_ref, given_ref, high_ref, low_ref, order_ref = refs[:6]
    out_refs = refs[6 : 6 + parts_x]
    held, sems = refs[6 + parts_x :]
    value = finish(cells, 2, inner_ref, halo_ref, given_ref, high_ref, low_ref)
    states, rows, thickness = held.shape
    layer = rows // parts_x
    nodes = rows // second
    group = lanes // cells
    groups = states // group
    size = second * nodes
    sources = []
    for h in range(groups):
        parts = [
            jnp.concatenate([value[iz, iy][:, h * lanes : (h + 1) * lanes] for iz in range(4)], 1)
            for iy in range(4)
        ]
        sources += list(two_parts(jnp.concatenate(parts, 0)))
    ordered = dot(jnp.concatenate(sources, 0), order_ref[...])
    for h in range(groups):
        part = ordered[2 * h * size : (2 * h + 1) * size] + ordered[(2 * h + 1) * size : (2 * h + 2) * size]
        for y in range(second):
            for s in range(group):
                lines = part[y * nodes : (y + 1) * nodes, s * thickness : (s + 1) * thickness]
                held[h * group + s, pl.ds(y, nodes, stride=second), :] = lines
    me = lax.axis_index("px")
    copies = []
    for step in range(parts_x):
        place = lax.rem(me + step, parts_x)
        source = held.at[:, pl.ds(pl.multiple_of(place * layer, layer), layer), :]
        copies.append(pltpu.make_async_copy(source, out_refs[step], sems.at[step]))
    start_all(copies)
    wait_all(copies)


def margin_kernel(parts_x, *refs):
    part_refs, block_ref = refs[:parts_x], refs[parts_x]
    tiles_ref, filtered_ref, sems = refs[parts_x + 1 :]
    me = lax.axis_index("px")
    states = filtered_ref.shape[0] // parts_x
    layer = filtered_ref.shape[1]
    owners = [lax.rem(me + (parts_x - step), parts_x) for step in range(parts_x)]
    copies = [
        pltpu.make_async_copy(part_refs[step], filtered_ref.at[pl.ds(owners[step] * states, states)], sems.at[step])
        for step in range(parts_x)
    ]
    start_all(copies)
    rows = []
    for part_ref in part_refs:
        flat = part_ref.reshape(states * layer, part_ref.shape[2])
        rows.append([flat[pl.ds(n, states, stride=layer), :].astype(bf16) for n in range(layer)])
    stacked = jnp.concatenate([jnp.concatenate([part[n] for part in rows], 0) for n in range(layer)], 1)
    product = lax.dot_general(
        block_ref[...], stacked, (((1,), (1,)), ((), ())), preferred_element_type=f32
    )
    group_rows = tiles_ref.shape[1]
    groups = block_ref.shape[0] // group_rows
    for step in range(parts_x):
        columns = slice(step * states, (step + 1) * states)
        tiles_ref[owners[step]] = jnp.concatenate(
            [product[g * group_rows : (g + 1) * group_rows, columns] for g in range(groups)], 1
        )
    wait_all(copies)


def sum_kernel(tiles_ref, out_ref):
    total = jnp.sum(tiles_ref[...], axis=0)
    tile_rows = out_ref.shape[1]
    groups = total.shape[1] // tile_rows
    out_ref[...] = jnp.concatenate([total[:, g * tile_rows : (g + 1) * tile_rows] for g in range(groups)], 0)


def shifted(value, axis, steps):
    count = lax.axis_size(axis)
    return lax.ppermute(value, axis, [(source, (source + steps) % count) for source in range(count)])


def kernel_call(body, outs, operands, name, scratch=(), in_specs=None, out_specs=None):
    many = isinstance(outs, list)
    return pl.pallas_call(
        body,
        out_shape=outs,
        in_specs=in_specs or [whole] * len(operands),
        out_specs=out_specs or ([whole] * len(outs) if many else whole),
        scratch_shapes=list(scratch),
        compiler_params=params,
        name=name,
    )(*operands)


def local(span, potential, cell_matrix, block):
    states, first, second, thickness = span.shape
    block_count = block.shape[0]
    parts_x, parts_y = lax.axis_size("px"), lax.axis_size("py")
    me = lax.axis_index("px")
    mine = states // parts_x
    layer = first * second
    nodes = parts_x * first
    cells = thickness // 4
    width = mine * cells
    rows = PADDED * nodes
    others = range(1, parts_x)

    order, spread = lane_orders(lanes // cells, thickness)
    matrix = jax.ShapeDtypeStruct((rows, rows), bf16)
    field = jax.ShapeDtypeStruct((4, 4, nodes, width), f32)
    message = jax.ShapeDtypeStruct((4, nodes, width), f32)
    part = jax.ShapeDtypeStruct((mine, layer, thickness), f32)
    sems = pltpu.SemaphoreType.DMA((parts_x,))
    held = [pltpu.VMEM((mine, parts_x * layer, thickness), f32), sems]

    span_rows = span.reshape(states, layer, thickness)
    received = []
    for step in others:
        chunk = lax.dynamic_slice_in_dim(span_rows, lax.rem(me + step, parts_x) * mine, mine, 0)
        received.append(shifted(chunk, "px", step))
    level_rows = potential.reshape(layer, thickness)
    level_parts = [level_rows] + [shifted(level_rows, "px", step) for step in others]

    high, low = kernel_call(
        matrix_kernel, [matrix] * 2, [cell_matrix, jnp.asarray(selections(nodes))], "assemble"
    )
    w, down, up = kernel_call(
        functools.partial(to_cells_kernel, cells, second, parts_x),
        [field, message, message],
        [span_rows] + received + [jnp.asarray(order), high, low],
        "to_cells",
        scratch=held,
        in_specs=[anywhere] * parts_x + [whole] * 3,
    )
    levels = kernel_call(
        functools.partial(levels_kernel, second, parts_x),
        jax.ShapeDtypeStruct((4, 4, nodes, lanes), f32),
        level_parts + [jnp.asarray(spread)],
        "levels",
        scratch=[pltpu.VMEM((parts_x * layer, thickness), f32)],
    )

    before = None
    for step in range(3):
        halo = shifted(down, "py", -1)
        given = shifted(up, "py", 1)
        operands = [w, levels, high, low] + ([before] if step > 0 else [])
        inner = kernel_call(functools.partial(inner_kernel, cells, step), field, operands, "inner")
        operands = [inner, halo, given, high, low]
        if step < 2:
            before, (w, down, up) = w, kernel_call(
                functools.partial(finish_kernel, cells, step), [field, message, message], operands, "finish"
            )
        else:
            pieces = kernel_call(
                functools.partial(from_cells_kernel, cells, second, parts_x),
                [part] * parts_x,
                operands + [jnp.asarray(np.ascontiguousarray(order.T))],
                "from_cells",
                scratch=held,
                out_specs=[anywhere] * parts_x,
            )
    pieces = [pieces[0]] + [shifted(pieces[step], "px", step) for step in others]

    tile_rows, tile_cols = mine, block_count // parts_y
    groups = min(tile_cols, lanes // tile_rows)
    ordered = block.reshape(parts_y, groups, tile_cols // groups, layer * thickness)
    ordered = ordered.transpose(1, 0, 2, 3).reshape(block_count, layer * thickness)
    tiles, filtered = kernel_call(
        functools.partial(margin_kernel, parts_x),
        [
            jax.ShapeDtypeStruct((parts_x, block_count // groups, groups * tile_rows), f32),
            jax.ShapeDtypeStruct((states, layer, thickness), f32),
        ],
        pieces + [ordered],
        "margin",
        scratch=[sems],
        out_specs=[whole, anywhere],
    )
    tiles = tiles.reshape(parts_x * parts_y, tile_cols // groups, groups * tile_rows)
    tiles = lax.all_to_all(tiles, ("px", "py"), 0, 0, tiled=True)
    margin = kernel_call(sum_kernel, jax.ShapeDtypeStruct((tile_cols, tile_rows), f32), [tiles], "tile_sum")
    return filtered.reshape(span.shape), margin.T


def solution(mesh):
    in_specs = (P(None, "px", "py", None), P("px", "py", None), P(), P(None, "px", "py", None))
    out_specs = (P(None, "px", "py", None), P("px", "py"))
    return jax.shard_map(local, mesh=mesh, in_specs=in_specs, out_specs=out_specs, check_vma=False)
```

time: 276 us -> 54.5 us (0.20); the launches traced: 272 us -> 54.2 us
  waiting for transfers between devices: 183 us -> 20.7 us
  local copies, waits for them, and re-layouts: 30.4 us -> 4.06 us
  between operations: 15.2 us -> 0.79 us
  matrix products: 13.6 us -> 0 us
  starting transfers between devices: 21.2 us -> 11.5 us
  blocking collectives: 0 us -> 9.02 us
  other arithmetic: 8.73 us -> 0 us
  Pallas kernels: 0 us -> 8.16 us
    psum x1 -> x0, waiting for transfers between devices: 118 us -> none  [local(): total = lax.psum(partial_margin, ('px', 'py'))]
    ppermute x12 -> x9, waiting for transfers between devices: 65.2 us -> 20.7 us  [shifted(): lax.ppermute(value, axis, [(source, (source + steps) % count) for source...]
    dot_general x4 -> x0, matrix products: 13.6 us -> none  [the longest x3 12.6 us: cell_products(): jnp.einsum('ij,sjc->sic', cell_matrix, flat_cells, precision=lax.Precisio...]
    ppermute x12 -> x9, starting transfers between devices: 21.1 us -> 11.5 us  [shifted(): lax.ppermute(value, axis, [(source, (source + steps) % count) for source...]
    transpose x9 -> x0, local copies, waits for them, and re-layouts: 9.37 us -> none  [the longest x3 7.47 us: cell_products(): jnp.einsum('ij,sjc->sic', cell_matrix, flat_cells, precision=lax.Precisio...]
    all_to_all x0 -> x1, blocking collectives: none -> 9.02 us  [local(): tiles = lax.all_to_all(tiles, ('px', 'py'), 0, 0, tiled=True)]
    pallas_call x0 -> x11, Pallas kernels: none -> 8.16 us  [kernel_call(): pl.pallas_call(body, out_shape=outs, in_specs=in_specs or [whole] * len(o...]
    transpose x18 -> x0, other arithmetic: 5.91 us -> none  [the longest x3 2.39 us: cell_products(): cell_values = jnp.transpose(sectioned, (6, 5, 3, 1, 4, 2, 0))]
  transfers between devices with their start and end apart: 13 -> 9, of which waited for: 12 -> 8; matrix products, arithmetic and copies ran while one was open for 2% -> 2% of each run, Pallas kernels for 0% -> 5%
where the time goes in v3:
time: 54.5 us; the launch traced here: 54.2 us
  waiting for transfers between devices  20.7 us (38%)
  starting transfers between devices  11.5 us (21%)
  blocking collectives  9.02 us (17%)
  Pallas kernels  8.16 us (15%)
  local copies, waits for them, and re-layouts  4.06 us (7%)
  between operations  0.79 us (1%)
    ppermute x9, waiting for transfers between devices, shifted(): lax.ppermute(value, axis, [(source, (source + steps) % count) for source...  20.7 us
    ppermute x9, starting transfers between devices, shifted(): lax.ppermute(value, axis, [(source, (source + steps) % count) for source...  11.5 us
    all_to_all x1, blocking collectives, local(): tiles = lax.all_to_all(tiles, ('px', 'py'), 0, 0, tiled=True)  9.02 us
    pallas_call x11, Pallas kernels, kernel_call(): pl.pallas_call(body, out_shape=outs, in_specs=in_specs or [whole] * len(o...  8.16 us
    unnamed x16, local copies, waits for them, and re-layouts  1.91 us
  transfers between devices with their start and end apart: 9, of which 8 were waited for; matrix products, arithmetic and copies ran while one was open for 2% of the time, Pallas kernels for 5%

profile of v3, /device:TPU:0, one launch (start us, length us, event | category | flops | bytes accessed | tf_op | source)
XLA Modules:
  0.0 54.2 jit_solution(10143143944286376030)
XLA Ops:
  0.7 1.0 %constant_dynamic-slice_fusion = f32[32,16,128]{2,1,0:T(8,128)S(1)} fusion(f32[64,16,128]{2,1,0:T(8,128)} %bitcast.8, s32[]{:T(128)S(6)} %select_n.3), kind=kLoop, calls=%fused_computation.1 | loop fusion | bytes 524292 | tf_op jit(solution)/shard_map/dynamic_slice | solution.py:352
  2.2 0.8 %copy-done.5 = f32[125,125]{1,0:T(8,128)S(1)} copy-done((f32[125,125]{1,0:T(8,128)S(1)}, f32[125,125]{1,0:T(8,128)}, u32[]{:S(2)}) %copy-start.5) | copy-done | bytes 62524
  3.1 0.7 %assemble.1 = (bf16[208,208]{1,0:T(8,128)(2,1)S(1)}, bf16[208,208]{1,0:T(8,128)(2,1)S(1)}) custom-call(f32[125,125]{1,0:T(8,128)S(1)} %copy-done.5, bf16[2,208,125]{2,1,0:T(8,128)(2,1)S(1)} %copy-done.4), custom_call_target="tpu_custom_call" | custom-call | tf_op jit(solution)/shard_map/assemble/pallas_call | solution.py:317
  3.8 1.0 %copy-done.2 = bf16[512,512]{1,0:T(8,128)(2,1)S(1)} copy-done((bf16[512,512]{1,0:T(8,128)(2,1)S(1)}, bf16[512,512]{1,0:T(8,128)(2,1)}, u32[]{:S(2)}) %copy-start.2) | copy-done | bytes 524312
  4.8 0.9 %to_cells.1 = (f32[4,4,8,1024]{3,2,1,0:T(8,128)S(1)}, f32[4,8,1024]{2,1,0:T(8,128)S(1)}, f32[4,8,1024]{2,1,0:T(8,128)S(1)}) custom-call(f32[64,16,128]{2,1,0:T(8,128)S(1)} %bitcast.9, f32[32,16,128]{2,1,0:T(8,128)S(1)} %collective-permute-done.refs_1_, bf16[512,512]{1,0:T(8,128)(2,1)S(1)} %copy-done.2, ...), custom_call_target="tpu_custom_call" | custom-call | tf_op jit(solution)/shard_map/to_cells/pallas_call | solution.py:317
  5.7 6.6 %collective-permute-start.2 = (f32[4,8,1024]{2,1,0:T(8,128)S(1)}, f32[4,8,1024]{2,1,0:T(8,128)S(1)}, u32[]{:S(2)}, u32[]{:S(2)}) collective-permute-start(f32[4,8,1024]{2,1,0:T(8,128)S(1)} %get-tuple-element.20), channel_id=1, source_target_pairs={{0,15},{1,0},{2,1},{3,2},{4,3},{5,4},{6,5},{7,6},{8,7},{9,8},{10,9... | collective-permute-start | bytes 393224 | tf_op jit(solution)/shard_map/ppermute | solution.py:312
  12.5 1.0 %collective-permute-done.1.refs_1_ = f32[16,128]{1,0:T(8,128)S(1)} collective-permute-done((f32[16,128]{1,0:T(8,128)S(1)}, f32[16,128]{1,0:T(8,128)S(1)}, u32[]{:S(2)}, u32[]{:S(2)}) %collective-permute-start.1) | collective-permute-done | bytes 8224 | tf_op jit(solution)/shard_map/ppermute | solution.py:312
  13.6 0.7 %inner.3.inner_ref = f32[4,4,8,1024]{3,2,1,0:T(8,128)S(1)} custom-call(f32[4,4,8,1024]{3,2,1,0:T(8,128)S(1)} %get-tuple-element.19.refs_0_.refs_4_, f32[4,4,8,128]{3,2,1,0:T(8,128)S(1)} %levels.1.refs_1_, bf16[208,208]{1,0:T(8,128)(2,1)S(1)} %get-tuple-element.17.refs_3_.refs_2_.high_ref, bf16[208,208]{1,0:T(8,128)(2,1)S(1)} %get-tuple-element.18.refs_4_.refs_3_.low_ref), custom_call_target="tpu_custom_call" | custom-call | tf_op jit(solution)/shard_map/inner/pallas_call | solution.py:317
  14.3 1.4 %collective-permute-done.2.halo_ref = f32[4,8,1024]{2,1,0:T(8,128)S(1)} collective-permute-done((f32[4,8,1024]{2,1,0:T(8,128)S(1)}, f32[4,8,1024]{2,1,0:T(8,128)S(1)}, u32[]{:S(2)}, u32[]{:S(2)}) %collective-permute-start.2) | collective-permute-done | bytes 131104 | tf_op jit(solution)/shard_map/ppermute | solution.py:312
  15.7 5.9 %collective-permute-done.3.given_ref = f32[4,8,1024]{2,1,0:T(8,128)S(1)} collective-permute-done((f32[4,8,1024]{2,1,0:T(8,128)S(1)}, f32[4,8,1024]{2,1,0:T(8,128)S(1)}, u32[]{:S(2)}, u32[]{:S(2)}) %collective-permute-start.3) | collective-permute-done | bytes 131104 | tf_op jit(solution)/shard_map/ppermute | solution.py:312
  21.6 1.0 %finish.2 = (f32[4,4,8,1024]{3,2,1,0:T(8,128)S(1)}, f32[4,8,1024]{2,1,0:T(8,128)S(1)}, f32[4,8,1024]{2,1,0:T(8,128)S(1)}) custom-call(f32[4,4,8,1024]{3,2,1,0:T(8,128)S(1)} %inner.3.inner_ref, f32[4,8,1024]{2,1,0:T(8,128)S(1)} %collective-permute-done.2.halo_ref, f32[4,8,1024]{2,1,0:T(8,128)S(1)} %collective-permute-done.3.given_ref, ...), custom_call_target="tpu_custom_call" | custom-call | tf_op jit(solution)/shard_map/finish/pallas_call | solution.py:317
  22.8 1.8 %collective-permute-start.5 = (f32[4,8,1024]{2,1,0:T(8,128)S(1)}, f32[4,8,1024]{2,1,0:T(8,128)S(1)}, u32[]{:S(2)}, u32[]{:S(2)}) collective-permute-start(f32[4,8,1024]{2,1,0:T(8,128)S(1)} %get-tuple-element.24), channel_id=1, source_target_pairs={{0,1},{1,2},{2,3},{3,4},{4,5},{5,6},{6,7},{7,8},{8,9},{9,10},{10,1... | collective-permute-start | bytes 393224 | tf_op jit(solution)/shard_map/ppermute | solution.py:312
  24.6 0.6 %inner.4.inner_ref = f32[4,4,8,1024]{3,2,1,0:T(8,128)S(1)} custom-call(f32[4,4,8,1024]{3,2,1,0:T(8,128)S(1)} %get-tuple-element.22.refs_0_.refs_4_, f32[4,4,8,128]{3,2,1,0:T(8,128)S(1)} %levels.1.refs_1_, bf16[208,208]{1,0:T(8,128)(2,1)S(1)} %get-tuple-element.17.refs_3_.refs_2_.high_ref, bf16[208,208]{1,0:T(8,128)(2,1)S(1)} %get-tuple-element.18.refs_4_.refs_3_.low_ref, ...), custom_call_target="tpu_custom_call" | custom-call | tf_op jit(solution)/shard_map/inner/pallas_call | solution.py:317
  25.3 3.4 %collective-permute-done.4.halo_ref = f32[4,8,1024]{2,1,0:T(8,128)S(1)} collective-permute-done((f32[4,8,1024]{2,1,0:T(8,128)S(1)}, f32[4,8,1024]{2,1,0:T(8,128)S(1)}, u32[]{:S(2)}, u32[]{:S(2)}) %collective-permute-start.4) | collective-permute-done | bytes 131104 | tf_op jit(solution)/shard_map/ppermute | solution.py:312
  28.7 2.7 %collective-permute-done.5.given_ref = f32[4,8,1024]{2,1,0:T(8,128)S(1)} collective-permute-done((f32[4,8,1024]{2,1,0:T(8,128)S(1)}, f32[4,8,1024]{2,1,0:T(8,128)S(1)}, u32[]{:S(2)}, u32[]{:S(2)}) %collective-permute-start.5) | collective-permute-done | bytes 131104 | tf_op jit(solution)/shard_map/ppermute | solution.py:312
  31.3 1.0 %finish.3 = (f32[4,4,8,1024]{3,2,1,0:T(8,128)S(1)}, f32[4,8,1024]{2,1,0:T(8,128)S(1)}, f32[4,8,1024]{2,1,0:T(8,128)S(1)}) custom-call(f32[4,4,8,1024]{3,2,1,0:T(8,128)S(1)} %inner.4.inner_ref, f32[4,8,1024]{2,1,0:T(8,128)S(1)} %collective-permute-done.4.halo_ref, f32[4,8,1024]{2,1,0:T(8,128)S(1)} %collective-permute-done.5.given_ref, ...), custom_call_target="tpu_custom_call" | custom-call | tf_op jit(solution)/shard_map/finish/pallas_call | solution.py:317
  32.5 1.9 %collective-permute-start.7 = (f32[4,8,1024]{2,1,0:T(8,128)S(1)}, f32[4,8,1024]{2,1,0:T(8,128)S(1)}, u32[]{:S(2)}, u32[]{:S(2)}) collective-permute-start(f32[4,8,1024]{2,1,0:T(8,128)S(1)} %get-tuple-element.27), channel_id=1, source_target_pairs={{0,1},{1,2},{2,3},{3,4},{4,5},{5,6},{6,7},{7,8},{8,9},{9,10},{10,1... | collective-permute-start | bytes 393224 | tf_op jit(solution)/shard_map/ppermute | solution.py:312
  34.4 0.6 %inner.5.refs_0_ = f32[4,4,8,1024]{3,2,1,0:T(8,128)S(1)} custom-call(f32[4,4,8,1024]{3,2,1,0:T(8,128)S(1)} %get-tuple-element.25.refs_0_, f32[4,4,8,128]{3,2,1,0:T(8,128)S(1)} %levels.1.refs_1_, bf16[208,208]{1,0:T(8,128)(2,1)S(1)} %get-tuple-element.17.refs_3_.refs_2_.high_ref, bf16[208,208]{1,0:T(8,128)(2,1)S(1)} %get-tuple-element.18.refs_4_.refs_3_.low_ref, ...), custom_call_target="tpu_custom_call" | custom-call | tf_op jit(solution)/shard_map/inner/pallas_call | solution.py:317
  35.0 2.4 %collective-permute-done.6.refs_1_ = f32[4,8,1024]{2,1,0:T(8,128)S(1)} collective-permute-done((f32[4,8,1024]{2,1,0:T(8,128)S(1)}, f32[4,8,1024]{2,1,0:T(8,128)S(1)}, u32[]{:S(2)}, u32[]{:S(2)}) %collective-permute-start.6) | collective-permute-done | bytes 131104 | tf_op jit(solution)/shard_map/ppermute | solution.py:312
  37.4 3.6 %collective-permute-done.7.refs_2_ = f32[4,8,1024]{2,1,0:T(8,128)S(1)} collective-permute-done((f32[4,8,1024]{2,1,0:T(8,128)S(1)}, f32[4,8,1024]{2,1,0:T(8,128)S(1)}, u32[]{:S(2)}, u32[]{:S(2)}) %collective-permute-start.7) | collective-permute-done | bytes 131104 | tf_op jit(solution)/shard_map/ppermute | solution.py:312
  41.0 1.0 %from_cells.1 = (f32[32,16,128]{2,1,0:T(8,128)S(1)}, f32[32,16,128]{2,1,0:T(8,128)S(1)}) custom-call(f32[4,4,8,1024]{3,2,1,0:T(8,128)S(1)} %inner.5.refs_0_, f32[4,8,1024]{2,1,0:T(8,128)S(1)} %collective-permute-done.6.refs_1_, f32[4,8,1024]{2,1,0:T(8,128)S(1)} %collective-permute-done.7.refs_2_, ...), custom_call_target="tpu_custom_call" | custom-call | tf_op jit(solution)/shard_map/from_cells/pallas_call | solution.py:317
  43.6 0.9 %margin.1 = (f32[2,64,128]{2,1,0:T(8,128)S(1)}, f32[64,16,128]{2,1,0:T(8,128)}) custom-call(f32[32,16,128]{2,1,0:T(8,128)S(1)} %get-tuple-element.28.refs_0_, f32[32,16,128]{2,1,0:T(8,128)S(1)} %collective-permute-done.8.refs_1_, bf16[256,2048]{1,0:T(8,128)(2,1)S(1)} %reshape.25.refs_2_), custom_call_target="tpu_custom_call" | custom-call | tf_op jit(solution)/shard_map/margin/pallas_call | solution.py:317
  44.5 9.0 %all_to_all.5.tiles_ref = f32[32,4,128]{2,1,0:T(4,128)S(1)} all-to-all(f32[32,4,128]{2,1,0:T(4,128)S(1)} %bitcast.10), channel_id=1, replica_groups=mesh['px'=2,'py'=16] {'px','py'}, dimensions={0} | all-to-all | bytes 131072 | tf_op jit(solution)/shard_map/all_to_all | solution.py:414
  53.5 0.7 %tile_sum.1 = f32[16,32]{1,0:T(8,128)} custom-call(f32[32,4,128]{2,1,0:T(4,128)S(1)} %all_to_all.5.tiles_ref), custom_call_target="tpu_custom_call" | custom-call | tf_op jit(solution)/shard_map/tile_sum/pallas_call | solution.py:317
  (26 shorter events, 2.9 us)
Async XLA Ops:
  0.6 1.6 %copy-start.4 = (bf16[2,208,125]{2,1,0:T(8,128)(2,1)S(1)}, bf16[2,208,125]{2,1,0:T(8,128)(2,1)}, u32[]{:S(2)}) copy-start(bf16[2,208,125]{2,1,0:T(8,128)(2,1)} %constant.25.clone.select_ref) | copy-start | bytes 312004
  0.6 3.1 %copy-start = (f32[64,4,4,128]{3,2,1,0:T(4,128)S(1)}, f32[64,4,4,128]{3,2,1,0:T(4,128)}, u32[]{:S(2)}) copy-start(f32[64,4,4,128]{3,2,1,0:T(4,128)} %param.8) | copy-start | bytes 1572868
  1.7 2.0 %collective-permute-start = (f32[32,16,128]{2,1,0:T(8,128)S(1)}, f32[32,16,128]{2,1,0:T(8,128)S(1)}, u32[]{:S(2)}, u32[]{:S(2)}) collective-permute-start(f32[32,16,128]{2,1,0:T(8,128)S(1)} %constant_dynamic-slice_fusion), channel_id=1, source_target_pairs={{0,16},{16,0},{1,17},{17,1},{2,18},{18,2},{3,19},{19,3},{4,20},{20... | collective-permute-start | bytes 786440 | tf_op jit(solution)/shard_map/ppermute | solution.py:312
  2.2 0.8 %copy-start.5 = (f32[125,125]{1,0:T(8,128)S(1)}, f32[125,125]{1,0:T(8,128)}, u32[]{:S(2)}) copy-start(f32[125,125]{1,0:T(8,128)} %cell_ref.1) | copy-start | bytes 187504
  3.8 1.0 %copy-start.2 = (bf16[512,512]{1,0:T(8,128)(2,1)S(1)}, bf16[512,512]{1,0:T(8,128)(2,1)}, u32[]{:S(2)}) copy-start(bf16[512,512]{1,0:T(8,128)(2,1)} %constant.26.clone.refs_2_) | copy-start | bytes 1572868
  4.8 7.5 %copy-start.6 = (f32[4,4,128]{2,1,0:T(4,128)S(1)}, f32[4,4,128]{2,1,0:T(4,128)}, u32[]{:S(2)}) copy-start(f32[4,4,128]{2,1,0:T(4,128)} %param.9) | copy-start | bytes 24580
  4.8 8.6 %copy-start.3 = (bf16[128,512]{1,0:T(8,128)(2,1)S(1)}, bf16[128,512]{1,0:T(8,128)(2,1)}, u32[]{:S(2)}) copy-start(bf16[128,512]{1,0:T(8,128)(2,1)} %constant.27.clone.refs_2_) | copy-start | bytes 393220
  5.7 10.0 %collective-permute-start.2 = (f32[4,8,1024]{2,1,0:T(8,128)S(1)}, f32[4,8,1024]{2,1,0:T(8,128)S(1)}, u32[]{:S(2)}, u32[]{:S(2)}) collective-permute-start(f32[4,8,1024]{2,1,0:T(8,128)S(1)} %get-tuple-element.20), channel_id=1, source_target_pairs={{0,15},{1,0},{2,1},{3,2},{4,3},{5,4},{6,5},{7,6},{8,7},{9,8},{10,9... | collective-permute-start | bytes 393224 | tf_op jit(solution)/shard_map/ppermute | solution.py:312
  12.3 9.3 %collective-permute-start.3 = (f32[4,8,1024]{2,1,0:T(8,128)S(1)}, f32[4,8,1024]{2,1,0:T(8,128)S(1)}, u32[]{:S(2)}, u32[]{:S(2)}) collective-permute-start(f32[4,8,1024]{2,1,0:T(8,128)S(1)} %get-tuple-element.21), channel_id=1, source_target_pairs={{0,1},{1,2},{2,3},{3,4},{4,5},{5,6},{6,7},{7,8},{8,9},{9,10},{10,1... | collective-permute-start | bytes 393224 | tf_op jit(solution)/shard_map/ppermute | solution.py:312
  12.3 1.2 %collective-permute-start.1 = (f32[16,128]{1,0:T(8,128)S(1)}, f32[16,128]{1,0:T(8,128)S(1)}, u32[]{:S(2)}, u32[]{:S(2)}) collective-permute-start(f32[16,128]{1,0:T(8,128)S(1)} %bitcast.11), channel_id=1, source_target_pairs={{0,16},{16,0},{1,17},{17,1},{2,18},{18,2},{3,19},{19,3},{4,20},{20... | collective-permute-start | bytes 24584 | tf_op jit(solution)/shard_map/ppermute | solution.py:312
  22.5 6.1 %collective-permute-start.4 = (f32[4,8,1024]{2,1,0:T(8,128)S(1)}, f32[4,8,1024]{2,1,0:T(8,128)S(1)}, u32[]{:S(2)}, u32[]{:S(2)}) collective-permute-start(f32[4,8,1024]{2,1,0:T(8,128)S(1)} %get-tuple-element.23), channel_id=1, source_target_pairs={{0,15},{1,0},{2,1},{3,2},{4,3},{5,4},{6,5},{7,6},{8,7},{9,8},{10,9... | collective-permute-start | bytes 393224 | tf_op jit(solution)/shard_map/ppermute | solution.py:312
  22.8 8.6 %collective-permute-start.5 = (f32[4,8,1024]{2,1,0:T(8,128)S(1)}, f32[4,8,1024]{2,1,0:T(8,128)S(1)}, u32[]{:S(2)}, u32[]{:S(2)}) collective-permute-start(f32[4,8,1024]{2,1,0:T(8,128)S(1)} %get-tuple-element.24), channel_id=1, source_target_pairs={{0,1},{1,2},{2,3},{3,4},{4,5},{5,6},{6,7},{7,8},{8,9},{9,10},{10,1... | collective-permute-start | bytes 393224 | tf_op jit(solution)/shard_map/ppermute | solution.py:312
  32.3 5.1 %collective-permute-start.6 = (f32[4,8,1024]{2,1,0:T(8,128)S(1)}, f32[4,8,1024]{2,1,0:T(8,128)S(1)}, u32[]{:S(2)}, u32[]{:S(2)}) collective-permute-start(f32[4,8,1024]{2,1,0:T(8,128)S(1)} %get-tuple-element.26), channel_id=1, source_target_pairs={{0,15},{1,0},{2,1},{3,2},{4,3},{5,4},{6,5},{7,6},{8,7},{9,8},{10,9... | collective-permute-start | bytes 393224 | tf_op jit(solution)/shard_map/ppermute | solution.py:312
  32.5 8.6 %collective-permute-start.7 = (f32[4,8,1024]{2,1,0:T(8,128)S(1)}, f32[4,8,1024]{2,1,0:T(8,128)S(1)}, u32[]{:S(2)}, u32[]{:S(2)}) collective-permute-start(f32[4,8,1024]{2,1,0:T(8,128)S(1)} %get-tuple-element.27), channel_id=1, source_target_pairs={{0,1},{1,2},{2,3},{3,4},{4,5},{5,6},{6,7},{7,8},{8,9},{9,10},{10,1... | collective-permute-start | bytes 393224 | tf_op jit(solution)/shard_map/ppermute | solution.py:312
  34.4 6.7 %copy-start.1 = (bf16[512,512]{1,0:T(8,128)(2,1)S(1)}, bf16[512,512]{1,0:T(8,128)(2,1)}, u32[]{:S(2)}) copy-start(bf16[512,512]{1,0:T(8,128)(2,1)} %constant.28.clone.refs_5_) | copy-start | bytes 1572868
  35.0 7.1 %copy-start.7 = (bf16[256,4,4,128]{3,2,1,0:T(4,128)(2,1)S(1)}, bf16[256,4,4,128]{3,2,1,0:T(4,128)(2,1)}, u32[]{:S(2)}) copy-start(bf16[256,4,4,128]{3,2,1,0:T(4,128)(2,1)} %param.11) | copy-start | bytes 3145732
  42.0 1.6 %collective-permute-start.8 = (f32[32,16,128]{2,1,0:T(8,128)S(1)}, f32[32,16,128]{2,1,0:T(8,128)S(1)}, u32[]{:S(2)}, u32[]{:S(2)}) collective-permute-start(f32[32,16,128]{2,1,0:T(8,128)S(1)} %get-tuple-element.29), channel_id=1, source_target_pairs={{0,16},{16,0},{1,17},{17,1},{2,18},{18,2},{3,19},{19,3},{4,20},{20... | collective-permute-start | bytes 786440 | tf_op jit(solution)/shard_map/ppermute | solution.py:312

commit v4 on v3

--- a/solution.py
+++ b/solution.py
@@ -2,8 +2,6 @@
 
 import jax
 import jax.numpy as jnp
-import ml_dtypes
-import numpy as np
 from jax import lax
 from jax.experimental import pallas as pl
 from jax.experimental.pallas import tpu as pltpu
@@ -36,42 +34,68 @@
     return jnp.dot(a, b, preferred_element_type=f32)
 
 
-def selections(first_nodes):
-    cells = first_nodes // 4
-    table = np.zeros((cells, PADDED * first_nodes, 125), np.float32)
-    for cell in range(cells):
-        for place, (jz, jy) in enumerate(BLOCKS):
-            for jx in range(5):
-                row = place * first_nodes + (4 * cell + jx) % first_nodes
-                table[cell, row, (jx * 5 + jy) * 5 + jz] = 1.0
-    return table.astype(ml_dtypes.bfloat16)
-
-
-def lane_orders(group, thickness):
-    cells = thickness // 4
-    order = np.zeros((group, cells, 4, 4, group, cells), np.float32)
-    spread = np.zeros((cells, 4, 4, group, cells), np.float32)
-    for iz in range(4):
-        for cell in range(cells):
-            for state in range(group):
-                order[state, cell, iz, iz, state, cell] = 1.0
-                spread[cell, iz, iz, state, cell] = 1.0
-    order = order.reshape(group * thickness, 4 * group * cells)
-    spread = spread.reshape(thickness, 4 * group * cells)
-    return order.astype(ml_dtypes.bfloat16), spread.astype(ml_dtypes.bfloat16)
-
-
-def matrix_kernel(cell_ref, select_ref, high_ref, low_ref):
+def chosen(rows, cols, target):
+    row = lax.broadcasted_iota(jnp.int32, (rows, cols), 0)
+    col = lax.broadcasted_iota(jnp.int32, (rows, cols), 1)
+    return jnp.where(col == target(row), 1.0, 0.0).astype(bf16)
+
+
+def select_target(cell, nodes, row):
+    place, x = lax.div(row, nodes), lax.rem(row, nodes)
+    jx = lax.rem(x + (nodes - 4 * cell), nodes)
+    jz = jnp.where(place < 16, lax.div(place, 4), jnp.where(place < 20, 4, place - 20))
+    jy = jnp.where(place < 16, lax.rem(place, 4), jnp.where(place < 20, place - 16, 4))
+    return jnp.where((jx <= 4) & (place < PADDED - 1), (jx * 5 + jy) * 5 + jz, -1)
+
+
+def cell_order_target(cells, row):
+    node, cell = lax.rem(row, 4), lax.rem(lax.div(row, 4), cells)
+    return node * lanes + lax.div(row, 4 * cells) * cells + cell
+
+
+def raw_order_target(cells, row):
+    node, state, cell = lax.div(row, lanes), lax.rem(lax.div(row, cells), lanes // cells), lax.rem(row, cells)
+    return (state * cells + cell) * 4 + node
+
+
+def matrix_kernel(cells, nodes, cell_ref, high_ref, low_ref, order_ref, back_ref, spread_ref):
     rest = cell_ref[...]
+    size, count = high_ref.shape[0], cell_ref.shape[0]
+    tables = [chosen(size, count, functools.partial(select_target, cell, nodes)) for cell in range(nodes // 4)]
     total = jnp.zeros(high_ref.shape, f32)
     for _ in range(3):
         part = rest.astype(bf16)
         rest = rest - part.astype(f32)
-        for cell in range(select_ref.shape[0]):
-            chosen = select_ref[cell]
-            left = dot(chosen, part).astype(bf16)
-            total = total + lax.dot_general(left, chosen, (((1,), (1,)), ((), ())), preferred_element_type=f32)
+        for table in tables:
+            left = dot(table, part).astype(bf16)
+            total = total + lax.dot_general(left, table, (((1,), (1,)), ((), ())), preferred_element_type=f32)
     high_ref[...], low_ref[...] = two_parts(total)
+    order_ref[...] = chosen(*order_ref.shape, functools.partial(cell_order_target, cells))
+    back_ref[...] = chosen(*back_ref.shape, functools.partial(raw_order_target, cells))
+    row = lax.broadcasted_iota(jnp.int32, spread_ref.shape, 0)
+    col = lax.broadcasted_iota(jnp.int32, spread_ref.shape, 1)
+    same = row == lax.rem(col, cells) * 4 + lax.div(col, lanes)
+    spread_ref[...] = jnp.where(same, 1.0, 0.0).astype(bf16)
+
+
+def pick_kernel(parts_x, span_ref, *refs):
+    out_refs, sems = refs[:-1], refs[-1]
+    me = lax.axis_index("px")
+    copies = []
+    for step, out_ref in enumerate(out_refs, 1):
+        states = out_ref.shape[0]
+        source = span_ref.at[pl.ds(lax.rem(me + step, parts_x) * states, states)]
+        copies.append(pltpu.make_async_copy(source, out_ref, sems.at[step]))
+    start_all(copies)
+    wait_all(copies)
+
+
+def widen_kernel(block_ref, out_ref):
+    out_ref[...] = block_ref[...].astype(f32)
+
+
+def narrow_kernel(block_ref, out_ref):
+    out_ref[...] = block_ref[...].astype(bf16)
 
 
 def roll_cells(value, cells, forward):
@@ -235,10 +259,11 @@
     send_edges(high_ref, low_ref, value, down_ref, up_ref, cells)
 
 
-def from_cells_kernel(cells, second, parts_x, *refs):
+def last_kernel(cells, second, parts_x, *refs):
     inner_ref, halo_ref, given_ref, high_ref, low_ref, order_ref = refs[:6]
-    out_refs = refs[6 : 6 + parts_x]
-    held, sems = refs[6 + parts_x :]
+    block_refs = refs[6 : 6 + parts_x]
+    out_refs = refs[6 + parts_x : 6 + 2 * parts_x]
+    tiles_ref, held, sems = refs[6 + 2 * parts_x :]
     value = finish(cells, 2, inner_ref, halo_ref, given_ref, high_ref, low_ref)
     states, rows, thickness = held.shape
     layer = rows // parts_x
@@ -267,36 +292,36 @@
         source = held.at[:, pl.ds(pl.multiple_of(place * layer, layer), layer), :]
         copies.append(pltpu.make_async_copy(source, out_refs[step], sems.at[step]))
     start_all(copies)
+
+    flat = held.reshape(states * rows, thickness)
+    product = None
+    for step in range(parts_x):
+        place = lax.rem(me + (parts_x - step), parts_x)
+        lines = [flat[pl.ds(place * layer + n, states, stride=rows), :].astype(bf16) for n in range(layer)]
+        added = lax.dot_general(
+            block_refs[step][...],
+            jnp.concatenate(lines, 1),
+            (((1,), (1,)), ((), ())),
+            preferred_element_type=f32,
+        )
+        product = added if product is None else product + added
+    group_rows = tiles_ref.shape[0]
+    tiles_ref[...] = jnp.concatenate(
+        [product[start : start + group_rows] for start in range(0, product.shape[0], group_rows)], 1
+    )
     wait_all(copies)
 
 
-def margin_kernel(parts_x, *refs):
-    part_refs, block_ref = refs[:parts_x], refs[parts_x]
-    tiles_ref, filtered_ref, sems = refs[parts_x + 1 :]
+def join_kernel(parts_x, *refs):
+    part_refs, filtered_ref, sems = refs[:parts_x], refs[parts_x], refs[parts_x + 1]
     me = lax.axis_index("px")
     states = filtered_ref.shape[0] // parts_x
-    layer = filtered_ref.shape[1]
-    owners = [lax.rem(me + (parts_x - step), parts_x) for step in range(parts_x)]
-    copies = [
-        pltpu.make_async_copy(part_refs[step], filtered_ref.at[pl.ds(owners[step] * states, states)], sems.at[step])
-        for step in range(parts_x)
-    ]
+    copies = []
+    for step in range(parts_x):
+        owner = lax.rem(me + (parts_x - step), parts_x)
+        target = filtered_ref.at[pl.ds(owner * states, states)]
+        copies.append(pltpu.make_async_copy(part_refs[step], target, sems.at[step]))
     start_all(copies)
-    rows = []
-    for part_ref in part_refs:
-        flat = part_ref.reshape(states * layer, part_ref.shape[2])
-        rows.append([flat[pl.ds(n, states, stride=layer), :].astype(bf16) for n in range(layer)])
-    stacked = jnp.concatenate([jnp.concatenate([part[n] for part in rows], 0) for n in range(layer)], 1)
-    product = lax.dot_general(
-        block_ref[...], stacked, (((1,), (1,)), ((), ())), preferred_element_type=f32
-    )
-    group_rows = tiles_ref.shape[1]
-    groups = block_ref.shape[0] // group_rows
-    for step in range(parts_x):
-        columns = slice(step * states, (step + 1) * states)
-        tiles_ref[owners[step]] = jnp.concatenate(
-            [product[g * group_rows : (g + 1) * group_rows, columns] for g in range(groups)], 1
-        )
     wait_all(copies)
 
 
@@ -329,7 +354,6 @@
     states, first, second, thickness = span.shape
     block_count = block.shape[0]
     parts_x, parts_y = lax.axis_size("px"), lax.axis_size("py")
-    me = lax.axis_index("px")
     mine = states // parts_x
     layer = first * second
     nodes = parts_x * first
@@ -338,8 +362,9 @@
     rows = PADDED * nodes
     others = range(1, parts_x)
 
-    order, spread = lane_orders(lanes // cells, thickness)
+    group = lanes // cells * thickness
     matrix = jax.ShapeDtypeStruct((rows, rows), bf16)
+    table = jax.ShapeDtypeStruct((group, group), bf16)
     field = jax.ShapeDtypeStruct((4, 4, nodes, width), f32)
     message = jax.ShapeDtypeStruct((4, nodes, width), f32)
     part = jax.ShapeDtypeStruct((mine, layer, thickness), f32)
@@ -347,31 +372,50 @@
     held = [pltpu.VMEM((mine, parts_x * layer, thickness), f32), sems]
 
     span_rows = span.reshape(states, layer, thickness)
-    received = []
-    for step in others:
-        chunk = lax.dynamic_slice_in_dim(span_rows, lax.rem(me + step, parts_x) * mine, mine, 0)
-        received.append(shifted(chunk, "px", step))
-    level_rows = potential.reshape(layer, thickness)
-    level_parts = [level_rows] + [shifted(level_rows, "px", step) for step in others]
-
-    high, low = kernel_call(
-        matrix_kernel, [matrix] * 2, [cell_matrix, jnp.asarray(selections(nodes))], "assemble"
+    picked = kernel_call(
+        functools.partial(pick_kernel, parts_x),
+        [part] * (parts_x - 1),
+        [span_rows],
+        "pick",
+        scratch=[sems],
+        in_specs=[anywhere],
+    )
+    received = [shifted(chunk, "px", step) for step, chunk in enumerate(picked, 1)]
+    high, low, order, back, spread = kernel_call(
+        functools.partial(matrix_kernel, cells, nodes),
+        [matrix, matrix, table, table, jax.ShapeDtypeStruct((thickness, 4 * lanes), bf16)],
+        [cell_matrix],
+        "assemble",
     )
     w, down, up = kernel_call(
         functools.partial(to_cells_kernel, cells, second, parts_x),
         [field, message, message],
-        [span_rows] + received + [jnp.asarray(order), high, low],
+        [span_rows] + received + [order, high, low],
         "to_cells",
         scratch=held,
         in_specs=[anywhere] * parts_x + [whole] * 3,
     )
+    level_rows = potential.reshape(layer, thickness)
     levels = kernel_call(
         functools.partial(levels_kernel, second, parts_x),
         jax.ShapeDtypeStruct((4, 4, nodes, lanes), f32),
-        level_parts + [jnp.asarray(spread)],
+        [level_rows] + [shifted(level_rows, "px", step) for step in others] + [spread],
         "levels",
         scratch=[pltpu.VMEM((parts_x * layer, thickness), f32)],
     )
+
+    tile_rows, tile_cols = mine, block_count // parts_y
+    groups = min(tile_cols, lanes // tile_rows)
+    block, up = lax.optimization_barrier((block, up))
+    ordered = block.reshape(parts_y, groups, tile_cols // groups, layer * thickness)
+    ordered = ordered.transpose(1, 0, 2, 3).reshape(block_count, layer * thickness)
+    wide = kernel_call(widen_kernel, jax.ShapeDtypeStruct(ordered.shape, f32), [ordered], "widen")
+    blocks = [ordered] + [
+        kernel_call(
+            narrow_kernel, jax.ShapeDtypeStruct(ordered.shape, bf16), [shifted(wide, "px", step)], "narrow"
+        )
+        for step in others
+    ]
 
     before = None
     for step in range(3):
@@ -385,33 +429,27 @@
                 functools.partial(finish_kernel, cells, step), [field, message, message], operands, "finish"
             )
         else:
-            pieces = kernel_call(
-                functools.partial(from_cells_kernel, cells, second, parts_x),
-                [part] * parts_x,
-                operands + [jnp.asarray(np.ascontiguousarray(order.T))],
-                "from_cells",
+            *pieces, tiles = kernel_call(
+                functools.partial(last_kernel, cells, second, parts_x),
+                [part] * parts_x + [jax.ShapeDtypeStruct((block_count // groups, groups * tile_rows), f32)],
+                operands + [back] + blocks,
+                "last",
                 scratch=held,
-                out_specs=[anywhere] * parts_x,
+                out_specs=[anywhere] * parts_x + [whole],
             )
+
     pieces = [pieces[0]] + [shifted(pieces[step], "px", step) for step in others]
-
-    tile_rows, tile_cols = mine, block_count // parts_y
-    groups = min(tile_cols, lanes // tile_rows)
-    ordered = block.reshape(parts_y, groups, tile_cols // groups, layer * thickness)
-    ordered = ordered.transpose(1, 0, 2, 3).reshape(block_count, layer * thickness)
-    tiles, filtered = kernel_call(
-        functools.partial(margin_kernel, parts_x),
-        [
-            jax.ShapeDtypeStruct((parts_x, block_count // groups, groups * tile_rows), f32),
-            jax.ShapeDtypeStruct((states, layer, thickness), f32),
-        ],
-        pieces + [ordered],
-        "margin",
+    tiles = tiles.reshape(parts_y, tile_cols // groups, groups * tile_rows)
+    tiles = lax.all_to_all(tiles, "py", 0, 0, tiled=True)
+    filtered = kernel_call(
+        functools.partial(join_kernel, parts_x),
+        jax.ShapeDtypeStruct((states, layer, thickness), f32),
+        pieces,
+        "join",
         scratch=[sems],
-        out_specs=[whole, anywhere],
-    )
-    tiles = tiles.reshape(parts_x * parts_y, tile_cols // groups, groups * tile_rows)
-    tiles = lax.all_to_all(tiles, ("px", "py"), 0, 0, tiled=True)
+        in_specs=[anywhere] * parts_x,
+        out_specs=anywhere,
+    )
     margin = kernel_call(sum_kernel, jax.ShapeDtypeStruct((tile_cols, tile_rows), f32), [tiles], "tile_sum")
     return filtered.reshape(span.shape), margin.T
 

time: 54.5 us -> 60.2 us (1.10)
  waiting for transfers between devices: 20.7 us -> 16.8 us
  starting transfers between devices: 11.5 us -> 15 us
  local copies, waits for them, and re-layouts: 4.06 us -> 7.13 us
  Pallas kernels: 8.16 us -> 10.1 us
  blocking collectives: 9.02 us -> 9.98 us
    ppermute x9 -> x10, waiting for transfers between devices: 20.7 us -> 16.8 us  [shifted(): lax.ppermute(value, axis, [(source, (source + steps) % count) for source...]
    ppermute x9 -> x10, starting transfers between devices: 11.5 us -> 15 us  [shifted(): lax.ppermute(value, axis, [(source, (source + steps) % count) for source...]
    reshape x2, local copies, waits for them, and re-layouts: 0.84 us -> 2.88 us  [local(): block.reshape(parts_y, groups, tile_cols // groups, layer * thickness)]
    pallas_call x11 -> x14, Pallas kernels: 8.16 us -> 10.1 us  [kernel_call(): pl.pallas_call(body, out_shape=outs, in_specs=in_specs or [whole] * len(o...]
    reshape x1, local copies, waits for them, and re-layouts: 0.28 us -> 1.33 us  [local(): ordered.transpose(1, 0, 2, 3).reshape(block_count, layer * thickness)]
    dynamic_slice x1 -> x0, local copies, waits for them, and re-layouts: 1.03 us -> none  [local(): lax.dynamic_slice_in_dim(span_rows, lax.rem(me + step, parts_x) * mine, m...]
    unnamed x16 -> x8, local copies, waits for them, and re-layouts: 1.91 us -> 2.92 us
    all_to_all x1, blocking collectives: 9.02 us -> 9.98 us  [local(): tiles = lax.all_to_all(tiles, 'py', 0, 0, tiled=True)]
  transfers between devices with their start and end apart: 9 -> 10, of which waited for: 8 -> 6; matrix products, arithmetic and copies ran while one was open for 2% -> 0% of each run, Pallas kernels for 5% -> 10%
where the time goes in v4:
time: 60.2 us; the launch traced here: 59.9 us
  waiting for transfers between devices  16.8 us (28%)
  starting transfers between devices  15 us (25%)
  Pallas kernels  10.1 us (17%)
  blocking collectives  9.98 us (17%)
  local copies, waits for them, and re-layouts  7.13 us (12%)
  between operations  0.78 us (1%)
    ppermute x10, waiting for transfers between devices, shifted(): lax.ppermute(value, axis, [(source, (source + steps) % count) for source...  16.8 us
    ppermute x10, starting transfers between devices, shifted(): lax.ppermute(value, axis, [(source, (source + steps) % count) for source...  15 us
    pallas_call x14, Pallas kernels, kernel_call(): pl.pallas_call(body, out_shape=outs, in_specs=in_specs or [whole] * len(o...  10.1 us
    all_to_all x1, blocking collectives, local(): tiles = lax.all_to_all(tiles, 'py', 0, 0, tiled=True)  9.98 us
    unnamed x8, local copies, waits for them, and re-layouts  2.92 us
    reshape x2, local copies, waits for them, and re-layouts, local(): block.reshape(parts_y, groups, tile_cols // groups, layer * thickness)  2.88 us
    reshape x1, local copies, waits for them, and re-layouts, local(): ordered.transpose(1, 0, 2, 3).reshape(block_count, layer * thickness)  1.33 us
  transfers between devices with their start and end apart: 10, of which 6 were waited for; matrix products, arithmetic and copies ran while one was open for 0% of the time, Pallas kernels for 10%

profile of v4, /device:TPU:0, one launch (start us, length us, event | category | flops | bytes accessed | tf_op | source)
XLA Modules:
  0.0 59.9 jit_solution(10566820355393808947)
XLA Ops:
  0.6 1.0 %copy-done = f32[64,4,4,128]{3,2,1,0:T(4,128)S(1)} copy-done((f32[64,4,4,128]{3,2,1,0:T(4,128)S(1)}, f32[64,4,4,128]{3,2,1,0:T(4,128)}, u32[]{:S(2)}) %copy-start) | copy-done | bytes 524312
  2.2 0.8 %copy-done.2 = f32[125,125]{1,0:T(8,128)S(1)} copy-done((f32[125,125]{1,0:T(8,128)S(1)}, f32[125,125]{1,0:T(8,128)}, u32[]{:S(2)}) %copy-start.2) | copy-done | bytes 62524
  3.1 1.1 %assemble.1 = (bf16[208,208]{1,0:T(8,128)(2,1)S(1)}, bf16[208,208]{1,0:T(8,128)(2,1)S(1)}, bf16[512,512]{1,0:T(8,128)(2,1)S(1)}, bf16[512,512]{1,0:T(8,128)(2,1)S(1)}, bf16[128,512]{1,0:T(8,128)(2,1)S(1)}) custom-call(f32[125,125]{1,0:T(8,128)S(1)} %copy-done.2), custom_call_target="tpu_custom_call" | custom-call | tf_op jit(solution)/shard_map/assemble/pallas_call | solution.py:342
  4.2 1.0 %copy-done.1 = f32[64,4,4,128]{3,2,1,0:T(4,128)S(1)} copy-done((f32[64,4,4,128]{3,2,1,0:T(4,128)S(1)}, f32[64,4,4,128]{3,2,1,0:T(4,128)}, u32[]{:S(2)}) %copy-start.1) | copy-done | bytes 524312
  5.3 0.9 %to_cells.1 = (f32[4,4,8,1024]{3,2,1,0:T(8,128)S(1)}, f32[4,8,1024]{2,1,0:T(8,128)S(1)}, f32[4,8,1024]{2,1,0:T(8,128)S(1)}) custom-call(f32[64,16,128]{2,1,0:T(8,128)S(1)} %bitcast.9, f32[32,16,128]{2,1,0:T(8,128)S(1)} %collective-permute-done.refs_1_, bf16[512,512]{1,0:T(8,128)(2,1)S(1)} %get-tuple-element.21.refs_2_, ...), custom_call_target="tpu_custom_call" | custom-call | tf_op jit(solution)/shard_map/to_cells/pallas_call | solution.py:342
  6.2 1.3 %reshape.24 = bf16[16,4,4,2048]{3,2,1,0:T(4,128)(2,1)S(1)} reshape(bf16[256,4,4,128]{3,2,1,0:T(4,128)(2,1)} %param.7) | data formatting | bytes 2097152 | tf_op jit(solution)/shard_map/reshape | solution.py:410
  7.5 1.5 %copy.8 = bf16[16,4,4,2048]{3,2,0,1:T(4,128)(2,1)} copy(bf16[16,4,4,2048]{3,2,1,0:T(4,128)(2,1)S(1)} %reshape.24) | data formatting | bytes 2097152 | tf_op jit(solution)/shard_map/reshape | solution.py:410
  9.1 1.3 %reshape.25.block_ref.refs_6_ = bf16[256,2048]{1,0:T(8,128)(2,1)S(1)} reshape(bf16[4,16,4,2048]{3,2,1,0:T(4,128)(2,1)} %bitcast.13) | data formatting | bytes 2097152 | tf_op jit(solution)/shard_map/reshape | solution.py:411
  10.7 2.9 %collective-permute-start.3 = (f32[4,8,1024]{2,1,0:T(8,128)S(1)}, f32[4,8,1024]{2,1,0:T(8,128)S(1)}, u32[]{:S(2)}, u32[]{:S(2)}) collective-permute-start(f32[4,8,1024]{2,1,0:T(8,128)S(1)} %get-tuple-element.28), channel_id=1, source_target_pairs={{0,1},{1,2},{2,3},{3,4},{4,5},{5,6},{6,7},{7,8},{8,9},{9,10},{10,1... | collective-permute-start | bytes 393224 | tf_op jit(solution)/shard_map/ppermute | solution.py:337
  13.6 4.0 %collective-permute-start.2 = (f32[4,8,1024]{2,1,0:T(8,128)S(1)}, f32[4,8,1024]{2,1,0:T(8,128)S(1)}, u32[]{:S(2)}, u32[]{:S(2)}) collective-permute-start(f32[4,8,1024]{2,1,0:T(8,128)S(1)} %get-tuple-element.26), channel_id=1, source_target_pairs={{0,15},{1,0},{2,1},{3,2},{4,3},{5,4},{6,5},{7,6},{8,7},{9,8},{10,9... | collective-permute-start | bytes 393224 | tf_op jit(solution)/shard_map/ppermute | solution.py:337
  17.6 1.2 %collective-permute-done.1.refs_1_ = f32[16,128]{1,0:T(8,128)S(1)} collective-permute-done((f32[16,128]{1,0:T(8,128)S(1)}, f32[16,128]{1,0:T(8,128)S(1)}, u32[]{:S(2)}, u32[]{:S(2)}) %collective-permute-start.1) | collective-permute-done | bytes 8224 | tf_op jit(solution)/shard_map/ppermute | solution.py:337
  19.6 1.8 %collective-permute-done.3.given_ref = f32[4,8,1024]{2,1,0:T(8,128)S(1)} collective-permute-done((f32[4,8,1024]{2,1,0:T(8,128)S(1)}, f32[4,8,1024]{2,1,0:T(8,128)S(1)}, u32[]{:S(2)}, u32[]{:S(2)}) %collective-permute-start.3) | collective-permute-done | bytes 131104 | tf_op jit(solution)/shard_map/ppermute | solution.py:337
  21.5 1.0 %finish.2 = (f32[4,4,8,1024]{3,2,1,0:T(8,128)S(1)}, f32[4,8,1024]{2,1,0:T(8,128)S(1)}, f32[4,8,1024]{2,1,0:T(8,128)S(1)}) custom-call(f32[4,4,8,1024]{3,2,1,0:T(8,128)S(1)} %inner.3.inner_ref, f32[4,8,1024]{2,1,0:T(8,128)S(1)} %collective-permute-done.2.halo_ref, f32[4,8,1024]{2,1,0:T(8,128)S(1)} %collective-permute-done.3.given_ref, ...), custom_call_target="tpu_custom_call" | custom-call | tf_op jit(solution)/shard_map/finish/pallas_call | solution.py:342
  22.4 5.3 %collective-permute-start.4 = (f32[4,8,1024]{2,1,0:T(8,128)S(1)}, f32[4,8,1024]{2,1,0:T(8,128)S(1)}, u32[]{:S(2)}, u32[]{:S(2)}) collective-permute-start(f32[4,8,1024]{2,1,0:T(8,128)S(1)} %get-tuple-element.30), channel_id=1, source_target_pairs={{0,15},{1,0},{2,1},{3,2},{4,3},{5,4},{6,5},{7,6},{8,7},{9,8},{10,9... | collective-permute-start | bytes 393224 | tf_op jit(solution)/shard_map/ppermute | solution.py:337
  28.4 1.9 %collective-permute-done.4.halo_ref = f32[4,8,1024]{2,1,0:T(8,128)S(1)} collective-permute-done((f32[4,8,1024]{2,1,0:T(8,128)S(1)}, f32[4,8,1024]{2,1,0:T(8,128)S(1)}, u32[]{:S(2)}, u32[]{:S(2)}) %collective-permute-start.4) | collective-permute-done | bytes 131104 | tf_op jit(solution)/shard_map/ppermute | solution.py:337
  30.3 6.1 %collective-permute-done.5.given_ref = f32[4,8,1024]{2,1,0:T(8,128)S(1)} collective-permute-done((f32[4,8,1024]{2,1,0:T(8,128)S(1)}, f32[4,8,1024]{2,1,0:T(8,128)S(1)}, u32[]{:S(2)}, u32[]{:S(2)}) %collective-permute-start.5) | collective-permute-done | bytes 131104 | tf_op jit(solution)/shard_map/ppermute | solution.py:337
  36.4 1.0 %finish.3 = (f32[4,4,8,1024]{3,2,1,0:T(8,128)S(1)}, f32[4,8,1024]{2,1,0:T(8,128)S(1)}, f32[4,8,1024]{2,1,0:T(8,128)S(1)}) custom-call(f32[4,4,8,1024]{3,2,1,0:T(8,128)S(1)} %inner.4.inner_ref, f32[4,8,1024]{2,1,0:T(8,128)S(1)} %collective-permute-done.4.halo_ref, f32[4,8,1024]{2,1,0:T(8,128)S(1)} %collective-permute-done.5.given_ref, ...), custom_call_target="tpu_custom_call" | custom-call | tf_op jit(solution)/shard_map/finish/pallas_call | solution.py:342
  37.5 2.0 %collective-permute-start.7 = (f32[4,8,1024]{2,1,0:T(8,128)S(1)}, f32[4,8,1024]{2,1,0:T(8,128)S(1)}, u32[]{:S(2)}, u32[]{:S(2)}) collective-permute-start(f32[4,8,1024]{2,1,0:T(8,128)S(1)} %get-tuple-element.34), channel_id=1, source_target_pairs={{0,1},{1,2},{2,3},{3,4},{4,5},{5,6},{6,7},{7,8},{8,9},{9,10},{10,1... | collective-permute-start | bytes 393224 | tf_op jit(solution)/shard_map/ppermute | solution.py:337
  40.2 2.2 %collective-permute-done.6.refs_1_ = f32[4,8,1024]{2,1,0:T(8,128)S(1)} collective-permute-done((f32[4,8,1024]{2,1,0:T(8,128)S(1)}, f32[4,8,1024]{2,1,0:T(8,128)S(1)}, u32[]{:S(2)}, u32[]{:S(2)}) %collective-permute-start.6) | collective-permute-done | bytes 131104 | tf_op jit(solution)/shard_map/ppermute | solution.py:337
  42.4 3.7 %collective-permute-done.7.refs_2_ = f32[4,8,1024]{2,1,0:T(8,128)S(1)} collective-permute-done((f32[4,8,1024]{2,1,0:T(8,128)S(1)}, f32[4,8,1024]{2,1,0:T(8,128)S(1)}, u32[]{:S(2)}, u32[]{:S(2)}) %collective-permute-start.7) | collective-permute-done | bytes 131104 | tf_op jit(solution)/shard_map/ppermute | solution.py:337
  46.1 2.3 %last.1 = (f32[32,16,128]{2,1,0:T(8,128)S(1)}, f32[32,16,128]{2,1,0:T(8,128)S(1)}, f32[64,128]{1,0:T(8,128)S(1)}) custom-call(f32[4,4,8,1024]{3,2,1,0:T(8,128)S(1)} %inner.5.refs_0_, f32[4,8,1024]{2,1,0:T(8,128)S(1)} %collective-permute-done.6.refs_1_, f32[4,8,1024]{2,1,0:T(8,128)S(1)} %collective-permute-done.7.refs_2_, ...), custom_call_target="tpu_custom_call" | custom-call | tf_op jit(solution)/shard_map/last/pallas_call | solution.py:342
  48.4 10.0 %all_to_all.5.tiles_ref = f32[16,4,128]{2,1,0:T(4,128)S(1)} all-to-all(f32[16,4,128]{2,1,0:T(4,128)S(1)} %bitcast.10), channel_id=1, replica_groups=mesh['px'=2,'py'=16] {'py'}, dimensions={0} | all-to-all | bytes 65536 | tf_op jit(solution)/shard_map/all_to_all | solution.py:443
  58.4 0.7 %tile_sum.1 = f32[16,32]{1,0:T(8,128)} custom-call(f32[16,4,128]{2,1,0:T(4,128)S(1)} %all_to_all.5.tiles_ref), custom_call_target="tpu_custom_call" | custom-call | tf_op jit(solution)/shard_map/tile_sum/pallas_call | solution.py:342
  59.1 0.8 %join.1 = f32[64,16,128]{2,1,0:T(8,128)} custom-call(f32[32,16,128]{2,1,0:T(8,128)S(1)} %get-tuple-element.37.refs_0_, f32[32,16,128]{2,1,0:T(8,128)S(1)} %collective-permute-done.9.refs_1_), custom_call_target="tpu_custom_call" | custom-call | tf_op jit(solution)/shard_map/join/pallas_call | solution.py:342
  (22 shorter events, 3.2 us)
Async XLA Ops:
  0.6 1.0 %copy-start = (f32[64,4,4,128]{3,2,1,0:T(4,128)S(1)}, f32[64,4,4,128]{3,2,1,0:T(4,128)}, u32[]{:S(2)}) copy-start(f32[64,4,4,128]{3,2,1,0:T(4,128)} %param.4) | copy-start | bytes 1572868
  1.7 2.5 %collective-permute-start = (f32[32,16,128]{2,1,0:T(8,128)S(1)}, f32[32,16,128]{2,1,0:T(8,128)S(1)}, u32[]{:S(2)}, u32[]{:S(2)}) collective-permute-start(f32[32,16,128]{2,1,0:T(8,128)S(1)} %pick.1), channel_id=1, source_target_pairs={{0,16},{16,0},{1,17},{17,1},{2,18},{18,2},{3,19},{19,3},{4,20},{20... | collective-permute-start | bytes 786440 | tf_op jit(solution)/shard_map/ppermute | solution.py:337
  2.2 0.8 %copy-start.2 = (f32[125,125]{1,0:T(8,128)S(1)}, f32[125,125]{1,0:T(8,128)}, u32[]{:S(2)}) copy-start(f32[125,125]{1,0:T(8,128)} %cell_ref.1) | copy-start | bytes 187504
  4.2 1.0 %copy-start.1 = (f32[64,4,4,128]{3,2,1,0:T(4,128)S(1)}, f32[64,4,4,128]{3,2,1,0:T(4,128)}, u32[]{:S(2)}) copy-start(f32[64,4,4,128]{3,2,1,0:T(4,128)} %param.4) | copy-start | bytes 1572868
  10.4 7.2 %copy-start.3 = (f32[4,4,128]{2,1,0:T(4,128)S(1)}, f32[4,4,128]{2,1,0:T(4,128)}, u32[]{:S(2)}) copy-start(f32[4,4,128]{2,1,0:T(4,128)} %param.5) | copy-start | bytes 24580
  10.6 29.6 %collective-permute-start.8 = (f32[256,2048]{1,0:T(8,128)S(1)}, f32[256,2048]{1,0:T(8,128)S(1)}, u32[]{:S(2)}, u32[]{:S(2)}) collective-permute-start(f32[256,2048]{1,0:T(8,128)S(1)} %widen.1), channel_id=1, source_target_pairs={{0,16},{16,0},{1,17},{17,1},{2,18},{18,2},{3,19},{19,3},{4,20},{20... | collective-permute-start | bytes 6291464 | tf_op jit(solution)/shard_map/ppermute | solution.py:337
  10.7 10.8 %collective-permute-start.3 = (f32[4,8,1024]{2,1,0:T(8,128)S(1)}, f32[4,8,1024]{2,1,0:T(8,128)S(1)}, u32[]{:S(2)}, u32[]{:S(2)}) collective-permute-start(f32[4,8,1024]{2,1,0:T(8,128)S(1)} %get-tuple-element.28), channel_id=1, source_target_pairs={{0,1},{1,2},{2,3},{3,4},{4,5},{5,6},{6,7},{7,8},{8,9},{9,10},{10,1... | collective-permute-start | bytes 393224 | tf_op jit(solution)/shard_map/ppermute | solution.py:337
  13.6 7.8 %collective-permute-start.2 = (f32[4,8,1024]{2,1,0:T(8,128)S(1)}, f32[4,8,1024]{2,1,0:T(8,128)S(1)}, u32[]{:S(2)}, u32[]{:S(2)}) collective-permute-start(f32[4,8,1024]{2,1,0:T(8,128)S(1)} %get-tuple-element.26), channel_id=1, source_target_pairs={{0,15},{1,0},{2,1},{3,2},{4,3},{5,4},{6,5},{7,6},{8,7},{9,8},{10,9... | collective-permute-start | bytes 393224 | tf_op jit(solution)/shard_map/ppermute | solution.py:337
  17.6 1.2 %collective-permute-start.1 = (f32[16,128]{1,0:T(8,128)S(1)}, f32[16,128]{1,0:T(8,128)S(1)}, u32[]{:S(2)}, u32[]{:S(2)}) collective-permute-start(f32[16,128]{1,0:T(8,128)S(1)} %bitcast.11), channel_id=1, source_target_pairs={{0,16},{16,0},{1,17},{17,1},{2,18},{18,2},{3,19},{19,3},{4,20},{20... | collective-permute-start | bytes 24584 | tf_op jit(solution)/shard_map/ppermute | solution.py:337
  22.4 7.9 %collective-permute-start.4 = (f32[4,8,1024]{2,1,0:T(8,128)S(1)}, f32[4,8,1024]{2,1,0:T(8,128)S(1)}, u32[]{:S(2)}, u32[]{:S(2)}) collective-permute-start(f32[4,8,1024]{2,1,0:T(8,128)S(1)} %get-tuple-element.30), channel_id=1, source_target_pairs={{0,15},{1,0},{2,1},{3,2},{4,3},{5,4},{6,5},{7,6},{8,7},{9,8},{10,9... | collective-permute-start | bytes 393224 | tf_op jit(solution)/shard_map/ppermute | solution.py:337
  27.8 8.7 %collective-permute-start.5 = (f32[4,8,1024]{2,1,0:T(8,128)S(1)}, f32[4,8,1024]{2,1,0:T(8,128)S(1)}, u32[]{:S(2)}, u32[]{:S(2)}) collective-permute-start(f32[4,8,1024]{2,1,0:T(8,128)S(1)} %get-tuple-element.31), channel_id=1, source_target_pairs={{0,1},{1,2},{2,3},{3,4},{4,5},{5,6},{6,7},{7,8},{8,9},{9,10},{10,1... | collective-permute-start | bytes 393224 | tf_op jit(solution)/shard_map/ppermute | solution.py:337
  37.4 5.0 %collective-permute-start.6 = (f32[4,8,1024]{2,1,0:T(8,128)S(1)}, f32[4,8,1024]{2,1,0:T(8,128)S(1)}, u32[]{:S(2)}, u32[]{:S(2)}) collective-permute-start(f32[4,8,1024]{2,1,0:T(8,128)S(1)} %get-tuple-element.33), channel_id=1, source_target_pairs={{0,15},{1,0},{2,1},{3,2},{4,3},{5,4},{6,5},{7,6},{8,7},{9,8},{10,9... | collective-permute-start | bytes 393224 | tf_op jit(solution)/shard_map/ppermute | solution.py:337
  37.5 8.6 %collective-permute-start.7 = (f32[4,8,1024]{2,1,0:T(8,128)S(1)}, f32[4,8,1024]{2,1,0:T(8,128)S(1)}, u32[]{:S(2)}, u32[]{:S(2)}) collective-permute-start(f32[4,8,1024]{2,1,0:T(8,128)S(1)} %get-tuple-element.34), channel_id=1, source_target_pairs={{0,1},{1,2},{2,3},{3,4},{4,5},{5,6},{6,7},{7,8},{8,9},{9,10},{10,1... | collective-permute-start | bytes 393224 | tf_op jit(solution)/shard_map/ppermute | solution.py:337
  48.4 10.7 %collective-permute-start.9 = (f32[32,16,128]{2,1,0:T(8,128)S(1)}, f32[32,16,128]{2,1,0:T(8,128)S(1)}, u32[]{:S(2)}, u32[]{:S(2)}) collective-permute-start(f32[32,16,128]{2,1,0:T(8,128)S(1)} %get-tuple-element.38), channel_id=1, source_target_pairs={{0,16},{16,0},{1,17},{17,1},{2,18},{18,2},{3,19},{19,3},{4,20},{20... | collective-permute-start | bytes 786440 | tf_op jit(solution)/shard_map/ppermute | solution.py:337

commit v5 on v4

--- a/solution.py
+++ b/solution.py
@@ -14,6 +14,7 @@
 f32 = jnp.float32
 whole = pl.BlockSpec(memory_space=pltpu.VMEM)
 anywhere = pl.BlockSpec(memory_space=pl.ANY)
+in_hbm = pl.BlockSpec(memory_space=pltpu.HBM)
 params = pltpu.CompilerParams(vmem_limit_bytes=48 * 2**20)
 
 BLOCKS = (
@@ -78,24 +79,25 @@
     spread_ref[...] = jnp.where(same, 1.0, 0.0).astype(bf16)
 
 
-def pick_kernel(parts_x, span_ref, *refs):
+def pick_kernel(parts_x, chunks, span_ref, potential_ref, cell_ref, *refs):
     out_refs, sems = refs[:-1], refs[-1]
     me = lax.axis_index("px")
     copies = []
-    for step, out_ref in enumerate(out_refs, 1):
-        states = out_ref.shape[0]
-        source = span_ref.at[pl.ds(lax.rem(me + step, parts_x) * states, states)]
-        copies.append(pltpu.make_async_copy(source, out_ref, sems.at[step]))
-    start_all(copies)
+
+    def copy(source, target):
+        copies.append(pltpu.make_async_copy(source, target, sems.at[len(copies)]))
+        copies[-1].start()
+
+    count = span_ref.shape[0] // (parts_x * chunks)
+    for step in range(parts_x):
+        for chunk in range(chunks):
+            start = (lax.rem(me + step, parts_x) * chunks + chunk) * count
+            target = out_refs[1 + step * chunks + chunk]
+            copy(span_ref.at[pl.ds(start, count)], target.at[pl.ds(0, count)])
+            if chunk == 0:
+                copy(potential_ref, target.at[count])
+    copy(cell_ref, out_refs[0])
     wait_all(copies)
-
-
-def widen_kernel(block_ref, out_ref):
-    out_ref[...] = block_ref[...].astype(f32)
-
-
-def narrow_kernel(block_ref, out_ref):
-    out_ref[...] = block_ref[...].astype(bf16)
 
 
 def roll_cells(value, cells, forward):
@@ -147,31 +149,22 @@
         copy.wait()
 
 
-def to_cells_kernel(cells, second, parts_x, *refs):
-    span_ref, other_refs = refs[0], refs[1:parts_x]
-    order_ref, high_ref, low_ref, w_ref, down_ref, up_ref, held, sems = refs[parts_x:]
-    me = lax.axis_index("px")
-    states, rows = held.shape[:2]
-    layer = rows // parts_x
-    nodes = rows // second
-    copies = []
-    for step in range(parts_x):
-        place = lax.rem(me + (parts_x - step), parts_x)
-        target = held.at[:, pl.ds(pl.multiple_of(place * layer, layer), layer), :]
-        source = span_ref.at[pl.ds(me * states, states)] if step == 0 else other_refs[step - 1]
-        copies.append(pltpu.make_async_copy(source, target, sems.at[step]))
-    start_all(copies)
-    wait_all(copies)
+def gathered(part_refs, state, second):
+    size = part_refs[0].shape[1] // second
+    return [ref[state, pl.ds(y, size, stride=second), :] for y in range(second) for ref in part_refs]
+
+
+def to_cells_kernel(cells, second, parts_x, states, *refs):
+    part_refs = refs[:parts_x]
+    order_ref, high_ref, low_ref, w_ref, down_ref, up_ref = refs[parts_x:]
+    nodes = w_ref.shape[2]
     group = lanes // cells
     groups = states // group
     size = second * nodes
-
-    def gathered(state):
-        return jnp.concatenate([held[state, pl.ds(y, nodes, stride=second), :] for y in range(second)], 0)
-
     sources = []
     for h in range(groups):
-        sources += list(two_parts(jnp.concatenate([gathered(h * group + s) for s in range(group)], 1)))
+        lines = [jnp.concatenate(gathered(part_refs, h * group + s, second), 0) for s in range(group)]
+        sources += list(two_parts(jnp.concatenate(lines, 1)))
     ordered = dot(jnp.concatenate(sources, 0), order_ref[...])
     values = [ordered[2 * h * size : (2 * h + 1) * size] + ordered[(2 * h + 1) * size : (2 * h + 2) * size] for h in range(groups)]
     value = {}
@@ -184,15 +177,10 @@
 
 
 def levels_kernel(second, parts_x, *refs):
-    spread_ref, levels_ref, held = refs[parts_x:]
-    me = lax.axis_index("px")
-    layer = held.shape[0] // parts_x
-    nodes = held.shape[0] // second
-    for step in range(parts_x):
-        place = lax.rem(me + (parts_x - step), parts_x)
-        held[pl.ds(pl.multiple_of(place * layer, layer), layer), :] = refs[step][...]
-    rows = [held[pl.ds(y, nodes, stride=second), :] for y in range(second)]
-    high, low = two_parts(jnp.concatenate(rows, 0))
+    part_refs, (spread_ref, levels_ref) = refs[:parts_x], refs[parts_x:]
+    nodes = levels_ref.shape[2]
+    rows = jnp.concatenate(gathered(part_refs, part_refs[0].shape[0] - 1, second), 0)
+    high, low = two_parts(rows)
     spread = dot(high, spread_ref[...]) + dot(low, spread_ref[...])
     for y in range(second):
         for iz in range(4):
@@ -259,15 +247,13 @@
     send_edges(high_ref, low_ref, value, down_ref, up_ref, cells)
 
 
-def last_kernel(cells, second, parts_x, *refs):
+def from_cells_kernel(cells, second, parts_x, *refs):
     inner_ref, halo_ref, given_ref, high_ref, low_ref, order_ref = refs[:6]
-    block_refs = refs[6 : 6 + parts_x]
-    out_refs = refs[6 + parts_x : 6 + 2 * parts_x]
-    tiles_ref, held, sems = refs[6 + 2 * parts_x :]
+    out_refs = refs[6:]
     value = finish(cells, 2, inner_ref, halo_ref, given_ref, high_ref, low_ref)
-    states, rows, thickness = held.shape
-    layer = rows // parts_x
-    nodes = rows // second
+    states, layer, thickness = out_refs[0].shape
+    first = layer // second
+    nodes = parts_x * first
     group = lanes // cells
     groups = states // group
     size = second * nodes
@@ -283,45 +269,40 @@
         part = ordered[2 * h * size : (2 * h + 1) * size] + ordered[(2 * h + 1) * size : (2 * h + 2) * size]
         for y in range(second):
             for s in range(group):
-                lines = part[y * nodes : (y + 1) * nodes, s * thickness : (s + 1) * thickness]
-                held[h * group + s, pl.ds(y, nodes, stride=second), :] = lines
+                for step, out_ref in enumerate(out_refs):
+                    start = y * nodes + step * first
+                    lines = part[start : start + first, s * thickness : (s + 1) * thickness]
+                    out_ref[h * group + s, pl.ds(y, first, stride=second), :] = lines
+
+
+def margin_kernel(parts_x, chunks, *refs):
+    part_refs, block_ref = refs[: parts_x * chunks], refs[parts_x * chunks]
+    tiles_ref, filtered_ref, sems = refs[parts_x * chunks + 1 :]
     me = lax.axis_index("px")
+    count, layer, thickness = part_refs[0].shape
+    mine = count * chunks
+    owners = [lax.rem(me + (parts_x - step), parts_x) for step in range(parts_x)]
     copies = []
+    for place, part_ref in enumerate(part_refs):
+        start = owners[place // chunks] * mine + place % chunks * count
+        target = filtered_ref.at[pl.ds(start, count)]
+        copies.append(pltpu.make_async_copy(part_ref, target, sems.at[place]))
+    start_all(copies)
+    flat = [ref.reshape(count * layer, thickness) for ref in part_refs]
+    lines = [
+        jnp.concatenate([ref[pl.ds(n, count, stride=layer), :].astype(bf16) for ref in flat], 0)
+        for n in range(layer)
+    ]
+    product = lax.dot_general(
+        block_ref[...], jnp.concatenate(lines, 1), (((1,), (1,)), ((), ())), preferred_element_type=f32
+    )
+    group_rows = tiles_ref.shape[1]
+    groups = block_ref.shape[0] // group_rows
     for step in range(parts_x):
-        place = lax.rem(me + step, parts_x)
-        source = held.at[:, pl.ds(pl.multiple_of(place * layer, layer), layer), :]
-        copies.append(pltpu.make_async_copy(source, out_refs[step], sems.at[step]))
-    start_all(copies)
-
-    flat = held.reshape(states * rows, thickness)
-    product = None
-    for step in range(parts_x):
-        place = lax.rem(me + (parts_x - step), parts_x)
-        lines = [flat[pl.ds(place * layer + n, states, stride=rows), :].astype(bf16) for n in range(layer)]
-        added = lax.dot_general(
-            block_refs[step][...],
-            jnp.concatenate(lines, 1),
-            (((1,), (1,)), ((), ())),
-            preferred_element_type=f32,
+        columns = slice(step * mine, (step + 1) * mine)
+        tiles_ref[owners[step]] = jnp.concatenate(
+            [product[g * group_rows : (g + 1) * group_rows, columns] for g in range(groups)], 1
         )
-        product = added if product is None else product + added
-    group_rows = tiles_ref.shape[0]
-    tiles_ref[...] = jnp.concatenate(
-        [product[start : start + group_rows] for start in range(0, product.shape[0], group_rows)], 1
-    )
-    wait_all(copies)
-
-
-def join_kernel(parts_x, *refs):
-    part_refs, filtered_ref, sems = refs[:parts_x], refs[parts_x], refs[parts_x + 1]
-    me = lax.axis_index("px")
-    states = filtered_ref.shape[0] // parts_x
-    copies = []
-    for step in range(parts_x):
-        owner = lax.rem(me + (parts_x - step), parts_x)
-        target = filtered_ref.at[pl.ds(owner * states, states)]
-        copies.append(pltpu.make_async_copy(part_refs[step], target, sems.at[step]))
-    start_all(copies)
     wait_all(copies)
 
 
@@ -358,98 +339,97 @@
     layer = first * second
     nodes = parts_x * first
     cells = thickness // 4
-    width = mine * cells
     rows = PADDED * nodes
     others = range(1, parts_x)
 
     group = lanes // cells * thickness
     matrix = jax.ShapeDtypeStruct((rows, rows), bf16)
     table = jax.ShapeDtypeStruct((group, group), bf16)
+
+    chunks = 2
+    count = mine // chunks
+    width = count * cells
     field = jax.ShapeDtypeStruct((4, 4, nodes, width), f32)
     message = jax.ShapeDtypeStruct((4, nodes, width), f32)
-    part = jax.ShapeDtypeStruct((mine, layer, thickness), f32)
-    sems = pltpu.SemaphoreType.DMA((parts_x,))
-    held = [pltpu.VMEM((mine, parts_x * layer, thickness), f32), sems]
-
-    span_rows = span.reshape(states, layer, thickness)
-    picked = kernel_call(
-        functools.partial(pick_kernel, parts_x),
-        [part] * (parts_x - 1),
-        [span_rows],
+    part = jax.ShapeDtypeStruct((count, layer, thickness), f32)
+    first_part = jax.ShapeDtypeStruct((count + 1, layer, thickness), f32)
+    cell_matrix, *parts = kernel_call(
+        functools.partial(pick_kernel, parts_x, chunks),
+        [jax.ShapeDtypeStruct(cell_matrix.shape, f32)] + ([first_part] + [part] * (chunks - 1)) * parts_x,
+        [span.reshape(states, layer, thickness), potential.reshape(layer, thickness), cell_matrix],
         "pick",
-        scratch=[sems],
-        in_specs=[anywhere],
+        scratch=[pltpu.SemaphoreType.DMA((parts_x * (chunks + 1) + 1,))],
+        in_specs=[in_hbm] * 3,
     )
-    received = [shifted(chunk, "px", step) for step, chunk in enumerate(picked, 1)]
+    places = [parts[:chunks]] + [
+        [shifted(parts[step * chunks + chunk], "px", step) for chunk in range(chunks)]
+        for step in reversed(others)
+    ]
     high, low, order, back, spread = kernel_call(
         functools.partial(matrix_kernel, cells, nodes),
         [matrix, matrix, table, table, jax.ShapeDtypeStruct((thickness, 4 * lanes), bf16)],
         [cell_matrix],
         "assemble",
     )
-    w, down, up = kernel_call(
-        functools.partial(to_cells_kernel, cells, second, parts_x),
-        [field, message, message],
-        [span_rows] + received + [order, high, low],
-        "to_cells",
-        scratch=held,
-        in_specs=[anywhere] * parts_x + [whole] * 3,
-    )
-    level_rows = potential.reshape(layer, thickness)
     levels = kernel_call(
         functools.partial(levels_kernel, second, parts_x),
         jax.ShapeDtypeStruct((4, 4, nodes, lanes), f32),
-        [level_rows] + [shifted(level_rows, "px", step) for step in others] + [spread],
+        [place[0] for place in places] + [spread],
         "levels",
-        scratch=[pltpu.VMEM((parts_x * layer, thickness), f32)],
     )
 
+    fields, before, edges = [None] * chunks, [None] * chunks, [None] * chunks
+    for chunk in range(chunks):
+        fields[chunk], *edges[chunk] = kernel_call(
+            functools.partial(to_cells_kernel, cells, second, parts_x, count),
+            [field, message, message],
+            [place[chunk] for place in places] + [order, high, low],
+            "to_cells",
+        )
+        edges[chunk] = [shifted(edges[chunk][0], "py", -1), shifted(edges[chunk][1], "py", 1)]
     tile_rows, tile_cols = mine, block_count // parts_y
     groups = min(tile_cols, lanes // tile_rows)
-    block, up = lax.optimization_barrier((block, up))
-    ordered = block.reshape(parts_y, groups, tile_cols // groups, layer * thickness)
-    ordered = ordered.transpose(1, 0, 2, 3).reshape(block_count, layer * thickness)
-    wide = kernel_call(widen_kernel, jax.ShapeDtypeStruct(ordered.shape, f32), [ordered], "widen")
-    blocks = [ordered] + [
-        kernel_call(
-            narrow_kernel, jax.ShapeDtypeStruct(ordered.shape, bf16), [shifted(wide, "px", step)], "narrow"
-        )
-        for step in others
-    ]
-
-    before = None
+    pieces = [None] * chunks
     for step in range(3):
-        halo = shifted(down, "py", -1)
-        given = shifted(up, "py", 1)
-        operands = [w, levels, high, low] + ([before] if step > 0 else [])
-        inner = kernel_call(functools.partial(inner_kernel, cells, step), field, operands, "inner")
-        operands = [inner, halo, given, high, low]
-        if step < 2:
-            before, (w, down, up) = w, kernel_call(
-                functools.partial(finish_kernel, cells, step), [field, message, message], operands, "finish"
-            )
-        else:
-            *pieces, tiles = kernel_call(
-                functools.partial(last_kernel, cells, second, parts_x),
-                [part] * parts_x + [jax.ShapeDtypeStruct((block_count // groups, groups * tile_rows), f32)],
-                operands + [back] + blocks,
-                "last",
-                scratch=held,
-                out_specs=[anywhere] * parts_x + [whole],
-            )
-
-    pieces = [pieces[0]] + [shifted(pieces[step], "px", step) for step in others]
-    tiles = tiles.reshape(parts_y, tile_cols // groups, groups * tile_rows)
-    tiles = lax.all_to_all(tiles, "py", 0, 0, tiled=True)
-    filtered = kernel_call(
-        functools.partial(join_kernel, parts_x),
-        jax.ShapeDtypeStruct((states, layer, thickness), f32),
-        pieces,
-        "join",
-        scratch=[sems],
-        in_specs=[anywhere] * parts_x,
-        out_specs=anywhere,
+        for chunk in range(chunks):
+            operands = [fields[chunk], levels, high, low] + ([before[chunk]] if step > 0 else [])
+            inner = kernel_call(functools.partial(inner_kernel, cells, step), field, operands, "inner")
+            if chunk == chunks - 1 and step == 0:
+                block, inner = lax.optimization_barrier((block, inner))
+                ordered = block.reshape(parts_y, groups, tile_cols // groups, layer * thickness)
+                ordered = ordered.transpose(1, 0, 2, 3).reshape(block_count, layer * thickness)
+            if chunk == chunks - 1 and step == 1:
+                ordered, inner = lax.optimization_barrier((ordered, inner))
+            operands = [inner] + edges[chunk] + [high, low]
+            if step < 2:
+                before[chunk] = fields[chunk]
+                fields[chunk], *edges[chunk] = kernel_call(
+                    functools.partial(finish_kernel, cells, step), [field, message, message], operands, "finish"
+                )
+                edges[chunk] = [shifted(edges[chunk][0], "py", -1), shifted(edges[chunk][1], "py", 1)]
+            else:
+                pieces[chunk] = kernel_call(
+                    functools.partial(from_cells_kernel, cells, second, parts_x),
+                    [part] * parts_x,
+                    operands + [back],
+                    "from_cells",
+                )
+    received = [pieces[chunk][0] for chunk in range(chunks)]
+    for step in others:
+        received += [shifted(pieces[chunk][step], "px", step) for chunk in range(chunks)]
+    tiles, filtered = kernel_call(
+        functools.partial(margin_kernel, parts_x, chunks),
+        [
+            jax.ShapeDtypeStruct((parts_x, block_count // groups, groups * tile_rows), f32),
+            jax.ShapeDtypeStruct((states, layer, thickness), f32),
+        ],
+        received + [ordered],
+        "margin",
+        scratch=[pltpu.SemaphoreType.DMA((parts_x * chunks,))],
+        out_specs=[whole, anywhere],
     )
+    tiles = tiles.reshape(parts_x * parts_y, tile_cols // groups, groups * tile_rows)
+    tiles = lax.all_to_all(tiles, ("px", "py"), 0, 0, tiled=True)
     margin = kernel_call(sum_kernel, jax.ShapeDtypeStruct((tile_cols, tile_rows), f32), [tiles], "tile_sum")
     return filtered.reshape(span.shape), margin.T
 

time: 60.2 us -> 72.8 us (1.21)
  starting transfers between devices: 15 us -> 34.4 us
  waiting for transfers between devices: 16.8 us -> 8.96 us
  Pallas kernels: 10.1 us -> 12.5 us
  blocking collectives: 9.98 us -> 9.02 us
    ppermute x10 -> x16, starting transfers between devices: 15 us -> 34.4 us  [shifted(): lax.ppermute(value, axis, [(source, (source + steps) % count) for source...]
    ppermute x10 -> x16, waiting for transfers between devices: 16.8 us -> 8.96 us  [shifted(): lax.ppermute(value, axis, [(source, (source + steps) % count) for source...]
    pallas_call x14 -> x19, Pallas kernels: 10.1 us -> 12.5 us  [kernel_call(): pl.pallas_call(body, out_shape=outs, in_specs=in_specs or [whole] * len(o...]
    all_to_all x1, blocking collectives: 9.98 us -> 9.02 us  [local(): tiles = lax.all_to_all(tiles, ('px', 'py'), 0, 0, tiled=True)]
    unnamed x8 -> x6, local copies, waits for them, and re-layouts: 2.92 us -> 2.57 us
  transfers between devices with their start and end apart: 10 -> 16, of which waited for: 6 -> 6; matrix products, arithmetic and copies ran while one was open for 0% -> 6% of each run, Pallas kernels for 10% -> 14%
where the time goes in v5:
time: 72.8 us; the launch traced here: 72.5 us
  starting transfers between devices  34.4 us (47%)
  Pallas kernels  12.5 us (17%)
  blocking collectives  9.02 us (12%)
  waiting for transfers between devices  8.96 us (12%)
  local copies, waits for them, and re-layouts  6.79 us (9%)
  between operations  0.82 us (1%)
    ppermute x16, starting transfers between devices, shifted(): lax.ppermute(value, axis, [(source, (source + steps) % count) for source...  34.4 us
    pallas_call x19, Pallas kernels, kernel_call(): pl.pallas_call(body, out_shape=outs, in_specs=in_specs or [whole] * len(o...  12.5 us
    all_to_all x1, blocking collectives, local(): tiles = lax.all_to_all(tiles, ('px', 'py'), 0, 0, tiled=True)  9.02 us
    ppermute x16, waiting for transfers between devices, shifted(): lax.ppermute(value, axis, [(source, (source + steps) % count) for source...  8.96 us
    reshape x2, local copies, waits for them, and re-layouts, local(): block.reshape(parts_y, groups, tile_cols // groups, layer * thickness)  2.89 us
    unnamed x6, local copies, waits for them, and re-layouts  2.57 us
  transfers between devices with their start and end apart: 16, of which 6 were waited for; matrix products, arithmetic and copies ran while one was open for 6% of the time, Pallas kernels for 14%

profile of v5, /device:TPU:0, one launch (start us, length us, event | category | flops | bytes accessed | tf_op | source)
XLA Modules:
  0.0 72.5 jit_solution(14181387306448269915)
XLA Ops:
  0.6 1.0 %copy-done = f32[64,4,4,128]{3,2,1,0:T(4,128)S(1)} copy-done((f32[64,4,4,128]{3,2,1,0:T(4,128)S(1)}, f32[64,4,4,128]{3,2,1,0:T(4,128)}, u32[]{:S(2)}) %copy-start) | copy-done | bytes 524312
  1.7 0.8 %copy-done.1 = f32[125,125]{1,0:T(8,128)S(1)} copy-done((f32[125,125]{1,0:T(8,128)S(1)}, f32[125,125]{1,0:T(8,128)}, u32[]{:S(2)}) %copy-start.1) | copy-done | bytes 62524
  2.5 0.7 copy-done.2
  3.2 0.8 %pick.1 = (f32[125,125]{1,0:T(8,128)S(1)}, f32[17,16,128]{2,1,0:T(8,128)S(1)}, f32[16,16,128]{2,1,0:T(8,128)S(1)}, f32[17,16,128]{2,1,0:T(8,128)S(1)}, f32[16,16,128]{2,1,0:T(8,128)S(1)}) custom-call(f32[64,16,128]{2,1,0:T(8,128)S(1)} %bitcast.8, f32[16,128]{1,0:T(8,128)S(1)} %bitcast.10, f32[125,125]{1,0:T(8,128)S(1)} %copy-done.1), custom_call_target="tpu_custom_call" | custom-call | tf_op jit(solution)/shard_map/pick/pallas_call | solution.py:323
  4.6 1.1 %assemble.1 = (bf16[208,208]{1,0:T(8,128)(2,1)S(1)}, bf16[208,208]{1,0:T(8,128)(2,1)S(1)}, bf16[512,512]{1,0:T(8,128)(2,1)S(1)}, bf16[512,512]{1,0:T(8,128)(2,1)S(1)}, bf16[128,512]{1,0:T(8,128)(2,1)S(1)}) custom-call(f32[125,125]{1,0:T(8,128)S(1)} %get-tuple-element.42.cell_ref), custom_call_target="tpu_custom_call" | custom-call | tf_op jit(solution)/shard_map/assemble/pallas_call | solution.py:323
  6.5 6.8 %collective-permute-start.8 = (f32[4,8,512]{2,1,0:T(8,128)S(1)}, f32[4,8,512]{2,1,0:T(8,128)S(1)}, u32[]{:S(2)}, u32[]{:S(2)}) collective-permute-start(f32[4,8,512]{2,1,0:T(8,128)S(1)} %get-tuple-element.63), channel_id=1, source_target_pairs={{0,15},{1,0},{2,1},{3,2},{4,3},{5,4},{6,5},{7,6},{8,7},{9,8},{10,9... | collective-permute-start | bytes 196616 | tf_op jit(solution)/shard_map/ppermute | solution.py:318
  14.0 5.7 %collective-permute-start.1 = (f32[4,8,512]{2,1,0:T(8,128)S(1)}, f32[4,8,512]{2,1,0:T(8,128)S(1)}, u32[]{:S(2)}, u32[]{:S(2)}) collective-permute-start(f32[4,8,512]{2,1,0:T(8,128)S(1)} %get-tuple-element.48), channel_id=1, source_target_pairs={{0,15},{1,0},{2,1},{3,2},{4,3},{5,4},{6,5},{7,6},{8,7},{9,8},{10,9... | collective-permute-start | bytes 196616 | tf_op jit(solution)/shard_map/ppermute | solution.py:318
  20.3 1.0 %collective-permute-done.9.given_ref = f32[4,8,512]{2,1,0:T(8,128)S(1)} collective-permute-done((f32[4,8,512]{2,1,0:T(8,128)S(1)}, f32[4,8,512]{2,1,0:T(8,128)S(1)}, u32[]{:S(2)}, u32[]{:S(2)}) %collective-permute-start.9) | collective-permute-done | bytes 65568 | tf_op jit(solution)/shard_map/ppermute | solution.py:318
  21.3 0.8 %finish.6 = (f32[4,4,8,512]{3,2,1,0:T(8,128)S(1)}, f32[4,8,512]{2,1,0:T(8,128)S(1)}, f32[4,8,512]{2,1,0:T(8,128)S(1)}) custom-call(f32[4,4,8,512]{3,2,1,0:T(8,128)S(1)} %inner.9.inner_ref, f32[4,8,512]{2,1,0:T(8,128)S(1)} %collective-permute-done.8.halo_ref, f32[4,8,512]{2,1,0:T(8,128)S(1)} %collective-permute-done.9.given_ref, ...), custom_call_target="tpu_custom_call" | custom-call | tf_op jit(solution)/shard_map/finish/pallas_call | solution.py:323
  22.0 4.7 %collective-permute-start.10 = (f32[4,8,512]{2,1,0:T(8,128)S(1)}, f32[4,8,512]{2,1,0:T(8,128)S(1)}, u32[]{:S(2)}, u32[]{:S(2)}) collective-permute-start(f32[4,8,512]{2,1,0:T(8,128)S(1)} %get-tuple-element.67), channel_id=1, source_target_pairs={{0,15},{1,0},{2,1},{3,2},{4,3},{5,4},{6,5},{7,6},{8,7},{9,8},{10,9... | collective-permute-start | bytes 196616 | tf_op jit(solution)/shard_map/ppermute | solution.py:318
  27.6 0.8 %finish.4 = (f32[4,4,8,512]{3,2,1,0:T(8,128)S(1)}, f32[4,8,512]{2,1,0:T(8,128)S(1)}, f32[4,8,512]{2,1,0:T(8,128)S(1)}) custom-call(f32[4,4,8,512]{3,2,1,0:T(8,128)S(1)} %inner.6.inner_ref, f32[4,8,512]{2,1,0:T(8,128)S(1)} %collective-permute-done.1.halo_ref, f32[4,8,512]{2,1,0:T(8,128)S(1)} %collective-permute-done.2.given_ref, ...), custom_call_target="tpu_custom_call" | custom-call | tf_op jit(solution)/shard_map/finish/pallas_call | solution.py:323
  28.3 5.2 %collective-permute-start.3 = (f32[4,8,512]{2,1,0:T(8,128)S(1)}, f32[4,8,512]{2,1,0:T(8,128)S(1)}, u32[]{:S(2)}, u32[]{:S(2)}) collective-permute-start(f32[4,8,512]{2,1,0:T(8,128)S(1)} %get-tuple-element.51), channel_id=1, source_target_pairs={{0,15},{1,0},{2,1},{3,2},{4,3},{5,4},{6,5},{7,6},{8,7},{9,8},{10,9... | collective-permute-start | bytes 196616 | tf_op jit(solution)/shard_map/ppermute | solution.py:318
  33.6 1.3 %reshape.24 = bf16[16,4,4,2048]{3,2,1,0:T(4,128)(2,1)S(1)} reshape(bf16[256,4,4,128]{3,2,1,0:T(4,128)(2,1)} %param.7) | data formatting | bytes 2097152 | tf_op jit(solution)/shard_map/reshape | solution.py:399
  34.9 1.5 %copy.8 = bf16[16,4,4,2048]{3,2,0,1:T(4,128)(2,1)} copy(bf16[16,4,4,2048]{3,2,1,0:T(4,128)(2,1)S(1)} %reshape.24) | data formatting | bytes 2097152 | tf_op jit(solution)/shard_map/reshape | solution.py:399
  36.5 1.3 %reshape.25.refs_4_ = bf16[256,2048]{1,0:T(8,128)(2,1)S(1)} reshape(bf16[4,16,4,2048]{3,2,1,0:T(4,128)(2,1)} %bitcast.11) | data formatting | bytes 2097152 | tf_op jit(solution)/shard_map/reshape | solution.py:400
  38.8 0.8 %finish.7 = (f32[4,4,8,512]{3,2,1,0:T(8,128)S(1)}, f32[4,8,512]{2,1,0:T(8,128)S(1)}, f32[4,8,512]{2,1,0:T(8,128)S(1)}) custom-call(f32[4,4,8,512]{3,2,1,0:T(8,128)S(1)} %inner.10.inner_ref, f32[4,8,512]{2,1,0:T(8,128)S(1)} %collective-permute-done.10.halo_ref, f32[4,8,512]{2,1,0:T(8,128)S(1)} %collective-permute-done.11.given_ref, ...), custom_call_target="tpu_custom_call" | custom-call | tf_op jit(solution)/shard_map/finish/pallas_call | solution.py:323
  39.6 5.6 %collective-permute-start.12 = (f32[4,8,512]{2,1,0:T(8,128)S(1)}, f32[4,8,512]{2,1,0:T(8,128)S(1)}, u32[]{:S(2)}, u32[]{:S(2)}) collective-permute-start(f32[4,8,512]{2,1,0:T(8,128)S(1)} %get-tuple-element.70), channel_id=1, source_target_pairs={{0,15},{1,0},{2,1},{3,2},{4,3},{5,4},{6,5},{7,6},{8,7},{9,8},{10,9... | collective-permute-start | bytes 196616 | tf_op jit(solution)/shard_map/ppermute | solution.py:318
  45.2 0.8 %finish.5 = (f32[4,4,8,512]{3,2,1,0:T(8,128)S(1)}, f32[4,8,512]{2,1,0:T(8,128)S(1)}, f32[4,8,512]{2,1,0:T(8,128)S(1)}) custom-call(f32[4,4,8,512]{3,2,1,0:T(8,128)S(1)} %inner.7.inner_ref, f32[4,8,512]{2,1,0:T(8,128)S(1)} %collective-permute-done.3.halo_ref, f32[4,8,512]{2,1,0:T(8,128)S(1)} %collective-permute-done.4.given_ref, ...), custom_call_target="tpu_custom_call" | custom-call | tf_op jit(solution)/shard_map/finish/pallas_call | solution.py:323
  46.0 5.6 %collective-permute-start.5 = (f32[4,8,512]{2,1,0:T(8,128)S(1)}, f32[4,8,512]{2,1,0:T(8,128)S(1)}, u32[]{:S(2)}, u32[]{:S(2)}) collective-permute-start(f32[4,8,512]{2,1,0:T(8,128)S(1)} %get-tuple-element.54), channel_id=1, source_target_pairs={{0,15},{1,0},{2,1},{3,2},{4,3},{5,4},{6,5},{7,6},{8,7},{9,8},{10,9... | collective-permute-start | bytes 196616 | tf_op jit(solution)/shard_map/ppermute | solution.py:318
  53.8 5.6 %collective-permute-done.6.refs_2_ = f32[4,8,512]{2,1,0:T(8,128)S(1)} collective-permute-done((f32[4,8,512]{2,1,0:T(8,128)S(1)}, f32[4,8,512]{2,1,0:T(8,128)S(1)}, u32[]{:S(2)}, u32[]{:S(2)}) %collective-permute-start.6) | collective-permute-done | bytes 65568 | tf_op jit(solution)/shard_map/ppermute | solution.py:318
  60.2 1.3 %collective-permute-done.14.refs_2_ = f32[16,16,128]{2,1,0:T(8,128)S(1)} collective-permute-done((f32[16,16,128]{2,1,0:T(8,128)S(1)}, f32[16,16,128]{2,1,0:T(8,128)S(1)}, u32[]{:S(2)}, u32[]{:S(2)}) %collective-permute-start.14) | collective-permute-done | bytes 131104 | tf_op jit(solution)/shard_map/ppermute | solution.py:318
  61.6 1.2 %margin.1 = (f32[2,64,128]{2,1,0:T(8,128)S(1)}, f32[64,16,128]{2,1,0:T(8,128)}) custom-call(f32[16,16,128]{2,1,0:T(8,128)S(1)} %get-tuple-element.57.refs_0_, f32[16,16,128]{2,1,0:T(8,128)S(1)} %get-tuple-element.72.refs_1_, f32[16,16,128]{2,1,0:T(8,128)S(1)} %collective-permute-done.14.refs_2_, f32[16,16,128]{2,1,0:T(8,128)S(1)} %collective-permute-done.15.refs_3_, ...), custom_call_target="tpu_custom_call" | custom-call | tf_op jit(solution)/shard_map/margin/pallas_call | solution.py:323
  62.8 9.0 %all_to_all.5.tiles_ref = f32[32,4,128]{2,1,0:T(4,128)S(1)} all-to-all(f32[32,4,128]{2,1,0:T(4,128)S(1)} %bitcast.9), channel_id=1, replica_groups=mesh['px'=2,'py'=16] {'px','py'}, dimensions={0} | all-to-all | bytes 131072 | tf_op jit(solution)/shard_map/all_to_all | solution.py:432
  71.8 0.7 tile_sum.1
  (37 shorter events, 7.4 us)
Async XLA Ops:
  0.6 1.0 %copy-start = (f32[64,4,4,128]{3,2,1,0:T(4,128)S(1)}, f32[64,4,4,128]{3,2,1,0:T(4,128)}, u32[]{:S(2)}) copy-start(f32[64,4,4,128]{3,2,1,0:T(4,128)} %param.4) | copy-start | bytes 1572868
  1.7 0.8 %copy-start.1 = (f32[125,125]{1,0:T(8,128)S(1)}, f32[125,125]{1,0:T(8,128)}, u32[]{:S(2)}) copy-start(f32[125,125]{1,0:T(8,128)} %cell_ref.1) | copy-start | bytes 187504
  2.5 0.7 copy-start.2
  4.0 9.3 %collective-permute-start = (f32[17,16,128]{2,1,0:T(8,128)S(1)}, f32[17,16,128]{2,1,0:T(8,128)S(1)}, u32[]{:S(2)}, u32[]{:S(2)}) collective-permute-start(f32[17,16,128]{2,1,0:T(8,128)S(1)} %get-tuple-element.41), channel_id=1, source_target_pairs={{0,16},{16,0},{1,17},{17,1},{2,18},{18,2},{3,19},{19,3},{4,20},{20... | collective-permute-start | bytes 417800 | tf_op jit(solution)/shard_map/ppermute | solution.py:318
  4.6 1.3 %collective-permute-start.7 = (f32[16,16,128]{2,1,0:T(8,128)S(1)}, f32[16,16,128]{2,1,0:T(8,128)S(1)}, u32[]{:S(2)}, u32[]{:S(2)}) collective-permute-start(f32[16,16,128]{2,1,0:T(8,128)S(1)} %get-tuple-element.59), channel_id=1, source_target_pairs={{0,16},{16,0},{1,17},{17,1},{2,18},{18,2},{3,19},{19,3},{4,20},{20... | collective-permute-start | bytes 393224 | tf_op jit(solution)/shard_map/ppermute | solution.py:318
  6.5 13.8 %collective-permute-start.8 = (f32[4,8,512]{2,1,0:T(8,128)S(1)}, f32[4,8,512]{2,1,0:T(8,128)S(1)}, u32[]{:S(2)}, u32[]{:S(2)}) collective-permute-start(f32[4,8,512]{2,1,0:T(8,128)S(1)} %get-tuple-element.63), channel_id=1, source_target_pairs={{0,15},{1,0},{2,1},{3,2},{4,3},{5,4},{6,5},{7,6},{8,7},{9,8},{10,9... | collective-permute-start | bytes 196616 | tf_op jit(solution)/shard_map/ppermute | solution.py:318
  13.3 7.9 %collective-permute-start.9 = (f32[4,8,512]{2,1,0:T(8,128)S(1)}, f32[4,8,512]{2,1,0:T(8,128)S(1)}, u32[]{:S(2)}, u32[]{:S(2)}) collective-permute-start(f32[4,8,512]{2,1,0:T(8,128)S(1)} %get-tuple-element.64), channel_id=1, source_target_pairs={{0,1},{1,2},{2,3},{3,4},{4,5},{5,6},{6,7},{7,8},{8,9},{9,10},{10,1... | collective-permute-start | bytes 196616 | tf_op jit(solution)/shard_map/ppermute | solution.py:318
  14.0 13.2 %collective-permute-start.1 = (f32[4,8,512]{2,1,0:T(8,128)S(1)}, f32[4,8,512]{2,1,0:T(8,128)S(1)}, u32[]{:S(2)}, u32[]{:S(2)}) collective-permute-start(f32[4,8,512]{2,1,0:T(8,128)S(1)} %get-tuple-element.48), channel_id=1, source_target_pairs={{0,15},{1,0},{2,1},{3,2},{4,3},{5,4},{6,5},{7,6},{8,7},{9,8},{10,9... | collective-permute-start | bytes 196616 | tf_op jit(solution)/shard_map/ppermute | solution.py:318
  19.6 8.0 %collective-permute-start.2 = (f32[4,8,512]{2,1,0:T(8,128)S(1)}, f32[4,8,512]{2,1,0:T(8,128)S(1)}, u32[]{:S(2)}, u32[]{:S(2)}) collective-permute-start(f32[4,8,512]{2,1,0:T(8,128)S(1)} %get-tuple-element.49), channel_id=1, source_target_pairs={{0,1},{1,2},{2,3},{3,4},{4,5},{5,6},{6,7},{7,8},{8,9},{9,10},{10,1... | collective-permute-start | bytes 196616 | tf_op jit(solution)/shard_map/ppermute | solution.py:318
  22.0 16.8 %collective-permute-start.10 = (f32[4,8,512]{2,1,0:T(8,128)S(1)}, f32[4,8,512]{2,1,0:T(8,128)S(1)}, u32[]{:S(2)}, u32[]{:S(2)}) collective-permute-start(f32[4,8,512]{2,1,0:T(8,128)S(1)} %get-tuple-element.67), channel_id=1, source_target_pairs={{0,15},{1,0},{2,1},{3,2},{4,3},{5,4},{6,5},{7,6},{8,7},{9,8},{10,9... | collective-permute-start | bytes 196616 | tf_op jit(solution)/shard_map/ppermute | solution.py:318
  26.7 12.1 %collective-permute-start.11 = (f32[4,8,512]{2,1,0:T(8,128)S(1)}, f32[4,8,512]{2,1,0:T(8,128)S(1)}, u32[]{:S(2)}, u32[]{:S(2)}) collective-permute-start(f32[4,8,512]{2,1,0:T(8,128)S(1)} %get-tuple-element.68), channel_id=1, source_target_pairs={{0,1},{1,2},{2,3},{3,4},{4,5},{5,6},{6,7},{7,8},{8,9},{9,10},{10,1... | collective-permute-start | bytes 196616 | tf_op jit(solution)/shard_map/ppermute | solution.py:318
  28.3 16.9 %collective-permute-start.3 = (f32[4,8,512]{2,1,0:T(8,128)S(1)}, f32[4,8,512]{2,1,0:T(8,128)S(1)}, u32[]{:S(2)}, u32[]{:S(2)}) collective-permute-start(f32[4,8,512]{2,1,0:T(8,128)S(1)} %get-tuple-element.51), channel_id=1, source_target_pairs={{0,15},{1,0},{2,1},{3,2},{4,3},{5,4},{6,5},{7,6},{8,7},{9,8},{10,9... | collective-permute-start | bytes 196616 | tf_op jit(solution)/shard_map/ppermute | solution.py:318
  33.6 11.6 %collective-permute-start.4 = (f32[4,8,512]{2,1,0:T(8,128)S(1)}, f32[4,8,512]{2,1,0:T(8,128)S(1)}, u32[]{:S(2)}, u32[]{:S(2)}) collective-permute-start(f32[4,8,512]{2,1,0:T(8,128)S(1)} %get-tuple-element.52), channel_id=1, source_target_pairs={{0,1},{1,2},{2,3},{3,4},{4,5},{5,6},{6,7},{7,8},{8,9},{9,10},{10,1... | collective-permute-start | bytes 196616 | tf_op jit(solution)/shard_map/ppermute | solution.py:318
  39.6 13.0 %collective-permute-start.12 = (f32[4,8,512]{2,1,0:T(8,128)S(1)}, f32[4,8,512]{2,1,0:T(8,128)S(1)}, u32[]{:S(2)}, u32[]{:S(2)}) collective-permute-start(f32[4,8,512]{2,1,0:T(8,128)S(1)} %get-tuple-element.70), channel_id=1, source_target_pairs={{0,15},{1,0},{2,1},{3,2},{4,3},{5,4},{6,5},{7,6},{8,7},{9,8},{10,9... | collective-permute-start | bytes 196616 | tf_op jit(solution)/shard_map/ppermute | solution.py:318
  45.2 7.9 %collective-permute-start.13 = (f32[4,8,512]{2,1,0:T(8,128)S(1)}, f32[4,8,512]{2,1,0:T(8,128)S(1)}, u32[]{:S(2)}, u32[]{:S(2)}) collective-permute-start(f32[4,8,512]{2,1,0:T(8,128)S(1)} %get-tuple-element.71), channel_id=1, source_target_pairs={{0,1},{1,2},{2,3},{3,4},{4,5},{5,6},{6,7},{7,8},{8,9},{9,10},{10,1... | collective-permute-start | bytes 196616 | tf_op jit(solution)/shard_map/ppermute | solution.py:318
  46.0 7.9 %collective-permute-start.5 = (f32[4,8,512]{2,1,0:T(8,128)S(1)}, f32[4,8,512]{2,1,0:T(8,128)S(1)}, u32[]{:S(2)}, u32[]{:S(2)}) collective-permute-start(f32[4,8,512]{2,1,0:T(8,128)S(1)} %get-tuple-element.54), channel_id=1, source_target_pairs={{0,15},{1,0},{2,1},{3,2},{4,3},{5,4},{6,5},{7,6},{8,7},{9,8},{10,9... | collective-permute-start | bytes 196616 | tf_op jit(solution)/shard_map/ppermute | solution.py:318
  51.6 7.9 %collective-permute-start.6 = (f32[4,8,512]{2,1,0:T(8,128)S(1)}, f32[4,8,512]{2,1,0:T(8,128)S(1)}, u32[]{:S(2)}, u32[]{:S(2)}) collective-permute-start(f32[4,8,512]{2,1,0:T(8,128)S(1)} %get-tuple-element.55), channel_id=1, source_target_pairs={{0,1},{1,2},{2,3},{3,4},{4,5},{5,6},{6,7},{7,8},{8,9},{9,10},{10,1... | collective-permute-start | bytes 196616 | tf_op jit(solution)/shard_map/ppermute | solution.py:318
  53.8 6.5 %collective-permute-start.15 = (f32[16,16,128]{2,1,0:T(8,128)S(1)}, f32[16,16,128]{2,1,0:T(8,128)S(1)}, u32[]{:S(2)}, u32[]{:S(2)}) collective-permute-start(f32[16,16,128]{2,1,0:T(8,128)S(1)} %get-tuple-element.74), channel_id=1, source_target_pairs={{0,16},{16,0},{1,17},{17,1},{2,18},{18,2},{3,19},{19,3},{4,20},{20... | collective-permute-start | bytes 393224 | tf_op jit(solution)/shard_map/ppermute | solution.py:318
  60.2 1.4 %collective-permute-start.14 = (f32[16,16,128]{2,1,0:T(8,128)S(1)}, f32[16,16,128]{2,1,0:T(8,128)S(1)}, u32[]{:S(2)}, u32[]{:S(2)}) collective-permute-start(f32[16,16,128]{2,1,0:T(8,128)S(1)} %get-tuple-element.73), channel_id=1, source_target_pairs={{0,16},{16,0},{1,17},{17,1},{2,18},{18,2},{3,19},{19,3},{4,20},{20... | collective-permute-start | bytes 393224 | tf_op jit(solution)/shard_map/ppermute | solution.py:318

commit v6 on v5

--- a/solution.py
+++ b/solution.py
@@ -14,7 +14,6 @@
 f32 = jnp.float32
 whole = pl.BlockSpec(memory_space=pltpu.VMEM)
 anywhere = pl.BlockSpec(memory_space=pl.ANY)
-in_hbm = pl.BlockSpec(memory_space=pltpu.HBM)
 params = pltpu.CompilerParams(vmem_limit_bytes=48 * 2**20)
 
 BLOCKS = (
@@ -79,27 +78,6 @@
     spread_ref[...] = jnp.where(same, 1.0, 0.0).astype(bf16)
 
 
-def pick_kernel(parts_x, chunks, span_ref, potential_ref, cell_ref, *refs):
-    out_refs, sems = refs[:-1], refs[-1]
-    me = lax.axis_index("px")
-    copies = []
-
-    def copy(source, target):
-        copies.append(pltpu.make_async_copy(source, target, sems.at[len(copies)]))
-        copies[-1].start()
-
-    count = span_ref.shape[0] // (parts_x * chunks)
-    for step in range(parts_x):
-        for chunk in range(chunks):
-            start = (lax.rem(me + step, parts_x) * chunks + chunk) * count
-            target = out_refs[1 + step * chunks + chunk]
-            copy(span_ref.at[pl.ds(start, count)], target.at[pl.ds(0, count)])
-            if chunk == 0:
-                copy(potential_ref, target.at[count])
-    copy(cell_ref, out_refs[0])
-    wait_all(copies)
-
-
 def roll_cells(value, cells, forward):
     out = []
     place = lax.broadcasted_iota(jnp.int32, (value.shape[0], lanes), 1) % cells
@@ -128,15 +106,20 @@
     return [roll_cells(row, cells, True) for row in rows]
 
 
-def send_edges(high_ref, low_ref, value, down_ref, up_ref, cells):
-    nodes = down_ref.shape[1]
+def even_place():
+    return lax.rem(lax.axis_index("py"), 2) == 0
+
+
+def send_edges(high_ref, low_ref, value, pair_ref, other_ref, cells):
+    nodes = pair_ref.shape[1]
+    even = even_place()
     own = [value[iz, iy] for iz in range(4) for iy in range(4)]
     stacked = jnp.concatenate(own + roll_rows(own[:4], cells), 0)
     rows, cols = slice(20 * nodes, PADDED * nodes), slice(0, 20 * nodes)
     up = fold_last(three_products(high_ref[rows, cols], low_ref[rows, cols], stacked), nodes, cells)
     for iz in range(4):
-        down_ref[iz] = value[iz, 0]
-        up_ref[iz] = up[iz]
+        pair_ref[iz] = jnp.where(even, up[iz], value[iz, 0])
+        other_ref[iz] = jnp.where(even, value[iz, 0], up[iz])
 
 
 def start_all(copies):
@@ -156,7 +139,7 @@
 
 def to_cells_kernel(cells, second, parts_x, states, *refs):
     part_refs = refs[:parts_x]
-    order_ref, high_ref, low_ref, w_ref, down_ref, up_ref = refs[parts_x:]
+    order_ref, high_ref, low_ref, w_ref, pair_ref, other_ref = refs[parts_x:]
     nodes = w_ref.shape[2]
     group = lanes // cells
     groups = states // group
@@ -173,13 +156,13 @@
             parts = [part[iy * nodes : (iy + 1) * nodes, iz * lanes : (iz + 1) * lanes] for part in values]
             value[iz, iy] = parts[0] if groups == 1 else jnp.concatenate(parts, 1)
             w_ref[iz, iy] = value[iz, iy]
-    send_edges(high_ref, low_ref, value, down_ref, up_ref, cells)
+    send_edges(high_ref, low_ref, value, pair_ref, other_ref, cells)
 
 
 def levels_kernel(second, parts_x, *refs):
     part_refs, (spread_ref, levels_ref) = refs[:parts_x], refs[parts_x:]
     nodes = levels_ref.shape[2]
-    rows = jnp.concatenate(gathered(part_refs, part_refs[0].shape[0] - 1, second), 0)
+    rows = jnp.concatenate(gathered(part_refs, 0, second), 0)
     high, low = two_parts(rows)
     spread = dot(high, spread_ref[...]) + dot(low, spread_ref[...])
     for y in range(second):
@@ -220,10 +203,12 @@
             out_ref[iz, iy] = total if step == 0 else total - before_ref[iz, iy]
 
 
-def finish(cells, step, inner_ref, halo_ref, given_ref, high_ref, low_ref):
+def finish(cells, step, inner_ref, pair_ref, other_ref, high_ref, low_ref):
     nodes, width = inner_ref.shape[2:]
     inside = 20 * nodes
-    halo = [halo_ref[iz] for iz in range(4)]
+    even = even_place()
+    halo = [jnp.where(even, pair_ref[iz], other_ref[iz]) for iz in range(4)]
+    given = [jnp.where(even, other_ref[iz], pair_ref[iz]) for iz in range(4)]
     halo = jnp.concatenate(halo + roll_rows(halo[:1], cells) + [jnp.zeros((nodes, width), f32)], 0)
     product = three_products(high_ref[:inside, inside:], low_ref[:inside, inside:], halo)
     result = {}
@@ -235,22 +220,22 @@
                 start = (16 + iy) * nodes
                 total = total + roll_cells(product[start : start + nodes], cells, False)
             if iy == 0:
-                total = total + given_ref[iz]
+                total = total + given[iz]
             result[iz, iy] = inner_ref[iz, iy] + total * scale_of(step)
     return result
 
 
-def finish_kernel(cells, step, inner_ref, halo_ref, given_ref, high_ref, low_ref, next_ref, down_ref, up_ref):
-    value = finish(cells, step, inner_ref, halo_ref, given_ref, high_ref, low_ref)
+def finish_kernel(cells, step, inner_ref, from_pair_ref, from_other_ref, high_ref, low_ref, next_ref, pair_ref, other_ref):
+    value = finish(cells, step, inner_ref, from_pair_ref, from_other_ref, high_ref, low_ref)
     for (iz, iy), part in value.items():
         next_ref[iz, iy] = part
-    send_edges(high_ref, low_ref, value, down_ref, up_ref, cells)
+    send_edges(high_ref, low_ref, value, pair_ref, other_ref, cells)
 
 
 def from_cells_kernel(cells, second, parts_x, *refs):
-    inner_ref, halo_ref, given_ref, high_ref, low_ref, order_ref = refs[:6]
+    inner_ref, pair_ref, other_ref, high_ref, low_ref, order_ref = refs[:6]
     out_refs = refs[6:]
-    value = finish(cells, 2, inner_ref, halo_ref, given_ref, high_ref, low_ref)
+    value = finish(cells, 2, inner_ref, pair_ref, other_ref, high_ref, low_ref)
     states, layer, thickness = out_refs[0].shape
     first = layer // second
     nodes = parts_x * first
@@ -313,6 +298,16 @@
     out_ref[...] = jnp.concatenate([total[:, g * tile_rows : (g + 1) * tile_rows] for g in range(groups)], 0)
 
 
+def swapped(edges):
+    count = lax.axis_size("py")
+    pairs = [(place, place + 1) for place in range(0, count, 2)]
+    others = [(place + 1, (place + 2) % count) for place in range(0, count, 2)]
+    pair, other = edges
+    other = lax.ppermute(other, "py", others + [(b, a) for a, b in others])
+    pair = lax.ppermute(pair, "py", pairs + [(b, a) for a, b in pairs])
+    return [pair, other]
+
+
 def shifted(value, axis, steps):
     count = lax.axis_size(axis)
     return lax.ppermute(value, axis, [(source, (source + steps) % count) for source in range(count)])
@@ -346,77 +341,64 @@
     matrix = jax.ShapeDtypeStruct((rows, rows), bf16)
     table = jax.ShapeDtypeStruct((group, group), bf16)
 
-    chunks = 2
+    chunks = 1
     count = mine // chunks
     width = count * cells
     field = jax.ShapeDtypeStruct((4, 4, nodes, width), f32)
     message = jax.ShapeDtypeStruct((4, nodes, width), f32)
     part = jax.ShapeDtypeStruct((count, layer, thickness), f32)
-    first_part = jax.ShapeDtypeStruct((count + 1, layer, thickness), f32)
-    cell_matrix, *parts = kernel_call(
-        functools.partial(pick_kernel, parts_x, chunks),
-        [jax.ShapeDtypeStruct(cell_matrix.shape, f32)] + ([first_part] + [part] * (chunks - 1)) * parts_x,
-        [span.reshape(states, layer, thickness), potential.reshape(layer, thickness), cell_matrix],
-        "pick",
-        scratch=[pltpu.SemaphoreType.DMA((parts_x * (chunks + 1) + 1,))],
-        in_specs=[in_hbm] * 3,
-    )
-    places = [parts[:chunks]] + [
-        [shifted(parts[step * chunks + chunk], "px", step) for chunk in range(chunks)]
-        for step in reversed(others)
-    ]
+    me = lax.axis_index("px")
+    span_rows = span.reshape(states, layer, thickness)
+
+    def part_for(step):
+        return lax.dynamic_slice_in_dim(span_rows, lax.rem(me + step, parts_x) * mine, mine, 0)
+
+    parts = [part_for(0)] + [shifted(part_for(step), "px", step) for step in reversed(others)]
     high, low, order, back, spread = kernel_call(
         functools.partial(matrix_kernel, cells, nodes),
         [matrix, matrix, table, table, jax.ShapeDtypeStruct((thickness, 4 * lanes), bf16)],
         [cell_matrix],
         "assemble",
     )
+    field_now, *edges = kernel_call(
+        functools.partial(to_cells_kernel, cells, second, parts_x, count),
+        [field, message, message],
+        parts + [order, high, low],
+        "to_cells",
+    )
+    edges = swapped(edges)
+    level_rows = potential.reshape(1, layer, thickness)
     levels = kernel_call(
         functools.partial(levels_kernel, second, parts_x),
         jax.ShapeDtypeStruct((4, 4, nodes, lanes), f32),
-        [place[0] for place in places] + [spread],
+        [level_rows] + [shifted(level_rows, "px", step) for step in reversed(others)] + [spread],
         "levels",
     )
 
-    fields, before, edges = [None] * chunks, [None] * chunks, [None] * chunks
-    for chunk in range(chunks):
-        fields[chunk], *edges[chunk] = kernel_call(
-            functools.partial(to_cells_kernel, cells, second, parts_x, count),
-            [field, message, message],
-            [place[chunk] for place in places] + [order, high, low],
-            "to_cells",
-        )
-        edges[chunk] = [shifted(edges[chunk][0], "py", -1), shifted(edges[chunk][1], "py", 1)]
+    before = None
+    for step in range(3):
+        operands = [field_now, levels, high, low] + ([before] if step > 0 else [])
+        inner = kernel_call(functools.partial(inner_kernel, cells, step), field, operands, "inner")
+        operands = [inner] + edges + [high, low]
+        if step < 2:
+            before = field_now
+            field_now, *edges = kernel_call(
+                functools.partial(finish_kernel, cells, step), [field, message, message], operands, "finish"
+            )
+            edges = swapped(edges)
+        else:
+            pieces = kernel_call(
+                functools.partial(from_cells_kernel, cells, second, parts_x),
+                [part] * parts_x,
+                operands + [back],
+                "from_cells",
+            )
+    received = [pieces[0]] + [shifted(pieces[step], "px", step) for step in others]
+
     tile_rows, tile_cols = mine, block_count // parts_y
     groups = min(tile_cols, lanes // tile_rows)
-    pieces = [None] * chunks
-    for step in range(3):
-        for chunk in range(chunks):
-            operands = [fields[chunk], levels, high, low] + ([before[chunk]] if step > 0 else [])
-            inner = kernel_call(functools.partial(inner_kernel, cells, step), field, operands, "inner")
-            if chunk == chunks - 1 and step == 0:
-                block, inner = lax.optimization_barrier((block, inner))
-                ordered = block.reshape(parts_y, groups, tile_cols // groups, layer * thickness)
-                ordered = ordered.transpose(1, 0, 2, 3).reshape(block_count, layer * thickness)
-            if chunk == chunks - 1 and step == 1:
-                ordered, inner = lax.optimization_barrier((ordered, inner))
-            operands = [inner] + edges[chunk] + [high, low]
-            if step < 2:
-                before[chunk] = fields[chunk]
-                fields[chunk], *edges[chunk] = kernel_call(
-                    functools.partial(finish_kernel, cells, step), [field, message, message], operands, "finish"
-                )
-                edges[chunk] = [shifted(edges[chunk][0], "py", -1), shifted(edges[chunk][1], "py", 1)]
-            else:
-                pieces[chunk] = kernel_call(
-                    functools.partial(from_cells_kernel, cells, second, parts_x),
-                    [part] * parts_x,
-                    operands + [back],
-                    "from_cells",
-                )
-    received = [pieces[chunk][0] for chunk in range(chunks)]
-    for step in others:
-        received += [shifted(pieces[chunk][step], "px", step) for chunk in range(chunks)]
+    ordered = block.reshape(parts_y, groups, tile_cols // groups, layer * thickness)
+    ordered = ordered.transpose(1, 0, 2, 3).reshape(block_count, layer * thickness)
     tiles, filtered = kernel_call(
         functools.partial(margin_kernel, parts_x, chunks),
         [

time: 72.8 us -> 51.7 us (0.71)
  starting transfers between devices: 34.4 us -> 17 us
  local copies, waits for them, and re-layouts: 6.79 us -> 2.24 us
  Pallas kernels: 12.5 us -> 8.48 us
  blocking collectives: 9.02 us -> 11.6 us
  waiting for transfers between devices: 8.96 us -> 11.4 us
    ppermute x16 -> x3, starting transfers between devices: 34.4 us -> 0.59 us  [shifted(): lax.ppermute(value, axis, [(source, (source + steps) % count) for source...]
    ppermute x0 -> x6, starting transfers between devices: none -> 16.4 us  [the longest x3 12.9 us: swapped(): other = lax.ppermute(other, 'py', others + [(b, a) for a, b in others])]
    ppermute x0 -> x6, waiting for transfers between devices: none -> 9.84 us  [the longest x3 9.21 us: swapped(): other = lax.ppermute(other, 'py', others + [(b, a) for a, b in others])]
    ppermute x16 -> x3, waiting for transfers between devices: 8.96 us -> 1.55 us  [shifted(): lax.ppermute(value, axis, [(source, (source + steps) % count) for source...]
    pallas_call x19 -> x11, Pallas kernels: 12.5 us -> 8.48 us  [kernel_call(): pl.pallas_call(body, out_shape=outs, in_specs=in_specs or [whole] * len(o...]
    all_to_all x1, blocking collectives: 9.02 us -> 11.6 us  [local(): tiles = lax.all_to_all(tiles, ('px', 'py'), 0, 0, tiled=True)]
    unnamed x6, local copies, waits for them, and re-layouts: 2.57 us -> 0.02 us
    reshape x2, local copies, waits for them, and re-layouts: 2.89 us -> 0.84 us  [local(): block.reshape(parts_y, groups, tile_cols // groups, layer * thickness)]
  transfers between devices with their start and end apart: 16 -> 9, of which waited for: 6 -> 7; matrix products, arithmetic and copies ran while one was open for 6% -> 2% of each run, Pallas kernels for 14% -> 6%
where the time goes in v6:
time: 51.7 us; the launch traced here: 51.5 us
  starting transfers between devices  17 us (33%)
  blocking collectives  11.6 us (22%)
  waiting for transfers between devices  11.4 us (22%)
  Pallas kernels  8.48 us (16%)
  local copies, waits for them, and re-layouts  2.24 us (4%)
  between operations  0.78 us (2%)
    ppermute x3, starting transfers between devices, swapped(): other = lax.ppermute(other, 'py', others + [(b, a) for a, b in others])  12.9 us
    all_to_all x1, blocking collectives, local(): tiles = lax.all_to_all(tiles, ('px', 'py'), 0, 0, tiled=True)  11.6 us
    ppermute x3, waiting for transfers between devices, swapped(): other = lax.ppermute(other, 'py', others + [(b, a) for a, b in others])  9.21 us
    pallas_call x11, Pallas kernels, kernel_call(): pl.pallas_call(body, out_shape=outs, in_specs=in_specs or [whole] * len(o...  8.48 us
    ppermute x3, starting transfers between devices, swapped(): pair = lax.ppermute(pair, 'py', pairs + [(b, a) for a, b in pairs])  3.47 us
    ppermute x3, waiting for transfers between devices, shifted(): lax.ppermute(value, axis, [(source, (source + steps) % count) for source...  1.55 us
    dynamic_slice x1, local copies, waits for them, and re-layouts, part_for(): lax.dynamic_slice_in_dim(span_rows, lax.rem(me + step, parts_x) * mine, m...  1.1 us
  transfers between devices with their start and end apart: 9, of which 7 were waited for; matrix products, arithmetic and copies ran while one was open for 2% of the time, Pallas kernels for 6%

profile of v6, /device:TPU:0, one launch (start us, length us, event | category | flops | bytes accessed | tf_op | source)
XLA Modules:
  0.0 51.5 jit_solution(13755484262286702088)
XLA Ops:
  0.7 1.1 %constant_dynamic-slice_fusion = (f32[32,16,128]{2,1,0:T(8,128)S(1)}, f32[32,16,128]{2,1,0:T(8,128)S(1)}) fusion(f32[64,16,128]{2,1,0:T(8,128)} %bitcast.12, s32[]{:T(128)S(6)} %select_n.7, s32[]{:T(128)S(6)} %select_n.6), kind=kLoop, calls=%fused_computation.1 | loop fusion | bytes 1048584 | tf_op jit(solution)/shard_map/dynamic_slice | solution.py:354
  1.8 0.5 %collective-permute-start = (f32[32,16,128]{2,1,0:T(8,128)S(1)}, f32[32,16,128]{2,1,0:T(8,128)S(1)}, u32[]{:S(2)}, u32[]{:S(2)}) collective-permute-start(f32[32,16,128]{2,1,0:T(8,128)S(1)} %get-tuple-element.38), channel_id=1, source_target_pairs={{0,16},{16,0},{1,17},{17,1},{2,18},{18,2},{3,19},{19,3},{4,20},{20... | collective-permute-start | bytes 786440 | tf_op jit(solution)/shard_map/ppermute | solution.py:313
  2.3 1.1 %assemble.1 = (bf16[208,208]{1,0:T(8,128)(2,1)S(1)}, bf16[208,208]{1,0:T(8,128)(2,1)S(1)}, bf16[512,512]{1,0:T(8,128)(2,1)S(1)}, bf16[512,512]{1,0:T(8,128)(2,1)S(1)}, bf16[128,512]{1,0:T(8,128)(2,1)S(1)}) custom-call(f32[125,125]{1,0:T(8,128)S(1)} %copy-done), custom_call_target="tpu_custom_call" | custom-call | tf_op jit(solution)/shard_map/assemble/pallas_call | solution.py:318
  3.5 0.8 %to_cells.1 = (f32[4,4,8,1024]{3,2,1,0:T(8,128)S(1)}, f32[4,8,1024]{2,1,0:T(8,128)S(1)}, f32[4,8,1024]{2,1,0:T(8,128)S(1)}) custom-call(f32[32,16,128]{2,1,0:T(8,128)S(1)} %get-tuple-element.39.refs_0_, f32[32,16,128]{2,1,0:T(8,128)S(1)} %collective-permute-done.refs_1_, bf16[512,512]{1,0:T(8,128)(2,1)S(1)} %get-tuple-element.20.refs_2_, ...), custom_call_target="tpu_custom_call" | custom-call | tf_op jit(solution)/shard_map/to_cells/pallas_call | solution.py:318
  4.2 2.9 %collective-permute-start.2 = (f32[4,8,1024]{2,1,0:T(8,128)S(1)}, f32[4,8,1024]{2,1,0:T(8,128)S(1)}, u32[]{:S(2)}, u32[]{:S(2)}) collective-permute-start(f32[4,8,1024]{2,1,0:T(8,128)S(1)} %get-tuple-element.25), channel_id=1, source_target_pairs={{0,1},{2,3},{4,5},{6,7},{8,9},{10,11},{12,13},{14,15},{1,0},{3,2},... | collective-permute-start | bytes 393224 | tf_op jit(solution)/shard_map/ppermute | solution.py:307
  7.2 4.5 %collective-permute-start.3 = (f32[4,8,1024]{2,1,0:T(8,128)S(1)}, f32[4,8,1024]{2,1,0:T(8,128)S(1)}, u32[]{:S(2)}, u32[]{:S(2)}) collective-permute-start(f32[4,8,1024]{2,1,0:T(8,128)S(1)} %get-tuple-element.26), channel_id=1, source_target_pairs={{1,2},{3,4},{5,6},{7,8},{9,10},{11,12},{13,14},{15,0},{2,1},{4,3},... | collective-permute-start | bytes 393224 | tf_op jit(solution)/shard_map/ppermute | solution.py:306
  11.7 1.2 %collective-permute-done.1.refs_1_ = f32[1,16,128]{2,1,0:T(8,128)S(1)} collective-permute-done((f32[1,16,128]{2,1,0:T(8,128)S(1)}, f32[1,16,128]{2,1,0:T(8,128)S(1)}, u32[]{:S(2)}, u32[]{:S(2)}) %collective-permute-start.1) | collective-permute-done | bytes 8224 | tf_op jit(solution)/shard_map/ppermute | solution.py:313
  13.0 0.7 %inner.3.inner_ref = f32[4,4,8,1024]{3,2,1,0:T(8,128)S(1)} custom-call(f32[4,4,8,1024]{3,2,1,0:T(8,128)S(1)} %get-tuple-element.23.refs_0_.refs_4_, f32[4,4,8,128]{3,2,1,0:T(8,128)S(1)} %levels.1.refs_1_, bf16[208,208]{1,0:T(8,128)(2,1)S(1)} %get-tuple-element.21.refs_3_.refs_2_.high_ref, bf16[208,208]{1,0:T(8,128)(2,1)S(1)} %get-tuple-element.22.refs_4_.refs_3_.low_ref), custom_call_target="tpu_custom_call" | custom-call | tf_op jit(solution)/shard_map/inner/pallas_call | solution.py:318
  13.7 2.3 %collective-permute-done.3.from_other_ref = f32[4,8,1024]{2,1,0:T(8,128)S(1)} collective-permute-done((f32[4,8,1024]{2,1,0:T(8,128)S(1)}, f32[4,8,1024]{2,1,0:T(8,128)S(1)}, u32[]{:S(2)}, u32[]{:S(2)}) %collective-permute-start.3) | collective-permute-done | bytes 131104 | tf_op jit(solution)/shard_map/ppermute | solution.py:306
  16.0 1.0 %finish.2 = (f32[4,4,8,1024]{3,2,1,0:T(8,128)S(1)}, f32[4,8,1024]{2,1,0:T(8,128)S(1)}, f32[4,8,1024]{2,1,0:T(8,128)S(1)}) custom-call(f32[4,4,8,1024]{3,2,1,0:T(8,128)S(1)} %inner.3.inner_ref, f32[4,8,1024]{2,1,0:T(8,128)S(1)} %collective-permute-done.2.from_pair_ref, f32[4,8,1024]{2,1,0:T(8,128)S(1)} %collective-permute-done.3.from_other_ref, ...), custom_call_target="tpu_custom_call" | custom-call | tf_op jit(solution)/shard_map/finish/pallas_call | solution.py:318
  17.0 0.5 collective-permute-start.4
  17.5 4.2 %collective-permute-start.5 = (f32[4,8,1024]{2,1,0:T(8,128)S(1)}, f32[4,8,1024]{2,1,0:T(8,128)S(1)}, u32[]{:S(2)}, u32[]{:S(2)}) collective-permute-start(f32[4,8,1024]{2,1,0:T(8,128)S(1)} %get-tuple-element.29), channel_id=1, source_target_pairs={{1,2},{3,4},{5,6},{7,8},{9,10},{11,12},{13,14},{15,0},{2,1},{4,3},... | collective-permute-start | bytes 393224 | tf_op jit(solution)/shard_map/ppermute | solution.py:306
  21.7 0.6 %inner.4.inner_ref = f32[4,4,8,1024]{3,2,1,0:T(8,128)S(1)} custom-call(f32[4,4,8,1024]{3,2,1,0:T(8,128)S(1)} %get-tuple-element.27.refs_0_.refs_4_, f32[4,4,8,128]{3,2,1,0:T(8,128)S(1)} %levels.1.refs_1_, bf16[208,208]{1,0:T(8,128)(2,1)S(1)} %get-tuple-element.21.refs_3_.refs_2_.high_ref, bf16[208,208]{1,0:T(8,128)(2,1)S(1)} %get-tuple-element.22.refs_4_.refs_3_.low_ref, ...), custom_call_target="tpu_custom_call" | custom-call | tf_op jit(solution)/shard_map/inner/pallas_call | solution.py:318
  22.3 0.6 %collective-permute-done.4.from_pair_ref = f32[4,8,1024]{2,1,0:T(8,128)S(1)} collective-permute-done((f32[4,8,1024]{2,1,0:T(8,128)S(1)}, f32[4,8,1024]{2,1,0:T(8,128)S(1)}, u32[]{:S(2)}, u32[]{:S(2)}) %collective-permute-start.4) | collective-permute-done | bytes 131104 | tf_op jit(solution)/shard_map/ppermute | solution.py:307
  22.9 3.2 %collective-permute-done.5.from_other_ref = f32[4,8,1024]{2,1,0:T(8,128)S(1)} collective-permute-done((f32[4,8,1024]{2,1,0:T(8,128)S(1)}, f32[4,8,1024]{2,1,0:T(8,128)S(1)}, u32[]{:S(2)}, u32[]{:S(2)}) %collective-permute-start.5) | collective-permute-done | bytes 131104 | tf_op jit(solution)/shard_map/ppermute | solution.py:306
  26.1 1.0 %finish.3 = (f32[4,4,8,1024]{3,2,1,0:T(8,128)S(1)}, f32[4,8,1024]{2,1,0:T(8,128)S(1)}, f32[4,8,1024]{2,1,0:T(8,128)S(1)}) custom-call(f32[4,4,8,1024]{3,2,1,0:T(8,128)S(1)} %inner.4.inner_ref, f32[4,8,1024]{2,1,0:T(8,128)S(1)} %collective-permute-done.4.from_pair_ref, f32[4,8,1024]{2,1,0:T(8,128)S(1)} %collective-permute-done.5.from_other_ref, ...), custom_call_target="tpu_custom_call" | custom-call | tf_op jit(solution)/shard_map/finish/pallas_call | solution.py:318
  27.1 4.2 %collective-permute-start.7 = (f32[4,8,1024]{2,1,0:T(8,128)S(1)}, f32[4,8,1024]{2,1,0:T(8,128)S(1)}, u32[]{:S(2)}, u32[]{:S(2)}) collective-permute-start(f32[4,8,1024]{2,1,0:T(8,128)S(1)} %get-tuple-element.32), channel_id=1, source_target_pairs={{1,2},{3,4},{5,6},{7,8},{9,10},{11,12},{13,14},{15,0},{2,1},{4,3},... | collective-permute-start | bytes 393224 | tf_op jit(solution)/shard_map/ppermute | solution.py:306
  31.3 0.6 %inner.5.refs_0_ = f32[4,4,8,1024]{3,2,1,0:T(8,128)S(1)} custom-call(f32[4,4,8,1024]{3,2,1,0:T(8,128)S(1)} %get-tuple-element.30.refs_0_, f32[4,4,8,128]{3,2,1,0:T(8,128)S(1)} %levels.1.refs_1_, bf16[208,208]{1,0:T(8,128)(2,1)S(1)} %get-tuple-element.21.refs_3_.refs_2_.high_ref, bf16[208,208]{1,0:T(8,128)(2,1)S(1)} %get-tuple-element.22.refs_4_.refs_3_.low_ref, ...), custom_call_target="tpu_custom_call" | custom-call | tf_op jit(solution)/shard_map/inner/pallas_call | solution.py:318
  32.1 3.7 %collective-permute-done.7.refs_2_ = f32[4,8,1024]{2,1,0:T(8,128)S(1)} collective-permute-done((f32[4,8,1024]{2,1,0:T(8,128)S(1)}, f32[4,8,1024]{2,1,0:T(8,128)S(1)}, u32[]{:S(2)}, u32[]{:S(2)}) %collective-permute-start.7) | collective-permute-done | bytes 131104 | tf_op jit(solution)/shard_map/ppermute | solution.py:306
  35.7 0.9 %from_cells.1 = (f32[32,16,128]{2,1,0:T(8,128)S(1)}, f32[32,16,128]{2,1,0:T(8,128)S(1)}) custom-call(f32[4,4,8,1024]{3,2,1,0:T(8,128)S(1)} %inner.5.refs_0_, f32[4,8,1024]{2,1,0:T(8,128)S(1)} %collective-permute-done.6.refs_1_, f32[4,8,1024]{2,1,0:T(8,128)S(1)} %collective-permute-done.7.refs_2_, ...), custom_call_target="tpu_custom_call" | custom-call | tf_op jit(solution)/shard_map/from_cells/pallas_call | solution.py:318
  37.0 0.6 %copy.8 = bf16[16,4,4,2048]{3,2,0,1:T(4,128)(2,1)S(1)} copy(bf16[16,4,4,2048]{3,2,1,0:T(4,128)(2,1)S(1)} %reshape.24) | data formatting | bytes 2097152 | tf_op jit(solution)/shard_map/reshape | solution.py:400
  38.3 0.9 %margin.1 = (f32[2,64,128]{2,1,0:T(8,128)S(1)}, f32[64,16,128]{2,1,0:T(8,128)}) custom-call(f32[32,16,128]{2,1,0:T(8,128)S(1)} %get-tuple-element.34.refs_0_, f32[32,16,128]{2,1,0:T(8,128)S(1)} %collective-permute-done.8.refs_1_, bf16[256,2048]{1,0:T(8,128)(2,1)S(1)} %reshape.25.refs_2_), custom_call_target="tpu_custom_call" | custom-call | tf_op jit(solution)/shard_map/margin/pallas_call | solution.py:318
  39.1 11.6 %all_to_all.5.tiles_ref = f32[32,4,128]{2,1,0:T(4,128)S(1)} all-to-all(f32[32,4,128]{2,1,0:T(4,128)S(1)} %bitcast.8), channel_id=1, replica_groups=mesh['px'=2,'py'=16] {'px','py'}, dimensions={0} | all-to-all | bytes 131072 | tf_op jit(solution)/shard_map/all_to_all | solution.py:414
  50.8 0.7 %tile_sum.1 = f32[16,32]{1,0:T(8,128)} custom-call(f32[32,4,128]{2,1,0:T(4,128)S(1)} %all_to_all.5.tiles_ref), custom_call_target="tpu_custom_call" | custom-call | tf_op jit(solution)/shard_map/tile_sum/pallas_call | solution.py:318
  (16 shorter events, 1.3 us)
Async XLA Ops:
  0.6 1.6 %copy-start = (f32[125,125]{1,0:T(8,128)S(1)}, f32[125,125]{1,0:T(8,128)}, u32[]{:S(2)}) copy-start(f32[125,125]{1,0:T(8,128)} %cell_ref.1) | copy-start | bytes 187504
  1.8 1.7 %collective-permute-start = (f32[32,16,128]{2,1,0:T(8,128)S(1)}, f32[32,16,128]{2,1,0:T(8,128)S(1)}, u32[]{:S(2)}, u32[]{:S(2)}) collective-permute-start(f32[32,16,128]{2,1,0:T(8,128)S(1)} %get-tuple-element.38), channel_id=1, source_target_pairs={{0,16},{16,0},{1,17},{17,1},{2,18},{18,2},{3,19},{19,3},{4,20},{20... | collective-permute-start | bytes 786440 | tf_op jit(solution)/shard_map/ppermute | solution.py:313
  3.4 8.2 %copy-start.1 = (f32[4,4,128]{2,1,0:T(4,128)S(1)}, f32[4,4,128]{2,1,0:T(4,128)}, u32[]{:S(2)}) copy-start(f32[4,4,128]{2,1,0:T(4,128)} %param.5) | copy-start | bytes 24580
  4.2 9.4 %collective-permute-start.2 = (f32[4,8,1024]{2,1,0:T(8,128)S(1)}, f32[4,8,1024]{2,1,0:T(8,128)S(1)}, u32[]{:S(2)}, u32[]{:S(2)}) collective-permute-start(f32[4,8,1024]{2,1,0:T(8,128)S(1)} %get-tuple-element.25), channel_id=1, source_target_pairs={{0,1},{2,3},{4,5},{6,7},{8,9},{10,11},{12,13},{14,15},{1,0},{3,2},... | collective-permute-start | bytes 393224 | tf_op jit(solution)/shard_map/ppermute | solution.py:307
  7.2 8.9 %collective-permute-start.3 = (f32[4,8,1024]{2,1,0:T(8,128)S(1)}, f32[4,8,1024]{2,1,0:T(8,128)S(1)}, u32[]{:S(2)}, u32[]{:S(2)}) collective-permute-start(f32[4,8,1024]{2,1,0:T(8,128)S(1)} %get-tuple-element.26), channel_id=1, source_target_pairs={{1,2},{3,4},{5,6},{7,8},{9,10},{11,12},{13,14},{15,0},{2,1},{4,3},... | collective-permute-start | bytes 393224 | tf_op jit(solution)/shard_map/ppermute | solution.py:306
  11.7 1.2 %collective-permute-start.1 = (f32[1,16,128]{2,1,0:T(8,128)S(1)}, f32[1,16,128]{2,1,0:T(8,128)S(1)}, u32[]{:S(2)}, u32[]{:S(2)}) collective-permute-start(f32[1,16,128]{2,1,0:T(8,128)S(1)} %bitcast.9), channel_id=1, source_target_pairs={{0,16},{16,0},{1,17},{17,1},{2,18},{18,2},{3,19},{19,3},{4,20},{20... | collective-permute-start | bytes 24584 | tf_op jit(solution)/shard_map/ppermute | solution.py:313
  17.0 5.9 %collective-permute-start.4 = (f32[4,8,1024]{2,1,0:T(8,128)S(1)}, f32[4,8,1024]{2,1,0:T(8,128)S(1)}, u32[]{:S(2)}, u32[]{:S(2)}) collective-permute-start(f32[4,8,1024]{2,1,0:T(8,128)S(1)} %get-tuple-element.28), channel_id=1, source_target_pairs={{0,1},{2,3},{4,5},{6,7},{8,9},{10,11},{12,13},{14,15},{1,0},{3,2},... | collective-permute-start | bytes 393224 | tf_op jit(solution)/shard_map/ppermute | solution.py:307
  17.5 8.6 %collective-permute-start.5 = (f32[4,8,1024]{2,1,0:T(8,128)S(1)}, f32[4,8,1024]{2,1,0:T(8,128)S(1)}, u32[]{:S(2)}, u32[]{:S(2)}) collective-permute-start(f32[4,8,1024]{2,1,0:T(8,128)S(1)} %get-tuple-element.29), channel_id=1, source_target_pairs={{1,2},{3,4},{5,6},{7,8},{9,10},{11,12},{13,14},{15,0},{2,1},{4,3},... | collective-permute-start | bytes 393224 | tf_op jit(solution)/shard_map/ppermute | solution.py:306
  27.0 5.0 %collective-permute-start.6 = (f32[4,8,1024]{2,1,0:T(8,128)S(1)}, f32[4,8,1024]{2,1,0:T(8,128)S(1)}, u32[]{:S(2)}, u32[]{:S(2)}) collective-permute-start(f32[4,8,1024]{2,1,0:T(8,128)S(1)} %get-tuple-element.31), channel_id=1, source_target_pairs={{0,1},{2,3},{4,5},{6,7},{8,9},{10,11},{12,13},{14,15},{1,0},{3,2},... | collective-permute-start | bytes 393224 | tf_op jit(solution)/shard_map/ppermute | solution.py:307
  27.1 8.6 %collective-permute-start.7 = (f32[4,8,1024]{2,1,0:T(8,128)S(1)}, f32[4,8,1024]{2,1,0:T(8,128)S(1)}, u32[]{:S(2)}, u32[]{:S(2)}) collective-permute-start(f32[4,8,1024]{2,1,0:T(8,128)S(1)} %get-tuple-element.32), channel_id=1, source_target_pairs={{1,2},{3,4},{5,6},{7,8},{9,10},{11,12},{13,14},{15,0},{2,1},{4,3},... | collective-permute-start | bytes 393224 | tf_op jit(solution)/shard_map/ppermute | solution.py:306
  32.0 4.8 %copy-start.2 = (bf16[256,4,4,128]{3,2,1,0:T(4,128)(2,1)S(1)}, bf16[256,4,4,128]{3,2,1,0:T(4,128)(2,1)}, u32[]{:S(2)}) copy-start(bf16[256,4,4,128]{3,2,1,0:T(4,128)(2,1)} %param.7) | copy-start | bytes 3145732
  36.7 1.6 %collective-permute-start.8 = (f32[32,16,128]{2,1,0:T(8,128)S(1)}, f32[32,16,128]{2,1,0:T(8,128)S(1)}, u32[]{:S(2)}, u32[]{:S(2)}) collective-permute-start(f32[32,16,128]{2,1,0:T(8,128)S(1)} %get-tuple-element.35), channel_id=1, source_target_pairs={{0,16},{16,0},{1,17},{17,1},{2,18},{18,2},{3,19},{19,3},{4,20},{20... | collective-permute-start | bytes 786440 | tf_op jit(solution)/shard_map/ppermute | solution.py:313

commit v7 on v6

--- a/solution.py
+++ b/solution.py
@@ -58,7 +58,7 @@
     return (state * cells + cell) * 4 + node
 
 
-def matrix_kernel(cells, nodes, cell_ref, high_ref, low_ref, order_ref, back_ref, spread_ref):
+def matrix_kernel(cells, nodes, cell_ref, high_ref, low_ref, halo_ref, order_ref):
     rest = cell_ref[...]
     size, count = high_ref.shape[0], cell_ref.shape[0]
     tables = [chosen(size, count, functools.partial(select_target, cell, nodes)) for cell in range(nodes // 4)]
@@ -69,13 +69,26 @@
         for table in tables:
             left = dot(table, part).astype(bf16)
             total = total + lax.dot_general(left, table, (((1,), (1,)), ((), ())), preferred_element_type=f32)
-    high_ref[...], low_ref[...] = two_parts(total)
+    high, low = two_parts(total)
+    high_ref[...], low_ref[...] = high, low
+    inside = halo_ref.shape[0]
+    from_halo = total[:inside, inside:]
+    high = from_halo.astype(bf16).astype(f32)
+    halo_ref[...] = jnp.concatenate([high, high, from_halo - high], 1).astype(bf16)
     order_ref[...] = chosen(*order_ref.shape, functools.partial(cell_order_target, cells))
-    back_ref[...] = chosen(*back_ref.shape, functools.partial(raw_order_target, cells))
-    row = lax.broadcasted_iota(jnp.int32, spread_ref.shape, 0)
-    col = lax.broadcasted_iota(jnp.int32, spread_ref.shape, 1)
-    same = row == lax.rem(col, cells) * 4 + lax.div(col, lanes)
-    spread_ref[...] = jnp.where(same, 1.0, 0.0).astype(bf16)
+
+
+def widen_kernel(block_ref, out_ref):
+    out_ref[...] = block_ref[...].astype(f32)
+
+
+def margin_rows_kernel(layer, parts_y, wide_ref, out_ref):
+    thickness = wide_ref.shape[1]
+    tile_cols = out_ref.shape[0] // parts_y
+    for n in range(layer):
+        for col in range(tile_cols):
+            lines = wide_ref[pl.ds(col * layer + n, parts_y, stride=tile_cols * layer), :]
+            out_ref[pl.ds(col * parts_y, parts_y), pl.ds(n * thickness, thickness)] = lines.astype(bf16)
 
 
 def roll_cells(value, cells, forward):
@@ -160,11 +173,16 @@
 
 
 def levels_kernel(second, parts_x, *refs):
-    part_refs, (spread_ref, levels_ref) = refs[:parts_x], refs[parts_x:]
+    part_refs, levels_ref = refs[:parts_x], refs[parts_x]
     nodes = levels_ref.shape[2]
+    thickness = part_refs[0].shape[2]
+    cells = thickness // 4
+    row = lax.broadcasted_iota(jnp.int32, (thickness, 4 * lanes), 0)
+    col = lax.broadcasted_iota(jnp.int32, (thickness, 4 * lanes), 1)
+    table = jnp.where(row == lax.rem(col, cells) * 4 + lax.div(col, lanes), 1.0, 0.0).astype(bf16)
     rows = jnp.concatenate(gathered(part_refs, 0, second), 0)
     high, low = two_parts(rows)
-    spread = dot(high, spread_ref[...]) + dot(low, spread_ref[...])
+    spread = dot(high, table) + dot(low, table)
     for y in range(second):
         for iz in range(4):
             levels_ref[iz, y] = spread[y * nodes : (y + 1) * nodes, iz * lanes : (iz + 1) * lanes] - centre
@@ -176,7 +194,11 @@
 
 def inner_kernel(cells, step, *refs):
     w_ref, levels_ref, high_ref, low_ref = refs[:4]
-    before_ref, out_ref = refs[4] if step > 0 else None, refs[-1]
+    before_ref = refs[4] if step > 0 else None
+    out_ref = refs[4 if step == 0 else 5]
+    if step == 2:
+        back_ref = refs[6]
+        back_ref[...] = chosen(*back_ref.shape, functools.partial(raw_order_target, cells))
     nodes, width = w_ref.shape[2:]
     groups = width // lanes
     inside = 20 * nodes
@@ -203,14 +225,14 @@
             out_ref[iz, iy] = total if step == 0 else total - before_ref[iz, iy]
 
 
-def finish(cells, step, inner_ref, pair_ref, other_ref, high_ref, low_ref):
+def finish(cells, step, inner_ref, pair_ref, other_ref, matrix_ref):
     nodes, width = inner_ref.shape[2:]
-    inside = 20 * nodes
     even = even_place()
     halo = [jnp.where(even, pair_ref[iz], other_ref[iz]) for iz in range(4)]
     given = [jnp.where(even, other_ref[iz], pair_ref[iz]) for iz in range(4)]
     halo = jnp.concatenate(halo + roll_rows(halo[:1], cells) + [jnp.zeros((nodes, width), f32)], 0)
-    product = three_products(high_ref[:inside, inside:], low_ref[:inside, inside:], halo)
+    halo_high, halo_low = two_parts(halo)
+    product = dot(matrix_ref[...], jnp.concatenate([halo_high, halo_low, halo_high], 0))
     result = {}
     for iz in range(4):
         for iy in range(4):
@@ -225,17 +247,17 @@
     return result
 
 
-def finish_kernel(cells, step, inner_ref, from_pair_ref, from_other_ref, high_ref, low_ref, next_ref, pair_ref, other_ref):
-    value = finish(cells, step, inner_ref, from_pair_ref, from_other_ref, high_ref, low_ref)
+def finish_kernel(cells, step, inner_ref, from_pair_ref, from_other_ref, matrix_ref, high_ref, low_ref, next_ref, pair_ref, other_ref):
+    value = finish(cells, step, inner_ref, from_pair_ref, from_other_ref, matrix_ref)
     for (iz, iy), part in value.items():
         next_ref[iz, iy] = part
     send_edges(high_ref, low_ref, value, pair_ref, other_ref, cells)
 
 
-def from_cells_kernel(cells, second, parts_x, *refs):
-    inner_ref, pair_ref, other_ref, high_ref, low_ref, order_ref = refs[:6]
-    out_refs = refs[6:]
-    value = finish(cells, 2, inner_ref, pair_ref, other_ref, high_ref, low_ref)
+def last_kernel(cells, second, parts_x, parts_y, *refs):
+    inner_ref, pair_ref, other_ref, matrix_ref, order_ref = refs[:5]
+    block_refs, out_refs, tiles_ref = refs[5 : 5 + parts_x], refs[5 + parts_x : -1], refs[-1]
+    value = finish(cells, 2, inner_ref, pair_ref, other_ref, matrix_ref)
     states, layer, thickness = out_refs[0].shape
     first = layer // second
     nodes = parts_x * first
@@ -259,43 +281,36 @@
                     lines = part[start : start + first, s * thickness : (s + 1) * thickness]
                     out_ref[h * group + s, pl.ds(y, first, stride=second), :] = lines
 
-
-def margin_kernel(parts_x, chunks, *refs):
-    part_refs, block_ref = refs[: parts_x * chunks], refs[parts_x * chunks]
-    tiles_ref, filtered_ref, sems = refs[parts_x * chunks + 1 :]
+    product = None
+    for out_ref, block_ref in zip(out_refs, block_refs):
+        flat = out_ref.reshape(states * layer, thickness)
+        lines = [flat[pl.ds(n, states, stride=layer), :].astype(bf16) for n in range(layer)]
+        added = lax.dot_general(
+            block_ref[...], jnp.concatenate(lines, 1), (((1,), (1,)), ((), ())), preferred_element_type=f32
+        )
+        product = added if product is None else product + added
+    groups = tiles_ref.shape[1] // states
+    group_cols = tiles_ref.shape[0] // parts_y
+    for col in range(group_cols):
+        starts = [(group * group_cols + col) * parts_y for group in range(groups)]
+        lines = jnp.concatenate([product[start : start + parts_y] for start in starts], 1)
+        tiles_ref[pl.ds(col, parts_y, stride=group_cols), :] = lines
+
+
+def result_kernel(parts_x, tiles_ref, *refs):
+    part_refs, (out_ref, filtered_ref, sems) = refs[:parts_x], refs[parts_x:]
     me = lax.axis_index("px")
-    count, layer, thickness = part_refs[0].shape
-    mine = count * chunks
-    owners = [lax.rem(me + (parts_x - step), parts_x) for step in range(parts_x)]
+    count = filtered_ref.shape[0] // parts_x
     copies = []
-    for place, part_ref in enumerate(part_refs):
-        start = owners[place // chunks] * mine + place % chunks * count
-        target = filtered_ref.at[pl.ds(start, count)]
-        copies.append(pltpu.make_async_copy(part_ref, target, sems.at[place]))
+    for step, part_ref in enumerate(part_refs):
+        owner = lax.rem(me + (parts_x - step), parts_x)
+        copies.append(pltpu.make_async_copy(part_ref, filtered_ref.at[pl.ds(owner * count, count)], sems.at[step]))
     start_all(copies)
-    flat = [ref.reshape(count * layer, thickness) for ref in part_refs]
-    lines = [
-        jnp.concatenate([ref[pl.ds(n, count, stride=layer), :].astype(bf16) for ref in flat], 0)
-        for n in range(layer)
-    ]
-    product = lax.dot_general(
-        block_ref[...], jnp.concatenate(lines, 1), (((1,), (1,)), ((), ())), preferred_element_type=f32
-    )
-    group_rows = tiles_ref.shape[1]
-    groups = block_ref.shape[0] // group_rows
-    for step in range(parts_x):
-        columns = slice(step * mine, (step + 1) * mine)
-        tiles_ref[owners[step]] = jnp.concatenate(
-            [product[g * group_rows : (g + 1) * group_rows, columns] for g in range(groups)], 1
-        )
-    wait_all(copies)
-
-
-def sum_kernel(tiles_ref, out_ref):
     total = jnp.sum(tiles_ref[...], axis=0)
     tile_rows = out_ref.shape[1]
     groups = total.shape[1] // tile_rows
     out_ref[...] = jnp.concatenate([total[:, g * tile_rows : (g + 1) * tile_rows] for g in range(groups)], 0)
+    wait_all(copies)
 
 
 def swapped(edges):
@@ -337,31 +352,32 @@
     rows = PADDED * nodes
     others = range(1, parts_x)
 
-    group = lanes // cells * thickness
+    width = mine * cells
     matrix = jax.ShapeDtypeStruct((rows, rows), bf16)
-    table = jax.ShapeDtypeStruct((group, group), bf16)
-
-    chunks = 1
-    count = mine // chunks
-    width = count * cells
+    from_halo = jax.ShapeDtypeStruct((20 * nodes, 3 * (rows - 20 * nodes)), bf16)
+    table = jax.ShapeDtypeStruct((4 * lanes, 4 * lanes), bf16)
     field = jax.ShapeDtypeStruct((4, 4, nodes, width), f32)
     message = jax.ShapeDtypeStruct((4, nodes, width), f32)
-    part = jax.ShapeDtypeStruct((count, layer, thickness), f32)
+    part = jax.ShapeDtypeStruct((mine, layer, thickness), f32)
+
     me = lax.axis_index("px")
     span_rows = span.reshape(states, layer, thickness)
 
     def part_for(step):
         return lax.dynamic_slice_in_dim(span_rows, lax.rem(me + step, parts_x) * mine, mine, 0)
 
-    parts = [part_for(0)] + [shifted(part_for(step), "px", step) for step in reversed(others)]
-    high, low, order, back, spread = kernel_call(
+    sent = [part_for(step) for step in others]
+    sent, span_rows = lax.optimization_barrier((sent, span_rows))
+    parts = [shifted(piece, "px", step) for step, piece in enumerate(sent, 1)]
+    parts = [part_for(0)] + parts[::-1]
+    high, low, halo_matrix, order = kernel_call(
         functools.partial(matrix_kernel, cells, nodes),
-        [matrix, matrix, table, table, jax.ShapeDtypeStruct((thickness, 4 * lanes), bf16)],
+        [matrix, matrix, from_halo, table],
         [cell_matrix],
         "assemble",
     )
     field_now, *edges = kernel_call(
-        functools.partial(to_cells_kernel, cells, second, parts_x, count),
+        functools.partial(to_cells_kernel, cells, second, parts_x, mine),
         [field, message, message],
         parts + [order, high, low],
         "to_cells",
@@ -371,48 +387,70 @@
     levels = kernel_call(
         functools.partial(levels_kernel, second, parts_x),
         jax.ShapeDtypeStruct((4, 4, nodes, lanes), f32),
-        [level_rows] + [shifted(level_rows, "px", step) for step in reversed(others)] + [spread],
+        [level_rows] + [shifted(level_rows, "px", step) for step in reversed(others)],
         "levels",
     )
 
+    tile_rows, tile_cols = mine, block_count // parts_y
+    groups = min(tile_cols, lanes // tile_rows)
     before = None
     for step in range(3):
         operands = [field_now, levels, high, low] + ([before] if step > 0 else [])
-        inner = kernel_call(functools.partial(inner_kernel, cells, step), field, operands, "inner")
-        operands = [inner] + edges + [high, low]
+        inner = kernel_call(
+            functools.partial(inner_kernel, cells, step), [field] + [table] * (step == 2), operands, "inner"
+        )
+        inner, back = inner if step == 2 else (inner[0], None)
+        if step == 0:
+            inner, block = lax.optimization_barrier((inner, block))
+            wide = kernel_call(
+                widen_kernel,
+                jax.ShapeDtypeStruct((block_count * layer, thickness), f32),
+                [block.reshape(block_count * layer, thickness)],
+                "widen",
+            )
+            wides = [wide] + [shifted(wide, "px", step) for step in others]
+        if step == 1:
+            blocks = [
+                kernel_call(
+                    functools.partial(margin_rows_kernel, layer, parts_y),
+                    jax.ShapeDtypeStruct((block_count, layer * thickness), bf16),
+                    [wide],
+                    "margin_rows",
+                )
+                for wide in lax.optimization_barrier((inner, wides))[1]
+            ]
+        operands = [inner] + edges + [halo_matrix]
         if step < 2:
             before = field_now
             field_now, *edges = kernel_call(
-                functools.partial(finish_kernel, cells, step), [field, message, message], operands, "finish"
+                functools.partial(finish_kernel, cells, step),
+                [field, message, message],
+                operands + [high, low],
+                "finish",
             )
             edges = swapped(edges)
         else:
-            pieces = kernel_call(
-                functools.partial(from_cells_kernel, cells, second, parts_x),
-                [part] * parts_x,
-                operands + [back],
-                "from_cells",
+            *pieces, tiles = kernel_call(
+                functools.partial(last_kernel, cells, second, parts_x, parts_y),
+                [part] * parts_x + [jax.ShapeDtypeStruct((block_count // groups, groups * tile_rows), f32)],
+                operands + [back] + [blocks[0]] + blocks[:0:-1],
+                "last",
             )
-    received = [pieces[0]] + [shifted(pieces[step], "px", step) for step in others]
-
-    tile_rows, tile_cols = mine, block_count // parts_y
-    groups = min(tile_cols, lanes // tile_rows)
-    ordered = block.reshape(parts_y, groups, tile_cols // groups, layer * thickness)
-    ordered = ordered.transpose(1, 0, 2, 3).reshape(block_count, layer * thickness)
-    tiles, filtered = kernel_call(
-        functools.partial(margin_kernel, parts_x, chunks),
+
+    pieces = [pieces[0]] + [shifted(pieces[step], "px", step) for step in others]
+    tiles = tiles.reshape(parts_y, tile_cols // groups, groups * tile_rows)
+    tiles = lax.all_to_all(tiles, "py", 0, 0, tiled=True)
+    margin, filtered = kernel_call(
+        functools.partial(result_kernel, parts_x),
         [
-            jax.ShapeDtypeStruct((parts_x, block_count // groups, groups * tile_rows), f32),
+            jax.ShapeDtypeStruct((tile_cols, tile_rows), f32),
             jax.ShapeDtypeStruct((states, layer, thickness), f32),
         ],
-        received + [ordered],
-        "margin",
-        scratch=[pltpu.SemaphoreType.DMA((parts_x * chunks,))],
+        [tiles] + pieces,
+        "result",
+        scratch=[pltpu.SemaphoreType.DMA((parts_x,))],
         out_specs=[whole, anywhere],
     )
-    tiles = tiles.reshape(parts_x * parts_y, tile_cols // groups, groups * tile_rows)
-    tiles = lax.all_to_all(tiles, ("px", "py"), 0, 0, tiled=True)
-    margin = kernel_call(sum_kernel, jax.ShapeDtypeStruct((tile_cols, tile_rows), f32), [tiles], "tile_sum")
     return filtered.reshape(span.shape), margin.T
 
 

time: 51.7 us -> 54.8 us (1.060)
  Pallas kernels: 8.48 us -> 11.8 us
  waiting for transfers between devices: 11.4 us -> 9.46 us
  blocking collectives: 11.6 us -> 12.7 us
    pallas_call x11 -> x13, Pallas kernels: 8.48 us -> 11.8 us  [kernel_call(): pl.pallas_call(body, out_shape=outs, in_specs=in_specs or [whole] * len(o...]
    unnamed x6 -> x8, local copies, waits for them, and re-layouts: 0.02 us -> 2.55 us
    ppermute x3, waiting for transfers between devices: 9.21 us -> 6.87 us  [swapped(): other = lax.ppermute(other, 'py', others + [(b, a) for a, b in others])]
    ppermute x3, waiting for transfers between devices: 0.63 us -> 2.56 us  [swapped(): pair = lax.ppermute(pair, 'py', pairs + [(b, a) for a, b in pairs])]
    ppermute x3 -> x4, waiting for transfers between devices: 1.55 us -> 0.02 us  [shifted(): lax.ppermute(value, axis, [(source, (source + steps) % count) for source...]
    reshape x3 -> x0, local copies, waits for them, and re-layouts: 1.12 us -> none  [the longest x2 0.84 us: local(): block.reshape(parts_y, groups, tile_cols // groups, layer * thickness)]
    all_to_all x1, blocking collectives: 11.6 us -> 12.7 us  [local(): tiles = lax.all_to_all(tiles, 'py', 0, 0, tiled=True)]
    dynamic_slice x1 -> x2, local copies, waits for them, and re-layouts: 1.1 us -> 0.04 us  [part_for(): lax.dynamic_slice_in_dim(span_rows, lax.rem(me + step, parts_x) * mine, m...]
  transfers between devices with their start and end apart: 9 -> 10, of which waited for: 7 -> 5; matrix products, arithmetic and copies ran while one was open for 2% -> 0% of each run, Pallas kernels for 6% -> 12%
where the time goes in v7:
time: 54.8 us; the launch traced here: 54.6 us
  starting transfers between devices  17.2 us (31%)
  blocking collectives  12.7 us (23%)
  Pallas kernels  11.8 us (22%)
  waiting for transfers between devices  9.46 us (17%)
  local copies, waits for them, and re-layouts  2.59 us (5%)
  between operations  0.8 us (1%)
    ppermute x3, starting transfers between devices, swapped(): other = lax.ppermute(other, 'py', others + [(b, a) for a, b in others])  12.9 us
    all_to_all x1, blocking collectives, local(): tiles = lax.all_to_all(tiles, 'py', 0, 0, tiled=True)  12.7 us
    pallas_call x13, Pallas kernels, kernel_call(): pl.pallas_call(body, out_shape=outs, in_specs=in_specs or [whole] * len(o...  11.8 us
    ppermute x3, waiting for transfers between devices, swapped(): other = lax.ppermute(other, 'py', others + [(b, a) for a, b in others])  6.87 us
    ppermute x3, starting transfers between devices, swapped(): pair = lax.ppermute(pair, 'py', pairs + [(b, a) for a, b in pairs])  3.14 us
    ppermute x3, waiting for transfers between devices, swapped(): pair = lax.ppermute(pair, 'py', pairs + [(b, a) for a, b in pairs])  2.56 us
    unnamed x8, local copies, waits for them, and re-layouts  2.55 us
    ppermute x4, starting transfers between devices, shifted(): lax.ppermute(value, axis, [(source, (source + steps) % count) for source...  1.16 us
  transfers between devices with their start and end apart: 10, of which 5 were waited for; matrix products, arithmetic and copies ran while one was open for 0% of the time, Pallas kernels for 12%

profile of v7, /device:TPU:0, one launch (start us, length us, event | category | flops | bytes accessed | tf_op | source)
XLA Modules:
  0.0 54.6 jit_solution(9059989676927837736)
XLA Ops:
  0.7 1.0 %copy-done = f32[64,4,4,128]{3,2,1,0:T(4,128)S(1)} copy-done((f32[64,4,4,128]{3,2,1,0:T(4,128)S(1)}, f32[64,4,4,128]{3,2,1,0:T(4,128)}, u32[]{:S(2)}) %copy-start) | copy-done | bytes 524312
  2.3 0.8 %copy-done.2 = f32[125,125]{1,0:T(8,128)S(1)} copy-done((f32[125,125]{1,0:T(8,128)S(1)}, f32[125,125]{1,0:T(8,128)}, u32[]{:S(2)}) %copy-start.2) | copy-done | bytes 62524
  3.2 0.9 %assemble.1 = (bf16[208,208]{1,0:T(8,128)(2,1)S(1)}, bf16[208,208]{1,0:T(8,128)(2,1)S(1)}, bf16[160,144]{1,0:T(8,128)(2,1)S(1)}, bf16[512,512]{1,0:T(8,128)(2,1)S(1)}) custom-call(f32[125,125]{1,0:T(8,128)S(1)} %copy-done.2), custom_call_target="tpu_custom_call" | custom-call | tf_op jit(solution)/shard_map/assemble/pallas_call | solution.py:333
  4.1 0.7 %copy-done.3 = f32[4,4,128]{2,1,0:T(4,128)S(1)} copy-done((f32[4,4,128]{2,1,0:T(4,128)S(1)}, f32[4,4,128]{2,1,0:T(4,128)}, u32[]{:S(2)}) %copy-start.3) | copy-done | bytes 8216
  5.0 0.8 %to_cells.1 = (f32[4,4,8,1024]{3,2,1,0:T(8,128)S(1)}, f32[4,8,1024]{2,1,0:T(8,128)S(1)}, f32[4,8,1024]{2,1,0:T(8,128)S(1)}) custom-call(f32[32,16,128]{2,1,0:T(8,128)S(1)} %constant_dynamic-slice_fusion.refs_0_, f32[32,16,128]{2,1,0:T(8,128)S(1)} %collective-permute-done.refs_1_, bf16[512,512]{1,0:T(8,128)(2,1)S(1)} %get-tuple-element.30.refs_2_, ...), custom_call_target="tpu_custom_call" | custom-call | tf_op jit(solution)/shard_map/to_cells/pallas_call | solution.py:333
  5.8 0.7 %inner.3.inner_ref = f32[4,4,8,1024]{3,2,1,0:T(8,128)S(1)} custom-call(f32[4,4,8,1024]{3,2,1,0:T(8,128)S(1)} %get-tuple-element.33.refs_0_.refs_4_, f32[4,4,8,128]{3,2,1,0:T(8,128)S(1)} %levels.1.refs_1_, bf16[208,208]{1,0:T(8,128)(2,1)S(1)} %get-tuple-element.31.refs_3_.refs_2_.high_ref, bf16[208,208]{1,0:T(8,128)(2,1)S(1)} %get-tuple-element.32.refs_4_.refs_3_.low_ref), custom_call_target="tpu_custom_call" | custom-call | tf_op jit(solution)/shard_map/inner/pallas_call | solution.py:333
  7.1 2.6 %collective-permute-start.2 = (f32[4,8,1024]{2,1,0:T(8,128)S(1)}, f32[4,8,1024]{2,1,0:T(8,128)S(1)}, u32[]{:S(2)}, u32[]{:S(2)}) collective-permute-start(f32[4,8,1024]{2,1,0:T(8,128)S(1)} %get-tuple-element.35), channel_id=1, source_target_pairs={{0,1},{2,3},{4,5},{6,7},{8,9},{10,11},{12,13},{14,15},{1,0},{3,2},... | collective-permute-start | bytes 393224 | tf_op jit(solution)/shard_map/ppermute | solution.py:322
  9.7 4.5 %collective-permute-start.3 = (f32[4,8,1024]{2,1,0:T(8,128)S(1)}, f32[4,8,1024]{2,1,0:T(8,128)S(1)}, u32[]{:S(2)}, u32[]{:S(2)}) collective-permute-start(f32[4,8,1024]{2,1,0:T(8,128)S(1)} %get-tuple-element.36), channel_id=1, source_target_pairs={{1,2},{3,4},{5,6},{7,8},{9,10},{11,12},{13,14},{15,0},{2,1},{4,3},... | collective-permute-start | bytes 393224 | tf_op jit(solution)/shard_map/ppermute | solution.py:321
  14.2 1.7 %collective-permute-done.2.from_pair_ref = f32[4,8,1024]{2,1,0:T(8,128)S(1)} collective-permute-done((f32[4,8,1024]{2,1,0:T(8,128)S(1)}, f32[4,8,1024]{2,1,0:T(8,128)S(1)}, u32[]{:S(2)}, u32[]{:S(2)}) %collective-permute-start.2) | collective-permute-done | bytes 131104 | tf_op jit(solution)/shard_map/ppermute | solution.py:322
  15.9 3.0 %collective-permute-done.3.from_other_ref = f32[4,8,1024]{2,1,0:T(8,128)S(1)} collective-permute-done((f32[4,8,1024]{2,1,0:T(8,128)S(1)}, f32[4,8,1024]{2,1,0:T(8,128)S(1)}, u32[]{:S(2)}, u32[]{:S(2)}) %collective-permute-start.3) | collective-permute-done | bytes 131104 | tf_op jit(solution)/shard_map/ppermute | solution.py:321
  18.9 0.8 %finish.2 = (f32[4,4,8,1024]{3,2,1,0:T(8,128)S(1)}, f32[4,8,1024]{2,1,0:T(8,128)S(1)}, f32[4,8,1024]{2,1,0:T(8,128)S(1)}) custom-call(f32[4,4,8,1024]{3,2,1,0:T(8,128)S(1)} %inner.3.inner_ref, f32[4,8,1024]{2,1,0:T(8,128)S(1)} %collective-permute-done.2.from_pair_ref, f32[4,8,1024]{2,1,0:T(8,128)S(1)} %collective-permute-done.3.from_other_ref, ...), custom_call_target="tpu_custom_call" | custom-call | tf_op jit(solution)/shard_map/finish/pallas_call | solution.py:333
  20.2 4.2 %collective-permute-start.5 = (f32[4,8,1024]{2,1,0:T(8,128)S(1)}, f32[4,8,1024]{2,1,0:T(8,128)S(1)}, u32[]{:S(2)}, u32[]{:S(2)}) collective-permute-start(f32[4,8,1024]{2,1,0:T(8,128)S(1)} %get-tuple-element.40), channel_id=1, source_target_pairs={{1,2},{3,4},{5,6},{7,8},{9,10},{11,12},{13,14},{15,0},{2,1},{4,3},... | collective-permute-start | bytes 393224 | tf_op jit(solution)/shard_map/ppermute | solution.py:321
  24.3 0.7 %inner.4.inner_ref = f32[4,4,8,1024]{3,2,1,0:T(8,128)S(1)} custom-call(f32[4,4,8,1024]{3,2,1,0:T(8,128)S(1)} %get-tuple-element.38.refs_0_.refs_4_, f32[4,4,8,128]{3,2,1,0:T(8,128)S(1)} %levels.1.refs_1_, bf16[208,208]{1,0:T(8,128)(2,1)S(1)} %get-tuple-element.31.refs_3_.refs_2_.high_ref, bf16[208,208]{1,0:T(8,128)(2,1)S(1)} %get-tuple-element.32.refs_4_.refs_3_.low_ref, ...), custom_call_target="tpu_custom_call" | custom-call | tf_op jit(solution)/shard_map/inner/pallas_call | solution.py:333
  25.0 0.9 %collective-permute-done.4.from_pair_ref = f32[4,8,1024]{2,1,0:T(8,128)S(1)} collective-permute-done((f32[4,8,1024]{2,1,0:T(8,128)S(1)}, f32[4,8,1024]{2,1,0:T(8,128)S(1)}, u32[]{:S(2)}, u32[]{:S(2)}) %collective-permute-start.4) | collective-permute-done | bytes 131104 | tf_op jit(solution)/shard_map/ppermute | solution.py:322
  25.9 2.9 %collective-permute-done.5.from_other_ref = f32[4,8,1024]{2,1,0:T(8,128)S(1)} collective-permute-done((f32[4,8,1024]{2,1,0:T(8,128)S(1)}, f32[4,8,1024]{2,1,0:T(8,128)S(1)}, u32[]{:S(2)}, u32[]{:S(2)}) %collective-permute-start.5) | collective-permute-done | bytes 131104 | tf_op jit(solution)/shard_map/ppermute | solution.py:321
  28.7 0.8 %finish.3 = (f32[4,4,8,1024]{3,2,1,0:T(8,128)S(1)}, f32[4,8,1024]{2,1,0:T(8,128)S(1)}, f32[4,8,1024]{2,1,0:T(8,128)S(1)}) custom-call(f32[4,4,8,1024]{3,2,1,0:T(8,128)S(1)} %inner.4.inner_ref, f32[4,8,1024]{2,1,0:T(8,128)S(1)} %collective-permute-done.4.from_pair_ref, f32[4,8,1024]{2,1,0:T(8,128)S(1)} %collective-permute-done.5.from_other_ref, ...), custom_call_target="tpu_custom_call" | custom-call | tf_op jit(solution)/shard_map/finish/pallas_call | solution.py:333
  29.6 4.2 %collective-permute-start.7 = (f32[4,8,1024]{2,1,0:T(8,128)S(1)}, f32[4,8,1024]{2,1,0:T(8,128)S(1)}, u32[]{:S(2)}, u32[]{:S(2)}) collective-permute-start(f32[4,8,1024]{2,1,0:T(8,128)S(1)} %get-tuple-element.44), channel_id=1, source_target_pairs={{1,2},{3,4},{5,6},{7,8},{9,10},{11,12},{13,14},{15,0},{2,1},{4,3},... | collective-permute-start | bytes 393224 | tf_op jit(solution)/shard_map/ppermute | solution.py:321
  33.8 0.9 %inner.5 = (f32[4,4,8,1024]{3,2,1,0:T(8,128)S(1)}, bf16[512,512]{1,0:T(8,128)(2,1)S(1)}) custom-call(f32[4,4,8,1024]{3,2,1,0:T(8,128)S(1)} %get-tuple-element.41.refs_0_, f32[4,4,8,128]{3,2,1,0:T(8,128)S(1)} %levels.1.refs_1_, bf16[208,208]{1,0:T(8,128)(2,1)S(1)} %get-tuple-element.31.refs_3_.refs_2_.high_ref, ...), custom_call_target="tpu_custom_call" | custom-call | tf_op jit(solution)/shard_map/inner/pallas_call | solution.py:333
  34.7 1.2 %margin_rows.2.refs_5_ = bf16[256,2048]{1,0:T(8,128)(2,1)S(1)} custom-call(f32[4096,128]{1,0:T(8,128)S(1)} %widen.1.wide_ref), custom_call_target="tpu_custom_call" | custom-call | tf_op jit(solution)/shard_map/margin_rows/pallas_call | solution.py:333
  36.0 1.2 %margin_rows.3.refs_6_ = bf16[256,2048]{1,0:T(8,128)(2,1)S(1)} custom-call(f32[4096,128]{1,0:T(8,128)S(1)} %collective-permute-done.8.wide_ref), custom_call_target="tpu_custom_call" | custom-call | tf_op jit(solution)/shard_map/margin_rows/pallas_call | solution.py:333
  37.2 1.0 %collective-permute-done.7.refs_2_ = f32[4,8,1024]{2,1,0:T(8,128)S(1)} collective-permute-done((f32[4,8,1024]{2,1,0:T(8,128)S(1)}, f32[4,8,1024]{2,1,0:T(8,128)S(1)}, u32[]{:S(2)}, u32[]{:S(2)}) %collective-permute-start.7) | collective-permute-done | bytes 131104 | tf_op jit(solution)/shard_map/ppermute | solution.py:321
  38.3 2.1 %last.1 = (f32[32,16,128]{2,1,0:T(8,128)S(1)}, f32[32,16,128]{2,1,0:T(8,128)S(1)}, f32[64,128]{1,0:T(8,128)S(1)}) custom-call(f32[4,4,8,1024]{3,2,1,0:T(8,128)S(1)} %get-tuple-element.42.refs_0_, f32[4,8,1024]{2,1,0:T(8,128)S(1)} %collective-permute-done.6.refs_1_, f32[4,8,1024]{2,1,0:T(8,128)S(1)} %collective-permute-done.7.refs_2_, ...), custom_call_target="tpu_custom_call" | custom-call | tf_op jit(solution)/shard_map/last/pallas_call | solution.py:333
  40.4 12.7 %all_to_all.5.tiles_ref = f32[16,4,128]{2,1,0:T(4,128)S(1)} all-to-all(f32[16,4,128]{2,1,0:T(4,128)S(1)} %bitcast.9), channel_id=1, replica_groups=mesh['px'=2,'py'=16] {'py'}, dimensions={0} | all-to-all | bytes 65536 | tf_op jit(solution)/shard_map/all_to_all | solution.py:442
  53.1 1.4 %result.1 = (f32[16,32]{1,0:T(8,128)}, f32[64,16,128]{2,1,0:T(8,128)}) custom-call(f32[16,4,128]{2,1,0:T(4,128)S(1)} %all_to_all.5.tiles_ref, f32[32,16,128]{2,1,0:T(8,128)S(1)} %get-tuple-element.50.refs_0_, f32[32,16,128]{2,1,0:T(8,128)S(1)} %collective-permute-done.9.refs_1_), custom_call_target="tpu_custom_call" | custom-call | tf_op jit(solution)/shard_map/result/pallas_call | solution.py:333
  (20 shorter events, 2.1 us)
Async XLA Ops:
  0.6 1.0 %copy-start = (f32[64,4,4,128]{3,2,1,0:T(4,128)S(1)}, f32[64,4,4,128]{3,2,1,0:T(4,128)}, u32[]{:S(2)}) copy-start(f32[64,4,4,128]{3,2,1,0:T(4,128)} %param.4) | copy-start | bytes 1572868
  0.6 5.8 %copy-start.1 = (bf16[256,4,4,128]{3,2,1,0:T(4,128)(2,1)S(1)}, bf16[256,4,4,128]{3,2,1,0:T(4,128)(2,1)}, u32[]{:S(2)}) copy-start(bf16[256,4,4,128]{3,2,1,0:T(4,128)(2,1)} %param.7) | copy-start | bytes 3145732
  1.7 3.3 %collective-permute-start = (f32[32,16,128]{2,1,0:T(8,128)S(1)}, f32[32,16,128]{2,1,0:T(8,128)S(1)}, u32[]{:S(2)}, u32[]{:S(2)}) collective-permute-start(f32[32,16,128]{2,1,0:T(8,128)S(1)} %constant_dynamic-slice_fusion.1), channel_id=1, source_target_pairs={{0,16},{16,0},{1,17},{17,1},{2,18},{18,2},{3,19},{19,3},{4,20},{20... | collective-permute-start | bytes 786440 | tf_op jit(solution)/shard_map/ppermute | solution.py:328
  2.2 1.9 %collective-permute-start.1 = (f32[1,16,128]{2,1,0:T(8,128)}, f32[1,16,128]{2,1,0:T(8,128)S(1)}, u32[]{:S(2)}, u32[]{:S(2)}) collective-permute-start(f32[1,16,128]{2,1,0:T(8,128)} %bitcast.10), channel_id=1, source_target_pairs={{0,16},{16,0},{1,17},{17,1},{2,18},{18,2},{3,19},{19,3},{4,20},{20... | collective-permute-start | bytes 24584 | tf_op jit(solution)/shard_map/ppermute | solution.py:328
  2.3 0.8 %copy-start.2 = (f32[125,125]{1,0:T(8,128)S(1)}, f32[125,125]{1,0:T(8,128)}, u32[]{:S(2)}) copy-start(f32[125,125]{1,0:T(8,128)} %cell_ref.1) | copy-start | bytes 187504
  4.1 0.7 %copy-start.3 = (f32[4,4,128]{2,1,0:T(4,128)S(1)}, f32[4,4,128]{2,1,0:T(4,128)}, u32[]{:S(2)}) copy-start(f32[4,4,128]{2,1,0:T(4,128)} %param.5) | copy-start | bytes 24580
  6.6 28.1 %collective-permute-start.8 = (f32[4096,128]{1,0:T(8,128)S(1)}, f32[4096,128]{1,0:T(8,128)S(1)}, u32[]{:S(2)}, u32[]{:S(2)}) collective-permute-start(f32[4096,128]{1,0:T(8,128)S(1)} %widen.1.wide_ref), channel_id=1, source_target_pairs={{0,16},{16,0},{1,17},{17,1},{2,18},{18,2},{3,19},{19,3},{4,20},{20... | collective-permute-start | bytes 6291464 | tf_op jit(solution)/shard_map/ppermute | solution.py:328
  7.1 8.8 %collective-permute-start.2 = (f32[4,8,1024]{2,1,0:T(8,128)S(1)}, f32[4,8,1024]{2,1,0:T(8,128)S(1)}, u32[]{:S(2)}, u32[]{:S(2)}) collective-permute-start(f32[4,8,1024]{2,1,0:T(8,128)S(1)} %get-tuple-element.35), channel_id=1, source_target_pairs={{0,1},{2,3},{4,5},{6,7},{8,9},{10,11},{12,13},{14,15},{1,0},{3,2},... | collective-permute-start | bytes 393224 | tf_op jit(solution)/shard_map/ppermute | solution.py:322
  9.7 9.2 %collective-permute-start.3 = (f32[4,8,1024]{2,1,0:T(8,128)S(1)}, f32[4,8,1024]{2,1,0:T(8,128)S(1)}, u32[]{:S(2)}, u32[]{:S(2)}) collective-permute-start(f32[4,8,1024]{2,1,0:T(8,128)S(1)} %get-tuple-element.36), channel_id=1, source_target_pairs={{1,2},{3,4},{5,6},{7,8},{9,10},{11,12},{13,14},{15,0},{2,1},{4,3},... | collective-permute-start | bytes 393224 | tf_op jit(solution)/shard_map/ppermute | solution.py:321
  19.7 6.2 %collective-permute-start.4 = (f32[4,8,1024]{2,1,0:T(8,128)S(1)}, f32[4,8,1024]{2,1,0:T(8,128)S(1)}, u32[]{:S(2)}, u32[]{:S(2)}) collective-permute-start(f32[4,8,1024]{2,1,0:T(8,128)S(1)} %get-tuple-element.39), channel_id=1, source_target_pairs={{0,1},{2,3},{4,5},{6,7},{8,9},{10,11},{12,13},{14,15},{1,0},{3,2},... | collective-permute-start | bytes 393224 | tf_op jit(solution)/shard_map/ppermute | solution.py:322
  20.2 8.6 %collective-permute-start.5 = (f32[4,8,1024]{2,1,0:T(8,128)S(1)}, f32[4,8,1024]{2,1,0:T(8,128)S(1)}, u32[]{:S(2)}, u32[]{:S(2)}) collective-permute-start(f32[4,8,1024]{2,1,0:T(8,128)S(1)} %get-tuple-element.40), channel_id=1, source_target_pairs={{1,2},{3,4},{5,6},{7,8},{9,10},{11,12},{13,14},{15,0},{2,1},{4,3},... | collective-permute-start | bytes 393224 | tf_op jit(solution)/shard_map/ppermute | solution.py:321
  29.6 7.6 %collective-permute-start.6 = (f32[4,8,1024]{2,1,0:T(8,128)S(1)}, f32[4,8,1024]{2,1,0:T(8,128)S(1)}, u32[]{:S(2)}, u32[]{:S(2)}) collective-permute-start(f32[4,8,1024]{2,1,0:T(8,128)S(1)} %get-tuple-element.43), channel_id=1, source_target_pairs={{0,1},{2,3},{4,5},{6,7},{8,9},{10,11},{12,13},{14,15},{1,0},{3,2},... | collective-permute-start | bytes 393224 | tf_op jit(solution)/shard_map/ppermute | solution.py:322
  29.6 8.6 %collective-permute-start.7 = (f32[4,8,1024]{2,1,0:T(8,128)S(1)}, f32[4,8,1024]{2,1,0:T(8,128)S(1)}, u32[]{:S(2)}, u32[]{:S(2)}) collective-permute-start(f32[4,8,1024]{2,1,0:T(8,128)S(1)} %get-tuple-element.44), channel_id=1, source_target_pairs={{1,2},{3,4},{5,6},{7,8},{9,10},{11,12},{13,14},{15,0},{2,1},{4,3},... | collective-permute-start | bytes 393224 | tf_op jit(solution)/shard_map/ppermute | solution.py:321
  40.3 12.8 %collective-permute-start.9 = (f32[32,16,128]{2,1,0:T(8,128)S(1)}, f32[32,16,128]{2,1,0:T(8,128)S(1)}, u32[]{:S(2)}, u32[]{:S(2)}) collective-permute-start(f32[32,16,128]{2,1,0:T(8,128)S(1)} %get-tuple-element.51), channel_id=1, source_target_pairs={{0,16},{16,0},{1,17},{17,1},{2,18},{18,2},{3,19},{19,3},{4,20},{20... | collective-permute-start | bytes 786440 | tf_op jit(solution)/shard_map/ppermute | solution.py:328

commit v8 on v6

--- a/solution.py
+++ b/solution.py
@@ -58,7 +58,7 @@
     return (state * cells + cell) * 4 + node
 
 
-def matrix_kernel(cells, nodes, cell_ref, high_ref, low_ref, order_ref, back_ref, spread_ref):
+def matrix_kernel(cells, nodes, cell_ref, high_ref, low_ref, halo_ref, order_ref):
     rest = cell_ref[...]
     size, count = high_ref.shape[0], cell_ref.shape[0]
     tables = [chosen(size, count, functools.partial(select_target, cell, nodes)) for cell in range(nodes // 4)]
@@ -69,13 +69,13 @@
         for table in tables:
             left = dot(table, part).astype(bf16)
             total = total + lax.dot_general(left, table, (((1,), (1,)), ((), ())), preferred_element_type=f32)
-    high_ref[...], low_ref[...] = two_parts(total)
+    high, low = two_parts(total)
+    high_ref[...], low_ref[...] = high, low
+    inside = halo_ref.shape[0]
+    from_halo = total[:inside, inside:]
+    high = from_halo.astype(bf16).astype(f32)
+    halo_ref[...] = jnp.concatenate([high, high, from_halo - high], 1).astype(bf16)
     order_ref[...] = chosen(*order_ref.shape, functools.partial(cell_order_target, cells))
-    back_ref[...] = chosen(*back_ref.shape, functools.partial(raw_order_target, cells))
-    row = lax.broadcasted_iota(jnp.int32, spread_ref.shape, 0)
-    col = lax.broadcasted_iota(jnp.int32, spread_ref.shape, 1)
-    same = row == lax.rem(col, cells) * 4 + lax.div(col, lanes)
-    spread_ref[...] = jnp.where(same, 1.0, 0.0).astype(bf16)
 
 
 def roll_cells(value, cells, forward):
@@ -160,11 +160,16 @@
 
 
 def levels_kernel(second, parts_x, *refs):
-    part_refs, (spread_ref, levels_ref) = refs[:parts_x], refs[parts_x:]
+    part_refs, levels_ref = refs[:parts_x], refs[parts_x]
     nodes = levels_ref.shape[2]
+    thickness = part_refs[0].shape[2]
+    cells = thickness // 4
+    row = lax.broadcasted_iota(jnp.int32, (thickness, 4 * lanes), 0)
+    col = lax.broadcasted_iota(jnp.int32, (thickness, 4 * lanes), 1)
+    table = jnp.where(row == lax.rem(col, cells) * 4 + lax.div(col, lanes), 1.0, 0.0).astype(bf16)
     rows = jnp.concatenate(gathered(part_refs, 0, second), 0)
     high, low = two_parts(rows)
-    spread = dot(high, spread_ref[...]) + dot(low, spread_ref[...])
+    spread = dot(high, table) + dot(low, table)
     for y in range(second):
         for iz in range(4):
             levels_ref[iz, y] = spread[y * nodes : (y + 1) * nodes, iz * lanes : (iz + 1) * lanes] - centre
@@ -176,7 +181,11 @@
 
 def inner_kernel(cells, step, *refs):
     w_ref, levels_ref, high_ref, low_ref = refs[:4]
-    before_ref, out_ref = refs[4] if step > 0 else None, refs[-1]
+    before_ref = refs[4] if step > 0 else None
+    out_ref = refs[4 if step == 0 else 5]
+    if step == 2:
+        back_ref = refs[6]
+        back_ref[...] = chosen(*back_ref.shape, functools.partial(raw_order_target, cells))
     nodes, width = w_ref.shape[2:]
     groups = width // lanes
     inside = 20 * nodes
@@ -203,14 +212,14 @@
             out_ref[iz, iy] = total if step == 0 else total - before_ref[iz, iy]
 
 
-def finish(cells, step, inner_ref, pair_ref, other_ref, high_ref, low_ref):
+def finish(cells, step, inner_ref, pair_ref, other_ref, matrix_ref):
     nodes, width = inner_ref.shape[2:]
-    inside = 20 * nodes
     even = even_place()
     halo = [jnp.where(even, pair_ref[iz], other_ref[iz]) for iz in range(4)]
     given = [jnp.where(even, other_ref[iz], pair_ref[iz]) for iz in range(4)]
     halo = jnp.concatenate(halo + roll_rows(halo[:1], cells) + [jnp.zeros((nodes, width), f32)], 0)
-    product = three_products(high_ref[:inside, inside:], low_ref[:inside, inside:], halo)
+    halo_high, halo_low = two_parts(halo)
+    product = dot(matrix_ref[...], jnp.concatenate([halo_high, halo_low, halo_high], 0))
     result = {}
     for iz in range(4):
         for iy in range(4):
@@ -225,17 +234,17 @@
     return result
 
 
-def finish_kernel(cells, step, inner_ref, from_pair_ref, from_other_ref, high_ref, low_ref, next_ref, pair_ref, other_ref):
-    value = finish(cells, step, inner_ref, from_pair_ref, from_other_ref, high_ref, low_ref)
+def finish_kernel(cells, step, inner_ref, from_pair_ref, from_other_ref, matrix_ref, high_ref, low_ref, next_ref, pair_ref, other_ref):
+    value = finish(cells, step, inner_ref, from_pair_ref, from_other_ref, matrix_ref)
     for (iz, iy), part in value.items():
         next_ref[iz, iy] = part
     send_edges(high_ref, low_ref, value, pair_ref, other_ref, cells)
 
 
 def from_cells_kernel(cells, second, parts_x, *refs):
-    inner_ref, pair_ref, other_ref, high_ref, low_ref, order_ref = refs[:6]
-    out_refs = refs[6:]
-    value = finish(cells, 2, inner_ref, pair_ref, other_ref, high_ref, low_ref)
+    inner_ref, pair_ref, other_ref, matrix_ref, order_ref = refs[:5]
+    out_refs = refs[5:]
+    value = finish(cells, 2, inner_ref, pair_ref, other_ref, matrix_ref)
     states, layer, thickness = out_refs[0].shape
     first = layer // second
     nodes = parts_x * first
@@ -260,18 +269,27 @@
                     out_ref[h * group + s, pl.ds(y, first, stride=second), :] = lines
 
 
-def margin_kernel(parts_x, chunks, *refs):
-    part_refs, block_ref = refs[: parts_x * chunks], refs[parts_x * chunks]
-    tiles_ref, filtered_ref, sems = refs[parts_x * chunks + 1 :]
+def reversed_bits(value, count):
+    bits = count.bit_length() - 1
+    return sum(lax.rem(lax.div(value, 2**bit), 2) * 2 ** (bits - 1 - bit) for bit in range(bits))
+
+
+def halved(total_ref, bit, keep_ref, send_ref):
+    half = keep_ref.shape[0]
+    keep_ref[...] = total_ref[pl.ds(pl.multiple_of(bit * half, half), half), :]
+    send_ref[...] = total_ref[pl.ds(pl.multiple_of((1 - bit) * half, half), half), :]
+
+
+def margin_kernel(parts_x, parts_y, *refs):
+    part_refs, block_ref = refs[:parts_x], refs[parts_x]
+    keep_ref, send_ref, filtered_ref, tiles_ref, sems = refs[parts_x + 1 :]
     me = lax.axis_index("px")
     count, layer, thickness = part_refs[0].shape
-    mine = count * chunks
     owners = [lax.rem(me + (parts_x - step), parts_x) for step in range(parts_x)]
     copies = []
-    for place, part_ref in enumerate(part_refs):
-        start = owners[place // chunks] * mine + place % chunks * count
-        target = filtered_ref.at[pl.ds(start, count)]
-        copies.append(pltpu.make_async_copy(part_ref, target, sems.at[place]))
+    for step, part_ref in enumerate(part_refs):
+        target = filtered_ref.at[pl.ds(owners[step] * count, count)]
+        copies.append(pltpu.make_async_copy(part_ref, target, sems.at[step]))
     start_all(copies)
     flat = [ref.reshape(count * layer, thickness) for ref in part_refs]
     lines = [
@@ -281,18 +299,29 @@
     product = lax.dot_general(
         block_ref[...], jnp.concatenate(lines, 1), (((1,), (1,)), ((), ())), preferred_element_type=f32
     )
-    group_rows = tiles_ref.shape[1]
+    group_rows = tiles_ref.shape[0] // parts_x
     groups = block_ref.shape[0] // group_rows
+    cols = group_rows // parts_y
+    digits = parts_y.bit_length() - 1
+    places = [int(format(place, "b").zfill(digits)[::-1], 2) for place in range(parts_y)]
     for step in range(parts_x):
-        columns = slice(step * mine, (step + 1) * mine)
-        tiles_ref[owners[step]] = jnp.concatenate(
-            [product[g * group_rows : (g + 1) * group_rows, columns] for g in range(groups)], 1
-        )
+        columns = slice(step * count, (step + 1) * count)
+        parts = [product[g * group_rows : (g + 1) * group_rows, columns] for g in range(groups)]
+        tiles = jnp.concatenate(parts, 1)
+        tiles = jnp.concatenate([tiles[place * cols : (place + 1) * cols] for place in places], 0)
+        start = pl.multiple_of(reversed_bits(owners[step], parts_x) * group_rows, group_rows)
+        tiles_ref[pl.ds(start, group_rows), :] = tiles
+    halved(tiles_ref, lax.rem(me, 2), keep_ref, send_ref)
     wait_all(copies)
 
 
-def sum_kernel(tiles_ref, out_ref):
-    total = jnp.sum(tiles_ref[...], axis=0)
+def half_kernel(axis, bit, kept_ref, received_ref, keep_ref, send_ref, total_ref):
+    total_ref[...] = kept_ref[...] + received_ref[...]
+    halved(total_ref, lax.rem(lax.div(lax.axis_index(axis), 2**bit), 2), keep_ref, send_ref)
+
+
+def tile_kernel(kept_ref, received_ref, out_ref):
+    total = kept_ref[...] + received_ref[...]
     tile_rows = out_ref.shape[1]
     groups = total.shape[1] // tile_rows
     out_ref[...] = jnp.concatenate([total[:, g * tile_rows : (g + 1) * tile_rows] for g in range(groups)], 0)
@@ -306,6 +335,10 @@
     other = lax.ppermute(other, "py", others + [(b, a) for a, b in others])
     pair = lax.ppermute(pair, "py", pairs + [(b, a) for a, b in pairs])
     return [pair, other]
+
+
+def mirrored(value, axis, bit):
+    return lax.ppermute(value, axis, [(place, place ^ 2**bit) for place in range(lax.axis_size(axis))])
 
 
 def shifted(value, axis, steps):
@@ -340,6 +373,7 @@
     group = lanes // cells * thickness
     matrix = jax.ShapeDtypeStruct((rows, rows), bf16)
     table = jax.ShapeDtypeStruct((group, group), bf16)
+    from_halo = jax.ShapeDtypeStruct((20 * nodes, 3 * (rows - 20 * nodes)), bf16)
 
     chunks = 1
     count = mine // chunks
@@ -354,9 +388,9 @@
         return lax.dynamic_slice_in_dim(span_rows, lax.rem(me + step, parts_x) * mine, mine, 0)
 
     parts = [part_for(0)] + [shifted(part_for(step), "px", step) for step in reversed(others)]
-    high, low, order, back, spread = kernel_call(
+    high, low, halo_matrix, order = kernel_call(
         functools.partial(matrix_kernel, cells, nodes),
-        [matrix, matrix, table, table, jax.ShapeDtypeStruct((thickness, 4 * lanes), bf16)],
+        [matrix, matrix, from_halo, table],
         [cell_matrix],
         "assemble",
     )
@@ -371,26 +405,31 @@
     levels = kernel_call(
         functools.partial(levels_kernel, second, parts_x),
         jax.ShapeDtypeStruct((4, 4, nodes, lanes), f32),
-        [level_rows] + [shifted(level_rows, "px", step) for step in reversed(others)] + [spread],
+        [level_rows] + [shifted(level_rows, "px", step) for step in reversed(others)],
         "levels",
     )
 
     before = None
     for step in range(3):
         operands = [field_now, levels, high, low] + ([before] if step > 0 else [])
-        inner = kernel_call(functools.partial(inner_kernel, cells, step), field, operands, "inner")
-        operands = [inner] + edges + [high, low]
+        inner, *back = kernel_call(
+            functools.partial(inner_kernel, cells, step), [field] + [table] * (step == 2), operands, "inner"
+        )
+        operands = [inner] + edges + [halo_matrix]
         if step < 2:
             before = field_now
             field_now, *edges = kernel_call(
-                functools.partial(finish_kernel, cells, step), [field, message, message], operands, "finish"
+                functools.partial(finish_kernel, cells, step),
+                [field, message, message],
+                operands + [high, low],
+                "finish",
             )
             edges = swapped(edges)
         else:
             pieces = kernel_call(
                 functools.partial(from_cells_kernel, cells, second, parts_x),
                 [part] * parts_x,
-                operands + [back],
+                operands + back,
                 "from_cells",
             )
     received = [pieces[0]] + [shifted(pieces[step], "px", step) for step in others]
@@ -399,20 +438,34 @@
     groups = min(tile_cols, lanes // tile_rows)
     ordered = block.reshape(parts_y, groups, tile_cols // groups, layer * thickness)
     ordered = ordered.transpose(1, 0, 2, 3).reshape(block_count, layer * thickness)
-    tiles, filtered = kernel_call(
-        functools.partial(margin_kernel, parts_x, chunks),
-        [
-            jax.ShapeDtypeStruct((parts_x, block_count // groups, groups * tile_rows), f32),
-            jax.ShapeDtypeStruct((states, layer, thickness), f32),
-        ],
+    size = parts_x * block_count // groups
+    half = jax.ShapeDtypeStruct((size // 2, groups * tile_rows), f32)
+    keep, send, filtered = kernel_call(
+        functools.partial(margin_kernel, parts_x, parts_y),
+        [half, half, jax.ShapeDtypeStruct((states, layer, thickness), f32)],
         received + [ordered],
         "margin",
-        scratch=[pltpu.SemaphoreType.DMA((parts_x * chunks,))],
-        out_specs=[whole, anywhere],
-    )
-    tiles = tiles.reshape(parts_x * parts_y, tile_cols // groups, groups * tile_rows)
-    tiles = lax.all_to_all(tiles, ("px", "py"), 0, 0, tiled=True)
-    margin = kernel_call(sum_kernel, jax.ShapeDtypeStruct((tile_cols, tile_rows), f32), [tiles], "tile_sum")
+        scratch=[pltpu.VMEM((size, groups * tile_rows), f32), pltpu.SemaphoreType.DMA((parts_x,))],
+        out_specs=[whole, whole, anywhere],
+    )
+    swaps = [(axis, bit) for axis, parts in (("px", parts_x), ("py", parts_y)) for bit in range(parts.bit_length() - 1)]
+    for place, (axis, bit) in enumerate(swaps[1:]):
+        size //= 2
+        got = mirrored(send, *swaps[place])
+        half = jax.ShapeDtypeStruct((size // 2, groups * tile_rows), f32)
+        keep, send = kernel_call(
+            functools.partial(half_kernel, axis, bit),
+            [half, half],
+            [keep, got],
+            "half",
+            scratch=[pltpu.VMEM((size, groups * tile_rows), f32)],
+        )
+    margin = kernel_call(
+        tile_kernel,
+        jax.ShapeDtypeStruct((tile_cols, tile_rows), f32),
+        [keep, mirrored(send, *swaps[-1])],
+        "tile",
+    )
     return filtered.reshape(span.shape), margin.T
 
 

time: 51.7 us -> 56.7 us (1.097)
  waiting for transfers between devices: 11.4 us -> 27.8 us
  blocking collectives: 11.6 us -> 0 us
    ppermute x0 -> x5, waiting for transfers between devices: none -> 16.5 us  [mirrored(): lax.ppermute(value, axis, [(place, place ^ 2 ** bit) for place in range(l...]
    all_to_all x1 -> x0, blocking collectives: 11.6 us -> none  [local(): tiles = lax.all_to_all(tiles, ('px', 'py'), 0, 0, tiled=True)]
    pallas_call x11 -> x15, Pallas kernels: 8.48 us -> 8.43 us  [kernel_call(): pl.pallas_call(body, out_shape=outs, in_specs=in_specs or [whole] * len(o...]
  transfers between devices with their start and end apart: 9 -> 14, of which waited for: 7 -> 12; matrix products, arithmetic and copies ran while one was open for 2% -> 2% of each run, Pallas kernels for 6% -> 6%
where the time goes in v8:
time: 56.7 us; the launch traced here: 56.6 us
  waiting for transfers between devices  27.8 us (49%)
  starting transfers between devices  17.3 us (31%)
  Pallas kernels  8.43 us (15%)
  local copies, waits for them, and re-layouts  2.23 us (4%)
  between operations  0.79 us (1%)
    ppermute x5, waiting for transfers between devices, mirrored(): lax.ppermute(value, axis, [(place, place ^ 2 ** bit) for place in range(l...  16.5 us
    ppermute x3, starting transfers between devices, swapped(): other = lax.ppermute(other, 'py', others + [(b, a) for a, b in others])  12.9 us
    ppermute x3, waiting for transfers between devices, swapped(): other = lax.ppermute(other, 'py', others + [(b, a) for a, b in others])  9.04 us
    pallas_call x15, Pallas kernels, kernel_call(): pl.pallas_call(body, out_shape=outs, in_specs=in_specs or [whole] * len(o...  8.43 us
    ppermute x3, starting transfers between devices, swapped(): pair = lax.ppermute(pair, 'py', pairs + [(b, a) for a, b in pairs])  3.5 us
    ppermute x3, waiting for transfers between devices, shifted(): lax.ppermute(value, axis, [(source, (source + steps) % count) for source...  1.75 us
  transfers between devices with their start and end apart: 14, of which 12 were waited for; matrix products, arithmetic and copies ran while one was open for 2% of the time, Pallas kernels for 6%

profile of v8, /device:TPU:0, one launch (start us, length us, event | category | flops | bytes accessed | tf_op | source)
XLA Modules:
  0.0 56.6 jit_solution(6749017636944038853)
XLA Ops:
  0.7 1.1 %constant_dynamic-slice_fusion = (f32[32,16,128]{2,1,0:T(8,128)S(1)}, f32[32,16,128]{2,1,0:T(8,128)S(1)}) fusion(f32[64,16,128]{2,1,0:T(8,128)} %bitcast.10, s32[]{:T(128)S(6)} %select_n.7, s32[]{:T(128)S(6)} %select_n.6), kind=kLoop, calls=%fused_computation.1 | loop fusion | bytes 1048584 | tf_op jit(solution)/shard_map/dynamic_slice | solution.py:388
  2.3 0.9 %assemble.1 = (bf16[208,208]{1,0:T(8,128)(2,1)S(1)}, bf16[208,208]{1,0:T(8,128)(2,1)S(1)}, bf16[160,144]{1,0:T(8,128)(2,1)S(1)}, bf16[512,512]{1,0:T(8,128)(2,1)S(1)}) custom-call(f32[125,125]{1,0:T(8,128)S(1)} %copy-done), custom_call_target="tpu_custom_call" | custom-call | tf_op jit(solution)/shard_map/assemble/pallas_call | solution.py:351
  3.4 0.8 %to_cells.1 = (f32[4,4,8,1024]{3,2,1,0:T(8,128)S(1)}, f32[4,8,1024]{2,1,0:T(8,128)S(1)}, f32[4,8,1024]{2,1,0:T(8,128)S(1)}) custom-call(f32[32,16,128]{2,1,0:T(8,128)S(1)} %get-tuple-element.59.refs_0_, f32[32,16,128]{2,1,0:T(8,128)S(1)} %collective-permute-done.refs_1_, bf16[512,512]{1,0:T(8,128)(2,1)S(1)} %get-tuple-element.30.refs_2_, ...), custom_call_target="tpu_custom_call" | custom-call | tf_op jit(solution)/shard_map/to_cells/pallas_call | solution.py:351
  4.2 2.9 %collective-permute-start.2 = (f32[4,8,1024]{2,1,0:T(8,128)S(1)}, f32[4,8,1024]{2,1,0:T(8,128)S(1)}, u32[]{:S(2)}, u32[]{:S(2)}) collective-permute-start(f32[4,8,1024]{2,1,0:T(8,128)S(1)} %get-tuple-element.34), channel_id=1, source_target_pairs={{0,1},{2,3},{4,5},{6,7},{8,9},{10,11},{12,13},{14,15},{1,0},{3,2},... | collective-permute-start | bytes 393224 | tf_op jit(solution)/shard_map/ppermute | solution.py:336
  7.2 4.5 %collective-permute-start.3 = (f32[4,8,1024]{2,1,0:T(8,128)S(1)}, f32[4,8,1024]{2,1,0:T(8,128)S(1)}, u32[]{:S(2)}, u32[]{:S(2)}) collective-permute-start(f32[4,8,1024]{2,1,0:T(8,128)S(1)} %get-tuple-element.35), channel_id=1, source_target_pairs={{1,2},{3,4},{5,6},{7,8},{9,10},{11,12},{13,14},{15,0},{2,1},{4,3},... | collective-permute-start | bytes 393224 | tf_op jit(solution)/shard_map/ppermute | solution.py:335
  11.7 1.2 %collective-permute-done.1.refs_1_ = f32[1,16,128]{2,1,0:T(8,128)S(1)} collective-permute-done((f32[1,16,128]{2,1,0:T(8,128)S(1)}, f32[1,16,128]{2,1,0:T(8,128)S(1)}, u32[]{:S(2)}, u32[]{:S(2)}) %collective-permute-start.1) | collective-permute-done | bytes 8224 | tf_op jit(solution)/shard_map/ppermute | solution.py:346
  13.0 0.7 %inner.3.inner_ref = f32[4,4,8,1024]{3,2,1,0:T(8,128)S(1)} custom-call(f32[4,4,8,1024]{3,2,1,0:T(8,128)S(1)} %get-tuple-element.33.refs_0_.refs_4_, f32[4,4,8,128]{3,2,1,0:T(8,128)S(1)} %levels.1.refs_1_, bf16[208,208]{1,0:T(8,128)(2,1)S(1)} %get-tuple-element.31.refs_3_.refs_2_.high_ref, bf16[208,208]{1,0:T(8,128)(2,1)S(1)} %get-tuple-element.32.refs_4_.refs_3_.low_ref), custom_call_target="tpu_custom_call" | custom-call | tf_op jit(solution)/shard_map/inner/pallas_call | solution.py:351
  13.7 2.3 %collective-permute-done.3.from_other_ref = f32[4,8,1024]{2,1,0:T(8,128)S(1)} collective-permute-done((f32[4,8,1024]{2,1,0:T(8,128)S(1)}, f32[4,8,1024]{2,1,0:T(8,128)S(1)}, u32[]{:S(2)}, u32[]{:S(2)}) %collective-permute-start.3) | collective-permute-done | bytes 131104 | tf_op jit(solution)/shard_map/ppermute | solution.py:335
  16.0 0.8 %finish.2 = (f32[4,4,8,1024]{3,2,1,0:T(8,128)S(1)}, f32[4,8,1024]{2,1,0:T(8,128)S(1)}, f32[4,8,1024]{2,1,0:T(8,128)S(1)}) custom-call(f32[4,4,8,1024]{3,2,1,0:T(8,128)S(1)} %inner.3.inner_ref, f32[4,8,1024]{2,1,0:T(8,128)S(1)} %collective-permute-done.2.from_pair_ref, f32[4,8,1024]{2,1,0:T(8,128)S(1)} %collective-permute-done.3.from_other_ref, ...), custom_call_target="tpu_custom_call" | custom-call | tf_op jit(solution)/shard_map/finish/pallas_call | solution.py:351
  17.3 4.2 %collective-permute-start.5 = (f32[4,8,1024]{2,1,0:T(8,128)S(1)}, f32[4,8,1024]{2,1,0:T(8,128)S(1)}, u32[]{:S(2)}, u32[]{:S(2)}) collective-permute-start(f32[4,8,1024]{2,1,0:T(8,128)S(1)} %get-tuple-element.39), channel_id=1, source_target_pairs={{1,2},{3,4},{5,6},{7,8},{9,10},{11,12},{13,14},{15,0},{2,1},{4,3},... | collective-permute-start | bytes 393224 | tf_op jit(solution)/shard_map/ppermute | solution.py:335
  21.5 0.6 %inner.4.inner_ref = f32[4,4,8,1024]{3,2,1,0:T(8,128)S(1)} custom-call(f32[4,4,8,1024]{3,2,1,0:T(8,128)S(1)} %get-tuple-element.37.refs_0_.refs_4_, f32[4,4,8,128]{3,2,1,0:T(8,128)S(1)} %levels.1.refs_1_, bf16[208,208]{1,0:T(8,128)(2,1)S(1)} %get-tuple-element.31.refs_3_.refs_2_.high_ref, bf16[208,208]{1,0:T(8,128)(2,1)S(1)} %get-tuple-element.32.refs_4_.refs_3_.low_ref, ...), custom_call_target="tpu_custom_call" | custom-call | tf_op jit(solution)/shard_map/inner/pallas_call | solution.py:351
  22.7 3.2 %collective-permute-done.5.from_other_ref = f32[4,8,1024]{2,1,0:T(8,128)S(1)} collective-permute-done((f32[4,8,1024]{2,1,0:T(8,128)S(1)}, f32[4,8,1024]{2,1,0:T(8,128)S(1)}, u32[]{:S(2)}, u32[]{:S(2)}) %collective-permute-start.5) | collective-permute-done | bytes 131104 | tf_op jit(solution)/shard_map/ppermute | solution.py:335
  25.9 0.8 %finish.3 = (f32[4,4,8,1024]{3,2,1,0:T(8,128)S(1)}, f32[4,8,1024]{2,1,0:T(8,128)S(1)}, f32[4,8,1024]{2,1,0:T(8,128)S(1)}) custom-call(f32[4,4,8,1024]{3,2,1,0:T(8,128)S(1)} %inner.4.inner_ref, f32[4,8,1024]{2,1,0:T(8,128)S(1)} %collective-permute-done.4.from_pair_ref, f32[4,8,1024]{2,1,0:T(8,128)S(1)} %collective-permute-done.5.from_other_ref, ...), custom_call_target="tpu_custom_call" | custom-call | tf_op jit(solution)/shard_map/finish/pallas_call | solution.py:351
  26.8 4.2 %collective-permute-start.7 = (f32[4,8,1024]{2,1,0:T(8,128)S(1)}, f32[4,8,1024]{2,1,0:T(8,128)S(1)}, u32[]{:S(2)}, u32[]{:S(2)}) collective-permute-start(f32[4,8,1024]{2,1,0:T(8,128)S(1)} %get-tuple-element.43), channel_id=1, source_target_pairs={{1,2},{3,4},{5,6},{7,8},{9,10},{11,12},{13,14},{15,0},{2,1},{4,3},... | collective-permute-start | bytes 393224 | tf_op jit(solution)/shard_map/ppermute | solution.py:335
  31.0 0.9 %inner.5 = (f32[4,4,8,1024]{3,2,1,0:T(8,128)S(1)}, bf16[512,512]{1,0:T(8,128)(2,1)S(1)}) custom-call(f32[4,4,8,1024]{3,2,1,0:T(8,128)S(1)} %get-tuple-element.40.refs_0_, f32[4,4,8,128]{3,2,1,0:T(8,128)S(1)} %levels.1.refs_1_, bf16[208,208]{1,0:T(8,128)(2,1)S(1)} %get-tuple-element.31.refs_3_.refs_2_.high_ref, ...), custom_call_target="tpu_custom_call" | custom-call | tf_op jit(solution)/shard_map/inner/pallas_call | solution.py:351
  31.9 3.5 %collective-permute-done.7.refs_2_ = f32[4,8,1024]{2,1,0:T(8,128)S(1)} collective-permute-done((f32[4,8,1024]{2,1,0:T(8,128)S(1)}, f32[4,8,1024]{2,1,0:T(8,128)S(1)}, u32[]{:S(2)}, u32[]{:S(2)}) %collective-permute-start.7) | collective-permute-done | bytes 131104 | tf_op jit(solution)/shard_map/ppermute | solution.py:335
  35.4 0.8 %from_cells.1 = (f32[32,16,128]{2,1,0:T(8,128)S(1)}, f32[32,16,128]{2,1,0:T(8,128)S(1)}) custom-call(f32[4,4,8,1024]{3,2,1,0:T(8,128)S(1)} %get-tuple-element.41.refs_0_, f32[4,8,1024]{2,1,0:T(8,128)S(1)} %collective-permute-done.6.refs_1_, f32[4,8,1024]{2,1,0:T(8,128)S(1)} %collective-permute-done.7.refs_2_, ...), custom_call_target="tpu_custom_call" | custom-call | tf_op jit(solution)/shard_map/from_cells/pallas_call | solution.py:351
  37.8 1.2 %margin.1 = (f32[64,128]{1,0:T(8,128)S(1)}, f32[64,128]{1,0:T(8,128)S(1)}, f32[64,16,128]{2,1,0:T(8,128)}) custom-call(f32[32,16,128]{2,1,0:T(8,128)S(1)} %get-tuple-element.45.refs_0_, f32[32,16,128]{2,1,0:T(8,128)S(1)} %collective-permute-done.8.refs_1_, bf16[256,2048]{1,0:T(8,128)(2,1)S(1)} %reshape.22.refs_2_), custom_call_target="tpu_custom_call" | custom-call | tf_op jit(solution)/shard_map/margin/pallas_call | solution.py:351
  39.2 1.1 %collective-permute-done.9.received_ref = f32[64,128]{1,0:T(8,128)S(1)} collective-permute-done((f32[64,128]{1,0:T(8,128)S(1)}, f32[64,128]{1,0:T(8,128)S(1)}, u32[]{:S(2)}, u32[]{:S(2)}) %collective-permute-start.9) | collective-permute-done | bytes 32800 | tf_op jit(solution)/shard_map/ppermute | solution.py:341
  40.4 3.7 %collective-permute-done.10.received_ref = f32[32,128]{1,0:T(8,128)S(1)} collective-permute-done((f32[32,128]{1,0:T(8,128)S(1)}, f32[32,128]{1,0:T(8,128)S(1)}, u32[]{:S(2)}, u32[]{:S(2)}) %collective-permute-start.10) | collective-permute-done | bytes 16416 | tf_op jit(solution)/shard_map/ppermute | solution.py:341
  44.1 3.6 %collective-permute-done.11.received_ref = f32[16,128]{1,0:T(8,128)S(1)} collective-permute-done((f32[16,128]{1,0:T(8,128)S(1)}, f32[16,128]{1,0:T(8,128)S(1)}, u32[]{:S(2)}, u32[]{:S(2)}) %collective-permute-start.11) | collective-permute-done | bytes 8224 | tf_op jit(solution)/shard_map/ppermute | solution.py:341
  47.8 3.6 %collective-permute-done.12.received_ref = f32[8,128]{1,0:T(8,128)S(1)} collective-permute-done((f32[8,128]{1,0:T(8,128)S(1)}, f32[8,128]{1,0:T(8,128)S(1)}, u32[]{:S(2)}, u32[]{:S(2)}) %collective-permute-start.12) | collective-permute-done | bytes 4128 | tf_op jit(solution)/shard_map/ppermute | solution.py:341
  51.4 4.5 %collective-permute-done.13.received_ref = f32[4,128]{1,0:T(4,128)S(1)} collective-permute-done((f32[4,128]{1,0:T(4,128)S(1)}, f32[4,128]{1,0:T(4,128)S(1)}, u32[]{:S(2)}, u32[]{:S(2)}) %collective-permute-start.13) | collective-permute-done | bytes 2080 | tf_op jit(solution)/shard_map/ppermute | solution.py:341
  55.9 0.7 %tile.1 = f32[16,32]{1,0:T(8,128)} custom-call(f32[4,128]{1,0:T(4,128)S(1)} %get-tuple-element.56.kept_ref, f32[4,128]{1,0:T(4,128)S(1)} %collective-permute-done.13.received_ref), custom_call_target="tpu_custom_call" | custom-call | tf_op jit(solution)/shard_map/tile/pallas_call | solution.py:351
  (29 shorter events, 3.9 us)
Async XLA Ops:
  0.6 1.6 %copy-start = (f32[125,125]{1,0:T(8,128)S(1)}, f32[125,125]{1,0:T(8,128)}, u32[]{:S(2)}) copy-start(f32[125,125]{1,0:T(8,128)} %cell_ref.1) | copy-start | bytes 187504
  1.8 1.7 %collective-permute-start = (f32[32,16,128]{2,1,0:T(8,128)S(1)}, f32[32,16,128]{2,1,0:T(8,128)S(1)}, u32[]{:S(2)}, u32[]{:S(2)}) collective-permute-start(f32[32,16,128]{2,1,0:T(8,128)S(1)} %get-tuple-element.58), channel_id=1, source_target_pairs={{0,16},{16,0},{1,17},{17,1},{2,18},{18,2},{3,19},{19,3},{4,20},{20... | collective-permute-start | bytes 786440 | tf_op jit(solution)/shard_map/ppermute | solution.py:346
  3.4 8.2 %copy-start.1 = (f32[4,4,128]{2,1,0:T(4,128)S(1)}, f32[4,4,128]{2,1,0:T(4,128)}, u32[]{:S(2)}) copy-start(f32[4,4,128]{2,1,0:T(4,128)} %param.5) | copy-start | bytes 24580
  4.2 9.5 %collective-permute-start.2 = (f32[4,8,1024]{2,1,0:T(8,128)S(1)}, f32[4,8,1024]{2,1,0:T(8,128)S(1)}, u32[]{:S(2)}, u32[]{:S(2)}) collective-permute-start(f32[4,8,1024]{2,1,0:T(8,128)S(1)} %get-tuple-element.34), channel_id=1, source_target_pairs={{0,1},{2,3},{4,5},{6,7},{8,9},{10,11},{12,13},{14,15},{1,0},{3,2},... | collective-permute-start | bytes 393224 | tf_op jit(solution)/shard_map/ppermute | solution.py:336
  7.2 8.9 %collective-permute-start.3 = (f32[4,8,1024]{2,1,0:T(8,128)S(1)}, f32[4,8,1024]{2,1,0:T(8,128)S(1)}, u32[]{:S(2)}, u32[]{:S(2)}) collective-permute-start(f32[4,8,1024]{2,1,0:T(8,128)S(1)} %get-tuple-element.35), channel_id=1, source_target_pairs={{1,2},{3,4},{5,6},{7,8},{9,10},{11,12},{13,14},{15,0},{2,1},{4,3},... | collective-permute-start | bytes 393224 | tf_op jit(solution)/shard_map/ppermute | solution.py:335
  11.7 1.2 %collective-permute-start.1 = (f32[1,16,128]{2,1,0:T(8,128)S(1)}, f32[1,16,128]{2,1,0:T(8,128)S(1)}, u32[]{:S(2)}, u32[]{:S(2)}) collective-permute-start(f32[1,16,128]{2,1,0:T(8,128)S(1)} %bitcast.7), channel_id=1, source_target_pairs={{0,16},{16,0},{1,17},{17,1},{2,18},{18,2},{3,19},{19,3},{4,20},{20... | collective-permute-start | bytes 24584 | tf_op jit(solution)/shard_map/ppermute | solution.py:346
  16.8 5.8 %collective-permute-start.4 = (f32[4,8,1024]{2,1,0:T(8,128)S(1)}, f32[4,8,1024]{2,1,0:T(8,128)S(1)}, u32[]{:S(2)}, u32[]{:S(2)}) collective-permute-start(f32[4,8,1024]{2,1,0:T(8,128)S(1)} %get-tuple-element.38), channel_id=1, source_target_pairs={{0,1},{2,3},{4,5},{6,7},{8,9},{10,11},{12,13},{14,15},{1,0},{3,2},... | collective-permute-start | bytes 393224 | tf_op jit(solution)/shard_map/ppermute | solution.py:336
  17.3 8.6 %collective-permute-start.5 = (f32[4,8,1024]{2,1,0:T(8,128)S(1)}, f32[4,8,1024]{2,1,0:T(8,128)S(1)}, u32[]{:S(2)}, u32[]{:S(2)}) collective-permute-start(f32[4,8,1024]{2,1,0:T(8,128)S(1)} %get-tuple-element.39), channel_id=1, source_target_pairs={{1,2},{3,4},{5,6},{7,8},{9,10},{11,12},{13,14},{15,0},{2,1},{4,3},... | collective-permute-start | bytes 393224 | tf_op jit(solution)/shard_map/ppermute | solution.py:335
  26.7 5.2 %collective-permute-start.6 = (f32[4,8,1024]{2,1,0:T(8,128)S(1)}, f32[4,8,1024]{2,1,0:T(8,128)S(1)}, u32[]{:S(2)}, u32[]{:S(2)}) collective-permute-start(f32[4,8,1024]{2,1,0:T(8,128)S(1)} %get-tuple-element.42), channel_id=1, source_target_pairs={{0,1},{2,3},{4,5},{6,7},{8,9},{10,11},{12,13},{14,15},{1,0},{3,2},... | collective-permute-start | bytes 393224 | tf_op jit(solution)/shard_map/ppermute | solution.py:336
  26.8 8.6 %collective-permute-start.7 = (f32[4,8,1024]{2,1,0:T(8,128)S(1)}, f32[4,8,1024]{2,1,0:T(8,128)S(1)}, u32[]{:S(2)}, u32[]{:S(2)}) collective-permute-start(f32[4,8,1024]{2,1,0:T(8,128)S(1)} %get-tuple-element.43), channel_id=1, source_target_pairs={{1,2},{3,4},{5,6},{7,8},{9,10},{11,12},{13,14},{15,0},{2,1},{4,3},... | collective-permute-start | bytes 393224 | tf_op jit(solution)/shard_map/ppermute | solution.py:335
  31.0 5.3 %copy-start.2 = (bf16[256,4,4,128]{3,2,1,0:T(4,128)(2,1)S(1)}, bf16[256,4,4,128]{3,2,1,0:T(4,128)(2,1)}, u32[]{:S(2)}) copy-start(bf16[256,4,4,128]{3,2,1,0:T(4,128)(2,1)} %param.7) | copy-start | bytes 3145732
  36.2 1.6 %collective-permute-start.8 = (f32[32,16,128]{2,1,0:T(8,128)S(1)}, f32[32,16,128]{2,1,0:T(8,128)S(1)}, u32[]{:S(2)}, u32[]{:S(2)}) collective-permute-start(f32[32,16,128]{2,1,0:T(8,128)S(1)} %get-tuple-element.46), channel_id=1, source_target_pairs={{0,16},{16,0},{1,17},{17,1},{2,18},{18,2},{3,19},{19,3},{4,20},{20... | collective-permute-start | bytes 786440 | tf_op jit(solution)/shard_map/ppermute | solution.py:346
  39.0 1.3 %collective-permute-start.9 = (f32[64,128]{1,0:T(8,128)S(1)}, f32[64,128]{1,0:T(8,128)S(1)}, u32[]{:S(2)}, u32[]{:S(2)}) collective-permute-start(f32[64,128]{1,0:T(8,128)S(1)} %get-tuple-element.49), channel_id=1, source_target_pairs={{0,16},{16,0},{1,17},{17,1},{2,18},{18,2},{3,19},{19,3},{4,20},{20... | collective-permute-start | bytes 98312 | tf_op jit(solution)/shard_map/ppermute | solution.py:341
  40.3 3.8 %collective-permute-start.10 = (f32[32,128]{1,0:T(8,128)S(1)}, f32[32,128]{1,0:T(8,128)S(1)}, u32[]{:S(2)}, u32[]{:S(2)}) collective-permute-start(f32[32,128]{1,0:T(8,128)S(1)} %get-tuple-element.51), channel_id=1, source_target_pairs={{0,1},{1,0},{2,3},{3,2},{4,5},{5,4},{6,7},{7,6},{8,9},{9,8},{10,11... | collective-permute-start | bytes 49160 | tf_op jit(solution)/shard_map/ppermute | solution.py:341
  44.1 3.7 %collective-permute-start.11 = (f32[16,128]{1,0:T(8,128)S(1)}, f32[16,128]{1,0:T(8,128)S(1)}, u32[]{:S(2)}, u32[]{:S(2)}) collective-permute-start(f32[16,128]{1,0:T(8,128)S(1)} %get-tuple-element.53), channel_id=1, source_target_pairs={{0,2},{1,3},{2,0},{3,1},{4,6},{5,7},{6,4},{7,5},{8,10},{9,11},{10,... | collective-permute-start | bytes 24584 | tf_op jit(solution)/shard_map/ppermute | solution.py:341
  47.8 3.6 %collective-permute-start.12 = (f32[8,128]{1,0:T(8,128)S(1)}, f32[8,128]{1,0:T(8,128)S(1)}, u32[]{:S(2)}, u32[]{:S(2)}) collective-permute-start(f32[8,128]{1,0:T(8,128)S(1)} %get-tuple-element.55), channel_id=1, source_target_pairs={{0,4},{1,5},{2,6},{3,7},{4,0},{5,1},{6,2},{7,3},{8,12},{9,13},{10,... | collective-permute-start | bytes 12296 | tf_op jit(solution)/shard_map/ppermute | solution.py:341
  51.4 4.5 %collective-permute-start.13 = (f32[4,128]{1,0:T(4,128)S(1)}, f32[4,128]{1,0:T(4,128)S(1)}, u32[]{:S(2)}, u32[]{:S(2)}) collective-permute-start(f32[4,128]{1,0:T(4,128)S(1)} %get-tuple-element.57), channel_id=1, source_target_pairs={{0,8},{1,9},{2,10},{3,11},{4,12},{5,13},{6,14},{7,15},{8,0},{9,1},... | collective-permute-start | bytes 6152 | tf_op jit(solution)/shard_map/ppermute | solution.py:341

commit v9 on v8

--- a/solution.py
+++ b/solution.py
@@ -269,29 +269,9 @@
                     out_ref[h * group + s, pl.ds(y, first, stride=second), :] = lines
 
 
-def reversed_bits(value, count):
-    bits = count.bit_length() - 1
-    return sum(lax.rem(lax.div(value, 2**bit), 2) * 2 ** (bits - 1 - bit) for bit in range(bits))
-
-
-def halved(total_ref, bit, keep_ref, send_ref):
-    half = keep_ref.shape[0]
-    keep_ref[...] = total_ref[pl.ds(pl.multiple_of(bit * half, half), half), :]
-    send_ref[...] = total_ref[pl.ds(pl.multiple_of((1 - bit) * half, half), half), :]
-
-
-def margin_kernel(parts_x, parts_y, *refs):
-    part_refs, block_ref = refs[:parts_x], refs[parts_x]
-    keep_ref, send_ref, filtered_ref, tiles_ref, sems = refs[parts_x + 1 :]
-    me = lax.axis_index("px")
-    count, layer, thickness = part_refs[0].shape
-    owners = [lax.rem(me + (parts_x - step), parts_x) for step in range(parts_x)]
-    copies = []
-    for step, part_ref in enumerate(part_refs):
-        target = filtered_ref.at[pl.ds(owners[step] * count, count)]
-        copies.append(pltpu.make_async_copy(part_ref, target, sems.at[step]))
-    start_all(copies)
-    flat = [ref.reshape(count * layer, thickness) for ref in part_refs]
+def margin_tiles(parts, block_ref, group_rows):
+    count, layer, thickness = parts[0].shape
+    flat = [ref.reshape(count * layer, thickness) for ref in parts]
     lines = [
         jnp.concatenate([ref[pl.ds(n, count, stride=layer), :].astype(bf16) for ref in flat], 0)
         for n in range(layer)
@@ -299,29 +279,39 @@
     product = lax.dot_general(
         block_ref[...], jnp.concatenate(lines, 1), (((1,), (1,)), ((), ())), preferred_element_type=f32
     )
-    group_rows = tiles_ref.shape[0] // parts_x
-    groups = block_ref.shape[0] // group_rows
-    cols = group_rows // parts_y
-    digits = parts_y.bit_length() - 1
-    places = [int(format(place, "b").zfill(digits)[::-1], 2) for place in range(parts_y)]
-    for step in range(parts_x):
-        columns = slice(step * count, (step + 1) * count)
-        parts = [product[g * group_rows : (g + 1) * group_rows, columns] for g in range(groups)]
-        tiles = jnp.concatenate(parts, 1)
-        tiles = jnp.concatenate([tiles[place * cols : (place + 1) * cols] for place in places], 0)
-        start = pl.multiple_of(reversed_bits(owners[step], parts_x) * group_rows, group_rows)
-        tiles_ref[pl.ds(start, group_rows), :] = tiles
-    halved(tiles_ref, lax.rem(me, 2), keep_ref, send_ref)
+    starts = range(0, product.shape[0], group_rows)
+    return [
+        jnp.concatenate([product[start : start + group_rows, part * count : (part + 1) * count] for start in starts], 1)
+        for part in range(len(parts))
+    ]
+
+
+def own_margin_kernel(part_ref, block_ref, tiles_ref, filtered_ref, sem):
+    count = part_ref.shape[0]
+    copy = pltpu.make_async_copy(part_ref, filtered_ref.at[pl.ds(lax.axis_index("px") * count, count)], sem)
+    copy.start()
+    tiles_ref[...] = margin_tiles([part_ref], block_ref, tiles_ref.shape[0])[0]
+    copy.wait()
+
+
+def other_margin_kernel(parts_x, own_ref, begun_ref, block_ref, *refs):
+    part_refs, (tiles_ref, filtered_ref, sems) = refs[: parts_x - 1], refs[parts_x - 1 :]
+    me = lax.axis_index("px")
+    count = part_refs[0].shape[0]
+    owners = [lax.rem(me + (parts_x - step), parts_x) for step in range(1, parts_x)]
+    copies = []
+    for place, (owner, part_ref) in enumerate(zip(owners, part_refs)):
+        target = filtered_ref.at[pl.ds(owner * count, count)]
+        copies.append(pltpu.make_async_copy(part_ref, target, sems.at[place]))
+    start_all(copies)
+    tiles_ref[me] = own_ref[...]
+    for owner, tiles in zip(owners, margin_tiles(part_refs, block_ref, tiles_ref.shape[1])):
+        tiles_ref[owner] = tiles
     wait_all(copies)
 
 
-def half_kernel(axis, bit, kept_ref, received_ref, keep_ref, send_ref, total_ref):
-    total_ref[...] = kept_ref[...] + received_ref[...]
-    halved(total_ref, lax.rem(lax.div(lax.axis_index(axis), 2**bit), 2), keep_ref, send_ref)
-
-
-def tile_kernel(kept_ref, received_ref, out_ref):
-    total = kept_ref[...] + received_ref[...]
+def sum_kernel(tiles_ref, out_ref):
+    total = jnp.sum(tiles_ref[...], axis=0)
     tile_rows = out_ref.shape[1]
     groups = total.shape[1] // tile_rows
     out_ref[...] = jnp.concatenate([total[:, g * tile_rows : (g + 1) * tile_rows] for g in range(groups)], 0)
@@ -337,16 +327,12 @@
     return [pair, other]
 
 
-def mirrored(value, axis, bit):
-    return lax.ppermute(value, axis, [(place, place ^ 2**bit) for place in range(lax.axis_size(axis))])
-
-
 def shifted(value, axis, steps):
     count = lax.axis_size(axis)
     return lax.ppermute(value, axis, [(source, (source + steps) % count) for source in range(count)])
 
 
-def kernel_call(body, outs, operands, name, scratch=(), in_specs=None, out_specs=None):
+def kernel_call(body, outs, operands, name, scratch=(), in_specs=None, out_specs=None, aliases=None):
     many = isinstance(outs, list)
     return pl.pallas_call(
         body,
@@ -354,6 +340,7 @@
         in_specs=in_specs or [whole] * len(operands),
         out_specs=out_specs or ([whole] * len(outs) if many else whole),
         scratch_shapes=list(scratch),
+        input_output_aliases=aliases or {},
         compiler_params=params,
         name=name,
     )(*operands)
@@ -409,12 +396,20 @@
         "levels",
     )
 
+    tile_rows, tile_cols = mine, block_count // parts_y
+    groups = min(tile_cols, lanes // tile_rows)
     before = None
     for step in range(3):
+        if step == 1:
+            field_now, block = lax.optimization_barrier((field_now, block))
+            ordered = block.reshape(parts_y, groups, tile_cols // groups, layer * thickness)
+            ordered = ordered.transpose(1, 0, 2, 3).reshape(block_count, layer * thickness)
         operands = [field_now, levels, high, low] + ([before] if step > 0 else [])
         inner, *back = kernel_call(
             functools.partial(inner_kernel, cells, step), [field] + [table] * (step == 2), operands, "inner"
         )
+        if step == 2:
+            inner, ordered = lax.optimization_barrier((inner, ordered))
         operands = [inner] + edges + [halo_matrix]
         if step < 2:
             before = field_now
@@ -432,40 +427,31 @@
                 operands + back,
                 "from_cells",
             )
-    received = [pieces[0]] + [shifted(pieces[step], "px", step) for step in others]
-
-    tile_rows, tile_cols = mine, block_count // parts_y
-    groups = min(tile_cols, lanes // tile_rows)
-    ordered = block.reshape(parts_y, groups, tile_cols // groups, layer * thickness)
-    ordered = ordered.transpose(1, 0, 2, 3).reshape(block_count, layer * thickness)
-    size = parts_x * block_count // groups
-    half = jax.ShapeDtypeStruct((size // 2, groups * tile_rows), f32)
-    keep, send, filtered = kernel_call(
-        functools.partial(margin_kernel, parts_x, parts_y),
-        [half, half, jax.ShapeDtypeStruct((states, layer, thickness), f32)],
-        received + [ordered],
-        "margin",
-        scratch=[pltpu.VMEM((size, groups * tile_rows), f32), pltpu.SemaphoreType.DMA((parts_x,))],
-        out_specs=[whole, whole, anywhere],
-    )
-    swaps = [(axis, bit) for axis, parts in (("px", parts_x), ("py", parts_y)) for bit in range(parts.bit_length() - 1)]
-    for place, (axis, bit) in enumerate(swaps[1:]):
-        size //= 2
-        got = mirrored(send, *swaps[place])
-        half = jax.ShapeDtypeStruct((size // 2, groups * tile_rows), f32)
-        keep, send = kernel_call(
-            functools.partial(half_kernel, axis, bit),
-            [half, half],
-            [keep, got],
-            "half",
-            scratch=[pltpu.VMEM((size, groups * tile_rows), f32)],
-        )
-    margin = kernel_call(
-        tile_kernel,
-        jax.ShapeDtypeStruct((tile_cols, tile_rows), f32),
-        [keep, mirrored(send, *swaps[-1])],
-        "tile",
-    )
+    received = [shifted(pieces[step], "px", step) for step in others]
+
+    tiles = jax.ShapeDtypeStruct((block_count // groups, groups * tile_rows), f32)
+    filtered = jax.ShapeDtypeStruct((states, layer, thickness), f32)
+    own, filtered = kernel_call(
+        own_margin_kernel,
+        [tiles, filtered],
+        [pieces[0], ordered],
+        "own_margin",
+        scratch=[pltpu.SemaphoreType.DMA],
+        out_specs=[whole, anywhere],
+    )
+    tiles, filtered = kernel_call(
+        functools.partial(other_margin_kernel, parts_x),
+        [jax.ShapeDtypeStruct((parts_x,) + own.shape, f32), jax.ShapeDtypeStruct(filtered.shape, f32)],
+        [own, filtered, ordered] + received,
+        "other_margin",
+        scratch=[pltpu.SemaphoreType.DMA((parts_x - 1,))],
+        in_specs=[whole, anywhere] + [whole] * parts_x,
+        out_specs=[whole, anywhere],
+        aliases={1: 1},
+    )
+    tiles = tiles.reshape(parts_x * parts_y, tile_cols // groups, groups * tile_rows)
+    tiles = lax.all_to_all(tiles, ("px", "py"), 0, 0, tiled=True)
+    margin = kernel_call(sum_kernel, jax.ShapeDtypeStruct((tile_cols, tile_rows), f32), [tiles], "tile_sum")
     return filtered.reshape(span.shape), margin.T
 
 

time: 56.7 us -> 51.5 us (0.908)
  waiting for transfers between devices: 27.8 us -> 8.22 us
  blocking collectives: 0 us -> 10.9 us
  local copies, waits for them, and re-layouts: 2.23 us -> 5.31 us
  Pallas kernels: 8.43 us -> 9.07 us
    ppermute x5 -> x0, waiting for transfers between devices: 16.5 us -> none  [mirrored(): lax.ppermute(value, axis, [(place, place ^ 2 ** bit) for place in range(l...]
    all_to_all x0 -> x1, blocking collectives: none -> 10.9 us  [local(): tiles = lax.all_to_all(tiles, ('px', 'py'), 0, 0, tiled=True)]
    ppermute x3, waiting for transfers between devices: 9.04 us -> 5.51 us  [swapped(): other = lax.ppermute(other, 'py', others + [(b, a) for a, b in others])]
    reshape x2, local copies, waits for them, and re-layouts: 0.84 us -> 2.87 us  [local(): block.reshape(parts_y, groups, tile_cols // groups, layer * thickness)]
    reshape x1, local copies, waits for them, and re-layouts: 0.28 us -> 1.33 us  [local(): ordered.transpose(1, 0, 2, 3).reshape(block_count, layer * thickness)]
    pallas_call x15 -> x12, Pallas kernels: 8.43 us -> 9.07 us  [kernel_call(): pl.pallas_call(body, out_shape=outs, in_specs=in_specs or [whole] * len(o...]
  transfers between devices with their start and end apart: 14 -> 9, of which waited for: 12 -> 6; matrix products, arithmetic and copies ran while one was open for 2% -> 8% of each run, Pallas kernels for 6% -> 8%
where the time goes in v9:
time: 51.5 us; the launch traced here: 51.3 us
  starting transfers between devices  17 us (33%)
  blocking collectives  10.9 us (21%)
  Pallas kernels  9.07 us (18%)
  waiting for transfers between devices  8.22 us (16%)
  local copies, waits for them, and re-layouts  5.31 us (10%)
  between operations  0.77 us (1%)
    ppermute x3, starting transfers between devices, swapped(): other = lax.ppermute(other, 'py', others + [(b, a) for a, b in others])  12.9 us
    all_to_all x1, blocking collectives, local(): tiles = lax.all_to_all(tiles, ('px', 'py'), 0, 0, tiled=True)  10.9 us
    pallas_call x12, Pallas kernels, kernel_call(): pl.pallas_call(body, out_shape=outs, in_specs=in_specs or [whole] * len(o...  9.07 us
    ppermute x3, waiting for transfers between devices, swapped(): other = lax.ppermute(other, 'py', others + [(b, a) for a, b in others])  5.51 us
    ppermute x3, starting transfers between devices, swapped(): pair = lax.ppermute(pair, 'py', pairs + [(b, a) for a, b in pairs])  3.48 us
    reshape x2, local copies, waits for them, and re-layouts, local(): block.reshape(parts_y, groups, tile_cols // groups, layer * thickness)  2.87 us
    ppermute x3, waiting for transfers between devices, shifted(): lax.ppermute(value, axis, [(source, (source + steps) % count) for source...  2.15 us
    reshape x1, local copies, waits for them, and re-layouts, local(): ordered.transpose(1, 0, 2, 3).reshape(block_count, layer * thickness)  1.33 us
  transfers between devices with their start and end apart: 9, of which 6 were waited for; matrix products, arithmetic and copies ran while one was open for 8% of the time, Pallas kernels for 8%

profile of v9, /device:TPU:0, one launch (start us, length us, event | category | flops | bytes accessed | tf_op | source)
XLA Modules:
  0.0 51.3 jit_solution(17883604481786050808)
XLA Ops:
  0.7 1.1 %constant_dynamic-slice_fusion = (f32[32,16,128]{2,1,0:T(8,128)S(1)}, f32[32,16,128]{2,1,0:T(8,128)S(1)}) fusion(f32[64,16,128]{2,1,0:T(8,128)} %bitcast.13, s32[]{:T(128)S(6)} %select_n.7, s32[]{:T(128)S(6)} %select_n.6), kind=kLoop, calls=%fused_computation.1 | loop fusion | bytes 1048584 | tf_op jit(solution)/shard_map/dynamic_slice | solution.py:375
  2.3 0.9 %assemble.1 = (bf16[208,208]{1,0:T(8,128)(2,1)S(1)}, bf16[208,208]{1,0:T(8,128)(2,1)S(1)}, bf16[160,144]{1,0:T(8,128)(2,1)S(1)}, bf16[512,512]{1,0:T(8,128)(2,1)S(1)}) custom-call(f32[125,125]{1,0:T(8,128)S(1)} %copy-done), custom_call_target="tpu_custom_call" | custom-call | tf_op jit(solution)/shard_map/assemble/pallas_call | solution.py:337
  3.4 0.8 %to_cells.1 = (f32[4,4,8,1024]{3,2,1,0:T(8,128)S(1)}, f32[4,8,1024]{2,1,0:T(8,128)S(1)}, f32[4,8,1024]{2,1,0:T(8,128)S(1)}) custom-call(f32[32,16,128]{2,1,0:T(8,128)S(1)} %get-tuple-element.53.refs_0_, f32[32,16,128]{2,1,0:T(8,128)S(1)} %collective-permute-done.refs_1_, bf16[512,512]{1,0:T(8,128)(2,1)S(1)} %get-tuple-element.27.refs_2_, ...), custom_call_target="tpu_custom_call" | custom-call | tf_op jit(solution)/shard_map/to_cells/pallas_call | solution.py:337
  4.2 2.9 %collective-permute-start.2 = (f32[4,8,1024]{2,1,0:T(8,128)S(1)}, f32[4,8,1024]{2,1,0:T(8,128)S(1)}, u32[]{:S(2)}, u32[]{:S(2)}) collective-permute-start(f32[4,8,1024]{2,1,0:T(8,128)S(1)} %get-tuple-element.31), channel_id=1, source_target_pairs={{0,1},{2,3},{4,5},{6,7},{8,9},{10,11},{12,13},{14,15},{1,0},{3,2},... | collective-permute-start | bytes 393224 | tf_op jit(solution)/shard_map/ppermute | solution.py:326
  7.2 4.5 %collective-permute-start.3 = (f32[4,8,1024]{2,1,0:T(8,128)S(1)}, f32[4,8,1024]{2,1,0:T(8,128)S(1)}, u32[]{:S(2)}, u32[]{:S(2)}) collective-permute-start(f32[4,8,1024]{2,1,0:T(8,128)S(1)} %get-tuple-element.32), channel_id=1, source_target_pairs={{1,2},{3,4},{5,6},{7,8},{9,10},{11,12},{13,14},{15,0},{2,1},{4,3},... | collective-permute-start | bytes 393224 | tf_op jit(solution)/shard_map/ppermute | solution.py:325
  11.7 1.2 %collective-permute-done.1.refs_1_ = f32[1,16,128]{2,1,0:T(8,128)S(1)} collective-permute-done((f32[1,16,128]{2,1,0:T(8,128)S(1)}, f32[1,16,128]{2,1,0:T(8,128)S(1)}, u32[]{:S(2)}, u32[]{:S(2)}) %collective-permute-start.1) | collective-permute-done | bytes 8224 | tf_op jit(solution)/shard_map/ppermute | solution.py:332
  13.0 0.7 %inner.3.inner_ref = f32[4,4,8,1024]{3,2,1,0:T(8,128)S(1)} custom-call(f32[4,4,8,1024]{3,2,1,0:T(8,128)S(1)} %get-tuple-element.30.refs_0_.refs_4_, f32[4,4,8,128]{3,2,1,0:T(8,128)S(1)} %levels.1.refs_1_, bf16[208,208]{1,0:T(8,128)(2,1)S(1)} %get-tuple-element.28.refs_3_.refs_2_.high_ref, bf16[208,208]{1,0:T(8,128)(2,1)S(1)} %get-tuple-element.29.refs_4_.refs_3_.low_ref), custom_call_target="tpu_custom_call" | custom-call | tf_op jit(solution)/shard_map/inner/pallas_call | solution.py:337
  13.7 2.3 %collective-permute-done.3.from_other_ref = f32[4,8,1024]{2,1,0:T(8,128)S(1)} collective-permute-done((f32[4,8,1024]{2,1,0:T(8,128)S(1)}, f32[4,8,1024]{2,1,0:T(8,128)S(1)}, u32[]{:S(2)}, u32[]{:S(2)}) %collective-permute-start.3) | collective-permute-done | bytes 131104 | tf_op jit(solution)/shard_map/ppermute | solution.py:325
  16.0 0.8 %finish.2 = (f32[4,4,8,1024]{3,2,1,0:T(8,128)S(1)}, f32[4,8,1024]{2,1,0:T(8,128)S(1)}, f32[4,8,1024]{2,1,0:T(8,128)S(1)}) custom-call(f32[4,4,8,1024]{3,2,1,0:T(8,128)S(1)} %inner.3.inner_ref, f32[4,8,1024]{2,1,0:T(8,128)S(1)} %collective-permute-done.2.from_pair_ref, f32[4,8,1024]{2,1,0:T(8,128)S(1)} %collective-permute-done.3.from_other_ref, ...), custom_call_target="tpu_custom_call" | custom-call | tf_op jit(solution)/shard_map/finish/pallas_call | solution.py:337
  17.3 4.2 %collective-permute-start.5 = (f32[4,8,1024]{2,1,0:T(8,128)S(1)}, f32[4,8,1024]{2,1,0:T(8,128)S(1)}, u32[]{:S(2)}, u32[]{:S(2)}) collective-permute-start(f32[4,8,1024]{2,1,0:T(8,128)S(1)} %get-tuple-element.37), channel_id=1, source_target_pairs={{1,2},{3,4},{5,6},{7,8},{9,10},{11,12},{13,14},{15,0},{2,1},{4,3},... | collective-permute-start | bytes 393224 | tf_op jit(solution)/shard_map/ppermute | solution.py:325
  21.5 0.7 %inner.4.inner_ref = f32[4,4,8,1024]{3,2,1,0:T(8,128)S(1)} custom-call(f32[4,4,8,1024]{3,2,1,0:T(8,128)S(1)} %get-tuple-element.35.refs_0_.refs_4_, f32[4,4,8,128]{3,2,1,0:T(8,128)S(1)} %levels.1.refs_1_, bf16[208,208]{1,0:T(8,128)(2,1)S(1)} %get-tuple-element.28.refs_3_.refs_2_.high_ref, bf16[208,208]{1,0:T(8,128)(2,1)S(1)} %get-tuple-element.29.refs_4_.refs_3_.low_ref, ...), custom_call_target="tpu_custom_call" | custom-call | tf_op jit(solution)/shard_map/inner/pallas_call | solution.py:337
  22.7 3.2 %collective-permute-done.5.from_other_ref = f32[4,8,1024]{2,1,0:T(8,128)S(1)} collective-permute-done((f32[4,8,1024]{2,1,0:T(8,128)S(1)}, f32[4,8,1024]{2,1,0:T(8,128)S(1)}, u32[]{:S(2)}, u32[]{:S(2)}) %collective-permute-start.5) | collective-permute-done | bytes 131104 | tf_op jit(solution)/shard_map/ppermute | solution.py:325
  25.9 0.8 %finish.3 = (f32[4,4,8,1024]{3,2,1,0:T(8,128)S(1)}, f32[4,8,1024]{2,1,0:T(8,128)S(1)}, f32[4,8,1024]{2,1,0:T(8,128)S(1)}) custom-call(f32[4,4,8,1024]{3,2,1,0:T(8,128)S(1)} %inner.4.inner_ref, f32[4,8,1024]{2,1,0:T(8,128)S(1)} %collective-permute-done.4.from_pair_ref, f32[4,8,1024]{2,1,0:T(8,128)S(1)} %collective-permute-done.5.from_other_ref, ...), custom_call_target="tpu_custom_call" | custom-call | tf_op jit(solution)/shard_map/finish/pallas_call | solution.py:337
  26.8 4.2 %collective-permute-start.7 = (f32[4,8,1024]{2,1,0:T(8,128)S(1)}, f32[4,8,1024]{2,1,0:T(8,128)S(1)}, u32[]{:S(2)}, u32[]{:S(2)}) collective-permute-start(f32[4,8,1024]{2,1,0:T(8,128)S(1)} %get-tuple-element.43), channel_id=1, source_target_pairs={{1,2},{3,4},{5,6},{7,8},{9,10},{11,12},{13,14},{15,0},{2,1},{4,3},... | collective-permute-start | bytes 393224 | tf_op jit(solution)/shard_map/ppermute | solution.py:325
  31.0 1.3 %reshape.24 = bf16[16,4,4,2048]{3,2,1,0:T(4,128)(2,1)S(1)} reshape(bf16[256,4,4,128]{3,2,1,0:T(4,128)(2,1)} %param.7) | data formatting | bytes 2097152 | tf_op jit(solution)/shard_map/reshape | solution.py:405
  32.3 1.5 %copy.9 = bf16[16,4,4,2048]{3,2,0,1:T(4,128)(2,1)} copy(bf16[16,4,4,2048]{3,2,1,0:T(4,128)(2,1)S(1)} %reshape.24) | data formatting | bytes 2097152 | tf_op jit(solution)/shard_map/reshape | solution.py:405
  33.9 1.3 %reshape.25.block_ref = bf16[256,2048]{1,0:T(8,128)(2,1)S(1)} reshape(bf16[4,16,4,2048]{3,2,1,0:T(4,128)(2,1)} %bitcast.11) | data formatting | bytes 2097152 | tf_op jit(solution)/shard_map/reshape | solution.py:406
  35.2 0.9 %inner.5 = (f32[4,4,8,1024]{3,2,1,0:T(8,128)S(1)}, bf16[512,512]{1,0:T(8,128)(2,1)S(1)}) custom-call(f32[4,4,8,1024]{3,2,1,0:T(8,128)S(1)} %get-tuple-element.38.refs_0_, f32[4,4,8,128]{3,2,1,0:T(8,128)S(1)} %levels.1.refs_1_, bf16[208,208]{1,0:T(8,128)(2,1)S(1)} %get-tuple-element.28.refs_3_.refs_2_.high_ref, ...), custom_call_target="tpu_custom_call" | custom-call | tf_op jit(solution)/shard_map/inner/pallas_call | solution.py:337
  36.1 0.8 %from_cells.1 = (f32[32,16,128]{2,1,0:T(8,128)S(1)}, f32[32,16,128]{2,1,0:T(8,128)S(1)}) custom-call(f32[4,4,8,1024]{3,2,1,0:T(8,128)S(1)} %get-tuple-element.41.refs_0_, f32[4,8,1024]{2,1,0:T(8,128)S(1)} %collective-permute-done.6.refs_1_, f32[4,8,1024]{2,1,0:T(8,128)S(1)} %collective-permute-done.7.refs_2_, ...), custom_call_target="tpu_custom_call" | custom-call | tf_op jit(solution)/shard_map/from_cells/pallas_call | solution.py:337
  37.0 0.7 %own_margin.1 = (f32[64,128]{1,0:T(8,128)S(1)}, f32[64,16,128]{2,1,0:T(8,128)}) custom-call(f32[32,16,128]{2,1,0:T(8,128)S(1)} %get-tuple-element.45.part_ref, bf16[256,2048]{1,0:T(8,128)(2,1)S(1)} %reshape.25.block_ref), custom_call_target="tpu_custom_call" | custom-call | tf_op jit(solution)/shard_map/own_margin/pallas_call | solution.py:337
  37.7 0.8 %collective-permute-done.8.refs_0_ = f32[32,16,128]{2,1,0:T(8,128)S(1)} collective-permute-done((f32[32,16,128]{2,1,0:T(8,128)S(1)}, f32[32,16,128]{2,1,0:T(8,128)S(1)}, u32[]{:S(2)}, u32[]{:S(2)}) %collective-permute-start.8) | collective-permute-done | bytes 262176 | tf_op jit(solution)/shard_map/ppermute | solution.py:332
  38.5 1.1 %other_margin.1 = (f32[2,64,128]{2,1,0:T(8,128)S(1)}, f32[64,16,128]{2,1,0:T(8,128)}) custom-call(f32[64,128]{1,0:T(8,128)S(1)} %get-tuple-element.47.own_ref, f32[64,16,128]{2,1,0:T(8,128)} %get-tuple-element.48.begun_ref, bf16[256,2048]{1,0:T(8,128)(2,1)S(1)} %reshape.25.block_ref, ...), custom_call_target="tpu_custom_call", output_to_operand_aliasing={{1}: (1, {})} | custom-call | tf_op jit(solution)/shard_map/other_margin/pallas_call | solution.py:337
  39.6 10.9 %all_to_all.5.tiles_ref = f32[32,4,128]{2,1,0:T(4,128)S(1)} all-to-all(f32[32,4,128]{2,1,0:T(4,128)S(1)} %bitcast.8), channel_id=1, replica_groups=mesh['px'=2,'py'=16] {'px','py'}, dimensions={0} | all-to-all | bytes 131072 | tf_op jit(solution)/shard_map/all_to_all | solution.py:453
  50.6 0.7 %tile_sum.1 = f32[16,32]{1,0:T(8,128)} custom-call(f32[32,4,128]{2,1,0:T(4,128)S(1)} %all_to_all.5.tiles_ref), custom_call_target="tpu_custom_call" | custom-call | tf_op jit(solution)/shard_map/tile_sum/pallas_call | solution.py:337
  (15 shorter events, 2.1 us)
Async XLA Ops:
  0.6 1.6 %copy-start = (f32[125,125]{1,0:T(8,128)S(1)}, f32[125,125]{1,0:T(8,128)}, u32[]{:S(2)}) copy-start(f32[125,125]{1,0:T(8,128)} %cell_ref.1) | copy-start | bytes 187504
  1.8 1.7 %collective-permute-start = (f32[32,16,128]{2,1,0:T(8,128)S(1)}, f32[32,16,128]{2,1,0:T(8,128)S(1)}, u32[]{:S(2)}, u32[]{:S(2)}) collective-permute-start(f32[32,16,128]{2,1,0:T(8,128)S(1)} %get-tuple-element.52), channel_id=1, source_target_pairs={{0,16},{16,0},{1,17},{17,1},{2,18},{18,2},{3,19},{19,3},{4,20},{20... | collective-permute-start | bytes 786440 | tf_op jit(solution)/shard_map/ppermute | solution.py:332
  3.4 8.2 %copy-start.1 = (f32[4,4,128]{2,1,0:T(4,128)S(1)}, f32[4,4,128]{2,1,0:T(4,128)}, u32[]{:S(2)}) copy-start(f32[4,4,128]{2,1,0:T(4,128)} %param.5) | copy-start | bytes 24580
  4.2 9.5 %collective-permute-start.2 = (f32[4,8,1024]{2,1,0:T(8,128)S(1)}, f32[4,8,1024]{2,1,0:T(8,128)S(1)}, u32[]{:S(2)}, u32[]{:S(2)}) collective-permute-start(f32[4,8,1024]{2,1,0:T(8,128)S(1)} %get-tuple-element.31), channel_id=1, source_target_pairs={{0,1},{2,3},{4,5},{6,7},{8,9},{10,11},{12,13},{14,15},{1,0},{3,2},... | collective-permute-start | bytes 393224 | tf_op jit(solution)/shard_map/ppermute | solution.py:326
  7.2 8.9 %collective-permute-start.3 = (f32[4,8,1024]{2,1,0:T(8,128)S(1)}, f32[4,8,1024]{2,1,0:T(8,128)S(1)}, u32[]{:S(2)}, u32[]{:S(2)}) collective-permute-start(f32[4,8,1024]{2,1,0:T(8,128)S(1)} %get-tuple-element.32), channel_id=1, source_target_pairs={{1,2},{3,4},{5,6},{7,8},{9,10},{11,12},{13,14},{15,0},{2,1},{4,3},... | collective-permute-start | bytes 393224 | tf_op jit(solution)/shard_map/ppermute | solution.py:325
  11.7 1.2 %collective-permute-start.1 = (f32[1,16,128]{2,1,0:T(8,128)S(1)}, f32[1,16,128]{2,1,0:T(8,128)S(1)}, u32[]{:S(2)}, u32[]{:S(2)}) collective-permute-start(f32[1,16,128]{2,1,0:T(8,128)S(1)} %bitcast.9), channel_id=1, source_target_pairs={{0,16},{16,0},{1,17},{17,1},{2,18},{18,2},{3,19},{19,3},{4,20},{20... | collective-permute-start | bytes 24584 | tf_op jit(solution)/shard_map/ppermute | solution.py:332
  16.8 5.9 %collective-permute-start.4 = (f32[4,8,1024]{2,1,0:T(8,128)S(1)}, f32[4,8,1024]{2,1,0:T(8,128)S(1)}, u32[]{:S(2)}, u32[]{:S(2)}) collective-permute-start(f32[4,8,1024]{2,1,0:T(8,128)S(1)} %get-tuple-element.36), channel_id=1, source_target_pairs={{0,1},{2,3},{4,5},{6,7},{8,9},{10,11},{12,13},{14,15},{1,0},{3,2},... | collective-permute-start | bytes 393224 | tf_op jit(solution)/shard_map/ppermute | solution.py:326
  17.3 8.6 %collective-permute-start.5 = (f32[4,8,1024]{2,1,0:T(8,128)S(1)}, f32[4,8,1024]{2,1,0:T(8,128)S(1)}, u32[]{:S(2)}, u32[]{:S(2)}) collective-permute-start(f32[4,8,1024]{2,1,0:T(8,128)S(1)} %get-tuple-element.37), channel_id=1, source_target_pairs={{1,2},{3,4},{5,6},{7,8},{9,10},{11,12},{13,14},{15,0},{2,1},{4,3},... | collective-permute-start | bytes 393224 | tf_op jit(solution)/shard_map/ppermute | solution.py:325
  26.7 9.4 %collective-permute-start.6 = (f32[4,8,1024]{2,1,0:T(8,128)S(1)}, f32[4,8,1024]{2,1,0:T(8,128)S(1)}, u32[]{:S(2)}, u32[]{:S(2)}) collective-permute-start(f32[4,8,1024]{2,1,0:T(8,128)S(1)} %get-tuple-element.42), channel_id=1, source_target_pairs={{0,1},{2,3},{4,5},{6,7},{8,9},{10,11},{12,13},{14,15},{1,0},{3,2},... | collective-permute-start | bytes 393224 | tf_op jit(solution)/shard_map/ppermute | solution.py:326
  26.8 9.4 %collective-permute-start.7 = (f32[4,8,1024]{2,1,0:T(8,128)S(1)}, f32[4,8,1024]{2,1,0:T(8,128)S(1)}, u32[]{:S(2)}, u32[]{:S(2)}) collective-permute-start(f32[4,8,1024]{2,1,0:T(8,128)S(1)} %get-tuple-element.43), channel_id=1, source_target_pairs={{1,2},{3,4},{5,6},{7,8},{9,10},{11,12},{13,14},{15,0},{2,1},{4,3},... | collective-permute-start | bytes 393224 | tf_op jit(solution)/shard_map/ppermute | solution.py:325
  36.9 1.6 %collective-permute-start.8 = (f32[32,16,128]{2,1,0:T(8,128)S(1)}, f32[32,16,128]{2,1,0:T(8,128)S(1)}, u32[]{:S(2)}, u32[]{:S(2)}) collective-permute-start(f32[32,16,128]{2,1,0:T(8,128)S(1)} %get-tuple-element.49), channel_id=1, source_target_pairs={{0,16},{16,0},{1,17},{17,1},{2,18},{18,2},{3,19},{19,3},{4,20},{20... | collective-permute-start | bytes 786440 | tf_op jit(solution)/shard_map/ppermute | solution.py:332

commit v10 on v9

--- a/solution.py
+++ b/solution.py
@@ -76,6 +76,16 @@
     high = from_halo.astype(bf16).astype(f32)
     halo_ref[...] = jnp.concatenate([high, high, from_halo - high], 1).astype(bf16)
     order_ref[...] = chosen(*order_ref.shape, functools.partial(cell_order_target, cells))
+
+
+def margin_rows_kernel(layer, parts_y, block_ref, out_ref, wide_ref):
+    wide_ref[...] = block_ref[...].astype(f32)
+    thickness = block_ref.shape[1]
+    tile_cols = out_ref.shape[0] // parts_y
+    for n in range(layer):
+        for col in range(tile_cols):
+            lines = wide_ref[pl.ds(col * layer + n, parts_y, stride=tile_cols * layer), :]
+            out_ref[pl.ds(col * parts_y, parts_y), pl.ds(n * thickness, thickness)] = lines.astype(bf16)
 
 
 def roll_cells(value, cells, forward):
@@ -212,7 +222,7 @@
             out_ref[iz, iy] = total if step == 0 else total - before_ref[iz, iy]
 
 
-def finish(cells, step, inner_ref, pair_ref, other_ref, matrix_ref):
+def finish(cells, step, inner_ref, other_ref, pair_ref, matrix_ref):
     nodes, width = inner_ref.shape[2:]
     even = even_place()
     halo = [jnp.where(even, pair_ref[iz], other_ref[iz]) for iz in range(4)]
@@ -234,17 +244,17 @@
     return result
 
 
-def finish_kernel(cells, step, inner_ref, from_pair_ref, from_other_ref, matrix_ref, high_ref, low_ref, next_ref, pair_ref, other_ref):
-    value = finish(cells, step, inner_ref, from_pair_ref, from_other_ref, matrix_ref)
+def finish_kernel(cells, step, inner_ref, from_other_ref, from_pair_ref, matrix_ref, high_ref, low_ref, next_ref, pair_ref, other_ref):
+    value = finish(cells, step, inner_ref, from_other_ref, from_pair_ref, matrix_ref)
     for (iz, iy), part in value.items():
         next_ref[iz, iy] = part
     send_edges(high_ref, low_ref, value, pair_ref, other_ref, cells)
 
 
 def from_cells_kernel(cells, second, parts_x, *refs):
-    inner_ref, pair_ref, other_ref, matrix_ref, order_ref = refs[:5]
+    inner_ref, other_ref, pair_ref, matrix_ref, order_ref = refs[:5]
     out_refs = refs[5:]
-    value = finish(cells, 2, inner_ref, pair_ref, other_ref, matrix_ref)
+    value = finish(cells, 2, inner_ref, other_ref, pair_ref, matrix_ref)
     states, layer, thickness = out_refs[0].shape
     first = layer // second
     nodes = parts_x * first
@@ -269,9 +279,18 @@
                     out_ref[h * group + s, pl.ds(y, first, stride=second), :] = lines
 
 
-def margin_tiles(parts, block_ref, group_rows):
-    count, layer, thickness = parts[0].shape
-    flat = [ref.reshape(count * layer, thickness) for ref in parts]
+def margin_kernel(parts_x, parts_y, *refs):
+    part_refs, block_ref = refs[:parts_x], refs[parts_x]
+    tiles_ref, filtered_ref, sems = refs[parts_x + 1 :]
+    me = lax.axis_index("px")
+    count, layer, thickness = part_refs[0].shape
+    owners = [lax.rem(me + (parts_x - step), parts_x) for step in range(parts_x)]
+    copies = []
+    for step, part_ref in enumerate(part_refs):
+        target = filtered_ref.at[pl.ds(owners[step] * count, count)]
+        copies.append(pltpu.make_async_copy(part_ref, target, sems.at[step]))
+    start_all(copies)
+    flat = [ref.reshape(count * layer, thickness) for ref in part_refs]
     lines = [
         jnp.concatenate([ref[pl.ds(n, count, stride=layer), :].astype(bf16) for ref in flat], 0)
         for n in range(layer)
@@ -279,34 +298,14 @@
     product = lax.dot_general(
         block_ref[...], jnp.concatenate(lines, 1), (((1,), (1,)), ((), ())), preferred_element_type=f32
     )
-    starts = range(0, product.shape[0], group_rows)
-    return [
-        jnp.concatenate([product[start : start + group_rows, part * count : (part + 1) * count] for start in starts], 1)
-        for part in range(len(parts))
-    ]
-
-
-def own_margin_kernel(part_ref, block_ref, tiles_ref, filtered_ref, sem):
-    count = part_ref.shape[0]
-    copy = pltpu.make_async_copy(part_ref, filtered_ref.at[pl.ds(lax.axis_index("px") * count, count)], sem)
-    copy.start()
-    tiles_ref[...] = margin_tiles([part_ref], block_ref, tiles_ref.shape[0])[0]
-    copy.wait()
-
-
-def other_margin_kernel(parts_x, own_ref, begun_ref, block_ref, *refs):
-    part_refs, (tiles_ref, filtered_ref, sems) = refs[: parts_x - 1], refs[parts_x - 1 :]
-    me = lax.axis_index("px")
-    count = part_refs[0].shape[0]
-    owners = [lax.rem(me + (parts_x - step), parts_x) for step in range(1, parts_x)]
-    copies = []
-    for place, (owner, part_ref) in enumerate(zip(owners, part_refs)):
-        target = filtered_ref.at[pl.ds(owner * count, count)]
-        copies.append(pltpu.make_async_copy(part_ref, target, sems.at[place]))
-    start_all(copies)
-    tiles_ref[me] = own_ref[...]
-    for owner, tiles in zip(owners, margin_tiles(part_refs, block_ref, tiles_ref.shape[1])):
-        tiles_ref[owner] = tiles
+    groups = tiles_ref.shape[2] // count
+    group_cols = tiles_ref.shape[1] // parts_y
+    for col in range(group_cols):
+        starts = [(group * group_cols + col) * parts_y for group in range(groups)]
+        for step in range(parts_x):
+            columns = slice(step * count, (step + 1) * count)
+            tiles = jnp.concatenate([product[start : start + parts_y, columns] for start in starts], 1)
+            tiles_ref[owners[step], pl.ds(col, parts_y, stride=group_cols), :] = tiles
     wait_all(copies)
 
 
@@ -324,7 +323,7 @@
     pair, other = edges
     other = lax.ppermute(other, "py", others + [(b, a) for a, b in others])
     pair = lax.ppermute(pair, "py", pairs + [(b, a) for a, b in pairs])
-    return [pair, other]
+    return [other, pair]
 
 
 def shifted(value, axis, steps):
@@ -332,7 +331,7 @@
     return lax.ppermute(value, axis, [(source, (source + steps) % count) for source in range(count)])
 
 
-def kernel_call(body, outs, operands, name, scratch=(), in_specs=None, out_specs=None, aliases=None):
+def kernel_call(body, outs, operands, name, scratch=(), in_specs=None, out_specs=None):
     many = isinstance(outs, list)
     return pl.pallas_call(
         body,
@@ -340,7 +339,6 @@
         in_specs=in_specs or [whole] * len(operands),
         out_specs=out_specs or ([whole] * len(outs) if many else whole),
         scratch_shapes=list(scratch),
-        input_output_aliases=aliases or {},
         compiler_params=params,
         name=name,
     )(*operands)
@@ -402,8 +400,13 @@
     for step in range(3):
         if step == 1:
             field_now, block = lax.optimization_barrier((field_now, block))
-            ordered = block.reshape(parts_y, groups, tile_cols // groups, layer * thickness)
-            ordered = ordered.transpose(1, 0, 2, 3).reshape(block_count, layer * thickness)
+            ordered = kernel_call(
+                functools.partial(margin_rows_kernel, layer, parts_y),
+                jax.ShapeDtypeStruct((block_count, layer * thickness), bf16),
+                [block.reshape(block_count * layer, thickness)],
+                "margin_rows",
+                scratch=[pltpu.VMEM((block_count * layer, thickness), f32)],
+            )
         operands = [field_now, levels, high, low] + ([before] if step > 0 else [])
         inner, *back = kernel_call(
             functools.partial(inner_kernel, cells, step), [field] + [table] * (step == 2), operands, "inner"
@@ -427,27 +430,18 @@
                 operands + back,
                 "from_cells",
             )
-    received = [shifted(pieces[step], "px", step) for step in others]
-
-    tiles = jax.ShapeDtypeStruct((block_count // groups, groups * tile_rows), f32)
-    filtered = jax.ShapeDtypeStruct((states, layer, thickness), f32)
-    own, filtered = kernel_call(
-        own_margin_kernel,
-        [tiles, filtered],
-        [pieces[0], ordered],
-        "own_margin",
-        scratch=[pltpu.SemaphoreType.DMA],
+    received = [pieces[0]] + [shifted(pieces[step], "px", step) for step in others]
+
+    tiles, filtered = kernel_call(
+        functools.partial(margin_kernel, parts_x, parts_y),
+        [
+            jax.ShapeDtypeStruct((parts_x, block_count // groups, groups * tile_rows), f32),
+            jax.ShapeDtypeStruct((states, layer, thickness), f32),
+        ],
+        received + [ordered],
+        "margin",
+        scratch=[pltpu.SemaphoreType.DMA((parts_x,))],
         out_specs=[whole, anywhere],
-    )
-    tiles, filtered = kernel_call(
-        functools.partial(other_margin_kernel, parts_x),
-        [jax.ShapeDtypeStruct((parts_x,) + own.shape, f32), jax.ShapeDtypeStruct(filtered.shape, f32)],
-        [own, filtered, ordered] + received,
-        "other_margin",
-        scratch=[pltpu.SemaphoreType.DMA((parts_x - 1,))],
-        in_specs=[whole, anywhere] + [whole] * parts_x,
-        out_specs=[whole, anywhere],
-        aliases={1: 1},
     )
     tiles = tiles.reshape(parts_x * parts_y, tile_cols // groups, groups * tile_rows)
     tiles = lax.all_to_all(tiles, ("px", "py"), 0, 0, tiled=True)

time: 51.5 us -> 51.3 us (level)
  waiting for transfers between devices: 8.22 us -> 13.2 us
  local copies, waits for them, and re-layouts: 5.31 us -> 1.11 us
  starting transfers between devices: 17 us -> 15.3 us
  Pallas kernels: 9.07 us -> 9.69 us
    reshape x3 -> x0, local copies, waits for them, and re-layouts: 4.21 us -> none  [the longest x2 2.87 us: local(): block.reshape(parts_y, groups, tile_cols // groups, layer * thickness)]
    ppermute x3, starting transfers between devices: 3.48 us -> 0.01 us  [swapped(): pair = lax.ppermute(pair, 'py', pairs + [(b, a) for a, b in pairs])]
    ppermute x3, waiting for transfers between devices: 5.51 us -> 8.58 us  [swapped(): other = lax.ppermute(other, 'py', others + [(b, a) for a, b in others])]
    ppermute x3, starting transfers between devices: 12.9 us -> 14.7 us  [swapped(): other = lax.ppermute(other, 'py', others + [(b, a) for a, b in others])]
    ppermute x3, waiting for transfers between devices: 0.56 us -> 1.69 us  [swapped(): pair = lax.ppermute(pair, 'py', pairs + [(b, a) for a, b in pairs])]
    ppermute x3, waiting for transfers between devices: 2.15 us -> 2.9 us  [shifted(): lax.ppermute(value, axis, [(source, (source + steps) % count) for source...]
    pallas_call x12, Pallas kernels: 9.07 us -> 9.69 us  [kernel_call(): pl.pallas_call(body, out_shape=outs, in_specs=in_specs or [whole] * len(o...]
  transfers between devices with their start and end apart: 9 -> 9, of which waited for: 6 -> 9; matrix products, arithmetic and copies ran while one was open for 8% -> 0% of each run, Pallas kernels for 8% -> 9%
where the time goes in v10:
time: 51.3 us; the launch traced here: 51.1 us
  starting transfers between devices  15.3 us (30%)
  waiting for transfers between devices  13.2 us (26%)
  blocking collectives  11.2 us (22%)
  Pallas kernels  9.69 us (19%)
  local copies, waits for them, and re-layouts  1.11 us (2%)
  between operations  0.72 us (1%)
    ppermute x3, starting transfers between devices, swapped(): other = lax.ppermute(other, 'py', others + [(b, a) for a, b in others])  14.7 us
    all_to_all x1, blocking collectives, local(): tiles = lax.all_to_all(tiles, ('px', 'py'), 0, 0, tiled=True)  11.2 us
    pallas_call x12, Pallas kernels, kernel_call(): pl.pallas_call(body, out_shape=outs, in_specs=in_specs or [whole] * len(o...  9.69 us
    ppermute x3, waiting for transfers between devices, swapped(): other = lax.ppermute(other, 'py', others + [(b, a) for a, b in others])  8.58 us
    ppermute x3, waiting for transfers between devices, shifted(): lax.ppermute(value, axis, [(source, (source + steps) % count) for source...  2.9 us
    ppermute x3, waiting for transfers between devices, swapped(): pair = lax.ppermute(pair, 'py', pairs + [(b, a) for a, b in pairs])  1.69 us
    dynamic_slice x1, local copies, waits for them, and re-layouts, part_for(): lax.dynamic_slice_in_dim(span_rows, lax.rem(me + step, parts_x) * mine, m...  1.1 us
  transfers between devices with their start and end apart: 9, of which 9 were waited for; matrix products, arithmetic and copies ran while one was open for 0% of the time, Pallas kernels for 9%

profile of v10, /device:TPU:0, one launch (start us, length us, event | category | flops | bytes accessed | tf_op | source)
XLA Modules:
  0.0 51.1 jit_solution(15533430271088452407)
XLA Ops:
  0.7 1.1 %constant_dynamic-slice_fusion = (f32[32,16,128]{2,1,0:T(8,128)S(1)}, f32[32,16,128]{2,1,0:T(8,128)S(1)}) fusion(f32[64,16,128]{2,1,0:T(8,128)} %bitcast.10, s32[]{:T(128)S(6)} %select_n.7, s32[]{:T(128)S(6)} %select_n.6), kind=kLoop, calls=%fused_computation | loop fusion | bytes 1048584 | tf_op jit(solution)/shard_map/dynamic_slice | solution.py:373
  1.8 0.5 %collective-permute-start = (f32[32,16,128]{2,1,0:T(8,128)S(1)}, f32[32,16,128]{2,1,0:T(8,128)S(1)}, u32[]{:S(2)}, u32[]{:S(2)}) collective-permute-start(f32[32,16,128]{2,1,0:T(8,128)S(1)} %get-tuple-element.48), channel_id=1, source_target_pairs={{0,16},{16,0},{1,17},{17,1},{2,18},{18,2},{3,19},{19,3},{4,20},{20... | collective-permute-start | bytes 786440 | tf_op jit(solution)/shard_map/ppermute | solution.py:331
  2.3 0.9 %assemble.1 = (bf16[208,208]{1,0:T(8,128)(2,1)S(1)}, bf16[208,208]{1,0:T(8,128)(2,1)S(1)}, bf16[160,144]{1,0:T(8,128)(2,1)S(1)}, bf16[512,512]{1,0:T(8,128)(2,1)S(1)}) custom-call(f32[125,125]{1,0:T(8,128)S(1)} %copy-done.1), custom_call_target="tpu_custom_call" | custom-call | tf_op jit(solution)/shard_map/assemble/pallas_call | solution.py:336
  3.4 0.8 %to_cells.1 = (f32[4,4,8,1024]{3,2,1,0:T(8,128)S(1)}, f32[4,8,1024]{2,1,0:T(8,128)S(1)}, f32[4,8,1024]{2,1,0:T(8,128)S(1)}) custom-call(f32[32,16,128]{2,1,0:T(8,128)S(1)} %get-tuple-element.49.refs_0_, f32[32,16,128]{2,1,0:T(8,128)S(1)} %collective-permute-done.refs_1_, bf16[512,512]{1,0:T(8,128)(2,1)S(1)} %get-tuple-element.25.refs_2_, ...), custom_call_target="tpu_custom_call" | custom-call | tf_op jit(solution)/shard_map/to_cells/pallas_call | solution.py:336
  4.2 6.9 %collective-permute-start.2 = (f32[4,8,1024]{2,1,0:T(8,128)S(1)}, f32[4,8,1024]{2,1,0:T(8,128)S(1)}, u32[]{:S(2)}, u32[]{:S(2)}) collective-permute-start(f32[4,8,1024]{2,1,0:T(8,128)S(1)} %get-tuple-element.29), channel_id=1, source_target_pairs={{1,2},{3,4},{5,6},{7,8},{9,10},{11,12},{13,14},{15,0},{2,1},{4,3},... | collective-permute-start | bytes 393224 | tf_op jit(solution)/shard_map/ppermute | solution.py:324
  11.2 1.2 %collective-permute-done.1.refs_1_ = f32[1,16,128]{2,1,0:T(8,128)S(1)} collective-permute-done((f32[1,16,128]{2,1,0:T(8,128)S(1)}, f32[1,16,128]{2,1,0:T(8,128)S(1)}, u32[]{:S(2)}, u32[]{:S(2)}) %collective-permute-start.1) | collective-permute-done | bytes 8224 | tf_op jit(solution)/shard_map/ppermute | solution.py:331
  12.5 0.7 %inner.3.inner_ref = f32[4,4,8,1024]{3,2,1,0:T(8,128)S(1)} custom-call(f32[4,4,8,1024]{3,2,1,0:T(8,128)S(1)} %get-tuple-element.28.refs_0_.refs_4_, f32[4,4,8,128]{3,2,1,0:T(8,128)S(1)} %levels.1.refs_1_, bf16[208,208]{1,0:T(8,128)(2,1)S(1)} %get-tuple-element.26.refs_3_.refs_2_.high_ref, bf16[208,208]{1,0:T(8,128)(2,1)S(1)} %get-tuple-element.27.refs_4_.refs_3_.low_ref), custom_call_target="tpu_custom_call" | custom-call | tf_op jit(solution)/shard_map/inner/pallas_call | solution.py:336
  13.2 1.9 %collective-permute-done.2.from_other_ref = f32[4,8,1024]{2,1,0:T(8,128)S(1)} collective-permute-done((f32[4,8,1024]{2,1,0:T(8,128)S(1)}, f32[4,8,1024]{2,1,0:T(8,128)S(1)}, u32[]{:S(2)}, u32[]{:S(2)}) %collective-permute-start.2) | collective-permute-done | bytes 131104 | tf_op jit(solution)/shard_map/ppermute | solution.py:324
  15.1 1.4 %collective-permute-done.3.from_pair_ref = f32[4,8,1024]{2,1,0:T(8,128)S(1)} collective-permute-done((f32[4,8,1024]{2,1,0:T(8,128)S(1)}, f32[4,8,1024]{2,1,0:T(8,128)S(1)}, u32[]{:S(2)}, u32[]{:S(2)}) %collective-permute-start.3) | collective-permute-done | bytes 131104 | tf_op jit(solution)/shard_map/ppermute | solution.py:325
  16.4 0.8 %finish.2 = (f32[4,4,8,1024]{3,2,1,0:T(8,128)S(1)}, f32[4,8,1024]{2,1,0:T(8,128)S(1)}, f32[4,8,1024]{2,1,0:T(8,128)S(1)}) custom-call(f32[4,4,8,1024]{3,2,1,0:T(8,128)S(1)} %inner.3.inner_ref, f32[4,8,1024]{2,1,0:T(8,128)S(1)} %collective-permute-done.2.from_other_ref, f32[4,8,1024]{2,1,0:T(8,128)S(1)} %collective-permute-done.3.from_pair_ref, ...), custom_call_target="tpu_custom_call" | custom-call | tf_op jit(solution)/shard_map/finish/pallas_call | solution.py:336
  17.2 4.0 %collective-permute-start.4 = (f32[4,8,1024]{2,1,0:T(8,128)S(1)}, f32[4,8,1024]{2,1,0:T(8,128)S(1)}, u32[]{:S(2)}, u32[]{:S(2)}) collective-permute-start(f32[4,8,1024]{2,1,0:T(8,128)S(1)} %get-tuple-element.34), channel_id=1, source_target_pairs={{1,2},{3,4},{5,6},{7,8},{9,10},{11,12},{13,14},{15,0},{2,1},{4,3},... | collective-permute-start | bytes 393224 | tf_op jit(solution)/shard_map/ppermute | solution.py:324
  21.3 0.6 %inner.4.inner_ref = f32[4,4,8,1024]{3,2,1,0:T(8,128)S(1)} custom-call(f32[4,4,8,1024]{3,2,1,0:T(8,128)S(1)} %get-tuple-element.33.refs_0_.refs_4_, f32[4,4,8,128]{3,2,1,0:T(8,128)S(1)} %levels.1.refs_1_, bf16[208,208]{1,0:T(8,128)(2,1)S(1)} %get-tuple-element.26.refs_3_.refs_2_.high_ref, bf16[208,208]{1,0:T(8,128)(2,1)S(1)} %get-tuple-element.27.refs_4_.refs_3_.low_ref, ...), custom_call_target="tpu_custom_call" | custom-call | tf_op jit(solution)/shard_map/inner/pallas_call | solution.py:336
  21.9 4.0 %collective-permute-done.4.from_other_ref = f32[4,8,1024]{2,1,0:T(8,128)S(1)} collective-permute-done((f32[4,8,1024]{2,1,0:T(8,128)S(1)}, f32[4,8,1024]{2,1,0:T(8,128)S(1)}, u32[]{:S(2)}, u32[]{:S(2)}) %collective-permute-start.4) | collective-permute-done | bytes 131104 | tf_op jit(solution)/shard_map/ppermute | solution.py:324
  25.9 0.3 collective-permute-done.5.from_pair_ref
  26.2 0.8 %finish.3 = (f32[4,4,8,1024]{3,2,1,0:T(8,128)S(1)}, f32[4,8,1024]{2,1,0:T(8,128)S(1)}, f32[4,8,1024]{2,1,0:T(8,128)S(1)}) custom-call(f32[4,4,8,1024]{3,2,1,0:T(8,128)S(1)} %inner.4.inner_ref, f32[4,8,1024]{2,1,0:T(8,128)S(1)} %collective-permute-done.4.from_other_ref, f32[4,8,1024]{2,1,0:T(8,128)S(1)} %collective-permute-done.5.from_pair_ref, ...), custom_call_target="tpu_custom_call" | custom-call | tf_op jit(solution)/shard_map/finish/pallas_call | solution.py:336
  27.0 3.7 %collective-permute-start.6 = (f32[4,8,1024]{2,1,0:T(8,128)S(1)}, f32[4,8,1024]{2,1,0:T(8,128)S(1)}, u32[]{:S(2)}, u32[]{:S(2)}) collective-permute-start(f32[4,8,1024]{2,1,0:T(8,128)S(1)} %get-tuple-element.40), channel_id=1, source_target_pairs={{1,2},{3,4},{5,6},{7,8},{9,10},{11,12},{13,14},{15,0},{2,1},{4,3},... | collective-permute-start | bytes 393224 | tf_op jit(solution)/shard_map/ppermute | solution.py:324
  30.7 1.3 %margin_rows.1.refs_2_ = bf16[256,2048]{1,0:T(8,128)(2,1)S(1)} custom-call(bf16[4096,128]{1,0:T(8,128)(2,1)S(1)} %bitcast.6), custom_call_target="tpu_custom_call" | custom-call | tf_op jit(solution)/shard_map/margin_rows/pallas_call | solution.py:336
  32.1 0.9 %inner.5 = (f32[4,4,8,1024]{3,2,1,0:T(8,128)S(1)}, bf16[512,512]{1,0:T(8,128)(2,1)S(1)}) custom-call(f32[4,4,8,1024]{3,2,1,0:T(8,128)S(1)} %get-tuple-element.36.refs_0_, f32[4,4,8,128]{3,2,1,0:T(8,128)S(1)} %levels.1.refs_1_, bf16[208,208]{1,0:T(8,128)(2,1)S(1)} %get-tuple-element.26.refs_3_.refs_2_.high_ref, ...), custom_call_target="tpu_custom_call" | custom-call | tf_op jit(solution)/shard_map/inner/pallas_call | solution.py:336
  33.0 2.7 %collective-permute-done.6.refs_1_ = f32[4,8,1024]{2,1,0:T(8,128)S(1)} collective-permute-done((f32[4,8,1024]{2,1,0:T(8,128)S(1)}, f32[4,8,1024]{2,1,0:T(8,128)S(1)}, u32[]{:S(2)}, u32[]{:S(2)}) %collective-permute-start.6) | collective-permute-done | bytes 131104 | tf_op jit(solution)/shard_map/ppermute | solution.py:324
  35.7 0.8 %from_cells.1 = (f32[32,16,128]{2,1,0:T(8,128)S(1)}, f32[32,16,128]{2,1,0:T(8,128)S(1)}) custom-call(f32[4,4,8,1024]{3,2,1,0:T(8,128)S(1)} %get-tuple-element.39.refs_0_, f32[4,8,1024]{2,1,0:T(8,128)S(1)} %collective-permute-done.6.refs_1_, f32[4,8,1024]{2,1,0:T(8,128)S(1)} %collective-permute-done.7.refs_2_, ...), custom_call_target="tpu_custom_call" | custom-call | tf_op jit(solution)/shard_map/from_cells/pallas_call | solution.py:336
  36.6 1.5 %collective-permute-done.8.refs_1_ = f32[32,16,128]{2,1,0:T(8,128)S(1)} collective-permute-done((f32[32,16,128]{2,1,0:T(8,128)S(1)}, f32[32,16,128]{2,1,0:T(8,128)S(1)}, u32[]{:S(2)}, u32[]{:S(2)}) %collective-permute-start.8) | collective-permute-done | bytes 262176 | tf_op jit(solution)/shard_map/ppermute | solution.py:331
  38.1 1.2 %margin.1 = (f32[2,64,128]{2,1,0:T(8,128)S(1)}, f32[64,16,128]{2,1,0:T(8,128)}) custom-call(f32[32,16,128]{2,1,0:T(8,128)S(1)} %get-tuple-element.43.refs_0_, f32[32,16,128]{2,1,0:T(8,128)S(1)} %collective-permute-done.8.refs_1_, bf16[256,2048]{1,0:T(8,128)(2,1)S(1)} %margin_rows.1.refs_2_), custom_call_target="tpu_custom_call" | custom-call | tf_op jit(solution)/shard_map/margin/pallas_call | solution.py:336
  39.3 11.2 %all_to_all.5.tiles_ref = f32[32,4,128]{2,1,0:T(4,128)S(1)} all-to-all(f32[32,4,128]{2,1,0:T(4,128)S(1)} %bitcast.7), channel_id=1, replica_groups=mesh['px'=2,'py'=16] {'px','py'}, dimensions={0} | all-to-all | bytes 131072 | tf_op jit(solution)/shard_map/all_to_all | solution.py:447
  50.4 0.7 %tile_sum.1 = f32[16,32]{1,0:T(8,128)} custom-call(f32[32,4,128]{2,1,0:T(4,128)S(1)} %all_to_all.5.tiles_ref), custom_call_target="tpu_custom_call" | custom-call | tf_op jit(solution)/shard_map/tile_sum/pallas_call | solution.py:336
  (14 shorter events, 0.5 us)
Async XLA Ops:
  0.6 1.6 %copy-start.1 = (f32[125,125]{1,0:T(8,128)S(1)}, f32[125,125]{1,0:T(8,128)}, u32[]{:S(2)}) copy-start(f32[125,125]{1,0:T(8,128)} %cell_ref.1) | copy-start | bytes 187504
  1.8 1.7 %collective-permute-start = (f32[32,16,128]{2,1,0:T(8,128)S(1)}, f32[32,16,128]{2,1,0:T(8,128)S(1)}, u32[]{:S(2)}, u32[]{:S(2)}) collective-permute-start(f32[32,16,128]{2,1,0:T(8,128)S(1)} %get-tuple-element.48), channel_id=1, source_target_pairs={{0,16},{16,0},{1,17},{17,1},{2,18},{18,2},{3,19},{19,3},{4,20},{20... | collective-permute-start | bytes 786440 | tf_op jit(solution)/shard_map/ppermute | solution.py:331
  3.4 7.7 %copy-start.2 = (f32[4,4,128]{2,1,0:T(4,128)S(1)}, f32[4,4,128]{2,1,0:T(4,128)}, u32[]{:S(2)}) copy-start(f32[4,4,128]{2,1,0:T(4,128)} %param.5) | copy-start | bytes 24580
  4.2 10.8 %collective-permute-start.2 = (f32[4,8,1024]{2,1,0:T(8,128)S(1)}, f32[4,8,1024]{2,1,0:T(8,128)S(1)}, u32[]{:S(2)}, u32[]{:S(2)}) collective-permute-start(f32[4,8,1024]{2,1,0:T(8,128)S(1)} %get-tuple-element.29), channel_id=1, source_target_pairs={{1,2},{3,4},{5,6},{7,8},{9,10},{11,12},{13,14},{15,0},{2,1},{4,3},... | collective-permute-start | bytes 393224 | tf_op jit(solution)/shard_map/ppermute | solution.py:324
  11.1 5.3 %collective-permute-start.3 = (f32[4,8,1024]{2,1,0:T(8,128)S(1)}, f32[4,8,1024]{2,1,0:T(8,128)S(1)}, u32[]{:S(2)}, u32[]{:S(2)}) collective-permute-start(f32[4,8,1024]{2,1,0:T(8,128)S(1)} %get-tuple-element.30), channel_id=1, source_target_pairs={{0,1},{2,3},{4,5},{6,7},{8,9},{10,11},{12,13},{14,15},{1,0},{3,2},... | collective-permute-start | bytes 393224 | tf_op jit(solution)/shard_map/ppermute | solution.py:325
  11.2 1.2 %collective-permute-start.1 = (f32[1,16,128]{2,1,0:T(8,128)S(1)}, f32[1,16,128]{2,1,0:T(8,128)S(1)}, u32[]{:S(2)}, u32[]{:S(2)}) collective-permute-start(f32[1,16,128]{2,1,0:T(8,128)S(1)} %bitcast.8), channel_id=1, source_target_pairs={{0,16},{16,0},{1,17},{17,1},{2,18},{18,2},{3,19},{19,3},{4,20},{20... | collective-permute-start | bytes 24584 | tf_op jit(solution)/shard_map/ppermute | solution.py:331
  17.2 8.7 %collective-permute-start.4 = (f32[4,8,1024]{2,1,0:T(8,128)S(1)}, f32[4,8,1024]{2,1,0:T(8,128)S(1)}, u32[]{:S(2)}, u32[]{:S(2)}) collective-permute-start(f32[4,8,1024]{2,1,0:T(8,128)S(1)} %get-tuple-element.34), channel_id=1, source_target_pairs={{1,2},{3,4},{5,6},{7,8},{9,10},{11,12},{13,14},{15,0},{2,1},{4,3},... | collective-permute-start | bytes 393224 | tf_op jit(solution)/shard_map/ppermute | solution.py:324
  21.3 5.0 %collective-permute-start.5 = (f32[4,8,1024]{2,1,0:T(8,128)S(1)}, f32[4,8,1024]{2,1,0:T(8,128)S(1)}, u32[]{:S(2)}, u32[]{:S(2)}) collective-permute-start(f32[4,8,1024]{2,1,0:T(8,128)S(1)} %get-tuple-element.35), channel_id=1, source_target_pairs={{0,1},{2,3},{4,5},{6,7},{8,9},{10,11},{12,13},{14,15},{1,0},{3,2},... | collective-permute-start | bytes 393224 | tf_op jit(solution)/shard_map/ppermute | solution.py:325
  21.3 9.5 %copy-start = (bf16[256,4,4,128]{3,2,1,0:T(4,128)(2,1)S(1)}, bf16[256,4,4,128]{3,2,1,0:T(4,128)(2,1)}, u32[]{:S(2)}) copy-start(bf16[256,4,4,128]{3,2,1,0:T(4,128)(2,1)} %param.7) | copy-start | bytes 3145732
  27.0 8.6 %collective-permute-start.6 = (f32[4,8,1024]{2,1,0:T(8,128)S(1)}, f32[4,8,1024]{2,1,0:T(8,128)S(1)}, u32[]{:S(2)}, u32[]{:S(2)}) collective-permute-start(f32[4,8,1024]{2,1,0:T(8,128)S(1)} %get-tuple-element.40), channel_id=1, source_target_pairs={{1,2},{3,4},{5,6},{7,8},{9,10},{11,12},{13,14},{15,0},{2,1},{4,3},... | collective-permute-start | bytes 393224 | tf_op jit(solution)/shard_map/ppermute | solution.py:324
  30.7 5.0 %collective-permute-start.7 = (f32[4,8,1024]{2,1,0:T(8,128)S(1)}, f32[4,8,1024]{2,1,0:T(8,128)S(1)}, u32[]{:S(2)}, u32[]{:S(2)}) collective-permute-start(f32[4,8,1024]{2,1,0:T(8,128)S(1)} %get-tuple-element.41), channel_id=1, source_target_pairs={{0,1},{2,3},{4,5},{6,7},{8,9},{10,11},{12,13},{14,15},{1,0},{3,2},... | collective-permute-start | bytes 393224 | tf_op jit(solution)/shard_map/ppermute | solution.py:325
  36.5 1.6 %collective-permute-start.8 = (f32[32,16,128]{2,1,0:T(8,128)S(1)}, f32[32,16,128]{2,1,0:T(8,128)S(1)}, u32[]{:S(2)}, u32[]{:S(2)}) collective-permute-start(f32[32,16,128]{2,1,0:T(8,128)S(1)} %get-tuple-element.44), channel_id=1, source_target_pairs={{0,16},{16,0},{1,17},{17,1},{2,18},{18,2},{3,19},{19,3},{4,20},{20... | collective-permute-start | bytes 786440 | tf_op jit(solution)/shard_map/ppermute | solution.py:331

commit v11 on v7

--- a/solution.py
+++ b/solution.py
@@ -225,7 +225,7 @@
             out_ref[iz, iy] = total if step == 0 else total - before_ref[iz, iy]
 
 
-def finish(cells, step, inner_ref, pair_ref, other_ref, matrix_ref):
+def finish(cells, step, inner_ref, other_ref, pair_ref, matrix_ref):
     nodes, width = inner_ref.shape[2:]
     even = even_place()
     halo = [jnp.where(even, pair_ref[iz], other_ref[iz]) for iz in range(4)]
@@ -247,17 +247,17 @@
     return result
 
 
-def finish_kernel(cells, step, inner_ref, from_pair_ref, from_other_ref, matrix_ref, high_ref, low_ref, next_ref, pair_ref, other_ref):
-    value = finish(cells, step, inner_ref, from_pair_ref, from_other_ref, matrix_ref)
+def finish_kernel(cells, step, inner_ref, from_other_ref, from_pair_ref, matrix_ref, high_ref, low_ref, next_ref, pair_ref, other_ref):
+    value = finish(cells, step, inner_ref, from_other_ref, from_pair_ref, matrix_ref)
     for (iz, iy), part in value.items():
         next_ref[iz, iy] = part
     send_edges(high_ref, low_ref, value, pair_ref, other_ref, cells)
 
 
 def last_kernel(cells, second, parts_x, parts_y, *refs):
-    inner_ref, pair_ref, other_ref, matrix_ref, order_ref = refs[:5]
+    inner_ref, other_ref, pair_ref, matrix_ref, order_ref = refs[:5]
     block_refs, out_refs, tiles_ref = refs[5 : 5 + parts_x], refs[5 + parts_x : -1], refs[-1]
-    value = finish(cells, 2, inner_ref, pair_ref, other_ref, matrix_ref)
+    value = finish(cells, 2, inner_ref, other_ref, pair_ref, matrix_ref)
     states, layer, thickness = out_refs[0].shape
     first = layer // second
     nodes = parts_x * first
@@ -286,9 +286,10 @@
         flat = out_ref.reshape(states * layer, thickness)
         lines = [flat[pl.ds(n, states, stride=layer), :].astype(bf16) for n in range(layer)]
         added = lax.dot_general(
-            block_ref[...], jnp.concatenate(lines, 1), (((1,), (1,)), ((), ())), preferred_element_type=f32
+            jnp.concatenate(lines, 1), block_ref[...], (((1,), (1,)), ((), ())), preferred_element_type=f32
         )
         product = added if product is None else product + added
+    product = product.T
     groups = tiles_ref.shape[1] // states
     group_cols = tiles_ref.shape[0] // parts_y
     for col in range(group_cols):
@@ -297,8 +298,8 @@
         tiles_ref[pl.ds(col, parts_y, stride=group_cols), :] = lines
 
 
-def result_kernel(parts_x, tiles_ref, *refs):
-    part_refs, (out_ref, filtered_ref, sems) = refs[:parts_x], refs[parts_x:]
+def join_kernel(parts_x, *refs):
+    part_refs, filtered_ref, sems = refs[:parts_x], refs[parts_x], refs[parts_x + 1]
     me = lax.axis_index("px")
     count = filtered_ref.shape[0] // parts_x
     copies = []
@@ -306,11 +307,14 @@
         owner = lax.rem(me + (parts_x - step), parts_x)
         copies.append(pltpu.make_async_copy(part_ref, filtered_ref.at[pl.ds(owner * count, count)], sems.at[step]))
     start_all(copies)
+    wait_all(copies)
+
+
+def sum_kernel(tiles_ref, out_ref):
     total = jnp.sum(tiles_ref[...], axis=0)
     tile_rows = out_ref.shape[1]
     groups = total.shape[1] // tile_rows
     out_ref[...] = jnp.concatenate([total[:, g * tile_rows : (g + 1) * tile_rows] for g in range(groups)], 0)
-    wait_all(copies)
 
 
 def swapped(edges):
@@ -320,7 +324,7 @@
     pair, other = edges
     other = lax.ppermute(other, "py", others + [(b, a) for a, b in others])
     pair = lax.ppermute(pair, "py", pairs + [(b, a) for a, b in pairs])
-    return [pair, other]
+    return [other, pair]
 
 
 def shifted(value, axis, steps):
@@ -328,8 +332,9 @@
     return lax.ppermute(value, axis, [(source, (source + steps) % count) for source in range(count)])
 
 
-def kernel_call(body, outs, operands, name, scratch=(), in_specs=None, out_specs=None):
+def kernel_call(body, outs, operands, name, scratch=(), in_specs=None, out_specs=None, work=0):
     many = isinstance(outs, list)
+    moved = sum(a.size * a.dtype.itemsize for a in list(operands) + (outs if many else [outs]))
     return pl.pallas_call(
         body,
         out_shape=outs,
@@ -337,6 +342,7 @@
         out_specs=out_specs or ([whole] * len(outs) if many else whole),
         scratch_shapes=list(scratch),
         compiler_params=params,
+        cost_estimate=pl.CostEstimate(flops=work or moved, bytes_accessed=moved, transcendentals=0),
         name=name,
     )(*operands)
 
@@ -352,24 +358,24 @@
     rows = PADDED * nodes
     others = range(1, parts_x)
 
-    width = mine * cells
+    group = lanes // cells * thickness
     matrix = jax.ShapeDtypeStruct((rows, rows), bf16)
+    table = jax.ShapeDtypeStruct((group, group), bf16)
     from_halo = jax.ShapeDtypeStruct((20 * nodes, 3 * (rows - 20 * nodes)), bf16)
-    table = jax.ShapeDtypeStruct((4 * lanes, 4 * lanes), bf16)
+
+    chunks = 1
+    count = mine // chunks
+    width = count * cells
     field = jax.ShapeDtypeStruct((4, 4, nodes, width), f32)
     message = jax.ShapeDtypeStruct((4, nodes, width), f32)
-    part = jax.ShapeDtypeStruct((mine, layer, thickness), f32)
-
+    part = jax.ShapeDtypeStruct((count, layer, thickness), f32)
     me = lax.axis_index("px")
     span_rows = span.reshape(states, layer, thickness)
 
     def part_for(step):
         return lax.dynamic_slice_in_dim(span_rows, lax.rem(me + step, parts_x) * mine, mine, 0)
 
-    sent = [part_for(step) for step in others]
-    sent, span_rows = lax.optimization_barrier((sent, span_rows))
-    parts = [shifted(piece, "px", step) for step, piece in enumerate(sent, 1)]
-    parts = [part_for(0)] + parts[::-1]
+    parts = [part_for(0)] + [shifted(part_for(step), "px", step) for step in reversed(others)]
     high, low, halo_matrix, order = kernel_call(
         functools.partial(matrix_kernel, cells, nodes),
         [matrix, matrix, from_halo, table],
@@ -377,7 +383,7 @@
         "assemble",
     )
     field_now, *edges = kernel_call(
-        functools.partial(to_cells_kernel, cells, second, parts_x, mine),
+        functools.partial(to_cells_kernel, cells, second, parts_x, count),
         [field, message, message],
         parts + [order, high, low],
         "to_cells",
@@ -395,30 +401,29 @@
     groups = min(tile_cols, lanes // tile_rows)
     before = None
     for step in range(3):
-        operands = [field_now, levels, high, low] + ([before] if step > 0 else [])
-        inner = kernel_call(
-            functools.partial(inner_kernel, cells, step), [field] + [table] * (step == 2), operands, "inner"
-        )
-        inner, back = inner if step == 2 else (inner[0], None)
-        if step == 0:
-            inner, block = lax.optimization_barrier((inner, block))
+        if step == 1:
+            field_now, block = lax.optimization_barrier((field_now, block))
             wide = kernel_call(
                 widen_kernel,
                 jax.ShapeDtypeStruct((block_count * layer, thickness), f32),
                 [block.reshape(block_count * layer, thickness)],
                 "widen",
             )
-            wides = [wide] + [shifted(wide, "px", step) for step in others]
-        if step == 1:
             blocks = [
                 kernel_call(
                     functools.partial(margin_rows_kernel, layer, parts_y),
                     jax.ShapeDtypeStruct((block_count, layer * thickness), bf16),
-                    [wide],
+                    [rows],
                     "margin_rows",
                 )
-                for wide in lax.optimization_barrier((inner, wides))[1]
+                for rows in [wide] + [shifted(wide, "px", away) for away in others]
             ]
+        operands = [field_now, levels, high, low] + ([before] if step > 0 else [])
+        inner, *back = kernel_call(
+            functools.partial(inner_kernel, cells, step), [field] + [table] * (step == 2), operands, "inner"
+        )
+        if step == 2:
+            inner, blocks = lax.optimization_barrier((inner, blocks))
         operands = [inner] + edges + [halo_matrix]
         if step < 2:
             before = field_now
@@ -433,24 +438,21 @@
             *pieces, tiles = kernel_call(
                 functools.partial(last_kernel, cells, second, parts_x, parts_y),
                 [part] * parts_x + [jax.ShapeDtypeStruct((block_count // groups, groups * tile_rows), f32)],
-                operands + [back] + [blocks[0]] + blocks[:0:-1],
+                operands + back + [blocks[0]] + blocks[:0:-1],
                 "last",
             )
-
     pieces = [pieces[0]] + [shifted(pieces[step], "px", step) for step in others]
     tiles = tiles.reshape(parts_y, tile_cols // groups, groups * tile_rows)
     tiles = lax.all_to_all(tiles, "py", 0, 0, tiled=True)
-    margin, filtered = kernel_call(
-        functools.partial(result_kernel, parts_x),
-        [
-            jax.ShapeDtypeStruct((tile_cols, tile_rows), f32),
-            jax.ShapeDtypeStruct((states, layer, thickness), f32),
-        ],
-        [tiles] + pieces,
-        "result",
+    filtered = kernel_call(
+        functools.partial(join_kernel, parts_x),
+        jax.ShapeDtypeStruct((states, layer, thickness), f32),
+        pieces,
+        "join",
         scratch=[pltpu.SemaphoreType.DMA((parts_x,))],
-        out_specs=[whole, anywhere],
+        out_specs=anywhere,
     )
+    margin = kernel_call(sum_kernel, jax.ShapeDtypeStruct((tile_cols, tile_rows), f32), [tiles], "tile_sum")
     return filtered.reshape(span.shape), margin.T
 
 

time: 54.8 us -> 53.6 us (0.978)
  starting transfers between devices: 17.2 us -> 15.5 us
  waiting for transfers between devices: 9.46 us -> 11.1 us
  local copies, waits for them, and re-layouts: 2.59 us -> 1.92 us
    ppermute x3, starting transfers between devices: 3.14 us -> 0.01 us  [swapped(): pair = lax.ppermute(pair, 'py', pairs + [(b, a) for a, b in pairs])]
    ppermute x3, starting transfers between devices: 12.9 us -> 14.7 us  [swapped(): other = lax.ppermute(other, 'py', others + [(b, a) for a, b in others])]
    unnamed x8 -> x6, local copies, waits for them, and re-layouts: 2.55 us -> 0.85 us
    ppermute x3, waiting for transfers between devices: 6.87 us -> 8.4 us  [swapped(): other = lax.ppermute(other, 'py', others + [(b, a) for a, b in others])]
    dynamic_slice x2 -> x1, local copies, waits for them, and re-layouts: 0.04 us -> 1.07 us  [part_for(): lax.dynamic_slice_in_dim(span_rows, lax.rem(me + step, parts_x) * mine, m...]
    ppermute x4, waiting for transfers between devices: 0.02 us -> 1.02 us  [shifted(): lax.ppermute(value, axis, [(source, (source + steps) % count) for source...]
    ppermute x3, waiting for transfers between devices: 2.56 us -> 1.67 us  [swapped(): pair = lax.ppermute(pair, 'py', pairs + [(b, a) for a, b in pairs])]
    pallas_call x13 -> x14, Pallas kernels: 11.8 us -> 11.8 us  [kernel_call(): pl.pallas_call(body, out_shape=outs, in_specs=in_specs or [whole] * len(o...]
  transfers between devices with their start and end apart: 10 -> 10, of which waited for: 5 -> 6; matrix products, arithmetic and copies ran while one was open for 0% -> 0% of each run, Pallas kernels for 12% -> 14%
where the time goes in v11:
time: 53.6 us; the launch traced here: 53.4 us
  starting transfers between devices  15.5 us (29%)
  blocking collectives  12.3 us (23%)
  Pallas kernels  11.8 us (22%)
  waiting for transfers between devices  11.1 us (21%)
  local copies, waits for them, and re-layouts  1.92 us (4%)
  between operations  0.76 us (1%)
    ppermute x3, starting transfers between devices, swapped(): other = lax.ppermute(other, 'py', others + [(b, a) for a, b in others])  14.7 us
    all_to_all x1, blocking collectives, local(): tiles = lax.all_to_all(tiles, 'py', 0, 0, tiled=True)  12.3 us
    pallas_call x14, Pallas kernels, kernel_call(): pl.pallas_call(body, out_shape=outs, in_specs=in_specs or [whole] * len(o...  11.8 us
    ppermute x3, waiting for transfers between devices, swapped(): other = lax.ppermute(other, 'py', others + [(b, a) for a, b in others])  8.4 us
    ppermute x3, waiting for transfers between devices, swapped(): pair = lax.ppermute(pair, 'py', pairs + [(b, a) for a, b in pairs])  1.67 us
  transfers between devices with their start and end apart: 10, of which 6 were waited for; matrix products, arithmetic and copies ran while one was open for 0% of the time, Pallas kernels for 14%

profile of v11, /device:TPU:0, one launch (start us, length us, event | category | flops | bytes accessed | tf_op | source)
XLA Modules:
  0.0 53.4 jit_solution(115096389186994733)
XLA Ops:
  0.7 1.1 %constant_dynamic-slice_fusion = (f32[32,16,128]{2,1,0:T(8,128)S(1)}, f32[32,16,128]{2,1,0:T(8,128)S(1)}) fusion(f32[64,16,128]{2,1,0:T(8,128)} %bitcast.10, s32[]{:T(128)S(6)} %select_n.7, s32[]{:T(128)S(6)} %select_n.6), kind=kLoop, calls=%fused_computation | loop fusion | bytes 1048584 | tf_op jit(solution)/shard_map/dynamic_slice | solution.py:376
  1.7 0.5 collective-permute-start
  2.3 0.8 %copy-done.1 = f32[125,125]{1,0:T(8,128)S(1)} copy-done((f32[125,125]{1,0:T(8,128)S(1)}, f32[125,125]{1,0:T(8,128)}, u32[]{:S(2)}) %copy-start.1) | copy-done | bytes 62524
  3.1 0.9 %assemble.1 = (bf16[208,208]{1,0:T(8,128)(2,1)S(1)}, bf16[208,208]{1,0:T(8,128)(2,1)S(1)}, bf16[160,144]{1,0:T(8,128)(2,1)S(1)}, bf16[512,512]{1,0:T(8,128)(2,1)S(1)}) custom-call(f32[125,125]{1,0:T(8,128)S(1)} %copy-done.1), custom_call_target="tpu_custom_call" | custom-call | flops 805924 | bytes 805924 | tf_op jit(solution)/shard_map/assemble/pallas_call | solution.py:338
  4.1 0.8 %to_cells.1 = (f32[4,4,8,1024]{3,2,1,0:T(8,128)S(1)}, f32[4,8,1024]{2,1,0:T(8,128)S(1)}, f32[4,8,1024]{2,1,0:T(8,128)S(1)}) custom-call(f32[32,16,128]{2,1,0:T(8,128)S(1)} %get-tuple-element.49.refs_0_, f32[32,16,128]{2,1,0:T(8,128)S(1)} %collective-permute-done.refs_1_, bf16[512,512]{1,0:T(8,128)(2,1)S(1)} %get-tuple-element.25.refs_2_, ...), custom_call_target="tpu_custom_call" | custom-call | flops 2008064 | bytes 2008064 | tf_op jit(solution)/shard_map/to_cells/pallas_call | solution.py:338
  4.9 6.6 %collective-permute-start.2 = (f32[4,8,1024]{2,1,0:T(8,128)S(1)}, f32[4,8,1024]{2,1,0:T(8,128)S(1)}, u32[]{:S(2)}, u32[]{:S(2)}) collective-permute-start(f32[4,8,1024]{2,1,0:T(8,128)S(1)} %get-tuple-element.29), channel_id=1, source_target_pairs={{1,2},{3,4},{5,6},{7,8},{9,10},{11,12},{13,14},{15,0},{2,1},{4,3},... | collective-permute-start | bytes 393224 | tf_op jit(solution)/shard_map/ppermute | solution.py:325
  11.6 1.0 %collective-permute-done.1.refs_1_ = f32[1,16,128]{2,1,0:T(8,128)S(1)} collective-permute-done((f32[1,16,128]{2,1,0:T(8,128)S(1)}, f32[1,16,128]{2,1,0:T(8,128)S(1)}, u32[]{:S(2)}, u32[]{:S(2)}) %collective-permute-start.1) | collective-permute-done | bytes 8224 | tf_op jit(solution)/shard_map/ppermute | solution.py:332
  12.8 0.7 %inner.3.inner_ref = f32[4,4,8,1024]{3,2,1,0:T(8,128)S(1)} custom-call(f32[4,4,8,1024]{3,2,1,0:T(8,128)S(1)} %get-tuple-element.28.refs_0_.refs_4_, f32[4,4,8,128]{3,2,1,0:T(8,128)S(1)} %levels.1.refs_1_, bf16[208,208]{1,0:T(8,128)(2,1)S(1)} %get-tuple-element.26.refs_3_.refs_2_.high_ref, bf16[208,208]{1,0:T(8,128)(2,1)S(1)} %get-tuple-element.27.refs_4_.refs_3_.low_ref), custom_call_target="tpu_custom_call" | custom-call | flops 1287168 | bytes 1287168 | tf_op jit(solution)/shard_map/inner/pallas_call | solution.py:338
  13.5 2.2 %collective-permute-done.2.from_other_ref = f32[4,8,1024]{2,1,0:T(8,128)S(1)} collective-permute-done((f32[4,8,1024]{2,1,0:T(8,128)S(1)}, f32[4,8,1024]{2,1,0:T(8,128)S(1)}, u32[]{:S(2)}, u32[]{:S(2)}) %collective-permute-start.2) | collective-permute-done | bytes 131104 | tf_op jit(solution)/shard_map/ppermute | solution.py:325
  15.7 1.4 %collective-permute-done.3.from_pair_ref = f32[4,8,1024]{2,1,0:T(8,128)S(1)} collective-permute-done((f32[4,8,1024]{2,1,0:T(8,128)S(1)}, f32[4,8,1024]{2,1,0:T(8,128)S(1)}, u32[]{:S(2)}, u32[]{:S(2)}) %collective-permute-start.3) | collective-permute-done | bytes 131104 | tf_op jit(solution)/shard_map/ppermute | solution.py:326
  17.0 0.8 %finish.2 = (f32[4,4,8,1024]{3,2,1,0:T(8,128)S(1)}, f32[4,8,1024]{2,1,0:T(8,128)S(1)}, f32[4,8,1024]{2,1,0:T(8,128)S(1)}) custom-call(f32[4,4,8,1024]{3,2,1,0:T(8,128)S(1)} %inner.3.inner_ref, f32[4,8,1024]{2,1,0:T(8,128)S(1)} %collective-permute-done.2.from_other_ref, f32[4,8,1024]{2,1,0:T(8,128)S(1)} %collective-permute-done.3.from_pair_ref, ...), custom_call_target="tpu_custom_call" | custom-call | flops 1792000 | bytes 1792000 | tf_op jit(solution)/shard_map/finish/pallas_call | solution.py:338
  18.1 4.0 %collective-permute-start.4 = (f32[4,8,1024]{2,1,0:T(8,128)S(1)}, f32[4,8,1024]{2,1,0:T(8,128)S(1)}, u32[]{:S(2)}, u32[]{:S(2)}) collective-permute-start(f32[4,8,1024]{2,1,0:T(8,128)S(1)} %get-tuple-element.34), channel_id=1, source_target_pairs={{1,2},{3,4},{5,6},{7,8},{9,10},{11,12},{13,14},{15,0},{2,1},{4,3},... | collective-permute-start | bytes 393224 | tf_op jit(solution)/shard_map/ppermute | solution.py:325
  22.1 0.7 %inner.4.inner_ref = f32[4,4,8,1024]{3,2,1,0:T(8,128)S(1)} custom-call(f32[4,4,8,1024]{3,2,1,0:T(8,128)S(1)} %get-tuple-element.33.refs_0_.refs_4_, f32[4,4,8,128]{3,2,1,0:T(8,128)S(1)} %levels.1.refs_1_, bf16[208,208]{1,0:T(8,128)(2,1)S(1)} %get-tuple-element.26.refs_3_.refs_2_.high_ref, bf16[208,208]{1,0:T(8,128)(2,1)S(1)} %get-tuple-element.27.refs_4_.refs_3_.low_ref, ...), custom_call_target="tpu_custom_call" | custom-call | flops 1811456 | bytes 1811456 | tf_op jit(solution)/shard_map/inner/pallas_call | solution.py:338
  22.8 4.9 %collective-permute-done.4.from_other_ref = f32[4,8,1024]{2,1,0:T(8,128)S(1)} collective-permute-done((f32[4,8,1024]{2,1,0:T(8,128)S(1)}, f32[4,8,1024]{2,1,0:T(8,128)S(1)}, u32[]{:S(2)}, u32[]{:S(2)}) %collective-permute-start.4) | collective-permute-done | bytes 131104 | tf_op jit(solution)/shard_map/ppermute | solution.py:325
  27.7 0.8 %finish.3 = (f32[4,4,8,1024]{3,2,1,0:T(8,128)S(1)}, f32[4,8,1024]{2,1,0:T(8,128)S(1)}, f32[4,8,1024]{2,1,0:T(8,128)S(1)}) custom-call(f32[4,4,8,1024]{3,2,1,0:T(8,128)S(1)} %inner.4.inner_ref, f32[4,8,1024]{2,1,0:T(8,128)S(1)} %collective-permute-done.4.from_other_ref, f32[4,8,1024]{2,1,0:T(8,128)S(1)} %collective-permute-done.5.from_pair_ref, ...), custom_call_target="tpu_custom_call" | custom-call | flops 1792000 | bytes 1792000 | tf_op jit(solution)/shard_map/finish/pallas_call | solution.py:338
  28.5 4.0 %collective-permute-start.7 = (f32[4,8,1024]{2,1,0:T(8,128)S(1)}, f32[4,8,1024]{2,1,0:T(8,128)S(1)}, u32[]{:S(2)}, u32[]{:S(2)}) collective-permute-start(f32[4,8,1024]{2,1,0:T(8,128)S(1)} %get-tuple-element.40), channel_id=1, source_target_pairs={{1,2},{3,4},{5,6},{7,8},{9,10},{11,12},{13,14},{15,0},{2,1},{4,3},... | collective-permute-start | bytes 393224 | tf_op jit(solution)/shard_map/ppermute | solution.py:325
  32.6 1.2 %margin_rows.2.refs_5_ = bf16[256,2048]{1,0:T(8,128)(2,1)S(1)} custom-call(f32[4096,128]{1,0:T(8,128)S(1)} %widen.1.wide_ref), custom_call_target="tpu_custom_call" | custom-call | flops 3145728 | bytes 3145728 | tf_op jit(solution)/shard_map/margin_rows/pallas_call | solution.py:338
  33.8 0.9 %inner.5 = (f32[4,4,8,1024]{3,2,1,0:T(8,128)S(1)}, bf16[512,512]{1,0:T(8,128)(2,1)S(1)}) custom-call(f32[4,4,8,1024]{3,2,1,0:T(8,128)S(1)} %get-tuple-element.36.refs_0_, f32[4,4,8,128]{3,2,1,0:T(8,128)S(1)} %levels.1.refs_1_, bf16[208,208]{1,0:T(8,128)(2,1)S(1)} %get-tuple-element.26.refs_3_.refs_2_.high_ref, ...), custom_call_target="tpu_custom_call" | custom-call | flops 2335744 | bytes 2335744 | tf_op jit(solution)/shard_map/inner/pallas_call | solution.py:338
  34.7 1.2 %margin_rows.3.refs_6_ = bf16[256,2048]{1,0:T(8,128)(2,1)S(1)} custom-call(f32[4096,128]{1,0:T(8,128)S(1)} %collective-permute-done.6.wide_ref), custom_call_target="tpu_custom_call" | custom-call | flops 3145728 | bytes 3145728 | tf_op jit(solution)/shard_map/margin_rows/pallas_call | solution.py:338
  35.9 1.3 %collective-permute-done.7.refs_1_ = f32[4,8,1024]{2,1,0:T(8,128)S(1)} collective-permute-done((f32[4,8,1024]{2,1,0:T(8,128)S(1)}, f32[4,8,1024]{2,1,0:T(8,128)S(1)}, u32[]{:S(2)}, u32[]{:S(2)}) %collective-permute-start.7) | collective-permute-done | bytes 131104 | tf_op jit(solution)/shard_map/ppermute | solution.py:325
  37.5 2.0 %last.1 = (f32[32,16,128]{2,1,0:T(8,128)S(1)}, f32[32,16,128]{2,1,0:T(8,128)S(1)}, f32[64,128]{1,0:T(8,128)S(1)}) custom-call(f32[4,4,8,1024]{3,2,1,0:T(8,128)S(1)} %get-tuple-element.39.refs_0_, f32[4,8,1024]{2,1,0:T(8,128)S(1)} %collective-permute-done.7.refs_1_, f32[4,8,1024]{2,1,0:T(8,128)S(1)} %collective-permute-done.8.refs_2_, ...), custom_call_target="tpu_custom_call" | custom-call | flops 4011008 | bytes 4011008 | tf_op jit(solution)/shard_map/last/pallas_call | solution.py:338
  39.6 12.3 %all_to_all.5.tiles_ref = f32[16,4,128]{2,1,0:T(4,128)S(1)} all-to-all(f32[16,4,128]{2,1,0:T(4,128)S(1)} %bitcast.7), channel_id=1, replica_groups=mesh['px'=2,'py'=16] {'py'}, dimensions={0} | all-to-all | bytes 65536 | tf_op jit(solution)/shard_map/all_to_all | solution.py:446
  51.9 0.7 %tile_sum.1 = f32[16,32]{1,0:T(8,128)} custom-call(f32[16,4,128]{2,1,0:T(4,128)S(1)} %all_to_all.5.tiles_ref), custom_call_target="tpu_custom_call" | custom-call | flops 34816 | bytes 34816 | tf_op jit(solution)/shard_map/tile_sum/pallas_call | solution.py:338
  52.6 0.8 %join.1 = f32[64,16,128]{2,1,0:T(8,128)} custom-call(f32[32,16,128]{2,1,0:T(8,128)S(1)} %get-tuple-element.45.refs_0_, f32[32,16,128]{2,1,0:T(8,128)S(1)} %collective-permute-done.9.refs_1_), custom_call_target="tpu_custom_call" | custom-call | flops 1048576 | bytes 1048576 | tf_op jit(solution)/shard_map/join/pallas_call | solution.py:338
  (18 shorter events, 0.9 us)
Async XLA Ops:
  0.6 10.9 %copy-start.2 = (f32[4,4,128]{2,1,0:T(4,128)S(1)}, f32[4,4,128]{2,1,0:T(4,128)}, u32[]{:S(2)}) copy-start(f32[4,4,128]{2,1,0:T(4,128)} %param.5) | copy-start | bytes 24580
  1.7 16.1 %copy-start = (bf16[256,4,4,128]{3,2,1,0:T(4,128)(2,1)S(1)}, bf16[256,4,4,128]{3,2,1,0:T(4,128)(2,1)}, u32[]{:S(2)}) copy-start(bf16[256,4,4,128]{3,2,1,0:T(4,128)(2,1)} %param.7) | copy-start | bytes 3145732
  1.7 2.3 %collective-permute-start = (f32[32,16,128]{2,1,0:T(8,128)S(1)}, f32[32,16,128]{2,1,0:T(8,128)S(1)}, u32[]{:S(2)}, u32[]{:S(2)}) collective-permute-start(f32[32,16,128]{2,1,0:T(8,128)S(1)} %get-tuple-element.48), channel_id=1, source_target_pairs={{0,16},{16,0},{1,17},{17,1},{2,18},{18,2},{3,19},{19,3},{4,20},{20... | collective-permute-start | bytes 786440 | tf_op jit(solution)/shard_map/ppermute | solution.py:332
  2.3 0.8 %copy-start.1 = (f32[125,125]{1,0:T(8,128)S(1)}, f32[125,125]{1,0:T(8,128)}, u32[]{:S(2)}) copy-start(f32[125,125]{1,0:T(8,128)} %cell_ref.1) | copy-start | bytes 187504
  4.9 10.8 %collective-permute-start.2 = (f32[4,8,1024]{2,1,0:T(8,128)S(1)}, f32[4,8,1024]{2,1,0:T(8,128)S(1)}, u32[]{:S(2)}, u32[]{:S(2)}) collective-permute-start(f32[4,8,1024]{2,1,0:T(8,128)S(1)} %get-tuple-element.29), channel_id=1, source_target_pairs={{1,2},{3,4},{5,6},{7,8},{9,10},{11,12},{13,14},{15,0},{2,1},{4,3},... | collective-permute-start | bytes 393224 | tf_op jit(solution)/shard_map/ppermute | solution.py:325
  11.5 5.6 %collective-permute-start.3 = (f32[4,8,1024]{2,1,0:T(8,128)S(1)}, f32[4,8,1024]{2,1,0:T(8,128)S(1)}, u32[]{:S(2)}, u32[]{:S(2)}) collective-permute-start(f32[4,8,1024]{2,1,0:T(8,128)S(1)} %get-tuple-element.30), channel_id=1, source_target_pairs={{0,1},{2,3},{4,5},{6,7},{8,9},{10,11},{12,13},{14,15},{1,0},{3,2},... | collective-permute-start | bytes 393224 | tf_op jit(solution)/shard_map/ppermute | solution.py:326
  11.5 1.2 %collective-permute-start.1 = (f32[1,16,128]{2,1,0:T(8,128)S(1)}, f32[1,16,128]{2,1,0:T(8,128)S(1)}, u32[]{:S(2)}, u32[]{:S(2)}) collective-permute-start(f32[1,16,128]{2,1,0:T(8,128)S(1)} %bitcast.8), channel_id=1, source_target_pairs={{0,16},{16,0},{1,17},{17,1},{2,18},{18,2},{3,19},{19,3},{4,20},{20... | collective-permute-start | bytes 24584 | tf_op jit(solution)/shard_map/ppermute | solution.py:332
  18.0 16.7 %collective-permute-start.6 = (f32[4096,128]{1,0:T(8,128)S(1)}, f32[4096,128]{1,0:T(8,128)S(1)}, u32[]{:S(2)}, u32[]{:S(2)}) collective-permute-start(f32[4096,128]{1,0:T(8,128)S(1)} %widen.1.wide_ref), channel_id=1, source_target_pairs={{0,16},{16,0},{1,17},{17,1},{2,18},{18,2},{3,19},{19,3},{4,20},{20... | collective-permute-start | bytes 6291464 | tf_op jit(solution)/shard_map/ppermute | solution.py:332
  18.1 9.6 %collective-permute-start.4 = (f32[4,8,1024]{2,1,0:T(8,128)S(1)}, f32[4,8,1024]{2,1,0:T(8,128)S(1)}, u32[]{:S(2)}, u32[]{:S(2)}) collective-permute-start(f32[4,8,1024]{2,1,0:T(8,128)S(1)} %get-tuple-element.34), channel_id=1, source_target_pairs={{1,2},{3,4},{5,6},{7,8},{9,10},{11,12},{13,14},{15,0},{2,1},{4,3},... | collective-permute-start | bytes 393224 | tf_op jit(solution)/shard_map/ppermute | solution.py:325
  22.1 5.6 %collective-permute-start.5 = (f32[4,8,1024]{2,1,0:T(8,128)S(1)}, f32[4,8,1024]{2,1,0:T(8,128)S(1)}, u32[]{:S(2)}, u32[]{:S(2)}) collective-permute-start(f32[4,8,1024]{2,1,0:T(8,128)S(1)} %get-tuple-element.35), channel_id=1, source_target_pairs={{0,1},{2,3},{4,5},{6,7},{8,9},{10,11},{12,13},{14,15},{1,0},{3,2},... | collective-permute-start | bytes 393224 | tf_op jit(solution)/shard_map/ppermute | solution.py:326
  28.5 8.7 %collective-permute-start.7 = (f32[4,8,1024]{2,1,0:T(8,128)S(1)}, f32[4,8,1024]{2,1,0:T(8,128)S(1)}, u32[]{:S(2)}, u32[]{:S(2)}) collective-permute-start(f32[4,8,1024]{2,1,0:T(8,128)S(1)} %get-tuple-element.40), channel_id=1, source_target_pairs={{1,2},{3,4},{5,6},{7,8},{9,10},{11,12},{13,14},{15,0},{2,1},{4,3},... | collective-permute-start | bytes 393224 | tf_op jit(solution)/shard_map/ppermute | solution.py:325
  32.6 5.0 %collective-permute-start.8 = (f32[4,8,1024]{2,1,0:T(8,128)S(1)}, f32[4,8,1024]{2,1,0:T(8,128)S(1)}, u32[]{:S(2)}, u32[]{:S(2)}) collective-permute-start(f32[4,8,1024]{2,1,0:T(8,128)S(1)} %get-tuple-element.41), channel_id=1, source_target_pairs={{0,1},{2,3},{4,5},{6,7},{8,9},{10,11},{12,13},{14,15},{1,0},{3,2},... | collective-permute-start | bytes 393224 | tf_op jit(solution)/shard_map/ppermute | solution.py:326
  39.5 13.0 %collective-permute-start.9 = (f32[32,16,128]{2,1,0:T(8,128)S(1)}, f32[32,16,128]{2,1,0:T(8,128)S(1)}, u32[]{:S(2)}, u32[]{:S(2)}) collective-permute-start(f32[32,16,128]{2,1,0:T(8,128)S(1)} %get-tuple-element.46), channel_id=1, source_target_pairs={{0,16},{16,0},{1,17},{17,1},{2,18},{18,2},{3,19},{19,3},{4,20},{20... | collective-permute-start | bytes 786440 | tf_op jit(solution)/shard_map/ppermute | solution.py:332

commit v12 on v10

--- a/solution.py
+++ b/solution.py
@@ -225,8 +225,8 @@
 def finish(cells, step, inner_ref, other_ref, pair_ref, matrix_ref):
     nodes, width = inner_ref.shape[2:]
     even = even_place()
-    halo = [jnp.where(even, pair_ref[iz], other_ref[iz]) for iz in range(4)]
-    given = [jnp.where(even, other_ref[iz], pair_ref[iz]) for iz in range(4)]
+    halo = [jnp.where(even, pair_ref[1, iz], other_ref[1, iz]) for iz in range(4)]
+    given = [jnp.where(even, other_ref[0, iz], pair_ref[0, iz]) for iz in range(4)]
     halo = jnp.concatenate(halo + roll_rows(halo[:1], cells) + [jnp.zeros((nodes, width), f32)], 0)
     halo_high, halo_low = two_parts(halo)
     product = dot(matrix_ref[...], jnp.concatenate([halo_high, halo_low, halo_high], 0))
@@ -318,11 +318,11 @@
 
 def swapped(edges):
     count = lax.axis_size("py")
-    pairs = [(place, place + 1) for place in range(0, count, 2)]
-    others = [(place + 1, (place + 2) % count) for place in range(0, count, 2)]
     pair, other = edges
-    other = lax.ppermute(other, "py", others + [(b, a) for a, b in others])
-    pair = lax.ppermute(pair, "py", pairs + [(b, a) for a, b in pairs])
+    others = [[place + 1, (place + 2) % count] for place in range(0, count, 2)]
+    pairs = [[place, place + 1] for place in range(0, count, 2)]
+    other = lax.all_gather(other, "py", axis_index_groups=others)
+    pair = lax.all_gather(pair, "py", axis_index_groups=pairs)
     return [other, pair]
 
 

time: 51.3 us -> 74.4 us (1.45)
  blocking collectives: 11.2 us -> 60.3 us
  starting transfers between devices: 15.3 us -> 0.67 us
  waiting for transfers between devices: 13.2 us -> 1.67 us
    all_gather x0 -> x6, blocking collectives: none -> 47.2 us  [the longest x3 30.2 us: swapped(): other = lax.all_gather(other, 'py', axis_index_groups=others)]
    ppermute x6 -> x0, starting transfers between devices: 14.7 us -> none  [the longest x3 14.7 us: swapped(): other = lax.ppermute(other, 'py', others + [(b, a) for a, b in others])]
    ppermute x6 -> x0, waiting for transfers between devices: 10.3 us -> none  [the longest x3 8.58 us: swapped(): other = lax.ppermute(other, 'py', others + [(b, a) for a, b in others])]
    all_to_all x1, blocking collectives: 11.2 us -> 13 us  [local(): tiles = lax.all_to_all(tiles, ('px', 'py'), 0, 0, tiled=True)]
    ppermute x3, waiting for transfers between devices: 2.9 us -> 1.67 us  [shifted(): lax.ppermute(value, axis, [(source, (source + steps) % count) for source...]
  transfers between devices with their start and end apart: 9 -> 3, of which waited for: 9 -> 2; matrix products, arithmetic and copies ran while one was open for 0% -> 0% of each run, Pallas kernels for 9% -> 2%
where the time goes in v12:
time: 74.4 us; the launch traced here: 74.2 us
  blocking collectives  60.3 us (81%)
  Pallas kernels  9.72 us (13%)
  waiting for transfers between devices  1.67 us (2%)
  local copies, waits for them, and re-layouts  1.11 us (1%)
    all_gather x3, blocking collectives, swapped(): other = lax.all_gather(other, 'py', axis_index_groups=others)  30.2 us
    all_gather x3, blocking collectives, swapped(): pair = lax.all_gather(pair, 'py', axis_index_groups=pairs)  17.1 us
    all_to_all x1, blocking collectives, local(): tiles = lax.all_to_all(tiles, ('px', 'py'), 0, 0, tiled=True)  13 us
    pallas_call x12, Pallas kernels, kernel_call(): pl.pallas_call(body, out_shape=outs, in_specs=in_specs or [whole] * len(o...  9.72 us
    ppermute x3, waiting for transfers between devices, shifted(): lax.ppermute(value, axis, [(source, (source + steps) % count) for source...  1.67 us
  transfers between devices with their start and end apart: 3, of which 2 were waited for; matrix products, arithmetic and copies ran while one was open for 0% of the time, Pallas kernels for 2%

profile of v12, /device:TPU:0, one launch (start us, length us, event | category | flops | bytes accessed | tf_op | source)
XLA Modules:
  0.0 74.2 jit_solution(9269589589932775320)
XLA Ops:
  0.7 1.1 %constant_dynamic-slice_fusion = (f32[32,16,128]{2,1,0:T(8,128)S(1)}, f32[32,16,128]{2,1,0:T(8,128)S(1)}) fusion(f32[64,16,128]{2,1,0:T(8,128)} %bitcast.22, s32[]{:T(128)S(6)} %select_n.7, s32[]{:T(128)S(6)} %select_n.6), kind=kLoop, calls=%fused_computation | loop fusion | bytes 1048584 | tf_op jit(solution)/shard_map/dynamic_slice | solution.py:373
  1.8 0.5 collective-permute-start
  2.3 0.1 collective-permute-start.1
  2.4 0.9 %assemble.1 = (bf16[208,208]{1,0:T(8,128)(2,1)S(1)}, bf16[208,208]{1,0:T(8,128)(2,1)S(1)}, bf16[160,144]{1,0:T(8,128)(2,1)S(1)}, bf16[512,512]{1,0:T(8,128)(2,1)S(1)}) custom-call(f32[125,125]{1,0:T(8,128)S(1)} %copy-done.1), custom_call_target="tpu_custom_call" | custom-call | tf_op jit(solution)/shard_map/assemble/pallas_call | solution.py:336
  3.3 0.1 collective-permute-done.1.refs_1_
  3.5 0.2 levels.1.refs_1_
  3.7 0.8 %to_cells.1 = (f32[4,4,8,1024]{3,2,1,0:T(8,128)S(1)}, f32[4,8,1024]{2,1,0:T(8,128)S(1)}, f32[4,8,1024]{2,1,0:T(8,128)S(1)}) custom-call(f32[32,16,128]{2,1,0:T(8,128)S(1)} %get-tuple-element.49.refs_0_, f32[32,16,128]{2,1,0:T(8,128)S(1)} %collective-permute-done.refs_1_, bf16[512,512]{1,0:T(8,128)(2,1)S(1)} %get-tuple-element.25.refs_2_, ...), custom_call_target="tpu_custom_call" | custom-call | tf_op jit(solution)/shard_map/to_cells/pallas_call | solution.py:336
  4.5 11.3 %all-gather = f32[8,8,1024]{2,1,0:T(8,128)S(1)} all-gather(f32[4,8,1024]{2,1,0:T(8,128)S(1)} %get-tuple-element.29), channel_id=2, replica_groups={{1,2},{3,4},{5,6},{7,8},{9,10},{11,12},{13,14},{15,0},{17,18},{19,20},{..., dimensions={0}, use_global_device_ids=true | all-gather | bytes 393216 | tf_op jit(solution)/shard_map/all_gather | solution.py:324
  15.8 5.7 %all-gather.1 = f32[8,8,1024]{2,1,0:T(8,128)S(1)} all-gather(f32[4,8,1024]{2,1,0:T(8,128)S(1)} %get-tuple-element.30), channel_id=3, replica_groups={{0,1},{2,3},{4,5},{6,7},{8,9},{10,11},{12,13},{14,15},{16,17},{18,19},{..., dimensions={0}, use_global_device_ids=true | all-gather | bytes 393216 | tf_op jit(solution)/shard_map/all_gather | solution.py:325
  21.5 0.6 inner.3.inner_ref
  22.1 0.8 %finish.2 = (f32[4,4,8,1024]{3,2,1,0:T(8,128)S(1)}, f32[4,8,1024]{2,1,0:T(8,128)S(1)}, f32[4,8,1024]{2,1,0:T(8,128)S(1)}) custom-call(f32[4,4,8,1024]{3,2,1,0:T(8,128)S(1)} %inner.3.inner_ref, f32[2,4,8,1024]{3,2,1,0:T(8,128)S(1)} %bitcast.15, f32[2,4,8,1024]{3,2,1,0:T(8,128)S(1)} %bitcast.16, bf16[160,144]{1,0:T(8,128)(2,1)S(1)} %get-tuple-element.31.matrix_ref.refs_3_, ...), custom_call_target="tpu_custom_call" | custom-call | tf_op jit(solution)/shard_map/finish/pallas_call | solution.py:336
  22.9 0.7 inner.4.inner_ref
  23.6 9.3 %all-gather.2 = f32[8,8,1024]{2,1,0:T(8,128)S(1)} all-gather(f32[4,8,1024]{2,1,0:T(8,128)S(1)} %get-tuple-element.34), channel_id=4, replica_groups={{1,2},{3,4},{5,6},{7,8},{9,10},{11,12},{13,14},{15,0},{17,18},{19,20},{..., dimensions={0}, use_global_device_ids=true | all-gather | bytes 393216 | tf_op jit(solution)/shard_map/all_gather | solution.py:324
  32.9 5.7 %all-gather.3 = f32[8,8,1024]{2,1,0:T(8,128)S(1)} all-gather(f32[4,8,1024]{2,1,0:T(8,128)S(1)} %get-tuple-element.35), channel_id=5, replica_groups={{0,1},{2,3},{4,5},{6,7},{8,9},{10,11},{12,13},{14,15},{16,17},{18,19},{..., dimensions={0}, use_global_device_ids=true | all-gather | bytes 393216 | tf_op jit(solution)/shard_map/all_gather | solution.py:325
  38.7 0.8 %finish.3 = (f32[4,4,8,1024]{3,2,1,0:T(8,128)S(1)}, f32[4,8,1024]{2,1,0:T(8,128)S(1)}, f32[4,8,1024]{2,1,0:T(8,128)S(1)}) custom-call(f32[4,4,8,1024]{3,2,1,0:T(8,128)S(1)} %inner.4.inner_ref, f32[2,4,8,1024]{3,2,1,0:T(8,128)S(1)} %bitcast.17, f32[2,4,8,1024]{3,2,1,0:T(8,128)S(1)} %bitcast.18, bf16[160,144]{1,0:T(8,128)(2,1)S(1)} %get-tuple-element.31.matrix_ref.refs_3_, ...), custom_call_target="tpu_custom_call" | custom-call | tf_op jit(solution)/shard_map/finish/pallas_call | solution.py:336
  39.5 0.9 %inner.5 = (f32[4,4,8,1024]{3,2,1,0:T(8,128)S(1)}, bf16[512,512]{1,0:T(8,128)(2,1)S(1)}) custom-call(f32[4,4,8,1024]{3,2,1,0:T(8,128)S(1)} %get-tuple-element.36.refs_0_, f32[4,4,8,128]{3,2,1,0:T(8,128)S(1)} %levels.1.refs_1_, bf16[208,208]{1,0:T(8,128)(2,1)S(1)} %get-tuple-element.26.refs_3_.refs_2_.high_ref, ...), custom_call_target="tpu_custom_call" | custom-call | tf_op jit(solution)/shard_map/inner/pallas_call | solution.py:336
  40.4 9.5 %all-gather.4 = f32[8,8,1024]{2,1,0:T(8,128)S(1)} all-gather(f32[4,8,1024]{2,1,0:T(8,128)S(1)} %get-tuple-element.40), channel_id=6, replica_groups={{1,2},{3,4},{5,6},{7,8},{9,10},{11,12},{13,14},{15,0},{17,18},{19,20},{..., dimensions={0}, use_global_device_ids=true | all-gather | bytes 393216 | tf_op jit(solution)/shard_map/all_gather | solution.py:324
  49.9 5.6 %all-gather.5 = f32[8,8,1024]{2,1,0:T(8,128)S(1)} all-gather(f32[4,8,1024]{2,1,0:T(8,128)S(1)} %get-tuple-element.41), channel_id=7, replica_groups={{0,1},{2,3},{4,5},{6,7},{8,9},{10,11},{12,13},{14,15},{16,17},{18,19},{..., dimensions={0}, use_global_device_ids=true | all-gather | bytes 393216 | tf_op jit(solution)/shard_map/all_gather | solution.py:325
  55.5 1.3 %margin_rows.1.refs_2_ = bf16[256,2048]{1,0:T(8,128)(2,1)S(1)} custom-call(bf16[4096,128]{1,0:T(8,128)(2,1)S(1)} %bitcast.14), custom_call_target="tpu_custom_call" | custom-call | tf_op jit(solution)/shard_map/margin_rows/pallas_call | solution.py:336
  56.9 0.8 %from_cells.1 = (f32[32,16,128]{2,1,0:T(8,128)S(1)}, f32[32,16,128]{2,1,0:T(8,128)S(1)}) custom-call(f32[4,4,8,1024]{3,2,1,0:T(8,128)S(1)} %get-tuple-element.39.refs_0_, f32[2,4,8,1024]{3,2,1,0:T(8,128)S(1)} %bitcast.12, f32[2,4,8,1024]{3,2,1,0:T(8,128)S(1)} %bitcast.13, bf16[160,144]{1,0:T(8,128)(2,1)S(1)} %get-tuple-element.31.matrix_ref.refs_3_, ...), custom_call_target="tpu_custom_call" | custom-call | tf_op jit(solution)/shard_map/from_cells/pallas_call | solution.py:336
  57.7 1.5 %collective-permute-done.2.refs_1_ = f32[32,16,128]{2,1,0:T(8,128)S(1)} collective-permute-done((f32[32,16,128]{2,1,0:T(8,128)S(1)}, f32[32,16,128]{2,1,0:T(8,128)S(1)}, u32[]{:S(2)}, u32[]{:S(2)}) %collective-permute-start.2) | collective-permute-done | bytes 262176 | tf_op jit(solution)/shard_map/ppermute | solution.py:331
  59.2 1.2 %margin.1 = (f32[2,64,128]{2,1,0:T(8,128)S(1)}, f32[64,16,128]{2,1,0:T(8,128)}) custom-call(f32[32,16,128]{2,1,0:T(8,128)S(1)} %get-tuple-element.43.refs_0_, f32[32,16,128]{2,1,0:T(8,128)S(1)} %collective-permute-done.2.refs_1_, bf16[256,2048]{1,0:T(8,128)(2,1)S(1)} %margin_rows.1.refs_2_), custom_call_target="tpu_custom_call" | custom-call | tf_op jit(solution)/shard_map/margin/pallas_call | solution.py:336
  60.4 13.0 %all_to_all.5.tiles_ref = f32[32,4,128]{2,1,0:T(4,128)S(1)} all-to-all(f32[32,4,128]{2,1,0:T(4,128)S(1)} %bitcast.19), channel_id=1, replica_groups=mesh['px'=2,'py'=16] {'px','py'}, dimensions={0} | all-to-all | bytes 131072 | tf_op jit(solution)/shard_map/all_to_all | solution.py:447
  73.5 0.7 tile_sum.1
  (8 shorter events, 0.1 us)
Async XLA Ops:
  0.6 1.6 %copy-start.2 = (f32[4,4,128]{2,1,0:T(4,128)S(1)}, f32[4,4,128]{2,1,0:T(4,128)}, u32[]{:S(2)}) copy-start(f32[4,4,128]{2,1,0:T(4,128)} %param.5) | copy-start | bytes 24580
  0.7 1.7 %copy-start.1 = (f32[125,125]{1,0:T(8,128)S(1)}, f32[125,125]{1,0:T(8,128)}, u32[]{:S(2)}) copy-start(f32[125,125]{1,0:T(8,128)} %cell_ref.1) | copy-start | bytes 187504
  1.8 1.9 %collective-permute-start = (f32[32,16,128]{2,1,0:T(8,128)S(1)}, f32[32,16,128]{2,1,0:T(8,128)S(1)}, u32[]{:S(2)}, u32[]{:S(2)}) collective-permute-start(f32[32,16,128]{2,1,0:T(8,128)S(1)} %get-tuple-element.48), channel_id=1, source_target_pairs={{0,16},{16,0},{1,17},{17,1},{2,18},{18,2},{3,19},{19,3},{4,20},{20... | collective-permute-start | bytes 786440 | tf_op jit(solution)/shard_map/ppermute | solution.py:331
  2.3 1.2 %collective-permute-start.1 = (f32[1,16,128]{2,1,0:T(8,128)S(1)}, f32[1,16,128]{2,1,0:T(8,128)S(1)}, u32[]{:S(2)}, u32[]{:S(2)}) collective-permute-start(f32[1,16,128]{2,1,0:T(8,128)S(1)} %bitcast.20), channel_id=1, source_target_pairs={{0,16},{16,0},{1,17},{17,1},{2,18},{18,2},{3,19},{19,3},{4,20},{20... | collective-permute-start | bytes 24584 | tf_op jit(solution)/shard_map/ppermute | solution.py:331
  39.5 16.1 %copy-start = (bf16[256,4,4,128]{3,2,1,0:T(4,128)(2,1)S(1)}, bf16[256,4,4,128]{3,2,1,0:T(4,128)(2,1)}, u32[]{:S(2)}) copy-start(bf16[256,4,4,128]{3,2,1,0:T(4,128)(2,1)} %param.7) | copy-start | bytes 3145732
  57.6 1.6 %collective-permute-start.2 = (f32[32,16,128]{2,1,0:T(8,128)S(1)}, f32[32,16,128]{2,1,0:T(8,128)S(1)}, u32[]{:S(2)}, u32[]{:S(2)}) collective-permute-start(f32[32,16,128]{2,1,0:T(8,128)S(1)} %get-tuple-element.44), channel_id=1, source_target_pairs={{0,16},{16,0},{1,17},{17,1},{2,18},{18,2},{3,19},{19,3},{4,20},{20... | collective-permute-start | bytes 786440 | tf_op jit(solution)/shard_map/ppermute | solution.py:331

commit v13 on v10

v13 whole, which is shorter than its diff:
```python
import functools

import jax
import jax.numpy as jnp
from jax import lax
from jax.experimental import pallas as pl
from jax.experimental.pallas import tpu as pltpu
from jax.sharding import PartitionSpec as P

centre = 13.0
half_width = 9.0
lanes = 128
bf16 = jnp.bfloat16
f32 = jnp.float32
whole = pl.BlockSpec(memory_space=pltpu.VMEM)
anywhere = pl.BlockSpec(memory_space=pl.ANY)
params = pltpu.CompilerParams(vmem_limit_bytes=48 * 2**20)

PADDED = 26


def two_parts(value):
    high = value.astype(bf16)
    return high, (value - high.astype(f32)).astype(bf16)


def dot(a, b):
    return jnp.dot(a, b, preferred_element_type=f32)


def chosen(rows, cols, target):
    row = lax.broadcasted_iota(jnp.int32, (rows, cols), 0)
    col = lax.broadcasted_iota(jnp.int32, (rows, cols), 1)
    return jnp.where(col == target(row), 1.0, 0.0).astype(bf16)


def select_target(cell, nodes, row):
    inside = row < 20 * nodes
    beyond = row - 20 * nodes
    jz = jnp.where(inside, lax.div(row, 4 * nodes), lax.div(beyond, nodes))
    jy = jnp.where(inside, lax.rem(row, 4), 4)
    x = jnp.where(inside, lax.div(lax.rem(row, 4 * nodes), 4), lax.rem(beyond, nodes))
    jx = lax.rem(x + (nodes - 4 * cell), nodes)
    return jnp.where((jx <= 4) & (jz <= 4), (jx * 5 + jy) * 5 + jz, -1)


def pick_target(nodes, row):
    return lax.div(row, nodes) * 4 * nodes + lax.rem(row, nodes) * 4


def place_target(nodes, row):
    first_layer = (lax.rem(row, 4) == 0) & (row < 16 * nodes)
    return jnp.where(first_layer, lax.div(row, 4 * nodes) * nodes + lax.div(lax.rem(row, 4 * nodes), 4), -1)


def cell_order_target(cells, row):
    node, cell = lax.rem(row, 4), lax.rem(lax.div(row, 4), cells)
    return node * lanes + lax.div(row, 4 * cells) * cells + cell


def raw_order_target(cells, row):
    node, state, cell = lax.div(row, lanes), lax.rem(lax.div(row, cells), lanes // cells), lax.rem(row, cells)
    return (state * cells + cell) * 4 + node


def matrix_kernel(cells, nodes, cell_ref, high_ref, low_ref, edge_ref, halo_ref, place_ref, order_ref):
    rest = cell_ref[...]
    size, count = high_ref.shape[0], cell_ref.shape[0]
    tables = [chosen(size, count, functools.partial(select_target, cell, nodes)) for cell in range(nodes // 4)]
    total = jnp.zeros(high_ref.shape, f32)
    for _ in range(3):
        part = rest.astype(bf16)
        rest = rest - part.astype(f32)
        for table in tables:
            left = dot(table, part).astype(bf16)
            total = total + lax.dot_general(left, table, (((1,), (1,)), ((), ())), preferred_element_type=f32)
    high, low = two_parts(total)
    high_ref[...], low_ref[...] = high, low
    inside, layer = 20 * nodes, 4 * nodes
    pick = chosen(layer, inside, functools.partial(pick_target, nodes))
    edge_ref[...] = jnp.concatenate([high[inside:, :inside], pick], 0)
    place = chosen(inside, layer, functools.partial(place_target, nodes))
    place_ref[...] = place
    from_halo = total[:inside, inside:]
    high = from_halo.astype(bf16).astype(f32)
    place = place.astype(f32)
    halo_ref[...] = jnp.concatenate([high, high, from_halo - high, place, place], 1).astype(bf16)
    order_ref[...] = chosen(*order_ref.shape, functools.partial(cell_order_target, cells))


def margin_rows_kernel(layer, parts_y, block_ref, out_ref, wide_ref):
    wide_ref[...] = block_ref[...].astype(f32)
    thickness = block_ref.shape[1]
    tile_cols = out_ref.shape[0] // parts_y
    for n in range(layer):
        for col in range(tile_cols):
            lines = wide_ref[pl.ds(col * layer + n, parts_y, stride=tile_cols * layer), :]
            out_ref[pl.ds(col * parts_y, parts_y), pl.ds(n * thickness, thickness)] = lines.astype(bf16)


def roll_cells(value, cells, forward):
    out = []
    place = lax.broadcasted_iota(jnp.int32, (value.shape[0], lanes), 1) % cells
    for start in range(0, value.shape[1], lanes):
        part = value[:, start : start + lanes]
        if forward:
            moved = jnp.where(place == cells - 1, pltpu.roll(part, cells - 1, 1), pltpu.roll(part, lanes - 1, 1))
        else:
            moved = jnp.where(place == 0, pltpu.roll(part, lanes - cells + 1, 1), pltpu.roll(part, 1, 1))
        out.append(moved)
    return out[0] if len(out) == 1 else jnp.concatenate(out, 1)


def three_products(high, low, value):
    value_high, value_low = two_parts(value)
    return dot(high, value_high) + (dot(low, value_high) + dot(high, value_low))


def fold_last(rows, nodes, cells):
    parts = [rows[iz * nodes : (iz + 1) * nodes] for iz in range(5)]
    parts[0] = parts[0] + roll_cells(parts[4], cells, False)
    return parts[:4]


def even_place():
    return lax.rem(lax.axis_index("py"), 2) == 0


def send_edges(edge_ref, low_ref, value, pair_ref, other_ref, cells):
    nodes = pair_ref.shape[1]
    even = even_place()
    inside, beyond = 20 * nodes, (PADDED - 20) * nodes
    high, low = two_parts(jnp.concatenate(value + [roll_cells(value[0], cells, True)], 0))
    product = dot(edge_ref[...], high) + dot(edge_ref[...], low)
    up = fold_last(product[:beyond] + dot(low_ref[inside:, :inside], high), nodes, cells)
    for iz in range(4):
        down = product[beyond + iz * nodes : beyond + (iz + 1) * nodes]
        pair_ref[iz] = jnp.where(even, up[iz], down)
        other_ref[iz] = jnp.where(even, down, up[iz])


def start_all(copies):
    for copy in copies:
        copy.start()


def wait_all(copies):
    for copy in copies:
        copy.wait()


def to_cells_kernel(cells, parts_x, *refs):
    part_refs = refs[:parts_x]
    order_ref, edge_ref, low_ref, w_ref, pair_ref, other_ref = refs[parts_x:]
    size = w_ref.shape[1]
    group = lanes // cells
    sources = []
    for start in range(0, part_refs[0].shape[0], group):
        lines = [jnp.concatenate([ref[start + s] for ref in part_refs], 0) for s in range(group)]
        sources += list(two_parts(jnp.concatenate(lines, 1)))
    ordered = dot(jnp.concatenate(sources, 0), order_ref[...])
    values = [ordered[start : start + size] + ordered[start + size : start + 2 * size] for start in range(0, ordered.shape[0], 2 * size)]
    value = [jnp.concatenate([part[:, iz * lanes : (iz + 1) * lanes] for part in values], 1) for iz in range(4)]
    for iz in range(4):
        w_ref[iz] = value[iz]
    send_edges(edge_ref, low_ref, value, pair_ref, other_ref, cells)


def levels_kernel(parts_x, *refs):
    part_refs, levels_ref = refs[:parts_x], refs[parts_x]
    thickness = part_refs[0].shape[1]
    cells = thickness // 4
    row = lax.broadcasted_iota(jnp.int32, (thickness, 4 * lanes), 0)
    col = lax.broadcasted_iota(jnp.int32, (thickness, 4 * lanes), 1)
    table = jnp.where(row == lax.rem(col, cells) * 4 + lax.div(col, lanes), 1.0, 0.0).astype(bf16)
    high, low = two_parts(jnp.concatenate([ref[...] for ref in part_refs], 0))
    spread = dot(high, table) + dot(low, table)
    for iz in range(4):
        levels_ref[iz] = spread[:, iz * lanes : (iz + 1) * lanes] - centre


def scale_of(step):
    return 1.0 / half_width if step == 0 else 2.0 / half_width


def inner_kernel(cells, step, *refs):
    w_ref, levels_ref, high_ref, low_ref, edge_ref, place_ref = refs[:6]
    before_ref = refs[6] if step > 0 else None
    out_ref = refs[6 if step == 0 else 7]
    if step == 2:
        back_ref = refs[8]
        back_ref[...] = chosen(*back_ref.shape, functools.partial(raw_order_target, cells))
    size, width = w_ref.shape[1:]
    nodes = size // 4
    groups = width // lanes
    inside = 20 * nodes
    value = [w_ref[iz] for iz in range(4)]
    high, low = two_parts(jnp.concatenate(value + [roll_cells(value[0], cells, True)], 0))
    product = dot(high_ref[:inside, :inside], high)
    product = product + (dot(low_ref[:inside, :inside], high) + dot(high_ref[:inside, :inside], low))

    pick = edge_ref[(PADDED - 20) * nodes :, :]
    edge = dot(pick, high) + dot(pick, low)
    edge = jnp.concatenate([edge, roll_cells(edge[:nodes], cells, True), jnp.zeros((nodes, width), f32)], 0)
    edge = fold_last(three_products(high_ref[inside:, inside:], low_ref[inside:, inside:], edge), nodes, cells)
    edge_high, edge_low = two_parts(jnp.concatenate(edge, 0))
    product = product + (dot(place_ref[...], edge_high) + dot(place_ref[...], edge_low))
    for iz in range(4):
        total = product[iz * size : (iz + 1) * size]
        if iz == 0:
            total = total + roll_cells(product[4 * size :], cells, False)
        level = levels_ref[iz]
        level = level if groups == 1 else jnp.concatenate([level] * groups, 1)
        total = (total + level * value[iz]) * scale_of(step)
        out_ref[iz] = total if step == 0 else total - before_ref[iz]


def finish(cells, step, inner_ref, other_ref, pair_ref, matrix_ref):
    size, width = inner_ref.shape[1:]
    nodes = size // 4
    even = even_place()
    halo = [jnp.where(even, pair_ref[iz], other_ref[iz]) for iz in range(4)]
    given = [jnp.where(even, other_ref[iz], pair_ref[iz]) for iz in range(4)]
    halo = jnp.concatenate(halo + [roll_cells(halo[0], cells, True), jnp.zeros((nodes, width), f32)], 0)
    halo_high, halo_low = two_parts(halo)
    given_high, given_low = two_parts(jnp.concatenate(given, 0))
    beside = jnp.concatenate([halo_high, halo_low, halo_high, given_high, given_low], 0)
    product = dot(matrix_ref[...], beside)
    result = []
    for iz in range(4):
        total = product[iz * size : (iz + 1) * size]
        if iz == 0:
            total = total + roll_cells(product[4 * size :], cells, False)
        result.append(inner_ref[iz] + total * scale_of(step))
    return result


def finish_kernel(
    cells, step, inner_ref, from_other_ref, from_pair_ref, matrix_ref, edge_ref, low_ref, next_ref, pair_ref, other_ref
):
    value = finish(cells, step, inner_ref, from_other_ref, from_pair_ref, matrix_ref)
    for iz in range(4):
        next_ref[iz] = value[iz]
    send_edges(edge_ref, low_ref, value, pair_ref, other_ref, cells)


def from_cells_kernel(cells, *refs):
    inner_ref, other_ref, pair_ref, matrix_ref, order_ref = refs[:5]
    out_refs = refs[5:]
    value = finish(cells, 2, inner_ref, other_ref, pair_ref, matrix_ref)
    states, layer, thickness = out_refs[0].shape
    group = lanes // cells
    size = value[0].shape[0]
    sources = []
    for h in range(states // group):
        parts = [value[iz][:, h * lanes : (h + 1) * lanes] for iz in range(4)]
        sources += list(two_parts(jnp.concatenate(parts, 1)))
    ordered = dot(jnp.concatenate(sources, 0), order_ref[...])
    for h in range(states // group):
        part = ordered[2 * h * size : (2 * h + 1) * size] + ordered[(2 * h + 1) * size : (2 * h + 2) * size]
        for s in range(group):
            for step, out_ref in enumerate(out_refs):
                rows = slice(step * layer, (step + 1) * layer)
                out_ref[h * group + s] = part[rows, s * thickness : (s + 1) * thickness]


def margin_kernel(parts_x, parts_y, *refs):
    part_refs, block_ref = refs[:parts_x], refs[parts_x]
    tiles_ref, filtered_ref, sems = refs[parts_x + 1 :]
    me = lax.axis_index("px")
    count, layer, thickness = part_refs[0].shape
    owners = [lax.rem(me + (parts_x - step), parts_x) for step in range(parts_x)]
    copies = []
    for step, part_ref in enumerate(part_refs):
        target = filtered_ref.at[pl.ds(owners[step] * count, count)]
        copies.append(pltpu.make_async_copy(part_ref, target, sems.at[step]))
    start_all(copies)
    turned = [jnp.swapaxes(ref[...], 0, 1) for ref in part_refs]
    lines = [jnp.concatenate([part[n] for part in turned], 0).astype(bf16) for n in range(layer)]
    product = lax.dot_general(
        block_ref[...], jnp.concatenate(lines, 1), (((1,), (1,)), ((), ())), preferred_element_type=f32
    )
    groups = tiles_ref.shape[2] // count
    group_cols = tiles_ref.shape[1] // parts_y
    for col in range(group_cols):
        starts = [(group * group_cols + col) * parts_y for group in range(groups)]
        for step in range(parts_x):
            columns = slice(step * count, (step + 1) * count)
            tiles = jnp.concatenate([product[start : start + parts_y, columns] for start in starts], 1)
            tiles_ref[owners[step], pl.ds(col, parts_y, stride=group_cols), :] = tiles
    wait_all(copies)


def sum_kernel(tiles_ref, out_ref):
    total = jnp.sum(tiles_ref[...], axis=0)
    tile_rows = out_ref.shape[1]
    groups = total.shape[1] // tile_rows
    out_ref[...] = jnp.concatenate([total[:, g * tile_rows : (g + 1) * tile_rows] for g in range(groups)], 0)


def swapped(edges):
    count = lax.axis_size("py")
    pairs = [(place, place + 1) for place in range(0, count, 2)]
    others = [(place + 1, (place + 2) % count) for place in range(0, count, 2)]
    pair, other = edges
    other = lax.ppermute(other, "py", others + [(b, a) for a, b in others])
    pair = lax.ppermute(pair, "py", pairs + [(b, a) for a, b in pairs])
    return [other, pair]


def shifted(value, axis, steps):
    count = lax.axis_size(axis)
    return lax.ppermute(value, axis, [(source, (source + steps) % count) for source in range(count)])


def kernel_call(body, outs, operands, name, scratch=(), in_specs=None, out_specs=None):
    many = isinstance(outs, list)
    return pl.pallas_call(
        body,
        out_shape=outs,
        in_specs=in_specs or [whole] * len(operands),
        out_specs=out_specs or ([whole] * len(outs) if many else whole),
        scratch_shapes=list(scratch),
        compiler_params=params,
        name=name,
    )(*operands)


def local(span, potential, cell_matrix, block):
    states, first, second, thickness = span.shape
    block_count = block.shape[0]
    parts_x, parts_y = lax.axis_size("px"), lax.axis_size("py")
    mine = states // parts_x
    layer = first * second
    nodes = parts_x * first
    cells = thickness // 4
    rows = PADDED * nodes
    others = range(1, parts_x)

    group = lanes // cells * thickness
    matrix = jax.ShapeDtypeStruct((rows, rows), bf16)
    table = jax.ShapeDtypeStruct((group, group), bf16)
    inside = 20 * nodes
    from_halo = jax.ShapeDtypeStruct((inside, 3 * (rows - inside) + 2 * 4 * nodes), bf16)
    edge_shape = jax.ShapeDtypeStruct((rows - inside + 4 * nodes, inside), bf16)
    place_shape = jax.ShapeDtypeStruct((inside, 4 * nodes), bf16)

    chunks = 1
    count = mine // chunks
    width = count * cells
    field = jax.ShapeDtypeStruct((4, second * nodes, width), f32)
    message = jax.ShapeDtypeStruct((4, nodes, width), f32)
    part = jax.ShapeDtypeStruct((count, layer, thickness), f32)
    me = lax.axis_index("px")
    span_rows = span.reshape(states, layer, thickness)

    def part_for(step):
        return lax.dynamic_slice_in_dim(span_rows, lax.rem(me + step, parts_x) * mine, mine, 0)

    parts = [part_for(0)] + [shifted(part_for(step), "px", step) for step in reversed(others)]
    high, low, edge_matrix, halo_matrix, place, order = kernel_call(
        functools.partial(matrix_kernel, cells, nodes),
        [matrix, matrix, edge_shape, from_halo, place_shape, table],
        [cell_matrix],
        "assemble",
    )
    field_now, *edges = kernel_call(
        functools.partial(to_cells_kernel, cells, parts_x),
        [field, message, message],
        parts + [order, edge_matrix, low],
        "to_cells",
    )
    edges = swapped(edges)
    level_rows = potential.reshape(layer, thickness)
    levels = kernel_call(
        functools.partial(levels_kernel, parts_x),
        jax.ShapeDtypeStruct((4, second * nodes, lanes), f32),
        [level_rows] + [shifted(level_rows, "px", step) for step in reversed(others)],
        "levels",
    )

    tile_rows, tile_cols = mine, block_count // parts_y
    groups = min(tile_cols, lanes // tile_rows)
    before = None
    for step in range(3):
        if step == 1:
            field_now, block = lax.optimization_barrier((field_now, block))
            ordered = kernel_call(
                functools.partial(margin_rows_kernel, layer, parts_y),
                jax.ShapeDtypeStruct((block_count, layer * thickness), bf16),
                [block.reshape(block_count * layer, thickness)],
                "margin_rows",
                scratch=[pltpu.VMEM((block_count * layer, thickness), f32)],
            )
        operands = [field_now, levels, high, low, edge_matrix, place] + ([before] if step > 0 else [])
        inner, *back = kernel_call(
            functools.partial(inner_kernel, cells, step), [field] + [table] * (step == 2), operands, "inner"
        )
        if step == 2:
            inner, ordered = lax.optimization_barrier((inner, ordered))
        operands = [inner] + edges + [halo_matrix]
        if step < 2:
            before = field_now
            field_now, *edges = kernel_call(
                functools.partial(finish_kernel, cells, step),
                [field, message, message],
                operands + [edge_matrix, low],
                "finish",
            )
            edges = swapped(edges)
        else:
            pieces = kernel_call(
                functools.partial(from_cells_kernel, cells),
                [part] * parts_x,
                operands + back,
                "from_cells",
            )
    received = [pieces[0]] + [shifted(pieces[step], "px", step) for step in others]

    tiles, filtered = kernel_call(
        functools.partial(margin_kernel, parts_x, parts_y),
        [
            jax.ShapeDtypeStruct((parts_x, block_count // groups, groups * tile_rows), f32),
            jax.ShapeDtypeStruct((states, layer, thickness), f32),
        ],
        received + [ordered],
        "margin",
        scratch=[pltpu.SemaphoreType.DMA((parts_x,))],
        out_specs=[whole, anywhere],
    )
    tiles = tiles.reshape(parts_x * parts_y, tile_cols // groups, groups * tile_rows)
    tiles = lax.all_to_all(tiles, ("px", "py"), 0, 0, tiled=True)
    margin = kernel_call(sum_kernel, jax.ShapeDtypeStruct((tile_cols, tile_rows), f32), [tiles], "tile_sum")
    return filtered.reshape(span.shape), margin.T


def solution(mesh):
    in_specs = (P(None, "px", "py", None), P("px", "py", None), P(), P(None, "px", "py", None))
    out_specs = (P(None, "px", "py", None), P("px", "py"))
    return jax.shard_map(local, mesh=mesh, in_specs=in_specs, out_specs=out_specs, check_vma=False)
```

time: 51.3 us -> 51.4 us (level)
  Pallas kernels: 9.69 us -> 11.7 us
  waiting for transfers between devices: 13.2 us -> 11.2 us
    pallas_call x12, Pallas kernels: 9.69 us -> 11.7 us  [kernel_call(): pl.pallas_call(body, out_shape=outs, in_specs=in_specs or [whole] * len(o...]
    ppermute x3, waiting for transfers between devices: 8.58 us -> 6.63 us  [swapped(): other = lax.ppermute(other, 'py', others + [(b, a) for a, b in others])]
  transfers between devices with their start and end apart: 9 -> 9, of which waited for: 9 -> 9; matrix products, arithmetic and copies ran while one was open for 0% -> 0% of each run, Pallas kernels for 9% -> 13%
where the time goes in v13:
time: 51.4 us; the launch traced here: 51.2 us
  starting transfers between devices  15.3 us (30%)
  Pallas kernels  11.7 us (23%)
  waiting for transfers between devices  11.2 us (22%)
  blocking collectives  11.2 us (22%)
  local copies, waits for them, and re-layouts  1.11 us (2%)
  between operations  0.72 us (1%)
    ppermute x3, starting transfers between devices, swapped(): other = lax.ppermute(other, 'py', others + [(b, a) for a, b in others])  14.7 us
    pallas_call x12, Pallas kernels, kernel_call(): pl.pallas_call(body, out_shape=outs, in_specs=in_specs or [whole] * len(o...  11.7 us
    all_to_all x1, blocking collectives, local(): tiles = lax.all_to_all(tiles, ('px', 'py'), 0, 0, tiled=True)  11.2 us
    ppermute x3, waiting for transfers between devices, swapped(): other = lax.ppermute(other, 'py', others + [(b, a) for a, b in others])  6.63 us
    ppermute x3, waiting for transfers between devices, shifted(): lax.ppermute(value, axis, [(source, (source + steps) % count) for source...  2.86 us
    ppermute x3, waiting for transfers between devices, swapped(): pair = lax.ppermute(pair, 'py', pairs + [(b, a) for a, b in pairs])  1.69 us
    dynamic_slice x1, local copies, waits for them, and re-layouts, part_for(): lax.dynamic_slice_in_dim(span_rows, lax.rem(me + step, parts_x) * mine, m...  1.1 us
  transfers between devices with their start and end apart: 9, of which 9 were waited for; matrix products, arithmetic and copies ran while one was open for 0% of the time, Pallas kernels for 13%

profile of v13, /device:TPU:0, one launch (start us, length us, event | category | flops | bytes accessed | tf_op | source)
XLA Modules:
  0.0 51.2 jit_solution(12945652074141642083)
XLA Ops:
  0.7 1.1 %constant_dynamic-slice_fusion = (f32[32,16,128]{2,1,0:T(8,128)S(1)}, f32[32,16,128]{2,1,0:T(8,128)S(1)}) fusion(f32[64,16,128]{2,1,0:T(8,128)} %bitcast.10, s32[]{:T(128)S(6)} %select_n.7, s32[]{:T(128)S(6)} %select_n.6), kind=kLoop, calls=%fused_computation | loop fusion | bytes 1048584 | tf_op jit(solution)/shard_map/dynamic_slice | solution.py:358
  1.8 0.5 %collective-permute-start = (f32[32,16,128]{2,1,0:T(8,128)S(1)}, f32[32,16,128]{2,1,0:T(8,128)S(1)}, u32[]{:S(2)}, u32[]{:S(2)}) collective-permute-start(f32[32,16,128]{2,1,0:T(8,128)S(1)} %get-tuple-element.52), channel_id=1, source_target_pairs={{0,16},{16,0},{1,17},{17,1},{2,18},{18,2},{3,19},{19,3},{4,20},{20... | collective-permute-start | bytes 786440 | tf_op jit(solution)/shard_map/ppermute | solution.py:313
  2.3 1.0 %assemble.1 = (bf16[208,208]{1,0:T(8,128)(2,1)S(1)}, bf16[208,208]{1,0:T(8,128)(2,1)S(1)}, bf16[80,160]{1,0:T(8,128)(2,1)S(1)}, bf16[160,208]{1,0:T(8,128)(2,1)S...) custom-call(f32[125,125]{1,0:T(8,128)S(1)} %copy-done.1), custom_call_target="tpu_custom_call" | custom-call | tf_op jit(solution)/shard_map/assemble/pallas_call | solution.py:318
  3.4 0.8 %to_cells.1 = (f32[4,32,1024]{2,1,0:T(8,128)S(1)}, f32[4,8,1024]{2,1,0:T(8,128)S(1)}, f32[4,8,1024]{2,1,0:T(8,128)S(1)}) custom-call(f32[32,16,128]{2,1,0:T(8,128)S(1)} %get-tuple-element.53.refs_0_, f32[32,16,128]{2,1,0:T(8,128)S(1)} %collective-permute-done.refs_1_, bf16[512,512]{1,0:T(8,128)(2,1)S(1)} %get-tuple-element.27.refs_2_, ...), custom_call_target="tpu_custom_call" | custom-call | tf_op jit(solution)/shard_map/to_cells/pallas_call | solution.py:318
  4.3 6.9 %collective-permute-start.2 = (f32[4,8,1024]{2,1,0:T(8,128)S(1)}, f32[4,8,1024]{2,1,0:T(8,128)S(1)}, u32[]{:S(2)}, u32[]{:S(2)}) collective-permute-start(f32[4,8,1024]{2,1,0:T(8,128)S(1)} %get-tuple-element.33), channel_id=1, source_target_pairs={{1,2},{3,4},{5,6},{7,8},{9,10},{11,12},{13,14},{15,0},{2,1},{4,3},... | collective-permute-start | bytes 393224 | tf_op jit(solution)/shard_map/ppermute | solution.py:306
  11.2 1.2 %collective-permute-done.1.refs_1_ = f32[16,128]{1,0:T(8,128)S(1)} collective-permute-done((f32[16,128]{1,0:T(8,128)S(1)}, f32[16,128]{1,0:T(8,128)S(1)}, u32[]{:S(2)}, u32[]{:S(2)}) %collective-permute-start.1) | collective-permute-done | bytes 8224 | tf_op jit(solution)/shard_map/ppermute | solution.py:313
  12.5 1.3 %inner.3.inner_ref = f32[4,32,1024]{2,1,0:T(8,128)S(1)} custom-call(f32[4,32,1024]{2,1,0:T(8,128)S(1)} %get-tuple-element.30.refs_0_.refs_6_, f32[4,32,128]{2,1,0:T(8,128)S(1)} %levels.1.refs_1_, bf16[208,208]{1,0:T(8,128)(2,1)S(1)} %get-tuple-element.31.refs_2_, bf16[208,208]{1,0:T(8,128)(2,1)S(1)} %get-tuple-element.29.refs_4_.refs_3_.low_ref, ...), custom_call_target="tpu_custom_call" | custom-call | tf_op jit(solution)/shard_map/inner/pallas_call | solution.py:318
  13.8 1.2 %collective-permute-done.2.from_other_ref = f32[4,8,1024]{2,1,0:T(8,128)S(1)} collective-permute-done((f32[4,8,1024]{2,1,0:T(8,128)S(1)}, f32[4,8,1024]{2,1,0:T(8,128)S(1)}, u32[]{:S(2)}, u32[]{:S(2)}) %collective-permute-start.2) | collective-permute-done | bytes 131104 | tf_op jit(solution)/shard_map/ppermute | solution.py:306
  15.1 1.4 %collective-permute-done.3.from_pair_ref = f32[4,8,1024]{2,1,0:T(8,128)S(1)} collective-permute-done((f32[4,8,1024]{2,1,0:T(8,128)S(1)}, f32[4,8,1024]{2,1,0:T(8,128)S(1)}, u32[]{:S(2)}, u32[]{:S(2)}) %collective-permute-start.3) | collective-permute-done | bytes 131104 | tf_op jit(solution)/shard_map/ppermute | solution.py:307
  16.4 0.8 %finish.2 = (f32[4,32,1024]{2,1,0:T(8,128)S(1)}, f32[4,8,1024]{2,1,0:T(8,128)S(1)}, f32[4,8,1024]{2,1,0:T(8,128)S(1)}) custom-call(f32[4,32,1024]{2,1,0:T(8,128)S(1)} %inner.3.inner_ref, f32[4,8,1024]{2,1,0:T(8,128)S(1)} %collective-permute-done.2.from_other_ref, f32[4,8,1024]{2,1,0:T(8,128)S(1)} %collective-permute-done.3.from_pair_ref, ...), custom_call_target="tpu_custom_call" | custom-call | tf_op jit(solution)/shard_map/finish/pallas_call | solution.py:318
  17.2 4.0 %collective-permute-start.4 = (f32[4,8,1024]{2,1,0:T(8,128)S(1)}, f32[4,8,1024]{2,1,0:T(8,128)S(1)}, u32[]{:S(2)}, u32[]{:S(2)}) collective-permute-start(f32[4,8,1024]{2,1,0:T(8,128)S(1)} %get-tuple-element.38), channel_id=1, source_target_pairs={{1,2},{3,4},{5,6},{7,8},{9,10},{11,12},{13,14},{15,0},{2,1},{4,3},... | collective-permute-start | bytes 393224 | tf_op jit(solution)/shard_map/ppermute | solution.py:306
  21.3 1.3 %inner.4.inner_ref = f32[4,32,1024]{2,1,0:T(8,128)S(1)} custom-call(f32[4,32,1024]{2,1,0:T(8,128)S(1)} %get-tuple-element.37.refs_0_.refs_6_, f32[4,32,128]{2,1,0:T(8,128)S(1)} %levels.1.refs_1_, bf16[208,208]{1,0:T(8,128)(2,1)S(1)} %get-tuple-element.31.refs_2_, bf16[208,208]{1,0:T(8,128)(2,1)S(1)} %get-tuple-element.29.refs_4_.refs_3_.low_ref, ...), custom_call_target="tpu_custom_call" | custom-call | tf_op jit(solution)/shard_map/inner/pallas_call | solution.py:318
  22.6 3.4 %collective-permute-done.4.from_other_ref = f32[4,8,1024]{2,1,0:T(8,128)S(1)} collective-permute-done((f32[4,8,1024]{2,1,0:T(8,128)S(1)}, f32[4,8,1024]{2,1,0:T(8,128)S(1)}, u32[]{:S(2)}, u32[]{:S(2)}) %collective-permute-start.4) | collective-permute-done | bytes 131104 | tf_op jit(solution)/shard_map/ppermute | solution.py:306
  26.0 0.3 collective-permute-done.5.from_pair_ref
  26.3 0.8 %finish.3 = (f32[4,32,1024]{2,1,0:T(8,128)S(1)}, f32[4,8,1024]{2,1,0:T(8,128)S(1)}, f32[4,8,1024]{2,1,0:T(8,128)S(1)}) custom-call(f32[4,32,1024]{2,1,0:T(8,128)S(1)} %inner.4.inner_ref, f32[4,8,1024]{2,1,0:T(8,128)S(1)} %collective-permute-done.4.from_other_ref, f32[4,8,1024]{2,1,0:T(8,128)S(1)} %collective-permute-done.5.from_pair_ref, ...), custom_call_target="tpu_custom_call" | custom-call | tf_op jit(solution)/shard_map/finish/pallas_call | solution.py:318
  27.1 3.7 %collective-permute-start.6 = (f32[4,8,1024]{2,1,0:T(8,128)S(1)}, f32[4,8,1024]{2,1,0:T(8,128)S(1)}, u32[]{:S(2)}, u32[]{:S(2)}) collective-permute-start(f32[4,8,1024]{2,1,0:T(8,128)S(1)} %get-tuple-element.44), channel_id=1, source_target_pairs={{1,2},{3,4},{5,6},{7,8},{9,10},{11,12},{13,14},{15,0},{2,1},{4,3},... | collective-permute-start | bytes 393224 | tf_op jit(solution)/shard_map/ppermute | solution.py:306
  30.8 1.3 %margin_rows.1.refs_2_ = bf16[256,2048]{1,0:T(8,128)(2,1)S(1)} custom-call(bf16[4096,128]{1,0:T(8,128)(2,1)S(1)} %bitcast.6), custom_call_target="tpu_custom_call" | custom-call | tf_op jit(solution)/shard_map/margin_rows/pallas_call | solution.py:318
  32.1 1.5 %inner.5 = (f32[4,32,1024]{2,1,0:T(8,128)S(1)}, bf16[512,512]{1,0:T(8,128)(2,1)S(1)}) custom-call(f32[4,32,1024]{2,1,0:T(8,128)S(1)} %get-tuple-element.40.refs_0_, f32[4,32,128]{2,1,0:T(8,128)S(1)} %levels.1.refs_1_, bf16[208,208]{1,0:T(8,128)(2,1)S(1)} %get-tuple-element.31.refs_2_, bf16[208,208]{1,0:T(8,128)(2,1)S(1)} %get-tuple-element.29.refs_4_.refs_3_.low_ref, ...), custom_call_target="tpu_custom_call" | custom-call | tf_op jit(solution)/shard_map/inner/pallas_call | solution.py:318
  33.7 2.0 %collective-permute-done.6.refs_1_ = f32[4,8,1024]{2,1,0:T(8,128)S(1)} collective-permute-done((f32[4,8,1024]{2,1,0:T(8,128)S(1)}, f32[4,8,1024]{2,1,0:T(8,128)S(1)}, u32[]{:S(2)}, u32[]{:S(2)}) %collective-permute-start.6) | collective-permute-done | bytes 131104 | tf_op jit(solution)/shard_map/ppermute | solution.py:306
  35.8 0.8 %from_cells.1 = (f32[32,16,128]{2,1,0:T(8,128)S(1)}, f32[32,16,128]{2,1,0:T(8,128)S(1)}) custom-call(f32[4,32,1024]{2,1,0:T(8,128)S(1)} %get-tuple-element.43.refs_0_, f32[4,8,1024]{2,1,0:T(8,128)S(1)} %collective-permute-done.6.refs_1_, f32[4,8,1024]{2,1,0:T(8,128)S(1)} %collective-permute-done.7.refs_2_, ...), custom_call_target="tpu_custom_call" | custom-call | tf_op jit(solution)/shard_map/from_cells/pallas_call | solution.py:318
  36.6 1.5 %collective-permute-done.8.refs_1_ = f32[32,16,128]{2,1,0:T(8,128)S(1)} collective-permute-done((f32[32,16,128]{2,1,0:T(8,128)S(1)}, f32[32,16,128]{2,1,0:T(8,128)S(1)}, u32[]{:S(2)}, u32[]{:S(2)}) %collective-permute-start.8) | collective-permute-done | bytes 262176 | tf_op jit(solution)/shard_map/ppermute | solution.py:313
  38.1 1.2 %margin.1 = (f32[2,64,128]{2,1,0:T(8,128)S(1)}, f32[64,16,128]{2,1,0:T(8,128)}) custom-call(f32[32,16,128]{2,1,0:T(8,128)S(1)} %get-tuple-element.47.refs_0_, f32[32,16,128]{2,1,0:T(8,128)S(1)} %collective-permute-done.8.refs_1_, bf16[256,2048]{1,0:T(8,128)(2,1)S(1)} %margin_rows.1.refs_2_), custom_call_target="tpu_custom_call" | custom-call | tf_op jit(solution)/shard_map/margin/pallas_call | solution.py:318
  39.3 11.2 %all_to_all.5.tiles_ref = f32[32,4,128]{2,1,0:T(4,128)S(1)} all-to-all(f32[32,4,128]{2,1,0:T(4,128)S(1)} %bitcast.7), channel_id=1, replica_groups=mesh['px'=2,'py'=16] {'px','py'}, dimensions={0} | all-to-all | bytes 131072 | tf_op jit(solution)/shard_map/all_to_all | solution.py:432
  50.5 0.7 %tile_sum.1 = f32[16,32]{1,0:T(8,128)} custom-call(f32[32,4,128]{2,1,0:T(4,128)S(1)} %all_to_all.5.tiles_ref), custom_call_target="tpu_custom_call" | custom-call | tf_op jit(solution)/shard_map/tile_sum/pallas_call | solution.py:318
  (14 shorter events, 0.5 us)
Async XLA Ops:
  0.6 1.6 %copy-start.1 = (f32[125,125]{1,0:T(8,128)S(1)}, f32[125,125]{1,0:T(8,128)}, u32[]{:S(2)}) copy-start(f32[125,125]{1,0:T(8,128)} %cell_ref.1) | copy-start | bytes 187504
  1.8 1.7 %collective-permute-start = (f32[32,16,128]{2,1,0:T(8,128)S(1)}, f32[32,16,128]{2,1,0:T(8,128)S(1)}, u32[]{:S(2)}, u32[]{:S(2)}) collective-permute-start(f32[32,16,128]{2,1,0:T(8,128)S(1)} %get-tuple-element.52), channel_id=1, source_target_pairs={{0,16},{16,0},{1,17},{17,1},{2,18},{18,2},{3,19},{19,3},{4,20},{20... | collective-permute-start | bytes 786440 | tf_op jit(solution)/shard_map/ppermute | solution.py:313
  3.4 7.7 %copy-start.2 = (f32[4,4,128]{2,1,0:T(4,128)S(1)}, f32[4,4,128]{2,1,0:T(4,128)}, u32[]{:S(2)}) copy-start(f32[4,4,128]{2,1,0:T(4,128)} %param.5) | copy-start | bytes 24580
  4.3 10.8 %collective-permute-start.2 = (f32[4,8,1024]{2,1,0:T(8,128)S(1)}, f32[4,8,1024]{2,1,0:T(8,128)S(1)}, u32[]{:S(2)}, u32[]{:S(2)}) collective-permute-start(f32[4,8,1024]{2,1,0:T(8,128)S(1)} %get-tuple-element.33), channel_id=1, source_target_pairs={{1,2},{3,4},{5,6},{7,8},{9,10},{11,12},{13,14},{15,0},{2,1},{4,3},... | collective-permute-start | bytes 393224 | tf_op jit(solution)/shard_map/ppermute | solution.py:306
  11.2 5.3 %collective-permute-start.3 = (f32[4,8,1024]{2,1,0:T(8,128)S(1)}, f32[4,8,1024]{2,1,0:T(8,128)S(1)}, u32[]{:S(2)}, u32[]{:S(2)}) collective-permute-start(f32[4,8,1024]{2,1,0:T(8,128)S(1)} %get-tuple-element.34), channel_id=1, source_target_pairs={{0,1},{2,3},{4,5},{6,7},{8,9},{10,11},{12,13},{14,15},{1,0},{3,2},... | collective-permute-start | bytes 393224 | tf_op jit(solution)/shard_map/ppermute | solution.py:307
  11.2 1.2 %collective-permute-start.1 = (f32[16,128]{1,0:T(8,128)S(1)}, f32[16,128]{1,0:T(8,128)S(1)}, u32[]{:S(2)}, u32[]{:S(2)}) collective-permute-start(f32[16,128]{1,0:T(8,128)S(1)} %bitcast.8), channel_id=1, source_target_pairs={{0,16},{16,0},{1,17},{17,1},{2,18},{18,2},{3,19},{19,3},{4,20},{20... | collective-permute-start | bytes 24584 | tf_op jit(solution)/shard_map/ppermute | solution.py:313
  17.2 8.7 %collective-permute-start.4 = (f32[4,8,1024]{2,1,0:T(8,128)S(1)}, f32[4,8,1024]{2,1,0:T(8,128)S(1)}, u32[]{:S(2)}, u32[]{:S(2)}) collective-permute-start(f32[4,8,1024]{2,1,0:T(8,128)S(1)} %get-tuple-element.38), channel_id=1, source_target_pairs={{1,2},{3,4},{5,6},{7,8},{9,10},{11,12},{13,14},{15,0},{2,1},{4,3},... | collective-permute-start | bytes 393224 | tf_op jit(solution)/shard_map/ppermute | solution.py:306
  21.3 5.0 %collective-permute-start.5 = (f32[4,8,1024]{2,1,0:T(8,128)S(1)}, f32[4,8,1024]{2,1,0:T(8,128)S(1)}, u32[]{:S(2)}, u32[]{:S(2)}) collective-permute-start(f32[4,8,1024]{2,1,0:T(8,128)S(1)} %get-tuple-element.39), channel_id=1, source_target_pairs={{0,1},{2,3},{4,5},{6,7},{8,9},{10,11},{12,13},{14,15},{1,0},{3,2},... | collective-permute-start | bytes 393224 | tf_op jit(solution)/shard_map/ppermute | solution.py:307
  21.3 9.5 %copy-start = (bf16[256,4,4,128]{3,2,1,0:T(4,128)(2,1)S(1)}, bf16[256,4,4,128]{3,2,1,0:T(4,128)(2,1)}, u32[]{:S(2)}) copy-start(bf16[256,4,4,128]{3,2,1,0:T(4,128)(2,1)} %param.7) | copy-start | bytes 3145732
  27.1 8.6 %collective-permute-start.6 = (f32[4,8,1024]{2,1,0:T(8,128)S(1)}, f32[4,8,1024]{2,1,0:T(8,128)S(1)}, u32[]{:S(2)}, u32[]{:S(2)}) collective-permute-start(f32[4,8,1024]{2,1,0:T(8,128)S(1)} %get-tuple-element.44), channel_id=1, source_target_pairs={{1,2},{3,4},{5,6},{7,8},{9,10},{11,12},{13,14},{15,0},{2,1},{4,3},... | collective-permute-start | bytes 393224 | tf_op jit(solution)/shard_map/ppermute | solution.py:306
  30.8 5.0 %collective-permute-start.7 = (f32[4,8,1024]{2,1,0:T(8,128)S(1)}, f32[4,8,1024]{2,1,0:T(8,128)S(1)}, u32[]{:S(2)}, u32[]{:S(2)}) collective-permute-start(f32[4,8,1024]{2,1,0:T(8,128)S(1)} %get-tuple-element.45), channel_id=1, source_target_pairs={{0,1},{2,3},{4,5},{6,7},{8,9},{10,11},{12,13},{14,15},{1,0},{3,2},... | collective-permute-start | bytes 393224 | tf_op jit(solution)/shard_map/ppermute | solution.py:307
  36.5 1.6 %collective-permute-start.8 = (f32[32,16,128]{2,1,0:T(8,128)S(1)}, f32[32,16,128]{2,1,0:T(8,128)S(1)}, u32[]{:S(2)}, u32[]{:S(2)}) collective-permute-start(f32[32,16,128]{2,1,0:T(8,128)S(1)} %get-tuple-element.48), channel_id=1, source_target_pairs={{0,16},{16,0},{1,17},{17,1},{2,18},{18,2},{3,19},{19,3},{4,20},{20... | collective-permute-start | bytes 786440 | tf_op jit(solution)/shard_map/ppermute | solution.py:313

commit v14 on v11

--- a/solution.py
+++ b/solution.py
@@ -225,7 +225,7 @@
             out_ref[iz, iy] = total if step == 0 else total - before_ref[iz, iy]
 
 
-def finish(cells, step, inner_ref, other_ref, pair_ref, matrix_ref):
+def finish(cells, step, inner_ref, pair_ref, other_ref, matrix_ref):
     nodes, width = inner_ref.shape[2:]
     even = even_place()
     halo = [jnp.where(even, pair_ref[iz], other_ref[iz]) for iz in range(4)]
@@ -247,17 +247,17 @@
     return result
 
 
-def finish_kernel(cells, step, inner_ref, from_other_ref, from_pair_ref, matrix_ref, high_ref, low_ref, next_ref, pair_ref, other_ref):
-    value = finish(cells, step, inner_ref, from_other_ref, from_pair_ref, matrix_ref)
+def finish_kernel(cells, step, inner_ref, from_pair_ref, from_other_ref, matrix_ref, high_ref, low_ref, next_ref, pair_ref, other_ref):
+    value = finish(cells, step, inner_ref, from_pair_ref, from_other_ref, matrix_ref)
     for (iz, iy), part in value.items():
         next_ref[iz, iy] = part
     send_edges(high_ref, low_ref, value, pair_ref, other_ref, cells)
 
 
 def last_kernel(cells, second, parts_x, parts_y, *refs):
-    inner_ref, other_ref, pair_ref, matrix_ref, order_ref = refs[:5]
+    inner_ref, pair_ref, other_ref, matrix_ref, order_ref = refs[:5]
     block_refs, out_refs, tiles_ref = refs[5 : 5 + parts_x], refs[5 + parts_x : -1], refs[-1]
-    value = finish(cells, 2, inner_ref, other_ref, pair_ref, matrix_ref)
+    value = finish(cells, 2, inner_ref, pair_ref, other_ref, matrix_ref)
     states, layer, thickness = out_refs[0].shape
     first = layer // second
     nodes = parts_x * first
@@ -324,7 +324,7 @@
     pair, other = edges
     other = lax.ppermute(other, "py", others + [(b, a) for a, b in others])
     pair = lax.ppermute(pair, "py", pairs + [(b, a) for a, b in pairs])
-    return [other, pair]
+    return [pair, other]
 
 
 def shifted(value, axis, steps):
@@ -332,9 +332,8 @@
     return lax.ppermute(value, axis, [(source, (source + steps) % count) for source in range(count)])
 
 
-def kernel_call(body, outs, operands, name, scratch=(), in_specs=None, out_specs=None, work=0):
+def kernel_call(body, outs, operands, name, scratch=(), in_specs=None, out_specs=None):
     many = isinstance(outs, list)
-    moved = sum(a.size * a.dtype.itemsize for a in list(operands) + (outs if many else [outs]))
     return pl.pallas_call(
         body,
         out_shape=outs,
@@ -342,7 +341,6 @@
         out_specs=out_specs or ([whole] * len(outs) if many else whole),
         scratch_shapes=list(scratch),
         compiler_params=params,
-        cost_estimate=pl.CostEstimate(flops=work or moved, bytes_accessed=moved, transcendentals=0),
         name=name,
     )(*operands)
 
@@ -422,6 +420,8 @@
         inner, *back = kernel_call(
             functools.partial(inner_kernel, cells, step), [field] + [table] * (step == 2), operands, "inner"
         )
+        if step == 1:
+            inner, blocks[0] = lax.optimization_barrier((inner, blocks[0]))
         if step == 2:
             inner, blocks = lax.optimization_barrier((inner, blocks))
         operands = [inner] + edges + [halo_matrix]

time: 53.6 us -> 53.6 us (level)
  waiting for transfers between devices: 11.1 us -> 8.97 us
  starting transfers between devices: 15.5 us -> 17 us
  blocking collectives: 12.3 us -> 12.9 us
    ppermute x3, starting transfers between devices: 0.01 us -> 3.21 us  [swapped(): pair = lax.ppermute(pair, 'py', pairs + [(b, a) for a, b in pairs])]
    ppermute x3, starting transfers between devices: 14.7 us -> 13.1 us  [swapped(): other = lax.ppermute(other, 'py', others + [(b, a) for a, b in others])]
    ppermute x3, waiting for transfers between devices: 1.67 us -> 0.13 us  [swapped(): pair = lax.ppermute(pair, 'py', pairs + [(b, a) for a, b in pairs])]
    ppermute x3, waiting for transfers between devices: 8.4 us -> 7.67 us  [swapped(): other = lax.ppermute(other, 'py', others + [(b, a) for a, b in others])]
    all_to_all x1, blocking collectives: 12.3 us -> 12.9 us  [local(): tiles = lax.all_to_all(tiles, 'py', 0, 0, tiled=True)]
  transfers between devices with their start and end apart: 10 -> 10, of which waited for: 6 -> 5; matrix products, arithmetic and copies ran while one was open for 0% -> 0% of each run, Pallas kernels for 14% -> 14%
where the time goes in v14:
time: 53.6 us; the launch traced here: 53.4 us
  starting transfers between devices  17 us (32%)
  blocking collectives  12.9 us (24%)
  Pallas kernels  11.8 us (22%)
  waiting for transfers between devices  8.97 us (17%)
  local copies, waits for them, and re-layouts  1.92 us (4%)
  between operations  0.79 us (1%)
    ppermute x3, starting transfers between devices, swapped(): other = lax.ppermute(other, 'py', others + [(b, a) for a, b in others])  13.1 us
    all_to_all x1, blocking collectives, local(): tiles = lax.all_to_all(tiles, 'py', 0, 0, tiled=True)  12.9 us
    pallas_call x14, Pallas kernels, kernel_call(): pl.pallas_call(body, out_shape=outs, in_specs=in_specs or [whole] * len(o...  11.8 us
    ppermute x3, waiting for transfers between devices, swapped(): other = lax.ppermute(other, 'py', others + [(b, a) for a, b in others])  7.67 us
    ppermute x3, starting transfers between devices, swapped(): pair = lax.ppermute(pair, 'py', pairs + [(b, a) for a, b in pairs])  3.21 us
    ppermute x4, waiting for transfers between devices, shifted(): lax.ppermute(value, axis, [(source, (source + steps) % count) for source...  1.18 us
  transfers between devices with their start and end apart: 10, of which 5 were waited for; matrix products, arithmetic and copies ran while one was open for 0% of the time, Pallas kernels for 14%

profile of v14, /device:TPU:0, one launch (start us, length us, event | category | flops | bytes accessed | tf_op | source)
XLA Modules:
  0.0 53.4 jit_solution(2174065579414463414)
XLA Ops:
  0.7 1.1 %constant_dynamic-slice_fusion = (f32[32,16,128]{2,1,0:T(8,128)S(1)}, f32[32,16,128]{2,1,0:T(8,128)S(1)}) fusion(f32[64,16,128]{2,1,0:T(8,128)} %bitcast.10, s32[]{:T(128)S(6)} %select_n.7, s32[]{:T(128)S(6)} %select_n.6), kind=kLoop, calls=%fused_computation | loop fusion | bytes 1048584 | tf_op jit(solution)/shard_map/dynamic_slice | solution.py:374
  1.7 0.5 collective-permute-start
  2.3 0.8 %copy-done.1 = f32[125,125]{1,0:T(8,128)S(1)} copy-done((f32[125,125]{1,0:T(8,128)S(1)}, f32[125,125]{1,0:T(8,128)}, u32[]{:S(2)}) %copy-start.1) | copy-done | bytes 62524
  3.1 0.9 %assemble.1 = (bf16[208,208]{1,0:T(8,128)(2,1)S(1)}, bf16[208,208]{1,0:T(8,128)(2,1)S(1)}, bf16[160,144]{1,0:T(8,128)(2,1)S(1)}, bf16[512,512]{1,0:T(8,128)(2,1)S(1)}) custom-call(f32[125,125]{1,0:T(8,128)S(1)} %copy-done.1), custom_call_target="tpu_custom_call" | custom-call | tf_op jit(solution)/shard_map/assemble/pallas_call | solution.py:337
  4.1 0.8 %to_cells.1 = (f32[4,4,8,1024]{3,2,1,0:T(8,128)S(1)}, f32[4,8,1024]{2,1,0:T(8,128)S(1)}, f32[4,8,1024]{2,1,0:T(8,128)S(1)}) custom-call(f32[32,16,128]{2,1,0:T(8,128)S(1)} %get-tuple-element.53.refs_0_, f32[32,16,128]{2,1,0:T(8,128)S(1)} %collective-permute-done.refs_1_, bf16[512,512]{1,0:T(8,128)(2,1)S(1)} %get-tuple-element.27.refs_2_, ...), custom_call_target="tpu_custom_call" | custom-call | tf_op jit(solution)/shard_map/to_cells/pallas_call | solution.py:337
  4.9 2.6 %collective-permute-start.2 = (f32[4,8,1024]{2,1,0:T(8,128)S(1)}, f32[4,8,1024]{2,1,0:T(8,128)S(1)}, u32[]{:S(2)}, u32[]{:S(2)}) collective-permute-start(f32[4,8,1024]{2,1,0:T(8,128)S(1)} %get-tuple-element.31), channel_id=1, source_target_pairs={{0,1},{2,3},{4,5},{6,7},{8,9},{10,11},{12,13},{14,15},{1,0},{3,2},... | collective-permute-start | bytes 393224 | tf_op jit(solution)/shard_map/ppermute | solution.py:326
  7.5 4.5 %collective-permute-start.3 = (f32[4,8,1024]{2,1,0:T(8,128)S(1)}, f32[4,8,1024]{2,1,0:T(8,128)S(1)}, u32[]{:S(2)}, u32[]{:S(2)}) collective-permute-start(f32[4,8,1024]{2,1,0:T(8,128)S(1)} %get-tuple-element.32), channel_id=1, source_target_pairs={{1,2},{3,4},{5,6},{7,8},{9,10},{11,12},{13,14},{15,0},{2,1},{4,3},... | collective-permute-start | bytes 393224 | tf_op jit(solution)/shard_map/ppermute | solution.py:325
  12.0 1.2 %collective-permute-done.1.refs_1_ = f32[1,16,128]{2,1,0:T(8,128)S(1)} collective-permute-done((f32[1,16,128]{2,1,0:T(8,128)S(1)}, f32[1,16,128]{2,1,0:T(8,128)S(1)}, u32[]{:S(2)}, u32[]{:S(2)}) %collective-permute-start.1) | collective-permute-done | bytes 8224 | tf_op jit(solution)/shard_map/ppermute | solution.py:332
  13.4 0.7 %inner.3.inner_ref = f32[4,4,8,1024]{3,2,1,0:T(8,128)S(1)} custom-call(f32[4,4,8,1024]{3,2,1,0:T(8,128)S(1)} %get-tuple-element.30.refs_0_.refs_4_, f32[4,4,8,128]{3,2,1,0:T(8,128)S(1)} %levels.1.refs_1_, bf16[208,208]{1,0:T(8,128)(2,1)S(1)} %get-tuple-element.28.refs_3_.refs_2_.high_ref, bf16[208,208]{1,0:T(8,128)(2,1)S(1)} %get-tuple-element.29.refs_4_.refs_3_.low_ref), custom_call_target="tpu_custom_call" | custom-call | tf_op jit(solution)/shard_map/inner/pallas_call | solution.py:337
  14.0 2.6 %collective-permute-done.3.from_other_ref = f32[4,8,1024]{2,1,0:T(8,128)S(1)} collective-permute-done((f32[4,8,1024]{2,1,0:T(8,128)S(1)}, f32[4,8,1024]{2,1,0:T(8,128)S(1)}, u32[]{:S(2)}, u32[]{:S(2)}) %collective-permute-start.3) | collective-permute-done | bytes 131104 | tf_op jit(solution)/shard_map/ppermute | solution.py:325
  16.6 0.8 %finish.2 = (f32[4,4,8,1024]{3,2,1,0:T(8,128)S(1)}, f32[4,8,1024]{2,1,0:T(8,128)S(1)}, f32[4,8,1024]{2,1,0:T(8,128)S(1)}) custom-call(f32[4,4,8,1024]{3,2,1,0:T(8,128)S(1)} %inner.3.inner_ref, f32[4,8,1024]{2,1,0:T(8,128)S(1)} %collective-permute-done.2.from_pair_ref, f32[4,8,1024]{2,1,0:T(8,128)S(1)} %collective-permute-done.3.from_other_ref, ...), custom_call_target="tpu_custom_call" | custom-call | tf_op jit(solution)/shard_map/finish/pallas_call | solution.py:337
  18.2 4.2 %collective-permute-start.5 = (f32[4,8,1024]{2,1,0:T(8,128)S(1)}, f32[4,8,1024]{2,1,0:T(8,128)S(1)}, u32[]{:S(2)}, u32[]{:S(2)}) collective-permute-start(f32[4,8,1024]{2,1,0:T(8,128)S(1)} %get-tuple-element.39), channel_id=1, source_target_pairs={{1,2},{3,4},{5,6},{7,8},{9,10},{11,12},{13,14},{15,0},{2,1},{4,3},... | collective-permute-start | bytes 393224 | tf_op jit(solution)/shard_map/ppermute | solution.py:325
  22.4 1.2 %margin_rows.2.refs_5_ = bf16[256,2048]{1,0:T(8,128)(2,1)S(1)} custom-call(f32[4096,128]{1,0:T(8,128)S(1)} %widen.1.wide_ref), custom_call_target="tpu_custom_call" | custom-call | tf_op jit(solution)/shard_map/margin_rows/pallas_call | solution.py:337
  23.6 0.7 %inner.4.inner_ref = f32[4,4,8,1024]{3,2,1,0:T(8,128)S(1)} custom-call(f32[4,4,8,1024]{3,2,1,0:T(8,128)S(1)} %get-tuple-element.35.refs_0_.refs_4_, f32[4,4,8,128]{3,2,1,0:T(8,128)S(1)} %levels.1.refs_1_, bf16[208,208]{1,0:T(8,128)(2,1)S(1)} %get-tuple-element.28.refs_3_.refs_2_.high_ref, bf16[208,208]{1,0:T(8,128)(2,1)S(1)} %get-tuple-element.29.refs_4_.refs_3_.low_ref, ...), custom_call_target="tpu_custom_call" | custom-call | tf_op jit(solution)/shard_map/inner/pallas_call | solution.py:337
  24.4 3.0 %collective-permute-done.5.from_other_ref = f32[4,8,1024]{2,1,0:T(8,128)S(1)} collective-permute-done((f32[4,8,1024]{2,1,0:T(8,128)S(1)}, f32[4,8,1024]{2,1,0:T(8,128)S(1)}, u32[]{:S(2)}, u32[]{:S(2)}) %collective-permute-start.5) | collective-permute-done | bytes 131104 | tf_op jit(solution)/shard_map/ppermute | solution.py:325
  27.4 0.8 %finish.3 = (f32[4,4,8,1024]{3,2,1,0:T(8,128)S(1)}, f32[4,8,1024]{2,1,0:T(8,128)S(1)}, f32[4,8,1024]{2,1,0:T(8,128)S(1)}) custom-call(f32[4,4,8,1024]{3,2,1,0:T(8,128)S(1)} %inner.4.inner_ref, f32[4,8,1024]{2,1,0:T(8,128)S(1)} %collective-permute-done.4.from_pair_ref, f32[4,8,1024]{2,1,0:T(8,128)S(1)} %collective-permute-done.5.from_other_ref, ...), custom_call_target="tpu_custom_call" | custom-call | tf_op jit(solution)/shard_map/finish/pallas_call | solution.py:337
  28.2 4.4 %collective-permute-start.8 = (f32[4,8,1024]{2,1,0:T(8,128)S(1)}, f32[4,8,1024]{2,1,0:T(8,128)S(1)}, u32[]{:S(2)}, u32[]{:S(2)}) collective-permute-start(f32[4,8,1024]{2,1,0:T(8,128)S(1)} %get-tuple-element.45), channel_id=1, source_target_pairs={{1,2},{3,4},{5,6},{7,8},{9,10},{11,12},{13,14},{15,0},{2,1},{4,3},... | collective-permute-start | bytes 393224 | tf_op jit(solution)/shard_map/ppermute | solution.py:325
  32.7 0.9 %inner.5 = (f32[4,4,8,1024]{3,2,1,0:T(8,128)S(1)}, bf16[512,512]{1,0:T(8,128)(2,1)S(1)}) custom-call(f32[4,4,8,1024]{3,2,1,0:T(8,128)S(1)} %get-tuple-element.40.refs_0_, f32[4,4,8,128]{3,2,1,0:T(8,128)S(1)} %levels.1.refs_1_, bf16[208,208]{1,0:T(8,128)(2,1)S(1)} %get-tuple-element.28.refs_3_.refs_2_.high_ref, ...), custom_call_target="tpu_custom_call" | custom-call | tf_op jit(solution)/shard_map/inner/pallas_call | solution.py:337
  33.6 1.2 %margin_rows.3.refs_6_ = bf16[256,2048]{1,0:T(8,128)(2,1)S(1)} custom-call(f32[4096,128]{1,0:T(8,128)S(1)} %collective-permute-done.6.wide_ref), custom_call_target="tpu_custom_call" | custom-call | tf_op jit(solution)/shard_map/margin_rows/pallas_call | solution.py:337
  34.8 2.1 %collective-permute-done.8.refs_2_ = f32[4,8,1024]{2,1,0:T(8,128)S(1)} collective-permute-done((f32[4,8,1024]{2,1,0:T(8,128)S(1)}, f32[4,8,1024]{2,1,0:T(8,128)S(1)}, u32[]{:S(2)}, u32[]{:S(2)}) %collective-permute-start.8) | collective-permute-done | bytes 131104 | tf_op jit(solution)/shard_map/ppermute | solution.py:325
  36.9 2.0 %last.1 = (f32[32,16,128]{2,1,0:T(8,128)S(1)}, f32[32,16,128]{2,1,0:T(8,128)S(1)}, f32[64,128]{1,0:T(8,128)S(1)}) custom-call(f32[4,4,8,1024]{3,2,1,0:T(8,128)S(1)} %get-tuple-element.43.refs_0_, f32[4,8,1024]{2,1,0:T(8,128)S(1)} %collective-permute-done.7.refs_1_, f32[4,8,1024]{2,1,0:T(8,128)S(1)} %collective-permute-done.8.refs_2_, ...), custom_call_target="tpu_custom_call" | custom-call | tf_op jit(solution)/shard_map/last/pallas_call | solution.py:337
  39.0 12.9 %all_to_all.5.tiles_ref = f32[16,4,128]{2,1,0:T(4,128)S(1)} all-to-all(f32[16,4,128]{2,1,0:T(4,128)S(1)} %bitcast.7), channel_id=1, replica_groups=mesh['px'=2,'py'=16] {'py'}, dimensions={0} | all-to-all | bytes 65536 | tf_op jit(solution)/shard_map/all_to_all | solution.py:446
  51.9 0.7 %tile_sum.1 = f32[16,32]{1,0:T(8,128)} custom-call(f32[16,4,128]{2,1,0:T(4,128)S(1)} %all_to_all.5.tiles_ref), custom_call_target="tpu_custom_call" | custom-call | tf_op jit(solution)/shard_map/tile_sum/pallas_call | solution.py:337
  52.6 0.8 %join.1 = f32[64,16,128]{2,1,0:T(8,128)} custom-call(f32[32,16,128]{2,1,0:T(8,128)S(1)} %get-tuple-element.49.refs_0_, f32[32,16,128]{2,1,0:T(8,128)S(1)} %collective-permute-done.9.refs_1_), custom_call_target="tpu_custom_call" | custom-call | tf_op jit(solution)/shard_map/join/pallas_call | solution.py:337
  (18 shorter events, 1.2 us)
Async XLA Ops:
  0.6 11.4 %copy-start.2 = (f32[4,4,128]{2,1,0:T(4,128)S(1)}, f32[4,4,128]{2,1,0:T(4,128)}, u32[]{:S(2)}) copy-start(f32[4,4,128]{2,1,0:T(4,128)} %param.5) | copy-start | bytes 24580
  1.7 15.7 %copy-start = (bf16[256,4,4,128]{3,2,1,0:T(4,128)(2,1)S(1)}, bf16[256,4,4,128]{3,2,1,0:T(4,128)(2,1)}, u32[]{:S(2)}) copy-start(bf16[256,4,4,128]{3,2,1,0:T(4,128)(2,1)} %param.7) | copy-start | bytes 3145732
  1.7 2.3 %collective-permute-start = (f32[32,16,128]{2,1,0:T(8,128)S(1)}, f32[32,16,128]{2,1,0:T(8,128)S(1)}, u32[]{:S(2)}, u32[]{:S(2)}) collective-permute-start(f32[32,16,128]{2,1,0:T(8,128)S(1)} %get-tuple-element.52), channel_id=1, source_target_pairs={{0,16},{16,0},{1,17},{17,1},{2,18},{18,2},{3,19},{19,3},{4,20},{20... | collective-permute-start | bytes 786440 | tf_op jit(solution)/shard_map/ppermute | solution.py:332
  2.3 0.8 %copy-start.1 = (f32[125,125]{1,0:T(8,128)S(1)}, f32[125,125]{1,0:T(8,128)}, u32[]{:S(2)}) copy-start(f32[125,125]{1,0:T(8,128)} %cell_ref.1) | copy-start | bytes 187504
  4.9 9.2 %collective-permute-start.2 = (f32[4,8,1024]{2,1,0:T(8,128)S(1)}, f32[4,8,1024]{2,1,0:T(8,128)S(1)}, u32[]{:S(2)}, u32[]{:S(2)}) collective-permute-start(f32[4,8,1024]{2,1,0:T(8,128)S(1)} %get-tuple-element.31), channel_id=1, source_target_pairs={{0,1},{2,3},{4,5},{6,7},{8,9},{10,11},{12,13},{14,15},{1,0},{3,2},... | collective-permute-start | bytes 393224 | tf_op jit(solution)/shard_map/ppermute | solution.py:326
  7.5 9.2 %collective-permute-start.3 = (f32[4,8,1024]{2,1,0:T(8,128)S(1)}, f32[4,8,1024]{2,1,0:T(8,128)S(1)}, u32[]{:S(2)}, u32[]{:S(2)}) collective-permute-start(f32[4,8,1024]{2,1,0:T(8,128)S(1)} %get-tuple-element.32), channel_id=1, source_target_pairs={{1,2},{3,4},{5,6},{7,8},{9,10},{11,12},{13,14},{15,0},{2,1},{4,3},... | collective-permute-start | bytes 393224 | tf_op jit(solution)/shard_map/ppermute | solution.py:325
  12.0 1.2 %collective-permute-start.1 = (f32[1,16,128]{2,1,0:T(8,128)S(1)}, f32[1,16,128]{2,1,0:T(8,128)S(1)}, u32[]{:S(2)}, u32[]{:S(2)}) collective-permute-start(f32[1,16,128]{2,1,0:T(8,128)S(1)} %bitcast.8), channel_id=1, source_target_pairs={{0,16},{16,0},{1,17},{17,1},{2,18},{18,2},{3,19},{19,3},{4,20},{20... | collective-permute-start | bytes 24584 | tf_op jit(solution)/shard_map/ppermute | solution.py:332
  17.6 15.9 %collective-permute-start.6 = (f32[4096,128]{1,0:T(8,128)S(1)}, f32[4096,128]{1,0:T(8,128)S(1)}, u32[]{:S(2)}, u32[]{:S(2)}) collective-permute-start(f32[4096,128]{1,0:T(8,128)S(1)} %widen.1.wide_ref), channel_id=1, source_target_pairs={{0,16},{16,0},{1,17},{17,1},{2,18},{18,2},{3,19},{19,3},{4,20},{20... | collective-permute-start | bytes 6291464 | tf_op jit(solution)/shard_map/ppermute | solution.py:332
  17.7 6.7 %collective-permute-start.4 = (f32[4,8,1024]{2,1,0:T(8,128)S(1)}, f32[4,8,1024]{2,1,0:T(8,128)S(1)}, u32[]{:S(2)}, u32[]{:S(2)}) collective-permute-start(f32[4,8,1024]{2,1,0:T(8,128)S(1)} %get-tuple-element.38), channel_id=1, source_target_pairs={{0,1},{2,3},{4,5},{6,7},{8,9},{10,11},{12,13},{14,15},{1,0},{3,2},... | collective-permute-start | bytes 393224 | tf_op jit(solution)/shard_map/ppermute | solution.py:326
  18.2 9.2 %collective-permute-start.5 = (f32[4,8,1024]{2,1,0:T(8,128)S(1)}, f32[4,8,1024]{2,1,0:T(8,128)S(1)}, u32[]{:S(2)}, u32[]{:S(2)}) collective-permute-start(f32[4,8,1024]{2,1,0:T(8,128)S(1)} %get-tuple-element.39), channel_id=1, source_target_pairs={{1,2},{3,4},{5,6},{7,8},{9,10},{11,12},{13,14},{15,0},{2,1},{4,3},... | collective-permute-start | bytes 393224 | tf_op jit(solution)/shard_map/ppermute | solution.py:325
  28.2 6.6 %collective-permute-start.7 = (f32[4,8,1024]{2,1,0:T(8,128)S(1)}, f32[4,8,1024]{2,1,0:T(8,128)S(1)}, u32[]{:S(2)}, u32[]{:S(2)}) collective-permute-start(f32[4,8,1024]{2,1,0:T(8,128)S(1)} %get-tuple-element.44), channel_id=1, source_target_pairs={{0,1},{2,3},{4,5},{6,7},{8,9},{10,11},{12,13},{14,15},{1,0},{3,2},... | collective-permute-start | bytes 393224 | tf_op jit(solution)/shard_map/ppermute | solution.py:326
  28.2 8.6 %collective-permute-start.8 = (f32[4,8,1024]{2,1,0:T(8,128)S(1)}, f32[4,8,1024]{2,1,0:T(8,128)S(1)}, u32[]{:S(2)}, u32[]{:S(2)}) collective-permute-start(f32[4,8,1024]{2,1,0:T(8,128)S(1)} %get-tuple-element.45), channel_id=1, source_target_pairs={{1,2},{3,4},{5,6},{7,8},{9,10},{11,12},{13,14},{15,0},{2,1},{4,3},... | collective-permute-start | bytes 393224 | tf_op jit(solution)/shard_map/ppermute | solution.py:325
  38.9 13.7 %collective-permute-start.9 = (f32[32,16,128]{2,1,0:T(8,128)S(1)}, f32[32,16,128]{2,1,0:T(8,128)S(1)}, u32[]{:S(2)}, u32[]{:S(2)}) collective-permute-start(f32[32,16,128]{2,1,0:T(8,128)S(1)} %get-tuple-element.50), channel_id=1, source_target_pairs={{0,16},{16,0},{1,17},{17,1},{2,18},{18,2},{3,19},{19,3},{4,20},{20... | collective-permute-start | bytes 786440 | tf_op jit(solution)/shard_map/ppermute | solution.py:332

commit v15 on v13

--- a/solution.py
+++ b/solution.py
@@ -88,14 +88,16 @@
     order_ref[...] = chosen(*order_ref.shape, functools.partial(cell_order_target, cells))
 
 
-def margin_rows_kernel(layer, parts_y, block_ref, out_ref, wide_ref):
+def margin_rows_kernel(layer, parts_y, groups, block_ref, out_ref, wide_ref, lines_ref):
     wide_ref[...] = block_ref[...].astype(f32)
     thickness = block_ref.shape[1]
     tile_cols = out_ref.shape[0] // parts_y
+    cols = tile_cols // groups
     for n in range(layer):
         for col in range(tile_cols):
             lines = wide_ref[pl.ds(col * layer + n, parts_y, stride=tile_cols * layer), :]
-            out_ref[pl.ds(col * parts_y, parts_y), pl.ds(n * thickness, thickness)] = lines.astype(bf16)
+            lines_ref[pl.ds(col // cols * cols * parts_y + col % cols, parts_y, stride=cols), :] = lines
+        out_ref[:, pl.ds(n * thickness, thickness)] = lines_ref[...].astype(bf16)
 
 
 def roll_cells(value, cells, forward):
@@ -149,18 +151,28 @@
         copy.wait()
 
 
-def to_cells_kernel(cells, parts_x, *refs):
-    part_refs = refs[:parts_x]
-    order_ref, edge_ref, low_ref, w_ref, pair_ref, other_ref = refs[parts_x:]
-    size = w_ref.shape[1]
-    group = lanes // cells
+def turned(part_ref, order_ref):
+    layer, thickness = part_ref.shape[1:]
+    group = lanes // (thickness // 4)
     sources = []
-    for start in range(0, part_refs[0].shape[0], group):
-        lines = [jnp.concatenate([ref[start + s] for ref in part_refs], 0) for s in range(group)]
-        sources += list(two_parts(jnp.concatenate(lines, 1)))
+    for start in range(0, part_ref.shape[0], group):
+        sources += list(two_parts(jnp.concatenate([part_ref[start + s] for s in range(group)], 1)))
     ordered = dot(jnp.concatenate(sources, 0), order_ref[...])
-    values = [ordered[start : start + size] + ordered[start + size : start + 2 * size] for start in range(0, ordered.shape[0], 2 * size)]
-    value = [jnp.concatenate([part[:, iz * lanes : (iz + 1) * lanes] for part in values], 1) for iz in range(4)]
+    starts = range(0, ordered.shape[0], 2 * layer)
+    values = [ordered[start : start + layer] + ordered[start + layer : start + 2 * layer] for start in starts]
+    return [jnp.concatenate([part[:, iz * lanes : (iz + 1) * lanes] for part in values], 1) for iz in range(4)]
+
+
+def turn_kernel(part_ref, order_ref, out_ref):
+    for iz, rows in enumerate(turned(part_ref, order_ref)):
+        out_ref[iz] = rows
+
+
+def to_cells_kernel(cells, own_ref, *refs):
+    part_refs = refs[:-6]
+    order_ref, edge_ref, low_ref, w_ref, pair_ref, other_ref = refs[-6:]
+    parts = [[own_ref[iz] for iz in range(4)]] + [turned(ref, order_ref) for ref in part_refs]
+    value = [jnp.concatenate([part[iz] for part in parts], 0) for iz in range(4)]
     for iz in range(4):
         w_ref[iz] = value[iz]
     send_edges(edge_ref, low_ref, value, pair_ref, other_ref, cells)
@@ -264,30 +276,35 @@
                 out_ref[h * group + s] = part[rows, s * thickness : (s + 1) * thickness]
 
 
-def margin_kernel(parts_x, parts_y, *refs):
-    part_refs, block_ref = refs[:parts_x], refs[parts_x]
-    tiles_ref, filtered_ref, sems = refs[parts_x + 1 :]
+def margin_kernel(parts_x, *refs):
+    part_refs, (block_ref, tiles_ref) = refs[:parts_x], refs[parts_x:]
     me = lax.axis_index("px")
     count, layer, thickness = part_refs[0].shape
-    owners = [lax.rem(me + (parts_x - step), parts_x) for step in range(parts_x)]
+    flat = [ref.reshape(count * layer, thickness) for ref in part_refs]
+    lines = [
+        jnp.concatenate([ref[pl.ds(n, count, stride=layer), :].astype(bf16) for ref in flat], 0)
+        for n in range(layer)
+    ]
+    product = lax.dot_general(
+        block_ref[...], jnp.concatenate(lines, 1), (((1,), (1,)), ((), ())), preferred_element_type=f32
+    )
+    group_rows = tiles_ref.shape[1]
+    starts = range(0, product.shape[0], group_rows)
+    for step in range(parts_x):
+        columns = slice(step * count, (step + 1) * count)
+        tiles = jnp.concatenate([product[start : start + group_rows, columns] for start in starts], 1)
+        tiles_ref[lax.rem(me + (parts_x - step), parts_x)] = tiles
+
+
+def join_kernel(parts_x, *refs):
+    part_refs, filtered_ref, sems = refs[:parts_x], refs[parts_x], refs[parts_x + 1]
+    me = lax.axis_index("px")
+    count = filtered_ref.shape[0] // parts_x
     copies = []
     for step, part_ref in enumerate(part_refs):
-        target = filtered_ref.at[pl.ds(owners[step] * count, count)]
-        copies.append(pltpu.make_async_copy(part_ref, target, sems.at[step]))
+        owner = lax.rem(me + (parts_x - step), parts_x)
+        copies.append(pltpu.make_async_copy(part_ref, filtered_ref.at[pl.ds(owner * count, count)], sems.at[step]))
     start_all(copies)
-    turned = [jnp.swapaxes(ref[...], 0, 1) for ref in part_refs]
-    lines = [jnp.concatenate([part[n] for part in turned], 0).astype(bf16) for n in range(layer)]
-    product = lax.dot_general(
-        block_ref[...], jnp.concatenate(lines, 1), (((1,), (1,)), ((), ())), preferred_element_type=f32
-    )
-    groups = tiles_ref.shape[2] // count
-    group_cols = tiles_ref.shape[1] // parts_y
-    for col in range(group_cols):
-        starts = [(group * group_cols + col) * parts_y for group in range(groups)]
-        for step in range(parts_x):
-            columns = slice(step * count, (step + 1) * count)
-            tiles = jnp.concatenate([product[start : start + parts_y, columns] for start in starts], 1)
-            tiles_ref[owners[step], pl.ds(col, parts_y, stride=group_cols), :] = tiles
     wait_all(copies)
 
 
@@ -364,10 +381,11 @@
         [cell_matrix],
         "assemble",
     )
+    own = kernel_call(turn_kernel, jax.ShapeDtypeStruct((4, layer, width), f32), [parts[0], order], "turn")
     field_now, *edges = kernel_call(
-        functools.partial(to_cells_kernel, cells, parts_x),
+        functools.partial(to_cells_kernel, cells),
         [field, message, message],
-        parts + [order, edge_matrix, low],
+        [own] + parts[1:] + [order, edge_matrix, low],
         "to_cells",
     )
     edges = swapped(edges)
@@ -386,11 +404,14 @@
         if step == 1:
             field_now, block = lax.optimization_barrier((field_now, block))
             ordered = kernel_call(
-                functools.partial(margin_rows_kernel, layer, parts_y),
+                functools.partial(margin_rows_kernel, layer, parts_y, groups),
                 jax.ShapeDtypeStruct((block_count, layer * thickness), bf16),
                 [block.reshape(block_count * layer, thickness)],
                 "margin_rows",
-                scratch=[pltpu.VMEM((block_count * layer, thickness), f32)],
+                scratch=[
+                    pltpu.VMEM((block_count * layer, thickness), f32),
+                    pltpu.VMEM((block_count, thickness), f32),
+                ],
             )
         operands = [field_now, levels, high, low, edge_matrix, place] + ([before] if step > 0 else [])
         inner, *back = kernel_call(
@@ -417,19 +438,23 @@
             )
     received = [pieces[0]] + [shifted(pieces[step], "px", step) for step in others]
 
-    tiles, filtered = kernel_call(
-        functools.partial(margin_kernel, parts_x, parts_y),
-        [
-            jax.ShapeDtypeStruct((parts_x, block_count // groups, groups * tile_rows), f32),
-            jax.ShapeDtypeStruct((states, layer, thickness), f32),
-        ],
+    tiles = kernel_call(
+        functools.partial(margin_kernel, parts_x),
+        jax.ShapeDtypeStruct((parts_x, block_count // groups, groups * tile_rows), f32),
         received + [ordered],
         "margin",
-        scratch=[pltpu.SemaphoreType.DMA((parts_x,))],
-        out_specs=[whole, anywhere],
     )
     tiles = tiles.reshape(parts_x * parts_y, tile_cols // groups, groups * tile_rows)
     tiles = lax.all_to_all(tiles, ("px", "py"), 0, 0, tiled=True)
+    filtered = kernel_call(
+        functools.partial(join_kernel, parts_x),
+        jax.ShapeDtypeStruct((states, layer, thickness), f32),
+        received,
+        "join",
+        scratch=[pltpu.SemaphoreType.DMA((parts_x,))],
+        out_specs=anywhere,
+    )
+    tiles, filtered = lax.optimization_barrier((tiles, filtered))
     margin = kernel_call(sum_kernel, jax.ShapeDtypeStruct((tile_cols, tile_rows), f32), [tiles], "tile_sum")
     return filtered.reshape(span.shape), margin.T
 

time: 51.4 us -> 51.6 us (level)
  blocking collectives: 11.2 us -> 0 us
  waiting for transfers between devices: 11.2 us -> 17.4 us
  starting transfers between devices: 15.3 us -> 19.2 us
  Pallas kernels: 11.7 us -> 12.9 us
    all_to_all x1 -> x0, blocking collectives: 11.2 us -> none  [local(): tiles = lax.all_to_all(tiles, ('px', 'py'), 0, 0, tiled=True)]
    all_to_all x0 -> x1, waiting for transfers between devices: none -> 6.49 us  [local(): tiles = lax.all_to_all(tiles, ('px', 'py'), 0, 0, tiled=True)]
    all_to_all x0 -> x1, starting transfers between devices: none -> 4.03 us  [local(): tiles = lax.all_to_all(tiles, ('px', 'py'), 0, 0, tiled=True)]
    pallas_call x12 -> x14, Pallas kernels: 11.7 us -> 12.9 us  [kernel_call(): pl.pallas_call(body, out_shape=outs, in_specs=in_specs or [whole] * len(o...]
  transfers between devices with their start and end apart: 9 -> 10, of which waited for: 9 -> 8; matrix products, arithmetic and copies ran while one was open for 0% -> 0% of each run, Pallas kernels for 13% -> 16%
where the time goes in v15:
time: 51.6 us; the launch traced here: 51.4 us
  starting transfers between devices  19.2 us (37%)
  waiting for transfers between devices  17.4 us (34%)
  Pallas kernels  12.9 us (25%)
  local copies, waits for them, and re-layouts  1.11 us (2%)
  between operations  0.75 us (1%)
    ppermute x3, starting transfers between devices, swapped(): other = lax.ppermute(other, 'py', others + [(b, a) for a, b in others])  14.5 us
    pallas_call x14, Pallas kernels, kernel_call(): pl.pallas_call(body, out_shape=outs, in_specs=in_specs or [whole] * len(o...  12.9 us
    ppermute x3, waiting for transfers between devices, swapped(): other = lax.ppermute(other, 'py', others + [(b, a) for a, b in others])  6.57 us
    all_to_all x1, waiting for transfers between devices, local(): tiles = lax.all_to_all(tiles, ('px', 'py'), 0, 0, tiled=True)  6.49 us
    all_to_all x1, starting transfers between devices, local(): tiles = lax.all_to_all(tiles, ('px', 'py'), 0, 0, tiled=True)  4.03 us
    ppermute x3, waiting for transfers between devices, shifted(): lax.ppermute(value, axis, [(source, (source + steps) % count) for source...  2.68 us
    ppermute x3, waiting for transfers between devices, swapped(): pair = lax.ppermute(pair, 'py', pairs + [(b, a) for a, b in pairs])  1.69 us
    dynamic_slice x1, local copies, waits for them, and re-layouts, part_for(): lax.dynamic_slice_in_dim(span_rows, lax.rem(me + step, parts_x) * mine, m...  1.1 us
  transfers between devices with their start and end apart: 10, of which 8 were waited for; matrix products, arithmetic and copies ran while one was open for 0% of the time, Pallas kernels for 16%

profile of v15, /device:TPU:0, one launch (start us, length us, event | category | flops | bytes accessed | tf_op | source)
XLA Modules:
  0.0 51.4 jit_solution(18134274600347707700)
XLA Ops:
  0.7 1.1 %constant_dynamic-slice_fusion = (f32[32,16,128]{2,1,0:T(8,128)S(1)}, f32[32,16,128]{2,1,0:T(8,128)S(1)}) fusion(f32[64,16,128]{2,1,0:T(8,128)} %bitcast.9, s32[]{:T(128)S(6)} %select_n.7, s32[]{:T(128)S(6)} %select_n.6), kind=kLoop, calls=%fused_computation | loop fusion | bytes 1048584 | tf_op jit(solution)/shard_map/dynamic_slice | solution.py:375
  2.3 1.0 %assemble.1 = (bf16[208,208]{1,0:T(8,128)(2,1)S(1)}, bf16[208,208]{1,0:T(8,128)(2,1)S(1)}, bf16[80,160]{1,0:T(8,128)(2,1)S(1)}, bf16[160,208]{1,0:T(8,128)(2,1)S...) custom-call(f32[125,125]{1,0:T(8,128)S(1)} %copy-done.1), custom_call_target="tpu_custom_call" | custom-call | tf_op jit(solution)/shard_map/assemble/pallas_call | solution.py:335
  3.6 0.7 %to_cells.1 = (f32[4,32,1024]{2,1,0:T(8,128)S(1)}, f32[4,8,1024]{2,1,0:T(8,128)S(1)}, f32[4,8,1024]{2,1,0:T(8,128)S(1)}) custom-call(f32[4,16,1024]{2,1,0:T(8,128)S(1)} %turn.1.own_ref, f32[32,16,128]{2,1,0:T(8,128)S(1)} %collective-permute-done.refs_0_, bf16[512,512]{1,0:T(8,128)(2,1)S(1)} %get-tuple-element.27.order_ref.refs_1_, ...), custom_call_target="tpu_custom_call" | custom-call | tf_op jit(solution)/shard_map/to_cells/pallas_call | solution.py:335
  4.3 6.8 %collective-permute-start.2 = (f32[4,8,1024]{2,1,0:T(8,128)S(1)}, f32[4,8,1024]{2,1,0:T(8,128)S(1)}, u32[]{:S(2)}, u32[]{:S(2)}) collective-permute-start(f32[4,8,1024]{2,1,0:T(8,128)S(1)} %get-tuple-element.33), channel_id=1, source_target_pairs={{1,2},{3,4},{5,6},{7,8},{9,10},{11,12},{13,14},{15,0},{2,1},{4,3},... | collective-permute-start | bytes 393224 | tf_op jit(solution)/shard_map/ppermute | solution.py:323
  11.1 1.2 %collective-permute-done.1.refs_1_ = f32[16,128]{1,0:T(8,128)S(1)} collective-permute-done((f32[16,128]{1,0:T(8,128)S(1)}, f32[16,128]{1,0:T(8,128)S(1)}, u32[]{:S(2)}, u32[]{:S(2)}) %collective-permute-start.1) | collective-permute-done | bytes 8224 | tf_op jit(solution)/shard_map/ppermute | solution.py:330
  12.4 1.3 %inner.3.inner_ref = f32[4,32,1024]{2,1,0:T(8,128)S(1)} custom-call(f32[4,32,1024]{2,1,0:T(8,128)S(1)} %get-tuple-element.30.refs_0_.refs_6_, f32[4,32,128]{2,1,0:T(8,128)S(1)} %levels.1.refs_1_, bf16[208,208]{1,0:T(8,128)(2,1)S(1)} %get-tuple-element.31.refs_2_, bf16[208,208]{1,0:T(8,128)(2,1)S(1)} %get-tuple-element.29.refs_3_.low_ref, ...), custom_call_target="tpu_custom_call" | custom-call | tf_op jit(solution)/shard_map/inner/pallas_call | solution.py:335
  13.7 1.4 %collective-permute-done.2.from_other_ref = f32[4,8,1024]{2,1,0:T(8,128)S(1)} collective-permute-done((f32[4,8,1024]{2,1,0:T(8,128)S(1)}, f32[4,8,1024]{2,1,0:T(8,128)S(1)}, u32[]{:S(2)}, u32[]{:S(2)}) %collective-permute-start.2) | collective-permute-done | bytes 131104 | tf_op jit(solution)/shard_map/ppermute | solution.py:323
  15.1 1.4 %collective-permute-done.3.from_pair_ref = f32[4,8,1024]{2,1,0:T(8,128)S(1)} collective-permute-done((f32[4,8,1024]{2,1,0:T(8,128)S(1)}, f32[4,8,1024]{2,1,0:T(8,128)S(1)}, u32[]{:S(2)}, u32[]{:S(2)}) %collective-permute-start.3) | collective-permute-done | bytes 131104 | tf_op jit(solution)/shard_map/ppermute | solution.py:324
  16.5 0.8 %finish.2 = (f32[4,32,1024]{2,1,0:T(8,128)S(1)}, f32[4,8,1024]{2,1,0:T(8,128)S(1)}, f32[4,8,1024]{2,1,0:T(8,128)S(1)}) custom-call(f32[4,32,1024]{2,1,0:T(8,128)S(1)} %inner.3.inner_ref, f32[4,8,1024]{2,1,0:T(8,128)S(1)} %collective-permute-done.2.from_other_ref, f32[4,8,1024]{2,1,0:T(8,128)S(1)} %collective-permute-done.3.from_pair_ref, ...), custom_call_target="tpu_custom_call" | custom-call | tf_op jit(solution)/shard_map/finish/pallas_call | solution.py:335
  17.3 4.1 %collective-permute-start.4 = (f32[4,8,1024]{2,1,0:T(8,128)S(1)}, f32[4,8,1024]{2,1,0:T(8,128)S(1)}, u32[]{:S(2)}, u32[]{:S(2)}) collective-permute-start(f32[4,8,1024]{2,1,0:T(8,128)S(1)} %get-tuple-element.38), channel_id=1, source_target_pairs={{1,2},{3,4},{5,6},{7,8},{9,10},{11,12},{13,14},{15,0},{2,1},{4,3},... | collective-permute-start | bytes 393224 | tf_op jit(solution)/shard_map/ppermute | solution.py:323
  21.3 1.3 %inner.4.inner_ref = f32[4,32,1024]{2,1,0:T(8,128)S(1)} custom-call(f32[4,32,1024]{2,1,0:T(8,128)S(1)} %get-tuple-element.37.refs_0_.refs_6_, f32[4,32,128]{2,1,0:T(8,128)S(1)} %levels.1.refs_1_, bf16[208,208]{1,0:T(8,128)(2,1)S(1)} %get-tuple-element.31.refs_2_, bf16[208,208]{1,0:T(8,128)(2,1)S(1)} %get-tuple-element.29.refs_3_.low_ref, ...), custom_call_target="tpu_custom_call" | custom-call | tf_op jit(solution)/shard_map/inner/pallas_call | solution.py:335
  22.6 3.3 %collective-permute-done.4.from_other_ref = f32[4,8,1024]{2,1,0:T(8,128)S(1)} collective-permute-done((f32[4,8,1024]{2,1,0:T(8,128)S(1)}, f32[4,8,1024]{2,1,0:T(8,128)S(1)}, u32[]{:S(2)}, u32[]{:S(2)}) %collective-permute-start.4) | collective-permute-done | bytes 131104 | tf_op jit(solution)/shard_map/ppermute | solution.py:323
  26.3 0.8 %finish.3 = (f32[4,32,1024]{2,1,0:T(8,128)S(1)}, f32[4,8,1024]{2,1,0:T(8,128)S(1)}, f32[4,8,1024]{2,1,0:T(8,128)S(1)}) custom-call(f32[4,32,1024]{2,1,0:T(8,128)S(1)} %inner.4.inner_ref, f32[4,8,1024]{2,1,0:T(8,128)S(1)} %collective-permute-done.4.from_other_ref, f32[4,8,1024]{2,1,0:T(8,128)S(1)} %collective-permute-done.5.from_pair_ref, ...), custom_call_target="tpu_custom_call" | custom-call | tf_op jit(solution)/shard_map/finish/pallas_call | solution.py:335
  27.1 3.7 %collective-permute-start.6 = (f32[4,8,1024]{2,1,0:T(8,128)S(1)}, f32[4,8,1024]{2,1,0:T(8,128)S(1)}, u32[]{:S(2)}, u32[]{:S(2)}) collective-permute-start(f32[4,8,1024]{2,1,0:T(8,128)S(1)} %get-tuple-element.44), channel_id=1, source_target_pairs={{1,2},{3,4},{5,6},{7,8},{9,10},{11,12},{13,14},{15,0},{2,1},{4,3},... | collective-permute-start | bytes 393224 | tf_op jit(solution)/shard_map/ppermute | solution.py:323
  30.8 1.6 %margin_rows.1.refs_2_ = bf16[256,2048]{1,0:T(8,128)(2,1)S(1)} custom-call(bf16[4096,128]{1,0:T(8,128)(2,1)S(1)} %bitcast.6), custom_call_target="tpu_custom_call" | custom-call | tf_op jit(solution)/shard_map/margin_rows/pallas_call | solution.py:335
  32.4 1.5 %inner.5 = (f32[4,32,1024]{2,1,0:T(8,128)S(1)}, bf16[512,512]{1,0:T(8,128)(2,1)S(1)}) custom-call(f32[4,32,1024]{2,1,0:T(8,128)S(1)} %get-tuple-element.40.refs_0_, f32[4,32,128]{2,1,0:T(8,128)S(1)} %levels.1.refs_1_, bf16[208,208]{1,0:T(8,128)(2,1)S(1)} %get-tuple-element.31.refs_2_, bf16[208,208]{1,0:T(8,128)(2,1)S(1)} %get-tuple-element.29.refs_3_.low_ref, ...), custom_call_target="tpu_custom_call" | custom-call | tf_op jit(solution)/shard_map/inner/pallas_call | solution.py:335
  34.0 1.8 %collective-permute-done.6.refs_1_ = f32[4,8,1024]{2,1,0:T(8,128)S(1)} collective-permute-done((f32[4,8,1024]{2,1,0:T(8,128)S(1)}, f32[4,8,1024]{2,1,0:T(8,128)S(1)}, u32[]{:S(2)}, u32[]{:S(2)}) %collective-permute-start.6) | collective-permute-done | bytes 131104 | tf_op jit(solution)/shard_map/ppermute | solution.py:323
  35.8 0.8 %from_cells.1 = (f32[32,16,128]{2,1,0:T(8,128)S(1)}, f32[32,16,128]{2,1,0:T(8,128)S(1)}) custom-call(f32[4,32,1024]{2,1,0:T(8,128)S(1)} %get-tuple-element.43.refs_0_, f32[4,8,1024]{2,1,0:T(8,128)S(1)} %collective-permute-done.6.refs_1_, f32[4,8,1024]{2,1,0:T(8,128)S(1)} %collective-permute-done.7.refs_2_, ...), custom_call_target="tpu_custom_call" | custom-call | tf_op jit(solution)/shard_map/from_cells/pallas_call | solution.py:335
  36.7 1.5 %collective-permute-done.8.refs_1_ = f32[32,16,128]{2,1,0:T(8,128)S(1)} collective-permute-done((f32[32,16,128]{2,1,0:T(8,128)S(1)}, f32[32,16,128]{2,1,0:T(8,128)S(1)}, u32[]{:S(2)}, u32[]{:S(2)}) %collective-permute-start.8) | collective-permute-done | bytes 262176 | tf_op jit(solution)/shard_map/ppermute | solution.py:330
  38.2 1.1 %margin.1 = f32[2,64,128]{2,1,0:T(8,128)} custom-call(f32[32,16,128]{2,1,0:T(8,128)S(1)} %get-tuple-element.47.refs_0_, f32[32,16,128]{2,1,0:T(8,128)S(1)} %collective-permute-done.8.refs_1_, bf16[256,2048]{1,0:T(8,128)(2,1)S(1)} %margin_rows.1.refs_2_), custom_call_target="tpu_custom_call" | custom-call | tf_op jit(solution)/shard_map/margin/pallas_call | solution.py:335
  39.3 4.0 %all-to-all-start = ((f32[32,4,128]{2,1,0:T(4,128)}), f32[32,4,128]{2,1,0:T(4,128)S(1)}, u32[]{:S(2)}, u32[]{:S(2)}) async-start(f32[32,4,128]{2,1,0:T(4,128)} %bitcast.3), calls=%async_computation | async-start | bytes 131072 | tf_op jit(solution)/shard_map/all_to_all | solution.py:448
  43.4 0.8 %join.1 = f32[64,16,128]{2,1,0:T(8,128)} custom-call(f32[32,16,128]{2,1,0:T(8,128)S(1)} %get-tuple-element.47.refs_0_, f32[32,16,128]{2,1,0:T(8,128)S(1)} %collective-permute-done.8.refs_1_), custom_call_target="tpu_custom_call" | custom-call | tf_op jit(solution)/shard_map/join/pallas_call | solution.py:335
  44.2 6.5 %all-to-all-done.tiles_ref = f32[32,4,128]{2,1,0:T(4,128)S(1)} async-done(((f32[32,4,128]{2,1,0:T(4,128)}), f32[32,4,128]{2,1,0:T(4,128)S(1)}, u32[]{:S(2)}, u32[]{:S(2)}) %all-to-all-start) | async-done | bytes 65568 | tf_op jit(solution)/shard_map/all_to_all | solution.py:448
  50.7 0.7 %tile_sum.1 = f32[16,32]{1,0:T(8,128)} custom-call(f32[32,4,128]{2,1,0:T(4,128)S(1)} %all-to-all-done.tiles_ref), custom_call_target="tpu_custom_call" | custom-call | tf_op jit(solution)/shard_map/tile_sum/pallas_call | solution.py:335
  (17 shorter events, 1.4 us)
Async XLA Ops:
  0.6 1.6 %copy-start.1 = (f32[125,125]{1,0:T(8,128)S(1)}, f32[125,125]{1,0:T(8,128)}, u32[]{:S(2)}) copy-start(f32[125,125]{1,0:T(8,128)} %cell_ref.1) | copy-start | bytes 187504
  1.8 1.8 %collective-permute-start = (f32[32,16,128]{2,1,0:T(8,128)S(1)}, f32[32,16,128]{2,1,0:T(8,128)S(1)}, u32[]{:S(2)}, u32[]{:S(2)}) collective-permute-start(f32[32,16,128]{2,1,0:T(8,128)S(1)} %get-tuple-element.52), channel_id=1, source_target_pairs={{0,16},{16,0},{1,17},{17,1},{2,18},{18,2},{3,19},{19,3},{4,20},{20... | collective-permute-start | bytes 786440 | tf_op jit(solution)/shard_map/ppermute | solution.py:330
  3.6 7.5 %copy-start.2 = (f32[4,4,128]{2,1,0:T(4,128)S(1)}, f32[4,4,128]{2,1,0:T(4,128)}, u32[]{:S(2)}) copy-start(f32[4,4,128]{2,1,0:T(4,128)} %param.5) | copy-start | bytes 24580
  4.3 10.8 %collective-permute-start.2 = (f32[4,8,1024]{2,1,0:T(8,128)S(1)}, f32[4,8,1024]{2,1,0:T(8,128)S(1)}, u32[]{:S(2)}, u32[]{:S(2)}) collective-permute-start(f32[4,8,1024]{2,1,0:T(8,128)S(1)} %get-tuple-element.33), channel_id=1, source_target_pairs={{1,2},{3,4},{5,6},{7,8},{9,10},{11,12},{13,14},{15,0},{2,1},{4,3},... | collective-permute-start | bytes 393224 | tf_op jit(solution)/shard_map/ppermute | solution.py:323
  11.0 5.4 %collective-permute-start.3 = (f32[4,8,1024]{2,1,0:T(8,128)S(1)}, f32[4,8,1024]{2,1,0:T(8,128)S(1)}, u32[]{:S(2)}, u32[]{:S(2)}) collective-permute-start(f32[4,8,1024]{2,1,0:T(8,128)S(1)} %get-tuple-element.34), channel_id=1, source_target_pairs={{0,1},{2,3},{4,5},{6,7},{8,9},{10,11},{12,13},{14,15},{1,0},{3,2},... | collective-permute-start | bytes 393224 | tf_op jit(solution)/shard_map/ppermute | solution.py:324
  11.1 1.2 %collective-permute-start.1 = (f32[16,128]{1,0:T(8,128)S(1)}, f32[16,128]{1,0:T(8,128)S(1)}, u32[]{:S(2)}, u32[]{:S(2)}) collective-permute-start(f32[16,128]{1,0:T(8,128)S(1)} %bitcast.7), channel_id=1, source_target_pairs={{0,16},{16,0},{1,17},{17,1},{2,18},{18,2},{3,19},{19,3},{4,20},{20... | collective-permute-start | bytes 24584 | tf_op jit(solution)/shard_map/ppermute | solution.py:330
  17.3 8.7 %collective-permute-start.4 = (f32[4,8,1024]{2,1,0:T(8,128)S(1)}, f32[4,8,1024]{2,1,0:T(8,128)S(1)}, u32[]{:S(2)}, u32[]{:S(2)}) collective-permute-start(f32[4,8,1024]{2,1,0:T(8,128)S(1)} %get-tuple-element.38), channel_id=1, source_target_pairs={{1,2},{3,4},{5,6},{7,8},{9,10},{11,12},{13,14},{15,0},{2,1},{4,3},... | collective-permute-start | bytes 393224 | tf_op jit(solution)/shard_map/ppermute | solution.py:323
  21.3 5.0 %collective-permute-start.5 = (f32[4,8,1024]{2,1,0:T(8,128)S(1)}, f32[4,8,1024]{2,1,0:T(8,128)S(1)}, u32[]{:S(2)}, u32[]{:S(2)}) collective-permute-start(f32[4,8,1024]{2,1,0:T(8,128)S(1)} %get-tuple-element.39), channel_id=1, source_target_pairs={{0,1},{2,3},{4,5},{6,7},{8,9},{10,11},{12,13},{14,15},{1,0},{3,2},... | collective-permute-start | bytes 393224 | tf_op jit(solution)/shard_map/ppermute | solution.py:324
  21.3 9.5 %copy-start = (bf16[256,4,4,128]{3,2,1,0:T(4,128)(2,1)S(1)}, bf16[256,4,4,128]{3,2,1,0:T(4,128)(2,1)}, u32[]{:S(2)}) copy-start(bf16[256,4,4,128]{3,2,1,0:T(4,128)(2,1)} %param.7) | copy-start | bytes 3145732
  27.1 8.7 %collective-permute-start.6 = (f32[4,8,1024]{2,1,0:T(8,128)S(1)}, f32[4,8,1024]{2,1,0:T(8,128)S(1)}, u32[]{:S(2)}, u32[]{:S(2)}) collective-permute-start(f32[4,8,1024]{2,1,0:T(8,128)S(1)} %get-tuple-element.44), channel_id=1, source_target_pairs={{1,2},{3,4},{5,6},{7,8},{9,10},{11,12},{13,14},{15,0},{2,1},{4,3},... | collective-permute-start | bytes 393224 | tf_op jit(solution)/shard_map/ppermute | solution.py:323
  30.8 5.0 %collective-permute-start.7 = (f32[4,8,1024]{2,1,0:T(8,128)S(1)}, f32[4,8,1024]{2,1,0:T(8,128)S(1)}, u32[]{:S(2)}, u32[]{:S(2)}) collective-permute-start(f32[4,8,1024]{2,1,0:T(8,128)S(1)} %get-tuple-element.45), channel_id=1, source_target_pairs={{0,1},{2,3},{4,5},{6,7},{8,9},{10,11},{12,13},{14,15},{1,0},{3,2},... | collective-permute-start | bytes 393224 | tf_op jit(solution)/shard_map/ppermute | solution.py:324
  36.6 1.6 %collective-permute-start.8 = (f32[32,16,128]{2,1,0:T(8,128)S(1)}, f32[32,16,128]{2,1,0:T(8,128)S(1)}, u32[]{:S(2)}, u32[]{:S(2)}) collective-permute-start(f32[32,16,128]{2,1,0:T(8,128)S(1)} %get-tuple-element.48), channel_id=1, source_target_pairs={{0,16},{16,0},{1,17},{17,1},{2,18},{18,2},{3,19},{19,3},{4,20},{20... | collective-permute-start | bytes 786440 | tf_op jit(solution)/shard_map/ppermute | solution.py:330
  39.3 11.4 %all-to-all-start = ((f32[32,4,128]{2,1,0:T(4,128)}), f32[32,4,128]{2,1,0:T(4,128)S(1)}, u32[]{:S(2)}, u32[]{:S(2)}) async-start(f32[32,4,128]{2,1,0:T(4,128)} %bitcast.3), calls=%async_computation | async-start | bytes 131072 | tf_op jit(solution)/shard_map/all_to_all | solution.py:448

commit v16 on v15

--- a/solution.py
+++ b/solution.py
@@ -151,27 +151,28 @@
         copy.wait()
 
 
-def turned(part_ref, order_ref):
+def turned(part_ref, order_ref, count):
     layer, thickness = part_ref.shape[1:]
     group = lanes // (thickness // 4)
+    first = 0 if part_ref.shape[0] == count else lax.axis_index("px") * count
     sources = []
-    for start in range(0, part_ref.shape[0], group):
-        sources += list(two_parts(jnp.concatenate([part_ref[start + s] for s in range(group)], 1)))
+    for start in range(0, count, group):
+        sources += list(two_parts(jnp.concatenate([part_ref[first + start + s] for s in range(group)], 1)))
     ordered = dot(jnp.concatenate(sources, 0), order_ref[...])
     starts = range(0, ordered.shape[0], 2 * layer)
     values = [ordered[start : start + layer] + ordered[start + layer : start + 2 * layer] for start in starts]
     return [jnp.concatenate([part[:, iz * lanes : (iz + 1) * lanes] for part in values], 1) for iz in range(4)]
 
 
-def turn_kernel(part_ref, order_ref, out_ref):
-    for iz, rows in enumerate(turned(part_ref, order_ref)):
+def turn_kernel(count, part_ref, order_ref, out_ref):
+    for iz, rows in enumerate(turned(part_ref, order_ref, count)):
         out_ref[iz] = rows
 
 
-def to_cells_kernel(cells, own_ref, *refs):
+def to_cells_kernel(cells, count, own_ref, *refs):
     part_refs = refs[:-6]
     order_ref, edge_ref, low_ref, w_ref, pair_ref, other_ref = refs[-6:]
-    parts = [[own_ref[iz] for iz in range(4)]] + [turned(ref, order_ref) for ref in part_refs]
+    parts = [[own_ref[iz] for iz in range(4)]] + [turned(ref, order_ref, count) for ref in part_refs]
     value = [jnp.concatenate([part[iz] for part in parts], 0) for iz in range(4)]
     for iz in range(4):
         w_ref[iz] = value[iz]
@@ -277,9 +278,16 @@
 
 
 def margin_kernel(parts_x, *refs):
-    part_refs, (block_ref, tiles_ref) = refs[:parts_x], refs[parts_x:]
+    part_refs, block_ref = refs[:parts_x], refs[parts_x]
+    tiles_ref, filtered_ref, sems = refs[parts_x + 1 :]
     me = lax.axis_index("px")
     count, layer, thickness = part_refs[0].shape
+    owners = [lax.rem(me + (parts_x - step), parts_x) for step in range(parts_x)]
+    copies = []
+    for step, part_ref in enumerate(part_refs):
+        target = filtered_ref.at[pl.ds(owners[step] * count, count)]
+        copies.append(pltpu.make_async_copy(part_ref, target, sems.at[step]))
+    start_all(copies)
     flat = [ref.reshape(count * layer, thickness) for ref in part_refs]
     lines = [
         jnp.concatenate([ref[pl.ds(n, count, stride=layer), :].astype(bf16) for ref in flat], 0)
@@ -293,18 +301,7 @@
     for step in range(parts_x):
         columns = slice(step * count, (step + 1) * count)
         tiles = jnp.concatenate([product[start : start + group_rows, columns] for start in starts], 1)
-        tiles_ref[lax.rem(me + (parts_x - step), parts_x)] = tiles
-
-
-def join_kernel(parts_x, *refs):
-    part_refs, filtered_ref, sems = refs[:parts_x], refs[parts_x], refs[parts_x + 1]
-    me = lax.axis_index("px")
-    count = filtered_ref.shape[0] // parts_x
-    copies = []
-    for step, part_ref in enumerate(part_refs):
-        owner = lax.rem(me + (parts_x - step), parts_x)
-        copies.append(pltpu.make_async_copy(part_ref, filtered_ref.at[pl.ds(owner * count, count)], sems.at[step]))
-    start_all(copies)
+        tiles_ref[owners[step]] = tiles
     wait_all(copies)
 
 
@@ -374,16 +371,19 @@
     def part_for(step):
         return lax.dynamic_slice_in_dim(span_rows, lax.rem(me + step, parts_x) * mine, mine, 0)
 
-    parts = [part_for(0)] + [shifted(part_for(step), "px", step) for step in reversed(others)]
+    if parts_x == 2:
+        parts = [span_rows, shifted(span_rows, "px", 1)]
+    else:
+        parts = [part_for(0)] + [shifted(part_for(step), "px", step) for step in reversed(others)]
     high, low, edge_matrix, halo_matrix, place, order = kernel_call(
         functools.partial(matrix_kernel, cells, nodes),
         [matrix, matrix, edge_shape, from_halo, place_shape, table],
         [cell_matrix],
         "assemble",
     )
-    own = kernel_call(turn_kernel, jax.ShapeDtypeStruct((4, layer, width), f32), [parts[0], order], "turn")
+    own = kernel_call(functools.partial(turn_kernel, mine), jax.ShapeDtypeStruct((4, layer, width), f32), [parts[0], order], "turn")
     field_now, *edges = kernel_call(
-        functools.partial(to_cells_kernel, cells),
+        functools.partial(to_cells_kernel, cells, mine),
         [field, message, message],
         [own] + parts[1:] + [order, edge_matrix, low],
         "to_cells",
@@ -438,23 +438,19 @@
             )
     received = [pieces[0]] + [shifted(pieces[step], "px", step) for step in others]
 
-    tiles = kernel_call(
+    tiles, filtered = kernel_call(
         functools.partial(margin_kernel, parts_x),
-        jax.ShapeDtypeStruct((parts_x, block_count // groups, groups * tile_rows), f32),
+        [
+            jax.ShapeDtypeStruct((parts_x, block_count // groups, groups * tile_rows), f32),
+            jax.ShapeDtypeStruct((states, layer, thickness), f32),
+        ],
         received + [ordered],
         "margin",
+        scratch=[pltpu.SemaphoreType.DMA((parts_x,))],
+        out_specs=[whole, anywhere],
     )
     tiles = tiles.reshape(parts_x * parts_y, tile_cols // groups, groups * tile_rows)
     tiles = lax.all_to_all(tiles, ("px", "py"), 0, 0, tiled=True)
-    filtered = kernel_call(
-        functools.partial(join_kernel, parts_x),
-        jax.ShapeDtypeStruct((states, layer, thickness), f32),
-        received,
-        "join",
-        scratch=[pltpu.SemaphoreType.DMA((parts_x,))],
-        out_specs=anywhere,
-    )
-    tiles, filtered = lax.optimization_barrier((tiles, filtered))
     margin = kernel_call(sum_kernel, jax.ShapeDtypeStruct((tile_cols, tile_rows), f32), [tiles], "tile_sum")
     return filtered.reshape(span.shape), margin.T
 

time: 51.6 us -> 52 us (level)
  blocking collectives: 0 us -> 11.2 us
  waiting for transfers between devices: 17.4 us -> 10.9 us
  starting transfers between devices: 19.2 us -> 15.2 us
  Pallas kernels: 12.9 us -> 11.9 us
  local copies, waits for them, and re-layouts: 1.11 us -> 1.89 us
    all_to_all x0 -> x1, blocking collectives: none -> 11.2 us  [local(): tiles = lax.all_to_all(tiles, ('px', 'py'), 0, 0, tiled=True)]
    all_to_all x1 -> x0, waiting for transfers between devices: 6.49 us -> none  [local(): tiles = lax.all_to_all(tiles, ('px', 'py'), 0, 0, tiled=True)]
    all_to_all x1 -> x0, starting transfers between devices: 4.03 us -> none  [local(): tiles = lax.all_to_all(tiles, ('px', 'py'), 0, 0, tiled=True)]
    unnamed x6 -> x8, local copies, waits for them, and re-layouts: 0.01 us -> 1.89 us
    dynamic_slice x1 -> x0, local copies, waits for them, and re-layouts: 1.1 us -> none  [part_for(): lax.dynamic_slice_in_dim(span_rows, lax.rem(me + step, parts_x) * mine, m...]
    pallas_call x14 -> x13, Pallas kernels: 12.9 us -> 11.9 us  [kernel_call(): pl.pallas_call(body, out_shape=outs, in_specs=in_specs or [whole] * len(o...]
  transfers between devices with their start and end apart: 10 -> 9, of which waited for: 8 -> 8; matrix products, arithmetic and copies ran while one was open for 0% -> 0% of each run, Pallas kernels for 16% -> 14%
where the time goes in v16:
time: 52 us; the launch traced here: 51.8 us
  starting transfers between devices  15.2 us (29%)
  Pallas kernels  11.9 us (23%)
  blocking collectives  11.2 us (22%)
  waiting for transfers between devices  10.9 us (21%)
  local copies, waits for them, and re-layouts  1.89 us (4%)
  between operations  0.72 us (1%)
    ppermute x3, starting transfers between devices, swapped(): other = lax.ppermute(other, 'py', others + [(b, a) for a, b in others])  14.4 us
    pallas_call x13, Pallas kernels, kernel_call(): pl.pallas_call(body, out_shape=outs, in_specs=in_specs or [whole] * len(o...  11.9 us
    all_to_all x1, blocking collectives, local(): tiles = lax.all_to_all(tiles, ('px', 'py'), 0, 0, tiled=True)  11.2 us
    ppermute x3, waiting for transfers between devices, swapped(): other = lax.ppermute(other, 'py', others + [(b, a) for a, b in others])  6.68 us
    ppermute x3, waiting for transfers between devices, shifted(): lax.ppermute(value, axis, [(source, (source + steps) % count) for source...  2.48 us
    unnamed x8, local copies, waits for them, and re-layouts  1.89 us
    ppermute x3, waiting for transfers between devices, swapped(): pair = lax.ppermute(pair, 'py', pairs + [(b, a) for a, b in pairs])  1.74 us
  transfers between devices with their start and end apart: 9, of which 8 were waited for; matrix products, arithmetic and copies ran while one was open for 0% of the time, Pallas kernels for 14%

profile of v16, /device:TPU:0, one launch (start us, length us, event | category | flops | bytes accessed | tf_op | source)
XLA Modules:
  0.0 51.8 jit_solution(5981470395779208554)
XLA Ops:
  0.6 0.5 collective-permute-start
  1.1 0.8 %copy-done.2 = f32[125,125]{1,0:T(8,128)S(1)} copy-done((f32[125,125]{1,0:T(8,128)S(1)}, f32[125,125]{1,0:T(8,128)}, u32[]{:S(2)}) %copy-start.2) | copy-done | bytes 62524
  2.0 1.0 %assemble.1 = (bf16[208,208]{1,0:T(8,128)(2,1)S(1)}, bf16[208,208]{1,0:T(8,128)(2,1)S(1)}, bf16[80,160]{1,0:T(8,128)(2,1)S(1)}, bf16[160,208]{1,0:T(8,128)(2,1)S...) custom-call(f32[125,125]{1,0:T(8,128)S(1)} %copy-done.2), custom_call_target="tpu_custom_call" | custom-call | tf_op jit(solution)/shard_map/assemble/pallas_call | solution.py:332
  3.0 1.0 %copy-done.1 = f32[64,4,4,128]{3,2,1,0:T(4,128)S(1)} copy-done((f32[64,4,4,128]{3,2,1,0:T(4,128)S(1)}, f32[64,4,4,128]{3,2,1,0:T(4,128)}, u32[]{:S(2)}) %copy-start.1) | copy-done | bytes 524312
  4.4 0.7 %to_cells.1 = (f32[4,32,1024]{2,1,0:T(8,128)S(1)}, f32[4,8,1024]{2,1,0:T(8,128)S(1)}, f32[4,8,1024]{2,1,0:T(8,128)S(1)}) custom-call(f32[4,16,1024]{2,1,0:T(8,128)S(1)} %turn.1.own_ref, f32[64,16,128]{2,1,0:T(8,128)S(1)} %collective-permute-done.refs_0_, bf16[512,512]{1,0:T(8,128)(2,1)S(1)} %get-tuple-element.27.order_ref.refs_1_, ...), custom_call_target="tpu_custom_call" | custom-call | tf_op jit(solution)/shard_map/to_cells/pallas_call | solution.py:332
  5.0 6.6 %collective-permute-start.2 = (f32[4,8,1024]{2,1,0:T(8,128)S(1)}, f32[4,8,1024]{2,1,0:T(8,128)S(1)}, u32[]{:S(2)}, u32[]{:S(2)}) collective-permute-start(f32[4,8,1024]{2,1,0:T(8,128)S(1)} %get-tuple-element.33), channel_id=1, source_target_pairs={{1,2},{3,4},{5,6},{7,8},{9,10},{11,12},{13,14},{15,0},{2,1},{4,3},... | collective-permute-start | bytes 393224 | tf_op jit(solution)/shard_map/ppermute | solution.py:320
  11.8 1.0 %collective-permute-done.1.refs_1_ = f32[16,128]{1,0:T(8,128)S(1)} collective-permute-done((f32[16,128]{1,0:T(8,128)S(1)}, f32[16,128]{1,0:T(8,128)S(1)}, u32[]{:S(2)}, u32[]{:S(2)}) %collective-permute-start.1) | collective-permute-done | bytes 8224 | tf_op jit(solution)/shard_map/ppermute | solution.py:327
  13.0 1.3 %inner.3.inner_ref = f32[4,32,1024]{2,1,0:T(8,128)S(1)} custom-call(f32[4,32,1024]{2,1,0:T(8,128)S(1)} %get-tuple-element.30.refs_0_.refs_6_, f32[4,32,128]{2,1,0:T(8,128)S(1)} %levels.1.refs_1_, bf16[208,208]{1,0:T(8,128)(2,1)S(1)} %get-tuple-element.31.refs_2_, bf16[208,208]{1,0:T(8,128)(2,1)S(1)} %get-tuple-element.29.refs_3_.low_ref, ...), custom_call_target="tpu_custom_call" | custom-call | tf_op jit(solution)/shard_map/inner/pallas_call | solution.py:332
  14.3 1.6 %collective-permute-done.2.from_other_ref = f32[4,8,1024]{2,1,0:T(8,128)S(1)} collective-permute-done((f32[4,8,1024]{2,1,0:T(8,128)S(1)}, f32[4,8,1024]{2,1,0:T(8,128)S(1)}, u32[]{:S(2)}, u32[]{:S(2)}) %collective-permute-start.2) | collective-permute-done | bytes 131104 | tf_op jit(solution)/shard_map/ppermute | solution.py:320
  15.9 1.4 %collective-permute-done.3.from_pair_ref = f32[4,8,1024]{2,1,0:T(8,128)S(1)} collective-permute-done((f32[4,8,1024]{2,1,0:T(8,128)S(1)}, f32[4,8,1024]{2,1,0:T(8,128)S(1)}, u32[]{:S(2)}, u32[]{:S(2)}) %collective-permute-start.3) | collective-permute-done | bytes 131104 | tf_op jit(solution)/shard_map/ppermute | solution.py:321
  17.2 0.8 %finish.2 = (f32[4,32,1024]{2,1,0:T(8,128)S(1)}, f32[4,8,1024]{2,1,0:T(8,128)S(1)}, f32[4,8,1024]{2,1,0:T(8,128)S(1)}) custom-call(f32[4,32,1024]{2,1,0:T(8,128)S(1)} %inner.3.inner_ref, f32[4,8,1024]{2,1,0:T(8,128)S(1)} %collective-permute-done.2.from_other_ref, f32[4,8,1024]{2,1,0:T(8,128)S(1)} %collective-permute-done.3.from_pair_ref, ...), custom_call_target="tpu_custom_call" | custom-call | tf_op jit(solution)/shard_map/finish/pallas_call | solution.py:332
  18.0 4.0 %collective-permute-start.4 = (f32[4,8,1024]{2,1,0:T(8,128)S(1)}, f32[4,8,1024]{2,1,0:T(8,128)S(1)}, u32[]{:S(2)}, u32[]{:S(2)}) collective-permute-start(f32[4,8,1024]{2,1,0:T(8,128)S(1)} %get-tuple-element.38), channel_id=1, source_target_pairs={{1,2},{3,4},{5,6},{7,8},{9,10},{11,12},{13,14},{15,0},{2,1},{4,3},... | collective-permute-start | bytes 393224 | tf_op jit(solution)/shard_map/ppermute | solution.py:320
  22.1 1.3 %inner.4.inner_ref = f32[4,32,1024]{2,1,0:T(8,128)S(1)} custom-call(f32[4,32,1024]{2,1,0:T(8,128)S(1)} %get-tuple-element.37.refs_0_.refs_6_, f32[4,32,128]{2,1,0:T(8,128)S(1)} %levels.1.refs_1_, bf16[208,208]{1,0:T(8,128)(2,1)S(1)} %get-tuple-element.31.refs_2_, bf16[208,208]{1,0:T(8,128)(2,1)S(1)} %get-tuple-element.29.refs_3_.low_ref, ...), custom_call_target="tpu_custom_call" | custom-call | tf_op jit(solution)/shard_map/inner/pallas_call | solution.py:332
  23.4 3.3 %collective-permute-done.4.from_other_ref = f32[4,8,1024]{2,1,0:T(8,128)S(1)} collective-permute-done((f32[4,8,1024]{2,1,0:T(8,128)S(1)}, f32[4,8,1024]{2,1,0:T(8,128)S(1)}, u32[]{:S(2)}, u32[]{:S(2)}) %collective-permute-start.4) | collective-permute-done | bytes 131104 | tf_op jit(solution)/shard_map/ppermute | solution.py:320
  27.0 0.8 %finish.3 = (f32[4,32,1024]{2,1,0:T(8,128)S(1)}, f32[4,8,1024]{2,1,0:T(8,128)S(1)}, f32[4,8,1024]{2,1,0:T(8,128)S(1)}) custom-call(f32[4,32,1024]{2,1,0:T(8,128)S(1)} %inner.4.inner_ref, f32[4,8,1024]{2,1,0:T(8,128)S(1)} %collective-permute-done.4.from_other_ref, f32[4,8,1024]{2,1,0:T(8,128)S(1)} %collective-permute-done.5.from_pair_ref, ...), custom_call_target="tpu_custom_call" | custom-call | tf_op jit(solution)/shard_map/finish/pallas_call | solution.py:332
  27.9 3.8 %collective-permute-start.6 = (f32[4,8,1024]{2,1,0:T(8,128)S(1)}, f32[4,8,1024]{2,1,0:T(8,128)S(1)}, u32[]{:S(2)}, u32[]{:S(2)}) collective-permute-start(f32[4,8,1024]{2,1,0:T(8,128)S(1)} %get-tuple-element.44), channel_id=1, source_target_pairs={{1,2},{3,4},{5,6},{7,8},{9,10},{11,12},{13,14},{15,0},{2,1},{4,3},... | collective-permute-start | bytes 393224 | tf_op jit(solution)/shard_map/ppermute | solution.py:320
  31.7 1.6 %margin_rows.1.refs_2_ = bf16[256,2048]{1,0:T(8,128)(2,1)S(1)} custom-call(bf16[4096,128]{1,0:T(8,128)(2,1)S(1)} %bitcast.6), custom_call_target="tpu_custom_call" | custom-call | tf_op jit(solution)/shard_map/margin_rows/pallas_call | solution.py:332
  33.3 1.5 %inner.5 = (f32[4,32,1024]{2,1,0:T(8,128)S(1)}, bf16[512,512]{1,0:T(8,128)(2,1)S(1)}) custom-call(f32[4,32,1024]{2,1,0:T(8,128)S(1)} %get-tuple-element.40.refs_0_, f32[4,32,128]{2,1,0:T(8,128)S(1)} %levels.1.refs_1_, bf16[208,208]{1,0:T(8,128)(2,1)S(1)} %get-tuple-element.31.refs_2_, bf16[208,208]{1,0:T(8,128)(2,1)S(1)} %get-tuple-element.29.refs_3_.low_ref, ...), custom_call_target="tpu_custom_call" | custom-call | tf_op jit(solution)/shard_map/inner/pallas_call | solution.py:332
  34.8 1.8 %collective-permute-done.6.refs_1_ = f32[4,8,1024]{2,1,0:T(8,128)S(1)} collective-permute-done((f32[4,8,1024]{2,1,0:T(8,128)S(1)}, f32[4,8,1024]{2,1,0:T(8,128)S(1)}, u32[]{:S(2)}, u32[]{:S(2)}) %collective-permute-start.6) | collective-permute-done | bytes 131104 | tf_op jit(solution)/shard_map/ppermute | solution.py:320
  36.6 0.8 %from_cells.1 = (f32[32,16,128]{2,1,0:T(8,128)S(1)}, f32[32,16,128]{2,1,0:T(8,128)S(1)}) custom-call(f32[4,32,1024]{2,1,0:T(8,128)S(1)} %get-tuple-element.43.refs_0_, f32[4,8,1024]{2,1,0:T(8,128)S(1)} %collective-permute-done.6.refs_1_, f32[4,8,1024]{2,1,0:T(8,128)S(1)} %collective-permute-done.7.refs_2_, ...), custom_call_target="tpu_custom_call" | custom-call | tf_op jit(solution)/shard_map/from_cells/pallas_call | solution.py:332
  37.5 1.5 %collective-permute-done.8.refs_1_ = f32[32,16,128]{2,1,0:T(8,128)S(1)} collective-permute-done((f32[32,16,128]{2,1,0:T(8,128)S(1)}, f32[32,16,128]{2,1,0:T(8,128)S(1)}, u32[]{:S(2)}, u32[]{:S(2)}) %collective-permute-start.8) | collective-permute-done | bytes 262176 | tf_op jit(solution)/shard_map/ppermute | solution.py:327
  39.0 0.9 %margin.1 = (f32[2,64,128]{2,1,0:T(8,128)S(1)}, f32[64,16,128]{2,1,0:T(8,128)}) custom-call(f32[32,16,128]{2,1,0:T(8,128)S(1)} %get-tuple-element.47.refs_0_, f32[32,16,128]{2,1,0:T(8,128)S(1)} %collective-permute-done.8.refs_1_, bf16[256,2048]{1,0:T(8,128)(2,1)S(1)} %margin_rows.1.refs_2_), custom_call_target="tpu_custom_call" | custom-call | tf_op jit(solution)/shard_map/margin/pallas_call | solution.py:332
  39.9 11.2 %all_to_all.5.tiles_ref = f32[32,4,128]{2,1,0:T(4,128)S(1)} all-to-all(f32[32,4,128]{2,1,0:T(4,128)S(1)} %bitcast.9), channel_id=1, replica_groups=mesh['px'=2,'py'=16] {'px','py'}, dimensions={0} | all-to-all | bytes 131072 | tf_op jit(solution)/shard_map/all_to_all | solution.py:453
  51.1 0.7 %tile_sum.1 = f32[16,32]{1,0:T(8,128)} custom-call(f32[32,4,128]{2,1,0:T(4,128)S(1)} %all_to_all.5.tiles_ref), custom_call_target="tpu_custom_call" | custom-call | tf_op jit(solution)/shard_map/tile_sum/pallas_call | solution.py:332
  (16 shorter events, 1.2 us)
Async XLA Ops:
  0.6 3.7 %collective-permute-start = (f32[64,16,128]{2,1,0:T(8,128)}, f32[64,16,128]{2,1,0:T(8,128)S(1)}, u32[]{:S(2)}, u32[]{:S(2)}) collective-permute-start(f32[64,16,128]{2,1,0:T(8,128)} %bitcast.7), channel_id=1, source_target_pairs={{0,16},{16,0},{1,17},{17,1},{2,18},{18,2},{3,19},{19,3},{4,20},{20... | collective-permute-start | bytes 1572872 | tf_op jit(solution)/shard_map/ppermute | solution.py:327
  1.1 0.8 %copy-start.2 = (f32[125,125]{1,0:T(8,128)S(1)}, f32[125,125]{1,0:T(8,128)}, u32[]{:S(2)}) copy-start(f32[125,125]{1,0:T(8,128)} %cell_ref.1) | copy-start | bytes 187504
  3.0 1.0 %copy-start.1 = (f32[64,4,4,128]{3,2,1,0:T(4,128)S(1)}, f32[64,4,4,128]{3,2,1,0:T(4,128)}, u32[]{:S(2)}) copy-start(f32[64,4,4,128]{3,2,1,0:T(4,128)} %param.4) | copy-start | bytes 1572868
  4.3 7.3 %copy-start.3 = (f32[4,4,128]{2,1,0:T(4,128)S(1)}, f32[4,4,128]{2,1,0:T(4,128)}, u32[]{:S(2)}) copy-start(f32[4,4,128]{2,1,0:T(4,128)} %param.5) | copy-start | bytes 24580
  5.0 10.8 %collective-permute-start.2 = (f32[4,8,1024]{2,1,0:T(8,128)S(1)}, f32[4,8,1024]{2,1,0:T(8,128)S(1)}, u32[]{:S(2)}, u32[]{:S(2)}) collective-permute-start(f32[4,8,1024]{2,1,0:T(8,128)S(1)} %get-tuple-element.33), channel_id=1, source_target_pairs={{1,2},{3,4},{5,6},{7,8},{9,10},{11,12},{13,14},{15,0},{2,1},{4,3},... | collective-permute-start | bytes 393224 | tf_op jit(solution)/shard_map/ppermute | solution.py:320
  11.6 5.6 %collective-permute-start.3 = (f32[4,8,1024]{2,1,0:T(8,128)S(1)}, f32[4,8,1024]{2,1,0:T(8,128)S(1)}, u32[]{:S(2)}, u32[]{:S(2)}) collective-permute-start(f32[4,8,1024]{2,1,0:T(8,128)S(1)} %get-tuple-element.34), channel_id=1, source_target_pairs={{0,1},{2,3},{4,5},{6,7},{8,9},{10,11},{12,13},{14,15},{1,0},{3,2},... | collective-permute-start | bytes 393224 | tf_op jit(solution)/shard_map/ppermute | solution.py:321
  11.6 1.2 %collective-permute-start.1 = (f32[16,128]{1,0:T(8,128)S(1)}, f32[16,128]{1,0:T(8,128)S(1)}, u32[]{:S(2)}, u32[]{:S(2)}) collective-permute-start(f32[16,128]{1,0:T(8,128)S(1)} %bitcast.10), channel_id=1, source_target_pairs={{0,16},{16,0},{1,17},{17,1},{2,18},{18,2},{3,19},{19,3},{4,20},{20... | collective-permute-start | bytes 24584 | tf_op jit(solution)/shard_map/ppermute | solution.py:327
  18.0 8.7 %collective-permute-start.4 = (f32[4,8,1024]{2,1,0:T(8,128)S(1)}, f32[4,8,1024]{2,1,0:T(8,128)S(1)}, u32[]{:S(2)}, u32[]{:S(2)}) collective-permute-start(f32[4,8,1024]{2,1,0:T(8,128)S(1)} %get-tuple-element.38), channel_id=1, source_target_pairs={{1,2},{3,4},{5,6},{7,8},{9,10},{11,12},{13,14},{15,0},{2,1},{4,3},... | collective-permute-start | bytes 393224 | tf_op jit(solution)/shard_map/ppermute | solution.py:320
  22.1 5.0 %collective-permute-start.5 = (f32[4,8,1024]{2,1,0:T(8,128)S(1)}, f32[4,8,1024]{2,1,0:T(8,128)S(1)}, u32[]{:S(2)}, u32[]{:S(2)}) collective-permute-start(f32[4,8,1024]{2,1,0:T(8,128)S(1)} %get-tuple-element.39), channel_id=1, source_target_pairs={{0,1},{2,3},{4,5},{6,7},{8,9},{10,11},{12,13},{14,15},{1,0},{3,2},... | collective-permute-start | bytes 393224 | tf_op jit(solution)/shard_map/ppermute | solution.py:321
  22.1 9.6 %copy-start = (bf16[256,4,4,128]{3,2,1,0:T(4,128)(2,1)S(1)}, bf16[256,4,4,128]{3,2,1,0:T(4,128)(2,1)}, u32[]{:S(2)}) copy-start(bf16[256,4,4,128]{3,2,1,0:T(4,128)(2,1)} %param.7) | copy-start | bytes 3145732
  27.9 8.7 %collective-permute-start.6 = (f32[4,8,1024]{2,1,0:T(8,128)S(1)}, f32[4,8,1024]{2,1,0:T(8,128)S(1)}, u32[]{:S(2)}, u32[]{:S(2)}) collective-permute-start(f32[4,8,1024]{2,1,0:T(8,128)S(1)} %get-tuple-element.44), channel_id=1, source_target_pairs={{1,2},{3,4},{5,6},{7,8},{9,10},{11,12},{13,14},{15,0},{2,1},{4,3},... | collective-permute-start | bytes 393224 | tf_op jit(solution)/shard_map/ppermute | solution.py:320
  31.7 5.0 %collective-permute-start.7 = (f32[4,8,1024]{2,1,0:T(8,128)S(1)}, f32[4,8,1024]{2,1,0:T(8,128)S(1)}, u32[]{:S(2)}, u32[]{:S(2)}) collective-permute-start(f32[4,8,1024]{2,1,0:T(8,128)S(1)} %get-tuple-element.45), channel_id=1, source_target_pairs={{0,1},{2,3},{4,5},{6,7},{8,9},{10,11},{12,13},{14,15},{1,0},{3,2},... | collective-permute-start | bytes 393224 | tf_op jit(solution)/shard_map/ppermute | solution.py:321
  37.4 1.6 %collective-permute-start.8 = (f32[32,16,128]{2,1,0:T(8,128)S(1)}, f32[32,16,128]{2,1,0:T(8,128)S(1)}, u32[]{:S(2)}, u32[]{:S(2)}) collective-permute-start(f32[32,16,128]{2,1,0:T(8,128)S(1)} %get-tuple-element.48), channel_id=1, source_target_pairs={{0,16},{16,0},{1,17},{17,1},{2,18},{18,2},{3,19},{19,3},{4,20},{20... | collective-permute-start | bytes 786440 | tf_op jit(solution)/shard_map/ppermute | solution.py:327

commit v17 on v16

--- a/solution.py
+++ b/solution.py
@@ -89,7 +89,7 @@
 
 
 def margin_rows_kernel(layer, parts_y, groups, block_ref, out_ref, wide_ref, lines_ref):
-    wide_ref[...] = block_ref[...].astype(f32)
+    wide_ref[: block_ref.shape[0], :] = block_ref[...].astype(f32)
     thickness = block_ref.shape[1]
     tile_cols = out_ref.shape[0] // parts_y
     cols = tile_cols // groups
@@ -97,7 +97,7 @@
         for col in range(tile_cols):
             lines = wide_ref[pl.ds(col * layer + n, parts_y, stride=tile_cols * layer), :]
             lines_ref[pl.ds(col // cols * cols * parts_y + col % cols, parts_y, stride=cols), :] = lines
-        out_ref[:, pl.ds(n * thickness, thickness)] = lines_ref[...].astype(bf16)
+        out_ref[:, pl.ds(n * thickness, thickness)] = lines_ref[: out_ref.shape[0], :].astype(bf16)
 
 
 def roll_cells(value, cells, forward):
@@ -151,28 +151,27 @@
         copy.wait()
 
 
-def turned(part_ref, order_ref, count):
-    layer, thickness = part_ref.shape[1:]
+def turned(part_ref, order_ref):
+    count, layer, thickness = part_ref.shape
     group = lanes // (thickness // 4)
-    first = 0 if part_ref.shape[0] == count else lax.axis_index("px") * count
     sources = []
     for start in range(0, count, group):
-        sources += list(two_parts(jnp.concatenate([part_ref[first + start + s] for s in range(group)], 1)))
+        sources += list(two_parts(jnp.concatenate([part_ref[start + s] for s in range(group)], 1)))
     ordered = dot(jnp.concatenate(sources, 0), order_ref[...])
     starts = range(0, ordered.shape[0], 2 * layer)
     values = [ordered[start : start + layer] + ordered[start + layer : start + 2 * layer] for start in starts]
     return [jnp.concatenate([part[:, iz * lanes : (iz + 1) * lanes] for part in values], 1) for iz in range(4)]
 
 
-def turn_kernel(count, part_ref, order_ref, out_ref):
-    for iz, rows in enumerate(turned(part_ref, order_ref, count)):
+def turn_kernel(part_ref, order_ref, out_ref):
+    for iz, rows in enumerate(turned(part_ref, order_ref)):
         out_ref[iz] = rows
 
 
-def to_cells_kernel(cells, count, own_ref, *refs):
+def to_cells_kernel(cells, own_ref, *refs):
     part_refs = refs[:-6]
     order_ref, edge_ref, low_ref, w_ref, pair_ref, other_ref = refs[-6:]
-    parts = [[own_ref[iz] for iz in range(4)]] + [turned(ref, order_ref, count) for ref in part_refs]
+    parts = [[own_ref[iz] for iz in range(4)]] + [turned(ref, order_ref) for ref in part_refs]
     value = [jnp.concatenate([part[iz] for part in parts], 0) for iz in range(4)]
     for iz in range(4):
         w_ref[iz] = value[iz]
@@ -288,11 +287,8 @@
         target = filtered_ref.at[pl.ds(owners[step] * count, count)]
         copies.append(pltpu.make_async_copy(part_ref, target, sems.at[step]))
     start_all(copies)
-    flat = [ref.reshape(count * layer, thickness) for ref in part_refs]
-    lines = [
-        jnp.concatenate([ref[pl.ds(n, count, stride=layer), :].astype(bf16) for ref in flat], 0)
-        for n in range(layer)
-    ]
+    turned_parts = [jnp.swapaxes(ref[...], 0, 1) for ref in part_refs]
+    lines = [jnp.concatenate([part[n] for part in turned_parts], 0).astype(bf16) for n in range(layer)]
     product = lax.dot_general(
         block_ref[...], jnp.concatenate(lines, 1), (((1,), (1,)), ((), ())), preferred_element_type=f32
     )
@@ -371,19 +367,16 @@
     def part_for(step):
         return lax.dynamic_slice_in_dim(span_rows, lax.rem(me + step, parts_x) * mine, mine, 0)
 
-    if parts_x == 2:
-        parts = [span_rows, shifted(span_rows, "px", 1)]
-    else:
-        parts = [part_for(0)] + [shifted(part_for(step), "px", step) for step in reversed(others)]
+    parts = [part_for(0)] + [shifted(part_for(step), "px", step) for step in reversed(others)]
     high, low, edge_matrix, halo_matrix, place, order = kernel_call(
         functools.partial(matrix_kernel, cells, nodes),
         [matrix, matrix, edge_shape, from_halo, place_shape, table],
         [cell_matrix],
         "assemble",
     )
-    own = kernel_call(functools.partial(turn_kernel, mine), jax.ShapeDtypeStruct((4, layer, width), f32), [parts[0], order], "turn")
+    own = kernel_call(turn_kernel, jax.ShapeDtypeStruct((4, layer, width), f32), [parts[0], order], "turn")
     field_now, *edges = kernel_call(
-        functools.partial(to_cells_kernel, cells, mine),
+        functools.partial(to_cells_kernel, cells),
         [field, message, message],
         [own] + parts[1:] + [order, edge_matrix, low],
         "to_cells",
@@ -409,8 +402,8 @@
                 [block.reshape(block_count * layer, thickness)],
                 "margin_rows",
                 scratch=[
-                    pltpu.VMEM((block_count * layer, thickness), f32),
-                    pltpu.VMEM((block_count, thickness), f32),
+                    pltpu.VMEM(((block_count + tile_cols) * layer, thickness), f32),
+                    pltpu.VMEM((block_count + 8 * tile_cols, thickness), f32),
                 ],
             )
         operands = [field_now, levels, high, low, edge_matrix, place] + ([before] if step > 0 else [])

time: 52 us -> 51.1 us (0.983)
  local copies, waits for them, and re-layouts: 1.89 us -> 1.11 us
    unnamed x8 -> x6, local copies, waits for them, and re-layouts: 1.89 us -> 0.01 us
    dynamic_slice x0 -> x1, local copies, waits for them, and re-layouts: none -> 1.1 us  [part_for(): lax.dynamic_slice_in_dim(span_rows, lax.rem(me + step, parts_x) * mine, m...]
  transfers between devices with their start and end apart: 9 -> 9, of which waited for: 8 -> 7; matrix products, arithmetic and copies ran while one was open for 0% -> 0% of each run, Pallas kernels for 14% -> 14%
where the time goes in v17:
time: 51.1 us; the launch traced here: 50.9 us
  starting transfers between devices  15.1 us (30%)
  Pallas kernels  11.8 us (23%)
  blocking collectives  11.2 us (22%)
  waiting for transfers between devices  10.9 us (21%)
  local copies, waits for them, and re-layouts  1.11 us (2%)
  between operations  0.74 us (1%)
    ppermute x3, starting transfers between devices, swapped(): other = lax.ppermute(other, 'py', others + [(b, a) for a, b in others])  14.5 us
    pallas_call x13, Pallas kernels, kernel_call(): pl.pallas_call(body, out_shape=outs, in_specs=in_specs or [whole] * len(o...  11.8 us
    all_to_all x1, blocking collectives, local(): tiles = lax.all_to_all(tiles, ('px', 'py'), 0, 0, tiled=True)  11.2 us
    ppermute x3, waiting for transfers between devices, swapped(): other = lax.ppermute(other, 'py', others + [(b, a) for a, b in others])  6.57 us
    ppermute x3, waiting for transfers between devices, shifted(): lax.ppermute(value, axis, [(source, (source + steps) % count) for source...  2.68 us
    ppermute x3, waiting for transfers between devices, swapped(): pair = lax.ppermute(pair, 'py', pairs + [(b, a) for a, b in pairs])  1.69 us
    dynamic_slice x1, local copies, waits for them, and re-layouts, part_for(): lax.dynamic_slice_in_dim(span_rows, lax.rem(me + step, parts_x) * mine, m...  1.1 us
  transfers between devices with their start and end apart: 9, of which 7 were waited for; matrix products, arithmetic and copies ran while one was open for 0% of the time, Pallas kernels for 14%

profile of v17, /device:TPU:0, one launch (start us, length us, event | category | flops | bytes accessed | tf_op | source)
XLA Modules:
  0.0 50.9 jit_solution(14197907316231115824)
XLA Ops:
  0.7 1.1 %constant_dynamic-slice_fusion = (f32[32,16,128]{2,1,0:T(8,128)S(1)}, f32[32,16,128]{2,1,0:T(8,128)S(1)}) fusion(f32[64,16,128]{2,1,0:T(8,128)} %bitcast.10, s32[]{:T(128)S(6)} %select_n.7, s32[]{:T(128)S(6)} %select_n.6), kind=kLoop, calls=%fused_computation | loop fusion | bytes 1048584 | tf_op jit(solution)/shard_map/dynamic_slice | solution.py:368
  1.8 0.5 %collective-permute-start = (f32[32,16,128]{2,1,0:T(8,128)S(1)}, f32[32,16,128]{2,1,0:T(8,128)S(1)}, u32[]{:S(2)}, u32[]{:S(2)}) collective-permute-start(f32[32,16,128]{2,1,0:T(8,128)S(1)} %get-tuple-element.52), channel_id=1, source_target_pairs={{0,16},{16,0},{1,17},{17,1},{2,18},{18,2},{3,19},{19,3},{4,20},{20... | collective-permute-start | bytes 786440 | tf_op jit(solution)/shard_map/ppermute | solution.py:323
  2.3 1.0 %assemble.1 = (bf16[208,208]{1,0:T(8,128)(2,1)S(1)}, bf16[208,208]{1,0:T(8,128)(2,1)S(1)}, bf16[80,160]{1,0:T(8,128)(2,1)S(1)}, bf16[160,208]{1,0:T(8,128)(2,1)S...) custom-call(f32[125,125]{1,0:T(8,128)S(1)} %copy-done.1), custom_call_target="tpu_custom_call" | custom-call | tf_op jit(solution)/shard_map/assemble/pallas_call | solution.py:328
  3.6 0.7 %to_cells.1 = (f32[4,32,1024]{2,1,0:T(8,128)S(1)}, f32[4,8,1024]{2,1,0:T(8,128)S(1)}, f32[4,8,1024]{2,1,0:T(8,128)S(1)}) custom-call(f32[4,16,1024]{2,1,0:T(8,128)S(1)} %turn.1.own_ref, f32[32,16,128]{2,1,0:T(8,128)S(1)} %collective-permute-done.refs_0_, bf16[512,512]{1,0:T(8,128)(2,1)S(1)} %get-tuple-element.27.order_ref.refs_1_, ...), custom_call_target="tpu_custom_call" | custom-call | tf_op jit(solution)/shard_map/to_cells/pallas_call | solution.py:328
  4.3 6.8 %collective-permute-start.2 = (f32[4,8,1024]{2,1,0:T(8,128)S(1)}, f32[4,8,1024]{2,1,0:T(8,128)S(1)}, u32[]{:S(2)}, u32[]{:S(2)}) collective-permute-start(f32[4,8,1024]{2,1,0:T(8,128)S(1)} %get-tuple-element.33), channel_id=1, source_target_pairs={{1,2},{3,4},{5,6},{7,8},{9,10},{11,12},{13,14},{15,0},{2,1},{4,3},... | collective-permute-start | bytes 393224 | tf_op jit(solution)/shard_map/ppermute | solution.py:316
  11.1 1.2 %collective-permute-done.1.refs_1_ = f32[16,128]{1,0:T(8,128)S(1)} collective-permute-done((f32[16,128]{1,0:T(8,128)S(1)}, f32[16,128]{1,0:T(8,128)S(1)}, u32[]{:S(2)}, u32[]{:S(2)}) %collective-permute-start.1) | collective-permute-done | bytes 8224 | tf_op jit(solution)/shard_map/ppermute | solution.py:323
  12.4 1.3 %inner.3.inner_ref = f32[4,32,1024]{2,1,0:T(8,128)S(1)} custom-call(f32[4,32,1024]{2,1,0:T(8,128)S(1)} %get-tuple-element.30.refs_0_.refs_6_, f32[4,32,128]{2,1,0:T(8,128)S(1)} %levels.1.refs_1_, bf16[208,208]{1,0:T(8,128)(2,1)S(1)} %get-tuple-element.31.refs_2_, bf16[208,208]{1,0:T(8,128)(2,1)S(1)} %get-tuple-element.29.refs_3_.low_ref, ...), custom_call_target="tpu_custom_call" | custom-call | tf_op jit(solution)/shard_map/inner/pallas_call | solution.py:328
  13.7 1.4 %collective-permute-done.2.from_other_ref = f32[4,8,1024]{2,1,0:T(8,128)S(1)} collective-permute-done((f32[4,8,1024]{2,1,0:T(8,128)S(1)}, f32[4,8,1024]{2,1,0:T(8,128)S(1)}, u32[]{:S(2)}, u32[]{:S(2)}) %collective-permute-start.2) | collective-permute-done | bytes 131104 | tf_op jit(solution)/shard_map/ppermute | solution.py:316
  15.1 1.4 %collective-permute-done.3.from_pair_ref = f32[4,8,1024]{2,1,0:T(8,128)S(1)} collective-permute-done((f32[4,8,1024]{2,1,0:T(8,128)S(1)}, f32[4,8,1024]{2,1,0:T(8,128)S(1)}, u32[]{:S(2)}, u32[]{:S(2)}) %collective-permute-start.3) | collective-permute-done | bytes 131104 | tf_op jit(solution)/shard_map/ppermute | solution.py:317
  16.5 0.8 %finish.2 = (f32[4,32,1024]{2,1,0:T(8,128)S(1)}, f32[4,8,1024]{2,1,0:T(8,128)S(1)}, f32[4,8,1024]{2,1,0:T(8,128)S(1)}) custom-call(f32[4,32,1024]{2,1,0:T(8,128)S(1)} %inner.3.inner_ref, f32[4,8,1024]{2,1,0:T(8,128)S(1)} %collective-permute-done.2.from_other_ref, f32[4,8,1024]{2,1,0:T(8,128)S(1)} %collective-permute-done.3.from_pair_ref, ...), custom_call_target="tpu_custom_call" | custom-call | tf_op jit(solution)/shard_map/finish/pallas_call | solution.py:328
  17.3 4.1 %collective-permute-start.4 = (f32[4,8,1024]{2,1,0:T(8,128)S(1)}, f32[4,8,1024]{2,1,0:T(8,128)S(1)}, u32[]{:S(2)}, u32[]{:S(2)}) collective-permute-start(f32[4,8,1024]{2,1,0:T(8,128)S(1)} %get-tuple-element.38), channel_id=1, source_target_pairs={{1,2},{3,4},{5,6},{7,8},{9,10},{11,12},{13,14},{15,0},{2,1},{4,3},... | collective-permute-start | bytes 393224 | tf_op jit(solution)/shard_map/ppermute | solution.py:316
  21.3 1.3 %inner.4.inner_ref = f32[4,32,1024]{2,1,0:T(8,128)S(1)} custom-call(f32[4,32,1024]{2,1,0:T(8,128)S(1)} %get-tuple-element.37.refs_0_.refs_6_, f32[4,32,128]{2,1,0:T(8,128)S(1)} %levels.1.refs_1_, bf16[208,208]{1,0:T(8,128)(2,1)S(1)} %get-tuple-element.31.refs_2_, bf16[208,208]{1,0:T(8,128)(2,1)S(1)} %get-tuple-element.29.refs_3_.low_ref, ...), custom_call_target="tpu_custom_call" | custom-call | tf_op jit(solution)/shard_map/inner/pallas_call | solution.py:328
  22.6 3.3 %collective-permute-done.4.from_other_ref = f32[4,8,1024]{2,1,0:T(8,128)S(1)} collective-permute-done((f32[4,8,1024]{2,1,0:T(8,128)S(1)}, f32[4,8,1024]{2,1,0:T(8,128)S(1)}, u32[]{:S(2)}, u32[]{:S(2)}) %collective-permute-start.4) | collective-permute-done | bytes 131104 | tf_op jit(solution)/shard_map/ppermute | solution.py:316
  26.0 0.3 collective-permute-done.5.from_pair_ref
  26.3 0.8 %finish.3 = (f32[4,32,1024]{2,1,0:T(8,128)S(1)}, f32[4,8,1024]{2,1,0:T(8,128)S(1)}, f32[4,8,1024]{2,1,0:T(8,128)S(1)}) custom-call(f32[4,32,1024]{2,1,0:T(8,128)S(1)} %inner.4.inner_ref, f32[4,8,1024]{2,1,0:T(8,128)S(1)} %collective-permute-done.4.from_other_ref, f32[4,8,1024]{2,1,0:T(8,128)S(1)} %collective-permute-done.5.from_pair_ref, ...), custom_call_target="tpu_custom_call" | custom-call | tf_op jit(solution)/shard_map/finish/pallas_call | solution.py:328
  27.1 3.7 %collective-permute-start.6 = (f32[4,8,1024]{2,1,0:T(8,128)S(1)}, f32[4,8,1024]{2,1,0:T(8,128)S(1)}, u32[]{:S(2)}, u32[]{:S(2)}) collective-permute-start(f32[4,8,1024]{2,1,0:T(8,128)S(1)} %get-tuple-element.44), channel_id=1, source_target_pairs={{1,2},{3,4},{5,6},{7,8},{9,10},{11,12},{13,14},{15,0},{2,1},{4,3},... | collective-permute-start | bytes 393224 | tf_op jit(solution)/shard_map/ppermute | solution.py:316
  30.8 1.6 %margin_rows.1.refs_2_ = bf16[256,2048]{1,0:T(8,128)(2,1)S(1)} custom-call(bf16[4096,128]{1,0:T(8,128)(2,1)S(1)} %bitcast.6), custom_call_target="tpu_custom_call" | custom-call | tf_op jit(solution)/shard_map/margin_rows/pallas_call | solution.py:328
  32.4 1.5 %inner.5 = (f32[4,32,1024]{2,1,0:T(8,128)S(1)}, bf16[512,512]{1,0:T(8,128)(2,1)S(1)}) custom-call(f32[4,32,1024]{2,1,0:T(8,128)S(1)} %get-tuple-element.40.refs_0_, f32[4,32,128]{2,1,0:T(8,128)S(1)} %levels.1.refs_1_, bf16[208,208]{1,0:T(8,128)(2,1)S(1)} %get-tuple-element.31.refs_2_, bf16[208,208]{1,0:T(8,128)(2,1)S(1)} %get-tuple-element.29.refs_3_.low_ref, ...), custom_call_target="tpu_custom_call" | custom-call | tf_op jit(solution)/shard_map/inner/pallas_call | solution.py:328
  34.0 1.8 %collective-permute-done.6.refs_1_ = f32[4,8,1024]{2,1,0:T(8,128)S(1)} collective-permute-done((f32[4,8,1024]{2,1,0:T(8,128)S(1)}, f32[4,8,1024]{2,1,0:T(8,128)S(1)}, u32[]{:S(2)}, u32[]{:S(2)}) %collective-permute-start.6) | collective-permute-done | bytes 131104 | tf_op jit(solution)/shard_map/ppermute | solution.py:316
  35.8 0.8 %from_cells.1 = (f32[32,16,128]{2,1,0:T(8,128)S(1)}, f32[32,16,128]{2,1,0:T(8,128)S(1)}) custom-call(f32[4,32,1024]{2,1,0:T(8,128)S(1)} %get-tuple-element.43.refs_0_, f32[4,8,1024]{2,1,0:T(8,128)S(1)} %collective-permute-done.6.refs_1_, f32[4,8,1024]{2,1,0:T(8,128)S(1)} %collective-permute-done.7.refs_2_, ...), custom_call_target="tpu_custom_call" | custom-call | tf_op jit(solution)/shard_map/from_cells/pallas_call | solution.py:328
  36.7 1.5 %collective-permute-done.8.refs_1_ = f32[32,16,128]{2,1,0:T(8,128)S(1)} collective-permute-done((f32[32,16,128]{2,1,0:T(8,128)S(1)}, f32[32,16,128]{2,1,0:T(8,128)S(1)}, u32[]{:S(2)}, u32[]{:S(2)}) %collective-permute-start.8) | collective-permute-done | bytes 262176 | tf_op jit(solution)/shard_map/ppermute | solution.py:323
  38.2 0.8 %margin.1 = (f32[2,64,128]{2,1,0:T(8,128)S(1)}, f32[64,16,128]{2,1,0:T(8,128)}) custom-call(f32[32,16,128]{2,1,0:T(8,128)S(1)} %get-tuple-element.47.refs_0_, f32[32,16,128]{2,1,0:T(8,128)S(1)} %collective-permute-done.8.refs_1_, bf16[256,2048]{1,0:T(8,128)(2,1)S(1)} %margin_rows.1.refs_2_), custom_call_target="tpu_custom_call" | custom-call | tf_op jit(solution)/shard_map/margin/pallas_call | solution.py:328
  39.0 11.2 %all_to_all.5.tiles_ref = f32[32,4,128]{2,1,0:T(4,128)S(1)} all-to-all(f32[32,4,128]{2,1,0:T(4,128)S(1)} %bitcast.7), channel_id=1, replica_groups=mesh['px'=2,'py'=16] {'px','py'}, dimensions={0} | all-to-all | bytes 131072 | tf_op jit(solution)/shard_map/all_to_all | solution.py:446
  50.2 0.7 %tile_sum.1 = f32[16,32]{1,0:T(8,128)} custom-call(f32[32,4,128]{2,1,0:T(4,128)S(1)} %all_to_all.5.tiles_ref), custom_call_target="tpu_custom_call" | custom-call | tf_op jit(solution)/shard_map/tile_sum/pallas_call | solution.py:328
  (15 shorter events, 0.6 us)
Async XLA Ops:
  0.6 1.6 %copy-start.1 = (f32[125,125]{1,0:T(8,128)S(1)}, f32[125,125]{1,0:T(8,128)}, u32[]{:S(2)}) copy-start(f32[125,125]{1,0:T(8,128)} %cell_ref.1) | copy-start | bytes 187504
  1.8 1.8 %collective-permute-start = (f32[32,16,128]{2,1,0:T(8,128)S(1)}, f32[32,16,128]{2,1,0:T(8,128)S(1)}, u32[]{:S(2)}, u32[]{:S(2)}) collective-permute-start(f32[32,16,128]{2,1,0:T(8,128)S(1)} %get-tuple-element.52), channel_id=1, source_target_pairs={{0,16},{16,0},{1,17},{17,1},{2,18},{18,2},{3,19},{19,3},{4,20},{20... | collective-permute-start | bytes 786440 | tf_op jit(solution)/shard_map/ppermute | solution.py:323
  3.6 7.5 %copy-start.2 = (f32[4,4,128]{2,1,0:T(4,128)S(1)}, f32[4,4,128]{2,1,0:T(4,128)}, u32[]{:S(2)}) copy-start(f32[4,4,128]{2,1,0:T(4,128)} %param.5) | copy-start | bytes 24580
  4.3 10.8 %collective-permute-start.2 = (f32[4,8,1024]{2,1,0:T(8,128)S(1)}, f32[4,8,1024]{2,1,0:T(8,128)S(1)}, u32[]{:S(2)}, u32[]{:S(2)}) collective-permute-start(f32[4,8,1024]{2,1,0:T(8,128)S(1)} %get-tuple-element.33), channel_id=1, source_target_pairs={{1,2},{3,4},{5,6},{7,8},{9,10},{11,12},{13,14},{15,0},{2,1},{4,3},... | collective-permute-start | bytes 393224 | tf_op jit(solution)/shard_map/ppermute | solution.py:316
  11.0 5.4 %collective-permute-start.3 = (f32[4,8,1024]{2,1,0:T(8,128)S(1)}, f32[4,8,1024]{2,1,0:T(8,128)S(1)}, u32[]{:S(2)}, u32[]{:S(2)}) collective-permute-start(f32[4,8,1024]{2,1,0:T(8,128)S(1)} %get-tuple-element.34), channel_id=1, source_target_pairs={{0,1},{2,3},{4,5},{6,7},{8,9},{10,11},{12,13},{14,15},{1,0},{3,2},... | collective-permute-start | bytes 393224 | tf_op jit(solution)/shard_map/ppermute | solution.py:317
  11.1 1.2 %collective-permute-start.1 = (f32[16,128]{1,0:T(8,128)S(1)}, f32[16,128]{1,0:T(8,128)S(1)}, u32[]{:S(2)}, u32[]{:S(2)}) collective-permute-start(f32[16,128]{1,0:T(8,128)S(1)} %bitcast.8), channel_id=1, source_target_pairs={{0,16},{16,0},{1,17},{17,1},{2,18},{18,2},{3,19},{19,3},{4,20},{20... | collective-permute-start | bytes 24584 | tf_op jit(solution)/shard_map/ppermute | solution.py:323
  17.3 8.7 %collective-permute-start.4 = (f32[4,8,1024]{2,1,0:T(8,128)S(1)}, f32[4,8,1024]{2,1,0:T(8,128)S(1)}, u32[]{:S(2)}, u32[]{:S(2)}) collective-permute-start(f32[4,8,1024]{2,1,0:T(8,128)S(1)} %get-tuple-element.38), channel_id=1, source_target_pairs={{1,2},{3,4},{5,6},{7,8},{9,10},{11,12},{13,14},{15,0},{2,1},{4,3},... | collective-permute-start | bytes 393224 | tf_op jit(solution)/shard_map/ppermute | solution.py:316
  21.3 5.0 %collective-permute-start.5 = (f32[4,8,1024]{2,1,0:T(8,128)S(1)}, f32[4,8,1024]{2,1,0:T(8,128)S(1)}, u32[]{:S(2)}, u32[]{:S(2)}) collective-permute-start(f32[4,8,1024]{2,1,0:T(8,128)S(1)} %get-tuple-element.39), channel_id=1, source_target_pairs={{0,1},{2,3},{4,5},{6,7},{8,9},{10,11},{12,13},{14,15},{1,0},{3,2},... | collective-permute-start | bytes 393224 | tf_op jit(solution)/shard_map/ppermute | solution.py:317
  21.3 9.5 %copy-start = (bf16[256,4,4,128]{3,2,1,0:T(4,128)(2,1)S(1)}, bf16[256,4,4,128]{3,2,1,0:T(4,128)(2,1)}, u32[]{:S(2)}) copy-start(bf16[256,4,4,128]{3,2,1,0:T(4,128)(2,1)} %param.7) | copy-start | bytes 3145732
  27.1 8.7 %collective-permute-start.6 = (f32[4,8,1024]{2,1,0:T(8,128)S(1)}, f32[4,8,1024]{2,1,0:T(8,128)S(1)}, u32[]{:S(2)}, u32[]{:S(2)}) collective-permute-start(f32[4,8,1024]{2,1,0:T(8,128)S(1)} %get-tuple-element.44), channel_id=1, source_target_pairs={{1,2},{3,4},{5,6},{7,8},{9,10},{11,12},{13,14},{15,0},{2,1},{4,3},... | collective-permute-start | bytes 393224 | tf_op jit(solution)/shard_map/ppermute | solution.py:316
  30.8 5.0 %collective-permute-start.7 = (f32[4,8,1024]{2,1,0:T(8,128)S(1)}, f32[4,8,1024]{2,1,0:T(8,128)S(1)}, u32[]{:S(2)}, u32[]{:S(2)}) collective-permute-start(f32[4,8,1024]{2,1,0:T(8,128)S(1)} %get-tuple-element.45), channel_id=1, source_target_pairs={{0,1},{2,3},{4,5},{6,7},{8,9},{10,11},{12,13},{14,15},{1,0},{3,2},... | collective-permute-start | bytes 393224 | tf_op jit(solution)/shard_map/ppermute | solution.py:317
  36.6 1.6 %collective-permute-start.8 = (f32[32,16,128]{2,1,0:T(8,128)S(1)}, f32[32,16,128]{2,1,0:T(8,128)S(1)}, u32[]{:S(2)}, u32[]{:S(2)}) collective-permute-start(f32[32,16,128]{2,1,0:T(8,128)S(1)} %get-tuple-element.48), channel_id=1, source_target_pairs={{0,16},{16,0},{1,17},{17,1},{2,18},{18,2},{3,19},{19,3},{4,20},{20... | collective-permute-start | bytes 786440 | tf_op jit(solution)/shard_map/ppermute | solution.py:323

commit v18 on v17

--- a/solution.py
+++ b/solution.py
@@ -125,7 +125,7 @@
 
 
 def even_place():
-    return lax.rem(lax.axis_index("py"), 2) == 0
+    return lax.rem(lax.axis_index("px") + lax.axis_index("py"), 2) == 0
 
 
 def send_edges(edge_ref, low_ref, value, pair_ref, other_ref, cells):
@@ -227,7 +227,7 @@
         out_ref[iz] = total if step == 0 else total - before_ref[iz]
 
 
-def finish(cells, step, inner_ref, other_ref, pair_ref, matrix_ref):
+def finish(cells, step, inner_ref, pair_ref, other_ref, matrix_ref):
     size, width = inner_ref.shape[1:]
     nodes = size // 4
     even = even_place()
@@ -248,18 +248,18 @@
 
 
 def finish_kernel(
-    cells, step, inner_ref, from_other_ref, from_pair_ref, matrix_ref, edge_ref, low_ref, next_ref, pair_ref, other_ref
+    cells, step, inner_ref, from_pair_ref, from_other_ref, matrix_ref, edge_ref, low_ref, next_ref, pair_ref, other_ref
 ):
-    value = finish(cells, step, inner_ref, from_other_ref, from_pair_ref, matrix_ref)
+    value = finish(cells, step, inner_ref, from_pair_ref, from_other_ref, matrix_ref)
     for iz in range(4):
         next_ref[iz] = value[iz]
     send_edges(edge_ref, low_ref, value, pair_ref, other_ref, cells)
 
 
 def from_cells_kernel(cells, *refs):
-    inner_ref, other_ref, pair_ref, matrix_ref, order_ref = refs[:5]
+    inner_ref, pair_ref, other_ref, matrix_ref, order_ref = refs[:5]
     out_refs = refs[5:]
-    value = finish(cells, 2, inner_ref, other_ref, pair_ref, matrix_ref)
+    value = finish(cells, 2, inner_ref, pair_ref, other_ref, matrix_ref)
     states, layer, thickness = out_refs[0].shape
     group = lanes // cells
     size = value[0].shape[0]
@@ -309,13 +309,14 @@
 
 
 def swapped(edges):
-    count = lax.axis_size("py")
-    pairs = [(place, place + 1) for place in range(0, count, 2)]
-    others = [(place + 1, (place + 2) % count) for place in range(0, count, 2)]
-    pair, other = edges
-    other = lax.ppermute(other, "py", others + [(b, a) for a, b in others])
-    pair = lax.ppermute(pair, "py", pairs + [(b, a) for a, b in pairs])
-    return [other, pair]
+    count_x, count = lax.axis_size("px"), lax.axis_size("py")
+    first, second = [], []
+    for px in range(count_x):
+        for place in range(count):
+            ways = (1, -1) if (px + place) % 2 == 0 else (-1, 1)
+            for pairs, way in zip((first, second), ways):
+                pairs.append((px * count + place, px * count + (place + way) % count))
+    return [lax.ppermute(edge, ("px", "py"), pairs) for edge, pairs in zip(edges, (first, second))]
 
 
 def shifted(value, axis, steps):

time: 51.1 us -> 51.5 us (level)
  waiting for transfers between devices: 10.9 us -> 8.27 us
  starting transfers between devices: 15.1 us -> 17.4 us
  blocking collectives: 11.2 us -> 12 us
    ppermute x6, waiting for transfers between devices: 8.26 us -> 5.58 us  [swapped(): lax.ppermute(edge, ('px', 'py'), pairs)]
    ppermute x6, starting transfers between devices: 14.5 us -> 16.8 us  [swapped(): lax.ppermute(edge, ('px', 'py'), pairs)]
    all_to_all x1, blocking collectives: 11.2 us -> 12 us  [local(): tiles = lax.all_to_all(tiles, ('px', 'py'), 0, 0, tiled=True)]
  transfers between devices with their start and end apart: 9 -> 9, of which waited for: 7 -> 5; matrix products, arithmetic and copies ran while one was open for 0% -> 0% of each run, Pallas kernels for 14% -> 14%
where the time goes in v18:
time: 51.5 us; the launch traced here: 51.3 us
  starting transfers between devices  17.4 us (34%)
  blocking collectives  12 us (23%)
  Pallas kernels  11.8 us (23%)
  waiting for transfers between devices  8.27 us (16%)
  local copies, waits for them, and re-layouts  1.11 us (2%)
  between operations  0.77 us (1%)
    ppermute x6, starting transfers between devices, swapped(): lax.ppermute(edge, ('px', 'py'), pairs)  16.8 us
    all_to_all x1, blocking collectives, local(): tiles = lax.all_to_all(tiles, ('px', 'py'), 0, 0, tiled=True)  12 us
    pallas_call x13, Pallas kernels, kernel_call(): pl.pallas_call(body, out_shape=outs, in_specs=in_specs or [whole] * len(o...  11.8 us
    ppermute x6, waiting for transfers between devices, swapped(): lax.ppermute(edge, ('px', 'py'), pairs)  5.58 us
    ppermute x3, waiting for transfers between devices, shifted(): lax.ppermute(value, axis, [(source, (source + steps) % count) for source...  2.7 us
    dynamic_slice x1, local copies, waits for them, and re-layouts, part_for(): lax.dynamic_slice_in_dim(span_rows, lax.rem(me + step, parts_x) * mine, m...  1.1 us
  transfers between devices with their start and end apart: 9, of which 5 were waited for; matrix products, arithmetic and copies ran while one was open for 0% of the time, Pallas kernels for 14%

profile of v18, /device:TPU:0, one launch (start us, length us, event | category | flops | bytes accessed | tf_op | source)
XLA Modules:
  0.0 51.3 jit_solution(11638750179023057186)
XLA Ops:
  0.7 1.1 %constant_dynamic-slice_fusion = (f32[32,16,128]{2,1,0:T(8,128)S(1)}, f32[32,16,128]{2,1,0:T(8,128)S(1)}) fusion(f32[64,16,128]{2,1,0:T(8,128)} %bitcast.10, s32[]{:T(128)S(6)} %select_n.7, s32[]{:T(128)S(6)} %select_n.6), kind=kLoop, calls=%fused_computation | loop fusion | bytes 1048584 | tf_op jit(solution)/shard_map/dynamic_slice | solution.py:369
  1.8 0.5 %collective-permute-start = (f32[32,16,128]{2,1,0:T(8,128)S(1)}, f32[32,16,128]{2,1,0:T(8,128)S(1)}, u32[]{:S(2)}, u32[]{:S(2)}) collective-permute-start(f32[32,16,128]{2,1,0:T(8,128)S(1)} %get-tuple-element.52), channel_id=1, source_target_pairs={{0,16},{16,0},{1,17},{17,1},{2,18},{18,2},{3,19},{19,3},{4,20},{20... | collective-permute-start | bytes 786440 | tf_op jit(solution)/shard_map/ppermute | solution.py:324
  2.3 1.0 %assemble.1 = (bf16[208,208]{1,0:T(8,128)(2,1)S(1)}, bf16[208,208]{1,0:T(8,128)(2,1)S(1)}, bf16[80,160]{1,0:T(8,128)(2,1)S(1)}, bf16[160,208]{1,0:T(8,128)(2,1)S...) custom-call(f32[125,125]{1,0:T(8,128)S(1)} %copy-done.1), custom_call_target="tpu_custom_call" | custom-call | tf_op jit(solution)/shard_map/assemble/pallas_call | solution.py:329
  3.6 0.7 %to_cells.1 = (f32[4,32,1024]{2,1,0:T(8,128)S(1)}, f32[4,8,1024]{2,1,0:T(8,128)S(1)}, f32[4,8,1024]{2,1,0:T(8,128)S(1)}) custom-call(f32[4,16,1024]{2,1,0:T(8,128)S(1)} %turn.1.own_ref, f32[32,16,128]{2,1,0:T(8,128)S(1)} %collective-permute-done.refs_0_, bf16[512,512]{1,0:T(8,128)(2,1)S(1)} %get-tuple-element.27.order_ref.refs_1_, ...), custom_call_target="tpu_custom_call" | custom-call | tf_op jit(solution)/shard_map/to_cells/pallas_call | solution.py:329
  4.3 2.8 %collective-permute-start.2 = (f32[4,8,1024]{2,1,0:T(8,128)S(1)}, f32[4,8,1024]{2,1,0:T(8,128)S(1)}, u32[]{:S(2)}, u32[]{:S(2)}) collective-permute-start(f32[4,8,1024]{2,1,0:T(8,128)S(1)} %get-tuple-element.33), channel_id=1, source_target_pairs={{0,1},{1,0},{2,3},{3,2},{4,5},{5,4},{6,7},{7,6},{8,9},{9,8},{10,11... | collective-permute-start | bytes 393224 | tf_op jit(solution)/shard_map/ppermute | solution.py:319
  7.1 4.5 %collective-permute-start.3 = (f32[4,8,1024]{2,1,0:T(8,128)S(1)}, f32[4,8,1024]{2,1,0:T(8,128)S(1)}, u32[]{:S(2)}, u32[]{:S(2)}) collective-permute-start(f32[4,8,1024]{2,1,0:T(8,128)S(1)} %get-tuple-element.34), channel_id=1, source_target_pairs={{0,15},{1,2},{2,1},{3,4},{4,3},{5,6},{6,5},{7,8},{8,7},{9,10},{10,... | collective-permute-start | bytes 393224 | tf_op jit(solution)/shard_map/ppermute | solution.py:319
  11.6 1.2 %collective-permute-done.1.refs_1_ = f32[16,128]{1,0:T(8,128)S(1)} collective-permute-done((f32[16,128]{1,0:T(8,128)S(1)}, f32[16,128]{1,0:T(8,128)S(1)}, u32[]{:S(2)}, u32[]{:S(2)}) %collective-permute-start.1) | collective-permute-done | bytes 8224 | tf_op jit(solution)/shard_map/ppermute | solution.py:324
  12.9 1.3 %inner.3.inner_ref = f32[4,32,1024]{2,1,0:T(8,128)S(1)} custom-call(f32[4,32,1024]{2,1,0:T(8,128)S(1)} %get-tuple-element.30.refs_0_.refs_6_, f32[4,32,128]{2,1,0:T(8,128)S(1)} %levels.1.refs_1_, bf16[208,208]{1,0:T(8,128)(2,1)S(1)} %get-tuple-element.31.refs_2_, bf16[208,208]{1,0:T(8,128)(2,1)S(1)} %get-tuple-element.29.refs_3_.low_ref, ...), custom_call_target="tpu_custom_call" | custom-call | tf_op jit(solution)/shard_map/inner/pallas_call | solution.py:329
  14.3 1.4 %collective-permute-done.3.from_other_ref = f32[4,8,1024]{2,1,0:T(8,128)S(1)} collective-permute-done((f32[4,8,1024]{2,1,0:T(8,128)S(1)}, f32[4,8,1024]{2,1,0:T(8,128)S(1)}, u32[]{:S(2)}, u32[]{:S(2)}) %collective-permute-start.3) | collective-permute-done | bytes 131104 | tf_op jit(solution)/shard_map/ppermute | solution.py:319
  15.7 0.8 %finish.2 = (f32[4,32,1024]{2,1,0:T(8,128)S(1)}, f32[4,8,1024]{2,1,0:T(8,128)S(1)}, f32[4,8,1024]{2,1,0:T(8,128)S(1)}) custom-call(f32[4,32,1024]{2,1,0:T(8,128)S(1)} %inner.3.inner_ref, f32[4,8,1024]{2,1,0:T(8,128)S(1)} %collective-permute-done.2.from_pair_ref, f32[4,8,1024]{2,1,0:T(8,128)S(1)} %collective-permute-done.3.from_other_ref, ...), custom_call_target="tpu_custom_call" | custom-call | tf_op jit(solution)/shard_map/finish/pallas_call | solution.py:329
  16.5 0.8 %collective-permute-start.4 = (f32[4,8,1024]{2,1,0:T(8,128)S(1)}, f32[4,8,1024]{2,1,0:T(8,128)S(1)}, u32[]{:S(2)}, u32[]{:S(2)}) collective-permute-start(f32[4,8,1024]{2,1,0:T(8,128)S(1)} %get-tuple-element.38), channel_id=1, source_target_pairs={{0,1},{1,0},{2,3},{3,2},{4,5},{5,4},{6,7},{7,6},{8,9},{9,8},{10,11... | collective-permute-start | bytes 393224 | tf_op jit(solution)/shard_map/ppermute | solution.py:319
  17.3 4.0 %collective-permute-start.5 = (f32[4,8,1024]{2,1,0:T(8,128)S(1)}, f32[4,8,1024]{2,1,0:T(8,128)S(1)}, u32[]{:S(2)}, u32[]{:S(2)}) collective-permute-start(f32[4,8,1024]{2,1,0:T(8,128)S(1)} %get-tuple-element.39), channel_id=1, source_target_pairs={{0,15},{1,2},{2,1},{3,4},{4,3},{5,6},{6,5},{7,8},{8,7},{9,10},{10,... | collective-permute-start | bytes 393224 | tf_op jit(solution)/shard_map/ppermute | solution.py:319
  21.4 1.3 %inner.4.inner_ref = f32[4,32,1024]{2,1,0:T(8,128)S(1)} custom-call(f32[4,32,1024]{2,1,0:T(8,128)S(1)} %get-tuple-element.37.refs_0_.refs_6_, f32[4,32,128]{2,1,0:T(8,128)S(1)} %levels.1.refs_1_, bf16[208,208]{1,0:T(8,128)(2,1)S(1)} %get-tuple-element.31.refs_2_, bf16[208,208]{1,0:T(8,128)(2,1)S(1)} %get-tuple-element.29.refs_3_.low_ref, ...), custom_call_target="tpu_custom_call" | custom-call | tf_op jit(solution)/shard_map/inner/pallas_call | solution.py:329
  22.7 3.2 %collective-permute-done.5.from_other_ref = f32[4,8,1024]{2,1,0:T(8,128)S(1)} collective-permute-done((f32[4,8,1024]{2,1,0:T(8,128)S(1)}, f32[4,8,1024]{2,1,0:T(8,128)S(1)}, u32[]{:S(2)}, u32[]{:S(2)}) %collective-permute-start.5) | collective-permute-done | bytes 131104 | tf_op jit(solution)/shard_map/ppermute | solution.py:319
  25.9 0.8 %finish.3 = (f32[4,32,1024]{2,1,0:T(8,128)S(1)}, f32[4,8,1024]{2,1,0:T(8,128)S(1)}, f32[4,8,1024]{2,1,0:T(8,128)S(1)}) custom-call(f32[4,32,1024]{2,1,0:T(8,128)S(1)} %inner.4.inner_ref, f32[4,8,1024]{2,1,0:T(8,128)S(1)} %collective-permute-done.4.from_pair_ref, f32[4,8,1024]{2,1,0:T(8,128)S(1)} %collective-permute-done.5.from_other_ref, ...), custom_call_target="tpu_custom_call" | custom-call | tf_op jit(solution)/shard_map/finish/pallas_call | solution.py:329
  26.8 4.5 %collective-permute-start.7 = (f32[4,8,1024]{2,1,0:T(8,128)S(1)}, f32[4,8,1024]{2,1,0:T(8,128)S(1)}, u32[]{:S(2)}, u32[]{:S(2)}) collective-permute-start(f32[4,8,1024]{2,1,0:T(8,128)S(1)} %get-tuple-element.45), channel_id=1, source_target_pairs={{0,15},{1,2},{2,1},{3,4},{4,3},{5,6},{6,5},{7,8},{8,7},{9,10},{10,... | collective-permute-start | bytes 393224 | tf_op jit(solution)/shard_map/ppermute | solution.py:319
  31.3 1.6 %margin_rows.1.refs_2_ = bf16[256,2048]{1,0:T(8,128)(2,1)S(1)} custom-call(bf16[4096,128]{1,0:T(8,128)(2,1)S(1)} %bitcast.6), custom_call_target="tpu_custom_call" | custom-call | tf_op jit(solution)/shard_map/margin_rows/pallas_call | solution.py:329
  32.9 1.5 %inner.5 = (f32[4,32,1024]{2,1,0:T(8,128)S(1)}, bf16[512,512]{1,0:T(8,128)(2,1)S(1)}) custom-call(f32[4,32,1024]{2,1,0:T(8,128)S(1)} %get-tuple-element.40.refs_0_, f32[4,32,128]{2,1,0:T(8,128)S(1)} %levels.1.refs_1_, bf16[208,208]{1,0:T(8,128)(2,1)S(1)} %get-tuple-element.31.refs_2_, bf16[208,208]{1,0:T(8,128)(2,1)S(1)} %get-tuple-element.29.refs_3_.low_ref, ...), custom_call_target="tpu_custom_call" | custom-call | tf_op jit(solution)/shard_map/inner/pallas_call | solution.py:329
  34.5 0.9 %collective-permute-done.7.refs_2_ = f32[4,8,1024]{2,1,0:T(8,128)S(1)} collective-permute-done((f32[4,8,1024]{2,1,0:T(8,128)S(1)}, f32[4,8,1024]{2,1,0:T(8,128)S(1)}, u32[]{:S(2)}, u32[]{:S(2)}) %collective-permute-start.7) | collective-permute-done | bytes 131104 | tf_op jit(solution)/shard_map/ppermute | solution.py:319
  35.4 0.8 %from_cells.1 = (f32[32,16,128]{2,1,0:T(8,128)S(1)}, f32[32,16,128]{2,1,0:T(8,128)S(1)}) custom-call(f32[4,32,1024]{2,1,0:T(8,128)S(1)} %get-tuple-element.43.refs_0_, f32[4,8,1024]{2,1,0:T(8,128)S(1)} %collective-permute-done.6.refs_1_, f32[4,8,1024]{2,1,0:T(8,128)S(1)} %collective-permute-done.7.refs_2_, ...), custom_call_target="tpu_custom_call" | custom-call | tf_op jit(solution)/shard_map/from_cells/pallas_call | solution.py:329
  36.3 1.5 %collective-permute-done.8.refs_1_ = f32[32,16,128]{2,1,0:T(8,128)S(1)} collective-permute-done((f32[32,16,128]{2,1,0:T(8,128)S(1)}, f32[32,16,128]{2,1,0:T(8,128)S(1)}, u32[]{:S(2)}, u32[]{:S(2)}) %collective-permute-start.8) | collective-permute-done | bytes 262176 | tf_op jit(solution)/shard_map/ppermute | solution.py:324
  37.8 0.8 %margin.1 = (f32[2,64,128]{2,1,0:T(8,128)S(1)}, f32[64,16,128]{2,1,0:T(8,128)}) custom-call(f32[32,16,128]{2,1,0:T(8,128)S(1)} %get-tuple-element.47.refs_0_, f32[32,16,128]{2,1,0:T(8,128)S(1)} %collective-permute-done.8.refs_1_, bf16[256,2048]{1,0:T(8,128)(2,1)S(1)} %margin_rows.1.refs_2_), custom_call_target="tpu_custom_call" | custom-call | tf_op jit(solution)/shard_map/margin/pallas_call | solution.py:329
  38.6 12.0 %all_to_all.5.tiles_ref = f32[32,4,128]{2,1,0:T(4,128)S(1)} all-to-all(f32[32,4,128]{2,1,0:T(4,128)S(1)} %bitcast.7), channel_id=1, replica_groups=mesh['px'=2,'py'=16] {'px','py'}, dimensions={0} | all-to-all | bytes 131072 | tf_op jit(solution)/shard_map/all_to_all | solution.py:447
  50.6 0.7 %tile_sum.1 = f32[16,32]{1,0:T(8,128)} custom-call(f32[32,4,128]{2,1,0:T(4,128)S(1)} %all_to_all.5.tiles_ref), custom_call_target="tpu_custom_call" | custom-call | tf_op jit(solution)/shard_map/tile_sum/pallas_call | solution.py:329
  (15 shorter events, 0.6 us)
Async XLA Ops:
  0.6 1.6 %copy-start.1 = (f32[125,125]{1,0:T(8,128)S(1)}, f32[125,125]{1,0:T(8,128)}, u32[]{:S(2)}) copy-start(f32[125,125]{1,0:T(8,128)} %cell_ref.1) | copy-start | bytes 187504
  1.8 1.8 %collective-permute-start = (f32[32,16,128]{2,1,0:T(8,128)S(1)}, f32[32,16,128]{2,1,0:T(8,128)S(1)}, u32[]{:S(2)}, u32[]{:S(2)}) collective-permute-start(f32[32,16,128]{2,1,0:T(8,128)S(1)} %get-tuple-element.52), channel_id=1, source_target_pairs={{0,16},{16,0},{1,17},{17,1},{2,18},{18,2},{3,19},{19,3},{4,20},{20... | collective-permute-start | bytes 786440 | tf_op jit(solution)/shard_map/ppermute | solution.py:324
  3.6 8.0 %copy-start.2 = (f32[4,4,128]{2,1,0:T(4,128)S(1)}, f32[4,4,128]{2,1,0:T(4,128)}, u32[]{:S(2)}) copy-start(f32[4,4,128]{2,1,0:T(4,128)} %param.5) | copy-start | bytes 24580
  4.3 10.0 %collective-permute-start.2 = (f32[4,8,1024]{2,1,0:T(8,128)S(1)}, f32[4,8,1024]{2,1,0:T(8,128)S(1)}, u32[]{:S(2)}, u32[]{:S(2)}) collective-permute-start(f32[4,8,1024]{2,1,0:T(8,128)S(1)} %get-tuple-element.33), channel_id=1, source_target_pairs={{0,1},{1,0},{2,3},{3,2},{4,5},{5,4},{6,7},{7,6},{8,9},{9,8},{10,11... | collective-permute-start | bytes 393224 | tf_op jit(solution)/shard_map/ppermute | solution.py:319
  7.1 8.6 %collective-permute-start.3 = (f32[4,8,1024]{2,1,0:T(8,128)S(1)}, f32[4,8,1024]{2,1,0:T(8,128)S(1)}, u32[]{:S(2)}, u32[]{:S(2)}) collective-permute-start(f32[4,8,1024]{2,1,0:T(8,128)S(1)} %get-tuple-element.34), channel_id=1, source_target_pairs={{0,15},{1,2},{2,1},{3,4},{4,3},{5,6},{6,5},{7,8},{8,7},{9,10},{10,... | collective-permute-start | bytes 393224 | tf_op jit(solution)/shard_map/ppermute | solution.py:319
  11.6 1.2 %collective-permute-start.1 = (f32[16,128]{1,0:T(8,128)S(1)}, f32[16,128]{1,0:T(8,128)S(1)}, u32[]{:S(2)}, u32[]{:S(2)}) collective-permute-start(f32[16,128]{1,0:T(8,128)S(1)} %bitcast.8), channel_id=1, source_target_pairs={{0,16},{16,0},{1,17},{17,1},{2,18},{18,2},{3,19},{19,3},{4,20},{20... | collective-permute-start | bytes 24584 | tf_op jit(solution)/shard_map/ppermute | solution.py:324
  16.5 6.2 %collective-permute-start.4 = (f32[4,8,1024]{2,1,0:T(8,128)S(1)}, f32[4,8,1024]{2,1,0:T(8,128)S(1)}, u32[]{:S(2)}, u32[]{:S(2)}) collective-permute-start(f32[4,8,1024]{2,1,0:T(8,128)S(1)} %get-tuple-element.38), channel_id=1, source_target_pairs={{0,1},{1,0},{2,3},{3,2},{4,5},{5,4},{6,7},{7,6},{8,9},{9,8},{10,11... | collective-permute-start | bytes 393224 | tf_op jit(solution)/shard_map/ppermute | solution.py:319
  17.3 8.6 %collective-permute-start.5 = (f32[4,8,1024]{2,1,0:T(8,128)S(1)}, f32[4,8,1024]{2,1,0:T(8,128)S(1)}, u32[]{:S(2)}, u32[]{:S(2)}) collective-permute-start(f32[4,8,1024]{2,1,0:T(8,128)S(1)} %get-tuple-element.39), channel_id=1, source_target_pairs={{0,15},{1,2},{2,1},{3,4},{4,3},{5,6},{6,5},{7,8},{8,7},{9,10},{10,... | collective-permute-start | bytes 393224 | tf_op jit(solution)/shard_map/ppermute | solution.py:319
  21.4 10.0 %copy-start = (bf16[256,4,4,128]{3,2,1,0:T(4,128)(2,1)S(1)}, bf16[256,4,4,128]{3,2,1,0:T(4,128)(2,1)}, u32[]{:S(2)}) copy-start(bf16[256,4,4,128]{3,2,1,0:T(4,128)(2,1)} %param.7) | copy-start | bytes 3145732
  26.7 7.8 %collective-permute-start.6 = (f32[4,8,1024]{2,1,0:T(8,128)S(1)}, f32[4,8,1024]{2,1,0:T(8,128)S(1)}, u32[]{:S(2)}, u32[]{:S(2)}) collective-permute-start(f32[4,8,1024]{2,1,0:T(8,128)S(1)} %get-tuple-element.44), channel_id=1, source_target_pairs={{0,1},{1,0},{2,3},{3,2},{4,5},{5,4},{6,7},{7,6},{8,9},{9,8},{10,11... | collective-permute-start | bytes 393224 | tf_op jit(solution)/shard_map/ppermute | solution.py:319
  26.8 8.6 %collective-permute-start.7 = (f32[4,8,1024]{2,1,0:T(8,128)S(1)}, f32[4,8,1024]{2,1,0:T(8,128)S(1)}, u32[]{:S(2)}, u32[]{:S(2)}) collective-permute-start(f32[4,8,1024]{2,1,0:T(8,128)S(1)} %get-tuple-element.45), channel_id=1, source_target_pairs={{0,15},{1,2},{2,1},{3,4},{4,3},{5,6},{6,5},{7,8},{8,7},{9,10},{10,... | collective-permute-start | bytes 393224 | tf_op jit(solution)/shard_map/ppermute | solution.py:319
  36.2 1.6 %collective-permute-start.8 = (f32[32,16,128]{2,1,0:T(8,128)S(1)}, f32[32,16,128]{2,1,0:T(8,128)S(1)}, u32[]{:S(2)}, u32[]{:S(2)}) collective-permute-start(f32[32,16,128]{2,1,0:T(8,128)S(1)} %get-tuple-element.48), channel_id=1, source_target_pairs={{0,16},{16,0},{1,17},{17,1},{2,18},{18,2},{3,19},{19,3},{4,20},{20... | collective-permute-start | bytes 786440 | tf_op jit(solution)/shard_map/ppermute | solution.py:324

commit v19 on v17

--- a/solution.py
+++ b/solution.py
@@ -151,12 +151,13 @@
         copy.wait()
 
 
-def turned(part_ref, order_ref):
-    count, layer, thickness = part_ref.shape
+def turned(part_ref, order_ref, count):
+    layer, thickness = part_ref.shape[1:]
     group = lanes // (thickness // 4)
+    first = 0 if part_ref.shape[0] == count else lax.axis_index("px") * count
     sources = []
     for start in range(0, count, group):
-        sources += list(two_parts(jnp.concatenate([part_ref[start + s] for s in range(group)], 1)))
+        sources += list(two_parts(jnp.concatenate([part_ref[first + start + s] for s in range(group)], 1)))
     ordered = dot(jnp.concatenate(sources, 0), order_ref[...])
     starts = range(0, ordered.shape[0], 2 * layer)
     values = [ordered[start : start + layer] + ordered[start + layer : start + 2 * layer] for start in starts]
@@ -164,14 +165,14 @@
 
 
 def turn_kernel(part_ref, order_ref, out_ref):
-    for iz, rows in enumerate(turned(part_ref, order_ref)):
+    for iz, rows in enumerate(turned(part_ref, order_ref, part_ref.shape[0])):
         out_ref[iz] = rows
 
 
-def to_cells_kernel(cells, own_ref, *refs):
+def to_cells_kernel(cells, count, own_ref, *refs):
     part_refs = refs[:-6]
     order_ref, edge_ref, low_ref, w_ref, pair_ref, other_ref = refs[-6:]
-    parts = [[own_ref[iz] for iz in range(4)]] + [turned(ref, order_ref) for ref in part_refs]
+    parts = [[own_ref[iz] for iz in range(4)]] + [turned(ref, order_ref, count) for ref in part_refs]
     value = [jnp.concatenate([part[iz] for part in parts], 0) for iz in range(4)]
     for iz in range(4):
         w_ref[iz] = value[iz]
@@ -256,16 +257,13 @@
     send_edges(edge_ref, low_ref, value, pair_ref, other_ref, cells)
 
 
-def from_cells_kernel(cells, *refs):
-    inner_ref, other_ref, pair_ref, matrix_ref, order_ref = refs[:5]
-    out_refs = refs[5:]
-    value = finish(cells, 2, inner_ref, other_ref, pair_ref, matrix_ref)
+def turn_back(value, order_ref, out_refs):
     states, layer, thickness = out_refs[0].shape
-    group = lanes // cells
+    group = lanes // (thickness // 4)
     size = value[0].shape[0]
     sources = []
     for h in range(states // group):
-        parts = [value[iz][:, h * lanes : (h + 1) * lanes] for iz in range(4)]
+        parts = [rows[:, h * lanes : (h + 1) * lanes] for rows in value]
         sources += list(two_parts(jnp.concatenate(parts, 1)))
     ordered = dot(jnp.concatenate(sources, 0), order_ref[...])
     for h in range(states // group):
@@ -274,6 +272,18 @@
             for step, out_ref in enumerate(out_refs):
                 rows = slice(step * layer, (step + 1) * layer)
                 out_ref[h * group + s] = part[rows, s * thickness : (s + 1) * thickness]
+
+
+def from_cells_kernel(cells, inner_ref, from_other_ref, from_pair_ref, matrix_ref, order_ref, own_ref, *out_refs):
+    value = finish(cells, 2, inner_ref, from_other_ref, from_pair_ref, matrix_ref)
+    layer = own_ref.shape[1]
+    for iz in range(4):
+        own_ref[iz] = value[iz][:layer]
+    turn_back([rows[layer:] for rows in value], order_ref, out_refs)
+
+
+def own_from_cells_kernel(own_ref, order_ref, out_ref):
+    turn_back([own_ref[iz] for iz in range(4)], order_ref, [out_ref])
 
 
 def margin_kernel(parts_x, *refs):
@@ -367,16 +377,20 @@
     def part_for(step):
         return lax.dynamic_slice_in_dim(span_rows, lax.rem(me + step, parts_x) * mine, mine, 0)
 
-    parts = [part_for(0)] + [shifted(part_for(step), "px", step) for step in reversed(others)]
+    if parts_x == 2:
+        parts = [part_for(0), shifted(span_rows, "px", 1)]
+    else:
+        parts = [part_for(0)] + [shifted(part_for(step), "px", step) for step in reversed(others)]
     high, low, edge_matrix, halo_matrix, place, order = kernel_call(
         functools.partial(matrix_kernel, cells, nodes),
         [matrix, matrix, edge_shape, from_halo, place_shape, table],
         [cell_matrix],
         "assemble",
     )
-    own = kernel_call(turn_kernel, jax.ShapeDtypeStruct((4, layer, width), f32), [parts[0], order], "turn")
+    own_cells = jax.ShapeDtypeStruct((4, layer, width), f32)
+    own = kernel_call(turn_kernel, own_cells, [parts[0], order], "turn")
     field_now, *edges = kernel_call(
-        functools.partial(to_cells_kernel, cells),
+        functools.partial(to_cells_kernel, cells, mine),
         [field, message, message],
         [own] + parts[1:] + [order, edge_matrix, low],
         "to_cells",
@@ -423,13 +437,14 @@
             )
             edges = swapped(edges)
         else:
-            pieces = kernel_call(
+            own, *pieces = kernel_call(
                 functools.partial(from_cells_kernel, cells),
-                [part] * parts_x,
+                [own_cells] + [part] * (parts_x - 1),
                 operands + back,
                 "from_cells",
             )
-    received = [pieces[0]] + [shifted(pieces[step], "px", step) for step in others]
+    received = [shifted(piece, "px", step) for step, piece in enumerate(pieces, 1)]
+    received = [kernel_call(own_from_cells_kernel, part, [own] + back, "own_from_cells")] + received
 
     tiles, filtered = kernel_call(
         functools.partial(margin_kernel, parts_x),

time: 51.1 us -> 51.7 us (1.012)
  local copies, waits for them, and re-layouts: 1.11 us -> 1.82 us
    unnamed x6, local copies, waits for them, and re-layouts: 0.01 us -> 0.85 us
    pallas_call x13 -> x14, Pallas kernels: 11.8 us -> 12 us  [kernel_call(): pl.pallas_call(body, out_shape=outs, in_specs=in_specs or [whole] * len(o...]
  transfers between devices with their start and end apart: 9 -> 9, of which waited for: 7 -> 7; matrix products, arithmetic and copies ran while one was open for 0% -> 2% of each run, Pallas kernels for 14% -> 15%
where the time goes in v19:
time: 51.7 us; the launch traced here: 51.5 us
  starting transfers between devices  15.2 us (29%)
  Pallas kernels  12 us (23%)
  blocking collectives  11.2 us (22%)
  waiting for transfers between devices  10.6 us (21%)
  local copies, waits for them, and re-layouts  1.82 us (4%)
  between operations  0.74 us (1%)
    ppermute x3, starting transfers between devices, swapped(): other = lax.ppermute(other, 'py', others + [(b, a) for a, b in others])  14.4 us
    pallas_call x14, Pallas kernels, kernel_call(): pl.pallas_call(body, out_shape=outs, in_specs=in_specs or [whole] * len(o...  12 us
    all_to_all x1, blocking collectives, local(): tiles = lax.all_to_all(tiles, ('px', 'py'), 0, 0, tiled=True)  11.2 us
    ppermute x3, waiting for transfers between devices, swapped(): other = lax.ppermute(other, 'py', others + [(b, a) for a, b in others])  6.71 us
    ppermute x3, waiting for transfers between devices, shifted(): lax.ppermute(value, axis, [(source, (source + steps) % count) for source...  2.18 us
    ppermute x3, waiting for transfers between devices, swapped(): pair = lax.ppermute(pair, 'py', pairs + [(b, a) for a, b in pairs])  1.71 us
  transfers between devices with their start and end apart: 9, of which 7 were waited for; matrix products, arithmetic and copies ran while one was open for 2% of the time, Pallas kernels for 15%

profile of v19, /device:TPU:0, one launch (start us, length us, event | category | flops | bytes accessed | tf_op | source)
XLA Modules:
  0.0 51.5 jit_solution(12808958972148292899)
XLA Ops:
  0.6 0.5 %collective-permute-start = (f32[64,16,128]{2,1,0:T(8,128)}, f32[64,16,128]{2,1,0:T(8,128)S(1)}, u32[]{:S(2)}, u32[]{:S(2)}) collective-permute-start(f32[64,16,128]{2,1,0:T(8,128)} %bitcast.10), channel_id=1, source_target_pairs={{0,16},{16,0},{1,17},{17,1},{2,18},{18,2},{3,19},{19,3},{4,20},{20... | collective-permute-start | bytes 1572872 | tf_op jit(solution)/shard_map/ppermute | solution.py:333
  1.1 0.8 %copy-done.1 = f32[125,125]{1,0:T(8,128)S(1)} copy-done((f32[125,125]{1,0:T(8,128)S(1)}, f32[125,125]{1,0:T(8,128)}, u32[]{:S(2)}) %copy-start.1) | copy-done | bytes 62524
  2.0 1.0 %assemble.1 = (bf16[208,208]{1,0:T(8,128)(2,1)S(1)}, bf16[208,208]{1,0:T(8,128)(2,1)S(1)}, bf16[80,160]{1,0:T(8,128)(2,1)S(1)}, bf16[160,208]{1,0:T(8,128)(2,1)S...) custom-call(f32[125,125]{1,0:T(8,128)S(1)} %copy-done.1), custom_call_target="tpu_custom_call" | custom-call | tf_op jit(solution)/shard_map/assemble/pallas_call | solution.py:338
  3.0 1.0 %constant_dynamic-slice_fusion.part_ref = f32[32,16,128]{2,1,0:T(8,128)S(1)} fusion(f32[64,16,128]{2,1,0:T(8,128)} %bitcast.11, s32[]{:T(128)S(6)} %select_n.3), kind=kLoop, calls=%fused_computation | loop fusion | bytes 524292 | tf_op jit(solution)/shard_map/dynamic_slice | solution.py:378
  4.3 0.7 %to_cells.1 = (f32[4,32,1024]{2,1,0:T(8,128)S(1)}, f32[4,8,1024]{2,1,0:T(8,128)S(1)}, f32[4,8,1024]{2,1,0:T(8,128)S(1)}) custom-call(f32[4,16,1024]{2,1,0:T(8,128)S(1)} %turn.1.own_ref, f32[64,16,128]{2,1,0:T(8,128)S(1)} %collective-permute-done.refs_0_, bf16[512,512]{1,0:T(8,128)(2,1)S(1)} %get-tuple-element.27.order_ref.refs_1_, ...), custom_call_target="tpu_custom_call" | custom-call | tf_op jit(solution)/shard_map/to_cells/pallas_call | solution.py:338
  5.0 6.6 %collective-permute-start.2 = (f32[4,8,1024]{2,1,0:T(8,128)S(1)}, f32[4,8,1024]{2,1,0:T(8,128)S(1)}, u32[]{:S(2)}, u32[]{:S(2)}) collective-permute-start(f32[4,8,1024]{2,1,0:T(8,128)S(1)} %get-tuple-element.33), channel_id=1, source_target_pairs={{1,2},{3,4},{5,6},{7,8},{9,10},{11,12},{13,14},{15,0},{2,1},{4,3},... | collective-permute-start | bytes 393224 | tf_op jit(solution)/shard_map/ppermute | solution.py:326
  11.8 1.0 %collective-permute-done.1.refs_1_ = f32[16,128]{1,0:T(8,128)S(1)} collective-permute-done((f32[16,128]{1,0:T(8,128)S(1)}, f32[16,128]{1,0:T(8,128)S(1)}, u32[]{:S(2)}, u32[]{:S(2)}) %collective-permute-start.1) | collective-permute-done | bytes 8224 | tf_op jit(solution)/shard_map/ppermute | solution.py:333
  12.9 1.3 %inner.3.inner_ref = f32[4,32,1024]{2,1,0:T(8,128)S(1)} custom-call(f32[4,32,1024]{2,1,0:T(8,128)S(1)} %get-tuple-element.30.refs_0_.refs_6_, f32[4,32,128]{2,1,0:T(8,128)S(1)} %levels.1.refs_1_, bf16[208,208]{1,0:T(8,128)(2,1)S(1)} %get-tuple-element.31.refs_2_, bf16[208,208]{1,0:T(8,128)(2,1)S(1)} %get-tuple-element.29.refs_3_.low_ref, ...), custom_call_target="tpu_custom_call" | custom-call | tf_op jit(solution)/shard_map/inner/pallas_call | solution.py:338
  14.2 1.6 %collective-permute-done.2.from_other_ref = f32[4,8,1024]{2,1,0:T(8,128)S(1)} collective-permute-done((f32[4,8,1024]{2,1,0:T(8,128)S(1)}, f32[4,8,1024]{2,1,0:T(8,128)S(1)}, u32[]{:S(2)}, u32[]{:S(2)}) %collective-permute-start.2) | collective-permute-done | bytes 131104 | tf_op jit(solution)/shard_map/ppermute | solution.py:326
  15.8 1.4 %collective-permute-done.3.from_pair_ref = f32[4,8,1024]{2,1,0:T(8,128)S(1)} collective-permute-done((f32[4,8,1024]{2,1,0:T(8,128)S(1)}, f32[4,8,1024]{2,1,0:T(8,128)S(1)}, u32[]{:S(2)}, u32[]{:S(2)}) %collective-permute-start.3) | collective-permute-done | bytes 131104 | tf_op jit(solution)/shard_map/ppermute | solution.py:327
  17.2 0.8 %finish.2 = (f32[4,32,1024]{2,1,0:T(8,128)S(1)}, f32[4,8,1024]{2,1,0:T(8,128)S(1)}, f32[4,8,1024]{2,1,0:T(8,128)S(1)}) custom-call(f32[4,32,1024]{2,1,0:T(8,128)S(1)} %inner.3.inner_ref, f32[4,8,1024]{2,1,0:T(8,128)S(1)} %collective-permute-done.2.from_other_ref, f32[4,8,1024]{2,1,0:T(8,128)S(1)} %collective-permute-done.3.from_pair_ref, ...), custom_call_target="tpu_custom_call" | custom-call | tf_op jit(solution)/shard_map/finish/pallas_call | solution.py:338
  18.0 4.0 %collective-permute-start.4 = (f32[4,8,1024]{2,1,0:T(8,128)S(1)}, f32[4,8,1024]{2,1,0:T(8,128)S(1)}, u32[]{:S(2)}, u32[]{:S(2)}) collective-permute-start(f32[4,8,1024]{2,1,0:T(8,128)S(1)} %get-tuple-element.38), channel_id=1, source_target_pairs={{1,2},{3,4},{5,6},{7,8},{9,10},{11,12},{13,14},{15,0},{2,1},{4,3},... | collective-permute-start | bytes 393224 | tf_op jit(solution)/shard_map/ppermute | solution.py:326
  22.0 1.3 %inner.4.inner_ref = f32[4,32,1024]{2,1,0:T(8,128)S(1)} custom-call(f32[4,32,1024]{2,1,0:T(8,128)S(1)} %get-tuple-element.37.refs_0_.refs_6_, f32[4,32,128]{2,1,0:T(8,128)S(1)} %levels.1.refs_1_, bf16[208,208]{1,0:T(8,128)(2,1)S(1)} %get-tuple-element.31.refs_2_, bf16[208,208]{1,0:T(8,128)(2,1)S(1)} %get-tuple-element.29.refs_3_.low_ref, ...), custom_call_target="tpu_custom_call" | custom-call | tf_op jit(solution)/shard_map/inner/pallas_call | solution.py:338
  23.3 3.3 %collective-permute-done.4.from_other_ref = f32[4,8,1024]{2,1,0:T(8,128)S(1)} collective-permute-done((f32[4,8,1024]{2,1,0:T(8,128)S(1)}, f32[4,8,1024]{2,1,0:T(8,128)S(1)}, u32[]{:S(2)}, u32[]{:S(2)}) %collective-permute-start.4) | collective-permute-done | bytes 131104 | tf_op jit(solution)/shard_map/ppermute | solution.py:326
  27.0 0.8 %finish.3 = (f32[4,32,1024]{2,1,0:T(8,128)S(1)}, f32[4,8,1024]{2,1,0:T(8,128)S(1)}, f32[4,8,1024]{2,1,0:T(8,128)S(1)}) custom-call(f32[4,32,1024]{2,1,0:T(8,128)S(1)} %inner.4.inner_ref, f32[4,8,1024]{2,1,0:T(8,128)S(1)} %collective-permute-done.4.from_other_ref, f32[4,8,1024]{2,1,0:T(8,128)S(1)} %collective-permute-done.5.from_pair_ref, ...), custom_call_target="tpu_custom_call" | custom-call | tf_op jit(solution)/shard_map/finish/pallas_call | solution.py:338
  27.8 3.8 %collective-permute-start.6 = (f32[4,8,1024]{2,1,0:T(8,128)S(1)}, f32[4,8,1024]{2,1,0:T(8,128)S(1)}, u32[]{:S(2)}, u32[]{:S(2)}) collective-permute-start(f32[4,8,1024]{2,1,0:T(8,128)S(1)} %get-tuple-element.44), channel_id=1, source_target_pairs={{1,2},{3,4},{5,6},{7,8},{9,10},{11,12},{13,14},{15,0},{2,1},{4,3},... | collective-permute-start | bytes 393224 | tf_op jit(solution)/shard_map/ppermute | solution.py:326
  31.6 1.6 %margin_rows.1.refs_2_ = bf16[256,2048]{1,0:T(8,128)(2,1)S(1)} custom-call(bf16[4096,128]{1,0:T(8,128)(2,1)S(1)} %bitcast.6), custom_call_target="tpu_custom_call" | custom-call | tf_op jit(solution)/shard_map/margin_rows/pallas_call | solution.py:338
  33.2 1.5 %inner.5 = (f32[4,32,1024]{2,1,0:T(8,128)S(1)}, bf16[512,512]{1,0:T(8,128)(2,1)S(1)}) custom-call(f32[4,32,1024]{2,1,0:T(8,128)S(1)} %get-tuple-element.40.refs_0_, f32[4,32,128]{2,1,0:T(8,128)S(1)} %levels.1.refs_1_, bf16[208,208]{1,0:T(8,128)(2,1)S(1)} %get-tuple-element.31.refs_2_, bf16[208,208]{1,0:T(8,128)(2,1)S(1)} %get-tuple-element.29.refs_3_.low_ref, ...), custom_call_target="tpu_custom_call" | custom-call | tf_op jit(solution)/shard_map/inner/pallas_call | solution.py:338
  34.8 1.8 %collective-permute-done.6.from_other_ref = f32[4,8,1024]{2,1,0:T(8,128)S(1)} collective-permute-done((f32[4,8,1024]{2,1,0:T(8,128)S(1)}, f32[4,8,1024]{2,1,0:T(8,128)S(1)}, u32[]{:S(2)}, u32[]{:S(2)}) %collective-permute-start.6) | collective-permute-done | bytes 131104 | tf_op jit(solution)/shard_map/ppermute | solution.py:326
  36.6 0.6 %from_cells.1 = (f32[4,16,1024]{2,1,0:T(8,128)S(1)}, f32[32,16,128]{2,1,0:T(8,128)S(1)}) custom-call(f32[4,32,1024]{2,1,0:T(8,128)S(1)} %get-tuple-element.43.inner_ref, f32[4,8,1024]{2,1,0:T(8,128)S(1)} %collective-permute-done.6.from_other_ref, f32[4,8,1024]{2,1,0:T(8,128)S(1)} %collective-permute-done.7.from_pair_ref, ...), custom_call_target="tpu_custom_call" | custom-call | tf_op jit(solution)/shard_map/from_cells/pallas_call | solution.py:338
  37.6 1.2 %collective-permute-done.8.refs_1_ = f32[32,16,128]{2,1,0:T(8,128)S(1)} collective-permute-done((f32[32,16,128]{2,1,0:T(8,128)S(1)}, f32[32,16,128]{2,1,0:T(8,128)S(1)}, u32[]{:S(2)}, u32[]{:S(2)}) %collective-permute-start.8) | collective-permute-done | bytes 262176 | tf_op jit(solution)/shard_map/ppermute | solution.py:333
  38.8 0.8 %margin.1 = (f32[2,64,128]{2,1,0:T(8,128)S(1)}, f32[64,16,128]{2,1,0:T(8,128)}) custom-call(f32[32,16,128]{2,1,0:T(8,128)S(1)} %own_from_cells.1.refs_0_, f32[32,16,128]{2,1,0:T(8,128)S(1)} %collective-permute-done.8.refs_1_, bf16[256,2048]{1,0:T(8,128)(2,1)S(1)} %margin_rows.1.refs_2_), custom_call_target="tpu_custom_call" | custom-call | tf_op jit(solution)/shard_map/margin/pallas_call | solution.py:338
  39.6 11.2 %all_to_all.5.tiles_ref = f32[32,4,128]{2,1,0:T(4,128)S(1)} all-to-all(f32[32,4,128]{2,1,0:T(4,128)S(1)} %bitcast.7), channel_id=1, replica_groups=mesh['px'=2,'py'=16] {'px','py'}, dimensions={0} | all-to-all | bytes 131072 | tf_op jit(solution)/shard_map/all_to_all | solution.py:461
  50.8 0.7 %tile_sum.1 = f32[16,32]{1,0:T(8,128)} custom-call(f32[32,4,128]{2,1,0:T(4,128)S(1)} %all_to_all.5.tiles_ref), custom_call_target="tpu_custom_call" | custom-call | tf_op jit(solution)/shard_map/tile_sum/pallas_call | solution.py:338
  (16 shorter events, 1.4 us)
Async XLA Ops:
  0.6 3.6 %collective-permute-start = (f32[64,16,128]{2,1,0:T(8,128)}, f32[64,16,128]{2,1,0:T(8,128)S(1)}, u32[]{:S(2)}, u32[]{:S(2)}) collective-permute-start(f32[64,16,128]{2,1,0:T(8,128)} %bitcast.10), channel_id=1, source_target_pairs={{0,16},{16,0},{1,17},{17,1},{2,18},{18,2},{3,19},{19,3},{4,20},{20... | collective-permute-start | bytes 1572872 | tf_op jit(solution)/shard_map/ppermute | solution.py:333
  1.1 0.8 %copy-start.1 = (f32[125,125]{1,0:T(8,128)S(1)}, f32[125,125]{1,0:T(8,128)}, u32[]{:S(2)}) copy-start(f32[125,125]{1,0:T(8,128)} %cell_ref.1) | copy-start | bytes 187504
  4.3 7.3 %copy-start.2 = (f32[4,4,128]{2,1,0:T(4,128)S(1)}, f32[4,4,128]{2,1,0:T(4,128)}, u32[]{:S(2)}) copy-start(f32[4,4,128]{2,1,0:T(4,128)} %param.5) | copy-start | bytes 24580
  5.0 10.8 %collective-permute-start.2 = (f32[4,8,1024]{2,1,0:T(8,128)S(1)}, f32[4,8,1024]{2,1,0:T(8,128)S(1)}, u32[]{:S(2)}, u32[]{:S(2)}) collective-permute-start(f32[4,8,1024]{2,1,0:T(8,128)S(1)} %get-tuple-element.33), channel_id=1, source_target_pairs={{1,2},{3,4},{5,6},{7,8},{9,10},{11,12},{13,14},{15,0},{2,1},{4,3},... | collective-permute-start | bytes 393224 | tf_op jit(solution)/shard_map/ppermute | solution.py:326
  11.5 5.6 %collective-permute-start.3 = (f32[4,8,1024]{2,1,0:T(8,128)S(1)}, f32[4,8,1024]{2,1,0:T(8,128)S(1)}, u32[]{:S(2)}, u32[]{:S(2)}) collective-permute-start(f32[4,8,1024]{2,1,0:T(8,128)S(1)} %get-tuple-element.34), channel_id=1, source_target_pairs={{0,1},{2,3},{4,5},{6,7},{8,9},{10,11},{12,13},{14,15},{1,0},{3,2},... | collective-permute-start | bytes 393224 | tf_op jit(solution)/shard_map/ppermute | solution.py:327
  11.6 1.2 %collective-permute-start.1 = (f32[16,128]{1,0:T(8,128)S(1)}, f32[16,128]{1,0:T(8,128)S(1)}, u32[]{:S(2)}, u32[]{:S(2)}) collective-permute-start(f32[16,128]{1,0:T(8,128)S(1)} %bitcast.8), channel_id=1, source_target_pairs={{0,16},{16,0},{1,17},{17,1},{2,18},{18,2},{3,19},{19,3},{4,20},{20... | collective-permute-start | bytes 24584 | tf_op jit(solution)/shard_map/ppermute | solution.py:333
  18.0 8.7 %collective-permute-start.4 = (f32[4,8,1024]{2,1,0:T(8,128)S(1)}, f32[4,8,1024]{2,1,0:T(8,128)S(1)}, u32[]{:S(2)}, u32[]{:S(2)}) collective-permute-start(f32[4,8,1024]{2,1,0:T(8,128)S(1)} %get-tuple-element.38), channel_id=1, source_target_pairs={{1,2},{3,4},{5,6},{7,8},{9,10},{11,12},{13,14},{15,0},{2,1},{4,3},... | collective-permute-start | bytes 393224 | tf_op jit(solution)/shard_map/ppermute | solution.py:326
  22.0 5.0 %collective-permute-start.5 = (f32[4,8,1024]{2,1,0:T(8,128)S(1)}, f32[4,8,1024]{2,1,0:T(8,128)S(1)}, u32[]{:S(2)}, u32[]{:S(2)}) collective-permute-start(f32[4,8,1024]{2,1,0:T(8,128)S(1)} %get-tuple-element.39), channel_id=1, source_target_pairs={{0,1},{2,3},{4,5},{6,7},{8,9},{10,11},{12,13},{14,15},{1,0},{3,2},... | collective-permute-start | bytes 393224 | tf_op jit(solution)/shard_map/ppermute | solution.py:327
  22.0 9.6 %copy-start = (bf16[256,4,4,128]{3,2,1,0:T(4,128)(2,1)S(1)}, bf16[256,4,4,128]{3,2,1,0:T(4,128)(2,1)}, u32[]{:S(2)}) copy-start(bf16[256,4,4,128]{3,2,1,0:T(4,128)(2,1)} %param.7) | copy-start | bytes 3145732
  27.8 8.7 %collective-permute-start.6 = (f32[4,8,1024]{2,1,0:T(8,128)S(1)}, f32[4,8,1024]{2,1,0:T(8,128)S(1)}, u32[]{:S(2)}, u32[]{:S(2)}) collective-permute-start(f32[4,8,1024]{2,1,0:T(8,128)S(1)} %get-tuple-element.44), channel_id=1, source_target_pairs={{1,2},{3,4},{5,6},{7,8},{9,10},{11,12},{13,14},{15,0},{2,1},{4,3},... | collective-permute-start | bytes 393224 | tf_op jit(solution)/shard_map/ppermute | solution.py:326
  31.6 5.0 %collective-permute-start.7 = (f32[4,8,1024]{2,1,0:T(8,128)S(1)}, f32[4,8,1024]{2,1,0:T(8,128)S(1)}, u32[]{:S(2)}, u32[]{:S(2)}) collective-permute-start(f32[4,8,1024]{2,1,0:T(8,128)S(1)} %get-tuple-element.45), channel_id=1, source_target_pairs={{0,1},{2,3},{4,5},{6,7},{8,9},{10,11},{12,13},{14,15},{1,0},{3,2},... | collective-permute-start | bytes 393224 | tf_op jit(solution)/shard_map/ppermute | solution.py:327
  37.2 1.6 %collective-permute-start.8 = (f32[32,16,128]{2,1,0:T(8,128)S(1)}, f32[32,16,128]{2,1,0:T(8,128)S(1)}, u32[]{:S(2)}, u32[]{:S(2)}) collective-permute-start(f32[32,16,128]{2,1,0:T(8,128)S(1)} %get-tuple-element.48), channel_id=1, source_target_pairs={{0,16},{16,0},{1,17},{17,1},{2,18},{18,2},{3,19},{19,3},{4,20},{20... | collective-permute-start | bytes 786440 | tf_op jit(solution)/shard_map/ppermute | solution.py:333

commit v20 on v16

--- a/solution.py
+++ b/solution.py
@@ -63,7 +63,7 @@
     return (state * cells + cell) * 4 + node
 
 
-def matrix_kernel(cells, nodes, cell_ref, high_ref, low_ref, edge_ref, halo_ref, place_ref, order_ref):
+def prepare_kernel(cells, nodes, cell_ref, part_ref, high_ref, low_ref, edge_ref, halo_ref, place_ref, order_ref, own_ref):
     rest = cell_ref[...]
     size, count = high_ref.shape[0], cell_ref.shape[0]
     tables = [chosen(size, count, functools.partial(select_target, cell, nodes)) for cell in range(nodes // 4)]
@@ -86,10 +86,12 @@
     place = place.astype(f32)
     halo_ref[...] = jnp.concatenate([high, high, from_halo - high, place, place], 1).astype(bf16)
     order_ref[...] = chosen(*order_ref.shape, functools.partial(cell_order_target, cells))
+    for iz, rows in enumerate(turned(part_ref, order_ref, part_ref.shape[0])):
+        own_ref[iz] = rows
 
 
 def margin_rows_kernel(layer, parts_y, groups, block_ref, out_ref, wide_ref, lines_ref):
-    wide_ref[...] = block_ref[...].astype(f32)
+    wide_ref[: block_ref.shape[0], :] = block_ref[...].astype(f32)
     thickness = block_ref.shape[1]
     tile_cols = out_ref.shape[0] // parts_y
     cols = tile_cols // groups
@@ -97,7 +99,7 @@
         for col in range(tile_cols):
             lines = wide_ref[pl.ds(col * layer + n, parts_y, stride=tile_cols * layer), :]
             lines_ref[pl.ds(col // cols * cols * parts_y + col % cols, parts_y, stride=cols), :] = lines
-        out_ref[:, pl.ds(n * thickness, thickness)] = lines_ref[...].astype(bf16)
+        out_ref[:, pl.ds(n * thickness, thickness)] = lines_ref[: out_ref.shape[0], :].astype(bf16)
 
 
 def roll_cells(value, cells, forward):
@@ -162,11 +164,6 @@
     starts = range(0, ordered.shape[0], 2 * layer)
     values = [ordered[start : start + layer] + ordered[start + layer : start + 2 * layer] for start in starts]
     return [jnp.concatenate([part[:, iz * lanes : (iz + 1) * lanes] for part in values], 1) for iz in range(4)]
-
-
-def turn_kernel(count, part_ref, order_ref, out_ref):
-    for iz, rows in enumerate(turned(part_ref, order_ref, count)):
-        out_ref[iz] = rows
 
 
 def to_cells_kernel(cells, count, own_ref, *refs):
@@ -288,11 +285,8 @@
         target = filtered_ref.at[pl.ds(owners[step] * count, count)]
         copies.append(pltpu.make_async_copy(part_ref, target, sems.at[step]))
     start_all(copies)
-    flat = [ref.reshape(count * layer, thickness) for ref in part_refs]
-    lines = [
-        jnp.concatenate([ref[pl.ds(n, count, stride=layer), :].astype(bf16) for ref in flat], 0)
-        for n in range(layer)
-    ]
+    turned_parts = [jnp.swapaxes(ref[...], 0, 1) for ref in part_refs]
+    lines = [jnp.concatenate([part[n] for part in turned_parts], 0).astype(bf16) for n in range(layer)]
     product = lax.dot_general(
         block_ref[...], jnp.concatenate(lines, 1), (((1,), (1,)), ((), ())), preferred_element_type=f32
     )
@@ -372,16 +366,16 @@
         return lax.dynamic_slice_in_dim(span_rows, lax.rem(me + step, parts_x) * mine, mine, 0)
 
     if parts_x == 2:
-        parts = [span_rows, shifted(span_rows, "px", 1)]
+        parts = [part_for(0), shifted(span_rows, "px", 1)]
     else:
         parts = [part_for(0)] + [shifted(part_for(step), "px", step) for step in reversed(others)]
-    high, low, edge_matrix, halo_matrix, place, order = kernel_call(
-        functools.partial(matrix_kernel, cells, nodes),
-        [matrix, matrix, edge_shape, from_halo, place_shape, table],
-        [cell_matrix],
-        "assemble",
+    own_shape = jax.ShapeDtypeStruct((4, layer, width), f32)
+    high, low, edge_matrix, halo_matrix, place, order, own = kernel_call(
+        functools.partial(prepare_kernel, cells, nodes),
+        [matrix, matrix, edge_shape, from_halo, place_shape, table, own_shape],
+        [cell_matrix, parts[0]],
+        "prepare",
     )
-    own = kernel_call(functools.partial(turn_kernel, mine), jax.ShapeDtypeStruct((4, layer, width), f32), [parts[0], order], "turn")
     field_now, *edges = kernel_call(
         functools.partial(to_cells_kernel, cells, mine),
         [field, message, message],
@@ -409,8 +403,8 @@
                 [block.reshape(block_count * layer, thickness)],
                 "margin_rows",
                 scratch=[
-                    pltpu.VMEM((block_count * layer, thickness), f32),
-                    pltpu.VMEM((block_count, thickness), f32),
+                    pltpu.VMEM(((block_count + tile_cols) * layer, thickness), f32),
+                    pltpu.VMEM((block_count + 8 * tile_cols, thickness), f32),
                 ],
             )
         operands = [field_now, levels, high, low, edge_matrix, place] + ([before] if step > 0 else [])

time: 52 us -> 50.5 us (0.971)
  local copies, waits for them, and re-layouts: 1.89 us -> 1.01 us
    unnamed x8 -> x6, local copies, waits for them, and re-layouts: 1.89 us -> 0.01 us
    dynamic_slice x0 -> x1, local copies, waits for them, and re-layouts: none -> 1 us  [part_for(): lax.dynamic_slice_in_dim(span_rows, lax.rem(me + step, parts_x) * mine, m...]
    pallas_call x13 -> x12, Pallas kernels: 11.9 us -> 11.4 us  [kernel_call(): pl.pallas_call(body, out_shape=outs, in_specs=in_specs or [whole] * len(o...]
  transfers between devices with their start and end apart: 9 -> 9, of which waited for: 8 -> 7; matrix products, arithmetic and copies ran while one was open for 0% -> 2% of each run, Pallas kernels for 14% -> 14%
where the time goes in v20:
time: 50.5 us; the launch traced here: 50.4 us
  starting transfers between devices  15.1 us (30%)
  Pallas kernels  11.4 us (23%)
  blocking collectives  11.2 us (22%)
  waiting for transfers between devices  10.9 us (22%)
  local copies, waits for them, and re-layouts  1.01 us (2%)
  between operations  0.7 us (1%)
    ppermute x3, starting transfers between devices, swapped(): other = lax.ppermute(other, 'py', others + [(b, a) for a, b in others])  14.5 us
    pallas_call x12, Pallas kernels, kernel_call(): pl.pallas_call(body, out_shape=outs, in_specs=in_specs or [whole] * len(o...  11.4 us
    all_to_all x1, blocking collectives, local(): tiles = lax.all_to_all(tiles, ('px', 'py'), 0, 0, tiled=True)  11.2 us
    ppermute x3, waiting for transfers between devices, swapped(): other = lax.ppermute(other, 'py', others + [(b, a) for a, b in others])  6.56 us
    ppermute x3, waiting for transfers between devices, shifted(): lax.ppermute(value, axis, [(source, (source + steps) % count) for source...  2.67 us
    ppermute x3, waiting for transfers between devices, swapped(): pair = lax.ppermute(pair, 'py', pairs + [(b, a) for a, b in pairs])  1.69 us
  transfers between devices with their start and end apart: 9, of which 7 were waited for; matrix products, arithmetic and copies ran while one was open for 2% of the time, Pallas kernels for 14%

profile of v20, /device:TPU:0, one launch (start us, length us, event | category | flops | bytes accessed | tf_op | source)
XLA Modules:
  0.0 50.4 jit_solution(11417301717848602661)
XLA Ops:
  0.6 0.5 %collective-permute-start = (f32[64,16,128]{2,1,0:T(8,128)}, f32[64,16,128]{2,1,0:T(8,128)S(1)}, u32[]{:S(2)}, u32[]{:S(2)}) collective-permute-start(f32[64,16,128]{2,1,0:T(8,128)} %bitcast.10), channel_id=1, source_target_pairs={{0,16},{16,0},{1,17},{17,1},{2,18},{18,2},{3,19},{19,3},{4,20},{20... | collective-permute-start | bytes 1572872 | tf_op jit(solution)/shard_map/ppermute | solution.py:321
  1.1 1.0 %constant_dynamic-slice_fusion.part_ref = f32[32,16,128]{2,1,0:T(8,128)S(1)} fusion(f32[64,16,128]{2,1,0:T(8,128)} %bitcast.11, s32[]{:T(128)S(6)} %select_n.3), kind=kLoop, calls=%fused_computation | loop fusion | bytes 524292 | tf_op jit(solution)/shard_map/dynamic_slice | solution.py:366
  2.2 0.9 %prepare.1 = (bf16[208,208]{1,0:T(8,128)(2,1)S(1)}, bf16[208,208]{1,0:T(8,128)(2,1)S(1)}, bf16[80,160]{1,0:T(8,128)(2,1)S(1)}, bf16[160,208]{1,0:T(8,128)(2,1)S(...) custom-call(f32[125,125]{1,0:T(8,128)S(1)} %copy-done.1, ...), custom_call_target="tpu_custom_call" | custom-call | tf_op jit(solution)/shard_map/prepare/pallas_call | solution.py:326
  3.1 0.7 %to_cells.1 = (f32[4,32,1024]{2,1,0:T(8,128)S(1)}, f32[4,8,1024]{2,1,0:T(8,128)S(1)}, f32[4,8,1024]{2,1,0:T(8,128)S(1)}) custom-call(f32[4,16,1024]{2,1,0:T(8,128)S(1)} %get-tuple-element.28.own_ref, f32[64,16,128]{2,1,0:T(8,128)S(1)} %collective-permute-done.refs_0_, bf16[512,512]{1,0:T(8,128)(2,1)S(1)} %get-tuple-element.29.refs_1_, ...), custom_call_target="tpu_custom_call" | custom-call | tf_op jit(solution)/shard_map/to_cells/pallas_call | solution.py:326
  3.8 6.7 %collective-permute-start.2 = (f32[4,8,1024]{2,1,0:T(8,128)S(1)}, f32[4,8,1024]{2,1,0:T(8,128)S(1)}, u32[]{:S(2)}, u32[]{:S(2)}) collective-permute-start(f32[4,8,1024]{2,1,0:T(8,128)S(1)} %get-tuple-element.35), channel_id=1, source_target_pairs={{1,2},{3,4},{5,6},{7,8},{9,10},{11,12},{13,14},{15,0},{2,1},{4,3},... | collective-permute-start | bytes 393224 | tf_op jit(solution)/shard_map/ppermute | solution.py:314
  10.5 1.1 %collective-permute-done.1.refs_1_ = f32[16,128]{1,0:T(8,128)S(1)} collective-permute-done((f32[16,128]{1,0:T(8,128)S(1)}, f32[16,128]{1,0:T(8,128)S(1)}, u32[]{:S(2)}, u32[]{:S(2)}) %collective-permute-start.1) | collective-permute-done | bytes 8224 | tf_op jit(solution)/shard_map/ppermute | solution.py:321
  11.8 1.3 %inner.3.inner_ref = f32[4,32,1024]{2,1,0:T(8,128)S(1)} custom-call(f32[4,32,1024]{2,1,0:T(8,128)S(1)} %get-tuple-element.32.refs_0_.refs_6_, f32[4,32,128]{2,1,0:T(8,128)S(1)} %levels.1.refs_1_, bf16[208,208]{1,0:T(8,128)(2,1)S(1)} %get-tuple-element.33.refs_2_, bf16[208,208]{1,0:T(8,128)(2,1)S(1)} %get-tuple-element.31.refs_3_.low_ref, ...), custom_call_target="tpu_custom_call" | custom-call | tf_op jit(solution)/shard_map/inner/pallas_call | solution.py:326
  13.2 1.4 %collective-permute-done.2.from_other_ref = f32[4,8,1024]{2,1,0:T(8,128)S(1)} collective-permute-done((f32[4,8,1024]{2,1,0:T(8,128)S(1)}, f32[4,8,1024]{2,1,0:T(8,128)S(1)}, u32[]{:S(2)}, u32[]{:S(2)}) %collective-permute-start.2) | collective-permute-done | bytes 131104 | tf_op jit(solution)/shard_map/ppermute | solution.py:314
  14.6 1.4 %collective-permute-done.3.from_pair_ref = f32[4,8,1024]{2,1,0:T(8,128)S(1)} collective-permute-done((f32[4,8,1024]{2,1,0:T(8,128)S(1)}, f32[4,8,1024]{2,1,0:T(8,128)S(1)}, u32[]{:S(2)}, u32[]{:S(2)}) %collective-permute-start.3) | collective-permute-done | bytes 131104 | tf_op jit(solution)/shard_map/ppermute | solution.py:315
  15.9 0.8 %finish.2 = (f32[4,32,1024]{2,1,0:T(8,128)S(1)}, f32[4,8,1024]{2,1,0:T(8,128)S(1)}, f32[4,8,1024]{2,1,0:T(8,128)S(1)}) custom-call(f32[4,32,1024]{2,1,0:T(8,128)S(1)} %inner.3.inner_ref, f32[4,8,1024]{2,1,0:T(8,128)S(1)} %collective-permute-done.2.from_other_ref, f32[4,8,1024]{2,1,0:T(8,128)S(1)} %collective-permute-done.3.from_pair_ref, ...), custom_call_target="tpu_custom_call" | custom-call | tf_op jit(solution)/shard_map/finish/pallas_call | solution.py:326
  16.7 4.1 %collective-permute-start.4 = (f32[4,8,1024]{2,1,0:T(8,128)S(1)}, f32[4,8,1024]{2,1,0:T(8,128)S(1)}, u32[]{:S(2)}, u32[]{:S(2)}) collective-permute-start(f32[4,8,1024]{2,1,0:T(8,128)S(1)} %get-tuple-element.40), channel_id=1, source_target_pairs={{1,2},{3,4},{5,6},{7,8},{9,10},{11,12},{13,14},{15,0},{2,1},{4,3},... | collective-permute-start | bytes 393224 | tf_op jit(solution)/shard_map/ppermute | solution.py:314
  20.8 1.3 %inner.4.inner_ref = f32[4,32,1024]{2,1,0:T(8,128)S(1)} custom-call(f32[4,32,1024]{2,1,0:T(8,128)S(1)} %get-tuple-element.39.refs_0_.refs_6_, f32[4,32,128]{2,1,0:T(8,128)S(1)} %levels.1.refs_1_, bf16[208,208]{1,0:T(8,128)(2,1)S(1)} %get-tuple-element.33.refs_2_, bf16[208,208]{1,0:T(8,128)(2,1)S(1)} %get-tuple-element.31.refs_3_.low_ref, ...), custom_call_target="tpu_custom_call" | custom-call | tf_op jit(solution)/shard_map/inner/pallas_call | solution.py:326
  22.1 3.3 %collective-permute-done.4.from_other_ref = f32[4,8,1024]{2,1,0:T(8,128)S(1)} collective-permute-done((f32[4,8,1024]{2,1,0:T(8,128)S(1)}, f32[4,8,1024]{2,1,0:T(8,128)S(1)}, u32[]{:S(2)}, u32[]{:S(2)}) %collective-permute-start.4) | collective-permute-done | bytes 131104 | tf_op jit(solution)/shard_map/ppermute | solution.py:314
  25.4 0.3 collective-permute-done.5.from_pair_ref
  25.8 0.8 %finish.3 = (f32[4,32,1024]{2,1,0:T(8,128)S(1)}, f32[4,8,1024]{2,1,0:T(8,128)S(1)}, f32[4,8,1024]{2,1,0:T(8,128)S(1)}) custom-call(f32[4,32,1024]{2,1,0:T(8,128)S(1)} %inner.4.inner_ref, f32[4,8,1024]{2,1,0:T(8,128)S(1)} %collective-permute-done.4.from_other_ref, f32[4,8,1024]{2,1,0:T(8,128)S(1)} %collective-permute-done.5.from_pair_ref, ...), custom_call_target="tpu_custom_call" | custom-call | tf_op jit(solution)/shard_map/finish/pallas_call | solution.py:326
  26.6 3.7 %collective-permute-start.6 = (f32[4,8,1024]{2,1,0:T(8,128)S(1)}, f32[4,8,1024]{2,1,0:T(8,128)S(1)}, u32[]{:S(2)}, u32[]{:S(2)}) collective-permute-start(f32[4,8,1024]{2,1,0:T(8,128)S(1)} %get-tuple-element.46), channel_id=1, source_target_pairs={{1,2},{3,4},{5,6},{7,8},{9,10},{11,12},{13,14},{15,0},{2,1},{4,3},... | collective-permute-start | bytes 393224 | tf_op jit(solution)/shard_map/ppermute | solution.py:314
  30.3 1.6 %margin_rows.1.refs_2_ = bf16[256,2048]{1,0:T(8,128)(2,1)S(1)} custom-call(bf16[4096,128]{1,0:T(8,128)(2,1)S(1)} %bitcast.6), custom_call_target="tpu_custom_call" | custom-call | tf_op jit(solution)/shard_map/margin_rows/pallas_call | solution.py:326
  31.9 1.5 %inner.5 = (f32[4,32,1024]{2,1,0:T(8,128)S(1)}, bf16[512,512]{1,0:T(8,128)(2,1)S(1)}) custom-call(f32[4,32,1024]{2,1,0:T(8,128)S(1)} %get-tuple-element.42.refs_0_, f32[4,32,128]{2,1,0:T(8,128)S(1)} %levels.1.refs_1_, bf16[208,208]{1,0:T(8,128)(2,1)S(1)} %get-tuple-element.33.refs_2_, bf16[208,208]{1,0:T(8,128)(2,1)S(1)} %get-tuple-element.31.refs_3_.low_ref, ...), custom_call_target="tpu_custom_call" | custom-call | tf_op jit(solution)/shard_map/inner/pallas_call | solution.py:326
  33.5 1.8 %collective-permute-done.6.refs_1_ = f32[4,8,1024]{2,1,0:T(8,128)S(1)} collective-permute-done((f32[4,8,1024]{2,1,0:T(8,128)S(1)}, f32[4,8,1024]{2,1,0:T(8,128)S(1)}, u32[]{:S(2)}, u32[]{:S(2)}) %collective-permute-start.6) | collective-permute-done | bytes 131104 | tf_op jit(solution)/shard_map/ppermute | solution.py:314
  35.3 0.8 %from_cells.1 = (f32[32,16,128]{2,1,0:T(8,128)S(1)}, f32[32,16,128]{2,1,0:T(8,128)S(1)}) custom-call(f32[4,32,1024]{2,1,0:T(8,128)S(1)} %get-tuple-element.45.refs_0_, f32[4,8,1024]{2,1,0:T(8,128)S(1)} %collective-permute-done.6.refs_1_, f32[4,8,1024]{2,1,0:T(8,128)S(1)} %collective-permute-done.7.refs_2_, ...), custom_call_target="tpu_custom_call" | custom-call | tf_op jit(solution)/shard_map/from_cells/pallas_call | solution.py:326
  36.1 1.5 %collective-permute-done.8.refs_1_ = f32[32,16,128]{2,1,0:T(8,128)S(1)} collective-permute-done((f32[32,16,128]{2,1,0:T(8,128)S(1)}, f32[32,16,128]{2,1,0:T(8,128)S(1)}, u32[]{:S(2)}, u32[]{:S(2)}) %collective-permute-start.8) | collective-permute-done | bytes 262176 | tf_op jit(solution)/shard_map/ppermute | solution.py:321
  37.7 0.8 %margin.1 = (f32[2,64,128]{2,1,0:T(8,128)S(1)}, f32[64,16,128]{2,1,0:T(8,128)}) custom-call(f32[32,16,128]{2,1,0:T(8,128)S(1)} %get-tuple-element.49.refs_0_, f32[32,16,128]{2,1,0:T(8,128)S(1)} %collective-permute-done.8.refs_1_, bf16[256,2048]{1,0:T(8,128)(2,1)S(1)} %margin_rows.1.refs_2_), custom_call_target="tpu_custom_call" | custom-call | tf_op jit(solution)/shard_map/margin/pallas_call | solution.py:326
  38.5 11.2 %all_to_all.5.tiles_ref = f32[32,4,128]{2,1,0:T(4,128)S(1)} all-to-all(f32[32,4,128]{2,1,0:T(4,128)S(1)} %bitcast.7), channel_id=1, replica_groups=mesh['px'=2,'py'=16] {'px','py'}, dimensions={0} | all-to-all | bytes 131072 | tf_op jit(solution)/shard_map/all_to_all | solution.py:447
  49.7 0.7 %tile_sum.1 = f32[16,32]{1,0:T(8,128)} custom-call(f32[32,4,128]{2,1,0:T(4,128)S(1)} %all_to_all.5.tiles_ref), custom_call_target="tpu_custom_call" | custom-call | tf_op jit(solution)/shard_map/tile_sum/pallas_call | solution.py:326
  (14 shorter events, 0.3 us)
Async XLA Ops:
  0.6 2.4 %collective-permute-start = (f32[64,16,128]{2,1,0:T(8,128)}, f32[64,16,128]{2,1,0:T(8,128)S(1)}, u32[]{:S(2)}, u32[]{:S(2)}) collective-permute-start(f32[64,16,128]{2,1,0:T(8,128)} %bitcast.10), channel_id=1, source_target_pairs={{0,16},{16,0},{1,17},{17,1},{2,18},{18,2},{3,19},{19,3},{4,20},{20... | collective-permute-start | bytes 1572872 | tf_op jit(solution)/shard_map/ppermute | solution.py:321
  1.1 1.0 %copy-start.1 = (f32[125,125]{1,0:T(8,128)S(1)}, f32[125,125]{1,0:T(8,128)}, u32[]{:S(2)}) copy-start(f32[125,125]{1,0:T(8,128)} %cell_ref.1) | copy-start | bytes 187504
  3.1 7.4 %copy-start.2 = (f32[4,4,128]{2,1,0:T(4,128)S(1)}, f32[4,4,128]{2,1,0:T(4,128)}, u32[]{:S(2)}) copy-start(f32[4,4,128]{2,1,0:T(4,128)} %param.5) | copy-start | bytes 24580
  3.8 10.8 %collective-permute-start.2 = (f32[4,8,1024]{2,1,0:T(8,128)S(1)}, f32[4,8,1024]{2,1,0:T(8,128)S(1)}, u32[]{:S(2)}, u32[]{:S(2)}) collective-permute-start(f32[4,8,1024]{2,1,0:T(8,128)S(1)} %get-tuple-element.35), channel_id=1, source_target_pairs={{1,2},{3,4},{5,6},{7,8},{9,10},{11,12},{13,14},{15,0},{2,1},{4,3},... | collective-permute-start | bytes 393224 | tf_op jit(solution)/shard_map/ppermute | solution.py:314
  10.5 5.4 %collective-permute-start.3 = (f32[4,8,1024]{2,1,0:T(8,128)S(1)}, f32[4,8,1024]{2,1,0:T(8,128)S(1)}, u32[]{:S(2)}, u32[]{:S(2)}) collective-permute-start(f32[4,8,1024]{2,1,0:T(8,128)S(1)} %get-tuple-element.36), channel_id=1, source_target_pairs={{0,1},{2,3},{4,5},{6,7},{8,9},{10,11},{12,13},{14,15},{1,0},{3,2},... | collective-permute-start | bytes 393224 | tf_op jit(solution)/shard_map/ppermute | solution.py:315
  10.5 1.2 %collective-permute-start.1 = (f32[16,128]{1,0:T(8,128)S(1)}, f32[16,128]{1,0:T(8,128)S(1)}, u32[]{:S(2)}, u32[]{:S(2)}) collective-permute-start(f32[16,128]{1,0:T(8,128)S(1)} %bitcast.8), channel_id=1, source_target_pairs={{0,16},{16,0},{1,17},{17,1},{2,18},{18,2},{3,19},{19,3},{4,20},{20... | collective-permute-start | bytes 24584 | tf_op jit(solution)/shard_map/ppermute | solution.py:321
  16.7 8.7 %collective-permute-start.4 = (f32[4,8,1024]{2,1,0:T(8,128)S(1)}, f32[4,8,1024]{2,1,0:T(8,128)S(1)}, u32[]{:S(2)}, u32[]{:S(2)}) collective-permute-start(f32[4,8,1024]{2,1,0:T(8,128)S(1)} %get-tuple-element.40), channel_id=1, source_target_pairs={{1,2},{3,4},{5,6},{7,8},{9,10},{11,12},{13,14},{15,0},{2,1},{4,3},... | collective-permute-start | bytes 393224 | tf_op jit(solution)/shard_map/ppermute | solution.py:314
  20.8 5.0 %collective-permute-start.5 = (f32[4,8,1024]{2,1,0:T(8,128)S(1)}, f32[4,8,1024]{2,1,0:T(8,128)S(1)}, u32[]{:S(2)}, u32[]{:S(2)}) collective-permute-start(f32[4,8,1024]{2,1,0:T(8,128)S(1)} %get-tuple-element.41), channel_id=1, source_target_pairs={{0,1},{2,3},{4,5},{6,7},{8,9},{10,11},{12,13},{14,15},{1,0},{3,2},... | collective-permute-start | bytes 393224 | tf_op jit(solution)/shard_map/ppermute | solution.py:315
  20.8 9.5 %copy-start = (bf16[256,4,4,128]{3,2,1,0:T(4,128)(2,1)S(1)}, bf16[256,4,4,128]{3,2,1,0:T(4,128)(2,1)}, u32[]{:S(2)}) copy-start(bf16[256,4,4,128]{3,2,1,0:T(4,128)(2,1)} %param.7) | copy-start | bytes 3145732
  26.6 8.7 %collective-permute-start.6 = (f32[4,8,1024]{2,1,0:T(8,128)S(1)}, f32[4,8,1024]{2,1,0:T(8,128)S(1)}, u32[]{:S(2)}, u32[]{:S(2)}) collective-permute-start(f32[4,8,1024]{2,1,0:T(8,128)S(1)} %get-tuple-element.46), channel_id=1, source_target_pairs={{1,2},{3,4},{5,6},{7,8},{9,10},{11,12},{13,14},{15,0},{2,1},{4,3},... | collective-permute-start | bytes 393224 | tf_op jit(solution)/shard_map/ppermute | solution.py:314
  30.3 5.0 %collective-permute-start.7 = (f32[4,8,1024]{2,1,0:T(8,128)S(1)}, f32[4,8,1024]{2,1,0:T(8,128)S(1)}, u32[]{:S(2)}, u32[]{:S(2)}) collective-permute-start(f32[4,8,1024]{2,1,0:T(8,128)S(1)} %get-tuple-element.47), channel_id=1, source_target_pairs={{0,1},{2,3},{4,5},{6,7},{8,9},{10,11},{12,13},{14,15},{1,0},{3,2},... | collective-permute-start | bytes 393224 | tf_op jit(solution)/shard_map/ppermute | solution.py:315
  36.1 1.6 %collective-permute-start.8 = (f32[32,16,128]{2,1,0:T(8,128)S(1)}, f32[32,16,128]{2,1,0:T(8,128)S(1)}, u32[]{:S(2)}, u32[]{:S(2)}) collective-permute-start(f32[32,16,128]{2,1,0:T(8,128)S(1)} %get-tuple-element.50), channel_id=1, source_target_pairs={{0,16},{16,0},{1,17},{17,1},{2,18},{18,2},{3,19},{19,3},{4,20},{20... | collective-permute-start | bytes 786440 | tf_op jit(solution)/shard_map/ppermute | solution.py:321

commit v21 on v20

--- a/solution.py
+++ b/solution.py
@@ -280,10 +280,11 @@
     me = lax.axis_index("px")
     count, layer, thickness = part_refs[0].shape
     owners = [lax.rem(me + (parts_x - step), parts_x) for step in range(parts_x)]
-    copies = []
+    copies, run = [], count // sems.shape[1]
     for step, part_ref in enumerate(part_refs):
-        target = filtered_ref.at[pl.ds(owners[step] * count, count)]
-        copies.append(pltpu.make_async_copy(part_ref, target, sems.at[step]))
+        for piece in range(sems.shape[1]):
+            target = filtered_ref.at[pl.ds(owners[step] * count + piece * run, run)]
+            copies.append(pltpu.make_async_copy(part_ref.at[pl.ds(piece * run, run)], target, sems.at[step, piece]))
     start_all(copies)
     turned_parts = [jnp.swapaxes(ref[...], 0, 1) for ref in part_refs]
     lines = [jnp.concatenate([part[n] for part in turned_parts], 0).astype(bf16) for n in range(layer)]
@@ -440,7 +441,7 @@
         ],
         received + [ordered],
         "margin",
-        scratch=[pltpu.SemaphoreType.DMA((parts_x,))],
+        scratch=[pltpu.SemaphoreType.DMA((parts_x, 8))],
         out_specs=[whole, anywhere],
     )
     tiles = tiles.reshape(parts_x * parts_y, tile_cols // groups, groups * tile_rows)

time: 50.5 us -> 51 us (level)
  transfers between devices with their start and end apart: 9 -> 9, of which waited for: 7 -> 7; matrix products, arithmetic and copies ran while one was open for 2% -> 2% of each run, Pallas kernels for 14% -> 13%
where the time goes in v21:
time: 51 us; the launch traced here: 50.9 us
  starting transfers between devices  15.1 us (30%)
  Pallas kernels  11.9 us (23%)
  blocking collectives  11.2 us (22%)
  waiting for transfers between devices  10.9 us (21%)
  local copies, waits for them, and re-layouts  1.01 us (2%)
  between operations  0.7 us (1%)
    ppermute x3, starting transfers between devices, swapped(): other = lax.ppermute(other, 'py', others + [(b, a) for a, b in others])  14.5 us
    pallas_call x12, Pallas kernels, kernel_call(): pl.pallas_call(body, out_shape=outs, in_specs=in_specs or [whole] * len(o...  11.9 us
    all_to_all x1, blocking collectives, local(): tiles = lax.all_to_all(tiles, ('px', 'py'), 0, 0, tiled=True)  11.2 us
    ppermute x3, waiting for transfers between devices, swapped(): other = lax.ppermute(other, 'py', others + [(b, a) for a, b in others])  6.56 us
    ppermute x3, waiting for transfers between devices, shifted(): lax.ppermute(value, axis, [(source, (source + steps) % count) for source...  2.67 us
    ppermute x3, waiting for transfers between devices, swapped(): pair = lax.ppermute(pair, 'py', pairs + [(b, a) for a, b in pairs])  1.69 us
  transfers between devices with their start and end apart: 9, of which 7 were waited for; matrix products, arithmetic and copies ran while one was open for 2% of the time, Pallas kernels for 13%

profile of v21, /device:TPU:0, one launch (start us, length us, event | category | flops | bytes accessed | tf_op | source)
XLA Modules:
  0.0 50.9 jit_solution(751296399650385666)
XLA Ops:
  0.6 0.5 %collective-permute-start = (f32[64,16,128]{2,1,0:T(8,128)}, f32[64,16,128]{2,1,0:T(8,128)S(1)}, u32[]{:S(2)}, u32[]{:S(2)}) collective-permute-start(f32[64,16,128]{2,1,0:T(8,128)} %bitcast.10), channel_id=1, source_target_pairs={{0,16},{16,0},{1,17},{17,1},{2,18},{18,2},{3,19},{19,3},{4,20},{20... | collective-permute-start | bytes 1572872 | tf_op jit(solution)/shard_map/ppermute | solution.py:322
  1.1 1.0 %constant_dynamic-slice_fusion.part_ref = f32[32,16,128]{2,1,0:T(8,128)S(1)} fusion(f32[64,16,128]{2,1,0:T(8,128)} %bitcast.11, s32[]{:T(128)S(6)} %select_n.3), kind=kLoop, calls=%fused_computation | loop fusion | bytes 524292 | tf_op jit(solution)/shard_map/dynamic_slice | solution.py:367
  2.2 0.9 %prepare.1 = (bf16[208,208]{1,0:T(8,128)(2,1)S(1)}, bf16[208,208]{1,0:T(8,128)(2,1)S(1)}, bf16[80,160]{1,0:T(8,128)(2,1)S(1)}, bf16[160,208]{1,0:T(8,128)(2,1)S(...) custom-call(f32[125,125]{1,0:T(8,128)S(1)} %copy-done.1, ...), custom_call_target="tpu_custom_call" | custom-call | tf_op jit(solution)/shard_map/prepare/pallas_call | solution.py:327
  3.1 0.7 %to_cells.1 = (f32[4,32,1024]{2,1,0:T(8,128)S(1)}, f32[4,8,1024]{2,1,0:T(8,128)S(1)}, f32[4,8,1024]{2,1,0:T(8,128)S(1)}) custom-call(f32[4,16,1024]{2,1,0:T(8,128)S(1)} %get-tuple-element.28.own_ref, f32[64,16,128]{2,1,0:T(8,128)S(1)} %collective-permute-done.refs_0_, bf16[512,512]{1,0:T(8,128)(2,1)S(1)} %get-tuple-element.29.refs_1_, ...), custom_call_target="tpu_custom_call" | custom-call | tf_op jit(solution)/shard_map/to_cells/pallas_call | solution.py:327
  3.8 6.7 %collective-permute-start.2 = (f32[4,8,1024]{2,1,0:T(8,128)S(1)}, f32[4,8,1024]{2,1,0:T(8,128)S(1)}, u32[]{:S(2)}, u32[]{:S(2)}) collective-permute-start(f32[4,8,1024]{2,1,0:T(8,128)S(1)} %get-tuple-element.35), channel_id=1, source_target_pairs={{1,2},{3,4},{5,6},{7,8},{9,10},{11,12},{13,14},{15,0},{2,1},{4,3},... | collective-permute-start | bytes 393224 | tf_op jit(solution)/shard_map/ppermute | solution.py:315
  10.5 1.1 %collective-permute-done.1.refs_1_ = f32[16,128]{1,0:T(8,128)S(1)} collective-permute-done((f32[16,128]{1,0:T(8,128)S(1)}, f32[16,128]{1,0:T(8,128)S(1)}, u32[]{:S(2)}, u32[]{:S(2)}) %collective-permute-start.1) | collective-permute-done | bytes 8224 | tf_op jit(solution)/shard_map/ppermute | solution.py:322
  11.8 1.3 %inner.3.inner_ref = f32[4,32,1024]{2,1,0:T(8,128)S(1)} custom-call(f32[4,32,1024]{2,1,0:T(8,128)S(1)} %get-tuple-element.32.refs_0_.refs_6_, f32[4,32,128]{2,1,0:T(8,128)S(1)} %levels.1.refs_1_, bf16[208,208]{1,0:T(8,128)(2,1)S(1)} %get-tuple-element.33.refs_2_, bf16[208,208]{1,0:T(8,128)(2,1)S(1)} %get-tuple-element.31.refs_3_.low_ref, ...), custom_call_target="tpu_custom_call" | custom-call | tf_op jit(solution)/shard_map/inner/pallas_call | solution.py:327
  13.2 1.4 %collective-permute-done.2.from_other_ref = f32[4,8,1024]{2,1,0:T(8,128)S(1)} collective-permute-done((f32[4,8,1024]{2,1,0:T(8,128)S(1)}, f32[4,8,1024]{2,1,0:T(8,128)S(1)}, u32[]{:S(2)}, u32[]{:S(2)}) %collective-permute-start.2) | collective-permute-done | bytes 131104 | tf_op jit(solution)/shard_map/ppermute | solution.py:315
  14.6 1.4 %collective-permute-done.3.from_pair_ref = f32[4,8,1024]{2,1,0:T(8,128)S(1)} collective-permute-done((f32[4,8,1024]{2,1,0:T(8,128)S(1)}, f32[4,8,1024]{2,1,0:T(8,128)S(1)}, u32[]{:S(2)}, u32[]{:S(2)}) %collective-permute-start.3) | collective-permute-done | bytes 131104 | tf_op jit(solution)/shard_map/ppermute | solution.py:316
  15.9 0.8 %finish.2 = (f32[4,32,1024]{2,1,0:T(8,128)S(1)}, f32[4,8,1024]{2,1,0:T(8,128)S(1)}, f32[4,8,1024]{2,1,0:T(8,128)S(1)}) custom-call(f32[4,32,1024]{2,1,0:T(8,128)S(1)} %inner.3.inner_ref, f32[4,8,1024]{2,1,0:T(8,128)S(1)} %collective-permute-done.2.from_other_ref, f32[4,8,1024]{2,1,0:T(8,128)S(1)} %collective-permute-done.3.from_pair_ref, ...), custom_call_target="tpu_custom_call" | custom-call | tf_op jit(solution)/shard_map/finish/pallas_call | solution.py:327
  16.7 4.1 %collective-permute-start.4 = (f32[4,8,1024]{2,1,0:T(8,128)S(1)}, f32[4,8,1024]{2,1,0:T(8,128)S(1)}, u32[]{:S(2)}, u32[]{:S(2)}) collective-permute-start(f32[4,8,1024]{2,1,0:T(8,128)S(1)} %get-tuple-element.40), channel_id=1, source_target_pairs={{1,2},{3,4},{5,6},{7,8},{9,10},{11,12},{13,14},{15,0},{2,1},{4,3},... | collective-permute-start | bytes 393224 | tf_op jit(solution)/shard_map/ppermute | solution.py:315
  20.8 1.3 %inner.4.inner_ref = f32[4,32,1024]{2,1,0:T(8,128)S(1)} custom-call(f32[4,32,1024]{2,1,0:T(8,128)S(1)} %get-tuple-element.39.refs_0_.refs_6_, f32[4,32,128]{2,1,0:T(8,128)S(1)} %levels.1.refs_1_, bf16[208,208]{1,0:T(8,128)(2,1)S(1)} %get-tuple-element.33.refs_2_, bf16[208,208]{1,0:T(8,128)(2,1)S(1)} %get-tuple-element.31.refs_3_.low_ref, ...), custom_call_target="tpu_custom_call" | custom-call | tf_op jit(solution)/shard_map/inner/pallas_call | solution.py:327
  22.1 3.3 %collective-permute-done.4.from_other_ref = f32[4,8,1024]{2,1,0:T(8,128)S(1)} collective-permute-done((f32[4,8,1024]{2,1,0:T(8,128)S(1)}, f32[4,8,1024]{2,1,0:T(8,128)S(1)}, u32[]{:S(2)}, u32[]{:S(2)}) %collective-permute-start.4) | collective-permute-done | bytes 131104 | tf_op jit(solution)/shard_map/ppermute | solution.py:315
  25.4 0.3 collective-permute-done.5.from_pair_ref
  25.8 0.8 %finish.3 = (f32[4,32,1024]{2,1,0:T(8,128)S(1)}, f32[4,8,1024]{2,1,0:T(8,128)S(1)}, f32[4,8,1024]{2,1,0:T(8,128)S(1)}) custom-call(f32[4,32,1024]{2,1,0:T(8,128)S(1)} %inner.4.inner_ref, f32[4,8,1024]{2,1,0:T(8,128)S(1)} %collective-permute-done.4.from_other_ref, f32[4,8,1024]{2,1,0:T(8,128)S(1)} %collective-permute-done.5.from_pair_ref, ...), custom_call_target="tpu_custom_call" | custom-call | tf_op jit(solution)/shard_map/finish/pallas_call | solution.py:327
  26.6 3.7 %collective-permute-start.6 = (f32[4,8,1024]{2,1,0:T(8,128)S(1)}, f32[4,8,1024]{2,1,0:T(8,128)S(1)}, u32[]{:S(2)}, u32[]{:S(2)}) collective-permute-start(f32[4,8,1024]{2,1,0:T(8,128)S(1)} %get-tuple-element.46), channel_id=1, source_target_pairs={{1,2},{3,4},{5,6},{7,8},{9,10},{11,12},{13,14},{15,0},{2,1},{4,3},... | collective-permute-start | bytes 393224 | tf_op jit(solution)/shard_map/ppermute | solution.py:315
  30.3 1.6 %margin_rows.1.refs_2_ = bf16[256,2048]{1,0:T(8,128)(2,1)S(1)} custom-call(bf16[4096,128]{1,0:T(8,128)(2,1)S(1)} %bitcast.6), custom_call_target="tpu_custom_call" | custom-call | tf_op jit(solution)/shard_map/margin_rows/pallas_call | solution.py:327
  31.9 1.5 %inner.5 = (f32[4,32,1024]{2,1,0:T(8,128)S(1)}, bf16[512,512]{1,0:T(8,128)(2,1)S(1)}) custom-call(f32[4,32,1024]{2,1,0:T(8,128)S(1)} %get-tuple-element.42.refs_0_, f32[4,32,128]{2,1,0:T(8,128)S(1)} %levels.1.refs_1_, bf16[208,208]{1,0:T(8,128)(2,1)S(1)} %get-tuple-element.33.refs_2_, bf16[208,208]{1,0:T(8,128)(2,1)S(1)} %get-tuple-element.31.refs_3_.low_ref, ...), custom_call_target="tpu_custom_call" | custom-call | tf_op jit(solution)/shard_map/inner/pallas_call | solution.py:327
  33.5 1.8 %collective-permute-done.6.refs_1_ = f32[4,8,1024]{2,1,0:T(8,128)S(1)} collective-permute-done((f32[4,8,1024]{2,1,0:T(8,128)S(1)}, f32[4,8,1024]{2,1,0:T(8,128)S(1)}, u32[]{:S(2)}, u32[]{:S(2)}) %collective-permute-start.6) | collective-permute-done | bytes 131104 | tf_op jit(solution)/shard_map/ppermute | solution.py:315
  35.3 0.8 %from_cells.1 = (f32[32,16,128]{2,1,0:T(8,128)S(1)}, f32[32,16,128]{2,1,0:T(8,128)S(1)}) custom-call(f32[4,32,1024]{2,1,0:T(8,128)S(1)} %get-tuple-element.45.refs_0_, f32[4,8,1024]{2,1,0:T(8,128)S(1)} %collective-permute-done.6.refs_1_, f32[4,8,1024]{2,1,0:T(8,128)S(1)} %collective-permute-done.7.refs_2_, ...), custom_call_target="tpu_custom_call" | custom-call | tf_op jit(solution)/shard_map/from_cells/pallas_call | solution.py:327
  36.1 1.5 %collective-permute-done.8.refs_1_ = f32[32,16,128]{2,1,0:T(8,128)S(1)} collective-permute-done((f32[32,16,128]{2,1,0:T(8,128)S(1)}, f32[32,16,128]{2,1,0:T(8,128)S(1)}, u32[]{:S(2)}, u32[]{:S(2)}) %collective-permute-start.8) | collective-permute-done | bytes 262176 | tf_op jit(solution)/shard_map/ppermute | solution.py:322
  37.7 1.3 %margin.1 = (f32[2,64,128]{2,1,0:T(8,128)S(1)}, f32[64,16,128]{2,1,0:T(8,128)}) custom-call(f32[32,16,128]{2,1,0:T(8,128)S(1)} %get-tuple-element.49.refs_0_, f32[32,16,128]{2,1,0:T(8,128)S(1)} %collective-permute-done.8.refs_1_, bf16[256,2048]{1,0:T(8,128)(2,1)S(1)} %margin_rows.1.refs_2_), custom_call_target="tpu_custom_call" | custom-call | tf_op jit(solution)/shard_map/margin/pallas_call | solution.py:327
  39.0 11.2 %all_to_all.5.tiles_ref = f32[32,4,128]{2,1,0:T(4,128)S(1)} all-to-all(f32[32,4,128]{2,1,0:T(4,128)S(1)} %bitcast.7), channel_id=1, replica_groups=mesh['px'=2,'py'=16] {'px','py'}, dimensions={0} | all-to-all | bytes 131072 | tf_op jit(solution)/shard_map/all_to_all | solution.py:448
  50.2 0.7 %tile_sum.1 = f32[16,32]{1,0:T(8,128)} custom-call(f32[32,4,128]{2,1,0:T(4,128)S(1)} %all_to_all.5.tiles_ref), custom_call_target="tpu_custom_call" | custom-call | tf_op jit(solution)/shard_map/tile_sum/pallas_call | solution.py:327
  (14 shorter events, 0.3 us)
Async XLA Ops:
  0.6 2.4 %collective-permute-start = (f32[64,16,128]{2,1,0:T(8,128)}, f32[64,16,128]{2,1,0:T(8,128)S(1)}, u32[]{:S(2)}, u32[]{:S(2)}) collective-permute-start(f32[64,16,128]{2,1,0:T(8,128)} %bitcast.10), channel_id=1, source_target_pairs={{0,16},{16,0},{1,17},{17,1},{2,18},{18,2},{3,19},{19,3},{4,20},{20... | collective-permute-start | bytes 1572872 | tf_op jit(solution)/shard_map/ppermute | solution.py:322
  1.1 1.0 %copy-start.1 = (f32[125,125]{1,0:T(8,128)S(1)}, f32[125,125]{1,0:T(8,128)}, u32[]{:S(2)}) copy-start(f32[125,125]{1,0:T(8,128)} %cell_ref.1) | copy-start | bytes 187504
  3.1 7.4 %copy-start.2 = (f32[4,4,128]{2,1,0:T(4,128)S(1)}, f32[4,4,128]{2,1,0:T(4,128)}, u32[]{:S(2)}) copy-start(f32[4,4,128]{2,1,0:T(4,128)} %param.5) | copy-start | bytes 24580
  3.8 10.8 %collective-permute-start.2 = (f32[4,8,1024]{2,1,0:T(8,128)S(1)}, f32[4,8,1024]{2,1,0:T(8,128)S(1)}, u32[]{:S(2)}, u32[]{:S(2)}) collective-permute-start(f32[4,8,1024]{2,1,0:T(8,128)S(1)} %get-tuple-element.35), channel_id=1, source_target_pairs={{1,2},{3,4},{5,6},{7,8},{9,10},{11,12},{13,14},{15,0},{2,1},{4,3},... | collective-permute-start | bytes 393224 | tf_op jit(solution)/shard_map/ppermute | solution.py:315
  10.5 5.4 %collective-permute-start.3 = (f32[4,8,1024]{2,1,0:T(8,128)S(1)}, f32[4,8,1024]{2,1,0:T(8,128)S(1)}, u32[]{:S(2)}, u32[]{:S(2)}) collective-permute-start(f32[4,8,1024]{2,1,0:T(8,128)S(1)} %get-tuple-element.36), channel_id=1, source_target_pairs={{0,1},{2,3},{4,5},{6,7},{8,9},{10,11},{12,13},{14,15},{1,0},{3,2},... | collective-permute-start | bytes 393224 | tf_op jit(solution)/shard_map/ppermute | solution.py:316
  10.5 1.2 %collective-permute-start.1 = (f32[16,128]{1,0:T(8,128)S(1)}, f32[16,128]{1,0:T(8,128)S(1)}, u32[]{:S(2)}, u32[]{:S(2)}) collective-permute-start(f32[16,128]{1,0:T(8,128)S(1)} %bitcast.8), channel_id=1, source_target_pairs={{0,16},{16,0},{1,17},{17,1},{2,18},{18,2},{3,19},{19,3},{4,20},{20... | collective-permute-start | bytes 24584 | tf_op jit(solution)/shard_map/ppermute | solution.py:322
  16.7 8.7 %collective-permute-start.4 = (f32[4,8,1024]{2,1,0:T(8,128)S(1)}, f32[4,8,1024]{2,1,0:T(8,128)S(1)}, u32[]{:S(2)}, u32[]{:S(2)}) collective-permute-start(f32[4,8,1024]{2,1,0:T(8,128)S(1)} %get-tuple-element.40), channel_id=1, source_target_pairs={{1,2},{3,4},{5,6},{7,8},{9,10},{11,12},{13,14},{15,0},{2,1},{4,3},... | collective-permute-start | bytes 393224 | tf_op jit(solution)/shard_map/ppermute | solution.py:315
  20.8 5.0 %collective-permute-start.5 = (f32[4,8,1024]{2,1,0:T(8,128)S(1)}, f32[4,8,1024]{2,1,0:T(8,128)S(1)}, u32[]{:S(2)}, u32[]{:S(2)}) collective-permute-start(f32[4,8,1024]{2,1,0:T(8,128)S(1)} %get-tuple-element.41), channel_id=1, source_target_pairs={{0,1},{2,3},{4,5},{6,7},{8,9},{10,11},{12,13},{14,15},{1,0},{3,2},... | collective-permute-start | bytes 393224 | tf_op jit(solution)/shard_map/ppermute | solution.py:316
  20.8 9.5 %copy-start = (bf16[256,4,4,128]{3,2,1,0:T(4,128)(2,1)S(1)}, bf16[256,4,4,128]{3,2,1,0:T(4,128)(2,1)}, u32[]{:S(2)}) copy-start(bf16[256,4,4,128]{3,2,1,0:T(4,128)(2,1)} %param.7) | copy-start | bytes 3145732
  26.6 8.7 %collective-permute-start.6 = (f32[4,8,1024]{2,1,0:T(8,128)S(1)}, f32[4,8,1024]{2,1,0:T(8,128)S(1)}, u32[]{:S(2)}, u32[]{:S(2)}) collective-permute-start(f32[4,8,1024]{2,1,0:T(8,128)S(1)} %get-tuple-element.46), channel_id=1, source_target_pairs={{1,2},{3,4},{5,6},{7,8},{9,10},{11,12},{13,14},{15,0},{2,1},{4,3},... | collective-permute-start | bytes 393224 | tf_op jit(solution)/shard_map/ppermute | solution.py:315
  30.3 5.0 %collective-permute-start.7 = (f32[4,8,1024]{2,1,0:T(8,128)S(1)}, f32[4,8,1024]{2,1,0:T(8,128)S(1)}, u32[]{:S(2)}, u32[]{:S(2)}) collective-permute-start(f32[4,8,1024]{2,1,0:T(8,128)S(1)} %get-tuple-element.47), channel_id=1, source_target_pairs={{0,1},{2,3},{4,5},{6,7},{8,9},{10,11},{12,13},{14,15},{1,0},{3,2},... | collective-permute-start | bytes 393224 | tf_op jit(solution)/shard_map/ppermute | solution.py:316
  36.1 1.6 %collective-permute-start.8 = (f32[32,16,128]{2,1,0:T(8,128)S(1)}, f32[32,16,128]{2,1,0:T(8,128)S(1)}, u32[]{:S(2)}, u32[]{:S(2)}) collective-permute-start(f32[32,16,128]{2,1,0:T(8,128)S(1)} %get-tuple-element.50), channel_id=1, source_target_pairs={{0,16},{16,0},{1,17},{17,1},{2,18},{18,2},{3,19},{19,3},{4,20},{20... | collective-permute-start | bytes 786440 | tf_op jit(solution)/shard_map/ppermute | solution.py:322

commit v22 on v20

--- a/solution.py
+++ b/solution.py
@@ -225,7 +225,7 @@
         out_ref[iz] = total if step == 0 else total - before_ref[iz]
 
 
-def finish(cells, step, inner_ref, other_ref, pair_ref, matrix_ref):
+def finish(cells, step, inner_ref, pair_ref, other_ref, matrix_ref):
     size, width = inner_ref.shape[1:]
     nodes = size // 4
     even = even_place()
@@ -246,18 +246,18 @@
 
 
 def finish_kernel(
-    cells, step, inner_ref, from_other_ref, from_pair_ref, matrix_ref, edge_ref, low_ref, next_ref, pair_ref, other_ref
+    cells, step, inner_ref, from_pair_ref, from_other_ref, matrix_ref, edge_ref, low_ref, next_ref, pair_ref, other_ref
 ):
-    value = finish(cells, step, inner_ref, from_other_ref, from_pair_ref, matrix_ref)
+    value = finish(cells, step, inner_ref, from_pair_ref, from_other_ref, matrix_ref)
     for iz in range(4):
         next_ref[iz] = value[iz]
     send_edges(edge_ref, low_ref, value, pair_ref, other_ref, cells)
 
 
 def from_cells_kernel(cells, *refs):
-    inner_ref, other_ref, pair_ref, matrix_ref, order_ref = refs[:5]
+    inner_ref, pair_ref, other_ref, matrix_ref, order_ref = refs[:5]
     out_refs = refs[5:]
-    value = finish(cells, 2, inner_ref, other_ref, pair_ref, matrix_ref)
+    value = finish(cells, 2, inner_ref, pair_ref, other_ref, matrix_ref)
     states, layer, thickness = out_refs[0].shape
     group = lanes // cells
     size = value[0].shape[0]
@@ -313,7 +313,7 @@
     pair, other = edges
     other = lax.ppermute(other, "py", others + [(b, a) for a, b in others])
     pair = lax.ppermute(pair, "py", pairs + [(b, a) for a, b in pairs])
-    return [other, pair]
+    return [pair, other]
 
 
 def shifted(value, axis, steps):

time: 50.5 us -> 50.7 us (level)
  waiting for transfers between devices: 10.9 us -> 8.87 us
  starting transfers between devices: 15.1 us -> 16.8 us
    ppermute x3, starting transfers between devices: 0.01 us -> 3.33 us  [swapped(): pair = lax.ppermute(pair, 'py', pairs + [(b, a) for a, b in pairs])]
    ppermute x3, starting transfers between devices: 14.5 us -> 12.9 us  [swapped(): other = lax.ppermute(other, 'py', others + [(b, a) for a, b in others])]
    ppermute x3, waiting for transfers between devices: 1.69 us -> 0.09 us  [swapped(): pair = lax.ppermute(pair, 'py', pairs + [(b, a) for a, b in pairs])]
  transfers between devices with their start and end apart: 9 -> 9, of which waited for: 7 -> 6; matrix products, arithmetic and copies ran while one was open for 2% -> 2% of each run, Pallas kernels for 14% -> 14%
where the time goes in v22:
time: 50.7 us; the launch traced here: 50.5 us
  starting transfers between devices  16.8 us (33%)
  blocking collectives  11.7 us (23%)
  Pallas kernels  11.4 us (22%)
  waiting for transfers between devices  8.87 us (17%)
  local copies, waits for them, and re-layouts  1.01 us (2%)
  between operations  0.72 us (1%)
    ppermute x3, starting transfers between devices, swapped(): other = lax.ppermute(other, 'py', others + [(b, a) for a, b in others])  12.9 us
    all_to_all x1, blocking collectives, local(): tiles = lax.all_to_all(tiles, ('px', 'py'), 0, 0, tiled=True)  11.7 us
    pallas_call x12, Pallas kernels, kernel_call(): pl.pallas_call(body, out_shape=outs, in_specs=in_specs or [whole] * len(o...  11.4 us
    ppermute x3, waiting for transfers between devices, swapped(): other = lax.ppermute(other, 'py', others + [(b, a) for a, b in others])  6.09 us
    ppermute x3, starting transfers between devices, swapped(): pair = lax.ppermute(pair, 'py', pairs + [(b, a) for a, b in pairs])  3.33 us
    ppermute x3, waiting for transfers between devices, shifted(): lax.ppermute(value, axis, [(source, (source + steps) % count) for source...  2.69 us
  transfers between devices with their start and end apart: 9, of which 6 were waited for; matrix products, arithmetic and copies ran while one was open for 2% of the time, Pallas kernels for 14%

profile of v22, /device:TPU:0, one launch (start us, length us, event | category | flops | bytes accessed | tf_op | source)
XLA Modules:
  0.0 50.5 jit_solution(15991119248529449059)
XLA Ops:
  0.6 0.5 %collective-permute-start = (f32[64,16,128]{2,1,0:T(8,128)}, f32[64,16,128]{2,1,0:T(8,128)S(1)}, u32[]{:S(2)}, u32[]{:S(2)}) collective-permute-start(f32[64,16,128]{2,1,0:T(8,128)} %bitcast.10), channel_id=1, source_target_pairs={{0,16},{16,0},{1,17},{17,1},{2,18},{18,2},{3,19},{19,3},{4,20},{20... | collective-permute-start | bytes 1572872 | tf_op jit(solution)/shard_map/ppermute | solution.py:321
  1.1 1.0 %constant_dynamic-slice_fusion.part_ref = f32[32,16,128]{2,1,0:T(8,128)S(1)} fusion(f32[64,16,128]{2,1,0:T(8,128)} %bitcast.11, s32[]{:T(128)S(6)} %select_n.3), kind=kLoop, calls=%fused_computation | loop fusion | bytes 524292 | tf_op jit(solution)/shard_map/dynamic_slice | solution.py:366
  2.2 0.9 %prepare.1 = (bf16[208,208]{1,0:T(8,128)(2,1)S(1)}, bf16[208,208]{1,0:T(8,128)(2,1)S(1)}, bf16[80,160]{1,0:T(8,128)(2,1)S(1)}, bf16[160,208]{1,0:T(8,128)(2,1)S(...) custom-call(f32[125,125]{1,0:T(8,128)S(1)} %copy-done.1, ...), custom_call_target="tpu_custom_call" | custom-call | tf_op jit(solution)/shard_map/prepare/pallas_call | solution.py:326
  3.1 0.7 %to_cells.1 = (f32[4,32,1024]{2,1,0:T(8,128)S(1)}, f32[4,8,1024]{2,1,0:T(8,128)S(1)}, f32[4,8,1024]{2,1,0:T(8,128)S(1)}) custom-call(f32[4,16,1024]{2,1,0:T(8,128)S(1)} %get-tuple-element.28.own_ref, f32[64,16,128]{2,1,0:T(8,128)S(1)} %collective-permute-done.refs_0_, bf16[512,512]{1,0:T(8,128)(2,1)S(1)} %get-tuple-element.29.refs_1_, ...), custom_call_target="tpu_custom_call" | custom-call | tf_op jit(solution)/shard_map/to_cells/pallas_call | solution.py:326
  3.8 2.8 %collective-permute-start.2 = (f32[4,8,1024]{2,1,0:T(8,128)S(1)}, f32[4,8,1024]{2,1,0:T(8,128)S(1)}, u32[]{:S(2)}, u32[]{:S(2)}) collective-permute-start(f32[4,8,1024]{2,1,0:T(8,128)S(1)} %get-tuple-element.35), channel_id=1, source_target_pairs={{0,1},{2,3},{4,5},{6,7},{8,9},{10,11},{12,13},{14,15},{1,0},{3,2},... | collective-permute-start | bytes 393224 | tf_op jit(solution)/shard_map/ppermute | solution.py:315
  6.5 4.5 %collective-permute-start.3 = (f32[4,8,1024]{2,1,0:T(8,128)S(1)}, f32[4,8,1024]{2,1,0:T(8,128)S(1)}, u32[]{:S(2)}, u32[]{:S(2)}) collective-permute-start(f32[4,8,1024]{2,1,0:T(8,128)S(1)} %get-tuple-element.36), channel_id=1, source_target_pairs={{1,2},{3,4},{5,6},{7,8},{9,10},{11,12},{13,14},{15,0},{2,1},{4,3},... | collective-permute-start | bytes 393224 | tf_op jit(solution)/shard_map/ppermute | solution.py:314
  11.0 1.2 %collective-permute-done.1.refs_1_ = f32[16,128]{1,0:T(8,128)S(1)} collective-permute-done((f32[16,128]{1,0:T(8,128)S(1)}, f32[16,128]{1,0:T(8,128)S(1)}, u32[]{:S(2)}, u32[]{:S(2)}) %collective-permute-start.1) | collective-permute-done | bytes 8224 | tf_op jit(solution)/shard_map/ppermute | solution.py:321
  12.4 1.3 %inner.3.inner_ref = f32[4,32,1024]{2,1,0:T(8,128)S(1)} custom-call(f32[4,32,1024]{2,1,0:T(8,128)S(1)} %get-tuple-element.32.refs_0_.refs_6_, f32[4,32,128]{2,1,0:T(8,128)S(1)} %levels.1.refs_1_, bf16[208,208]{1,0:T(8,128)(2,1)S(1)} %get-tuple-element.33.refs_2_, bf16[208,208]{1,0:T(8,128)(2,1)S(1)} %get-tuple-element.31.refs_3_.low_ref, ...), custom_call_target="tpu_custom_call" | custom-call | tf_op jit(solution)/shard_map/inner/pallas_call | solution.py:326
  13.7 1.8 %collective-permute-done.3.from_other_ref = f32[4,8,1024]{2,1,0:T(8,128)S(1)} collective-permute-done((f32[4,8,1024]{2,1,0:T(8,128)S(1)}, f32[4,8,1024]{2,1,0:T(8,128)S(1)}, u32[]{:S(2)}, u32[]{:S(2)}) %collective-permute-start.3) | collective-permute-done | bytes 131104 | tf_op jit(solution)/shard_map/ppermute | solution.py:314
  15.5 0.8 %finish.2 = (f32[4,32,1024]{2,1,0:T(8,128)S(1)}, f32[4,8,1024]{2,1,0:T(8,128)S(1)}, f32[4,8,1024]{2,1,0:T(8,128)S(1)}) custom-call(f32[4,32,1024]{2,1,0:T(8,128)S(1)} %inner.3.inner_ref, f32[4,8,1024]{2,1,0:T(8,128)S(1)} %collective-permute-done.2.from_pair_ref, f32[4,8,1024]{2,1,0:T(8,128)S(1)} %collective-permute-done.3.from_other_ref, ...), custom_call_target="tpu_custom_call" | custom-call | tf_op jit(solution)/shard_map/finish/pallas_call | solution.py:326
  16.4 0.5 %collective-permute-start.4 = (f32[4,8,1024]{2,1,0:T(8,128)S(1)}, f32[4,8,1024]{2,1,0:T(8,128)S(1)}, u32[]{:S(2)}, u32[]{:S(2)}) collective-permute-start(f32[4,8,1024]{2,1,0:T(8,128)S(1)} %get-tuple-element.40), channel_id=1, source_target_pairs={{0,1},{2,3},{4,5},{6,7},{8,9},{10,11},{12,13},{14,15},{1,0},{3,2},... | collective-permute-start | bytes 393224 | tf_op jit(solution)/shard_map/ppermute | solution.py:315
  16.9 4.2 %collective-permute-start.5 = (f32[4,8,1024]{2,1,0:T(8,128)S(1)}, f32[4,8,1024]{2,1,0:T(8,128)S(1)}, u32[]{:S(2)}, u32[]{:S(2)}) collective-permute-start(f32[4,8,1024]{2,1,0:T(8,128)S(1)} %get-tuple-element.41), channel_id=1, source_target_pairs={{1,2},{3,4},{5,6},{7,8},{9,10},{11,12},{13,14},{15,0},{2,1},{4,3},... | collective-permute-start | bytes 393224 | tf_op jit(solution)/shard_map/ppermute | solution.py:314
  21.0 1.3 %inner.4.inner_ref = f32[4,32,1024]{2,1,0:T(8,128)S(1)} custom-call(f32[4,32,1024]{2,1,0:T(8,128)S(1)} %get-tuple-element.39.refs_0_.refs_6_, f32[4,32,128]{2,1,0:T(8,128)S(1)} %levels.1.refs_1_, bf16[208,208]{1,0:T(8,128)(2,1)S(1)} %get-tuple-element.33.refs_2_, bf16[208,208]{1,0:T(8,128)(2,1)S(1)} %get-tuple-element.31.refs_3_.low_ref, ...), custom_call_target="tpu_custom_call" | custom-call | tf_op jit(solution)/shard_map/inner/pallas_call | solution.py:326
  22.4 3.0 %collective-permute-done.5.from_other_ref = f32[4,8,1024]{2,1,0:T(8,128)S(1)} collective-permute-done((f32[4,8,1024]{2,1,0:T(8,128)S(1)}, f32[4,8,1024]{2,1,0:T(8,128)S(1)}, u32[]{:S(2)}, u32[]{:S(2)}) %collective-permute-start.5) | collective-permute-done | bytes 131104 | tf_op jit(solution)/shard_map/ppermute | solution.py:314
  25.4 0.8 %finish.3 = (f32[4,32,1024]{2,1,0:T(8,128)S(1)}, f32[4,8,1024]{2,1,0:T(8,128)S(1)}, f32[4,8,1024]{2,1,0:T(8,128)S(1)}) custom-call(f32[4,32,1024]{2,1,0:T(8,128)S(1)} %inner.4.inner_ref, f32[4,8,1024]{2,1,0:T(8,128)S(1)} %collective-permute-done.4.from_pair_ref, f32[4,8,1024]{2,1,0:T(8,128)S(1)} %collective-permute-done.5.from_other_ref, ...), custom_call_target="tpu_custom_call" | custom-call | tf_op jit(solution)/shard_map/finish/pallas_call | solution.py:326
  26.3 4.2 %collective-permute-start.7 = (f32[4,8,1024]{2,1,0:T(8,128)S(1)}, f32[4,8,1024]{2,1,0:T(8,128)S(1)}, u32[]{:S(2)}, u32[]{:S(2)}) collective-permute-start(f32[4,8,1024]{2,1,0:T(8,128)S(1)} %get-tuple-element.47), channel_id=1, source_target_pairs={{1,2},{3,4},{5,6},{7,8},{9,10},{11,12},{13,14},{15,0},{2,1},{4,3},... | collective-permute-start | bytes 393224 | tf_op jit(solution)/shard_map/ppermute | solution.py:314
  30.5 1.6 %margin_rows.1.refs_2_ = bf16[256,2048]{1,0:T(8,128)(2,1)S(1)} custom-call(bf16[4096,128]{1,0:T(8,128)(2,1)S(1)} %bitcast.6), custom_call_target="tpu_custom_call" | custom-call | tf_op jit(solution)/shard_map/margin_rows/pallas_call | solution.py:326
  32.1 1.5 %inner.5 = (f32[4,32,1024]{2,1,0:T(8,128)S(1)}, bf16[512,512]{1,0:T(8,128)(2,1)S(1)}) custom-call(f32[4,32,1024]{2,1,0:T(8,128)S(1)} %get-tuple-element.42.refs_0_, f32[4,32,128]{2,1,0:T(8,128)S(1)} %levels.1.refs_1_, bf16[208,208]{1,0:T(8,128)(2,1)S(1)} %get-tuple-element.33.refs_2_, bf16[208,208]{1,0:T(8,128)(2,1)S(1)} %get-tuple-element.31.refs_3_.low_ref, ...), custom_call_target="tpu_custom_call" | custom-call | tf_op jit(solution)/shard_map/inner/pallas_call | solution.py:326
  33.7 1.2 %collective-permute-done.7.refs_2_ = f32[4,8,1024]{2,1,0:T(8,128)S(1)} collective-permute-done((f32[4,8,1024]{2,1,0:T(8,128)S(1)}, f32[4,8,1024]{2,1,0:T(8,128)S(1)}, u32[]{:S(2)}, u32[]{:S(2)}) %collective-permute-start.7) | collective-permute-done | bytes 131104 | tf_op jit(solution)/shard_map/ppermute | solution.py:314
  34.9 0.8 %from_cells.1 = (f32[32,16,128]{2,1,0:T(8,128)S(1)}, f32[32,16,128]{2,1,0:T(8,128)S(1)}) custom-call(f32[4,32,1024]{2,1,0:T(8,128)S(1)} %get-tuple-element.45.refs_0_, f32[4,8,1024]{2,1,0:T(8,128)S(1)} %collective-permute-done.6.refs_1_, f32[4,8,1024]{2,1,0:T(8,128)S(1)} %collective-permute-done.7.refs_2_, ...), custom_call_target="tpu_custom_call" | custom-call | tf_op jit(solution)/shard_map/from_cells/pallas_call | solution.py:326
  35.8 1.5 %collective-permute-done.8.refs_1_ = f32[32,16,128]{2,1,0:T(8,128)S(1)} collective-permute-done((f32[32,16,128]{2,1,0:T(8,128)S(1)}, f32[32,16,128]{2,1,0:T(8,128)S(1)}, u32[]{:S(2)}, u32[]{:S(2)}) %collective-permute-start.8) | collective-permute-done | bytes 262176 | tf_op jit(solution)/shard_map/ppermute | solution.py:321
  37.3 0.8 %margin.1 = (f32[2,64,128]{2,1,0:T(8,128)S(1)}, f32[64,16,128]{2,1,0:T(8,128)}) custom-call(f32[32,16,128]{2,1,0:T(8,128)S(1)} %get-tuple-element.49.refs_0_, f32[32,16,128]{2,1,0:T(8,128)S(1)} %collective-permute-done.8.refs_1_, bf16[256,2048]{1,0:T(8,128)(2,1)S(1)} %margin_rows.1.refs_2_), custom_call_target="tpu_custom_call" | custom-call | tf_op jit(solution)/shard_map/margin/pallas_call | solution.py:326
  38.1 11.7 %all_to_all.5.tiles_ref = f32[32,4,128]{2,1,0:T(4,128)S(1)} all-to-all(f32[32,4,128]{2,1,0:T(4,128)S(1)} %bitcast.7), channel_id=1, replica_groups=mesh['px'=2,'py'=16] {'px','py'}, dimensions={0} | all-to-all | bytes 131072 | tf_op jit(solution)/shard_map/all_to_all | solution.py:447
  49.8 0.7 %tile_sum.1 = f32[16,32]{1,0:T(8,128)} custom-call(f32[32,4,128]{2,1,0:T(4,128)S(1)} %all_to_all.5.tiles_ref), custom_call_target="tpu_custom_call" | custom-call | tf_op jit(solution)/shard_map/tile_sum/pallas_call | solution.py:326
  (14 shorter events, 0.4 us)
Async XLA Ops:
  0.6 2.4 %collective-permute-start = (f32[64,16,128]{2,1,0:T(8,128)}, f32[64,16,128]{2,1,0:T(8,128)S(1)}, u32[]{:S(2)}, u32[]{:S(2)}) collective-permute-start(f32[64,16,128]{2,1,0:T(8,128)} %bitcast.10), channel_id=1, source_target_pairs={{0,16},{16,0},{1,17},{17,1},{2,18},{18,2},{3,19},{19,3},{4,20},{20... | collective-permute-start | bytes 1572872 | tf_op jit(solution)/shard_map/ppermute | solution.py:321
  1.1 1.0 %copy-start.1 = (f32[125,125]{1,0:T(8,128)S(1)}, f32[125,125]{1,0:T(8,128)}, u32[]{:S(2)}) copy-start(f32[125,125]{1,0:T(8,128)} %cell_ref.1) | copy-start | bytes 187504
  3.1 8.0 %copy-start.2 = (f32[4,4,128]{2,1,0:T(4,128)S(1)}, f32[4,4,128]{2,1,0:T(4,128)}, u32[]{:S(2)}) copy-start(f32[4,4,128]{2,1,0:T(4,128)} %param.5) | copy-start | bytes 24580
  3.8 9.9 %collective-permute-start.2 = (f32[4,8,1024]{2,1,0:T(8,128)S(1)}, f32[4,8,1024]{2,1,0:T(8,128)S(1)}, u32[]{:S(2)}, u32[]{:S(2)}) collective-permute-start(f32[4,8,1024]{2,1,0:T(8,128)S(1)} %get-tuple-element.35), channel_id=1, source_target_pairs={{0,1},{2,3},{4,5},{6,7},{8,9},{10,11},{12,13},{14,15},{1,0},{3,2},... | collective-permute-start | bytes 393224 | tf_op jit(solution)/shard_map/ppermute | solution.py:315
  6.5 9.0 %collective-permute-start.3 = (f32[4,8,1024]{2,1,0:T(8,128)S(1)}, f32[4,8,1024]{2,1,0:T(8,128)S(1)}, u32[]{:S(2)}, u32[]{:S(2)}) collective-permute-start(f32[4,8,1024]{2,1,0:T(8,128)S(1)} %get-tuple-element.36), channel_id=1, source_target_pairs={{1,2},{3,4},{5,6},{7,8},{9,10},{11,12},{13,14},{15,0},{2,1},{4,3},... | collective-permute-start | bytes 393224 | tf_op jit(solution)/shard_map/ppermute | solution.py:314
  11.0 1.2 %collective-permute-start.1 = (f32[16,128]{1,0:T(8,128)S(1)}, f32[16,128]{1,0:T(8,128)S(1)}, u32[]{:S(2)}, u32[]{:S(2)}) collective-permute-start(f32[16,128]{1,0:T(8,128)S(1)} %bitcast.8), channel_id=1, source_target_pairs={{0,16},{16,0},{1,17},{17,1},{2,18},{18,2},{3,19},{19,3},{4,20},{20... | collective-permute-start | bytes 24584 | tf_op jit(solution)/shard_map/ppermute | solution.py:321
  16.4 6.1 %collective-permute-start.4 = (f32[4,8,1024]{2,1,0:T(8,128)S(1)}, f32[4,8,1024]{2,1,0:T(8,128)S(1)}, u32[]{:S(2)}, u32[]{:S(2)}) collective-permute-start(f32[4,8,1024]{2,1,0:T(8,128)S(1)} %get-tuple-element.40), channel_id=1, source_target_pairs={{0,1},{2,3},{4,5},{6,7},{8,9},{10,11},{12,13},{14,15},{1,0},{3,2},... | collective-permute-start | bytes 393224 | tf_op jit(solution)/shard_map/ppermute | solution.py:315
  16.9 8.6 %collective-permute-start.5 = (f32[4,8,1024]{2,1,0:T(8,128)S(1)}, f32[4,8,1024]{2,1,0:T(8,128)S(1)}, u32[]{:S(2)}, u32[]{:S(2)}) collective-permute-start(f32[4,8,1024]{2,1,0:T(8,128)S(1)} %get-tuple-element.41), channel_id=1, source_target_pairs={{1,2},{3,4},{5,6},{7,8},{9,10},{11,12},{13,14},{15,0},{2,1},{4,3},... | collective-permute-start | bytes 393224 | tf_op jit(solution)/shard_map/ppermute | solution.py:314
  21.0 9.5 %copy-start = (bf16[256,4,4,128]{3,2,1,0:T(4,128)(2,1)S(1)}, bf16[256,4,4,128]{3,2,1,0:T(4,128)(2,1)}, u32[]{:S(2)}) copy-start(bf16[256,4,4,128]{3,2,1,0:T(4,128)(2,1)} %param.7) | copy-start | bytes 3145732
  26.2 7.5 %collective-permute-start.6 = (f32[4,8,1024]{2,1,0:T(8,128)S(1)}, f32[4,8,1024]{2,1,0:T(8,128)S(1)}, u32[]{:S(2)}, u32[]{:S(2)}) collective-permute-start(f32[4,8,1024]{2,1,0:T(8,128)S(1)} %get-tuple-element.46), channel_id=1, source_target_pairs={{0,1},{2,3},{4,5},{6,7},{8,9},{10,11},{12,13},{14,15},{1,0},{3,2},... | collective-permute-start | bytes 393224 | tf_op jit(solution)/shard_map/ppermute | solution.py:315
  26.3 8.6 %collective-permute-start.7 = (f32[4,8,1024]{2,1,0:T(8,128)S(1)}, f32[4,8,1024]{2,1,0:T(8,128)S(1)}, u32[]{:S(2)}, u32[]{:S(2)}) collective-permute-start(f32[4,8,1024]{2,1,0:T(8,128)S(1)} %get-tuple-element.47), channel_id=1, source_target_pairs={{1,2},{3,4},{5,6},{7,8},{9,10},{11,12},{13,14},{15,0},{2,1},{4,3},... | collective-permute-start | bytes 393224 | tf_op jit(solution)/shard_map/ppermute | solution.py:314
  35.7 1.6 %collective-permute-start.8 = (f32[32,16,128]{2,1,0:T(8,128)S(1)}, f32[32,16,128]{2,1,0:T(8,128)S(1)}, u32[]{:S(2)}, u32[]{:S(2)}) collective-permute-start(f32[32,16,128]{2,1,0:T(8,128)S(1)} %get-tuple-element.50), channel_id=1, source_target_pairs={{0,16},{16,0},{1,17},{17,1},{2,18},{18,2},{3,19},{19,3},{4,20},{20... | collective-permute-start | bytes 786440 | tf_op jit(solution)/shard_map/ppermute | solution.py:321

commit v23 on v20

--- a/solution.py
+++ b/solution.py
@@ -78,7 +78,7 @@
     high_ref[...], low_ref[...] = high, low
     inside, layer = 20 * nodes, 4 * nodes
     pick = chosen(layer, inside, functools.partial(pick_target, nodes))
-    edge_ref[...] = jnp.concatenate([high[inside:, :inside], pick], 0)
+    edge_ref[...] = jnp.concatenate([high[inside:, :inside], pick, low[inside:, :inside]], 0)
     place = chosen(inside, layer, functools.partial(place_target, nodes))
     place_ref[...] = place
     from_halo = total[:inside, inside:]
@@ -130,13 +130,15 @@
     return lax.rem(lax.axis_index("py"), 2) == 0
 
 
-def send_edges(edge_ref, low_ref, value, pair_ref, other_ref, cells):
+def send_edges(edge_ref, value, pair_ref, other_ref, cells):
     nodes = pair_ref.shape[1]
     even = even_place()
-    inside, beyond = 20 * nodes, (PADDED - 20) * nodes
+    beyond = (PADDED - 20) * nodes
+    both = beyond + 4 * nodes
     high, low = two_parts(jnp.concatenate(value + [roll_cells(value[0], cells, True)], 0))
-    product = dot(edge_ref[...], high) + dot(edge_ref[...], low)
-    up = fold_last(product[:beyond] + dot(low_ref[inside:, :inside], high), nodes, cells)
+    from_high = dot(edge_ref[...], high)
+    product = from_high[:both] + dot(edge_ref[:both, :], low)
+    up = fold_last(product[:beyond] + from_high[both:], nodes, cells)
     for iz in range(4):
         down = product[beyond + iz * nodes : beyond + (iz + 1) * nodes]
         pair_ref[iz] = jnp.where(even, up[iz], down)
@@ -167,13 +169,13 @@
 
 
 def to_cells_kernel(cells, count, own_ref, *refs):
-    part_refs = refs[:-6]
-    order_ref, edge_ref, low_ref, w_ref, pair_ref, other_ref = refs[-6:]
+    part_refs = refs[:-5]
+    order_ref, edge_ref, w_ref, pair_ref, other_ref = refs[-5:]
     parts = [[own_ref[iz] for iz in range(4)]] + [turned(ref, order_ref, count) for ref in part_refs]
     value = [jnp.concatenate([part[iz] for part in parts], 0) for iz in range(4)]
     for iz in range(4):
         w_ref[iz] = value[iz]
-    send_edges(edge_ref, low_ref, value, pair_ref, other_ref, cells)
+    send_edges(edge_ref, value, pair_ref, other_ref, cells)
 
 
 def levels_kernel(parts_x, *refs):
@@ -209,7 +211,7 @@
     product = dot(high_ref[:inside, :inside], high)
     product = product + (dot(low_ref[:inside, :inside], high) + dot(high_ref[:inside, :inside], low))
 
-    pick = edge_ref[(PADDED - 20) * nodes :, :]
+    pick = edge_ref[(PADDED - 20) * nodes : (PADDED - 16) * nodes, :]
     edge = dot(pick, high) + dot(pick, low)
     edge = jnp.concatenate([edge, roll_cells(edge[:nodes], cells, True), jnp.zeros((nodes, width), f32)], 0)
     edge = fold_last(three_products(high_ref[inside:, inside:], low_ref[inside:, inside:], edge), nodes, cells)
@@ -246,12 +248,12 @@
 
 
 def finish_kernel(
-    cells, step, inner_ref, from_other_ref, from_pair_ref, matrix_ref, edge_ref, low_ref, next_ref, pair_ref, other_ref
+    cells, step, inner_ref, from_other_ref, from_pair_ref, matrix_ref, edge_ref, next_ref, pair_ref, other_ref
 ):
     value = finish(cells, step, inner_ref, from_other_ref, from_pair_ref, matrix_ref)
     for iz in range(4):
         next_ref[iz] = value[iz]
-    send_edges(edge_ref, low_ref, value, pair_ref, other_ref, cells)
+    send_edges(edge_ref, value, pair_ref, other_ref, cells)
 
 
 def from_cells_kernel(cells, *refs):
@@ -275,16 +277,9 @@
 
 
 def margin_kernel(parts_x, *refs):
-    part_refs, block_ref = refs[:parts_x], refs[parts_x]
-    tiles_ref, filtered_ref, sems = refs[parts_x + 1 :]
+    part_refs, (block_ref, tiles_ref) = refs[:parts_x], refs[parts_x:]
     me = lax.axis_index("px")
-    count, layer, thickness = part_refs[0].shape
-    owners = [lax.rem(me + (parts_x - step), parts_x) for step in range(parts_x)]
-    copies = []
-    for step, part_ref in enumerate(part_refs):
-        target = filtered_ref.at[pl.ds(owners[step] * count, count)]
-        copies.append(pltpu.make_async_copy(part_ref, target, sems.at[step]))
-    start_all(copies)
+    count, layer, _ = part_refs[0].shape
     turned_parts = [jnp.swapaxes(ref[...], 0, 1) for ref in part_refs]
     lines = [jnp.concatenate([part[n] for part in turned_parts], 0).astype(bf16) for n in range(layer)]
     product = lax.dot_general(
@@ -295,15 +290,25 @@
     for step in range(parts_x):
         columns = slice(step * count, (step + 1) * count)
         tiles = jnp.concatenate([product[start : start + group_rows, columns] for start in starts], 1)
-        tiles_ref[owners[step]] = tiles
+        tiles_ref[lax.rem(me + (parts_x - step), parts_x)] = tiles
+
+
+def result_kernel(parts_x, tiles_ref, *refs):
+    part_refs, (out_ref, filtered_ref, tile_ref, sems) = refs[:parts_x], refs[parts_x:]
+    me = lax.axis_index("px")
+    count = filtered_ref.shape[0] // parts_x
+    copies = []
+    for step, part_ref in enumerate(part_refs):
+        owner = lax.rem(me + (parts_x - step), parts_x)
+        copies.append(pltpu.make_async_copy(part_ref, filtered_ref.at[pl.ds(owner * count, count)], sems.at[step]))
+        copies[-1].start()
+    total = jnp.sum(tiles_ref[...], axis=0)
+    tile_rows = tile_ref.shape[1]
+    groups = total.shape[1] // tile_rows
+    tile_ref[...] = jnp.concatenate([total[:, g * tile_rows : (g + 1) * tile_rows] for g in range(groups)], 0)
+    copies.append(pltpu.make_async_copy(tile_ref, out_ref, sems.at[parts_x]))
+    copies[-1].start()
     wait_all(copies)
-
-
-def sum_kernel(tiles_ref, out_ref):
-    total = jnp.sum(tiles_ref[...], axis=0)
-    tile_rows = out_ref.shape[1]
-    groups = total.shape[1] // tile_rows
-    out_ref[...] = jnp.concatenate([total[:, g * tile_rows : (g + 1) * tile_rows] for g in range(groups)], 0)
 
 
 def swapped(edges):
@@ -350,7 +355,7 @@
     table = jax.ShapeDtypeStruct((group, group), bf16)
     inside = 20 * nodes
     from_halo = jax.ShapeDtypeStruct((inside, 3 * (rows - inside) + 2 * 4 * nodes), bf16)
-    edge_shape = jax.ShapeDtypeStruct((rows - inside + 4 * nodes, inside), bf16)
+    edge_shape = jax.ShapeDtypeStruct((2 * (rows - inside) + 4 * nodes, inside), bf16)
     place_shape = jax.ShapeDtypeStruct((inside, 4 * nodes), bf16)
 
     chunks = 1
@@ -379,7 +384,7 @@
     field_now, *edges = kernel_call(
         functools.partial(to_cells_kernel, cells, mine),
         [field, message, message],
-        [own] + parts[1:] + [order, edge_matrix, low],
+        [own] + parts[1:] + [order, edge_matrix],
         "to_cells",
     )
     edges = swapped(edges)
@@ -419,7 +424,7 @@
             field_now, *edges = kernel_call(
                 functools.partial(finish_kernel, cells, step),
                 [field, message, message],
-                operands + [edge_matrix, low],
+                operands + [edge_matrix],
                 "finish",
             )
             edges = swapped(edges)
@@ -432,20 +437,25 @@
             )
     received = [pieces[0]] + [shifted(pieces[step], "px", step) for step in others]
 
-    tiles, filtered = kernel_call(
+    tiles = kernel_call(
         functools.partial(margin_kernel, parts_x),
+        jax.ShapeDtypeStruct((parts_x, block_count // groups, groups * tile_rows), f32),
+        received + [ordered],
+        "margin",
+    )
+    tiles = tiles.reshape(parts_x * parts_y, tile_cols // groups, groups * tile_rows)
+    tiles = lax.all_to_all(tiles, ("px", "py"), 0, 0, tiled=True)
+    margin, filtered = kernel_call(
+        functools.partial(result_kernel, parts_x),
         [
-            jax.ShapeDtypeStruct((parts_x, block_count // groups, groups * tile_rows), f32),
+            jax.ShapeDtypeStruct((tile_cols, tile_rows), f32),
             jax.ShapeDtypeStruct((states, layer, thickness), f32),
         ],
-        received + [ordered],
-        "margin",
-        scratch=[pltpu.SemaphoreType.DMA((parts_x,))],
-        out_specs=[whole, anywhere],
-    )
-    tiles = tiles.reshape(parts_x * parts_y, tile_cols // groups, groups * tile_rows)
-    tiles = lax.all_to_all(tiles, ("px", "py"), 0, 0, tiled=True)
-    margin = kernel_call(sum_kernel, jax.ShapeDtypeStruct((tile_cols, tile_rows), f32), [tiles], "tile_sum")
+        [tiles] + received,
+        "result",
+        scratch=[pltpu.VMEM((tile_cols, tile_rows), f32), pltpu.SemaphoreType.DMA((parts_x + 1,))],
+        out_specs=[anywhere] * 2,
+    )
     return filtered.reshape(span.shape), margin.T
 
 

time: 50.5 us -> 50.3 us (level)
  no operation moved by 1% of the time
where the time goes in v23:
time: 50.3 us; the launch traced here: 50.1 us
  starting transfers between devices  15.1 us (30%)
  Pallas kernels  11.2 us (22%)
  blocking collectives  11.2 us (22%)
  waiting for transfers between devices  10.9 us (22%)
  local copies, waits for them, and re-layouts  1.01 us (2%)
  between operations  0.7 us (1%)
    ppermute x3, starting transfers between devices, swapped(): other = lax.ppermute(other, 'py', others + [(b, a) for a, b in others])  14.5 us
    pallas_call x12, Pallas kernels, kernel_call(): pl.pallas_call(body, out_shape=outs, in_specs=in_specs or [whole] * len(o...  11.2 us
    all_to_all x1, blocking collectives, local(): tiles = lax.all_to_all(tiles, ('px', 'py'), 0, 0, tiled=True)  11.2 us
    ppermute x3, waiting for transfers between devices, swapped(): other = lax.ppermute(other, 'py', others + [(b, a) for a, b in others])  6.56 us
    ppermute x3, waiting for transfers between devices, shifted(): lax.ppermute(value, axis, [(source, (source + steps) % count) for source...  2.67 us
    ppermute x3, waiting for transfers between devices, swapped(): pair = lax.ppermute(pair, 'py', pairs + [(b, a) for a, b in pairs])  1.7 us
  transfers between devices with their start and end apart: 9, of which 7 were waited for; matrix products, arithmetic and copies ran while one was open for 2% of the time, Pallas kernels for 14%

profile of v23, /device:TPU:0, one launch (start us, length us, event | category | flops | bytes accessed | tf_op | source)
XLA Modules:
  0.0 50.1 jit_solution(8088913282268549357)
XLA Ops:
  0.6 0.5 %collective-permute-start = (f32[64,16,128]{2,1,0:T(8,128)}, f32[64,16,128]{2,1,0:T(8,128)S(1)}, u32[]{:S(2)}, u32[]{:S(2)}) collective-permute-start(f32[64,16,128]{2,1,0:T(8,128)} %bitcast.10), channel_id=1, source_target_pairs={{0,16},{16,0},{1,17},{17,1},{2,18},{18,2},{3,19},{19,3},{4,20},{20... | collective-permute-start | bytes 1572872 | tf_op jit(solution)/shard_map/ppermute | solution.py:326
  1.1 1.0 %constant_dynamic-slice_fusion.part_ref = f32[32,16,128]{2,1,0:T(8,128)S(1)} fusion(f32[64,16,128]{2,1,0:T(8,128)} %bitcast.11, s32[]{:T(128)S(6)} %select_n.3), kind=kLoop, calls=%fused_computation | loop fusion | bytes 524292 | tf_op jit(solution)/shard_map/dynamic_slice | solution.py:371
  2.2 0.9 %prepare.1 = (bf16[208,208]{1,0:T(8,128)(2,1)S(1)}, bf16[208,208]{1,0:T(8,128)(2,1)S(1)}, bf16[128,160]{1,0:T(8,128)(2,1)S(1)}, bf16[160,208]{1,0:T(8,128)(2,1)S...) custom-call(f32[125,125]{1,0:T(8,128)S(1)} %copy-done.1, ...), custom_call_target="tpu_custom_call" | custom-call | tf_op jit(solution)/shard_map/prepare/pallas_call | solution.py:331
  3.1 0.7 %to_cells.1 = (f32[4,32,1024]{2,1,0:T(8,128)S(1)}, f32[4,8,1024]{2,1,0:T(8,128)S(1)}, f32[4,8,1024]{2,1,0:T(8,128)S(1)}) custom-call(f32[4,16,1024]{2,1,0:T(8,128)S(1)} %get-tuple-element.28.own_ref, f32[64,16,128]{2,1,0:T(8,128)S(1)} %collective-permute-done.refs_0_, bf16[512,512]{1,0:T(8,128)(2,1)S(1)} %get-tuple-element.29.refs_1_, ...), custom_call_target="tpu_custom_call" | custom-call | tf_op jit(solution)/shard_map/to_cells/pallas_call | solution.py:331
  3.7 6.7 %collective-permute-start.2 = (f32[4,8,1024]{2,1,0:T(8,128)S(1)}, f32[4,8,1024]{2,1,0:T(8,128)S(1)}, u32[]{:S(2)}, u32[]{:S(2)}) collective-permute-start(f32[4,8,1024]{2,1,0:T(8,128)S(1)} %get-tuple-element.35), channel_id=1, source_target_pairs={{1,2},{3,4},{5,6},{7,8},{9,10},{11,12},{13,14},{15,0},{2,1},{4,3},... | collective-permute-start | bytes 393224 | tf_op jit(solution)/shard_map/ppermute | solution.py:319
  10.5 1.1 %collective-permute-done.1.refs_1_ = f32[16,128]{1,0:T(8,128)S(1)} collective-permute-done((f32[16,128]{1,0:T(8,128)S(1)}, f32[16,128]{1,0:T(8,128)S(1)}, u32[]{:S(2)}, u32[]{:S(2)}) %collective-permute-start.1) | collective-permute-done | bytes 8224 | tf_op jit(solution)/shard_map/ppermute | solution.py:326
  11.8 1.3 %inner.3.inner_ref = f32[4,32,1024]{2,1,0:T(8,128)S(1)} custom-call(f32[4,32,1024]{2,1,0:T(8,128)S(1)} %get-tuple-element.31.refs_0_.refs_6_, f32[4,32,128]{2,1,0:T(8,128)S(1)} %levels.1.refs_1_, bf16[208,208]{1,0:T(8,128)(2,1)S(1)} %get-tuple-element.32.refs_2_, bf16[208,208]{1,0:T(8,128)(2,1)S(1)} %get-tuple-element.33.refs_3_, ...), custom_call_target="tpu_custom_call" | custom-call | tf_op jit(solution)/shard_map/inner/pallas_call | solution.py:331
  13.1 1.4 %collective-permute-done.2.from_other_ref = f32[4,8,1024]{2,1,0:T(8,128)S(1)} collective-permute-done((f32[4,8,1024]{2,1,0:T(8,128)S(1)}, f32[4,8,1024]{2,1,0:T(8,128)S(1)}, u32[]{:S(2)}, u32[]{:S(2)}) %collective-permute-start.2) | collective-permute-done | bytes 131104 | tf_op jit(solution)/shard_map/ppermute | solution.py:319
  14.6 1.4 %collective-permute-done.3.from_pair_ref = f32[4,8,1024]{2,1,0:T(8,128)S(1)} collective-permute-done((f32[4,8,1024]{2,1,0:T(8,128)S(1)}, f32[4,8,1024]{2,1,0:T(8,128)S(1)}, u32[]{:S(2)}, u32[]{:S(2)}) %collective-permute-start.3) | collective-permute-done | bytes 131104 | tf_op jit(solution)/shard_map/ppermute | solution.py:320
  15.9 0.8 %finish.2 = (f32[4,32,1024]{2,1,0:T(8,128)S(1)}, f32[4,8,1024]{2,1,0:T(8,128)S(1)}, f32[4,8,1024]{2,1,0:T(8,128)S(1)}) custom-call(f32[4,32,1024]{2,1,0:T(8,128)S(1)} %inner.3.inner_ref, f32[4,8,1024]{2,1,0:T(8,128)S(1)} %collective-permute-done.2.from_other_ref, f32[4,8,1024]{2,1,0:T(8,128)S(1)} %collective-permute-done.3.from_pair_ref, ...), custom_call_target="tpu_custom_call" | custom-call | tf_op jit(solution)/shard_map/finish/pallas_call | solution.py:331
  16.7 4.1 %collective-permute-start.4 = (f32[4,8,1024]{2,1,0:T(8,128)S(1)}, f32[4,8,1024]{2,1,0:T(8,128)S(1)}, u32[]{:S(2)}, u32[]{:S(2)}) collective-permute-start(f32[4,8,1024]{2,1,0:T(8,128)S(1)} %get-tuple-element.40), channel_id=1, source_target_pairs={{1,2},{3,4},{5,6},{7,8},{9,10},{11,12},{13,14},{15,0},{2,1},{4,3},... | collective-permute-start | bytes 393224 | tf_op jit(solution)/shard_map/ppermute | solution.py:319
  20.7 1.3 %inner.4.inner_ref = f32[4,32,1024]{2,1,0:T(8,128)S(1)} custom-call(f32[4,32,1024]{2,1,0:T(8,128)S(1)} %get-tuple-element.39.refs_0_.refs_6_, f32[4,32,128]{2,1,0:T(8,128)S(1)} %levels.1.refs_1_, bf16[208,208]{1,0:T(8,128)(2,1)S(1)} %get-tuple-element.32.refs_2_, bf16[208,208]{1,0:T(8,128)(2,1)S(1)} %get-tuple-element.33.refs_3_, ...), custom_call_target="tpu_custom_call" | custom-call | tf_op jit(solution)/shard_map/inner/pallas_call | solution.py:331
  22.1 3.3 %collective-permute-done.4.from_other_ref = f32[4,8,1024]{2,1,0:T(8,128)S(1)} collective-permute-done((f32[4,8,1024]{2,1,0:T(8,128)S(1)}, f32[4,8,1024]{2,1,0:T(8,128)S(1)}, u32[]{:S(2)}, u32[]{:S(2)}) %collective-permute-start.4) | collective-permute-done | bytes 131104 | tf_op jit(solution)/shard_map/ppermute | solution.py:319
  25.4 0.3 collective-permute-done.5.from_pair_ref
  25.7 0.8 %finish.3 = (f32[4,32,1024]{2,1,0:T(8,128)S(1)}, f32[4,8,1024]{2,1,0:T(8,128)S(1)}, f32[4,8,1024]{2,1,0:T(8,128)S(1)}) custom-call(f32[4,32,1024]{2,1,0:T(8,128)S(1)} %inner.4.inner_ref, f32[4,8,1024]{2,1,0:T(8,128)S(1)} %collective-permute-done.4.from_other_ref, f32[4,8,1024]{2,1,0:T(8,128)S(1)} %collective-permute-done.5.from_pair_ref, ...), custom_call_target="tpu_custom_call" | custom-call | tf_op jit(solution)/shard_map/finish/pallas_call | solution.py:331
  26.5 3.7 %collective-permute-start.6 = (f32[4,8,1024]{2,1,0:T(8,128)S(1)}, f32[4,8,1024]{2,1,0:T(8,128)S(1)}, u32[]{:S(2)}, u32[]{:S(2)}) collective-permute-start(f32[4,8,1024]{2,1,0:T(8,128)S(1)} %get-tuple-element.46), channel_id=1, source_target_pairs={{1,2},{3,4},{5,6},{7,8},{9,10},{11,12},{13,14},{15,0},{2,1},{4,3},... | collective-permute-start | bytes 393224 | tf_op jit(solution)/shard_map/ppermute | solution.py:319
  30.2 1.6 %margin_rows.1.refs_2_ = bf16[256,2048]{1,0:T(8,128)(2,1)S(1)} custom-call(bf16[4096,128]{1,0:T(8,128)(2,1)S(1)} %bitcast.6), custom_call_target="tpu_custom_call" | custom-call | tf_op jit(solution)/shard_map/margin_rows/pallas_call | solution.py:331
  31.8 1.5 %inner.5 = (f32[4,32,1024]{2,1,0:T(8,128)S(1)}, bf16[512,512]{1,0:T(8,128)(2,1)S(1)}) custom-call(f32[4,32,1024]{2,1,0:T(8,128)S(1)} %get-tuple-element.42.refs_0_, f32[4,32,128]{2,1,0:T(8,128)S(1)} %levels.1.refs_1_, bf16[208,208]{1,0:T(8,128)(2,1)S(1)} %get-tuple-element.32.refs_2_, bf16[208,208]{1,0:T(8,128)(2,1)S(1)} %get-tuple-element.33.refs_3_, ...), custom_call_target="tpu_custom_call" | custom-call | tf_op jit(solution)/shard_map/inner/pallas_call | solution.py:331
  33.4 1.8 %collective-permute-done.6.refs_1_ = f32[4,8,1024]{2,1,0:T(8,128)S(1)} collective-permute-done((f32[4,8,1024]{2,1,0:T(8,128)S(1)}, f32[4,8,1024]{2,1,0:T(8,128)S(1)}, u32[]{:S(2)}, u32[]{:S(2)}) %collective-permute-start.6) | collective-permute-done | bytes 131104 | tf_op jit(solution)/shard_map/ppermute | solution.py:319
  35.2 0.8 %from_cells.1 = (f32[32,16,128]{2,1,0:T(8,128)S(1)}, f32[32,16,128]{2,1,0:T(8,128)S(1)}) custom-call(f32[4,32,1024]{2,1,0:T(8,128)S(1)} %get-tuple-element.45.refs_0_, f32[4,8,1024]{2,1,0:T(8,128)S(1)} %collective-permute-done.6.refs_1_, f32[4,8,1024]{2,1,0:T(8,128)S(1)} %collective-permute-done.7.refs_2_, ...), custom_call_target="tpu_custom_call" | custom-call | tf_op jit(solution)/shard_map/from_cells/pallas_call | solution.py:331
  36.1 1.5 %collective-permute-done.8.refs_1_ = f32[32,16,128]{2,1,0:T(8,128)S(1)} collective-permute-done((f32[32,16,128]{2,1,0:T(8,128)S(1)}, f32[32,16,128]{2,1,0:T(8,128)S(1)}, u32[]{:S(2)}, u32[]{:S(2)}) %collective-permute-start.8) | collective-permute-done | bytes 262176 | tf_op jit(solution)/shard_map/ppermute | solution.py:326
  37.6 0.5 %margin.1 = f32[2,64,128]{2,1,0:T(8,128)S(1)} custom-call(f32[32,16,128]{2,1,0:T(8,128)S(1)} %get-tuple-element.49.refs_0_, f32[32,16,128]{2,1,0:T(8,128)S(1)} %collective-permute-done.8.refs_1_, bf16[256,2048]{1,0:T(8,128)(2,1)S(1)} %margin_rows.1.refs_2_), custom_call_target="tpu_custom_call" | custom-call | tf_op jit(solution)/shard_map/margin/pallas_call | solution.py:331
  38.1 11.2 %all_to_all.5.tiles_ref = f32[32,4,128]{2,1,0:T(4,128)S(1)} all-to-all(f32[32,4,128]{2,1,0:T(4,128)S(1)} %bitcast.7), channel_id=1, replica_groups=mesh['px'=2,'py'=16] {'px','py'}, dimensions={0} | all-to-all | bytes 131072 | tf_op jit(solution)/shard_map/all_to_all | solution.py:447
  49.3 0.8 %result.1 = (f32[16,32]{1,0:T(8,128)}, f32[64,16,128]{2,1,0:T(8,128)}) custom-call(f32[32,4,128]{2,1,0:T(4,128)S(1)} %all_to_all.5.tiles_ref, f32[32,16,128]{2,1,0:T(8,128)S(1)} %get-tuple-element.49.refs_0_, f32[32,16,128]{2,1,0:T(8,128)S(1)} %collective-permute-done.8.refs_1_), custom_call_target="tpu_custom_call" | custom-call | tf_op jit(solution)/shard_map/result/pallas_call | solution.py:331
  (14 shorter events, 0.3 us)
Async XLA Ops:
  0.6 2.4 %collective-permute-start = (f32[64,16,128]{2,1,0:T(8,128)}, f32[64,16,128]{2,1,0:T(8,128)S(1)}, u32[]{:S(2)}, u32[]{:S(2)}) collective-permute-start(f32[64,16,128]{2,1,0:T(8,128)} %bitcast.10), channel_id=1, source_target_pairs={{0,16},{16,0},{1,17},{17,1},{2,18},{18,2},{3,19},{19,3},{4,20},{20... | collective-permute-start | bytes 1572872 | tf_op jit(solution)/shard_map/ppermute | solution.py:326
  1.1 1.0 %copy-start.1 = (f32[125,125]{1,0:T(8,128)S(1)}, f32[125,125]{1,0:T(8,128)}, u32[]{:S(2)}) copy-start(f32[125,125]{1,0:T(8,128)} %cell_ref.1) | copy-start | bytes 187504
  3.1 7.4 %copy-start.2 = (f32[4,4,128]{2,1,0:T(4,128)S(1)}, f32[4,4,128]{2,1,0:T(4,128)}, u32[]{:S(2)}) copy-start(f32[4,4,128]{2,1,0:T(4,128)} %param.5) | copy-start | bytes 24580
  3.7 10.8 %collective-permute-start.2 = (f32[4,8,1024]{2,1,0:T(8,128)S(1)}, f32[4,8,1024]{2,1,0:T(8,128)S(1)}, u32[]{:S(2)}, u32[]{:S(2)}) collective-permute-start(f32[4,8,1024]{2,1,0:T(8,128)S(1)} %get-tuple-element.35), channel_id=1, source_target_pairs={{1,2},{3,4},{5,6},{7,8},{9,10},{11,12},{13,14},{15,0},{2,1},{4,3},... | collective-permute-start | bytes 393224 | tf_op jit(solution)/shard_map/ppermute | solution.py:319
  10.5 5.4 %collective-permute-start.3 = (f32[4,8,1024]{2,1,0:T(8,128)S(1)}, f32[4,8,1024]{2,1,0:T(8,128)S(1)}, u32[]{:S(2)}, u32[]{:S(2)}) collective-permute-start(f32[4,8,1024]{2,1,0:T(8,128)S(1)} %get-tuple-element.36), channel_id=1, source_target_pairs={{0,1},{2,3},{4,5},{6,7},{8,9},{10,11},{12,13},{14,15},{1,0},{3,2},... | collective-permute-start | bytes 393224 | tf_op jit(solution)/shard_map/ppermute | solution.py:320
  10.5 1.2 %collective-permute-start.1 = (f32[16,128]{1,0:T(8,128)S(1)}, f32[16,128]{1,0:T(8,128)S(1)}, u32[]{:S(2)}, u32[]{:S(2)}) collective-permute-start(f32[16,128]{1,0:T(8,128)S(1)} %bitcast.8), channel_id=1, source_target_pairs={{0,16},{16,0},{1,17},{17,1},{2,18},{18,2},{3,19},{19,3},{4,20},{20... | collective-permute-start | bytes 24584 | tf_op jit(solution)/shard_map/ppermute | solution.py:326
  16.7 8.7 %collective-permute-start.4 = (f32[4,8,1024]{2,1,0:T(8,128)S(1)}, f32[4,8,1024]{2,1,0:T(8,128)S(1)}, u32[]{:S(2)}, u32[]{:S(2)}) collective-permute-start(f32[4,8,1024]{2,1,0:T(8,128)S(1)} %get-tuple-element.40), channel_id=1, source_target_pairs={{1,2},{3,4},{5,6},{7,8},{9,10},{11,12},{13,14},{15,0},{2,1},{4,3},... | collective-permute-start | bytes 393224 | tf_op jit(solution)/shard_map/ppermute | solution.py:319
  20.7 5.0 %collective-permute-start.5 = (f32[4,8,1024]{2,1,0:T(8,128)S(1)}, f32[4,8,1024]{2,1,0:T(8,128)S(1)}, u32[]{:S(2)}, u32[]{:S(2)}) collective-permute-start(f32[4,8,1024]{2,1,0:T(8,128)S(1)} %get-tuple-element.41), channel_id=1, source_target_pairs={{0,1},{2,3},{4,5},{6,7},{8,9},{10,11},{12,13},{14,15},{1,0},{3,2},... | collective-permute-start | bytes 393224 | tf_op jit(solution)/shard_map/ppermute | solution.py:320
  20.7 9.5 %copy-start = (bf16[256,4,4,128]{3,2,1,0:T(4,128)(2,1)S(1)}, bf16[256,4,4,128]{3,2,1,0:T(4,128)(2,1)}, u32[]{:S(2)}) copy-start(bf16[256,4,4,128]{3,2,1,0:T(4,128)(2,1)} %param.7) | copy-start | bytes 3145732
  26.5 8.7 %collective-permute-start.6 = (f32[4,8,1024]{2,1,0:T(8,128)S(1)}, f32[4,8,1024]{2,1,0:T(8,128)S(1)}, u32[]{:S(2)}, u32[]{:S(2)}) collective-permute-start(f32[4,8,1024]{2,1,0:T(8,128)S(1)} %get-tuple-element.46), channel_id=1, source_target_pairs={{1,2},{3,4},{5,6},{7,8},{9,10},{11,12},{13,14},{15,0},{2,1},{4,3},... | collective-permute-start | bytes 393224 | tf_op jit(solution)/shard_map/ppermute | solution.py:319
  30.2 5.0 %collective-permute-start.7 = (f32[4,8,1024]{2,1,0:T(8,128)S(1)}, f32[4,8,1024]{2,1,0:T(8,128)S(1)}, u32[]{:S(2)}, u32[]{:S(2)}) collective-permute-start(f32[4,8,1024]{2,1,0:T(8,128)S(1)} %get-tuple-element.47), channel_id=1, source_target_pairs={{0,1},{2,3},{4,5},{6,7},{8,9},{10,11},{12,13},{14,15},{1,0},{3,2},... | collective-permute-start | bytes 393224 | tf_op jit(solution)/shard_map/ppermute | solution.py:320
  36.0 1.6 %collective-permute-start.8 = (f32[32,16,128]{2,1,0:T(8,128)S(1)}, f32[32,16,128]{2,1,0:T(8,128)S(1)}, u32[]{:S(2)}, u32[]{:S(2)}) collective-permute-start(f32[32,16,128]{2,1,0:T(8,128)S(1)} %get-tuple-element.50), channel_id=1, source_target_pairs={{0,16},{16,0},{1,17},{17,1},{2,18},{18,2},{3,19},{19,3},{4,20},{20... | collective-permute-start | bytes 786440 | tf_op jit(solution)/shard_map/ppermute | solution.py:326

commit v24 on v23

--- a/solution.py
+++ b/solution.py
@@ -276,29 +276,42 @@
                 out_ref[h * group + s] = part[rows, s * thickness : (s + 1) * thickness]
 
 
-def margin_kernel(parts_x, *refs):
-    part_refs, (block_ref, tiles_ref) = refs[:parts_x], refs[parts_x:]
-    me = lax.axis_index("px")
+def margin_tiles(part_refs, block_ref, group_rows):
     count, layer, _ = part_refs[0].shape
     turned_parts = [jnp.swapaxes(ref[...], 0, 1) for ref in part_refs]
     lines = [jnp.concatenate([part[n] for part in turned_parts], 0).astype(bf16) for n in range(layer)]
     product = lax.dot_general(
         block_ref[...], jnp.concatenate(lines, 1), (((1,), (1,)), ((), ())), preferred_element_type=f32
     )
-    group_rows = tiles_ref.shape[1]
     starts = range(0, product.shape[0], group_rows)
-    for step in range(parts_x):
-        columns = slice(step * count, (step + 1) * count)
-        tiles = jnp.concatenate([product[start : start + group_rows, columns] for start in starts], 1)
+    return [
+        jnp.concatenate([product[start : start + group_rows, part * count : (part + 1) * count] for start in starts], 1)
+        for part in range(len(part_refs))
+    ]
+
+
+def own_margin_kernel(part_ref, block_ref, tiles_ref, filtered_ref, sem):
+    count = part_ref.shape[0]
+    copy = pltpu.make_async_copy(part_ref, filtered_ref.at[pl.ds(lax.axis_index("px") * count, count)], sem)
+    copy.start()
+    tiles_ref[...] = margin_tiles([part_ref], block_ref, tiles_ref.shape[0])[0]
+    copy.wait()
+
+
+def margin_kernel(parts_x, own_ref, *refs):
+    part_refs, (block_ref, tiles_ref) = refs[: parts_x - 1], refs[parts_x - 1 :]
+    me = lax.axis_index("px")
+    tiles_ref[me] = own_ref[...]
+    for step, tiles in enumerate(margin_tiles(part_refs, block_ref, tiles_ref.shape[1]), 1):
         tiles_ref[lax.rem(me + (parts_x - step), parts_x)] = tiles
 
 
-def result_kernel(parts_x, tiles_ref, *refs):
-    part_refs, (out_ref, filtered_ref, tile_ref, sems) = refs[:parts_x], refs[parts_x:]
+def result_kernel(parts_x, begun_ref, tiles_ref, *refs):
+    part_refs, (out_ref, filtered_ref, tile_ref, sems) = refs[: parts_x - 1], refs[parts_x - 1 :]
     me = lax.axis_index("px")
     count = filtered_ref.shape[0] // parts_x
     copies = []
-    for step, part_ref in enumerate(part_refs):
+    for step, part_ref in enumerate(part_refs, 1):
         owner = lax.rem(me + (parts_x - step), parts_x)
         copies.append(pltpu.make_async_copy(part_ref, filtered_ref.at[pl.ds(owner * count, count)], sems.at[step]))
         copies[-1].start()
@@ -306,7 +319,7 @@
     tile_rows = tile_ref.shape[1]
     groups = total.shape[1] // tile_rows
     tile_ref[...] = jnp.concatenate([total[:, g * tile_rows : (g + 1) * tile_rows] for g in range(groups)], 0)
-    copies.append(pltpu.make_async_copy(tile_ref, out_ref, sems.at[parts_x]))
+    copies.append(pltpu.make_async_copy(tile_ref, out_ref, sems.at[0]))
     copies[-1].start()
     wait_all(copies)
 
@@ -326,7 +339,7 @@
     return lax.ppermute(value, axis, [(source, (source + steps) % count) for source in range(count)])
 
 
-def kernel_call(body, outs, operands, name, scratch=(), in_specs=None, out_specs=None):
+def kernel_call(body, outs, operands, name, scratch=(), in_specs=None, out_specs=None, aliases=None):
     many = isinstance(outs, list)
     return pl.pallas_call(
         body,
@@ -334,6 +347,7 @@
         in_specs=in_specs or [whole] * len(operands),
         out_specs=out_specs or ([whole] * len(outs) if many else whole),
         scratch_shapes=list(scratch),
+        input_output_aliases=aliases or {},
         compiler_params=params,
         name=name,
     )(*operands)
@@ -437,24 +451,33 @@
             )
     received = [pieces[0]] + [shifted(pieces[step], "px", step) for step in others]
 
+    tiles = jax.ShapeDtypeStruct((block_count // groups, groups * tile_rows), f32)
+    filtered = jax.ShapeDtypeStruct((states, layer, thickness), f32)
+    own_tiles, begun = kernel_call(
+        own_margin_kernel,
+        [tiles, filtered],
+        [received[0], ordered],
+        "own_margin",
+        scratch=[pltpu.SemaphoreType.DMA],
+        out_specs=[whole, anywhere],
+    )
     tiles = kernel_call(
         functools.partial(margin_kernel, parts_x),
-        jax.ShapeDtypeStruct((parts_x, block_count // groups, groups * tile_rows), f32),
-        received + [ordered],
+        jax.ShapeDtypeStruct((parts_x,) + tiles.shape, f32),
+        [own_tiles] + received[1:] + [ordered],
         "margin",
     )
     tiles = tiles.reshape(parts_x * parts_y, tile_cols // groups, groups * tile_rows)
     tiles = lax.all_to_all(tiles, ("px", "py"), 0, 0, tiled=True)
     margin, filtered = kernel_call(
         functools.partial(result_kernel, parts_x),
-        [
-            jax.ShapeDtypeStruct((tile_cols, tile_rows), f32),
-            jax.ShapeDtypeStruct((states, layer, thickness), f32),
-        ],
-        [tiles] + received,
+        [jax.ShapeDtypeStruct((tile_cols, tile_rows), f32), filtered],
+        [begun, tiles] + received[1:],
         "result",
-        scratch=[pltpu.VMEM((tile_cols, tile_rows), f32), pltpu.SemaphoreType.DMA((parts_x + 1,))],
+        scratch=[pltpu.VMEM((tile_cols, tile_rows), f32), pltpu.SemaphoreType.DMA((parts_x,))],
+        in_specs=[anywhere] + [whole] * parts_x,
         out_specs=[anywhere] * 2,
+        aliases={0: 1},
     )
     return filtered.reshape(span.shape), margin.T
 

time: 50.3 us -> 50.1 us (level)
  waiting for transfers between devices: 10.9 us -> 10.2 us
  Pallas kernels: 11.2 us -> 11.8 us
    ppermute x3, waiting for transfers between devices: 2.67 us -> 1.94 us  [shifted(): lax.ppermute(value, axis, [(source, (source + steps) % count) for source...]
    pallas_call x12 -> x13, Pallas kernels: 11.2 us -> 11.8 us  [kernel_call(): pl.pallas_call(body, out_shape=outs, in_specs=in_specs or [whole] * len(o...]
  transfers between devices with their start and end apart: 9 -> 9, of which waited for: 7 -> 7; matrix products, arithmetic and copies ran while one was open for 2% -> 2% of each run, Pallas kernels for 14% -> 15%
where the time goes in v24:
time: 50.1 us; the launch traced here: 50 us
  starting transfers between devices  15.1 us (30%)
  Pallas kernels  11.8 us (24%)
  blocking collectives  11.2 us (22%)
  waiting for transfers between devices  10.2 us (20%)
  local copies, waits for them, and re-layouts  1.01 us (2%)
  between operations  0.7 us (1%)
    ppermute x3, starting transfers between devices, swapped(): other = lax.ppermute(other, 'py', others + [(b, a) for a, b in others])  14.5 us
    pallas_call x13, Pallas kernels, kernel_call(): pl.pallas_call(body, out_shape=outs, in_specs=in_specs or [whole] * len(o...  11.8 us
    all_to_all x1, blocking collectives, local(): tiles = lax.all_to_all(tiles, ('px', 'py'), 0, 0, tiled=True)  11.2 us
    ppermute x3, waiting for transfers between devices, swapped(): other = lax.ppermute(other, 'py', others + [(b, a) for a, b in others])  6.56 us
    ppermute x3, waiting for transfers between devices, shifted(): lax.ppermute(value, axis, [(source, (source + steps) % count) for source...  1.94 us
    ppermute x3, waiting for transfers between devices, swapped(): pair = lax.ppermute(pair, 'py', pairs + [(b, a) for a, b in pairs])  1.7 us
  transfers between devices with their start and end apart: 9, of which 7 were waited for; matrix products, arithmetic and copies ran while one was open for 2% of the time, Pallas kernels for 15%

profile of v24, /device:TPU:0, one launch (start us, length us, event | category | flops | bytes accessed | tf_op | source)
XLA Modules:
  0.0 50.0 jit_solution(5776634441304081820)
XLA Ops:
  0.6 0.5 %collective-permute-start = (f32[64,16,128]{2,1,0:T(8,128)}, f32[64,16,128]{2,1,0:T(8,128)S(1)}, u32[]{:S(2)}, u32[]{:S(2)}) collective-permute-start(f32[64,16,128]{2,1,0:T(8,128)} %bitcast.11), channel_id=1, source_target_pairs={{0,16},{16,0},{1,17},{17,1},{2,18},{18,2},{3,19},{19,3},{4,20},{20... | collective-permute-start | bytes 1572872 | tf_op jit(solution)/shard_map/ppermute | solution.py:339
  1.1 1.0 %constant_dynamic-slice_fusion.part_ref = f32[32,16,128]{2,1,0:T(8,128)S(1)} fusion(f32[64,16,128]{2,1,0:T(8,128)} %bitcast.12, s32[]{:T(128)S(6)} %select_n.3), kind=kLoop, calls=%fused_computation | loop fusion | bytes 524292 | tf_op jit(solution)/shard_map/dynamic_slice | solution.py:385
  2.2 0.9 %prepare.1 = (bf16[208,208]{1,0:T(8,128)(2,1)S(1)}, bf16[208,208]{1,0:T(8,128)(2,1)S(1)}, bf16[128,160]{1,0:T(8,128)(2,1)S(1)}, bf16[160,208]{1,0:T(8,128)(2,1)S...) custom-call(f32[125,125]{1,0:T(8,128)S(1)} %copy-done.1, ...), custom_call_target="tpu_custom_call" | custom-call | tf_op jit(solution)/shard_map/prepare/pallas_call | solution.py:344
  3.1 0.7 %to_cells.1 = (f32[4,32,1024]{2,1,0:T(8,128)S(1)}, f32[4,8,1024]{2,1,0:T(8,128)S(1)}, f32[4,8,1024]{2,1,0:T(8,128)S(1)}) custom-call(f32[4,16,1024]{2,1,0:T(8,128)S(1)} %get-tuple-element.30.own_ref, f32[64,16,128]{2,1,0:T(8,128)S(1)} %collective-permute-done.refs_0_, bf16[512,512]{1,0:T(8,128)(2,1)S(1)} %get-tuple-element.31.refs_1_, ...), custom_call_target="tpu_custom_call" | custom-call | tf_op jit(solution)/shard_map/to_cells/pallas_call | solution.py:344
  3.7 6.7 %collective-permute-start.2 = (f32[4,8,1024]{2,1,0:T(8,128)S(1)}, f32[4,8,1024]{2,1,0:T(8,128)S(1)}, u32[]{:S(2)}, u32[]{:S(2)}) collective-permute-start(f32[4,8,1024]{2,1,0:T(8,128)S(1)} %get-tuple-element.37), channel_id=1, source_target_pairs={{1,2},{3,4},{5,6},{7,8},{9,10},{11,12},{13,14},{15,0},{2,1},{4,3},... | collective-permute-start | bytes 393224 | tf_op jit(solution)/shard_map/ppermute | solution.py:332
  10.5 1.1 %collective-permute-done.1.refs_1_ = f32[16,128]{1,0:T(8,128)S(1)} collective-permute-done((f32[16,128]{1,0:T(8,128)S(1)}, f32[16,128]{1,0:T(8,128)S(1)}, u32[]{:S(2)}, u32[]{:S(2)}) %collective-permute-start.1) | collective-permute-done | bytes 8224 | tf_op jit(solution)/shard_map/ppermute | solution.py:339
  11.8 1.3 %inner.3.inner_ref = f32[4,32,1024]{2,1,0:T(8,128)S(1)} custom-call(f32[4,32,1024]{2,1,0:T(8,128)S(1)} %get-tuple-element.33.refs_0_.refs_6_, f32[4,32,128]{2,1,0:T(8,128)S(1)} %levels.1.refs_1_, bf16[208,208]{1,0:T(8,128)(2,1)S(1)} %get-tuple-element.34.refs_2_, bf16[208,208]{1,0:T(8,128)(2,1)S(1)} %get-tuple-element.35.refs_3_, ...), custom_call_target="tpu_custom_call" | custom-call | tf_op jit(solution)/shard_map/inner/pallas_call | solution.py:344
  13.1 1.4 %collective-permute-done.2.from_other_ref = f32[4,8,1024]{2,1,0:T(8,128)S(1)} collective-permute-done((f32[4,8,1024]{2,1,0:T(8,128)S(1)}, f32[4,8,1024]{2,1,0:T(8,128)S(1)}, u32[]{:S(2)}, u32[]{:S(2)}) %collective-permute-start.2) | collective-permute-done | bytes 131104 | tf_op jit(solution)/shard_map/ppermute | solution.py:332
  14.6 1.4 %collective-permute-done.3.from_pair_ref = f32[4,8,1024]{2,1,0:T(8,128)S(1)} collective-permute-done((f32[4,8,1024]{2,1,0:T(8,128)S(1)}, f32[4,8,1024]{2,1,0:T(8,128)S(1)}, u32[]{:S(2)}, u32[]{:S(2)}) %collective-permute-start.3) | collective-permute-done | bytes 131104 | tf_op jit(solution)/shard_map/ppermute | solution.py:333
  15.9 0.8 %finish.2 = (f32[4,32,1024]{2,1,0:T(8,128)S(1)}, f32[4,8,1024]{2,1,0:T(8,128)S(1)}, f32[4,8,1024]{2,1,0:T(8,128)S(1)}) custom-call(f32[4,32,1024]{2,1,0:T(8,128)S(1)} %inner.3.inner_ref, f32[4,8,1024]{2,1,0:T(8,128)S(1)} %collective-permute-done.2.from_other_ref, f32[4,8,1024]{2,1,0:T(8,128)S(1)} %collective-permute-done.3.from_pair_ref, ...), custom_call_target="tpu_custom_call" | custom-call | tf_op jit(solution)/shard_map/finish/pallas_call | solution.py:344
  16.7 4.1 %collective-permute-start.4 = (f32[4,8,1024]{2,1,0:T(8,128)S(1)}, f32[4,8,1024]{2,1,0:T(8,128)S(1)}, u32[]{:S(2)}, u32[]{:S(2)}) collective-permute-start(f32[4,8,1024]{2,1,0:T(8,128)S(1)} %get-tuple-element.42), channel_id=1, source_target_pairs={{1,2},{3,4},{5,6},{7,8},{9,10},{11,12},{13,14},{15,0},{2,1},{4,3},... | collective-permute-start | bytes 393224 | tf_op jit(solution)/shard_map/ppermute | solution.py:332
  20.7 1.3 %inner.4.inner_ref = f32[4,32,1024]{2,1,0:T(8,128)S(1)} custom-call(f32[4,32,1024]{2,1,0:T(8,128)S(1)} %get-tuple-element.41.refs_0_.refs_6_, f32[4,32,128]{2,1,0:T(8,128)S(1)} %levels.1.refs_1_, bf16[208,208]{1,0:T(8,128)(2,1)S(1)} %get-tuple-element.34.refs_2_, bf16[208,208]{1,0:T(8,128)(2,1)S(1)} %get-tuple-element.35.refs_3_, ...), custom_call_target="tpu_custom_call" | custom-call | tf_op jit(solution)/shard_map/inner/pallas_call | solution.py:344
  22.1 3.3 %collective-permute-done.4.from_other_ref = f32[4,8,1024]{2,1,0:T(8,128)S(1)} collective-permute-done((f32[4,8,1024]{2,1,0:T(8,128)S(1)}, f32[4,8,1024]{2,1,0:T(8,128)S(1)}, u32[]{:S(2)}, u32[]{:S(2)}) %collective-permute-start.4) | collective-permute-done | bytes 131104 | tf_op jit(solution)/shard_map/ppermute | solution.py:332
  25.7 0.8 %finish.3 = (f32[4,32,1024]{2,1,0:T(8,128)S(1)}, f32[4,8,1024]{2,1,0:T(8,128)S(1)}, f32[4,8,1024]{2,1,0:T(8,128)S(1)}) custom-call(f32[4,32,1024]{2,1,0:T(8,128)S(1)} %inner.4.inner_ref, f32[4,8,1024]{2,1,0:T(8,128)S(1)} %collective-permute-done.4.from_other_ref, f32[4,8,1024]{2,1,0:T(8,128)S(1)} %collective-permute-done.5.from_pair_ref, ...), custom_call_target="tpu_custom_call" | custom-call | tf_op jit(solution)/shard_map/finish/pallas_call | solution.py:344
  26.5 3.7 %collective-permute-start.6 = (f32[4,8,1024]{2,1,0:T(8,128)S(1)}, f32[4,8,1024]{2,1,0:T(8,128)S(1)}, u32[]{:S(2)}, u32[]{:S(2)}) collective-permute-start(f32[4,8,1024]{2,1,0:T(8,128)S(1)} %get-tuple-element.48), channel_id=1, source_target_pairs={{1,2},{3,4},{5,6},{7,8},{9,10},{11,12},{13,14},{15,0},{2,1},{4,3},... | collective-permute-start | bytes 393224 | tf_op jit(solution)/shard_map/ppermute | solution.py:332
  30.2 1.6 %margin_rows.1.block_ref.refs_1_ = bf16[256,2048]{1,0:T(8,128)(2,1)S(1)} custom-call(bf16[4096,128]{1,0:T(8,128)(2,1)S(1)} %bitcast.6), custom_call_target="tpu_custom_call" | custom-call | tf_op jit(solution)/shard_map/margin_rows/pallas_call | solution.py:344
  31.8 1.5 %inner.5 = (f32[4,32,1024]{2,1,0:T(8,128)S(1)}, bf16[512,512]{1,0:T(8,128)(2,1)S(1)}) custom-call(f32[4,32,1024]{2,1,0:T(8,128)S(1)} %get-tuple-element.44.refs_0_, f32[4,32,128]{2,1,0:T(8,128)S(1)} %levels.1.refs_1_, bf16[208,208]{1,0:T(8,128)(2,1)S(1)} %get-tuple-element.34.refs_2_, bf16[208,208]{1,0:T(8,128)(2,1)S(1)} %get-tuple-element.35.refs_3_, ...), custom_call_target="tpu_custom_call" | custom-call | tf_op jit(solution)/shard_map/inner/pallas_call | solution.py:344
  33.4 1.8 %collective-permute-done.6.refs_1_ = f32[4,8,1024]{2,1,0:T(8,128)S(1)} collective-permute-done((f32[4,8,1024]{2,1,0:T(8,128)S(1)}, f32[4,8,1024]{2,1,0:T(8,128)S(1)}, u32[]{:S(2)}, u32[]{:S(2)}) %collective-permute-start.6) | collective-permute-done | bytes 131104 | tf_op jit(solution)/shard_map/ppermute | solution.py:332
  35.2 0.8 %from_cells.1 = (f32[32,16,128]{2,1,0:T(8,128)S(1)}, f32[32,16,128]{2,1,0:T(8,128)S(1)}) custom-call(f32[4,32,1024]{2,1,0:T(8,128)S(1)} %get-tuple-element.47.refs_0_, f32[4,8,1024]{2,1,0:T(8,128)S(1)} %collective-permute-done.6.refs_1_, f32[4,8,1024]{2,1,0:T(8,128)S(1)} %collective-permute-done.7.refs_2_, ...), custom_call_target="tpu_custom_call" | custom-call | tf_op jit(solution)/shard_map/from_cells/pallas_call | solution.py:344
  36.1 0.7 %own_margin.1 = (f32[64,128]{1,0:T(8,128)S(1)}, f32[64,16,128]{2,1,0:T(8,128)}) custom-call(f32[32,16,128]{2,1,0:T(8,128)S(1)} %get-tuple-element.51.part_ref, bf16[256,2048]{1,0:T(8,128)(2,1)S(1)} %margin_rows.1.block_ref.refs_1_), custom_call_target="tpu_custom_call" | custom-call | tf_op jit(solution)/shard_map/own_margin/pallas_call | solution.py:344
  36.8 0.8 %collective-permute-done.8.refs_0_ = f32[32,16,128]{2,1,0:T(8,128)S(1)} collective-permute-done((f32[32,16,128]{2,1,0:T(8,128)S(1)}, f32[32,16,128]{2,1,0:T(8,128)S(1)}, u32[]{:S(2)}, u32[]{:S(2)}) %collective-permute-start.8) | collective-permute-done | bytes 262176 | tf_op jit(solution)/shard_map/ppermute | solution.py:339
  37.6 0.5 margin.1
  38.1 11.2 %all_to_all.5.tiles_ref = f32[32,4,128]{2,1,0:T(4,128)S(1)} all-to-all(f32[32,4,128]{2,1,0:T(4,128)S(1)} %bitcast.7), channel_id=1, replica_groups=mesh['px'=2,'py'=16] {'px','py'}, dimensions={0} | all-to-all | bytes 131072 | tf_op jit(solution)/shard_map/all_to_all | solution.py:471
  49.2 0.7 %result.1 = (f32[16,32]{1,0:T(8,128)}, f32[64,16,128]{2,1,0:T(8,128)}) custom-call(f32[64,16,128]{2,1,0:T(8,128)} %get-tuple-element.53.begun_ref, f32[32,4,128]{2,1,0:T(4,128)S(1)} %all_to_all.5.tiles_ref, f32[32,16,128]{2,1,0:T(8,128)S(1)} %collective-permute-done.8.refs_0_), custom_call_target="tpu_custom_call", output_to_operand_aliasing={{1}: (0, {})} | custom-call | tf_op jit(solution)/shard_map/result/pallas_call | solution.py:344
  (15 shorter events, 0.6 us)
Async XLA Ops:
  0.6 2.4 %collective-permute-start = (f32[64,16,128]{2,1,0:T(8,128)}, f32[64,16,128]{2,1,0:T(8,128)S(1)}, u32[]{:S(2)}, u32[]{:S(2)}) collective-permute-start(f32[64,16,128]{2,1,0:T(8,128)} %bitcast.11), channel_id=1, source_target_pairs={{0,16},{16,0},{1,17},{17,1},{2,18},{18,2},{3,19},{19,3},{4,20},{20... | collective-permute-start | bytes 1572872 | tf_op jit(solution)/shard_map/ppermute | solution.py:339
  1.1 1.0 %copy-start.1 = (f32[125,125]{1,0:T(8,128)S(1)}, f32[125,125]{1,0:T(8,128)}, u32[]{:S(2)}) copy-start(f32[125,125]{1,0:T(8,128)} %cell_ref.1) | copy-start | bytes 187504
  3.1 7.4 %copy-start.2 = (f32[4,4,128]{2,1,0:T(4,128)S(1)}, f32[4,4,128]{2,1,0:T(4,128)}, u32[]{:S(2)}) copy-start(f32[4,4,128]{2,1,0:T(4,128)} %param.5) | copy-start | bytes 24580
  3.7 10.8 %collective-permute-start.2 = (f32[4,8,1024]{2,1,0:T(8,128)S(1)}, f32[4,8,1024]{2,1,0:T(8,128)S(1)}, u32[]{:S(2)}, u32[]{:S(2)}) collective-permute-start(f32[4,8,1024]{2,1,0:T(8,128)S(1)} %get-tuple-element.37), channel_id=1, source_target_pairs={{1,2},{3,4},{5,6},{7,8},{9,10},{11,12},{13,14},{15,0},{2,1},{4,3},... | collective-permute-start | bytes 393224 | tf_op jit(solution)/shard_map/ppermute | solution.py:332
  10.5 5.4 %collective-permute-start.3 = (f32[4,8,1024]{2,1,0:T(8,128)S(1)}, f32[4,8,1024]{2,1,0:T(8,128)S(1)}, u32[]{:S(2)}, u32[]{:S(2)}) collective-permute-start(f32[4,8,1024]{2,1,0:T(8,128)S(1)} %get-tuple-element.38), channel_id=1, source_target_pairs={{0,1},{2,3},{4,5},{6,7},{8,9},{10,11},{12,13},{14,15},{1,0},{3,2},... | collective-permute-start | bytes 393224 | tf_op jit(solution)/shard_map/ppermute | solution.py:333
  10.5 1.2 %collective-permute-start.1 = (f32[16,128]{1,0:T(8,128)S(1)}, f32[16,128]{1,0:T(8,128)S(1)}, u32[]{:S(2)}, u32[]{:S(2)}) collective-permute-start(f32[16,128]{1,0:T(8,128)S(1)} %bitcast.8), channel_id=1, source_target_pairs={{0,16},{16,0},{1,17},{17,1},{2,18},{18,2},{3,19},{19,3},{4,20},{20... | collective-permute-start | bytes 24584 | tf_op jit(solution)/shard_map/ppermute | solution.py:339
  16.7 8.7 %collective-permute-start.4 = (f32[4,8,1024]{2,1,0:T(8,128)S(1)}, f32[4,8,1024]{2,1,0:T(8,128)S(1)}, u32[]{:S(2)}, u32[]{:S(2)}) collective-permute-start(f32[4,8,1024]{2,1,0:T(8,128)S(1)} %get-tuple-element.42), channel_id=1, source_target_pairs={{1,2},{3,4},{5,6},{7,8},{9,10},{11,12},{13,14},{15,0},{2,1},{4,3},... | collective-permute-start | bytes 393224 | tf_op jit(solution)/shard_map/ppermute | solution.py:332
  20.7 5.0 %collective-permute-start.5 = (f32[4,8,1024]{2,1,0:T(8,128)S(1)}, f32[4,8,1024]{2,1,0:T(8,128)S(1)}, u32[]{:S(2)}, u32[]{:S(2)}) collective-permute-start(f32[4,8,1024]{2,1,0:T(8,128)S(1)} %get-tuple-element.43), channel_id=1, source_target_pairs={{0,1},{2,3},{4,5},{6,7},{8,9},{10,11},{12,13},{14,15},{1,0},{3,2},... | collective-permute-start | bytes 393224 | tf_op jit(solution)/shard_map/ppermute | solution.py:333
  20.7 9.5 %copy-start = (bf16[256,4,4,128]{3,2,1,0:T(4,128)(2,1)S(1)}, bf16[256,4,4,128]{3,2,1,0:T(4,128)(2,1)}, u32[]{:S(2)}) copy-start(bf16[256,4,4,128]{3,2,1,0:T(4,128)(2,1)} %param.7) | copy-start | bytes 3145732
  26.5 8.7 %collective-permute-start.6 = (f32[4,8,1024]{2,1,0:T(8,128)S(1)}, f32[4,8,1024]{2,1,0:T(8,128)S(1)}, u32[]{:S(2)}, u32[]{:S(2)}) collective-permute-start(f32[4,8,1024]{2,1,0:T(8,128)S(1)} %get-tuple-element.48), channel_id=1, source_target_pairs={{1,2},{3,4},{5,6},{7,8},{9,10},{11,12},{13,14},{15,0},{2,1},{4,3},... | collective-permute-start | bytes 393224 | tf_op jit(solution)/shard_map/ppermute | solution.py:332
  30.2 5.0 %collective-permute-start.7 = (f32[4,8,1024]{2,1,0:T(8,128)S(1)}, f32[4,8,1024]{2,1,0:T(8,128)S(1)}, u32[]{:S(2)}, u32[]{:S(2)}) collective-permute-start(f32[4,8,1024]{2,1,0:T(8,128)S(1)} %get-tuple-element.49), channel_id=1, source_target_pairs={{0,1},{2,3},{4,5},{6,7},{8,9},{10,11},{12,13},{14,15},{1,0},{3,2},... | collective-permute-start | bytes 393224 | tf_op jit(solution)/shard_map/ppermute | solution.py:333
  36.0 1.6 %collective-permute-start.8 = (f32[32,16,128]{2,1,0:T(8,128)S(1)}, f32[32,16,128]{2,1,0:T(8,128)S(1)}, u32[]{:S(2)}, u32[]{:S(2)}) collective-permute-start(f32[32,16,128]{2,1,0:T(8,128)S(1)} %get-tuple-element.55), channel_id=1, source_target_pairs={{0,16},{16,0},{1,17},{17,1},{2,18},{18,2},{3,19},{19,3},{4,20},{20... | collective-permute-start | bytes 786440 | tf_op jit(solution)/shard_map/ppermute | solution.py:339

commit v25 on v23

--- a/solution.py
+++ b/solution.py
@@ -228,6 +228,8 @@
 
 
 def finish(cells, step, inner_ref, other_ref, pair_ref, matrix_ref):
+    if step == 0:
+        other_ref, pair_ref = pair_ref, other_ref
     size, width = inner_ref.shape[1:]
     nodes = size // 4
     even = even_place()
@@ -418,7 +420,7 @@
         )
         if step == 2:
             inner, ordered = lax.optimization_barrier((inner, ordered))
-        operands = [inner] + edges + [halo_matrix]
+        operands = [inner] + (edges[::-1] if step == 0 else edges) + [halo_matrix]
         if step < 2:
             before = field_now
             field_now, *edges = kernel_call(

time: 50.3 us -> 50.2 us (level)
  starting transfers between devices: 15.1 us -> 16.1 us
  waiting for transfers between devices: 10.9 us -> 9.97 us
    ppermute x3, starting transfers between devices: 0.01 us -> 2.76 us  [swapped(): pair = lax.ppermute(pair, 'py', pairs + [(b, a) for a, b in pairs])]
    ppermute x3, starting transfers between devices: 14.5 us -> 12.8 us  [swapped(): other = lax.ppermute(other, 'py', others + [(b, a) for a, b in others])]
    ppermute x3, waiting for transfers between devices: 1.7 us -> 0.87 us  [swapped(): pair = lax.ppermute(pair, 'py', pairs + [(b, a) for a, b in pairs])]
  transfers between devices with their start and end apart: 9 -> 9, of which waited for: 7 -> 6; matrix products, arithmetic and copies ran while one was open for 2% -> 2% of each run, Pallas kernels for 14% -> 14%
where the time goes in v25:
time: 50.2 us; the launch traced here: 50.1 us
  starting transfers between devices  16.1 us (32%)
  Pallas kernels  11.2 us (22%)
  blocking collectives  11.1 us (22%)
  waiting for transfers between devices  9.97 us (20%)
  local copies, waits for them, and re-layouts  1.01 us (2%)
  between operations  0.7 us (1%)
    ppermute x3, starting transfers between devices, swapped(): other = lax.ppermute(other, 'py', others + [(b, a) for a, b in others])  12.8 us
    pallas_call x12, Pallas kernels, kernel_call(): pl.pallas_call(body, out_shape=outs, in_specs=in_specs or [whole] * len(o...  11.2 us
    all_to_all x1, blocking collectives, local(): tiles = lax.all_to_all(tiles, ('px', 'py'), 0, 0, tiled=True)  11.1 us
    ppermute x3, waiting for transfers between devices, swapped(): other = lax.ppermute(other, 'py', others + [(b, a) for a, b in others])  6.41 us
    ppermute x3, starting transfers between devices, swapped(): pair = lax.ppermute(pair, 'py', pairs + [(b, a) for a, b in pairs])  2.76 us
    ppermute x3, waiting for transfers between devices, shifted(): lax.ppermute(value, axis, [(source, (source + steps) % count) for source...  2.69 us
  transfers between devices with their start and end apart: 9, of which 6 were waited for; matrix products, arithmetic and copies ran while one was open for 2% of the time, Pallas kernels for 14%

profile of v25, /device:TPU:0, one launch (start us, length us, event | category | flops | bytes accessed | tf_op | source)
XLA Modules:
  0.0 50.1 jit_solution(2656708462001435120)
XLA Ops:
  0.6 0.5 %collective-permute-start = (f32[64,16,128]{2,1,0:T(8,128)}, f32[64,16,128]{2,1,0:T(8,128)S(1)}, u32[]{:S(2)}, u32[]{:S(2)}) collective-permute-start(f32[64,16,128]{2,1,0:T(8,128)} %bitcast.10), channel_id=1, source_target_pairs={{0,16},{16,0},{1,17},{17,1},{2,18},{18,2},{3,19},{19,3},{4,20},{20... | collective-permute-start | bytes 1572872 | tf_op jit(solution)/shard_map/ppermute | solution.py:328
  1.1 1.0 %constant_dynamic-slice_fusion.part_ref = f32[32,16,128]{2,1,0:T(8,128)S(1)} fusion(f32[64,16,128]{2,1,0:T(8,128)} %bitcast.11, s32[]{:T(128)S(6)} %select_n.3), kind=kLoop, calls=%fused_computation | loop fusion | bytes 524292 | tf_op jit(solution)/shard_map/dynamic_slice | solution.py:373
  2.2 0.9 %prepare.1 = (bf16[208,208]{1,0:T(8,128)(2,1)S(1)}, bf16[208,208]{1,0:T(8,128)(2,1)S(1)}, bf16[128,160]{1,0:T(8,128)(2,1)S(1)}, bf16[160,208]{1,0:T(8,128)(2,1)S...) custom-call(f32[125,125]{1,0:T(8,128)S(1)} %copy-done.1, ...), custom_call_target="tpu_custom_call" | custom-call | tf_op jit(solution)/shard_map/prepare/pallas_call | solution.py:333
  3.1 0.7 %to_cells.1 = (f32[4,32,1024]{2,1,0:T(8,128)S(1)}, f32[4,8,1024]{2,1,0:T(8,128)S(1)}, f32[4,8,1024]{2,1,0:T(8,128)S(1)}) custom-call(f32[4,16,1024]{2,1,0:T(8,128)S(1)} %get-tuple-element.28.own_ref, f32[64,16,128]{2,1,0:T(8,128)S(1)} %collective-permute-done.refs_0_, bf16[512,512]{1,0:T(8,128)(2,1)S(1)} %get-tuple-element.29.refs_1_, ...), custom_call_target="tpu_custom_call" | custom-call | tf_op jit(solution)/shard_map/to_cells/pallas_call | solution.py:333
  3.7 2.8 %collective-permute-start.2 = (f32[4,8,1024]{2,1,0:T(8,128)S(1)}, f32[4,8,1024]{2,1,0:T(8,128)S(1)}, u32[]{:S(2)}, u32[]{:S(2)}) collective-permute-start(f32[4,8,1024]{2,1,0:T(8,128)S(1)} %get-tuple-element.35), channel_id=1, source_target_pairs={{0,1},{2,3},{4,5},{6,7},{8,9},{10,11},{12,13},{14,15},{1,0},{3,2},... | collective-permute-start | bytes 393224 | tf_op jit(solution)/shard_map/ppermute | solution.py:322
  6.5 4.5 %collective-permute-start.3 = (f32[4,8,1024]{2,1,0:T(8,128)S(1)}, f32[4,8,1024]{2,1,0:T(8,128)S(1)}, u32[]{:S(2)}, u32[]{:S(2)}) collective-permute-start(f32[4,8,1024]{2,1,0:T(8,128)S(1)} %get-tuple-element.36), channel_id=1, source_target_pairs={{1,2},{3,4},{5,6},{7,8},{9,10},{11,12},{13,14},{15,0},{2,1},{4,3},... | collective-permute-start | bytes 393224 | tf_op jit(solution)/shard_map/ppermute | solution.py:321
  11.0 1.2 %collective-permute-done.1.refs_1_ = f32[16,128]{1,0:T(8,128)S(1)} collective-permute-done((f32[16,128]{1,0:T(8,128)S(1)}, f32[16,128]{1,0:T(8,128)S(1)}, u32[]{:S(2)}, u32[]{:S(2)}) %collective-permute-start.1) | collective-permute-done | bytes 8224 | tf_op jit(solution)/shard_map/ppermute | solution.py:328
  12.4 1.3 %inner.3.inner_ref = f32[4,32,1024]{2,1,0:T(8,128)S(1)} custom-call(f32[4,32,1024]{2,1,0:T(8,128)S(1)} %get-tuple-element.31.refs_0_.refs_6_, f32[4,32,128]{2,1,0:T(8,128)S(1)} %levels.1.refs_1_, bf16[208,208]{1,0:T(8,128)(2,1)S(1)} %get-tuple-element.32.refs_2_, bf16[208,208]{1,0:T(8,128)(2,1)S(1)} %get-tuple-element.33.refs_3_, ...), custom_call_target="tpu_custom_call" | custom-call | tf_op jit(solution)/shard_map/inner/pallas_call | solution.py:333
  13.7 1.8 %collective-permute-done.3.from_pair_ref = f32[4,8,1024]{2,1,0:T(8,128)S(1)} collective-permute-done((f32[4,8,1024]{2,1,0:T(8,128)S(1)}, f32[4,8,1024]{2,1,0:T(8,128)S(1)}, u32[]{:S(2)}, u32[]{:S(2)}) %collective-permute-start.3) | collective-permute-done | bytes 131104 | tf_op jit(solution)/shard_map/ppermute | solution.py:321
  15.5 0.8 %finish.2 = (f32[4,32,1024]{2,1,0:T(8,128)S(1)}, f32[4,8,1024]{2,1,0:T(8,128)S(1)}, f32[4,8,1024]{2,1,0:T(8,128)S(1)}) custom-call(f32[4,32,1024]{2,1,0:T(8,128)S(1)} %inner.3.inner_ref, f32[4,8,1024]{2,1,0:T(8,128)S(1)} %collective-permute-done.2.from_other_ref, f32[4,8,1024]{2,1,0:T(8,128)S(1)} %collective-permute-done.3.from_pair_ref, ...), custom_call_target="tpu_custom_call" | custom-call | tf_op jit(solution)/shard_map/finish/pallas_call | solution.py:333
  16.3 4.6 %collective-permute-start.4 = (f32[4,8,1024]{2,1,0:T(8,128)S(1)}, f32[4,8,1024]{2,1,0:T(8,128)S(1)}, u32[]{:S(2)}, u32[]{:S(2)}) collective-permute-start(f32[4,8,1024]{2,1,0:T(8,128)S(1)} %get-tuple-element.40), channel_id=1, source_target_pairs={{1,2},{3,4},{5,6},{7,8},{9,10},{11,12},{13,14},{15,0},{2,1},{4,3},... | collective-permute-start | bytes 393224 | tf_op jit(solution)/shard_map/ppermute | solution.py:321
  20.9 1.3 %inner.4.inner_ref = f32[4,32,1024]{2,1,0:T(8,128)S(1)} custom-call(f32[4,32,1024]{2,1,0:T(8,128)S(1)} %get-tuple-element.39.refs_0_.refs_6_, f32[4,32,128]{2,1,0:T(8,128)S(1)} %levels.1.refs_1_, bf16[208,208]{1,0:T(8,128)(2,1)S(1)} %get-tuple-element.32.refs_2_, bf16[208,208]{1,0:T(8,128)(2,1)S(1)} %get-tuple-element.33.refs_3_, ...), custom_call_target="tpu_custom_call" | custom-call | tf_op jit(solution)/shard_map/inner/pallas_call | solution.py:333
  22.2 2.8 %collective-permute-done.4.from_other_ref = f32[4,8,1024]{2,1,0:T(8,128)S(1)} collective-permute-done((f32[4,8,1024]{2,1,0:T(8,128)S(1)}, f32[4,8,1024]{2,1,0:T(8,128)S(1)}, u32[]{:S(2)}, u32[]{:S(2)}) %collective-permute-start.4) | collective-permute-done | bytes 131104 | tf_op jit(solution)/shard_map/ppermute | solution.py:321
  25.0 0.9 %collective-permute-done.5.from_pair_ref = f32[4,8,1024]{2,1,0:T(8,128)S(1)} collective-permute-done((f32[4,8,1024]{2,1,0:T(8,128)S(1)}, f32[4,8,1024]{2,1,0:T(8,128)S(1)}, u32[]{:S(2)}, u32[]{:S(2)}) %collective-permute-start.5) | collective-permute-done | bytes 131104 | tf_op jit(solution)/shard_map/ppermute | solution.py:322
  25.8 0.8 %finish.3 = (f32[4,32,1024]{2,1,0:T(8,128)S(1)}, f32[4,8,1024]{2,1,0:T(8,128)S(1)}, f32[4,8,1024]{2,1,0:T(8,128)S(1)}) custom-call(f32[4,32,1024]{2,1,0:T(8,128)S(1)} %inner.4.inner_ref, f32[4,8,1024]{2,1,0:T(8,128)S(1)} %collective-permute-done.4.from_other_ref, f32[4,8,1024]{2,1,0:T(8,128)S(1)} %collective-permute-done.5.from_pair_ref, ...), custom_call_target="tpu_custom_call" | custom-call | tf_op jit(solution)/shard_map/finish/pallas_call | solution.py:333
  26.6 3.7 %collective-permute-start.6 = (f32[4,8,1024]{2,1,0:T(8,128)S(1)}, f32[4,8,1024]{2,1,0:T(8,128)S(1)}, u32[]{:S(2)}, u32[]{:S(2)}) collective-permute-start(f32[4,8,1024]{2,1,0:T(8,128)S(1)} %get-tuple-element.46), channel_id=1, source_target_pairs={{1,2},{3,4},{5,6},{7,8},{9,10},{11,12},{13,14},{15,0},{2,1},{4,3},... | collective-permute-start | bytes 393224 | tf_op jit(solution)/shard_map/ppermute | solution.py:321
  30.3 1.6 %margin_rows.1.refs_2_ = bf16[256,2048]{1,0:T(8,128)(2,1)S(1)} custom-call(bf16[4096,128]{1,0:T(8,128)(2,1)S(1)} %bitcast.6), custom_call_target="tpu_custom_call" | custom-call | tf_op jit(solution)/shard_map/margin_rows/pallas_call | solution.py:333
  31.9 1.6 %inner.5 = (f32[4,32,1024]{2,1,0:T(8,128)S(1)}, bf16[512,512]{1,0:T(8,128)(2,1)S(1)}) custom-call(f32[4,32,1024]{2,1,0:T(8,128)S(1)} %get-tuple-element.42.refs_0_, f32[4,32,128]{2,1,0:T(8,128)S(1)} %levels.1.refs_1_, bf16[208,208]{1,0:T(8,128)(2,1)S(1)} %get-tuple-element.32.refs_2_, bf16[208,208]{1,0:T(8,128)(2,1)S(1)} %get-tuple-element.33.refs_3_, ...), custom_call_target="tpu_custom_call" | custom-call | tf_op jit(solution)/shard_map/inner/pallas_call | solution.py:333
  33.4 1.8 %collective-permute-done.6.refs_1_ = f32[4,8,1024]{2,1,0:T(8,128)S(1)} collective-permute-done((f32[4,8,1024]{2,1,0:T(8,128)S(1)}, f32[4,8,1024]{2,1,0:T(8,128)S(1)}, u32[]{:S(2)}, u32[]{:S(2)}) %collective-permute-start.6) | collective-permute-done | bytes 131104 | tf_op jit(solution)/shard_map/ppermute | solution.py:321
  35.2 0.8 %from_cells.1 = (f32[32,16,128]{2,1,0:T(8,128)S(1)}, f32[32,16,128]{2,1,0:T(8,128)S(1)}) custom-call(f32[4,32,1024]{2,1,0:T(8,128)S(1)} %get-tuple-element.45.refs_0_, f32[4,8,1024]{2,1,0:T(8,128)S(1)} %collective-permute-done.6.refs_1_, f32[4,8,1024]{2,1,0:T(8,128)S(1)} %collective-permute-done.7.refs_2_, ...), custom_call_target="tpu_custom_call" | custom-call | tf_op jit(solution)/shard_map/from_cells/pallas_call | solution.py:333
  36.1 1.5 %collective-permute-done.8.refs_1_ = f32[32,16,128]{2,1,0:T(8,128)S(1)} collective-permute-done((f32[32,16,128]{2,1,0:T(8,128)S(1)}, f32[32,16,128]{2,1,0:T(8,128)S(1)}, u32[]{:S(2)}, u32[]{:S(2)}) %collective-permute-start.8) | collective-permute-done | bytes 262176 | tf_op jit(solution)/shard_map/ppermute | solution.py:328
  37.6 0.5 %margin.1 = f32[2,64,128]{2,1,0:T(8,128)S(1)} custom-call(f32[32,16,128]{2,1,0:T(8,128)S(1)} %get-tuple-element.49.refs_0_, f32[32,16,128]{2,1,0:T(8,128)S(1)} %collective-permute-done.8.refs_1_, bf16[256,2048]{1,0:T(8,128)(2,1)S(1)} %margin_rows.1.refs_2_), custom_call_target="tpu_custom_call" | custom-call | tf_op jit(solution)/shard_map/margin/pallas_call | solution.py:333
  38.1 11.1 %all_to_all.5.tiles_ref = f32[32,4,128]{2,1,0:T(4,128)S(1)} all-to-all(f32[32,4,128]{2,1,0:T(4,128)S(1)} %bitcast.7), channel_id=1, replica_groups=mesh['px'=2,'py'=16] {'px','py'}, dimensions={0} | all-to-all | bytes 131072 | tf_op jit(solution)/shard_map/all_to_all | solution.py:449
  49.2 0.8 %result.1 = (f32[16,32]{1,0:T(8,128)}, f32[64,16,128]{2,1,0:T(8,128)}) custom-call(f32[32,4,128]{2,1,0:T(4,128)S(1)} %all_to_all.5.tiles_ref, f32[32,16,128]{2,1,0:T(8,128)S(1)} %get-tuple-element.49.refs_0_, f32[32,16,128]{2,1,0:T(8,128)S(1)} %collective-permute-done.8.refs_1_), custom_call_target="tpu_custom_call" | custom-call | tf_op jit(solution)/shard_map/result/pallas_call | solution.py:333
  (14 shorter events, 0.3 us)
Async XLA Ops:
  0.6 2.4 %collective-permute-start = (f32[64,16,128]{2,1,0:T(8,128)}, f32[64,16,128]{2,1,0:T(8,128)S(1)}, u32[]{:S(2)}, u32[]{:S(2)}) collective-permute-start(f32[64,16,128]{2,1,0:T(8,128)} %bitcast.10), channel_id=1, source_target_pairs={{0,16},{16,0},{1,17},{17,1},{2,18},{18,2},{3,19},{19,3},{4,20},{20... | collective-permute-start | bytes 1572872 | tf_op jit(solution)/shard_map/ppermute | solution.py:328
  1.1 1.0 %copy-start.1 = (f32[125,125]{1,0:T(8,128)S(1)}, f32[125,125]{1,0:T(8,128)}, u32[]{:S(2)}) copy-start(f32[125,125]{1,0:T(8,128)} %cell_ref.1) | copy-start | bytes 187504
  3.1 7.9 %copy-start.2 = (f32[4,4,128]{2,1,0:T(4,128)S(1)}, f32[4,4,128]{2,1,0:T(4,128)}, u32[]{:S(2)}) copy-start(f32[4,4,128]{2,1,0:T(4,128)} %param.5) | copy-start | bytes 24580
  3.7 9.9 %collective-permute-start.2 = (f32[4,8,1024]{2,1,0:T(8,128)S(1)}, f32[4,8,1024]{2,1,0:T(8,128)S(1)}, u32[]{:S(2)}, u32[]{:S(2)}) collective-permute-start(f32[4,8,1024]{2,1,0:T(8,128)S(1)} %get-tuple-element.35), channel_id=1, source_target_pairs={{0,1},{2,3},{4,5},{6,7},{8,9},{10,11},{12,13},{14,15},{1,0},{3,2},... | collective-permute-start | bytes 393224 | tf_op jit(solution)/shard_map/ppermute | solution.py:322
  6.5 9.0 %collective-permute-start.3 = (f32[4,8,1024]{2,1,0:T(8,128)S(1)}, f32[4,8,1024]{2,1,0:T(8,128)S(1)}, u32[]{:S(2)}, u32[]{:S(2)}) collective-permute-start(f32[4,8,1024]{2,1,0:T(8,128)S(1)} %get-tuple-element.36), channel_id=1, source_target_pairs={{1,2},{3,4},{5,6},{7,8},{9,10},{11,12},{13,14},{15,0},{2,1},{4,3},... | collective-permute-start | bytes 393224 | tf_op jit(solution)/shard_map/ppermute | solution.py:321
  11.0 1.2 %collective-permute-start.1 = (f32[16,128]{1,0:T(8,128)S(1)}, f32[16,128]{1,0:T(8,128)S(1)}, u32[]{:S(2)}, u32[]{:S(2)}) collective-permute-start(f32[16,128]{1,0:T(8,128)S(1)} %bitcast.8), channel_id=1, source_target_pairs={{0,16},{16,0},{1,17},{17,1},{2,18},{18,2},{3,19},{19,3},{4,20},{20... | collective-permute-start | bytes 24584 | tf_op jit(solution)/shard_map/ppermute | solution.py:328
  16.3 8.7 %collective-permute-start.4 = (f32[4,8,1024]{2,1,0:T(8,128)S(1)}, f32[4,8,1024]{2,1,0:T(8,128)S(1)}, u32[]{:S(2)}, u32[]{:S(2)}) collective-permute-start(f32[4,8,1024]{2,1,0:T(8,128)S(1)} %get-tuple-element.40), channel_id=1, source_target_pairs={{1,2},{3,4},{5,6},{7,8},{9,10},{11,12},{13,14},{15,0},{2,1},{4,3},... | collective-permute-start | bytes 393224 | tf_op jit(solution)/shard_map/ppermute | solution.py:321
  20.9 5.0 %collective-permute-start.5 = (f32[4,8,1024]{2,1,0:T(8,128)S(1)}, f32[4,8,1024]{2,1,0:T(8,128)S(1)}, u32[]{:S(2)}, u32[]{:S(2)}) collective-permute-start(f32[4,8,1024]{2,1,0:T(8,128)S(1)} %get-tuple-element.41), channel_id=1, source_target_pairs={{0,1},{2,3},{4,5},{6,7},{8,9},{10,11},{12,13},{14,15},{1,0},{3,2},... | collective-permute-start | bytes 393224 | tf_op jit(solution)/shard_map/ppermute | solution.py:322
  20.9 9.4 %copy-start = (bf16[256,4,4,128]{3,2,1,0:T(4,128)(2,1)S(1)}, bf16[256,4,4,128]{3,2,1,0:T(4,128)(2,1)}, u32[]{:S(2)}) copy-start(bf16[256,4,4,128]{3,2,1,0:T(4,128)(2,1)} %param.7) | copy-start | bytes 3145732
  26.6 8.6 %collective-permute-start.6 = (f32[4,8,1024]{2,1,0:T(8,128)S(1)}, f32[4,8,1024]{2,1,0:T(8,128)S(1)}, u32[]{:S(2)}, u32[]{:S(2)}) collective-permute-start(f32[4,8,1024]{2,1,0:T(8,128)S(1)} %get-tuple-element.46), channel_id=1, source_target_pairs={{1,2},{3,4},{5,6},{7,8},{9,10},{11,12},{13,14},{15,0},{2,1},{4,3},... | collective-permute-start | bytes 393224 | tf_op jit(solution)/shard_map/ppermute | solution.py:321
  30.3 5.0 %collective-permute-start.7 = (f32[4,8,1024]{2,1,0:T(8,128)S(1)}, f32[4,8,1024]{2,1,0:T(8,128)S(1)}, u32[]{:S(2)}, u32[]{:S(2)}) collective-permute-start(f32[4,8,1024]{2,1,0:T(8,128)S(1)} %get-tuple-element.47), channel_id=1, source_target_pairs={{0,1},{2,3},{4,5},{6,7},{8,9},{10,11},{12,13},{14,15},{1,0},{3,2},... | collective-permute-start | bytes 393224 | tf_op jit(solution)/shard_map/ppermute | solution.py:322
  36.0 1.6 %collective-permute-start.8 = (f32[32,16,128]{2,1,0:T(8,128)S(1)}, f32[32,16,128]{2,1,0:T(8,128)S(1)}, u32[]{:S(2)}, u32[]{:S(2)}) collective-permute-start(f32[32,16,128]{2,1,0:T(8,128)S(1)} %get-tuple-element.50), channel_id=1, source_target_pairs={{0,16},{16,0},{1,17},{17,1},{2,18},{18,2},{3,19},{19,3},{4,20},{20... | collective-permute-start | bytes 786440 | tf_op jit(solution)/shard_map/ppermute | solution.py:328

commit v26 on v23

--- a/solution.py
+++ b/solution.py
@@ -68,7 +68,7 @@
     size, count = high_ref.shape[0], cell_ref.shape[0]
     tables = [chosen(size, count, functools.partial(select_target, cell, nodes)) for cell in range(nodes // 4)]
     total = jnp.zeros(high_ref.shape, f32)
-    for _ in range(3):
+    for _ in range(2):
         part = rest.astype(bf16)
         rest = rest - part.astype(f32)
         for table in tables:

time: 50.3 us -> 50.2 us (level)
  transfers between devices with their start and end apart: 9 -> 9, of which waited for: 7 -> 8; matrix products, arithmetic and copies ran while one was open for 2% -> 2% of each run, Pallas kernels for 14% -> 13%
where the time goes in v26:
time: 50.2 us; the launch traced here: 50 us
  starting transfers between devices  15.2 us (30%)
  blocking collectives  11.2 us (22%)
  Pallas kernels  11.1 us (22%)
  waiting for transfers between devices  10.8 us (22%)
  local copies, waits for them, and re-layouts  1.01 us (2%)
  between operations  0.7 us (1%)
    ppermute x3, starting transfers between devices, swapped(): other = lax.ppermute(other, 'py', others + [(b, a) for a, b in others])  14.6 us
    all_to_all x1, blocking collectives, local(): tiles = lax.all_to_all(tiles, ('px', 'py'), 0, 0, tiled=True)  11.2 us
    pallas_call x12, Pallas kernels, kernel_call(): pl.pallas_call(body, out_shape=outs, in_specs=in_specs or [whole] * len(o...  11.1 us
    ppermute x3, waiting for transfers between devices, swapped(): other = lax.ppermute(other, 'py', others + [(b, a) for a, b in others])  6.35 us
    ppermute x3, waiting for transfers between devices, shifted(): lax.ppermute(value, axis, [(source, (source + steps) % count) for source...  2.69 us
    ppermute x3, waiting for transfers between devices, swapped(): pair = lax.ppermute(pair, 'py', pairs + [(b, a) for a, b in pairs])  1.75 us
  transfers between devices with their start and end apart: 9, of which 8 were waited for; matrix products, arithmetic and copies ran while one was open for 2% of the time, Pallas kernels for 13%

profile of v26, /device:TPU:0, one launch (start us, length us, event | category | flops | bytes accessed | tf_op | source)
XLA Modules:
  0.0 50.0 jit_solution(1559377499974996442)
XLA Ops:
  0.6 0.5 %collective-permute-start = (f32[64,16,128]{2,1,0:T(8,128)}, f32[64,16,128]{2,1,0:T(8,128)S(1)}, u32[]{:S(2)}, u32[]{:S(2)}) collective-permute-start(f32[64,16,128]{2,1,0:T(8,128)} %bitcast.10), channel_id=1, source_target_pairs={{0,16},{16,0},{1,17},{17,1},{2,18},{18,2},{3,19},{19,3},{4,20},{20... | collective-permute-start | bytes 1572872 | tf_op jit(solution)/shard_map/ppermute | solution.py:326
  1.1 1.0 %constant_dynamic-slice_fusion.part_ref = f32[32,16,128]{2,1,0:T(8,128)S(1)} fusion(f32[64,16,128]{2,1,0:T(8,128)} %bitcast.11, s32[]{:T(128)S(6)} %select_n.3), kind=kLoop, calls=%fused_computation | loop fusion | bytes 524292 | tf_op jit(solution)/shard_map/dynamic_slice | solution.py:371
  2.2 0.8 %prepare.1 = (bf16[208,208]{1,0:T(8,128)(2,1)S(1)}, bf16[208,208]{1,0:T(8,128)(2,1)S(1)}, bf16[128,160]{1,0:T(8,128)(2,1)S(1)}, bf16[160,208]{1,0:T(8,128)(2,1)S...) custom-call(f32[125,125]{1,0:T(8,128)S(1)} %copy-done.1, ...), custom_call_target="tpu_custom_call" | custom-call | tf_op jit(solution)/shard_map/prepare/pallas_call | solution.py:331
  3.0 0.7 %to_cells.1 = (f32[4,32,1024]{2,1,0:T(8,128)S(1)}, f32[4,8,1024]{2,1,0:T(8,128)S(1)}, f32[4,8,1024]{2,1,0:T(8,128)S(1)}) custom-call(f32[4,16,1024]{2,1,0:T(8,128)S(1)} %get-tuple-element.28.own_ref, f32[64,16,128]{2,1,0:T(8,128)S(1)} %collective-permute-done.refs_0_, bf16[512,512]{1,0:T(8,128)(2,1)S(1)} %get-tuple-element.29.refs_1_, ...), custom_call_target="tpu_custom_call" | custom-call | tf_op jit(solution)/shard_map/to_cells/pallas_call | solution.py:331
  3.6 6.8 %collective-permute-start.2 = (f32[4,8,1024]{2,1,0:T(8,128)S(1)}, f32[4,8,1024]{2,1,0:T(8,128)S(1)}, u32[]{:S(2)}, u32[]{:S(2)}) collective-permute-start(f32[4,8,1024]{2,1,0:T(8,128)S(1)} %get-tuple-element.35), channel_id=1, source_target_pairs={{1,2},{3,4},{5,6},{7,8},{9,10},{11,12},{13,14},{15,0},{2,1},{4,3},... | collective-permute-start | bytes 393224 | tf_op jit(solution)/shard_map/ppermute | solution.py:319
  10.5 1.2 %collective-permute-done.1.refs_1_ = f32[16,128]{1,0:T(8,128)S(1)} collective-permute-done((f32[16,128]{1,0:T(8,128)S(1)}, f32[16,128]{1,0:T(8,128)S(1)}, u32[]{:S(2)}, u32[]{:S(2)}) %collective-permute-start.1) | collective-permute-done | bytes 8224 | tf_op jit(solution)/shard_map/ppermute | solution.py:326
  11.8 1.3 %inner.3.inner_ref = f32[4,32,1024]{2,1,0:T(8,128)S(1)} custom-call(f32[4,32,1024]{2,1,0:T(8,128)S(1)} %get-tuple-element.31.refs_0_.refs_6_, f32[4,32,128]{2,1,0:T(8,128)S(1)} %levels.1.refs_1_, bf16[208,208]{1,0:T(8,128)(2,1)S(1)} %get-tuple-element.32.refs_2_, bf16[208,208]{1,0:T(8,128)(2,1)S(1)} %get-tuple-element.33.refs_3_, ...), custom_call_target="tpu_custom_call" | custom-call | tf_op jit(solution)/shard_map/inner/pallas_call | solution.py:331
  13.1 1.3 %collective-permute-done.2.from_other_ref = f32[4,8,1024]{2,1,0:T(8,128)S(1)} collective-permute-done((f32[4,8,1024]{2,1,0:T(8,128)S(1)}, f32[4,8,1024]{2,1,0:T(8,128)S(1)}, u32[]{:S(2)}, u32[]{:S(2)}) %collective-permute-start.2) | collective-permute-done | bytes 131104 | tf_op jit(solution)/shard_map/ppermute | solution.py:319
  14.4 1.4 %collective-permute-done.3.from_pair_ref = f32[4,8,1024]{2,1,0:T(8,128)S(1)} collective-permute-done((f32[4,8,1024]{2,1,0:T(8,128)S(1)}, f32[4,8,1024]{2,1,0:T(8,128)S(1)}, u32[]{:S(2)}, u32[]{:S(2)}) %collective-permute-start.3) | collective-permute-done | bytes 131104 | tf_op jit(solution)/shard_map/ppermute | solution.py:320
  15.8 0.8 %finish.2 = (f32[4,32,1024]{2,1,0:T(8,128)S(1)}, f32[4,8,1024]{2,1,0:T(8,128)S(1)}, f32[4,8,1024]{2,1,0:T(8,128)S(1)}) custom-call(f32[4,32,1024]{2,1,0:T(8,128)S(1)} %inner.3.inner_ref, f32[4,8,1024]{2,1,0:T(8,128)S(1)} %collective-permute-done.2.from_other_ref, f32[4,8,1024]{2,1,0:T(8,128)S(1)} %collective-permute-done.3.from_pair_ref, ...), custom_call_target="tpu_custom_call" | custom-call | tf_op jit(solution)/shard_map/finish/pallas_call | solution.py:331
  16.6 4.0 %collective-permute-start.4 = (f32[4,8,1024]{2,1,0:T(8,128)S(1)}, f32[4,8,1024]{2,1,0:T(8,128)S(1)}, u32[]{:S(2)}, u32[]{:S(2)}) collective-permute-start(f32[4,8,1024]{2,1,0:T(8,128)S(1)} %get-tuple-element.40), channel_id=1, source_target_pairs={{1,2},{3,4},{5,6},{7,8},{9,10},{11,12},{13,14},{15,0},{2,1},{4,3},... | collective-permute-start | bytes 393224 | tf_op jit(solution)/shard_map/ppermute | solution.py:319
  20.6 1.3 %inner.4.inner_ref = f32[4,32,1024]{2,1,0:T(8,128)S(1)} custom-call(f32[4,32,1024]{2,1,0:T(8,128)S(1)} %get-tuple-element.39.refs_0_.refs_6_, f32[4,32,128]{2,1,0:T(8,128)S(1)} %levels.1.refs_1_, bf16[208,208]{1,0:T(8,128)(2,1)S(1)} %get-tuple-element.32.refs_2_, bf16[208,208]{1,0:T(8,128)(2,1)S(1)} %get-tuple-element.33.refs_3_, ...), custom_call_target="tpu_custom_call" | custom-call | tf_op jit(solution)/shard_map/inner/pallas_call | solution.py:331
  21.9 3.3 %collective-permute-done.4.from_other_ref = f32[4,8,1024]{2,1,0:T(8,128)S(1)} collective-permute-done((f32[4,8,1024]{2,1,0:T(8,128)S(1)}, f32[4,8,1024]{2,1,0:T(8,128)S(1)}, u32[]{:S(2)}, u32[]{:S(2)}) %collective-permute-start.4) | collective-permute-done | bytes 131104 | tf_op jit(solution)/shard_map/ppermute | solution.py:319
  25.3 0.3 collective-permute-done.5.from_pair_ref
  25.6 0.8 %finish.3 = (f32[4,32,1024]{2,1,0:T(8,128)S(1)}, f32[4,8,1024]{2,1,0:T(8,128)S(1)}, f32[4,8,1024]{2,1,0:T(8,128)S(1)}) custom-call(f32[4,32,1024]{2,1,0:T(8,128)S(1)} %inner.4.inner_ref, f32[4,8,1024]{2,1,0:T(8,128)S(1)} %collective-permute-done.4.from_other_ref, f32[4,8,1024]{2,1,0:T(8,128)S(1)} %collective-permute-done.5.from_pair_ref, ...), custom_call_target="tpu_custom_call" | custom-call | tf_op jit(solution)/shard_map/finish/pallas_call | solution.py:331
  26.4 3.7 %collective-permute-start.6 = (f32[4,8,1024]{2,1,0:T(8,128)S(1)}, f32[4,8,1024]{2,1,0:T(8,128)S(1)}, u32[]{:S(2)}, u32[]{:S(2)}) collective-permute-start(f32[4,8,1024]{2,1,0:T(8,128)S(1)} %get-tuple-element.46), channel_id=1, source_target_pairs={{1,2},{3,4},{5,6},{7,8},{9,10},{11,12},{13,14},{15,0},{2,1},{4,3},... | collective-permute-start | bytes 393224 | tf_op jit(solution)/shard_map/ppermute | solution.py:319
  30.1 1.6 %margin_rows.1.refs_2_ = bf16[256,2048]{1,0:T(8,128)(2,1)S(1)} custom-call(bf16[4096,128]{1,0:T(8,128)(2,1)S(1)} %bitcast.6), custom_call_target="tpu_custom_call" | custom-call | tf_op jit(solution)/shard_map/margin_rows/pallas_call | solution.py:331
  31.7 1.5 %inner.5 = (f32[4,32,1024]{2,1,0:T(8,128)S(1)}, bf16[512,512]{1,0:T(8,128)(2,1)S(1)}) custom-call(f32[4,32,1024]{2,1,0:T(8,128)S(1)} %get-tuple-element.42.refs_0_, f32[4,32,128]{2,1,0:T(8,128)S(1)} %levels.1.refs_1_, bf16[208,208]{1,0:T(8,128)(2,1)S(1)} %get-tuple-element.32.refs_2_, bf16[208,208]{1,0:T(8,128)(2,1)S(1)} %get-tuple-element.33.refs_3_, ...), custom_call_target="tpu_custom_call" | custom-call | tf_op jit(solution)/shard_map/inner/pallas_call | solution.py:331
  33.3 1.7 %collective-permute-done.6.refs_1_ = f32[4,8,1024]{2,1,0:T(8,128)S(1)} collective-permute-done((f32[4,8,1024]{2,1,0:T(8,128)S(1)}, f32[4,8,1024]{2,1,0:T(8,128)S(1)}, u32[]{:S(2)}, u32[]{:S(2)}) %collective-permute-start.6) | collective-permute-done | bytes 131104 | tf_op jit(solution)/shard_map/ppermute | solution.py:319
  35.1 0.8 %from_cells.1 = (f32[32,16,128]{2,1,0:T(8,128)S(1)}, f32[32,16,128]{2,1,0:T(8,128)S(1)}) custom-call(f32[4,32,1024]{2,1,0:T(8,128)S(1)} %get-tuple-element.45.refs_0_, f32[4,8,1024]{2,1,0:T(8,128)S(1)} %collective-permute-done.6.refs_1_, f32[4,8,1024]{2,1,0:T(8,128)S(1)} %collective-permute-done.7.refs_2_, ...), custom_call_target="tpu_custom_call" | custom-call | tf_op jit(solution)/shard_map/from_cells/pallas_call | solution.py:331
  35.9 1.5 %collective-permute-done.8.refs_1_ = f32[32,16,128]{2,1,0:T(8,128)S(1)} collective-permute-done((f32[32,16,128]{2,1,0:T(8,128)S(1)}, f32[32,16,128]{2,1,0:T(8,128)S(1)}, u32[]{:S(2)}, u32[]{:S(2)}) %collective-permute-start.8) | collective-permute-done | bytes 262176 | tf_op jit(solution)/shard_map/ppermute | solution.py:326
  37.4 0.5 %margin.1 = f32[2,64,128]{2,1,0:T(8,128)S(1)} custom-call(f32[32,16,128]{2,1,0:T(8,128)S(1)} %get-tuple-element.49.refs_0_, f32[32,16,128]{2,1,0:T(8,128)S(1)} %collective-permute-done.8.refs_1_, bf16[256,2048]{1,0:T(8,128)(2,1)S(1)} %margin_rows.1.refs_2_), custom_call_target="tpu_custom_call" | custom-call | tf_op jit(solution)/shard_map/margin/pallas_call | solution.py:331
  38.0 11.2 %all_to_all.5.tiles_ref = f32[32,4,128]{2,1,0:T(4,128)S(1)} all-to-all(f32[32,4,128]{2,1,0:T(4,128)S(1)} %bitcast.7), channel_id=1, replica_groups=mesh['px'=2,'py'=16] {'px','py'}, dimensions={0} | all-to-all | bytes 131072 | tf_op jit(solution)/shard_map/all_to_all | solution.py:447
  49.2 0.8 %result.1 = (f32[16,32]{1,0:T(8,128)}, f32[64,16,128]{2,1,0:T(8,128)}) custom-call(f32[32,4,128]{2,1,0:T(4,128)S(1)} %all_to_all.5.tiles_ref, f32[32,16,128]{2,1,0:T(8,128)S(1)} %get-tuple-element.49.refs_0_, f32[32,16,128]{2,1,0:T(8,128)S(1)} %collective-permute-done.8.refs_1_), custom_call_target="tpu_custom_call" | custom-call | tf_op jit(solution)/shard_map/result/pallas_call | solution.py:331
  (14 shorter events, 0.3 us)
Async XLA Ops:
  0.6 2.3 %collective-permute-start = (f32[64,16,128]{2,1,0:T(8,128)}, f32[64,16,128]{2,1,0:T(8,128)S(1)}, u32[]{:S(2)}, u32[]{:S(2)}) collective-permute-start(f32[64,16,128]{2,1,0:T(8,128)} %bitcast.10), channel_id=1, source_target_pairs={{0,16},{16,0},{1,17},{17,1},{2,18},{18,2},{3,19},{19,3},{4,20},{20... | collective-permute-start | bytes 1572872 | tf_op jit(solution)/shard_map/ppermute | solution.py:326
  1.1 1.0 %copy-start.1 = (f32[125,125]{1,0:T(8,128)S(1)}, f32[125,125]{1,0:T(8,128)}, u32[]{:S(2)}) copy-start(f32[125,125]{1,0:T(8,128)} %cell_ref.1) | copy-start | bytes 187504
  3.0 7.5 %copy-start.2 = (f32[4,4,128]{2,1,0:T(4,128)S(1)}, f32[4,4,128]{2,1,0:T(4,128)}, u32[]{:S(2)}) copy-start(f32[4,4,128]{2,1,0:T(4,128)} %param.5) | copy-start | bytes 24580
  3.6 10.8 %collective-permute-start.2 = (f32[4,8,1024]{2,1,0:T(8,128)S(1)}, f32[4,8,1024]{2,1,0:T(8,128)S(1)}, u32[]{:S(2)}, u32[]{:S(2)}) collective-permute-start(f32[4,8,1024]{2,1,0:T(8,128)S(1)} %get-tuple-element.35), channel_id=1, source_target_pairs={{1,2},{3,4},{5,6},{7,8},{9,10},{11,12},{13,14},{15,0},{2,1},{4,3},... | collective-permute-start | bytes 393224 | tf_op jit(solution)/shard_map/ppermute | solution.py:319
  10.5 5.3 %collective-permute-start.3 = (f32[4,8,1024]{2,1,0:T(8,128)S(1)}, f32[4,8,1024]{2,1,0:T(8,128)S(1)}, u32[]{:S(2)}, u32[]{:S(2)}) collective-permute-start(f32[4,8,1024]{2,1,0:T(8,128)S(1)} %get-tuple-element.36), channel_id=1, source_target_pairs={{0,1},{2,3},{4,5},{6,7},{8,9},{10,11},{12,13},{14,15},{1,0},{3,2},... | collective-permute-start | bytes 393224 | tf_op jit(solution)/shard_map/ppermute | solution.py:320
  10.5 1.2 %collective-permute-start.1 = (f32[16,128]{1,0:T(8,128)S(1)}, f32[16,128]{1,0:T(8,128)S(1)}, u32[]{:S(2)}, u32[]{:S(2)}) collective-permute-start(f32[16,128]{1,0:T(8,128)S(1)} %bitcast.8), channel_id=1, source_target_pairs={{0,16},{16,0},{1,17},{17,1},{2,18},{18,2},{3,19},{19,3},{4,20},{20... | collective-permute-start | bytes 24584 | tf_op jit(solution)/shard_map/ppermute | solution.py:326
  16.6 8.7 %collective-permute-start.4 = (f32[4,8,1024]{2,1,0:T(8,128)S(1)}, f32[4,8,1024]{2,1,0:T(8,128)S(1)}, u32[]{:S(2)}, u32[]{:S(2)}) collective-permute-start(f32[4,8,1024]{2,1,0:T(8,128)S(1)} %get-tuple-element.40), channel_id=1, source_target_pairs={{1,2},{3,4},{5,6},{7,8},{9,10},{11,12},{13,14},{15,0},{2,1},{4,3},... | collective-permute-start | bytes 393224 | tf_op jit(solution)/shard_map/ppermute | solution.py:319
  20.6 5.0 %collective-permute-start.5 = (f32[4,8,1024]{2,1,0:T(8,128)S(1)}, f32[4,8,1024]{2,1,0:T(8,128)S(1)}, u32[]{:S(2)}, u32[]{:S(2)}) collective-permute-start(f32[4,8,1024]{2,1,0:T(8,128)S(1)} %get-tuple-element.41), channel_id=1, source_target_pairs={{0,1},{2,3},{4,5},{6,7},{8,9},{10,11},{12,13},{14,15},{1,0},{3,2},... | collective-permute-start | bytes 393224 | tf_op jit(solution)/shard_map/ppermute | solution.py:320
  20.6 9.5 %copy-start = (bf16[256,4,4,128]{3,2,1,0:T(4,128)(2,1)S(1)}, bf16[256,4,4,128]{3,2,1,0:T(4,128)(2,1)}, u32[]{:S(2)}) copy-start(bf16[256,4,4,128]{3,2,1,0:T(4,128)(2,1)} %param.7) | copy-start | bytes 3145732
  26.4 8.6 %collective-permute-start.6 = (f32[4,8,1024]{2,1,0:T(8,128)S(1)}, f32[4,8,1024]{2,1,0:T(8,128)S(1)}, u32[]{:S(2)}, u32[]{:S(2)}) collective-permute-start(f32[4,8,1024]{2,1,0:T(8,128)S(1)} %get-tuple-element.46), channel_id=1, source_target_pairs={{1,2},{3,4},{5,6},{7,8},{9,10},{11,12},{13,14},{15,0},{2,1},{4,3},... | collective-permute-start | bytes 393224 | tf_op jit(solution)/shard_map/ppermute | solution.py:319
  30.1 5.0 %collective-permute-start.7 = (f32[4,8,1024]{2,1,0:T(8,128)S(1)}, f32[4,8,1024]{2,1,0:T(8,128)S(1)}, u32[]{:S(2)}, u32[]{:S(2)}) collective-permute-start(f32[4,8,1024]{2,1,0:T(8,128)S(1)} %get-tuple-element.47), channel_id=1, source_target_pairs={{0,1},{2,3},{4,5},{6,7},{8,9},{10,11},{12,13},{14,15},{1,0},{3,2},... | collective-permute-start | bytes 393224 | tf_op jit(solution)/shard_map/ppermute | solution.py:320
  35.8 1.6 %collective-permute-start.8 = (f32[32,16,128]{2,1,0:T(8,128)S(1)}, f32[32,16,128]{2,1,0:T(8,128)S(1)}, u32[]{:S(2)}, u32[]{:S(2)}) collective-permute-start(f32[32,16,128]{2,1,0:T(8,128)S(1)} %get-tuple-element.50), channel_id=1, source_target_pairs={{0,16},{16,0},{1,17},{17,1},{2,18},{18,2},{3,19},{19,3},{4,20},{20... | collective-permute-start | bytes 786440 | tf_op jit(solution)/shard_map/ppermute | solution.py:326
